TPU v7x, 32 devices: a whole 2x2x4 slice. The times are simulated.
32 devices in a mesh: runs: 2 (over y), sec: 8 (over z, x), env: 2 (over core).
Axes of the slice: x: 2, y: 2, z: 4, core: 2. Of those that a mesh axis runs over, the one named last changes fastest.
Arguments:
- amplitudes: bfloat16 [16, 128, 1024], P(('runs', 'sec'), None, 'env'), parts along dimension 0, may hold values from -6 to 6
- widths: int32 [16], P('runs'), parts along dimension 0, may hold values from 1 to 1024, 4096 in all
- holders: int32 [16], P('runs'), parts along dimension 0, may hold values from 0 to 7, each once
- left_env: bfloat16 [16, 3, 1024, 1024], P(('runs', 'sec'), None, None, 'env'), parts along dimension 0, may hold values from -1 to 4
- right_env: bfloat16 [6, 128, 128], P('runs'), parts along dimension 0, may hold values from -1 to 2
Outputs:
- first_product: bfloat16 [16, 128, 1024], P(('runs', 'sec'), None, 'env'), parts along dimension 0
- second_product: bfloat16 [16, 128, 1024], P(('runs', 'sec'), None, 'env'), parts along dimension 0
There are 2 independent parts, one for each index of `runs`. A program takes and returns all parts, laid end to end along the dimension named above; each array names one. Nothing has to cross between parts.
Inputs may be any that keep to these rules, and one draw needn't show every extreme that they name: `holders`: each sector of 0 to 7 is held by exactly one slot; sector p has up charge p // 4 and down charge p % 4. The widths sum to 4096; the largest is exactly 1024.
All inputs are finite; a program needn't handle non-finite values.
Results may differ from a plain program's by a relative error of at most 0.0058.
Values may be sent and summed in bfloat16 or wider, within the bound.
No kernel may reach another device: no remote copies, remote signals or barrier semaphores. Data moves between devices by JAX's collectives and lax.ppermute only.
A program may use at most 64 MiB of HBM per device.

v0:
```python
import jax
import jax.numpy as jnp
from jax import lax
from jax.sharding import PartitionSpec as P

QDOWN = 4


term_shifts = ((0, 0), (1, 0), (0, 1))


def routing_table(holders):
    n_slots = holders.shape[0]
    tables = []
    for shifted in term_shifts:
        up_charge = holders // QDOWN - shifted[0]
        down_charge = holders % QDOWN - shifted[1]
        permitted = (
            (up_charge >= 0)
            & (up_charge < n_slots // QDOWN)
            & (down_charge >= 0)
            & (down_charge < QDOWN)
        )
        wanted = holders - QDOWN * shifted[0] - shifted[1]
        hits = (holders[None, :] == wanted[:, None]) & permitted[:, None]
        tables.append(hits)
    return jnp.stack(tables).astype(jnp.bfloat16)


def make_combine(routes):

    def combine(received):
        summed = jnp.einsum("tsr,trck->sck", routes, received, preferred_element_type=jnp.float32)
        return lax.all_to_all(
            summed.astype(jnp.bfloat16), "sec", split_axis=0, concat_axis=1, tiled=True
        ).astype(summed.dtype)

    return combine


def hamiltonian_product(vector, live_mask, routing, left_env, right_env):
    own_products = jnp.einsum(
        "tij,sjw->tsiw", right_env, vector, preferred_element_type=jnp.float32
    ).astype(jnp.bfloat16)
    outgoing = jnp.einsum(
        "tsik,stkw->tsiw",
        lax.all_gather(own_products, "env", axis=3, tiled=True),
        left_env,
        preferred_element_type=jnp.float32,
    )
    outgoing = outgoing.astype(jnp.bfloat16)
    summer = make_combine(routing)
    gathered = summer(lax.all_to_all(outgoing, "sec", split_axis=2, concat_axis=1, tiled=True))
    return (gathered * live_mask).astype(jnp.bfloat16)


def on_device(amplitudes, widths, holders, left_env, right_env):
    slots_dev, right_dim, half_width = amplitudes.shape
    owner_index = lax.axis_index("sec")
    env_side = lax.axis_index("env")
    my_sectors = lax.dynamic_slice_in_dim(holders, owner_index * slots_dev, slots_dev)
    sector_ids = jnp.arange(holders.shape[0], dtype=jnp.int32)
    my_widths = jnp.sum(
        jnp.where(my_sectors[:, None] == sector_ids[None, :], widths[None, :], 0), axis=1
    )
    row_index = env_side * half_width + jnp.arange(half_width, dtype=jnp.int32)
    live_mask = (row_index[None, None, :] < my_widths[:, None, None]).astype(jnp.float32)
    routing = routing_table(holders)
    start_vector = jnp.where(live_mask > 0, amplitudes, jnp.zeros_like(amplitudes))
    first_product = hamiltonian_product(start_vector, live_mask, routing, left_env, right_env)
    basis_f = start_vector.astype(jnp.float32)
    first_f = first_product.astype(jnp.float32)
    correlation, self_norm = lax.psum(
        (jnp.sum(basis_f * first_f), jnp.sum(basis_f * basis_f)), ("sec", "env")
    )
    quotient = correlation / self_norm
    residual = first_f - quotient * basis_f
    resid_norm = lax.psum(jnp.sum(residual * residual), ("sec", "env"))
    live_count = right_dim * jnp.sum(widths).astype(jnp.float32)
    probe_vector = (residual * lax.rsqrt(resid_norm / live_count + 1e-06)).astype(jnp.bfloat16)
    second_product = hamiltonian_product(probe_vector, live_mask, routing, left_env, right_env)
    return (first_product, second_product)


def solution(mesh):
    in_specs = (
        P(("runs", "sec"), None, "env"),
        P("runs"),
        P("runs"),
        P(("runs", "sec"), None, None, "env"),
        P("runs", None, None),
    )
    out_specs = (P(("runs", "sec"), None, "env"), P(("runs", "sec"), None, "env"))
    return jax.shard_map(
        on_device, mesh=mesh, in_specs=in_specs, out_specs=out_specs, check_vma=False
    )
```

profile of v0, /device:TPU:0, one launch (start us, length us, event | category | flops | bytes accessed | tf_op | source)
XLA Modules:
  0.0 143.1 jit_solution(6405057631710294311)
XLA Ops:
  0.6 0.0 copy-start
  0.6 1.4 dynamic_slice.3
  2.0 1.9 %fusion.41 = (s32[]{:T(128)}, s32[]{:T(128)}) fusion(s32[8]{0:T(128)} %param.6, s32[]{:T(128)} %bitcast.1), kind=kLoop, calls=%fused_computation.63 | loop fusion | flops 30 | bytes 44 | tf_op jit(solution)/shard_map/reduce_sum | solution.py:79
  4.0 0.6 broadcast_compare_fusion
  4.6 1.2 fusion.16
  5.8 2.4 %all_gather.6 = bf16[3,1,128,1024]{2,3,0,1:T(8,128)(2,1)S(1)} all-gather(bf16[3,1,128,512]{2,3,0,1:T(8,128)(2,1)S(1)} %fusion.16), channel_id=1, replica_groups=mesh['runs'=2,'sec'=8,'env'=2] {'env'}, dimensions={3}, use_global_device_ids=true | all-gather | bytes 1179648 | tf_op jit(solution)/shard_map/all_gather | solution.py:47
  8.3 0.0 copy-done
  8.3 0.7 fusion.13
  8.9 1.1 copy.31
  10.1 7.2 %all-to-all-start = ((bf16[3,1,128,512]{3,0,1,2:T(4,128)(2,1)}), bf16[3,1,128,512]{3,0,1,2:T(4,128)(2,1)}, u32[]{:S(2)}, u32[]{:S(2)}) async-start(bf16[3,1,128,512]{3,0,1,2:T(4,128)(2,1)} %copy.31), calls=%async_computation | async-start | bytes 1048576 | tf_op jit(solution)/shard_map/all_to_all | solution.py:53
  17.3 0.0 copy-done.3
  17.3 0.1 compare_and_fusion.2
  17.4 14.8 %all-to-all-done = bf16[3,1,128,512]{3,0,1,2:T(4,128)(2,1)} async-done(((bf16[3,1,128,512]{3,0,1,2:T(4,128)(2,1)}), bf16[3,1,128,512]{3,0,1,2:T(4,128)(2,1)}, u32[]{:S(2)}, u32[]{:S(2)}) %all-to-all-start) | async-done | bytes 393248 | tf_op jit(solution)/shard_map/all_to_all | solution.py:53
  32.2 1.4 fusion.18
  33.6 0.7 copy.34
  34.3 3.6 %all-to-all-start.1 = ((bf16[8,16,512]{2,1,0:T(8,128)(2,1)}), bf16[8,16,512]{2,1,0:T(8,128)(2,1)S(1)}, u32[]{:S(2)}, u32[]{:S(2)}) async-start(bf16[8,16,512]{2,1,0:T(8,128)(2,1)} %copy.34), calls=%async_computation.1 | async-start | bytes 262144 | tf_op jit(solution)/shard_map/all_to_all | solution.py:34
  38.6 0.6 fusion.35
  39.2 6.1 %all-to-all-done.1 = bf16[8,16,512]{2,1,0:T(8,128)(2,1)S(1)} async-done(((bf16[8,16,512]{2,1,0:T(8,128)(2,1)}), bf16[8,16,512]{2,1,0:T(8,128)(2,1)S(1)}, u32[]{:S(2)}, u32[]{:S(2)}) %all-to-all-start.1) | async-done | bytes 131104 | tf_op jit(solution)/shard_map/all_to_all | solution.py:34
  45.3 0.0 copy-done.4
  45.3 0.0 copy-done.1
  45.3 0.8 fusion.25
  46.1 30.3 %all-reduce = (f32[]{:T(128)}, f32[]{:T(128)}) all-reduce(f32[]{:T(128)} %get-tuple-element.3, f32[]{:T(128)} %get-tuple-element.2), channel_id=1, replica_groups=mesh['runs'=2,'sec'=8,'env'=2] {'sec','env'}, use_global_device_ids=true, to_apply=%region_2.3 | all-reduce | flops 2 | bytes 16 | tf_op jit(solution)/shard_map/psum | solution.py:73
  77.7 0.7 multiply_reduce_fusion
  78.3 30.1 %psum.23 = f32[]{:T(128)} all-reduce(f32[]{:T(128)} %multiply_reduce_fusion), channel_id=1, replica_groups=mesh['runs'=2,'sec'=8,'env'=2] {'sec','env'}, use_global_device_ids=true, to_apply=%region_6.7 | all-reduce | flops 1 | bytes 8 | tf_op jit(solution)/shard_map/psum | solution.py:78
  109.1 1.2 fusion.17
  110.3 2.4 %all_gather.7 = bf16[3,1,128,1024]{2,3,0,1:T(8,128)(2,1)S(1)} all-gather(bf16[3,1,128,512]{2,3,0,1:T(8,128)(2,1)S(1)} %fusion.17), channel_id=1, replica_groups=mesh['runs'=2,'sec'=8,'env'=2] {'env'}, dimensions={3}, use_global_device_ids=true | all-gather | bytes 1179648 | tf_op jit(solution)/shard_map/all_gather | solution.py:47
  112.7 0.7 fusion.10
  113.4 0.3 copy.37
  113.7 17.5 %all_to_all.42 = bf16[3,1,128,512]{3,0,1,2:T(4,128)(2,1)S(1)} all-to-all(bf16[3,1,128,512]{3,0,1,2:T(4,128)(2,1)S(1)} %copy.37), channel_id=1, replica_groups=mesh['runs'=2,'sec'=8,'env'=2] {'sec'}, dimensions={2} | all-to-all | bytes 786432 | tf_op jit(solution)/shard_map/all_to_all | solution.py:53
  131.2 0.4 fusion.19
  131.7 10.8 %all_to_all.43 = bf16[8,16,512]{2,1,0:T(8,128)(2,1)S(1)} all-to-all(bf16[8,16,512]{2,1,0:T(8,128)(2,1)S(1)} %copy.40), channel_id=1, replica_groups=mesh['runs'=2,'sec'=8,'env'=2] {'sec'}, dimensions={0} | all-to-all | bytes 262144 | tf_op jit(solution)/shard_map/all_to_all | solution.py:34
  142.4 0.7 fusion.26
  (11 shorter events, 0.1 us)
Async XLA Ops:
  0.6 7.6 %copy-start = (bf16[1,3,1024,512]{3,2,1,0:T(8,128)(2,1)S(1)}, bf16[1,3,1024,512]{3,2,1,0:T(8,128)(2,1)}, u32[]{:S(2)}) copy-start(bf16[1,3,1024,512]{3,2,1,0:T(8,128)(2,1)} %param.8) | copy-start | bytes 9437188
  8.3 9.0 %copy-start.3 = (s32[8]{0:T(128)S(1)}, s32[8]{0:T(128)}, u32[]{:S(2)}) copy-start(s32[8]{0:T(128)} %param.7) | copy-start | bytes 100
  8.3 37.0 %copy-start.1 = (bf16[1,128,512]{2,1,0:T(8,128)(2,1)S(1)}, bf16[1,128,512]{2,1,0:T(8,128)(2,1)}, u32[]{:S(2)}) copy-start(bf16[1,128,512]{2,1,0:T(8,128)(2,1)} %param.5) | copy-start | bytes 393220
  10.1 22.1 %all-to-all-start = ((bf16[3,1,128,512]{3,0,1,2:T(4,128)(2,1)}), bf16[3,1,128,512]{3,0,1,2:T(4,128)(2,1)}, u32[]{:S(2)}, u32[]{:S(2)}) async-start(bf16[3,1,128,512]{3,0,1,2:T(4,128)(2,1)} %copy.31), calls=%async_computation | async-start | bytes 1048576 | tf_op jit(solution)/shard_map/all_to_all | solution.py:53
  17.4 27.9 %copy-start.4 = (pred[1,8,8]{2,1,0:T(8,128)(4,1)}, pred[1,8,8]{2,1,0:T(8,128)(4,1)S(1)}, u32[]{:S(2)}) copy-start(pred[1,8,8]{2,1,0:T(8,128)(4,1)S(1)} %get-tuple-element.16) | copy-start | bytes 196
  34.3 11.0 %all-to-all-start.1 = ((bf16[8,16,512]{2,1,0:T(8,128)(2,1)}), bf16[8,16,512]{2,1,0:T(8,128)(2,1)S(1)}, u32[]{:S(2)}, u32[]{:S(2)}) async-start(bf16[8,16,512]{2,1,0:T(8,128)(2,1)} %copy.34), calls=%async_computation.1 | async-start | bytes 262144 | tf_op jit(solution)/shard_map/all_to_all | solution.py:34
  46.1 67.3 %copy-start.2 = (bf16[1,128,512]{2,1,0:T(8,128)(2,1)}, bf16[1,128,512]{2,1,0:T(8,128)(2,1)S(1)}, u32[]{:S(2)}) copy-start(bf16[1,128,512]{2,1,0:T(8,128)(2,1)S(1)} %get-tuple-element.8) | copy-start | bytes 393220
  112.7 18.5 %copy-start.5 = (pred[1,8,8]{2,1,0:T(8,128)(4,1)S(1)}, pred[1,8,8]{2,1,0:T(8,128)(4,1)}, u32[]{:S(2)}) copy-start(pred[1,8,8]{2,1,0:T(8,128)(4,1)} %copy-done.4) | copy-start | bytes 196
where the time goes:
time: 144 us; the launch traced here: 143 us
  blocking collectives  93.5 us (65%)
  waiting for transfers between devices  20.9 us (15%)
  starting transfers between devices  10.8 us (8%)
  matrix products  5.61 us (4%)
  other arithmetic  5.3 us (4%)
  local copies, waits for them, and re-layouts  3.67 us (3%)
  between operations  3.35 us (2%)
    psum x1, blocking collectives, on_device(): lax.psum((jnp.sum(basis_f * first_f), jnp.sum(basis_f * basis_f)), ('sec'...  30.3 us
    psum x1, blocking collectives, on_device(): resid_norm = lax.psum(jnp.sum(residual * residual), ('sec', 'env'))  30.1 us
    all_to_all x1, blocking collectives, hamiltonian_product(): lax.all_to_all(outgoing, 'sec', split_axis=2, concat_axis=1, tiled=True)  17.5 us
    all_to_all x1, waiting for transfers between devices, hamiltonian_product(): lax.all_to_all(outgoing, 'sec', split_axis=2, concat_axis=1, tiled=True)  14.8 us
    all_to_all x1, blocking collectives, combine(): lax.all_to_all(summed.astype(jnp.bfloat16), 'sec', split_axis=0, concat_a...  10.8 us
    all_to_all x1, starting transfers between devices, hamiltonian_product(): lax.all_to_all(outgoing, 'sec', split_axis=2, concat_axis=1, tiled=True)  7.18 us
    all_to_all x1, waiting for transfers between devices, combine(): lax.all_to_all(summed.astype(jnp.bfloat16), 'sec', split_axis=0, concat_a...  6.12 us
    all_gather x2, blocking collectives, hamiltonian_product(): lax.all_gather(own_products, 'env', axis=3, tiled=True)  4.82 us
  transfers between devices with their start and end apart: 2, of which 2 were waited for; matrix products, arithmetic and copies ran while one was open for 0% of the time, Pallas kernels for 0%

commit v1 on v0

v1 whole, which is shorter than its diff:
```python
import jax
import jax.numpy as jnp
from jax import lax
from jax.sharding import PartitionSpec as P

QDOWN = 4

term_shifts = ((0, 0), (1, 0), (0, 1))


def route(holders):
    n_slots = holders.shape[0]
    sector_ids = jnp.arange(n_slots, dtype=jnp.int32)
    slot_of = jnp.argmax(holders[None, :] == sector_ids[:, None], axis=1)
    sources = []
    allowed = []
    for up, down in term_shifts[1:]:
        permitted = (holders // QDOWN - up >= 0) & (holders % QDOWN - down >= 0)
        wanted = jnp.clip(holders - QDOWN * up - down, 0, n_slots - 1)
        sources.append(slot_of[wanted])
        allowed.append(permitted)
    return sources, allowed


def contract(vector, left_env, right_env):
    products = jnp.einsum(
        "tij,jw->tiw", right_env, vector, preferred_element_type=jnp.float32
    ).astype(jnp.bfloat16)
    return jnp.einsum("tik,tkw->tiw", products, left_env, preferred_element_type=jnp.float32)


def spread(blocks, n_slots):
    terms, rows, width = blocks.shape
    pieces = blocks.reshape(terms, n_slots, rows // n_slots, width).swapaxes(0, 1)
    return lax.all_to_all(pieces, "sec", split_axis=0, concat_axis=0)


def collect(merged):
    n_slots, rows, width = merged.shape
    home = lax.all_to_all(merged, "sec", split_axis=0, concat_axis=0)
    return home.reshape(n_slots * rows, width)


def share(values, n_slots, me):
    lanes = jnp.zeros((1, 128), jnp.float32).at[0, : values.shape[0]].set(values)
    if n_slots & (n_slots - 1) or n_slots > 16:
        return lax.all_gather(lanes[0], "sec")
    table = jnp.where(jnp.arange(n_slots)[:, None] == me, lanes, 0.0)
    for offset in range(1, n_slots):
        pairs = [(i, i ^ offset) for i in range(n_slots)]
        other = lax.ppermute(lanes, "sec", pairs)
        table = jnp.where(jnp.arange(n_slots)[:, None] == (me ^ offset), other, table)
    return table


def merge(received, sources, allowed):
    total = 0.0
    for term, (source, permitted) in enumerate(zip(sources, allowed)):
        picked = received[source, term]
        total = total + jnp.where(permitted[:, None, None], picked, 0).astype(jnp.float32)
    return total


def on_device(amplitudes, widths, holders, left_env, right_env):
    slots_dev, right_dim, half_width = amplitudes.shape
    assert slots_dev == 1
    n_slots = holders.shape[0]
    me = lax.axis_index("sec")
    side = lax.axis_index("env")
    my_width = widths[holders[me]]
    row_index = side * half_width + jnp.arange(half_width, dtype=jnp.int32)
    live = (row_index < my_width)[None, :]
    sources, allowed = route(holders)
    envs = left_env[0]

    start = jnp.where(live, amplitudes[0], jnp.zeros_like(amplitudes[0]))
    start_full = lax.all_gather(start, "env", axis=1, tiled=True)
    outgoing = contract(start_full, envs, right_env).astype(jnp.bfloat16)
    stay = outgoing[0].astype(jnp.float32)
    received = spread(outgoing[1:], n_slots)
    arrived = collect(merge(received, sources, allowed).astype(jnp.bfloat16))
    first = jnp.where(live, stay + arrived.astype(jnp.float32), 0.0).astype(jnp.bfloat16)

    first_full = lax.all_gather(first, "env", axis=1, tiled=True).astype(jnp.float32)
    basis = start_full.astype(jnp.float32)
    overlap = jnp.sum(basis * first_full)
    norm = jnp.sum(basis * basis)
    own_quotient = jnp.where(norm > 0, overlap / jnp.where(norm > 0, norm, 1.0), 0.0)
    deflated = first_full - own_quotient * basis
    rest = jnp.sum(deflated * deflated)
    sums = share(jnp.stack([overlap, norm, own_quotient, rest]), n_slots, me)
    outgoing_2 = contract(deflated.astype(jnp.bfloat16), envs, right_env)
    received_2 = spread(outgoing_2[1:].astype(jnp.bfloat16), n_slots)

    quotient = jnp.sum(sums[:, 0]) / jnp.sum(sums[:, 1])
    shift = sums[:, 2] - quotient
    resid_norm = jnp.sum(sums[:, 3] + shift * shift * sums[:, 1])
    live_count = right_dim * jnp.sum(widths).astype(jnp.float32)
    scale = lax.rsqrt(resid_norm / live_count + 1e-06)
    mixed = received_2.astype(jnp.float32) + shift[:, None, None, None] * received.astype(
        jnp.float32
    )
    merged_2 = scale * merge(mixed, sources, allowed)
    arrived_2 = collect(merged_2.astype(jnp.bfloat16))
    stay_2 = scale * (outgoing_2[0] + (own_quotient - quotient) * stay)
    second = jnp.where(live, stay_2 + arrived_2.astype(jnp.float32), 0.0).astype(jnp.bfloat16)
    return first[None], second[None]


def solution(mesh):
    in_specs = (
        P(("runs", "sec"), None, "env"),
        P("runs"),
        P("runs"),
        P(("runs", "sec"), None, None, "env"),
        P("runs", None, None),
    )
    out_specs = (P(("runs", "sec"), None, "env"), P(("runs", "sec"), None, "env"))
    return jax.shard_map(
        on_device, mesh=mesh, in_specs=in_specs, out_specs=out_specs, check_vma=False
    )
```

time: 144 us -> 121 us (0.84)
  blocking collectives: 93.5 us -> 4.08 us
  local copies, waits for them, and re-layouts: 3.67 us -> 31 us
  starting transfers between devices: 10.8 us -> 29.4 us
  other arithmetic: 5.3 us -> 22.9 us
  between operations: 3.35 us -> 7.35 us
  waiting for transfers between devices: 20.9 us -> 18.9 us
    psum x2 -> x0, blocking collectives: 60.4 us -> none  [the longest x1 30.3 us: on_device(): lax.psum((jnp.sum(basis_f * first_f), jnp.sum(basis_f * basis_f)), ('sec'...]
    all_to_all x2 -> x0, blocking collectives: 28.2 us -> none  [the longest x1 17.5 us: hamiltonian_product(): lax.all_to_all(outgoing, 'sec', split_axis=2, concat_axis=1, tiled=True)]
    ppermute x0 -> x7, starting transfers between devices: none -> 11.2 us  [share(): other = lax.ppermute(lanes, 'sec', pairs)]
    gather x0 -> x6, local copies, waits for them, and re-layouts: none -> 9.57 us  [the longest x4 8.29 us: merge(): picked = received[source, term]]
    all_to_all x2 -> x4, starting transfers between devices: 10.8 us -> 18.2 us  [the longest x2 11.2 us: spread(): return lax.all_to_all(pieces, 'sec', split_axis=0, concat_axis=0)]
    convert_element_type x2 -> x6, other arithmetic: 1.24 us -> 7.96 us  [the longest x1 1.89 us: on_device(): jnp.where(live, stay_2 + arrived_2.astype(jnp.float32), 0.0)]
    slice x0 -> x4, local copies, waits for them, and re-layouts: none -> 6.24 us  [the longest x2 3.45 us: on_device(): received = spread(outgoing[1:], n_slots)]
    unnamed x12 -> x28, local copies, waits for them, and re-layouts: 0.03 us -> 5.78 us
  transfers between devices with their start and end apart: 2 -> 11, of which waited for: 2 -> 4; matrix products, arithmetic and copies ran while one was open for 0% -> 14% of each run, Pallas kernels for 0% -> 0%
where the time goes in v1:
time: 121 us; the launch traced here: 119 us
  local copies, waits for them, and re-layouts  31 us (26%)
  starting transfers between devices  29.4 us (24%)
  other arithmetic  22.9 us (19%)
  waiting for transfers between devices  18.9 us (16%)
  between operations  7.35 us (6%)
  matrix products  5.8 us (5%)
  blocking collectives  4.08 us (3%)
    ppermute x7, starting transfers between devices, share(): other = lax.ppermute(lanes, 'sec', pairs)  11.2 us
    all_to_all x2, starting transfers between devices, spread(): return lax.all_to_all(pieces, 'sec', split_axis=0, concat_axis=0)  11.2 us
    all_to_all x2, waiting for transfers between devices, spread(): return lax.all_to_all(pieces, 'sec', split_axis=0, concat_axis=0)  10.2 us
    all_to_all x2, waiting for transfers between devices, collect(): home = lax.all_to_all(merged, 'sec', split_axis=0, concat_axis=0)  8.66 us
    gather x4, local copies, waits for them, and re-layouts, merge(): picked = received[source, term]  8.29 us
    all_to_all x2, starting transfers between devices, collect(): home = lax.all_to_all(merged, 'sec', split_axis=0, concat_axis=0)  6.96 us
    dot_general x2, matrix products, contract(): jnp.einsum('tik,tkw->tiw', products, left_env, preferred_element_type=jnp...  5.8 us
    unnamed x28, local copies, waits for them, and re-layouts  5.78 us
  transfers between devices with their start and end apart: 11, of which 4 were waited for; matrix products, arithmetic and copies ran while one was open for 14% of the time, Pallas kernels for 0%

profile of v1, /device:TPU:0, one launch (start us, length us, event | category | flops | bytes accessed | tf_op | source)
XLA Modules:
  0.0 119.4 jit_solution(10218692468311721433)
XLA Ops:
  7.1 2.1 %all_gather.6 = bf16[128,1024]{0,1:T(8,128)(2,1)S(1)} all-gather(bf16[128,512]{0,1:T(8,128)(2,1)S(1)} %bitcast_select_fusion), channel_id=1, replica_groups=mesh['runs'=2,'sec'=8,'env'=2] {'env'}, dimensions={1}, use_global_device_ids=true | all-gather | bytes 393216 | tf_op jit(solution)/shard_map/all_gather | solution.py:77
  9.2 3.0 %fusion.6 = bf16[3,128,512]{1,2,0:T(8,128)(2,1)} fusion(bf16[1,3,1024,512]{3,2,1,0:T(8,128)(2,1)S(1)} %copy-done, bf16[3,128,128]{2,1,0:T(8,128)(2,1)} %param.11, bf16[128,1024]{0,1:T(8,128)(2,1)S(1)} %all_gather.6), kind=kOutput, calls=%fused_computation.14 | convolution fusion | flops 503906304 | bytes 3899392 | tf_op jit(solution)/shard_map/tik,tkw->tiw/dot_general | solution.py:29
  12.2 1.7 %slice.63 = bf16[2,128,512]{1,2,0:T(8,128)(2,1)} slice(bf16[3,128,512]{1,2,0:T(8,128)(2,1)} %fusion.6), slice={[1:3], [0:128], [0:512]} | slice | bytes 524288 | tf_op jit(solution)/shard_map/slice | solution.py:80
  13.8 1.8 %copy.35 = bf16[2,128,512]{2,1,0:T(8,128)(2,1)} copy(bf16[2,128,512]{1,2,0:T(8,128)(2,1)} %slice.63) | data formatting | bytes 524288 | tf_op jit(solution)/shard_map/slice | solution.py:80
  15.6 1.7 %copy.36 = bf16[8,2,16,512]{3,2,1,0:T(8,128)(2,1)} copy(bf16[8,2,16,512]{3,2,0,1:T(8,128)(2,1)} %bitcast.89) | data formatting | bytes 524288 | tf_op jit(solution)/shard_map/transpose | solution.py:34
  17.3 7.2 %all-to-all-start = ((bf16[8,2,16,512]{3,2,1,0:T(8,128)(2,1)}), bf16[8,2,16,512]{3,2,1,0:T(8,128)(2,1)}, u32[]{:S(2)}, u32[]{:S(2)}) async-start(bf16[8,2,16,512]{3,2,1,0:T(8,128)(2,1)} %copy.36), calls=%async_computation | async-start | bytes 524288 | tf_op jit(solution)/shard_map/all_to_all | solution.py:35
  27.0 6.8 %all-to-all-done = bf16[8,2,16,512]{3,2,1,0:T(8,128)(2,1)} async-done(((bf16[8,2,16,512]{3,2,1,0:T(8,128)(2,1)}), bf16[8,2,16,512]{3,2,1,0:T(8,128)(2,1)}, u32[]{:S(2)}, u32[]{:S(2)}) %all-to-all-start) | async-done | bytes 262176 | tf_op jit(solution)/shard_map/all_to_all | solution.py:35
  33.8 1.5 %gather_fusion.3 = bf16[8,16,512]{2,1,0:T(8,128)(2,1)S(1)} fusion(bf16[8,2,16,512]{3,2,1,0:T(8,128)(2,1)} %all-to-all-done, s32[8]{0:T(128)S(1)} %fusion.35), kind=kCustom, calls=%fused_computation.3 | custom fusion | bytes 262208 | tf_op jit(solution)/shard_map/gather | solution.py:59
  35.3 2.2 %gather_fusion.1 = bf16[8,16,512]{2,1,0:T(8,128)(2,1)} fusion(bf16[8,2,16,512]{3,2,1,0:T(8,128)(2,1)} %all-to-all-done, s32[8]{0:T(128)S(1)} %fusion.31), kind=kCustom, calls=%fused_computation.1 | custom fusion | bytes 262208 | tf_op jit(solution)/shard_map/gather | solution.py:59
  37.5 1.7 %add_convert_fusion = bf16[8,16,512]{2,1,0:T(8,128)(2,1)} fusion(bf16[8,16,512]{2,1,0:T(8,128)(2,1)S(1)} %gather_fusion.3, bf16[8,16,512]{2,1,0:T(8,128)(2,1)} %gather_fusion.1, pred[8]{0:T(512)(128)(4,1)} %compare_and_fusion, pred[8]{0:T(512)(128)(4,1)S(1)} %get-tuple-element.28), kind=kLoop, calls=%fused_computation.43 | loop fusion | flops 393216 | bytes 393232 | tf_op jit(solution)/shard_map/convert_element_type | solution.py:81
  39.2 3.6 %all-to-all-start.1 = ((bf16[8,16,512]{2,1,0:T(8,128)(2,1)}), bf16[8,16,512]{2,1,0:T(8,128)(2,1)S(1)}, u32[]{:S(2)}, u32[]{:S(2)}) async-start(bf16[8,16,512]{2,1,0:T(8,128)(2,1)} %add_convert_fusion), calls=%async_computation.1 | async-start | bytes 262144 | tf_op jit(solution)/shard_map/all_to_all | solution.py:40
  45.1 5.0 %all-to-all-done.1 = bf16[8,16,512]{2,1,0:T(8,128)(2,1)S(1)} async-done(((bf16[8,16,512]{2,1,0:T(8,128)(2,1)}), bf16[8,16,512]{2,1,0:T(8,128)(2,1)S(1)}, u32[]{:S(2)}, u32[]{:S(2)}) %all-to-all-start.1) | async-done | bytes 131104 | tf_op jit(solution)/shard_map/all_to_all | solution.py:40
  50.9 1.8 %copy.38 = f32[128,512]{0,1:T(8,128)} copy(f32[128,512]{1,0:T(8,128)} %bitcast.86) | data formatting | bytes 524288 | tf_op jit(solution)/shard_map/convert_element_type | solution.py:82
  53.7 2.0 %all_gather.7 = bf16[128,1024]{0,1:T(8,128)(2,1)S(1)} all-gather(bf16[128,512]{0,1:T(8,128)(2,1)S(1)} %fusion.21), channel_id=1, replica_groups=mesh['runs'=2,'sec'=8,'env'=2] {'env'}, dimensions={1}, use_global_device_ids=true | all-gather | bytes 393216 | tf_op jit(solution)/shard_map/all_gather | solution.py:84
  59.0 1.8 %multiply_reduce_fusion = f32[]{:T(128)} fusion(bf16[128,1024]{0,1:T(8,128)(2,1)S(1)} %all_gather.6, bf16[128,1024]{0,1:T(8,128)(2,1)} %copy-done.1, f32[]{:T(128)} %select_n.129), kind=kLoop, calls=%fused_computation.23 | loop fusion | flops 786431 | bytes 524296 | tf_op jit(solution)/shard_map/reduce_sum | solution.py:90
  60.8 2.6 %broadcast_select_fusion = f32[1,4]{1,0:T(1,128)S(1)} fusion(pred[]{:T(512)} %compare_reduce_fusion, f32[1,1]{1,0:T(1,128)} %bitcast.18, f32[1,1]{1,0:T(1,128)} %bitcast.17, f32[1,1]{1,0:T(1,128)} %bitcast.16, f32[1,1]{1,0:T(1,128)} %bitcast.15), kind=kLoop, calls=%fused_computation.64 | loop fusion | flops 16 | bytes 33 | tf_op jit(solution)/shard_map/select.13
  66.7 2.2 %collective-permute-start.4 = (f32[1,128]{1,0:T(1,128)S(1)}, f32[1,128]{1,0:T(1,128)S(1)}, u32[]{:S(2)}, u32[]{:S(2)}) collective-permute-start(f32[1,128]{1,0:T(1,128)S(1)} %get-tuple-element.33), channel_id=1, source_target_pairs={{0,6},{2,4},{4,2},{6,0},{8,14},{10,12},{12,10},{14,8},{1,7},{3,5},... | collective-permute-start | bytes 1544 | tf_op jit(solution)/shard_map/ppermute | solution.py:51
  69.4 2.2 %collective-permute-start.2 = (f32[1,128]{1,0:T(1,128)S(1)}, f32[1,128]{1,0:T(1,128)S(1)}, u32[]{:S(2)}, u32[]{:S(2)}) collective-permute-start(f32[1,128]{1,0:T(1,128)S(1)} %get-tuple-element.33), channel_id=1, source_target_pairs={{0,10},{2,8},{4,14},{6,12},{8,2},{10,0},{12,6},{14,4},{1,11},{3,9}... | collective-permute-start | bytes 1544 | tf_op jit(solution)/shard_map/ppermute | solution.py:51
  73.0 3.6 %collective-permute-start = (f32[1,128]{1,0:T(1,128)S(1)}, f32[1,128]{1,0:T(1,128)S(1)}, u32[]{:S(2)}, u32[]{:S(2)}) collective-permute-start(f32[1,128]{1,0:T(1,128)S(1)} %get-tuple-element.33), channel_id=1, source_target_pairs={{0,14},{2,12},{4,10},{6,8},{8,6},{10,4},{12,2},{14,0},{1,15},{3,13... | collective-permute-start | bytes 1544 | tf_op jit(solution)/shard_map/ppermute | solution.py:51
  76.6 2.8 %fusion = f32[3,128,512]{2,1,0:T(8,128)} fusion(bf16[1,3,1024,512]{3,2,1,0:T(8,128)(2,1)S(1)} %copy-done, bf16[3,128,128]{2,1,0:T(8,128)(2,1)} %param.11, bf16[128,1024]{0,1:T(8,128)(2,1)S(1)} %all_gather.6, bf16[128,1024]{0,1:T(8,128)(2,1)} %copy-done.1, f32[]{:T(128)} %select_n.129), kind=kOutput, calls=%fused_computation.6 | convolution fusion | flops 504365056 | bytes 4554756 | tf_op jit(solution)/shard_map/tik,tkw->tiw/dot_general | solution.py:29
  81.3 4.0 %all-to-all-start.2 = ((bf16[8,2,16,512]{3,2,1,0:T(8,128)(2,1)}), bf16[8,2,16,512]{3,2,1,0:T(8,128)(2,1)}, u32[]{:S(2)}, u32[]{:S(2)}) async-start(bf16[8,2,16,512]{3,2,1,0:T(8,128)(2,1)} %bitcast.88), calls=%async_computation.2 | async-start | bytes 524288 | tf_op jit(solution)/shard_map/all_to_all | solution.py:35
  90.1 3.4 %all-to-all-done.2 = bf16[8,2,16,512]{3,2,1,0:T(8,128)(2,1)} async-done(((bf16[8,2,16,512]{3,2,1,0:T(8,128)(2,1)}), bf16[8,2,16,512]{3,2,1,0:T(8,128)(2,1)}, u32[]{:S(2)}, u32[]{:S(2)}) %all-to-all-start.2) | async-done | bytes 262176 | tf_op jit(solution)/shard_map/all_to_all | solution.py:35
  93.6 2.0 %multiply_add_fusion = f32[8,2,16,512]{3,2,1,0:T(8,128)} fusion(bf16[8,2,16,512]{3,2,1,0:T(8,128)(2,1)} %all-to-all-done, bf16[8,2,16,512]{3,2,1,0:T(8,128)(2,1)} %all-to-all-done.2, f32[8]{0:T(128)S(1)} %get-tuple-element.27), kind=kLoop, calls=%fused_computation.22 | loop fusion | flops 524288 | bytes 1048608 | tf_op jit(solution)/shard_map/add | solution.py:100
  95.5 2.3 %gather_fusion.5 = f32[8,16,512]{2,1,0:T(8,128)} fusion(f32[8,2,16,512]{3,2,1,0:T(8,128)} %multiply_add_fusion, s32[8]{0:T(128)S(1)} %fusion.35), kind=kCustom, calls=%fused_computation.5 | custom fusion | bytes 524352 | tf_op jit(solution)/shard_map/gather | solution.py:59
  97.8 2.3 %gather_fusion.4 = f32[8,16,512]{2,1,0:T(8,128)} fusion(f32[8,2,16,512]{3,2,1,0:T(8,128)} %multiply_add_fusion, s32[8]{0:T(128)S(1)} %fusion.31), kind=kCustom, calls=%fused_computation.4 | custom fusion | bytes 524352 | tf_op jit(solution)/shard_map/gather | solution.py:59
  100.1 1.8 %multiply_convert_fusion = bf16[8,16,512]{2,1,0:T(8,128)(2,1)} fusion(f32[8,16,512]{2,1,0:T(8,128)} %gather_fusion.5, f32[8,16,512]{2,1,0:T(8,128)} %gather_fusion.4, f32[]{:T(128)S(6)} %rsqrt.3, pred[8]{0:T(512)(128)(4,1)S(1)} %copy-done.9, pred[8]{0:T(512)(128)(4,1)S(1)} %get-tuple-element.28), kind=kLoop, calls=%fused_computation.41 | loop fusion | flops 327680 | bytes 655380 | tf_op jit(solution)/shard_map/convert_element_type | solution.py:104
  101.9 3.4 %all-to-all-start.3 = ((bf16[8,16,512]{2,1,0:T(8,128)(2,1)}), bf16[8,16,512]{2,1,0:T(8,128)(2,1)S(1)}, u32[]{:S(2)}, u32[]{:S(2)}) async-start(bf16[8,16,512]{2,1,0:T(8,128)(2,1)} %multiply_convert_fusion), calls=%async_computation.3 | async-start | bytes 262144 | tf_op jit(solution)/shard_map/all_to_all | solution.py:40
  105.3 1.7 %slice.68 = f32[1,128,512]{2,1,0:T(8,128)} slice(f32[3,128,512]{2,1,0:T(8,128)} %fusion), slice={[0:1], [0:128], [0:512]} | slice | bytes 524288 | tf_op jit(solution)/shard_map/slice | solution.py:105
  108.9 3.7 %all-to-all-done.3 = bf16[8,16,512]{2,1,0:T(8,128)(2,1)S(1)} async-done(((bf16[8,16,512]{2,1,0:T(8,128)(2,1)}), bf16[8,16,512]{2,1,0:T(8,128)(2,1)S(1)}, u32[]{:S(2)}, u32[]{:S(2)}) %all-to-all-start.3) | async-done | bytes 131104 | tf_op jit(solution)/shard_map/all_to_all | solution.py:40
  113.3 1.8 %copy.42 = f32[1,128,512]{1,2,0:T(8,128)} copy(f32[1,128,512]{2,1,0:T(8,128)} %bitcast_convert_fusion) | data formatting | bytes 524288 | tf_op jit(solution)/shard_map/convert_element_type | solution.py:106
  115.1 1.9 %fusion.18 = (bf16[1,128,512]{1,2,0:T(8,128)(2,1)}, bf16[1,128,512]{1,2,0:T(8,128)(2,1)S(1)}) fusion(f32[1,128,512]{1,2,0:T(8,128)} %copy.42, f32[1,128,512]{1,2,0:T(8,128)S(1)} %copy.48, f32[]{:T(128)S(6)} %sub.45, f32[]{:T(128)S(6)} %rsqrt.3, pred[512]{0:T(512)(128)(4,1)S(1)} %add_compare_fusion, bf16[3,128,512]{1,2,0:T(8,128)(2,1)} %fusion.6, ...), kind=kLoop, calls=%fused_computation.34 | loop fusion | flops 655360 | bytes 1180168 | tf_op jit(solution)/shard_map/convert_element_type | solution.py:106
  117.0 1.7 %copy.44 = bf16[1,128,512]{2,1,0:T(8,128)(2,1)} copy(bf16[1,128,512]{1,2,0:T(8,128)(2,1)} %get-tuple-element.31) | data formatting | bytes 262144
  (68 shorter events, 25.0 us)
Async XLA Ops:
  0.6 8.5 %copy-start = (bf16[1,3,1024,512]{3,2,1,0:T(8,128)(2,1)S(1)}, bf16[1,3,1024,512]{3,2,1,0:T(8,128)(2,1)}, u32[]{:S(2)}) copy-start(bf16[1,3,1024,512]{3,2,1,0:T(8,128)(2,1)} %param.10) | copy-start | bytes 9437188
  7.1 17.4 %copy-start.11 = (s32[8]{0:T(128)S(1)}, s32[8]{0:T(128)}, u32[]{:S(2)}) copy-start(s32[8]{0:T(128)} %param.9) | copy-start | bytes 100
  17.3 16.5 %all-to-all-start = ((bf16[8,2,16,512]{3,2,1,0:T(8,128)(2,1)}), bf16[8,2,16,512]{3,2,1,0:T(8,128)(2,1)}, u32[]{:S(2)}, u32[]{:S(2)}) async-start(bf16[8,2,16,512]{3,2,1,0:T(8,128)(2,1)} %copy.36), calls=%async_computation | async-start | bytes 524288 | tf_op jit(solution)/shard_map/all_to_all | solution.py:35
  39.2 10.9 %all-to-all-start.1 = ((bf16[8,16,512]{2,1,0:T(8,128)(2,1)}), bf16[8,16,512]{2,1,0:T(8,128)(2,1)S(1)}, u32[]{:S(2)}, u32[]{:S(2)}) async-start(bf16[8,16,512]{2,1,0:T(8,128)(2,1)} %add_convert_fusion), calls=%async_computation.1 | async-start | bytes 262144 | tf_op jit(solution)/shard_map/all_to_all | solution.py:40
  55.7 0.7 copy-start.1
  60.8 25.1 %copy-start.3 = (pred[8]{0:T(512)(128)(4,1)S(1)}, pred[8]{0:T(512)(128)(4,1)}, u32[]{:S(2)}) copy-start(pred[8]{0:T(512)(128)(4,1)} %get-tuple-element.39) | copy-start | bytes 28
  60.8 25.1 %copy-start.4 = (pred[8]{0:T(512)(128)(4,1)S(1)}, pred[8]{0:T(512)(128)(4,1)}, u32[]{:S(2)}) copy-start(pred[8]{0:T(512)(128)(4,1)} %get-tuple-element.40) | copy-start | bytes 28
  60.8 25.1 %copy-start.5 = (pred[8]{0:T(512)(128)(4,1)S(1)}, pred[8]{0:T(512)(128)(4,1)}, u32[]{:S(2)}) copy-start(pred[8]{0:T(512)(128)(4,1)} %get-tuple-element.45) | copy-start | bytes 28
  60.8 25.1 %copy-start.6 = (pred[8]{0:T(512)(128)(4,1)S(1)}, pred[8]{0:T(512)(128)(4,1)}, u32[]{:S(2)}) copy-start(pred[8]{0:T(512)(128)(4,1)} %get-tuple-element.46) | copy-start | bytes 28
  60.8 25.1 %copy-start.7 = (pred[8]{0:T(512)(128)(4,1)S(1)}, pred[8]{0:T(512)(128)(4,1)}, u32[]{:S(2)}) copy-start(pred[8]{0:T(512)(128)(4,1)} %get-tuple-element.43) | copy-start | bytes 28
  60.8 25.1 %copy-start.8 = (pred[8]{0:T(512)(128)(4,1)S(1)}, pred[8]{0:T(512)(128)(4,1)}, u32[]{:S(2)}) copy-start(pred[8]{0:T(512)(128)(4,1)} %get-tuple-element.44) | copy-start | bytes 28
  63.4 8.1 %collective-permute-start.6 = (f32[1,128]{1,0:T(1,128)S(1)}, f32[1,128]{1,0:T(1,128)S(1)}, u32[]{:S(2)}, u32[]{:S(2)}) collective-permute-start(f32[1,128]{1,0:T(1,128)S(1)} %get-tuple-element.33), channel_id=1, source_target_pairs={{0,2},{2,0},{4,6},{6,4},{8,10},{10,8},{12,14},{14,12},{1,3},{3,1},... | collective-permute-start | bytes 1544 | tf_op jit(solution)/shard_map/ppermute | solution.py:51
  63.7 9.3 %collective-permute-start.5 = (f32[1,128]{1,0:T(1,128)S(1)}, f32[1,128]{1,0:T(1,128)S(1)}, u32[]{:S(2)}, u32[]{:S(2)}) collective-permute-start(f32[1,128]{1,0:T(1,128)S(1)} %get-tuple-element.33), channel_id=1, source_target_pairs={{0,4},{2,6},{4,0},{6,2},{8,12},{10,14},{12,8},{14,10},{1,5},{3,7},... | collective-permute-start | bytes 1544 | tf_op jit(solution)/shard_map/ppermute | solution.py:51
  66.7 33.4 %copy-start.9 = (pred[8]{0:T(512)(128)(4,1)S(1)}, pred[8]{0:T(512)(128)(4,1)}, u32[]{:S(2)}) copy-start(pred[8]{0:T(512)(128)(4,1)} %compare_and_fusion) | copy-start | bytes 28
  66.7 18.6 %collective-permute-start.4 = (f32[1,128]{1,0:T(1,128)S(1)}, f32[1,128]{1,0:T(1,128)S(1)}, u32[]{:S(2)}, u32[]{:S(2)}) collective-permute-start(f32[1,128]{1,0:T(1,128)S(1)} %get-tuple-element.33), channel_id=1, source_target_pairs={{0,6},{2,4},{4,2},{6,0},{8,14},{10,12},{12,10},{14,8},{1,7},{3,5},... | collective-permute-start | bytes 1544 | tf_op jit(solution)/shard_map/ppermute | solution.py:51
  69.0 16.4 %collective-permute-start.3 = (f32[1,128]{1,0:T(1,128)S(1)}, f32[1,128]{1,0:T(1,128)S(1)}, u32[]{:S(2)}, u32[]{:S(2)}) collective-permute-start(f32[1,128]{1,0:T(1,128)S(1)} %get-tuple-element.33), channel_id=1, source_target_pairs={{0,8},{2,10},{4,12},{6,14},{8,0},{10,2},{12,4},{14,6},{1,9},{3,11}... | collective-permute-start | bytes 1544 | tf_op jit(solution)/shard_map/ppermute | solution.py:51
  69.4 16.0 %collective-permute-start.2 = (f32[1,128]{1,0:T(1,128)S(1)}, f32[1,128]{1,0:T(1,128)S(1)}, u32[]{:S(2)}, u32[]{:S(2)}) collective-permute-start(f32[1,128]{1,0:T(1,128)S(1)} %get-tuple-element.33), channel_id=1, source_target_pairs={{0,10},{2,8},{4,14},{6,12},{8,2},{10,0},{12,6},{14,4},{1,11},{3,9}... | collective-permute-start | bytes 1544 | tf_op jit(solution)/shard_map/ppermute | solution.py:51
  71.5 13.8 %collective-permute-start.1 = (f32[1,128]{1,0:T(1,128)S(1)}, f32[1,128]{1,0:T(1,128)S(1)}, u32[]{:S(2)}, u32[]{:S(2)}) collective-permute-start(f32[1,128]{1,0:T(1,128)S(1)} %get-tuple-element.33), channel_id=1, source_target_pairs={{0,12},{2,14},{4,8},{6,10},{8,4},{10,6},{12,0},{14,2},{1,13},{3,15... | collective-permute-start | bytes 1544 | tf_op jit(solution)/shard_map/ppermute | solution.py:51
  73.0 12.4 %collective-permute-start = (f32[1,128]{1,0:T(1,128)S(1)}, f32[1,128]{1,0:T(1,128)S(1)}, u32[]{:S(2)}, u32[]{:S(2)}) collective-permute-start(f32[1,128]{1,0:T(1,128)S(1)} %get-tuple-element.33), channel_id=1, source_target_pairs={{0,14},{2,12},{4,10},{6,8},{8,6},{10,4},{12,2},{14,0},{1,15},{3,13... | collective-permute-start | bytes 1544 | tf_op jit(solution)/shard_map/ppermute | solution.py:51
  79.4 27.6 %copy-start.2 = (f32[8,16,512]{2,1,0:T(8,128)S(1)}, f32[8,16,512]{2,1,0:T(8,128)}, u32[]{:S(2)}) copy-start(f32[8,16,512]{2,1,0:T(8,128)} %convert_element_type.130) | copy-start | bytes 786436
  81.3 12.3 %all-to-all-start.2 = ((bf16[8,2,16,512]{3,2,1,0:T(8,128)(2,1)}), bf16[8,2,16,512]{3,2,1,0:T(8,128)(2,1)}, u32[]{:S(2)}, u32[]{:S(2)}) async-start(bf16[8,2,16,512]{3,2,1,0:T(8,128)(2,1)} %bitcast.88), calls=%async_computation.2 | async-start | bytes 524288 | tf_op jit(solution)/shard_map/all_to_all | solution.py:35
  85.4 0.5 copy-start.10
  101.9 10.7 %all-to-all-start.3 = ((bf16[8,16,512]{2,1,0:T(8,128)(2,1)}), bf16[8,16,512]{2,1,0:T(8,128)(2,1)S(1)}, u32[]{:S(2)}, u32[]{:S(2)}) async-start(bf16[8,16,512]{2,1,0:T(8,128)(2,1)} %multiply_convert_fusion), calls=%async_computation.3 | async-start | bytes 262144 | tf_op jit(solution)/shard_map/all_to_all | solution.py:40

commit v2 on v1

--- a/solution.py
+++ b/solution.py
@@ -1,6 +1,8 @@
 import jax
 import jax.numpy as jnp
 from jax import lax
+from jax.experimental import pallas as pl
+from jax.experimental.pallas import tpu as pltpu
 from jax.sharding import PartitionSpec as P
 
 QDOWN = 4
@@ -61,7 +63,7 @@
     return total
 
 
-def on_device(amplitudes, widths, holders, left_env, right_env):
+def on_device_any(amplitudes, widths, holders, left_env, right_env):
     slots_dev, right_dim, half_width = amplitudes.shape
     assert slots_dev == 1
     n_slots = holders.shape[0]
@@ -107,6 +109,280 @@
     return first[None], second[None]
 
 
+LANES = 128
+PIECES = 2
+
+
+def find_slot(holders, sector):
+    slot = jnp.int32(0)
+    for s in range(holders.shape[0]):
+        slot = slot + jnp.where(holders[s] == sector, s, 0)
+    return slot
+
+
+def live_columns(widths, holders, half, side):
+    width = widths[holders[lax.axis_index("sec")]]
+    columns = side * half + lax.broadcasted_iota(jnp.int32, (1, half), 1)
+    return columns < width
+
+
+def start_copies(left, left_vmem, sems):
+    copies = []
+    for term in (1, 2, 0):
+        copy = pltpu.make_async_copy(left.at[0, term], left_vmem.at[term], sems.at[term])
+        copy.start()
+        copies.append((term, copy))
+    return copies
+
+
+def apply_term(right, left_vmem, vector, term):
+    products = jnp.dot(right[term], vector, preferred_element_type=jnp.float32)
+    return jnp.dot(
+        products.astype(jnp.bfloat16), left_vmem[term], preferred_element_type=jnp.float32
+    )
+
+
+def store_pieces(pieces, block):
+    width = block.shape[1] // len(pieces)
+    for i, piece in enumerate(pieces):
+        piece[...] = block[:, i * width : (i + 1) * width].astype(piece.dtype)
+
+
+def write_turns(widths, holders, half, turns):
+    me = lax.axis_index("sec")
+    sector = holders[me]
+    down = sector % QDOWN
+    inner = (down == 1) | (down == 2)
+    group = sector - down
+    plan = (
+        (sector ^ QDOWN, sector & (QDOWN - 1), sector | QDOWN, True),
+        (sector ^ 1, sector - sector % 2, sector | 1, True),
+        (sector ^ 3, group + 1, group + 2, inner),
+    )
+    for step, (partner, sender, target, used) in enumerate(plan):
+        offset = me ^ find_slot(holders, partner)
+        backward = jnp.where(find_slot(holders, sender) > find_slot(holders, target), 1, 0)
+        columns = widths[target] - lax.axis_index("env") * half
+        count = jnp.int32(0)
+        for i in range(PIECES):
+            count = count + jnp.where(columns > i * (half // PIECES), 1, 0)
+        count = jnp.where(used, count, 0)
+        kind = jnp.where(count > 0, backward * PIECES + count, 0)
+        turns[step][0] = jnp.where(kind > 0, (offset - 1) * 2 * PIECES + kind, 0)
+        turns[step + 3][0] = (offset - 1) * (2 * PIECES + 1) + kind
+
+
+def first_kernel(widths, holders, amps, right, left, *rest):
+    half = amps.shape[2]
+    pieces_1, pieces_2 = rest[:PIECES], rest[PIECES : 2 * PIECES]
+    stay, *turns, left_vmem, sems = rest[2 * PIECES :]
+    copies = start_copies(left, left_vmem, sems)
+    write_turns(widths, holders, half, turns)
+    vector = jnp.concatenate(
+        [
+            jnp.where(live_columns(widths, holders, half, h), amps[h], jnp.zeros_like(amps[h]))
+            for h in range(2)
+        ],
+        axis=1,
+    )
+    for term, copy in copies:
+        copy.wait()
+        block = apply_term(right, left_vmem, vector, term)
+        store_pieces(((stay,), pieces_1, pieces_2)[term], block)
+
+
+def incoming(holders, arrived_1, arrived_2, arrived_3):
+    sector = holders[lax.axis_index("sec")]
+    down = sector % QDOWN
+    block_1, block_2, block_3 = (
+        jnp.concatenate([piece[...] for piece in pieces], axis=1).astype(jnp.float32)
+        for pieces in (arrived_1, arrived_2, arrived_3)
+    )
+    block_1 = jnp.where(sector >= QDOWN, block_1, 0.0)
+    block_2 = jnp.where(down % 2 == 1, block_2, jnp.where(down == 2, block_3, 0.0))
+    return block_1, block_2
+
+
+def thirds(refs):
+    return refs[:PIECES], refs[PIECES : 2 * PIECES], refs[2 * PIECES :]
+
+
+def sum_kernel(widths, holders, stay, *rest):
+    *arrived, first = rest
+    live = live_columns(widths, holders, stay.shape[1], lax.axis_index("env"))
+    block_1, block_2 = incoming(holders, *thirds(arrived))
+    total = stay[...].astype(jnp.float32) + block_1 + block_2
+    first[...] = jnp.where(live, total, 0.0).astype(jnp.bfloat16)
+
+
+def total_of(array):
+    return jnp.sum(jnp.sum(array, axis=0, keepdims=True), axis=1, keepdims=True)
+
+
+def second_kernel(widths, holders, amps, first, right, left, *outs):
+    half = amps.shape[2]
+    pieces_1, pieces_2 = outs[:PIECES], outs[PIECES : 2 * PIECES]
+    stay, tag, left_vmem, sems = outs[2 * PIECES :]
+    copies = start_copies(left, left_vmem, sems)
+    sector = holders[lax.axis_index("sec")]
+    basis = [
+        jnp.where(
+            live_columns(widths, holders, half, h), amps[h].astype(jnp.float32), 0.0
+        )
+        for h in range(2)
+    ]
+    firsts = [first[h].astype(jnp.float32) for h in range(2)]
+    overlap = total_of(basis[0] * firsts[0]) + total_of(basis[1] * firsts[1])
+    norm = total_of(basis[0] * basis[0]) + total_of(basis[1] * basis[1])
+    quotient = jnp.where(norm > 0, overlap / jnp.where(norm > 0, norm, 1.0), 0.0)
+    deflated = [firsts[h] - quotient * basis[h] for h in range(2)]
+    rest = total_of(deflated[0] * deflated[0]) + total_of(deflated[1] * deflated[1])
+    vector = jnp.concatenate(deflated, axis=1).astype(jnp.bfloat16)
+
+    row = lax.broadcasted_iota(jnp.int32, tag.shape, 0)
+    lane = lax.broadcasted_iota(jnp.int32, tag.shape, 1)
+    values = jnp.zeros(tag.shape, jnp.float32)
+    for place, value in enumerate((overlap, norm, quotient, rest)):
+        values = jnp.where(row == place, value, values)
+    tag[...] = jnp.where(lane == sector, values, 0.0)
+
+    for term, copy in copies:
+        copy.wait()
+        block = apply_term(right, left_vmem, vector, term)
+        store_pieces(((stay,), pieces_1, pieces_2)[term], block)
+
+
+def final_kernel(widths, holders, tag, stay, stay_2, *rest):
+    rows, half = stay.shape
+    *arrived, second = rest
+    old, new = arrived[: 3 * PIECES], arrived[3 * PIECES :]
+    slots = holders.shape[0]
+    sector = holders[lax.axis_index("sec")]
+    live = live_columns(widths, holders, half, lax.axis_index("env"))
+    total = jnp.int32(0)
+    for s in range(slots):
+        total = total + widths[s]
+    live_count = rows * total.astype(jnp.float32)
+    overlaps, norms, quotients, rests = (tag[i : i + 1, :] for i in range(4))
+    quotient = total_of(overlaps) / total_of(norms)
+    lane = lax.broadcasted_iota(jnp.int32, (1, LANES), 1)
+    shifts = jnp.where(lane < slots, quotients - quotient, 0.0)
+    resid_norm = total_of(rests + shifts * shifts * norms)
+    scale = lax.rsqrt(resid_norm / live_count + 1e-06)
+
+    def shift_of(source):
+        return total_of(jnp.where(lane == source, shifts, 0.0))
+
+    old_1, old_2 = incoming(holders, *thirds(old))
+    new_1, new_2 = incoming(holders, *thirds(new))
+    result = stay_2[...] + shift_of(sector) * stay[...].astype(jnp.float32)
+    result = result + new_1 + shift_of(sector - QDOWN) * old_1
+    result = result + new_2 + shift_of(sector - 1) * old_2
+    second[...] = jnp.where(live, scale * result, 0.0).astype(jnp.bfloat16)
+
+
+SMEM = pl.BlockSpec(memory_space=pltpu.SMEM)
+VMEM = pl.BlockSpec(memory_space=pltpu.VMEM)
+ANY = pl.BlockSpec(memory_space=pl.ANY)
+
+
+def choose(index, branches, *operands):
+    jaxprs = tuple(jax.make_jaxpr(branch)(*operands) for branch in branches)
+    return lax.cond_p.bind(index.reshape(()), *operands, branches=jaxprs)
+
+
+def send(pieces, offset, backward, count, n_slots):
+    pairs = [(i, i ^ offset) for i in range(n_slots) if (i > i ^ offset) == bool(backward)]
+    sent = [lax.ppermute(piece, "sec", pairs) for piece in pieces[:count]]
+    return sent + [jnp.zeros_like(piece) for piece in pieces[count:]]
+
+
+def exchange(turn, pieces, n_slots):
+    branches = [lambda *sent: [jnp.zeros_like(piece) for piece in sent]]
+    for offset in range(1, n_slots):
+        for backward in range(2):
+            for count in range(1, PIECES + 1):
+                branches.append(
+                    lambda *sent, o=offset, b=backward, c=count: send(sent, o, b, c, n_slots)
+                )
+    return choose(turn, branches, *pieces)
+
+
+def exchange_tagged(turn, tag, pieces, n_slots):
+    def swapped(tag, offset):
+        return tag + lax.ppermute(tag, "sec", [(i, i ^ offset) for i in range(n_slots)])
+
+    branches = []
+    for offset in range(1, n_slots):
+        for backward, count in [(0, 0)] + [
+            (b, c) for b in range(2) for c in range(1, PIECES + 1)
+        ]:
+            branches.append(
+                lambda tag, *sent, o=offset, b=backward, c=count: [swapped(tag, o)]
+                + send(sent, o, b, c, n_slots)
+            )
+    tag, *arrived = choose(turn, branches, tag, *pieces)
+    return tag, arrived
+
+
+def on_device(amplitudes, widths, holders, left_env, right_env):
+    slots_dev, right_dim, half = amplitudes.shape
+    n_slots = holders.shape[0]
+    assert slots_dev == 1
+    if n_slots != 2 * QDOWN:
+        return on_device_any(amplitudes, widths, holders, left_env, right_env)
+    piece = jax.ShapeDtypeStruct((right_dim, half // PIECES), jnp.bfloat16)
+    block = jax.ShapeDtypeStruct((right_dim, half), jnp.bfloat16)
+    wide = jax.ShapeDtypeStruct((right_dim, half), jnp.float32)
+    tag_shape = jax.ShapeDtypeStruct((8, LANES), jnp.float32)
+    turn = jax.ShapeDtypeStruct((1,), jnp.int32)
+    left_scratch = [
+        pltpu.VMEM(left_env.shape[1:], jnp.bfloat16),
+        pltpu.SemaphoreType.DMA((left_env.shape[1],)),
+    ]
+
+    amps_full = lax.all_gather(amplitudes[0], "env")
+    *pieces, stay, turn_1, turn_2, turn_3, turn_4, turn_5, turn_6 = pl.pallas_call(
+        first_kernel,
+        out_shape=(piece,) * (2 * PIECES) + (block,) + (turn,) * 6,
+        in_specs=[SMEM, SMEM, VMEM, VMEM, ANY],
+        out_specs=(VMEM,) * (2 * PIECES + 1) + (SMEM,) * 6,
+        scratch_shapes=left_scratch,
+    )(widths, holders, amps_full, right_env, left_env)
+    pieces_1, pieces_2 = pieces[:PIECES], pieces[PIECES:]
+    old = [
+        *exchange(turn_1, pieces_1, n_slots),
+        *exchange(turn_2, pieces_2, n_slots),
+        *exchange(turn_3, pieces_2, n_slots),
+    ]
+    first = pl.pallas_call(
+        sum_kernel,
+        out_shape=block,
+        in_specs=[SMEM, SMEM] + [VMEM] * (1 + 3 * PIECES),
+        out_specs=VMEM,
+    )(widths, holders, stay, *old)
+
+    first_full = lax.all_gather(first, "env")
+    *pieces, stay_2, tag = pl.pallas_call(
+        second_kernel,
+        out_shape=(piece,) * (2 * PIECES) + (wide, tag_shape),
+        in_specs=[SMEM, SMEM, VMEM, VMEM, VMEM, ANY],
+        out_specs=(VMEM,) * (2 * PIECES + 2),
+        scratch_shapes=left_scratch,
+    )(widths, holders, amps_full, first_full, right_env, left_env)
+    pieces_1, pieces_2 = pieces[:PIECES], pieces[PIECES:]
+    tag, new_1 = exchange_tagged(turn_4, tag, pieces_1, n_slots)
+    tag, new_2 = exchange_tagged(turn_5, tag, pieces_2, n_slots)
+    tag, new_3 = exchange_tagged(turn_6, tag, pieces_2, n_slots)
+    second = pl.pallas_call(
+        final_kernel,
+        out_shape=block,
+        in_specs=[SMEM, SMEM] + [VMEM] * (3 + 6 * PIECES),
+        out_specs=VMEM,
+    )(widths, holders, tag, stay, stay_2, *old, *new_1, *new_2, *new_3)
+    return first[None], second[None]
+
+
 def solution(mesh):
     in_specs = (
         P(("runs", "sec"), None, "env"),

time: 121 us -> 83.4 us (0.69)
  the two profiles are of different devices: /device:TPU:0 before, /device:TPU:4 now
where the time goes in v2:
time: 83.4 us; the launch traced here: 81.9 us
  starting transfers between devices  36.9 us (44%)
  waiting for transfers between devices  19 us (23%)
  Pallas kernels  12.5 us (15%)
  blocking collectives  7.21 us (9%)
  loops' own time  4.19 us (5%)
  other arithmetic  1.37 us (2%)
    ppermute x12, starting transfers between devices, send(): sent = [lax.ppermute(piece, 'sec', pairs) for piece in pieces[:count]]  32.2 us
    ppermute x3, waiting for transfers between devices, swapped(): lax.ppermute(tag, 'sec', [(i, i ^ offset) for i in range(n_slots)])  9.97 us
    ppermute x12, waiting for transfers between devices, send(): sent = [lax.ppermute(piece, 'sec', pairs) for piece in pieces[:count]]  9.03 us
    ppermute x3, starting transfers between devices, swapped(): lax.ppermute(tag, 'sec', [(i, i ^ offset) for i in range(n_slots)])  4.76 us
    pallas_call x1, Pallas kernels, on_device(): pl.pallas_call(second_kernel, out_shape=(piece,) * (2 * PIECES) + (wide,...  4.28 us
    another operation x6, loops' own time, choose(): return lax.cond_p.bind(index.reshape(()), *operands, branches=jaxprs)  4.19 us
    pallas_call x1, Pallas kernels, on_device(): pl.pallas_call(first_kernel, out_shape=(piece,) * (2 * PIECES) + (block,)...  4.16 us
    all_gather x1, blocking collectives, on_device(): first_full = lax.all_gather(first, 'env')  3.72 us
  transfers between devices with their start and end apart: 15, of which 7 were waited for; matrix products, arithmetic and copies ran while one was open for 0% of the time, Pallas kernels for 0%

profile of v2, /device:TPU:4, one launch (start us, length us, event | category | flops | bytes accessed | tf_op | source)
XLA Modules:
  0.0 81.9 jit_solution(13839365491886676733)
XLA Ops:
  0.6 3.5 %all_gather.7.amps = bf16[2,128,512]{2,1,0:T(8,128)(2,1)} all-gather(bf16[1,128,512]{2,1,0:T(8,128)(2,1)} %param.197), channel_id=1, replica_groups=mesh['runs'=2,'sec'=8,'env'=2] {'env'}, dimensions={0}, use_global_device_ids=true | all-gather | bytes 393216 | tf_op jit(solution)/shard_map/all_gather | solution.py:344
  4.1 4.2 %shard_map.68 = (bf16[128,256]{1,0:T(8,128)(2,1)S(1)}, bf16[128,256]{1,0:T(8,128)(2,1)S(1)}, bf16[128,256]{1,0:T(8,128)(2,1)S(1)}, bf16[128,256]{1,0:T(8,128)(2,...) custom-call(s32[8]{0:T(128)} %widths.7, ...), custom_call_target="tpu_custom_call" | custom-call | tf_op jit(solution)/shard_map/pallas_call | solution.py:345
  8.3 8.9 %conditional.6 = (bf16[128,256]{1,0:T(8,128)(2,1)}, bf16[128,256]{1,0:T(8,128)(2,1)}) conditional(s32[]{:T(128)} %bitcast, () %tuple.916, bf16[128,256]{1,0:T(8,128)(2,1)S(1)} %get-tuple-element.985, (bf16[128,256]{1,0:T(8,128)(2,1)S(1)}, bf16[128,256]{1,0:T(8,128)(2,1)S(1)}) %tuple.917, ...), branch_computations={%region_0.0_spmd, %region_1.0_spmd, %region_2.0_spmd, %region_3.0_... | conditional | bytes 524384 | solution.py:291
  9.0 5.0 %collective-permute-start.13 = (bf16[128,256]{1,0:T(8,128)(2,1)S(1)}, bf16[128,256]{1,0:T(8,128)(2,1)}, u32[]{:S(2)}, u32[]{:S(2)}) collective-permute-start(bf16[128,256]{1,0:T(8,128)(2,1)S(1)} %get-tuple-element.661), channel_id=1, source_target_pairs={{0,6},{2,4},{8,14},{10,12},{1,7},{3,5},{9,15},{11,13},{16,22},{18,... | collective-permute-start | bytes 196616 | tf_op jit(solution)/shard_map/cond/branch_10_fun/ppermute | solution.py:296
  14.0 1.9 %collective-permute-start.14 = (bf16[128,256]{1,0:T(8,128)(2,1)S(1)}, bf16[128,256]{1,0:T(8,128)(2,1)}, u32[]{:S(2)}, u32[]{:S(2)}) collective-permute-start(bf16[128,256]{1,0:T(8,128)(2,1)S(1)} %get-tuple-element.662), channel_id=1, source_target_pairs={{0,6},{2,4},{8,14},{10,12},{1,7},{3,5},{9,15},{11,13},{16,22},{18,... | collective-permute-start | bytes 196616 | tf_op jit(solution)/shard_map/cond/branch_10_fun/ppermute | solution.py:296
  15.9 1.3 %collective-permute-done.14 = bf16[128,256]{1,0:T(8,128)(2,1)} collective-permute-done((bf16[128,256]{1,0:T(8,128)(2,1)S(1)}, bf16[128,256]{1,0:T(8,128)(2,1)}, u32[]{:S(2)}, u32[]{:S(2)}) %collective-permute-start.14) | collective-permute-done | bytes 65568 | tf_op jit(solution)/shard_map/cond/branch_10_fun/ppermute | solution.py:296
  17.2 8.0 %conditional.8 = (bf16[128,256]{1,0:T(8,128)(2,1)}, bf16[128,256]{1,0:T(8,128)(2,1)}) conditional(s32[]{:T(128)} %bitcast.2, () %tuple.920, bf16[128,256]{1,0:T(8,128)(2,1)S(1)} %get-tuple-element.990, (bf16[128,256]{1,0:T(8,128)(2,1)S(1)}, bf16[128,256]{1,0:T(8,128)(2,1)S(1)}) %tuple.919, ...), branch_computations={%region_58.0_spmd, %region_59.0_spmd, %region_60.0_spmd, %region_6... | conditional | bytes 524384 | solution.py:291
  17.9 4.1 %collective-permute-start.85 = (bf16[128,256]{1,0:T(8,128)(2,1)S(1)}, bf16[128,256]{1,0:T(8,128)(2,1)}, u32[]{:S(2)}, u32[]{:S(2)}) collective-permute-start(bf16[128,256]{1,0:T(8,128)(2,1)S(1)} %get-tuple-element.709), channel_id=1, source_target_pairs={{0,2},{4,6},{8,10},{12,14},{1,3},{5,7},{9,11},{13,15},{16,18},{20,... | collective-permute-start | bytes 196616 | tf_op jit(solution)/shard_map/cond/branch_2_fun/ppermute | solution.py:296
  22.0 1.9 %collective-permute-start.86 = (bf16[128,256]{1,0:T(8,128)(2,1)S(1)}, bf16[128,256]{1,0:T(8,128)(2,1)}, u32[]{:S(2)}, u32[]{:S(2)}) collective-permute-start(bf16[128,256]{1,0:T(8,128)(2,1)S(1)} %get-tuple-element.710), channel_id=1, source_target_pairs={{0,2},{4,6},{8,10},{12,14},{1,3},{5,7},{9,11},{13,15},{16,18},{20,... | collective-permute-start | bytes 196616 | tf_op jit(solution)/shard_map/cond/branch_2_fun/ppermute | solution.py:296
  24.0 1.3 %collective-permute-done.86 = bf16[128,256]{1,0:T(8,128)(2,1)} collective-permute-done((bf16[128,256]{1,0:T(8,128)(2,1)S(1)}, bf16[128,256]{1,0:T(8,128)(2,1)}, u32[]{:S(2)}, u32[]{:S(2)}) %collective-permute-start.86) | collective-permute-done | bytes 65568 | tf_op jit(solution)/shard_map/cond/branch_2_fun/ppermute | solution.py:296
  25.2 9.8 %conditional.7 = (bf16[128,256]{1,0:T(8,128)(2,1)}, bf16[128,256]{1,0:T(8,128)(2,1)}) conditional(s32[]{:T(128)} %bitcast.1, () %tuple.918, bf16[128,256]{1,0:T(8,128)(2,1)S(1)} %get-tuple-element.990, (bf16[128,256]{1,0:T(8,128)(2,1)S(1)}, bf16[128,256]{1,0:T(8,128)(2,1)S(1)}) %tuple.919, ...), branch_computations={%region_29.0_spmd, %region_30.0_spmd, %region_31.0_spmd, %region_3... | conditional | bytes 524384 | solution.py:291
  25.9 1.3 %collective-permute-start.64 = (bf16[128,256]{1,0:T(8,128)(2,1)S(1)}, bf16[128,256]{1,0:T(8,128)(2,1)}, u32[]{:S(2)}, u32[]{:S(2)}) collective-permute-start(bf16[128,256]{1,0:T(8,128)(2,1)S(1)} %get-tuple-element.695), channel_id=1, source_target_pairs={{8,0},{10,2},{12,4},{14,6},{9,1},{11,3},{13,5},{15,7},{24,16},{26,... | collective-permute-start | bytes 196616 | tf_op jit(solution)/shard_map/cond/branch_16_fun/ppermute | solution.py:296
  27.2 1.3 %collective-permute-start.65 = (bf16[128,256]{1,0:T(8,128)(2,1)S(1)}, bf16[128,256]{1,0:T(8,128)(2,1)}, u32[]{:S(2)}, u32[]{:S(2)}) collective-permute-start(bf16[128,256]{1,0:T(8,128)(2,1)S(1)} %get-tuple-element.696), channel_id=1, source_target_pairs={{8,0},{10,2},{12,4},{14,6},{9,1},{11,3},{13,5},{15,7},{24,16},{26,... | collective-permute-start | bytes 196616 | tf_op jit(solution)/shard_map/cond/branch_16_fun/ppermute | solution.py:296
  28.5 4.6 %collective-permute-done.64 = bf16[128,256]{1,0:T(8,128)(2,1)} collective-permute-done((bf16[128,256]{1,0:T(8,128)(2,1)S(1)}, bf16[128,256]{1,0:T(8,128)(2,1)}, u32[]{:S(2)}, u32[]{:S(2)}) %collective-permute-start.64) | collective-permute-done | bytes 65568 | tf_op jit(solution)/shard_map/cond/branch_16_fun/ppermute | solution.py:296
  33.1 1.9 %collective-permute-done.65 = bf16[128,256]{1,0:T(8,128)(2,1)} collective-permute-done((bf16[128,256]{1,0:T(8,128)(2,1)S(1)}, bf16[128,256]{1,0:T(8,128)(2,1)}, u32[]{:S(2)}, u32[]{:S(2)}) %collective-permute-start.65) | collective-permute-done | bytes 65568 | tf_op jit(solution)/shard_map/cond/branch_16_fun/ppermute | solution.py:296
  35.0 1.8 %shard_map.69 = bf16[128,512]{1,0:T(8,128)(2,1)} custom-call(s32[8]{0:T(128)} %widths.7, s32[8]{0:T(128)} %holders.7, bf16[128,512]{1,0:T(8,128)(2,1)} %get-tuple-element.983.stay, bf16[128,256]{1,0:T(8,128)(2,1)} %get-tuple-element.987.rest_0_, bf16[128,256]{1,0:T(8,128)(2,1)} %get-tuple-element.988.rest_1_, bf16[128,256]{1,0:T(8,128)(2,1)} %get-tuple-element.992.rest_2_, ...), custom_call_target="tpu_custom_call" | custom-call | tf_op jit(solution)/shard_map/pallas_call | solution.py:358
  36.8 3.7 %all-gather = bf16[256,512]{1,0:T(8,128)(2,1)} all-gather(bf16[128,512]{1,0:T(8,128)(2,1)} %shard_map.69), channel_id=2, replica_groups=mesh['runs'=2,'sec'=8,'env'=2] {'env'}, dimensions={0}, use_global_device_ids=true | all-gather | bytes 393216 | tf_op jit(solution)/shard_map/all_gather | solution.py:365
  40.5 4.3 %shard_map.70 = (bf16[128,256]{1,0:T(8,128)(2,1)S(1)}, bf16[128,256]{1,0:T(8,128)(2,1)S(1)}, bf16[128,256]{1,0:T(8,128)(2,1)S(1)}, bf16[128,256]{1,0:T(8,128)(2,...) custom-call(s32[8]{0:T(128)} %widths.7, s32[8]{0:T(128)} %holders.7, bf16[2,128,512]{2,1,0:T(8,128)(2,1)} %all_gather.7.amps, ...), custom_call_target="tpu_custom_call" | custom-call | tf_op jit(solution)/shard_map/pallas_call | solution.py:366
  44.8 13.1 %conditional.9 = (bf16[128,256]{1,0:T(8,128)(2,1)}, bf16[128,256]{1,0:T(8,128)(2,1)}, f32[8,128]{1,0:T(8,128)S(1)}, f32[8,128]{1,0:T(8,128)}) conditional(s32[]{:T(128)} %bitcast.6, f32[8,128]{1,0:T(8,128)S(1)} %get-tuple-element.1000, (f32[8,128]{1,0:T(8,128)S(1)}, bf16[128,256]{1,0:T(8,128)(2,1)S(1)}) %tuple.921, ...), branch_computations={%region_87.0_spmd, %region_88.0_spmd, %region_89.0_spmd, %region_9... | conditional | bytes 540824 | solution.py:291
  45.5 5.9 %collective-permute-start.152 = (bf16[128,256]{1,0:T(8,128)(2,1)S(1)}, bf16[128,256]{1,0:T(8,128)(2,1)}, u32[]{:S(2)}, u32[]{:S(2)}) collective-permute-start(bf16[128,256]{1,0:T(8,128)(2,1)S(1)} %get-tuple-element.760), channel_id=1, source_target_pairs={{0,6},{2,4},{8,14},{10,12},{1,7},{3,5},{9,15},{11,13},{16,22},{18,... | collective-permute-start | bytes 196616 | tf_op jit(solution)/shard_map/cond/branch_12_fun/ppermute | solution.py:296
  51.4 1.9 %collective-permute-start.153 = (bf16[128,256]{1,0:T(8,128)(2,1)S(1)}, bf16[128,256]{1,0:T(8,128)(2,1)}, u32[]{:S(2)}, u32[]{:S(2)}) collective-permute-start(bf16[128,256]{1,0:T(8,128)(2,1)S(1)} %get-tuple-element.761), channel_id=1, source_target_pairs={{0,6},{2,4},{8,14},{10,12},{1,7},{3,5},{9,15},{11,13},{16,22},{18,... | collective-permute-start | bytes 196616 | tf_op jit(solution)/shard_map/cond/branch_12_fun/ppermute | solution.py:296
  53.3 4.6 %collective-permute-done.151 = f32[8,128]{1,0:T(8,128)} collective-permute-done((f32[8,128]{1,0:T(8,128)S(1)}, f32[8,128]{1,0:T(8,128)}, u32[]{:S(2)}, u32[]{:S(2)}) %collective-permute-start.151) | collective-permute-done | bytes 4128 | tf_op jit(solution)/shard_map/cond/branch_12_fun/ppermute | solution.py:313
  58.6 9.8 %conditional.10 = (bf16[128,256]{1,0:T(8,128)(2,1)}, bf16[128,256]{1,0:T(8,128)(2,1)}, f32[8,128]{1,0:T(8,128)S(1)}, f32[8,128]{1,0:T(8,128)}) conditional(s32[]{:T(128)} %bitcast.5, f32[8,128]{1,0:T(8,128)S(1)} %add.315, (f32[8,128]{1,0:T(8,128)S(1)}, bf16[128,256]{1,0:T(8,128)(2,1)S(1)}) %tuple.923, ...), branch_computations={%region_122.0_spmd, %region_123.0_spmd, %region_124.0_spmd, %regio... | conditional | bytes 540824 | solution.py:291
  59.3 1.3 %collective-permute-start.245 = (bf16[128,256]{1,0:T(8,128)(2,1)S(1)}, bf16[128,256]{1,0:T(8,128)(2,1)}, u32[]{:S(2)}, u32[]{:S(2)}) collective-permute-start(bf16[128,256]{1,0:T(8,128)(2,1)S(1)} %get-tuple-element.845), channel_id=1, source_target_pairs={{8,0},{10,2},{12,4},{14,6},{9,1},{11,3},{13,5},{15,7},{24,16},{26,... | collective-permute-start | bytes 196616 | tf_op jit(solution)/shard_map/cond/branch_19_fun/ppermute | solution.py:296
  60.6 1.3 %collective-permute-start.246 = (bf16[128,256]{1,0:T(8,128)(2,1)S(1)}, bf16[128,256]{1,0:T(8,128)(2,1)}, u32[]{:S(2)}, u32[]{:S(2)}) collective-permute-start(bf16[128,256]{1,0:T(8,128)(2,1)S(1)} %get-tuple-element.846), channel_id=1, source_target_pairs={{8,0},{10,2},{12,4},{14,6},{9,1},{11,3},{13,5},{15,7},{24,16},{26,... | collective-permute-start | bytes 196616 | tf_op jit(solution)/shard_map/cond/branch_19_fun/ppermute | solution.py:296
  61.9 4.8 %collective-permute-start.244 = (f32[8,128]{1,0:T(8,128)S(1)}, f32[8,128]{1,0:T(8,128)}, u32[]{:S(2)}, u32[]{:S(2)}) collective-permute-start(f32[8,128]{1,0:T(8,128)S(1)} %get-tuple-element.1417), channel_id=1, source_target_pairs={{0,8},{2,10},{4,12},{6,14},{8,0},{10,2},{12,4},{14,6},{1,9},{3,11}... | collective-permute-start | bytes 12296 | tf_op jit(solution)/shard_map/cond/branch_19_fun/ppermute | solution.py:313
  66.7 1.8 %collective-permute-done.244 = f32[8,128]{1,0:T(8,128)} collective-permute-done((f32[8,128]{1,0:T(8,128)S(1)}, f32[8,128]{1,0:T(8,128)}, u32[]{:S(2)}, u32[]{:S(2)}) %collective-permute-start.244) | collective-permute-done | bytes 4128 | tf_op jit(solution)/shard_map/cond/branch_19_fun/ppermute | solution.py:313
  69.1 10.5 %conditional.11 = (f32[8,128]{1,0:T(8,128)S(1)}, bf16[128,256]{1,0:T(8,128)(2,1)}, bf16[128,256]{1,0:T(8,128)(2,1)}) conditional(s32[]{:T(128)} %bitcast.4, f32[8,128]{1,0:T(8,128)S(1)} %add.316, (f32[8,128]{1,0:T(8,128)S(1)}, bf16[128,256]{1,0:T(8,128)(2,1)S(1)}) %tuple.925, (f32[8,128]{1,0:T(8,128)S(1)}, ...), branch_computations={%region_157.0_spmd, %region_158.0_spmd, %region_159.0_spmd, %regio... | conditional | flops 1024 | bytes 553104 | solution.py:291
  69.8 4.3 %collective-permute-start.284 = (bf16[128,256]{1,0:T(8,128)(2,1)S(1)}, bf16[128,256]{1,0:T(8,128)(2,1)}, u32[]{:S(2)}, u32[]{:S(2)}) collective-permute-start(bf16[128,256]{1,0:T(8,128)(2,1)S(1)} %get-tuple-element.880), channel_id=1, source_target_pairs={{0,2},{4,6},{8,10},{12,14},{1,3},{5,7},{9,11},{13,15},{16,18},{20,... | collective-permute-start | bytes 196616 | tf_op jit(solution)/shard_map/cond/branch_2_fun/ppermute | solution.py:296
  74.1 1.9 %collective-permute-start.285 = (bf16[128,256]{1,0:T(8,128)(2,1)S(1)}, bf16[128,256]{1,0:T(8,128)(2,1)}, u32[]{:S(2)}, u32[]{:S(2)}) collective-permute-start(bf16[128,256]{1,0:T(8,128)(2,1)S(1)} %get-tuple-element.881), channel_id=1, source_target_pairs={{0,2},{4,6},{8,10},{12,14},{1,3},{5,7},{9,11},{13,15},{16,18},{20,... | collective-permute-start | bytes 196616 | tf_op jit(solution)/shard_map/cond/branch_2_fun/ppermute | solution.py:296
  76.0 3.6 %collective-permute-done.283 = f32[8,128]{1,0:T(8,128)S(1)} collective-permute-done((f32[8,128]{1,0:T(8,128)S(1)}, f32[8,128]{1,0:T(8,128)S(1)}, u32[]{:S(2)}, u32[]{:S(2)}) %collective-permute-start.283) | collective-permute-done | bytes 4128 | tf_op jit(solution)/shard_map/cond/branch_2_fun/ppermute | solution.py:313
  79.6 2.3 %shard_map.71 = bf16[128,512]{1,0:T(8,128)(2,1)} custom-call(s32[8]{0:T(128)} %widths.7, s32[8]{0:T(128)} %holders.7, f32[8,128]{1,0:T(8,128)S(1)} %get-tuple-element.1009.tag, bf16[128,512]{1,0:T(8,128)(2,1)} %get-tuple-element.983.stay, f32[128,512]{1,0:T(8,128)} %get-tuple-element.1010.stay_2, bf16[128,256]{1,0:T(8,128)(2,1)} %get-tuple-element.987.rest_0_, ...), custom_call_target="tpu_custom_call" | custom-call | tf_op jit(solution)/shard_map/pallas_call | solution.py:377
  (13 shorter events, 1.4 us)
Async XLA Ops:
  9.0 6.9 %collective-permute-start.13 = (bf16[128,256]{1,0:T(8,128)(2,1)S(1)}, bf16[128,256]{1,0:T(8,128)(2,1)}, u32[]{:S(2)}, u32[]{:S(2)}) collective-permute-start(bf16[128,256]{1,0:T(8,128)(2,1)S(1)} %get-tuple-element.661), channel_id=1, source_target_pairs={{0,6},{2,4},{8,14},{10,12},{1,7},{3,5},{9,15},{11,13},{16,22},{18,... | collective-permute-start | bytes 196616 | tf_op jit(solution)/shard_map/cond/branch_10_fun/ppermute | solution.py:296
  14.0 3.2 %collective-permute-start.14 = (bf16[128,256]{1,0:T(8,128)(2,1)S(1)}, bf16[128,256]{1,0:T(8,128)(2,1)}, u32[]{:S(2)}, u32[]{:S(2)}) collective-permute-start(bf16[128,256]{1,0:T(8,128)(2,1)S(1)} %get-tuple-element.662), channel_id=1, source_target_pairs={{0,6},{2,4},{8,14},{10,12},{1,7},{3,5},{9,15},{11,13},{16,22},{18,... | collective-permute-start | bytes 196616 | tf_op jit(solution)/shard_map/cond/branch_10_fun/ppermute | solution.py:296
  17.9 6.0 %collective-permute-start.85 = (bf16[128,256]{1,0:T(8,128)(2,1)S(1)}, bf16[128,256]{1,0:T(8,128)(2,1)}, u32[]{:S(2)}, u32[]{:S(2)}) collective-permute-start(bf16[128,256]{1,0:T(8,128)(2,1)S(1)} %get-tuple-element.709), channel_id=1, source_target_pairs={{0,2},{4,6},{8,10},{12,14},{1,3},{5,7},{9,11},{13,15},{16,18},{20,... | collective-permute-start | bytes 196616 | tf_op jit(solution)/shard_map/cond/branch_2_fun/ppermute | solution.py:296
  22.0 3.2 %collective-permute-start.86 = (bf16[128,256]{1,0:T(8,128)(2,1)S(1)}, bf16[128,256]{1,0:T(8,128)(2,1)}, u32[]{:S(2)}, u32[]{:S(2)}) collective-permute-start(bf16[128,256]{1,0:T(8,128)(2,1)S(1)} %get-tuple-element.710), channel_id=1, source_target_pairs={{0,2},{4,6},{8,10},{12,14},{1,3},{5,7},{9,11},{13,15},{16,18},{20,... | collective-permute-start | bytes 196616 | tf_op jit(solution)/shard_map/cond/branch_2_fun/ppermute | solution.py:296
  25.9 7.2 %collective-permute-start.64 = (bf16[128,256]{1,0:T(8,128)(2,1)S(1)}, bf16[128,256]{1,0:T(8,128)(2,1)}, u32[]{:S(2)}, u32[]{:S(2)}) collective-permute-start(bf16[128,256]{1,0:T(8,128)(2,1)S(1)} %get-tuple-element.695), channel_id=1, source_target_pairs={{8,0},{10,2},{12,4},{14,6},{9,1},{11,3},{13,5},{15,7},{24,16},{26,... | collective-permute-start | bytes 196616 | tf_op jit(solution)/shard_map/cond/branch_16_fun/ppermute | solution.py:296
  27.2 7.8 %collective-permute-start.65 = (bf16[128,256]{1,0:T(8,128)(2,1)S(1)}, bf16[128,256]{1,0:T(8,128)(2,1)}, u32[]{:S(2)}, u32[]{:S(2)}) collective-permute-start(bf16[128,256]{1,0:T(8,128)(2,1)S(1)} %get-tuple-element.696), channel_id=1, source_target_pairs={{8,0},{10,2},{12,4},{14,6},{9,1},{11,3},{13,5},{15,7},{24,16},{26,... | collective-permute-start | bytes 196616 | tf_op jit(solution)/shard_map/cond/branch_16_fun/ppermute | solution.py:296
  45.5 12.4 %collective-permute-start.152 = (bf16[128,256]{1,0:T(8,128)(2,1)S(1)}, bf16[128,256]{1,0:T(8,128)(2,1)}, u32[]{:S(2)}, u32[]{:S(2)}) collective-permute-start(bf16[128,256]{1,0:T(8,128)(2,1)S(1)} %get-tuple-element.760), channel_id=1, source_target_pairs={{0,6},{2,4},{8,14},{10,12},{1,7},{3,5},{9,15},{11,13},{16,22},{18,... | collective-permute-start | bytes 196616 | tf_op jit(solution)/shard_map/cond/branch_12_fun/ppermute | solution.py:296
  51.4 6.5 %collective-permute-start.153 = (bf16[128,256]{1,0:T(8,128)(2,1)S(1)}, bf16[128,256]{1,0:T(8,128)(2,1)}, u32[]{:S(2)}, u32[]{:S(2)}) collective-permute-start(bf16[128,256]{1,0:T(8,128)(2,1)S(1)} %get-tuple-element.761), channel_id=1, source_target_pairs={{0,6},{2,4},{8,14},{10,12},{1,7},{3,5},{9,15},{11,13},{16,22},{18,... | collective-permute-start | bytes 196616 | tf_op jit(solution)/shard_map/cond/branch_12_fun/ppermute | solution.py:296
  53.3 4.6 %collective-permute-start.151 = (f32[8,128]{1,0:T(8,128)S(1)}, f32[8,128]{1,0:T(8,128)}, u32[]{:S(2)}, u32[]{:S(2)}) collective-permute-start(f32[8,128]{1,0:T(8,128)S(1)} %get-tuple-element.1249), channel_id=1, source_target_pairs={{0,6},{2,4},{4,2},{6,0},{8,14},{10,12},{12,10},{14,8},{1,7},{3,5},... | collective-permute-start | bytes 12296 | tf_op jit(solution)/shard_map/cond/branch_12_fun/ppermute | solution.py:313
  59.3 9.1 %collective-permute-start.245 = (bf16[128,256]{1,0:T(8,128)(2,1)S(1)}, bf16[128,256]{1,0:T(8,128)(2,1)}, u32[]{:S(2)}, u32[]{:S(2)}) collective-permute-start(bf16[128,256]{1,0:T(8,128)(2,1)S(1)} %get-tuple-element.845), channel_id=1, source_target_pairs={{8,0},{10,2},{12,4},{14,6},{9,1},{11,3},{13,5},{15,7},{24,16},{26,... | collective-permute-start | bytes 196616 | tf_op jit(solution)/shard_map/cond/branch_19_fun/ppermute | solution.py:296
  60.6 7.8 %collective-permute-start.246 = (bf16[128,256]{1,0:T(8,128)(2,1)S(1)}, bf16[128,256]{1,0:T(8,128)(2,1)}, u32[]{:S(2)}, u32[]{:S(2)}) collective-permute-start(bf16[128,256]{1,0:T(8,128)(2,1)S(1)} %get-tuple-element.846), channel_id=1, source_target_pairs={{8,0},{10,2},{12,4},{14,6},{9,1},{11,3},{13,5},{15,7},{24,16},{26,... | collective-permute-start | bytes 196616 | tf_op jit(solution)/shard_map/cond/branch_19_fun/ppermute | solution.py:296
  61.9 6.5 %collective-permute-start.244 = (f32[8,128]{1,0:T(8,128)S(1)}, f32[8,128]{1,0:T(8,128)}, u32[]{:S(2)}, u32[]{:S(2)}) collective-permute-start(f32[8,128]{1,0:T(8,128)S(1)} %get-tuple-element.1417), channel_id=1, source_target_pairs={{0,8},{2,10},{4,12},{6,14},{8,0},{10,2},{12,4},{14,6},{1,9},{3,11}... | collective-permute-start | bytes 12296 | tf_op jit(solution)/shard_map/cond/branch_19_fun/ppermute | solution.py:313
  69.8 9.8 %collective-permute-start.284 = (bf16[128,256]{1,0:T(8,128)(2,1)S(1)}, bf16[128,256]{1,0:T(8,128)(2,1)}, u32[]{:S(2)}, u32[]{:S(2)}) collective-permute-start(bf16[128,256]{1,0:T(8,128)(2,1)S(1)} %get-tuple-element.880), channel_id=1, source_target_pairs={{0,2},{4,6},{8,10},{12,14},{1,3},{5,7},{9,11},{13,15},{16,18},{20,... | collective-permute-start | bytes 196616 | tf_op jit(solution)/shard_map/cond/branch_2_fun/ppermute | solution.py:296
  74.1 5.5 %collective-permute-start.285 = (bf16[128,256]{1,0:T(8,128)(2,1)S(1)}, bf16[128,256]{1,0:T(8,128)(2,1)}, u32[]{:S(2)}, u32[]{:S(2)}) collective-permute-start(bf16[128,256]{1,0:T(8,128)(2,1)S(1)} %get-tuple-element.881), channel_id=1, source_target_pairs={{0,2},{4,6},{8,10},{12,14},{1,3},{5,7},{9,11},{13,15},{16,18},{20,... | collective-permute-start | bytes 196616 | tf_op jit(solution)/shard_map/cond/branch_2_fun/ppermute | solution.py:296
  76.0 3.6 %collective-permute-start.283 = (f32[8,128]{1,0:T(8,128)S(1)}, f32[8,128]{1,0:T(8,128)S(1)}, u32[]{:S(2)}, u32[]{:S(2)}) collective-permute-start(f32[8,128]{1,0:T(8,128)S(1)} %get-tuple-element.879), channel_id=1, source_target_pairs={{0,2},{2,0},{4,6},{6,4},{8,10},{10,8},{12,14},{14,12},{1,3},{3,1},... | collective-permute-start | bytes 12296 | tf_op jit(solution)/shard_map/cond/branch_2_fun/ppermute | solution.py:313

commit v3 on v1

--- a/solution.py
+++ b/solution.py
@@ -1,6 +1,8 @@
 import jax
 import jax.numpy as jnp
 from jax import lax
+from jax.experimental import pallas as pl
+from jax.experimental.pallas import tpu as pltpu
 from jax.sharding import PartitionSpec as P
 
 QDOWN = 4
@@ -61,7 +63,7 @@
     return total
 
 
-def on_device(amplitudes, widths, holders, left_env, right_env):
+def on_device_any(amplitudes, widths, holders, left_env, right_env):
     slots_dev, right_dim, half_width = amplitudes.shape
     assert slots_dev == 1
     n_slots = holders.shape[0]
@@ -107,6 +109,241 @@
     return first[None], second[None]
 
 
+LANES = 128
+TAG = 16
+
+
+def find_slot(holders, sector):
+    slot = jnp.int32(0)
+    for s in range(holders.shape[0]):
+        slot = slot + jnp.where(holders[s] == sector, s, 0)
+    return slot
+
+
+def live_columns(widths, holders, half, side):
+    width = widths[holders[lax.axis_index("sec")]]
+    columns = side * half + lax.broadcasted_iota(jnp.int32, (1, half), 1)
+    return columns < width
+
+
+def start_copies(left, left_vmem, sems):
+    copies = []
+    for term in (1, 2, 0):
+        copy = pltpu.make_async_copy(left.at[0, term], left_vmem.at[term], sems.at[term])
+        copy.start()
+        copies.append((term, copy))
+    return copies
+
+
+def apply_term(right, left_vmem, vector, term):
+    products = jnp.dot(right[term], vector, preferred_element_type=jnp.float32)
+    return jnp.dot(
+        products.astype(jnp.bfloat16), left_vmem[term], preferred_element_type=jnp.float32
+    )
+
+
+def first_kernel(widths, holders, amps, right, left, message, stay, left_vmem, sems):
+    rows, half = stay.shape
+    copies = start_copies(left, left_vmem, sems)
+    vector = jnp.concatenate(
+        [
+            jnp.where(live_columns(widths, holders, half, h), amps[h], jnp.zeros_like(amps[h]))
+            for h in range(2)
+        ],
+        axis=1,
+    )
+    for term, copy in copies:
+        copy.wait()
+        block = apply_term(right, left_vmem, vector, term).astype(jnp.bfloat16)
+        if term == 0:
+            stay[...] = block
+        else:
+            message[pl.ds((term - 1) * rows, rows), :] = block
+
+
+def fetch(holders, gathered, first_row, rows, blocks, sems):
+    sector = holders[lax.axis_index("sec")]
+    sources = (find_slot(holders, sector & (QDOWN - 1)), find_slot(holders, sector - 1))
+    copies = []
+    for i, source in enumerate(sources):
+        place = gathered.at[source, pl.ds(first_row + i * rows, rows)]
+        copy = pltpu.make_async_copy(place, blocks.at[i], sems.at[i])
+        copy.start()
+        copies.append(copy)
+    return copies
+
+
+def incoming(holders, blocks):
+    sector = holders[lax.axis_index("sec")]
+    has = (sector >= QDOWN, sector % QDOWN > 0)
+    return [jnp.where(has[i], blocks[i].astype(jnp.float32), 0.0) for i in range(2)]
+
+
+def sum_kernel(widths, holders, stay, gathered, first, old, sems):
+    rows, half = stay.shape
+    copies = fetch(holders, gathered, 0, rows, old, sems)
+    live = live_columns(widths, holders, half, lax.axis_index("env"))
+    for copy in copies:
+        copy.wait()
+    block_1, block_2 = incoming(holders, old)
+    total = stay[...].astype(jnp.float32) + block_1 + block_2
+    first[...] = jnp.where(live, total, 0.0).astype(jnp.bfloat16)
+
+
+def total_of(array):
+    return jnp.sum(jnp.sum(array, axis=0, keepdims=True), axis=1, keepdims=True)
+
+
+def make_tag(values, sector):
+    row = lax.broadcasted_iota(jnp.int32, (TAG, LANES), 0)
+    lane = lax.broadcasted_iota(jnp.int32, (TAG, LANES), 1)
+    spread = jnp.zeros((TAG, LANES), jnp.float32)
+    for place, value in enumerate(values):
+        spread = jnp.where(row // 3 == place, value, spread)
+    high = spread.astype(jnp.bfloat16).astype(jnp.float32)
+    middle = (spread - high).astype(jnp.bfloat16).astype(jnp.float32)
+    low = spread - high - middle
+    parts = jnp.where(row % 3 == 0, high, jnp.where(row % 3 == 1, middle, low))
+    return jnp.where((lane == sector) & (row < 3 * len(values)), parts, 0.0).astype(jnp.bfloat16)
+
+
+def second_kernel(widths, holders, amps, first, right, left, message, stay, left_vmem, sems):
+    rows, half = stay.shape
+    copies = start_copies(left, left_vmem, sems)
+    basis = [
+        jnp.where(
+            live_columns(widths, holders, half, h), amps[h].astype(jnp.float32), 0.0
+        )
+        for h in range(2)
+    ]
+    firsts = [first[h].astype(jnp.float32) for h in range(2)]
+    overlap = total_of(basis[0] * firsts[0]) + total_of(basis[1] * firsts[1])
+    norm = total_of(basis[0] * basis[0]) + total_of(basis[1] * basis[1])
+    quotient = jnp.where(norm > 0, overlap / jnp.where(norm > 0, norm, 1.0), 0.0)
+    deflated = [firsts[h] - quotient * basis[h] for h in range(2)]
+    rest = total_of(deflated[0] * deflated[0]) + total_of(deflated[1] * deflated[1])
+    vector = jnp.concatenate(deflated, axis=1).astype(jnp.bfloat16)
+    sector = holders[lax.axis_index("sec")]
+    message[pl.ds(0, TAG), pl.ds(0, LANES)] = make_tag((overlap, norm, quotient, rest), sector)
+    message[pl.ds(0, TAG), pl.ds(LANES, half - LANES)] = jnp.zeros(
+        (TAG, half - LANES), jnp.bfloat16
+    )
+    for term, copy in copies:
+        copy.wait()
+        block = apply_term(right, left_vmem, vector, term)
+        if term == 0:
+            stay[...] = block
+        else:
+            message[pl.ds(TAG + (term - 1) * rows, rows), :] = block.astype(jnp.bfloat16)
+
+
+def final_kernel(widths, holders, stay, old, stay_2, gathered, second, tags, blocks, sems):
+    rows, half = stay.shape
+    slots = holders.shape[0]
+    tag_copy = pltpu.make_async_copy(
+        gathered.at[:, pl.ds(0, TAG), pl.ds(0, LANES)], tags, sems.at[2]
+    )
+    tag_copy.start()
+    copies = fetch(holders, gathered, TAG, rows, blocks, sems)
+    sector = holders[lax.axis_index("sec")]
+    live = live_columns(widths, holders, half, lax.axis_index("env"))
+    total = jnp.int32(0)
+    for s in range(slots):
+        total = total + widths[s]
+    live_count = rows * total.astype(jnp.float32)
+    tag_copy.wait()
+    table = jnp.sum(tags[...].astype(jnp.float32), axis=0)
+
+    def value(place):
+        parts = [table[3 * place + i : 3 * place + i + 1, :] for i in range(3)]
+        return parts[0] + parts[1] + parts[2]
+
+    overlaps, norms, quotients, rests = (value(place) for place in range(4))
+    quotient = total_of(overlaps) / total_of(norms)
+    lane = lax.broadcasted_iota(jnp.int32, (1, LANES), 1)
+    shifts = jnp.where(lane < slots, quotients - quotient, 0.0)
+    resid_norm = total_of(rests + shifts * shifts * norms)
+    scale = lax.rsqrt(resid_norm / live_count + 1e-06)
+
+    def shift_of(source):
+        return total_of(jnp.where(lane == source, shifts, 0.0))
+
+    old_1, old_2 = incoming(holders, old)
+    result = stay_2[...] + shift_of(sector) * stay[...].astype(jnp.float32)
+    result = result + shift_of(sector - QDOWN) * old_1 + shift_of(sector - 1) * old_2
+    for copy in copies:
+        copy.wait()
+    new_1, new_2 = incoming(holders, blocks)
+    result = result + new_1 + new_2
+    second[...] = jnp.where(live, scale * result, 0.0).astype(jnp.bfloat16)
+
+
+SMEM = pl.BlockSpec(memory_space=pltpu.SMEM)
+VMEM = pl.BlockSpec(memory_space=pltpu.VMEM)
+HBM = pl.BlockSpec(memory_space=pltpu.HBM)
+PARAMS = pltpu.CompilerParams(vmem_limit_bytes=16 * 1024 * 1024)
+
+
+def on_device(amplitudes, widths, holders, left_env, right_env):
+    slots_dev, right_dim, half = amplitudes.shape
+    n_slots = holders.shape[0]
+    assert slots_dev == 1
+    if n_slots != 2 * QDOWN:
+        return on_device_any(amplitudes, widths, holders, left_env, right_env)
+    block = jax.ShapeDtypeStruct((right_dim, half), jnp.bfloat16)
+    wide = jax.ShapeDtypeStruct((right_dim, half), jnp.float32)
+    pair = jax.ShapeDtypeStruct((2, right_dim, half), jnp.bfloat16)
+    plain = jax.ShapeDtypeStruct((2 * right_dim, half), jnp.bfloat16)
+    tagged = jax.ShapeDtypeStruct((TAG + 2 * right_dim, half), jnp.bfloat16)
+    left_scratch = [
+        pltpu.VMEM(left_env.shape[1:], jnp.bfloat16),
+        pltpu.SemaphoreType.DMA((left_env.shape[1],)),
+    ]
+
+    amps_full = lax.all_gather(amplitudes[0], "env")
+    message, stay = pl.pallas_call(
+        first_kernel,
+        out_shape=(plain, block),
+        in_specs=[SMEM, SMEM, VMEM, VMEM, HBM],
+        out_specs=(VMEM, VMEM),
+        scratch_shapes=left_scratch,
+        compiler_params=PARAMS,
+    )(widths, holders, amps_full, right_env, left_env)
+    gathered = lax.all_gather(message, "sec")
+    first, old = pl.pallas_call(
+        sum_kernel,
+        out_shape=(block, pair),
+        in_specs=[SMEM, SMEM, VMEM, HBM],
+        out_specs=(VMEM, VMEM),
+        scratch_shapes=[pltpu.SemaphoreType.DMA((2,))],
+        compiler_params=PARAMS,
+    )(widths, holders, stay, gathered)
+
+    first_full = lax.all_gather(first, "env")
+    message, stay_2 = pl.pallas_call(
+        second_kernel,
+        out_shape=(tagged, wide),
+        in_specs=[SMEM, SMEM, VMEM, VMEM, VMEM, HBM],
+        out_specs=(VMEM, VMEM),
+        scratch_shapes=left_scratch,
+        compiler_params=PARAMS,
+    )(widths, holders, amps_full, first_full, right_env, left_env)
+    gathered = lax.all_gather(message, "sec")
+    second = pl.pallas_call(
+        final_kernel,
+        out_shape=block,
+        in_specs=[SMEM, SMEM, VMEM, VMEM, VMEM, HBM],
+        out_specs=VMEM,
+        scratch_shapes=[
+            pltpu.VMEM((n_slots, TAG, LANES), jnp.bfloat16),
+            pltpu.VMEM((2, right_dim, half), jnp.bfloat16),
+            pltpu.SemaphoreType.DMA((3,)),
+        ],
+        compiler_params=PARAMS,
+    )(widths, holders, stay, old, stay_2, gathered)
+    return first[None], second[None]
+
+
 def solution(mesh):
     in_specs = (
         P(("runs", "sec"), None, "env"),

time: 121 us -> 140 us (1.16)
  waiting for transfers between devices: 18.9 us -> 101 us
  starting transfers between devices: 29.4 us -> 0.08 us
  other arithmetic: 22.9 us -> 0 us
  local copies, waits for them, and re-layouts: 31 us -> 11.3 us
  Pallas kernels: 0 us -> 8.29 us
  between operations: 7.35 us -> 14.1 us
  matrix products: 5.8 us -> 0 us
    all_gather x0 -> x2, waiting for transfers between devices: none -> 101 us  [on_device(): gathered = lax.all_gather(message, 'sec')]
    all_to_all x4 -> x0, waiting for transfers between devices: 18.9 us -> none  [the longest x2 10.2 us: spread(): return lax.all_to_all(pieces, 'sec', split_axis=0, concat_axis=0)]
    all_to_all x4 -> x0, starting transfers between devices: 18.2 us -> none  [the longest x2 11.2 us: spread(): return lax.all_to_all(pieces, 'sec', split_axis=0, concat_axis=0)]
    ppermute x7 -> x0, starting transfers between devices: 11.2 us -> none  [share(): other = lax.ppermute(lanes, 'sec', pairs)]
    gather x6 -> x0, local copies, waits for them, and re-layouts: 9.57 us -> none  [the longest x4 8.29 us: merge(): picked = received[source, term]]
    pallas_call x0 -> x4, Pallas kernels: none -> 8.29 us  [the longest x1 2.5 us: on_device(): pl.pallas_call(second_kernel, out_shape=(tagged, wide), in_specs=[SMEM, S...]
    convert_element_type x6 -> x0, other arithmetic: 7.96 us -> none  [the longest x1 1.89 us: on_device(): jnp.where(live, stay_2 + arrived_2.astype(jnp.float32), 0.0)]
    slice x4 -> x0, local copies, waits for them, and re-layouts: 6.24 us -> none  [the longest x2 3.45 us: on_device(): received = spread(outgoing[1:], n_slots)]
  transfers between devices with their start and end apart: 11 -> 2, of which waited for: 4 -> 2; matrix products, arithmetic and copies ran while one was open for 14% -> 0% of each run, Pallas kernels for 0% -> 0%
where the time goes in v3:
time: 140 us
  waiting for transfers between devices  101 us (72%)
  between operations  14.1 us (10%)
  local copies, waits for them, and re-layouts  11.3 us (8%)
  Pallas kernels  8.29 us (6%)
  blocking collectives  4.5 us (3%)
    all_gather x2, waiting for transfers between devices, on_device(): gathered = lax.all_gather(message, 'sec')  101 us
    unnamed x32, local copies, waits for them, and re-layouts  11.3 us
  transfers between devices with their start and end apart: 2, of which 2 were waited for; matrix products, arithmetic and copies ran while one was open for 0% of the time, Pallas kernels for 0%

profile of v3, /device:TPU:0, one launch (start us, length us, event | category | flops | bytes accessed | tf_op | source)
XLA Modules:
  0.0 139.7 jit_solution(15226324150240620075)
XLA Ops:
  7.2 0.0 copy-start.15
  7.2 0.0 copy-start.13
  7.2 0.0 all-gather.6.cloned.1.call-start
  7.2 2.3 %all_gather.19.amps = bf16[2,128,512]{2,1,0:T(8,128)(2,1)S(1)} all-gather(bf16[1,128,512]{2,1,0:T(8,128)(2,1)} %param.5), channel_id=1, replica_groups=mesh['runs'=2,'sec'=8,'env'=2] {'env'}, dimensions={0}, use_global_device_ids=true | all-gather | bytes 393216 | tf_op jit(solution)/shard_map/all_gather | solution.py:303
  9.5 1.9 %copy-done = bf16[1,3,1024,512]{3,2,1,0:T(8,128)(2,1)S(1)} copy-done((bf16[1,3,1024,512]{3,2,1,0:T(8,128)(2,1)S(1)}, bf16[1,3,1024,512]{3,2,1,0:T(8,128)(2,1)}, u32[]{:S(2)}) %copy-start) | copy-done | bytes 3145752
  11.4 0.9 copy-done.4
  12.3 0.7 copy-done.12
  13.0 0.7 copy-done.14
  13.6 2.1 %shard_map.68 = (bf16[256,512]{1,0:T(8,128)(2,1)S(1)}, bf16[128,512]{1,0:T(8,128)(2,1)S(1)}) custom-call(s32[8]{0:T(128)S(1)} %copy-done.12, s32[8]{0:T(128)S(1)} %copy-done.14, bf16[2,128,512]{2,1,0:T(8,128)(2,1)S(1)} %all_gather.19.amps, bf16[3,128,128]{2,1,0:T(8,128)(2,1)S(1)} %copy-done.4, bf16[1,3,1024,512]{3,2,1,0:T(8,128)(2,1)S(1)} %copy-done), custom_call_target="tpu_custom_call" | custom-call | tf_op jit(solution)/shard_map/pallas_call | solution.py:304
  15.7 0.0 copy-start.7
  15.7 0.7 copy-done.7
  16.4 0.0 all-gather.6.cloned.1.call-update
  16.4 0.0 all-gather.8.cloned.1.call-start
  16.5 52.0 %all-gather.6.cloned.1.call-done = bf16[2048,512]{1,0:T(8,128)(2,1)} async-done(((bf16[256,512]{1,0:T(8,128)(2,1)}), bf16[2048,512]{1,0:T(8,128)(2,1)}) %all-gather.6.cloned.1.call-update) | async-done | bytes 2097168 | tf_op jit(solution)/shard_map/all_gather | solution.py:312
  68.5 0.0 copy-done.15
  68.5 0.0 copy-done.13
  68.5 1.6 %copy-done.3 = bf16[2048,512]{1,0:T(8,128)(2,1)S(1)} copy-done((bf16[2048,512]{1,0:T(8,128)(2,1)S(1)}, bf16[2048,512]{1,0:T(8,128)(2,1)}, u32[]{:S(2)}) %copy-start.3) | copy-done | bytes 2097176
  70.1 1.7 %shard_map.69 = (bf16[128,512]{1,0:T(8,128)(2,1)}, bf16[2,128,512]{2,1,0:T(8,128)(2,1)S(1)}) custom-call(s32[8]{0:T(128)S(1)} %copy-done.13, s32[8]{0:T(128)S(1)} %copy-done.15, bf16[128,512]{1,0:T(8,128)(2,1)S(1)} %get-tuple-element.8.stay, bf16[8,256,512]{2,1,0:T(8,128)(2,1)S(1)} %bitcast.6), custom_call_target="tpu_custom_call" | custom-call | tf_op jit(solution)/shard_map/pallas_call | solution.py:313
  71.8 0.0 copy-start.8
  71.8 2.2 %all-gather.1 = bf16[256,512]{1,0:T(8,128)(2,1)S(1)} all-gather(bf16[128,512]{1,0:T(8,128)(2,1)} %get-tuple-element.10), channel_id=3, replica_groups=mesh['runs'=2,'sec'=8,'env'=2] {'env'}, dimensions={0}, use_global_device_ids=true | all-gather | bytes 393216 | tf_op jit(solution)/shard_map/all_gather | solution.py:322
  74.0 0.0 copy-done.1
  74.0 0.0 copy-done.5
  74.0 2.5 %shard_map.70 = (bf16[272,512]{1,0:T(8,128)(2,1)S(1)}, f32[128,512]{1,0:T(8,128)S(1)}) custom-call(s32[8]{0:T(128)S(1)} %copy-done.13, s32[8]{0:T(128)S(1)} %copy-done.15, bf16[2,128,512]{2,1,0:T(8,128)(2,1)S(1)} %all_gather.19.amps, bf16[2,128,512]{2,1,0:T(8,128)(2,1)S(1)} %bitcast.7, bf16[3,128,128]{2,1,0:T(8,128)(2,1)S(1)} %copy-done.5, ...), custom_call_target="tpu_custom_call" | custom-call | tf_op jit(solution)/shard_map/pallas_call | solution.py:323
  76.5 0.0 copy-done.8
  76.5 0.7 copy-done.6
  77.2 0.7 copy-done.10
  77.9 0.0 all-gather.8.cloned.1.call-update
  77.9 49.3 %all-gather.8.cloned.1.call-done = bf16[2176,512]{1,0:T(8,128)(2,1)} async-done(((bf16[272,512]{1,0:T(8,128)(2,1)}), bf16[2176,512]{1,0:T(8,128)(2,1)}) %all-gather.8.cloned.1.call-update) | async-done | bytes 2228240 | tf_op jit(solution)/shard_map/all_gather | solution.py:331
  127.3 1.6 %copy-done.2 = bf16[2176,512]{1,0:T(8,128)(2,1)S(1)} copy-done((bf16[2176,512]{1,0:T(8,128)(2,1)S(1)}, bf16[2176,512]{1,0:T(8,128)(2,1)}, u32[]{:S(2)}) %copy-start.2) | copy-done | bytes 2228248
  128.9 0.9 copy-done.9
  129.8 0.9 copy-done.11
  130.8 2.0 %shard_map.71 = bf16[128,512]{1,0:T(8,128)(2,1)} custom-call(s32[8]{0:T(128)S(1)} %copy-done.13, s32[8]{0:T(128)S(1)} %copy-done.15, bf16[128,512]{1,0:T(8,128)(2,1)S(1)} %get-tuple-element.8.stay, bf16[2,128,512]{2,1,0:T(8,128)(2,1)S(1)} %copy-done.9, f32[128,512]{1,0:T(8,128)S(1)} %copy-done.11, bf16[8,272,512]{2,1,0:T(8,128)(2,1)S(1)} %bitcast.5), custom_call_target="tpu_custom_call" | custom-call | tf_op jit(solution)/shard_map/pallas_call | solution.py:332
  (12 shorter events, 0.0 us)
Async XLA Ops:
  7.2 61.3 %copy-start.15 = (s32[8]{0:T(128)S(1)}, s32[8]{0:T(128)}, u32[]{:S(2)}) copy-start(s32[8]{0:T(128)} %holders.7) | copy-start | bytes 100
  7.2 61.3 %copy-start.13 = (s32[8]{0:T(128)S(1)}, s32[8]{0:T(128)}, u32[]{:S(2)}) copy-start(s32[8]{0:T(128)} %widths.7) | copy-start | bytes 100
  7.2 61.3 %all-gather.6.cloned.1.call-start = ((), (), s32[]{:S(2)}) async-start(), calls=%async_computation | async-start | bytes 2359296 | tf_op jit(solution)/shard_map/all_gather | solution.py:312
  9.5 1.9 %copy-start = (bf16[1,3,1024,512]{3,2,1,0:T(8,128)(2,1)S(1)}, bf16[1,3,1024,512]{3,2,1,0:T(8,128)(2,1)}, u32[]{:S(2)}) copy-start(bf16[1,3,1024,512]{3,2,1,0:T(8,128)(2,1)} %left.3) | copy-start | bytes 9437188
  11.4 0.9 copy-start.4
  12.3 0.7 copy-start.12
  13.0 0.7 copy-start.14
  13.6 60.4 %copy-start.1 = (bf16[1,3,1024,512]{3,2,1,0:T(8,128)(2,1)S(1)}, bf16[1,3,1024,512]{3,2,1,0:T(8,128)(2,1)}, u32[]{:S(2)}) copy-start(bf16[1,3,1024,512]{3,2,1,0:T(8,128)(2,1)} %left.3) | copy-start | bytes 9437188
  15.7 0.7 copy-start.7
  16.4 110.8 %all-gather.8.cloned.1.call-start = ((), (), s32[]{:S(2)}) async-start(), calls=%async_computation.1 | async-start | bytes 2506752 | tf_op jit(solution)/shard_map/all_gather | solution.py:331
  68.5 1.6 %copy-start.3 = (bf16[2048,512]{1,0:T(8,128)(2,1)S(1)}, bf16[2048,512]{1,0:T(8,128)(2,1)}, u32[]{:S(2)}) copy-start(bf16[2048,512]{1,0:T(8,128)(2,1)} %all-gather.6.cloned.1.call-done) | copy-start | bytes 6291460
  70.1 3.9 %copy-start.5 = (bf16[3,128,128]{2,1,0:T(8,128)(2,1)S(1)}, bf16[3,128,128]{2,1,0:T(8,128)(2,1)}, u32[]{:S(2)}) copy-start(bf16[3,128,128]{2,1,0:T(8,128)(2,1)} %right.3) | copy-start | bytes 294916
  71.8 4.7 %copy-start.8 = (bf16[2,128,512]{2,1,0:T(8,128)(2,1)}, bf16[2,128,512]{2,1,0:T(8,128)(2,1)S(1)}, u32[]{:S(2)}) copy-start(bf16[2,128,512]{2,1,0:T(8,128)(2,1)S(1)} %get-tuple-element.11.old) | copy-start | bytes 786436
  76.5 0.7 copy-start.6
  77.2 0.7 copy-start.10
  127.3 1.6 %copy-start.2 = (bf16[2176,512]{1,0:T(8,128)(2,1)S(1)}, bf16[2176,512]{1,0:T(8,128)(2,1)}, u32[]{:S(2)}) copy-start(bf16[2176,512]{1,0:T(8,128)(2,1)} %all-gather.8.cloned.1.call-done) | copy-start | bytes 6684676
  128.9 0.9 copy-start.9
  129.8 0.9 copy-start.11
Sparse Core Ops, SparseCore 0:
  16.6 51.8 all-gather.5
  78.1 49.1 all-gather.7

commit v4 on v1

--- a/solution.py
+++ b/solution.py
@@ -1,6 +1,8 @@
 import jax
 import jax.numpy as jnp
 from jax import lax
+from jax.experimental import pallas as pl
+from jax.experimental.pallas import tpu as pltpu
 from jax.sharding import PartitionSpec as P
 
 QDOWN = 4
@@ -61,7 +63,7 @@
     return total
 
 
-def on_device(amplitudes, widths, holders, left_env, right_env):
+def on_device_any(amplitudes, widths, holders, left_env, right_env):
     slots_dev, right_dim, half_width = amplitudes.shape
     assert slots_dev == 1
     n_slots = holders.shape[0]
@@ -107,6 +109,261 @@
     return first[None], second[None]
 
 
+LANES = 128
+
+
+def find_slot(holders, sector):
+    slot = jnp.int32(0)
+    for s in range(holders.shape[0]):
+        slot = slot + jnp.where(holders[s] == sector, s, 0)
+    return slot
+
+
+def live_columns(widths, holders, half, side):
+    width = widths[holders[lax.axis_index("sec")]]
+    columns = side * half + lax.broadcasted_iota(jnp.int32, (1, half), 1)
+    return columns < width
+
+
+def apply_term(right, left, vector, term):
+    products = jnp.dot(right[term], vector, preferred_element_type=jnp.float32)
+    return jnp.dot(products.astype(jnp.bfloat16), left, preferred_element_type=jnp.float32)
+
+
+def store_message(full, part, block):
+    block = block.astype(full.dtype)
+    full[...] = block
+    part[...] = block[:, : part.shape[1]]
+
+
+def write_plan(widths, holders, half, turns, flags):
+    me = lax.axis_index("sec")
+    side = lax.axis_index("env")
+    sector = holders[me]
+    down = sector % QDOWN
+    inner = (down == 1) | (down == 2)
+    plan = (
+        (sector ^ QDOWN, sector | QDOWN, True),
+        (sector ^ 1, sector | 1, True),
+        (sector ^ 3, sector - down + 2, inner),
+    )
+    for step, (partner, target, used) in enumerate(plan):
+        offset = me ^ find_slot(holders, partner)
+        columns = jnp.where(used, widths[target] - side * half, 0)
+        kind = jnp.where(columns > half // 2, 2, 1)
+        turns[step][0] = jnp.where(columns > 0, (offset - 1) * 2 + kind, 0)
+    flags[0] = widths[sector] - side * half
+    flags[1] = jnp.where(sector >= QDOWN, 1, 0)
+    flags[2] = jnp.where(down % 2 == 1, 1, 0)
+    flags[3] = jnp.where(down == 2, 1, 0)
+
+
+def first_kernel(
+    widths,
+    holders,
+    amps,
+    right,
+    left,
+    full_1,
+    part_1,
+    full_2,
+    part_2,
+    stay,
+    turn_1,
+    turn_2,
+    turn_3,
+    flags,
+    left_vmem,
+    sems,
+):
+    half = amps.shape[2]
+    copies = []
+    for term in (1, 2, 0):
+        copy = pltpu.make_async_copy(left.at[0, term], left_vmem.at[term], sems.at[term])
+        copy.start()
+        copies.append((term, copy))
+    write_plan(widths, holders, half, (turn_1, turn_2, turn_3), flags)
+    vector = jnp.concatenate(
+        [
+            jnp.where(live_columns(widths, holders, half, h), amps[h], jnp.zeros_like(amps[h]))
+            for h in range(2)
+        ],
+        axis=1,
+    )
+    for term, copy in copies:
+        copy.wait()
+        block = apply_term(right, left_vmem[term], vector, term)
+        if term == 0:
+            stay[...] = block.astype(jnp.bfloat16)
+        else:
+            store_message(*((full_1, part_1), (full_2, part_2))[term - 1], block)
+
+
+def total_of(array):
+    return jnp.sum(jnp.sum(array, axis=0, keepdims=True), axis=1, keepdims=True)
+
+
+def second_kernel(
+    widths, holders, amps, first, right, left, full_1, part_1, full_2, part_2, stay, tag
+):
+    half = amps.shape[2]
+    basis = [
+        jnp.where(
+            live_columns(widths, holders, half, h), amps[h].astype(jnp.float32), 0.0
+        )
+        for h in range(2)
+    ]
+    firsts = [first[h].astype(jnp.float32) for h in range(2)]
+    overlap = total_of(basis[0] * firsts[0]) + total_of(basis[1] * firsts[1])
+    norm = total_of(basis[0] * basis[0]) + total_of(basis[1] * basis[1])
+    quotient = jnp.where(norm > 0, overlap / jnp.where(norm > 0, norm, 1.0), 0.0)
+    deflated = [firsts[h] - quotient * basis[h] for h in range(2)]
+    rest = total_of(deflated[0] * deflated[0]) + total_of(deflated[1] * deflated[1])
+    vector = jnp.concatenate(deflated, axis=1).astype(jnp.bfloat16)
+
+    row = lax.broadcasted_iota(jnp.int32, tag.shape, 0)
+    values = jnp.zeros(tag.shape, jnp.float32)
+    for place, value in enumerate((overlap, norm, quotient, rest)):
+        values = jnp.where(row == place, value, values)
+    tag[...] = values
+
+    for term in (1, 2, 0):
+        block = apply_term(right, left[0, term], vector, term)
+        if term == 0:
+            stay[...] = block
+        else:
+            store_message(*((full_1, part_1), (full_2, part_2))[term - 1], block)
+
+
+def incoming(holders, arrived_1, arrived_2, arrived_3):
+    sector = holders[lax.axis_index("sec")]
+    down = sector % QDOWN
+    block_1, block_2, block_3 = (
+        arrived[...].astype(jnp.float32) for arrived in (arrived_1, arrived_2, arrived_3)
+    )
+    block_1 = jnp.where(sector >= QDOWN, block_1, 0.0)
+    block_2 = jnp.where(down % 2 == 1, block_2, jnp.where(down == 2, block_3, 0.0))
+    return block_1, block_2
+
+
+def final_kernel(
+    widths, holders, tags, stay, stay_2, old_1, old_2, old_3, new_1, new_2, new_3, second
+):
+    rows, half = stay.shape
+    slots = holders.shape[0]
+    me = lax.axis_index("sec")
+    sector = holders[me]
+    live = live_columns(widths, holders, half, lax.axis_index("env"))
+    total = jnp.int32(0)
+    for s in range(slots):
+        total = total + widths[s]
+    live_count = rows * total.astype(jnp.float32)
+    overlaps, norms, quotients, rests = (tags[:, i, :] for i in range(4))
+    quotient = jnp.sum(overlaps, axis=0, keepdims=True) / jnp.sum(norms, axis=0, keepdims=True)
+    shifts = quotients - quotient
+    resid_norm = jnp.sum(rests + shifts * shifts * norms, axis=0, keepdims=True)
+    scale = lax.rsqrt(resid_norm / live_count + 1e-06)[:, :1]
+    slot = lax.broadcasted_iota(jnp.int32, shifts.shape, 0)
+
+    def shift_of(source):
+        picked = jnp.where(slot == find_slot(holders, source), shifts, 0.0)
+        return jnp.sum(picked, axis=0, keepdims=True)[:, :1]
+
+    old_block_1, old_block_2 = incoming(holders, old_1, old_2, old_3)
+    new_block_1, new_block_2 = incoming(holders, new_1, new_2, new_3)
+    result = stay_2[...] + shift_of(sector) * stay[...].astype(jnp.float32)
+    result = result + new_block_1 + shift_of(sector - QDOWN) * old_block_1
+    result = result + new_block_2 + shift_of(sector - 1) * old_block_2
+    second[...] = jnp.where(live, scale * result, 0.0).astype(jnp.bfloat16)
+
+
+SMEM = pl.BlockSpec(memory_space=pltpu.SMEM)
+VMEM = pl.BlockSpec(memory_space=pltpu.VMEM)
+HBM = pl.BlockSpec(memory_space=pltpu.HBM)
+SMALL = pltpu.CompilerParams(vmem_limit_bytes=16 * 1024 * 1024)
+LARGE = pltpu.CompilerParams(vmem_limit_bytes=61 * 1024 * 1024)
+
+
+def choose(index, branches, *operands):
+    jaxprs = tuple(jax.make_jaxpr(branch)(*operands) for branch in branches)
+    return lax.cond_p.bind(index.reshape(()), *operands, branches=jaxprs)
+
+
+def exchange(turn, full, part, n_slots):
+    def swap_part(offset):
+        pairs = [(i, i ^ offset) for i in range(n_slots)]
+        missing = full.shape[1] - part.shape[1]
+        return lambda full, part: [
+            jnp.pad(lax.ppermute(part, "sec", pairs), ((0, 0), (0, missing)))
+        ]
+
+    def swap_full(offset):
+        pairs = [(i, i ^ offset) for i in range(n_slots)]
+        return lambda full, part: [lax.ppermute(full, "sec", pairs)]
+
+    branches = [lambda full, part: [jnp.zeros_like(full)]]
+    for offset in range(1, n_slots):
+        branches += [swap_part(offset), swap_full(offset)]
+    (arrived,) = choose(turn, branches, full, part)
+    return arrived
+
+
+def on_device(amplitudes, widths, holders, left_env, right_env):
+    slots_dev, right_dim, half = amplitudes.shape
+    n_slots = holders.shape[0]
+    assert slots_dev == 1
+    if n_slots != 2 * QDOWN:
+        return on_device_any(amplitudes, widths, holders, left_env, right_env)
+    part = jax.ShapeDtypeStruct((right_dim, half // 2), jnp.bfloat16)
+    block = jax.ShapeDtypeStruct((right_dim, half), jnp.bfloat16)
+    wide = jax.ShapeDtypeStruct((right_dim, half), jnp.float32)
+    tag_shape = jax.ShapeDtypeStruct((8, LANES), jnp.float32)
+    turn = jax.ShapeDtypeStruct((1,), jnp.int32)
+
+    amps_full = lax.all_gather(amplitudes[0], "env")
+    full_1, part_1, full_2, part_2, stay, turn_1, turn_2, turn_3, flags = pl.pallas_call(
+        first_kernel,
+        out_shape=(block, part) * 2
+        + (block, turn, turn, turn, jax.ShapeDtypeStruct((4,), jnp.int32)),
+        in_specs=[SMEM, SMEM, VMEM, VMEM, HBM],
+        out_specs=(VMEM,) * 5 + (SMEM,) * 4,
+        scratch_shapes=[
+            pltpu.VMEM(left_env.shape[1:], jnp.bfloat16),
+            pltpu.SemaphoreType.DMA((left_env.shape[1],)),
+        ],
+        compiler_params=LARGE,
+    )(widths, holders, amps_full, right_env, left_env)
+    old_1 = exchange(turn_1, full_1, part_1, n_slots)
+    old_2 = exchange(turn_2, full_2, part_2, n_slots)
+    old_3 = exchange(turn_3, full_2, part_2, n_slots)
+    live = lax.broadcasted_iota(jnp.int32, (right_dim, half), 1) < flags[0]
+    total = stay.astype(jnp.float32) + jnp.where(flags[1] > 0, old_1, 0).astype(jnp.float32)
+    side_block = jnp.where(flags[2] > 0, old_2, jnp.where(flags[3] > 0, old_3, 0))
+    total = total + side_block.astype(jnp.float32)
+    first = jnp.where(live, total, 0.0).astype(jnp.bfloat16)
+
+    first_full = lax.all_gather(first, "env")
+    full_1, part_1, full_2, part_2, stay_2, tag = pl.pallas_call(
+        second_kernel,
+        out_shape=(block, part) * 2 + (wide, tag_shape),
+        in_specs=[SMEM, SMEM, VMEM, VMEM, VMEM, VMEM],
+        out_specs=(VMEM,) * 6,
+        compiler_params=SMALL,
+    )(widths, holders, amps_full, first_full, right_env, left_env)
+    tags = lax.all_gather(tag, "sec")
+    new_1 = exchange(turn_1, full_1, part_1, n_slots)
+    new_2 = exchange(turn_2, full_2, part_2, n_slots)
+    new_3 = exchange(turn_3, full_2, part_2, n_slots)
+    second = pl.pallas_call(
+        final_kernel,
+        out_shape=block,
+        in_specs=[SMEM, SMEM] + [VMEM] * 9,
+        out_specs=VMEM,
+        compiler_params=SMALL,
+    )(widths, holders, tags, stay, stay_2, old_1, old_2, old_3, new_1, new_2, new_3)
+    return first[None], second[None]
+
+
 def solution(mesh):
     in_specs = (
         P(("runs", "sec"), None, "env"),

time: 121 us -> 99.1 us (0.82); the launches traced: 119 us -> 99.9 us
  blocking collectives: 4.08 us -> 37.7 us
  local copies, waits for them, and re-layouts: 31 us -> 4.4 us
  other arithmetic: 22.9 us -> 1.63 us
  starting transfers between devices: 29.4 us -> 10.8 us
  waiting for transfers between devices: 18.9 us -> 30.1 us
  Pallas kernels: 0 us -> 8.68 us
  matrix products: 5.8 us -> 0 us
  between operations: 7.35 us -> 2.55 us
  loops' own time: 0 us -> 4.01 us
    all_gather x2 -> x3, blocking collectives: 4.08 us -> 37.7 us  [the longest x1 31.9 us: on_device(): tags = lax.all_gather(tag, 'sec')]
    ppermute x7 -> x6, waiting for transfers between devices: 0.02 us -> 30.1 us  [the longest x4 17.6 us: swap_full(): return lambda full, part: [lax.ppermute(full, 'sec', pairs)]]
    all_to_all x4 -> x0, waiting for transfers between devices: 18.9 us -> none  [the longest x2 10.2 us: spread(): return lax.all_to_all(pieces, 'sec', split_axis=0, concat_axis=0)]
    all_to_all x4 -> x0, starting transfers between devices: 18.2 us -> none  [the longest x2 11.2 us: spread(): return lax.all_to_all(pieces, 'sec', split_axis=0, concat_axis=0)]
    gather x6 -> x0, local copies, waits for them, and re-layouts: 9.57 us -> none  [the longest x4 8.29 us: merge(): picked = received[source, term]]
    pallas_call x0 -> x3, Pallas kernels: none -> 8.68 us  [the longest x1 4.16 us: on_device(): pl.pallas_call(first_kernel, out_shape=(block, part) * 2 + (block, turn,...]
    convert_element_type x6 -> x1, other arithmetic: 7.96 us -> 1 us  [on_device(): first = jnp.where(live, total, 0.0).astype(jnp.bfloat16)]
    dot_general x2 -> x0, matrix products: 5.8 us -> none  [contract(): jnp.einsum('tik,tkw->tiw', products, left_env, preferred_element_type=jnp...]
  transfers between devices with their start and end apart: 11 -> 6, of which waited for: 4 -> 6; matrix products, arithmetic and copies ran while one was open for 14% -> 0% of each run, Pallas kernels for 0% -> 0%
where the time goes in v4:
time: 99.1 us; the launch traced here: 99.9 us
  blocking collectives  37.7 us (38%)
  waiting for transfers between devices  30.1 us (30%)
  starting transfers between devices  10.8 us (11%)
  Pallas kernels  8.68 us (9%)
  local copies, waits for them, and re-layouts  4.4 us (4%)
  loops' own time  4.01 us (4%)
  between operations  2.55 us (3%)
  other arithmetic  1.63 us (2%)
    all_gather x1, blocking collectives, on_device(): tags = lax.all_gather(tag, 'sec')  31.9 us
    ppermute x4, waiting for transfers between devices, swap_full(): return lambda full, part: [lax.ppermute(full, 'sec', pairs)]  17.6 us
    ppermute x2, waiting for transfers between devices, swap_part(): lax.ppermute(part, 'sec', pairs)  12.5 us
    ppermute x4, starting transfers between devices, swap_full(): return lambda full, part: [lax.ppermute(full, 'sec', pairs)]  10.7 us
    pallas_call x1, Pallas kernels, on_device(): pl.pallas_call(first_kernel, out_shape=(block, part) * 2 + (block, turn,...  4.16 us
    another operation x6, loops' own time, choose(): return lax.cond_p.bind(index.reshape(()), *operands, branches=jaxprs)  4.01 us
    all_gather x1, blocking collectives, on_device(): amps_full = lax.all_gather(amplitudes[0], 'env')  3.78 us
    pallas_call x1, Pallas kernels, on_device(): pl.pallas_call(second_kernel, out_shape=(block, part) * 2 + (wide, tag_sh...  2.32 us
  transfers between devices with their start and end apart: 6, of which 6 were waited for; matrix products, arithmetic and copies ran while one was open for 0% of the time, Pallas kernels for 0%

profile of v4, /device:TPU:0, one launch (start us, length us, event | category | flops | bytes accessed | tf_op | source)
XLA Modules:
  0.0 99.9 jit_solution(10281207734653179732)
XLA Ops:
  0.6 3.8 %all_gather.13.amps = bf16[2,128,512]{2,1,0:T(8,128)(2,1)} all-gather(bf16[1,128,512]{2,1,0:T(8,128)(2,1)} %param.95), channel_id=1, replica_groups=mesh['runs'=2,'sec'=8,'env'=2] {'env'}, dimensions={0}, use_global_device_ids=true | all-gather | bytes 393216 | tf_op jit(solution)/shard_map/all_gather | solution.py:323
  4.4 4.2 %shard_map.68 = (bf16[128,512]{1,0:T(8,128)(2,1)}, bf16[128,256]{1,0:T(8,128)(2,1)}, bf16[128,512]{1,0:T(8,128)(2,1)}, bf16[128,256]{1,0:T(8,128)(2,1)}, bf16[12...) custom-call(s32[8]{0:T(128)} %widths.5, s32[8]{0:T(128)} %holders.5, ...), custom_call_target="tpu_custom_call" | custom-call | tf_op jit(solution)/shard_map/pallas_call | solution.py:324
  8.6 0.0 copy-start.6
  8.6 1.5 %fusion = (s32[1]{0:T(128)}, s32[1]{0:T(128)}, s32[1]{0:T(128)}, s32[1]{0:T(128)}) fusion(s32[4]{0:T(128)} %get-tuple-element.197), kind=kLoop, calls=%fused_computation.2 | loop fusion | bytes 32 | tf_op jit(solution)/shard_map/slice | solution.py:339
  11.9 0.6 iota_compare_fusion
  12.6 10.1 %conditional.6 = (bf16[128,512]{1,0:T(8,128)(2,1)}) conditional(s32[]{:T(128)} %bitcast.2, () %tuple.278, bf16[128,256]{1,0:T(8,128)(2,1)} %get-tuple-element.200, bf16[128,512]{1,0:T(8,128)(2,1)} %get-tuple-element.201, bf16[128,256]{1,0:T(8,128)(2,1)} %get-tuple-element.200, ...), branch_computations={%region_0.0_spmd, %region_1.2_spmd, %region_2.3_spmd, %region_3.4_... | conditional | bytes 524336 | solution.py:289
  13.3 5.8 %collective-permute-start.13 = (bf16[128,512]{1,0:T(8,128)(2,1)}, bf16[128,512]{1,0:T(8,128)(2,1)}, u32[]{:S(2)}, u32[]{:S(2)}) collective-permute-start(bf16[128,512]{1,0:T(8,128)(2,1)} %param.14), channel_id=1, source_target_pairs={{0,14},{2,12},{4,10},{6,8},{8,6},{10,4},{12,2},{14,0},{1,15},{3,13... | collective-permute-start | bytes 393224 | tf_op jit(solution)/shard_map/cond/branch_14_fun/ppermute | solution.py:302
  19.0 3.6 %collective-permute-done.13 = bf16[128,512]{1,0:T(8,128)(2,1)} collective-permute-done((bf16[128,512]{1,0:T(8,128)(2,1)}, bf16[128,512]{1,0:T(8,128)(2,1)}, u32[]{:S(2)}, u32[]{:S(2)}) %collective-permute-start.13) | collective-permute-done | bytes 131104 | tf_op jit(solution)/shard_map/cond/branch_14_fun/ppermute | solution.py:302
  22.7 6.1 %conditional.8 = (bf16[128,512]{1,0:T(8,128)(2,1)}) conditional(s32[]{:T(128)} %bitcast.6, () %tuple.280, bf16[128,256]{1,0:T(8,128)(2,1)} %get-tuple-element.203, bf16[128,512]{1,0:T(8,128)(2,1)} %get-tuple-element.204, bf16[128,256]{1,0:T(8,128)(2,1)} %get-tuple-element.203, ...), branch_computations={%region_30.31_spmd, %region_31.32_spmd, %region_32.33_spmd, %regio... | conditional | bytes 524336 | solution.py:289
  23.3 0.1 collective-permute-start.31
  23.3 5.4 %collective-permute-done.31 = bf16[128,512]{1,0:T(8,128)(2,1)} collective-permute-done((bf16[128,512]{1,0:T(8,128)(2,1)}, bf16[128,512]{1,0:T(8,128)(2,1)}, u32[]{:S(2)}, u32[]{:S(2)}) %collective-permute-start.31) | collective-permute-done | bytes 131104 | tf_op jit(solution)/shard_map/cond/branch_4_fun/ppermute | solution.py:302
  28.8 7.7 %conditional.7 = (bf16[128,512]{1,0:T(8,128)(2,1)}) conditional(s32[]{:T(128)} %bitcast.4, () %tuple.279, bf16[128,256]{1,0:T(8,128)(2,1)} %get-tuple-element.203, bf16[128,512]{1,0:T(8,128)(2,1)} %get-tuple-element.204, bf16[128,256]{1,0:T(8,128)(2,1)} %get-tuple-element.203, ...), branch_computations={%region_15.16_spmd, %region_16.17_spmd, %region_17.18_spmd, %regio... | conditional | bytes 524336 | solution.py:289
  29.4 0.1 collective-permute-start.24
  29.5 6.3 %collective-permute-done.24 = bf16[128,256]{1,0:T(8,128)(2,1)S(1)} collective-permute-done((bf16[128,256]{1,0:T(8,128)(2,1)}, bf16[128,256]{1,0:T(8,128)(2,1)S(1)}, u32[]{:S(2)}, u32[]{:S(2)}) %collective-permute-start.24) | collective-permute-done | bytes 65568 | tf_op jit(solution)/shard_map/cond/branch_11_fun/ppermute | solution.py:297
  35.8 0.7 pad.97
  36.4 1.0 %select_convert_fusion = bf16[128,512]{1,0:T(8,128)(2,1)S(1)} fusion(bf16[128,512]{1,0:T(8,128)(2,1)S(1)} %copy-done.2, bf16[128,512]{1,0:T(8,128)(2,1)} %get-tuple-element.217.old_2, bf16[128,512]{1,0:T(8,128)(2,1)} %get-tuple-element.218.old_3, bf16[128,512]{1,0:T(8,128)(2,1)} %get-tuple-element.216.old_1, pred[]{:T(512)} %bitcast.5, pred[]{:T(512)} %bitcast.3, ...), kind=kLoop, calls=%fused_computation | loop fusion | flops 655360 | bytes 655875 | tf_op jit(solution)/shard_map/convert_element_type | solution.py:343
  37.5 2.0 %all-gather = bf16[256,512]{1,0:T(8,128)(2,1)S(1)} all-gather(bf16[128,512]{1,0:T(8,128)(2,1)S(1)} %select_convert_fusion), channel_id=2, replica_groups=mesh['runs'=2,'sec'=8,'env'=2] {'env'}, dimensions={0}, use_global_device_ids=true | all-gather | bytes 393216 | tf_op jit(solution)/shard_map/all_gather | solution.py:345
  39.5 0.9 copy-done.3
  40.4 2.3 %shard_map.69 = (bf16[128,512]{1,0:T(8,128)(2,1)}, bf16[128,256]{1,0:T(8,128)(2,1)}, bf16[128,512]{1,0:T(8,128)(2,1)}, bf16[128,256]{1,0:T(8,128)(2,1)}, f32[128,512]{1,0:T(8,128)S(1)}, /*index=5*/f32[8,128]{1,0:T(8,128)S(1)}) custom-call(s32[8]{0:T(128)S(1)} %copy-done.6, s32[8]{0:T(128)S(1)} %copy-done.7, bf16[2,128,512]{2,1,0:T(8,128)(2,1)S(1)} %copy-done.1, ...), custom_call_target="tpu_custom_call" | custom-call | tf_op jit(solution)/shard_map/pallas_call | solution.py:346
  42.7 0.7 copy-done.4
  43.4 31.9 %all-gather.1 = f32[64,128]{1,0:T(8,128)S(1)} all-gather(f32[8,128]{1,0:T(8,128)S(1)} %get-tuple-element.206), channel_id=3, replica_groups=mesh['runs'=2,'sec'=8,'env'=2] {'sec'}, dimensions={0}, use_global_device_ids=true | all-gather | bytes 36864 | tf_op jit(solution)/shard_map/all_gather | solution.py:353
  75.3 8.8 %conditional.9 = (bf16[128,512]{1,0:T(8,128)(2,1)}) conditional(s32[]{:T(128)} %bitcast.2, () %tuple.281, bf16[128,256]{1,0:T(8,128)(2,1)} %get-tuple-element.208, bf16[128,512]{1,0:T(8,128)(2,1)} %get-tuple-element.209, bf16[128,256]{1,0:T(8,128)(2,1)} %get-tuple-element.208, ...), branch_computations={%region_45.46_spmd, %region_46.47_spmd, %region_47.48_spmd, %regio... | conditional | bytes 524336 | solution.py:289
  76.0 4.8 %collective-permute-start.55 = (bf16[128,512]{1,0:T(8,128)(2,1)}, bf16[128,512]{1,0:T(8,128)(2,1)}, u32[]{:S(2)}, u32[]{:S(2)}) collective-permute-start(bf16[128,512]{1,0:T(8,128)(2,1)} %param.59), channel_id=1, source_target_pairs={{0,14},{2,12},{4,10},{6,8},{8,6},{10,4},{12,2},{14,0},{1,15},{3,13... | collective-permute-start | bytes 393224 | tf_op jit(solution)/shard_map/cond/branch_14_fun/ppermute | solution.py:302
  80.8 3.3 %collective-permute-done.55 = bf16[128,512]{1,0:T(8,128)(2,1)} collective-permute-done((bf16[128,512]{1,0:T(8,128)(2,1)}, bf16[128,512]{1,0:T(8,128)(2,1)}, u32[]{:S(2)}, u32[]{:S(2)}) %collective-permute-start.55) | collective-permute-done | bytes 131104 | tf_op jit(solution)/shard_map/cond/branch_14_fun/ppermute | solution.py:302
  84.1 5.9 %conditional.11 = (bf16[128,512]{1,0:T(8,128)(2,1)}) conditional(s32[]{:T(128)} %bitcast.6, () %tuple.283, bf16[128,256]{1,0:T(8,128)(2,1)} %get-tuple-element.210, bf16[128,512]{1,0:T(8,128)(2,1)} %get-tuple-element.211, bf16[128,256]{1,0:T(8,128)(2,1)} %get-tuple-element.210, ...), branch_computations={%region_75.76_spmd, %region_76.77_spmd, %region_77.78_spmd, %regio... | conditional | bytes 524336 | solution.py:289
  84.7 0.1 collective-permute-start.73
  84.8 5.3 %collective-permute-done.73 = bf16[128,512]{1,0:T(8,128)(2,1)} collective-permute-done((bf16[128,512]{1,0:T(8,128)(2,1)}, bf16[128,512]{1,0:T(8,128)(2,1)}, u32[]{:S(2)}, u32[]{:S(2)}) %collective-permute-start.73) | collective-permute-done | bytes 131104 | tf_op jit(solution)/shard_map/cond/branch_4_fun/ppermute | solution.py:302
  90.0 7.7 %conditional.10 = (bf16[128,512]{1,0:T(8,128)(2,1)}) conditional(s32[]{:T(128)} %bitcast.4, () %tuple.282, bf16[128,256]{1,0:T(8,128)(2,1)} %get-tuple-element.210, bf16[128,512]{1,0:T(8,128)(2,1)} %get-tuple-element.211, bf16[128,256]{1,0:T(8,128)(2,1)} %get-tuple-element.210, ...), branch_computations={%region_60.61_spmd, %region_61.62_spmd, %region_62.63_spmd, %regio... | conditional | bytes 524336 | solution.py:289
  90.7 0.1 collective-permute-start.66
  90.8 6.3 %collective-permute-done.66 = bf16[128,256]{1,0:T(8,128)(2,1)S(1)} collective-permute-done((bf16[128,256]{1,0:T(8,128)(2,1)}, bf16[128,256]{1,0:T(8,128)(2,1)S(1)}, u32[]{:S(2)}, u32[]{:S(2)}) %collective-permute-start.66) | collective-permute-done | bytes 65568 | tf_op jit(solution)/shard_map/cond/branch_11_fun/ppermute | solution.py:297
  97.0 0.7 pad.118
  97.7 2.2 %shard_map.70 = bf16[128,512]{1,0:T(8,128)(2,1)} custom-call(s32[8]{0:T(128)S(1)} %copy-done.6, s32[8]{0:T(128)S(1)} %copy-done.7, f32[8,8,128]{2,1,0:T(8,128)S(1)} %bitcast.12, bf16[128,512]{1,0:T(8,128)(2,1)S(1)} %copy-done.2, f32[128,512]{1,0:T(8,128)S(1)} %copy-done.5, bf16[128,512]{1,0:T(8,128)(2,1)} %get-tuple-element.216.old_1, ...), custom_call_target="tpu_custom_call" | custom-call | tf_op jit(solution)/shard_map/pallas_call | solution.py:357
  (15 shorter events, 0.0 us)
Async XLA Ops:
  8.6 27.9 %copy-start.2 = (bf16[128,512]{1,0:T(8,128)(2,1)S(1)}, bf16[128,512]{1,0:T(8,128)(2,1)}, u32[]{:S(2)}) copy-start(bf16[128,512]{1,0:T(8,128)(2,1)} %get-tuple-element.198.stay) | copy-start | bytes 393220
  8.6 30.9 %copy-start = (bf16[1,3,1024,512]{3,2,1,0:T(8,128)(2,1)S(1)}, bf16[1,3,1024,512]{3,2,1,0:T(8,128)(2,1)}, u32[]{:S(2)}) copy-start(bf16[1,3,1024,512]{3,2,1,0:T(8,128)(2,1)} %left.3) | copy-start | bytes 9437188
  8.6 30.9 %copy-start.1 = (bf16[2,128,512]{2,1,0:T(8,128)(2,1)S(1)}, bf16[2,128,512]{2,1,0:T(8,128)(2,1)}, u32[]{:S(2)}) copy-start(bf16[2,128,512]{2,1,0:T(8,128)(2,1)} %all_gather.13.amps) | copy-start | bytes 786436
  8.6 30.9 %copy-start.6 = (s32[8]{0:T(128)S(1)}, s32[8]{0:T(128)}, u32[]{:S(2)}) copy-start(s32[8]{0:T(128)} %widths.5) | copy-start | bytes 100
  8.6 30.9 %copy-start.7 = (s32[8]{0:T(128)S(1)}, s32[8]{0:T(128)}, u32[]{:S(2)}) copy-start(s32[8]{0:T(128)} %holders.5) | copy-start | bytes 100
  13.3 9.4 %collective-permute-start.13 = (bf16[128,512]{1,0:T(8,128)(2,1)}, bf16[128,512]{1,0:T(8,128)(2,1)}, u32[]{:S(2)}, u32[]{:S(2)}) collective-permute-start(bf16[128,512]{1,0:T(8,128)(2,1)} %param.14), channel_id=1, source_target_pairs={{0,14},{2,12},{4,10},{6,8},{8,6},{10,4},{12,2},{14,0},{1,15},{3,13... | collective-permute-start | bytes 393224 | tf_op jit(solution)/shard_map/cond/branch_14_fun/ppermute | solution.py:302
  23.3 5.5 %collective-permute-start.31 = (bf16[128,512]{1,0:T(8,128)(2,1)}, bf16[128,512]{1,0:T(8,128)(2,1)}, u32[]{:S(2)}, u32[]{:S(2)}) collective-permute-start(bf16[128,512]{1,0:T(8,128)(2,1)} %param.34), channel_id=1, source_target_pairs={{0,4},{2,6},{4,0},{6,2},{8,12},{10,14},{12,8},{14,10},{1,5},{3,7},... | collective-permute-start | bytes 393224 | tf_op jit(solution)/shard_map/cond/branch_4_fun/ppermute | solution.py:302
  29.4 6.3 %collective-permute-start.24 = (bf16[128,256]{1,0:T(8,128)(2,1)}, bf16[128,256]{1,0:T(8,128)(2,1)S(1)}, u32[]{:S(2)}, u32[]{:S(2)}) collective-permute-start(bf16[128,256]{1,0:T(8,128)(2,1)} %param.26), channel_id=1, source_target_pairs={{0,12},{2,14},{4,8},{6,10},{8,4},{10,6},{12,0},{14,2},{1,13},{3,15... | collective-permute-start | bytes 196616 | tf_op jit(solution)/shard_map/cond/branch_11_fun/ppermute | solution.py:297
  37.4 2.0 %copy-start.8 = (bf16[128,512]{1,0:T(8,128)(2,1)}, bf16[128,512]{1,0:T(8,128)(2,1)S(1)}, u32[]{:S(2)}) copy-start(bf16[128,512]{1,0:T(8,128)(2,1)S(1)} %select_convert_fusion) | copy-start | bytes 393220
  39.5 0.9 copy-start.3
  42.7 0.7 copy-start.4
  43.4 54.3 %copy-start.5 = (f32[128,512]{1,0:T(8,128)S(1)}, f32[128,512]{1,0:T(8,128)}, u32[]{:S(2)}) copy-start(f32[128,512]{1,0:T(8,128)} %copy-done.4) | copy-start | bytes 786436
  76.0 8.0 %collective-permute-start.55 = (bf16[128,512]{1,0:T(8,128)(2,1)}, bf16[128,512]{1,0:T(8,128)(2,1)}, u32[]{:S(2)}, u32[]{:S(2)}) collective-permute-start(bf16[128,512]{1,0:T(8,128)(2,1)} %param.59), channel_id=1, source_target_pairs={{0,14},{2,12},{4,10},{6,8},{8,6},{10,4},{12,2},{14,0},{1,15},{3,13... | collective-permute-start | bytes 393224 | tf_op jit(solution)/shard_map/cond/branch_14_fun/ppermute | solution.py:302
  84.7 5.3 %collective-permute-start.73 = (bf16[128,512]{1,0:T(8,128)(2,1)}, bf16[128,512]{1,0:T(8,128)(2,1)}, u32[]{:S(2)}, u32[]{:S(2)}) collective-permute-start(bf16[128,512]{1,0:T(8,128)(2,1)} %param.79), channel_id=1, source_target_pairs={{0,4},{2,6},{4,0},{6,2},{8,12},{10,14},{12,8},{14,10},{1,5},{3,7},... | collective-permute-start | bytes 393224 | tf_op jit(solution)/shard_map/cond/branch_4_fun/ppermute | solution.py:302
  90.7 6.3 %collective-permute-start.66 = (bf16[128,256]{1,0:T(8,128)(2,1)}, bf16[128,256]{1,0:T(8,128)(2,1)S(1)}, u32[]{:S(2)}, u32[]{:S(2)}) collective-permute-start(bf16[128,256]{1,0:T(8,128)(2,1)} %param.71), channel_id=1, source_target_pairs={{0,12},{2,14},{4,8},{6,10},{8,4},{10,6},{12,0},{14,2},{1,13},{3,15... | collective-permute-start | bytes 196616 | tf_op jit(solution)/shard_map/cond/branch_11_fun/ppermute | solution.py:297

commit v5 on v1

--- a/solution.py
+++ b/solution.py
@@ -1,6 +1,8 @@
 import jax
 import jax.numpy as jnp
 from jax import lax
+from jax.experimental import pallas as pl
+from jax.experimental.pallas import tpu as pltpu
 from jax.sharding import PartitionSpec as P
 
 QDOWN = 4
@@ -61,7 +63,7 @@
     return total
 
 
-def on_device(amplitudes, widths, holders, left_env, right_env):
+def on_device_any(amplitudes, widths, holders, left_env, right_env):
     slots_dev, right_dim, half_width = amplitudes.shape
     assert slots_dev == 1
     n_slots = holders.shape[0]
@@ -107,6 +109,308 @@
     return first[None], second[None]
 
 
+LANES = 128
+TAG = 16
+
+
+def live_columns(widths, holders, half, side):
+    width = widths[holders[lax.axis_index("sec")]]
+    columns = side * half + lax.broadcasted_iota(jnp.int32, (1, half), 1)
+    return columns < width
+
+
+def start_copies(left, left_vmem, sems):
+    copies = []
+    for term in (1, 2, 0):
+        copy = pltpu.make_async_copy(left.at[0, term], left_vmem.at[term], sems.at[term])
+        copy.start()
+        copies.append((term, copy))
+    return copies
+
+
+def apply_term(right, left, vector, term):
+    products = jnp.dot(right[term], vector, preferred_element_type=jnp.float32)
+    return jnp.dot(products.astype(jnp.bfloat16), left, preferred_element_type=jnp.float32)
+
+
+def first_kernel(widths, holders, amps, right, left, *rest):
+    slots = holders.shape[0]
+    pieces = rest[:slots]
+    stay, left_vmem, block_vmem, sems = rest[slots:]
+    half = amps.shape[2]
+    rows = pieces[0].shape[1]
+    me = lax.axis_index("sec")
+    copies = start_copies(left, left_vmem, sems)
+    vector = jnp.concatenate(
+        [
+            jnp.where(live_columns(widths, holders, half, h), amps[h], jnp.zeros_like(amps[h]))
+            for h in range(2)
+        ],
+        axis=1,
+    )
+    for term, copy in copies:
+        copy.wait()
+        block = apply_term(right, left_vmem[term], vector, term).astype(jnp.bfloat16)
+        if term == 0:
+            stay[...] = block
+        else:
+            block_vmem[...] = block.reshape(block_vmem.shape)
+            for offset in range(slots):
+                pieces[offset][term - 1] = block_vmem[me ^ offset]
+
+
+def fill_slots(holders, slot_of):
+    for s in range(holders.shape[0]):
+        slot_of[holders[s]] = jnp.int32(s)
+
+
+def sources_of(holders, slot_of, target):
+    sector = holders[target]
+    has = (sector >= QDOWN, sector % QDOWN > 0)
+    source = (slot_of[sector & (QDOWN - 1)], slot_of[jnp.maximum(sector - 1, 0)])
+    return has, source
+
+
+def merge_kernel(holders, *rest):
+    slots = holders.shape[0]
+    pieces, outs = rest[:slots], rest[slots : 2 * slots]
+    table, slot_of = rest[2 * slots :]
+    me = lax.axis_index("sec")
+    fill_slots(holders, slot_of)
+    for offset in range(slots):
+        table[me ^ offset] = pieces[offset][...]
+    for offset in range(slots):
+        has, source = sources_of(holders, slot_of, me ^ offset)
+        total = 0.0
+        for i in range(2):
+            block = table[source[i], i].astype(jnp.float32)
+            total = total + jnp.where(has[i], block, 0.0)
+        outs[offset][...] = total.astype(jnp.bfloat16)
+
+
+def sum_kernel(widths, holders, stay, *rest):
+    *pieces, first = rest
+    half = stay.shape[1]
+    rows = pieces[0].shape[0]
+    me = lax.axis_index("sec")
+    live = live_columns(widths, holders, half, lax.axis_index("env"))
+    for offset, piece in enumerate(pieces):
+        place = pl.ds(pl.multiple_of((me ^ offset) * rows, rows), rows)
+        total = stay[place, :].astype(jnp.float32) + piece[...].astype(jnp.float32)
+        first[place, :] = jnp.where(live, total, 0.0).astype(jnp.bfloat16)
+
+
+def total_of(array):
+    return jnp.sum(jnp.sum(array, axis=0, keepdims=True), axis=1, keepdims=True)
+
+
+def make_tag(values, me):
+    row = lax.broadcasted_iota(jnp.int32, (TAG, LANES), 0)
+    lane = lax.broadcasted_iota(jnp.int32, (TAG, LANES), 1)
+    spread = jnp.zeros((TAG, LANES), jnp.float32)
+    for place, value in enumerate(values):
+        spread = jnp.where(row // 3 == place, value, spread)
+    high = spread.astype(jnp.bfloat16).astype(jnp.float32)
+    middle = (spread - high).astype(jnp.bfloat16).astype(jnp.float32)
+    low = spread - high - middle
+    parts = jnp.where(row % 3 == 0, high, jnp.where(row % 3 == 1, middle, low))
+    return jnp.where((lane == me) & (row < 3 * len(values)), parts, 0.0).astype(jnp.bfloat16)
+
+
+def second_kernel(widths, holders, amps, first, right, left, *rest):
+    slots = holders.shape[0]
+    pieces = rest[:slots]
+    stay, block_vmem = rest[slots:]
+    half = amps.shape[2]
+    rows = block_vmem.shape[1]
+    chunks = half // LANES
+    me = lax.axis_index("sec")
+    basis = [
+        jnp.where(
+            live_columns(widths, holders, half, h), amps[h].astype(jnp.float32), 0.0
+        )
+        for h in range(2)
+    ]
+    firsts = [first[h].astype(jnp.float32) for h in range(2)]
+    overlap = total_of(basis[0] * firsts[0]) + total_of(basis[1] * firsts[1])
+    norm = total_of(basis[0] * basis[0]) + total_of(basis[1] * basis[1])
+    quotient = jnp.where(norm > 0, overlap / jnp.where(norm > 0, norm, 1.0), 0.0)
+    deflated = [firsts[h] - quotient * basis[h] for h in range(2)]
+    rest_norm = total_of(deflated[0] * deflated[0]) + total_of(deflated[1] * deflated[1])
+    vector = jnp.concatenate(deflated, axis=1).astype(jnp.bfloat16)
+    tag = make_tag((overlap, norm, quotient, rest_norm), me)
+    for piece in pieces:
+        piece[pl.ds(2 * chunks * rows, TAG), :] = tag
+    for term in (1, 2, 0):
+        block = apply_term(right, left[0, term], vector, term)
+        if term == 0:
+            stay[...] = block
+        else:
+            block_vmem[...] = block.astype(jnp.bfloat16).reshape(block_vmem.shape)
+            for offset in range(slots):
+                part = block_vmem[me ^ offset]
+                for c in range(chunks):
+                    place = pl.ds(((term - 1) * chunks + c) * rows, rows)
+                    pieces[offset][place, :] = part[:, c * LANES : (c + 1) * LANES]
+
+
+def mix_kernel(widths, holders, *rest):
+    slots = holders.shape[0]
+    old, new, outs = rest[:slots], rest[slots : 2 * slots], rest[2 * slots : 3 * slots]
+    factors, old_table, new_table, slot_of = rest[3 * slots :]
+    rows, half = outs[0].shape
+    chunks = half // LANES
+    me = lax.axis_index("sec")
+    fill_slots(holders, slot_of)
+    tag = jnp.zeros((TAG, LANES), jnp.float32)
+    for offset in range(slots):
+        old_table[me ^ offset] = old[offset][...]
+        new_table[me ^ offset] = new[offset][...]
+        tag = tag + new[offset][pl.ds(2 * chunks * rows, TAG), :].astype(jnp.float32)
+    total = jnp.int32(0)
+    for s in range(slots):
+        total = total + widths[s]
+    live_count = slots * rows * total.astype(jnp.float32)
+
+    def value(place):
+        parts = [tag[3 * place + i : 3 * place + i + 1, :] for i in range(3)]
+        return parts[0] + parts[1] + parts[2]
+
+    overlaps, norms, quotients, rests = (value(place) for place in range(4))
+    quotient = total_of(overlaps) / total_of(norms)
+    lane = lax.broadcasted_iota(jnp.int32, (1, LANES), 1)
+    shifts = jnp.where(lane < slots, quotients - quotient, 0.0)
+    resid_norm = total_of(rests + shifts * shifts * norms)
+    scale = lax.rsqrt(resid_norm / live_count + 1e-06)
+
+    def shift_of(slot):
+        return total_of(jnp.where(lane == slot, shifts, 0.0))
+
+    row = lax.broadcasted_iota(jnp.int32, factors.shape, 0)
+    factors[...] = jnp.where(row == 0, scale, scale * shift_of(me))
+    for offset in range(slots):
+        has, source = sources_of(holders, slot_of, me ^ offset)
+        total = 0.0
+        for i in range(2):
+            block = jnp.concatenate(
+                [
+                    new_table[source[i], pl.ds((i * chunks + c) * rows, rows), :]
+                    for c in range(chunks)
+                ],
+                axis=1,
+            ).astype(jnp.float32)
+            block = block + shift_of(source[i]) * old_table[source[i], i].astype(jnp.float32)
+            total = total + jnp.where(has[i], block, 0.0)
+        outs[offset][...] = (scale * total).astype(jnp.bfloat16)
+
+
+def final_kernel(widths, holders, factors, stay, stay_2, *rest):
+    *pieces, second = rest
+    half = stay.shape[1]
+    rows = pieces[0].shape[0]
+    me = lax.axis_index("sec")
+    live = live_columns(widths, holders, half, lax.axis_index("env"))
+    scale, shift = factors[0:1, 0:1], factors[1:2, 0:1]
+    for offset, piece in enumerate(pieces):
+        place = pl.ds(pl.multiple_of((me ^ offset) * rows, rows), rows)
+        total = scale * stay_2[place, :] + shift * stay[place, :].astype(jnp.float32)
+        total = total + piece[...].astype(jnp.float32)
+        second[place, :] = jnp.where(live, total, 0.0).astype(jnp.bfloat16)
+
+
+SMEM = pl.BlockSpec(memory_space=pltpu.SMEM)
+VMEM = pl.BlockSpec(memory_space=pltpu.VMEM)
+HBM = pl.BlockSpec(memory_space=pltpu.HBM)
+SMALL = pltpu.CompilerParams(vmem_limit_bytes=16 * 1024 * 1024)
+LARGE = pltpu.CompilerParams(vmem_limit_bytes=61 * 1024 * 1024)
+
+
+def swap_all(pieces):
+    slots = len(pieces)
+    return [pieces[0]] + [
+        lax.ppermute(pieces[offset], "sec", [(i, i ^ offset) for i in range(slots)])
+        for offset in range(1, slots)
+    ]
+
+
+def on_device(amplitudes, widths, holders, left_env, right_env):
+    slots_dev, right_dim, half = amplitudes.shape
+    slots = holders.shape[0]
+    assert slots_dev == 1
+    if slots != 2 * QDOWN:
+        return on_device_any(amplitudes, widths, holders, left_env, right_env)
+    rows = right_dim // slots
+    block = jax.ShapeDtypeStruct((right_dim, half), jnp.bfloat16)
+    wide = jax.ShapeDtypeStruct((right_dim, half), jnp.float32)
+    pair = jax.ShapeDtypeStruct((2, rows, half), jnp.bfloat16)
+    single = jax.ShapeDtypeStruct((rows, half), jnp.bfloat16)
+    tagged = jax.ShapeDtypeStruct((2 * rows * half // LANES + TAG, LANES), jnp.bfloat16)
+    factor_shape = jax.ShapeDtypeStruct((8, LANES), jnp.float32)
+    split = pltpu.VMEM((slots, rows, half), jnp.bfloat16)
+    slot_table = pltpu.SMEM((slots,), jnp.int32)
+
+    amps_full = lax.all_gather(amplitudes[0], "env")
+    *pieces, stay = pl.pallas_call(
+        first_kernel,
+        out_shape=(pair,) * slots + (block,),
+        in_specs=[SMEM, SMEM, VMEM, VMEM, HBM],
+        out_specs=(VMEM,) * (slots + 1),
+        scratch_shapes=[
+            pltpu.VMEM(left_env.shape[1:], jnp.bfloat16),
+            split,
+            pltpu.SemaphoreType.DMA((left_env.shape[1],)),
+        ],
+        compiler_params=LARGE,
+    )(widths, holders, amps_full, right_env, left_env)
+    old = swap_all(pieces)
+    merged = pl.pallas_call(
+        merge_kernel,
+        out_shape=(single,) * slots,
+        in_specs=[SMEM] + [VMEM] * slots,
+        out_specs=(VMEM,) * slots,
+        scratch_shapes=[pltpu.VMEM((slots, *pair.shape), jnp.bfloat16), slot_table],
+        compiler_params=SMALL,
+    )(holders, *old)
+    first = pl.pallas_call(
+        sum_kernel,
+        out_shape=block,
+        in_specs=[SMEM, SMEM] + [VMEM] * (slots + 1),
+        out_specs=VMEM,
+        compiler_params=SMALL,
+    )(widths, holders, stay, *swap_all(merged))
+
+    first_full = lax.all_gather(first, "env")
+    *pieces, stay_2 = pl.pallas_call(
+        second_kernel,
+        out_shape=(tagged,) * slots + (wide,),
+        in_specs=[SMEM, SMEM, VMEM, VMEM, VMEM, VMEM],
+        out_specs=(VMEM,) * (slots + 1),
+        scratch_shapes=[split],
+        compiler_params=SMALL,
+    )(widths, holders, amps_full, first_full, right_env, left_env)
+    new = swap_all(pieces)
+    *mixed, factors = pl.pallas_call(
+        mix_kernel,
+        out_shape=(single,) * slots + (factor_shape,),
+        in_specs=[SMEM, SMEM] + [VMEM] * (2 * slots),
+        out_specs=(VMEM,) * (slots + 1),
+        scratch_shapes=[
+            pltpu.VMEM((slots, *pair.shape), jnp.bfloat16),
+            pltpu.VMEM((slots, *tagged.shape), jnp.bfloat16),
+            slot_table,
+        ],
+        compiler_params=SMALL,
+    )(widths, holders, *old, *new)
+    second = pl.pallas_call(
+        final_kernel,
+        out_shape=block,
+        in_specs=[SMEM, SMEM] + [VMEM] * (slots + 3),
+        out_specs=VMEM,
+        compiler_params=SMALL,
+    )(widths, holders, factors, stay, stay_2, *swap_all(mixed))
+    return first[None], second[None]
+
+
 def solution(mesh):
     in_specs = (
         P(("runs", "sec"), None, "env"),

time: 121 us -> 84 us (0.69)
  local copies, waits for them, and re-layouts: 31 us -> 3.58 us
  other arithmetic: 22.9 us -> 0 us
  starting transfers between devices: 29.4 us -> 45.8 us
  Pallas kernels: 0 us -> 10.1 us
  between operations: 7.35 us -> 0.74 us
  matrix products: 5.8 us -> 0 us
  blocking collectives: 4.08 us -> 6.12 us
  waiting for transfers between devices: 18.9 us -> 17.2 us
    ppermute x7 -> x28, starting transfers between devices: 11.2 us -> 45.8 us  [swap_all(): lax.ppermute(pieces[offset], 'sec', [(i, i ^ offset) for i in range(slots)])]
    all_to_all x4 -> x0, waiting for transfers between devices: 18.9 us -> none  [the longest x2 10.2 us: spread(): return lax.all_to_all(pieces, 'sec', split_axis=0, concat_axis=0)]
    all_to_all x4 -> x0, starting transfers between devices: 18.2 us -> none  [the longest x2 11.2 us: spread(): return lax.all_to_all(pieces, 'sec', split_axis=0, concat_axis=0)]
    ppermute x7 -> x28, waiting for transfers between devices: 0.02 us -> 17.2 us  [swap_all(): lax.ppermute(pieces[offset], 'sec', [(i, i ^ offset) for i in range(slots)])]
    pallas_call x0 -> x6, Pallas kernels: none -> 10.1 us  [the longest x1 4.22 us: on_device(): pl.pallas_call(first_kernel, out_shape=(pair,) * slots + (block,), in_spe...]
    gather x6 -> x0, local copies, waits for them, and re-layouts: 9.57 us -> none  [the longest x4 8.29 us: merge(): picked = received[source, term]]
    convert_element_type x6 -> x0, other arithmetic: 7.96 us -> none  [the longest x1 1.89 us: on_device(): jnp.where(live, stay_2 + arrived_2.astype(jnp.float32), 0.0)]
    slice x4 -> x0, local copies, waits for them, and re-layouts: 6.24 us -> none  [the longest x2 3.45 us: on_device(): received = spread(outgoing[1:], n_slots)]
  transfers between devices with their start and end apart: 11 -> 28, of which waited for: 4 -> 10; matrix products, arithmetic and copies ran while one was open for 14% -> 0% of each run, Pallas kernels for 0% -> 0%
where the time goes in v5:
time: 84 us; the launch traced here: 83.6 us
  starting transfers between devices  45.8 us (55%)
  waiting for transfers between devices  17.2 us (20%)
  Pallas kernels  10.1 us (12%)
  blocking collectives  6.12 us (7%)
  local copies, waits for them, and re-layouts  3.58 us (4%)
    ppermute x28, starting transfers between devices, swap_all(): lax.ppermute(pieces[offset], 'sec', [(i, i ^ offset) for i in range(slots)])  45.8 us
    ppermute x28, waiting for transfers between devices, swap_all(): lax.ppermute(pieces[offset], 'sec', [(i, i ^ offset) for i in range(slots)])  17.2 us
    pallas_call x1, Pallas kernels, on_device(): pl.pallas_call(first_kernel, out_shape=(pair,) * slots + (block,), in_spe...  4.22 us
    all_gather x1, blocking collectives, on_device(): amps_full = lax.all_gather(amplitudes[0], 'env')  3.93 us
    unnamed x18, local copies, waits for them, and re-layouts  3.58 us
    all_gather x1, blocking collectives, on_device(): first_full = lax.all_gather(first, 'env')  2.19 us
    pallas_call x1, Pallas kernels, on_device(): pl.pallas_call(second_kernel, out_shape=(tagged,) * slots + (wide,), in_s...  1.82 us
  transfers between devices with their start and end apart: 28, of which 10 were waited for; matrix products, arithmetic and copies ran while one was open for 0% of the time, Pallas kernels for 0%

profile of v5, /device:TPU:0, one launch (start us, length us, event | category | flops | bytes accessed | tf_op | source)
XLA Modules:
  0.0 83.6 jit_solution(12955607322324134337)
XLA Ops:
  0.7 3.9 %all_gather.7.amps = bf16[2,128,512]{2,1,0:T(8,128)(2,1)} all-gather(bf16[1,128,512]{2,1,0:T(8,128)(2,1)} %param.5), channel_id=1, replica_groups=mesh['runs'=2,'sec'=8,'env'=2] {'env'}, dimensions={0}, use_global_device_ids=true | all-gather | bytes 393216 | tf_op jit(solution)/shard_map/all_gather | solution.py:352
  4.6 4.2 %shard_map.68 = (bf16[2,16,512]{2,1,0:T(8,128)(2,1)}, bf16[2,16,512]{2,1,0:T(8,128)(2,1)}, bf16[2,16,512]{2,1,0:T(8,128)(2,1)}, bf16[2,16,512]{2,1,0:T(8,128)(2,...) custom-call(s32[8]{0:T(128)} %widths.9, ...), custom_call_target="tpu_custom_call" | custom-call | tf_op jit(solution)/shard_map/pallas_call | solution.py:353
  8.8 2.7 %collective-permute-start = (bf16[2,16,512]{2,1,0:T(8,128)(2,1)}, bf16[2,16,512]{2,1,0:T(8,128)(2,1)S(1)}, u32[]{:S(2)}, u32[]{:S(2)}) collective-permute-start(bf16[2,16,512]{2,1,0:T(8,128)(2,1)} %get-tuple-element.39), channel_id=1, source_target_pairs={{0,2},{2,0},{4,6},{6,4},{8,10},{10,8},{12,14},{14,12},{1,3},{3,1},... | collective-permute-start | bytes 98312 | tf_op jit(solution)/shard_map/ppermute | solution.py:331
  11.5 1.6 %collective-permute-start.1 = (bf16[2,16,512]{2,1,0:T(8,128)(2,1)}, bf16[2,16,512]{2,1,0:T(8,128)(2,1)S(1)}, u32[]{:S(2)}, u32[]{:S(2)}) collective-permute-start(bf16[2,16,512]{2,1,0:T(8,128)(2,1)} %get-tuple-element.40), channel_id=1, source_target_pairs={{0,4},{2,6},{4,0},{6,2},{8,12},{10,14},{12,8},{14,10},{1,5},{3,7},... | collective-permute-start | bytes 98312 | tf_op jit(solution)/shard_map/ppermute | solution.py:331
  13.1 3.0 %collective-permute-start.3 = (bf16[2,16,512]{2,1,0:T(8,128)(2,1)}, bf16[2,16,512]{2,1,0:T(8,128)(2,1)S(1)}, u32[]{:S(2)}, u32[]{:S(2)}) collective-permute-start(bf16[2,16,512]{2,1,0:T(8,128)(2,1)} %get-tuple-element.42), channel_id=1, source_target_pairs={{0,8},{2,10},{4,12},{6,14},{8,0},{10,2},{12,4},{14,6},{1,9},{3,11}... | collective-permute-start | bytes 98312 | tf_op jit(solution)/shard_map/ppermute | solution.py:331
  16.1 1.3 %collective-permute-start.4 = (bf16[2,16,512]{2,1,0:T(8,128)(2,1)}, bf16[2,16,512]{2,1,0:T(8,128)(2,1)S(1)}, u32[]{:S(2)}, u32[]{:S(2)}) collective-permute-start(bf16[2,16,512]{2,1,0:T(8,128)(2,1)} %get-tuple-element.43), channel_id=1, source_target_pairs={{0,10},{2,8},{4,14},{6,12},{8,2},{10,0},{12,6},{14,4},{1,11},{3,9}... | collective-permute-start | bytes 98312 | tf_op jit(solution)/shard_map/ppermute | solution.py:331
  17.4 3.6 %collective-permute-start.5 = (bf16[2,16,512]{2,1,0:T(8,128)(2,1)}, bf16[2,16,512]{2,1,0:T(8,128)(2,1)S(1)}, u32[]{:S(2)}, u32[]{:S(2)}) collective-permute-start(bf16[2,16,512]{2,1,0:T(8,128)(2,1)} %get-tuple-element.44), channel_id=1, source_target_pairs={{0,12},{2,14},{4,8},{6,10},{8,4},{10,6},{12,0},{14,2},{1,13},{3,15... | collective-permute-start | bytes 98312 | tf_op jit(solution)/shard_map/ppermute | solution.py:331
  21.1 1.0 %collective-permute-done.4.rest_5_ = bf16[2,16,512]{2,1,0:T(8,128)(2,1)S(1)} collective-permute-done((bf16[2,16,512]{2,1,0:T(8,128)(2,1)}, bf16[2,16,512]{2,1,0:T(8,128)(2,1)S(1)}, u32[]{:S(2)}, u32[]{:S(2)}) %collective-permute-start.4) | collective-permute-done | bytes 32800 | tf_op jit(solution)/shard_map/ppermute | solution.py:331
  22.1 1.4 %collective-permute-done.5.rest_6_ = bf16[2,16,512]{2,1,0:T(8,128)(2,1)S(1)} collective-permute-done((bf16[2,16,512]{2,1,0:T(8,128)(2,1)}, bf16[2,16,512]{2,1,0:T(8,128)(2,1)S(1)}, u32[]{:S(2)}, u32[]{:S(2)}) %collective-permute-start.5) | collective-permute-done | bytes 32800 | tf_op jit(solution)/shard_map/ppermute | solution.py:331
  23.5 4.4 %collective-permute-done.6.rest_7_ = bf16[2,16,512]{2,1,0:T(8,128)(2,1)S(1)} collective-permute-done((bf16[2,16,512]{2,1,0:T(8,128)(2,1)}, bf16[2,16,512]{2,1,0:T(8,128)(2,1)S(1)}, u32[]{:S(2)}, u32[]{:S(2)}) %collective-permute-start.6) | collective-permute-done | bytes 32800 | tf_op jit(solution)/shard_map/ppermute | solution.py:331
  29.8 2.9 %collective-permute-start.9 = (bf16[16,512]{1,0:T(8,128)(2,1)S(1)}, bf16[16,512]{1,0:T(8,128)(2,1)S(1)}, u32[]{:S(2)}, u32[]{:S(2)}) collective-permute-start(bf16[16,512]{1,0:T(8,128)(2,1)S(1)} %get-tuple-element.49), channel_id=1, source_target_pairs={{0,6},{2,4},{4,2},{6,0},{8,14},{10,12},{12,10},{14,8},{1,7},{3,5},... | collective-permute-start | bytes 49160 | tf_op jit(solution)/shard_map/ppermute | solution.py:331
  32.8 2.9 %collective-permute-start.11 = (bf16[16,512]{1,0:T(8,128)(2,1)S(1)}, bf16[16,512]{1,0:T(8,128)(2,1)S(1)}, u32[]{:S(2)}, u32[]{:S(2)}) collective-permute-start(bf16[16,512]{1,0:T(8,128)(2,1)S(1)} %get-tuple-element.51), channel_id=1, source_target_pairs={{0,10},{2,8},{4,14},{6,12},{8,2},{10,0},{12,6},{14,4},{1,11},{3,9}... | collective-permute-start | bytes 49160 | tf_op jit(solution)/shard_map/ppermute | solution.py:331
  36.1 4.4 %collective-permute-start.13 = (bf16[16,512]{1,0:T(8,128)(2,1)S(1)}, bf16[16,512]{1,0:T(8,128)(2,1)S(1)}, u32[]{:S(2)}, u32[]{:S(2)}) collective-permute-start(bf16[16,512]{1,0:T(8,128)(2,1)S(1)} %get-tuple-element.53), channel_id=1, source_target_pairs={{0,14},{2,12},{4,10},{6,8},{8,6},{10,4},{12,2},{14,0},{1,15},{3,13... | collective-permute-start | bytes 49160 | tf_op jit(solution)/shard_map/ppermute | solution.py:331
  41.2 1.3 %collective-permute-done.13.rest_7_ = bf16[16,512]{1,0:T(8,128)(2,1)S(1)} collective-permute-done((bf16[16,512]{1,0:T(8,128)(2,1)S(1)}, bf16[16,512]{1,0:T(8,128)(2,1)S(1)}, u32[]{:S(2)}, u32[]{:S(2)}) %collective-permute-start.13) | collective-permute-done | bytes 16416 | tf_op jit(solution)/shard_map/ppermute | solution.py:331
  42.5 0.9 %copy-done.2 = bf16[128,512]{1,0:T(8,128)(2,1)S(1)} copy-done((bf16[128,512]{1,0:T(8,128)(2,1)S(1)}, bf16[128,512]{1,0:T(8,128)(2,1)}, u32[]{:S(2)}) %copy-start.2) | copy-done | bytes 131096
  43.4 1.2 %shard_map.70 = bf16[128,512]{1,0:T(8,128)(2,1)} custom-call(s32[8]{0:T(128)S(1)} %copy-done.8, s32[8]{0:T(128)S(1)} %copy-done.7, bf16[128,512]{1,0:T(8,128)(2,1)S(1)} %copy-done.2, bf16[16,512]{1,0:T(8,128)(2,1)S(1)} %get-tuple-element.46.rest_0_, bf16[16,512]{1,0:T(8,128)(2,1)S(1)} %collective-permute-done.7.rest_1_, ...), custom_call_target="tpu_custom_call" | custom-call | tf_op jit(solution)/shard_map/pallas_call | solution.py:374
  44.7 2.2 %all-gather = bf16[256,512]{1,0:T(8,128)(2,1)S(1)} all-gather(bf16[128,512]{1,0:T(8,128)(2,1)} %shard_map.70), channel_id=2, replica_groups=mesh['runs'=2,'sec'=8,'env'=2] {'env'}, dimensions={0}, use_global_device_ids=true | all-gather | bytes 393216 | tf_op jit(solution)/shard_map/all_gather | solution.py:382
  46.9 1.9 %copy-done = bf16[1,3,1024,512]{3,2,1,0:T(8,128)(2,1)S(1)} copy-done((bf16[1,3,1024,512]{3,2,1,0:T(8,128)(2,1)S(1)}, bf16[1,3,1024,512]{3,2,1,0:T(8,128)(2,1)}, u32[]{:S(2)}) %copy-start) | copy-done | bytes 3145752
  48.8 1.8 %shard_map.71 = (bf16[144,128]{1,0:T(8,128)(2,1)S(1)}, bf16[144,128]{1,0:T(8,128)(2,1)S(1)}, bf16[144,128]{1,0:T(8,128)(2,1)S(1)}, bf16[144,128]{1,0:T(8,128)(2,...) custom-call(s32[8]{0:T(128)S(1)} %copy-done.8, ...), custom_call_target="tpu_custom_call" | custom-call | tf_op jit(solution)/shard_map/pallas_call | solution.py:383
  50.6 1.4 %collective-permute-start.14 = (bf16[144,128]{1,0:T(8,128)(2,1)S(1)}, bf16[144,128]{1,0:T(8,128)(2,1)S(1)}, u32[]{:S(2)}, u32[]{:S(2)}) collective-permute-start(bf16[144,128]{1,0:T(8,128)(2,1)S(1)} %get-tuple-element.55), channel_id=1, source_target_pairs={{0,2},{2,0},{4,6},{6,4},{8,10},{10,8},{12,14},{14,12},{1,3},{3,1},... | collective-permute-start | bytes 110600 | tf_op jit(solution)/shard_map/ppermute | solution.py:331
  52.0 2.2 %collective-permute-start.16 = (bf16[144,128]{1,0:T(8,128)(2,1)S(1)}, bf16[144,128]{1,0:T(8,128)(2,1)S(1)}, u32[]{:S(2)}, u32[]{:S(2)}) collective-permute-start(bf16[144,128]{1,0:T(8,128)(2,1)S(1)} %get-tuple-element.57), channel_id=1, source_target_pairs={{0,6},{2,4},{4,2},{6,0},{8,14},{10,12},{12,10},{14,8},{1,7},{3,5},... | collective-permute-start | bytes 110600 | tf_op jit(solution)/shard_map/ppermute | solution.py:331
  54.1 2.0 %collective-permute-start.17 = (bf16[144,128]{1,0:T(8,128)(2,1)S(1)}, bf16[144,128]{1,0:T(8,128)(2,1)S(1)}, u32[]{:S(2)}, u32[]{:S(2)}) collective-permute-start(bf16[144,128]{1,0:T(8,128)(2,1)S(1)} %get-tuple-element.58), channel_id=1, source_target_pairs={{0,8},{2,10},{4,12},{6,14},{8,0},{10,2},{12,4},{14,6},{1,9},{3,11}... | collective-permute-start | bytes 110600 | tf_op jit(solution)/shard_map/ppermute | solution.py:331
  56.2 1.7 %collective-permute-start.18 = (bf16[144,128]{1,0:T(8,128)(2,1)S(1)}, bf16[144,128]{1,0:T(8,128)(2,1)S(1)}, u32[]{:S(2)}, u32[]{:S(2)}) collective-permute-start(bf16[144,128]{1,0:T(8,128)(2,1)S(1)} %get-tuple-element.59), channel_id=1, source_target_pairs={{0,10},{2,8},{4,14},{6,12},{8,2},{10,0},{12,6},{14,4},{1,11},{3,9}... | collective-permute-start | bytes 110600 | tf_op jit(solution)/shard_map/ppermute | solution.py:331
  57.8 3.6 %collective-permute-start.19 = (bf16[144,128]{1,0:T(8,128)(2,1)S(1)}, bf16[144,128]{1,0:T(8,128)(2,1)S(1)}, u32[]{:S(2)}, u32[]{:S(2)}) collective-permute-start(bf16[144,128]{1,0:T(8,128)(2,1)S(1)} %get-tuple-element.60), channel_id=1, source_target_pairs={{0,12},{2,14},{4,8},{6,10},{8,4},{10,6},{12,0},{14,2},{1,13},{3,15... | collective-permute-start | bytes 110600 | tf_op jit(solution)/shard_map/ppermute | solution.py:331
  62.2 1.6 %collective-permute-done.19.rest_14_ = bf16[144,128]{1,0:T(8,128)(2,1)S(1)} collective-permute-done((bf16[144,128]{1,0:T(8,128)(2,1)S(1)}, bf16[144,128]{1,0:T(8,128)(2,1)S(1)}, u32[]{:S(2)}, u32[]{:S(2)}) %collective-permute-start.19) | collective-permute-done | bytes 36896 | tf_op jit(solution)/shard_map/ppermute | solution.py:331
  63.8 4.3 %collective-permute-done.20.rest_15_ = bf16[144,128]{1,0:T(8,128)(2,1)S(1)} collective-permute-done((bf16[144,128]{1,0:T(8,128)(2,1)S(1)}, bf16[144,128]{1,0:T(8,128)(2,1)S(1)}, u32[]{:S(2)}, u32[]{:S(2)}) %collective-permute-start.20) | collective-permute-done | bytes 36896 | tf_op jit(solution)/shard_map/ppermute | solution.py:331
  68.1 0.9 %shard_map.72 = (bf16[16,512]{1,0:T(8,128)(2,1)S(1)}, bf16[16,512]{1,0:T(8,128)(2,1)S(1)}, bf16[16,512]{1,0:T(8,128)(2,1)S(1)}, bf16[16,512]{1,0:T(8,128)(2,1)S(...) custom-call(s32[8]{0:T(128)S(1)} %copy-done.8, ...), custom_call_target="tpu_custom_call" | custom-call | tf_op jit(solution)/shard_map/pallas_call | solution.py:392
  69.6 2.9 %collective-permute-start.23 = (bf16[16,512]{1,0:T(8,128)(2,1)S(1)}, bf16[16,512]{1,0:T(8,128)(2,1)S(1)}, u32[]{:S(2)}, u32[]{:S(2)}) collective-permute-start(bf16[16,512]{1,0:T(8,128)(2,1)S(1)} %get-tuple-element.67), channel_id=1, source_target_pairs={{0,6},{2,4},{4,2},{6,0},{8,14},{10,12},{12,10},{14,8},{1,7},{3,5},... | collective-permute-start | bytes 49160 | tf_op jit(solution)/shard_map/ppermute | solution.py:331
  72.6 2.9 %collective-permute-start.25 = (bf16[16,512]{1,0:T(8,128)(2,1)S(1)}, bf16[16,512]{1,0:T(8,128)(2,1)S(1)}, u32[]{:S(2)}, u32[]{:S(2)}) collective-permute-start(bf16[16,512]{1,0:T(8,128)(2,1)S(1)} %get-tuple-element.69), channel_id=1, source_target_pairs={{0,10},{2,8},{4,14},{6,12},{8,2},{10,0},{12,6},{14,4},{1,11},{3,9}... | collective-permute-start | bytes 49160 | tf_op jit(solution)/shard_map/ppermute | solution.py:331
  75.9 4.3 %collective-permute-start.27 = (bf16[16,512]{1,0:T(8,128)(2,1)S(1)}, bf16[16,512]{1,0:T(8,128)(2,1)S(1)}, u32[]{:S(2)}, u32[]{:S(2)}) collective-permute-start(bf16[16,512]{1,0:T(8,128)(2,1)S(1)} %get-tuple-element.71), channel_id=1, source_target_pairs={{0,14},{2,12},{4,10},{6,8},{8,6},{10,4},{12,2},{14,0},{1,15},{3,13... | collective-permute-start | bytes 49160 | tf_op jit(solution)/shard_map/ppermute | solution.py:331
  81.0 1.3 %collective-permute-done.27.rest_7_ = bf16[16,512]{1,0:T(8,128)(2,1)S(1)} collective-permute-done((bf16[16,512]{1,0:T(8,128)(2,1)S(1)}, bf16[16,512]{1,0:T(8,128)(2,1)S(1)}, u32[]{:S(2)}, u32[]{:S(2)}) %collective-permute-start.27) | collective-permute-done | bytes 16416 | tf_op jit(solution)/shard_map/ppermute | solution.py:331
  82.3 1.3 %shard_map.73 = bf16[128,512]{1,0:T(8,128)(2,1)} custom-call(s32[8]{0:T(128)S(1)} %copy-done.8, s32[8]{0:T(128)S(1)} %copy-done.7, f32[8,128]{1,0:T(8,128)S(1)} %get-tuple-element.62.factors, bf16[128,512]{1,0:T(8,128)(2,1)S(1)} %copy-done.3, f32[128,512]{1,0:T(8,128)S(1)} %get-tuple-element.63.stay_2, bf16[16,512]{1,0:T(8,128)(2,1)S(1)} %get-tuple-element.64.rest_0_, ...), custom_call_target="tpu_custom_call" | custom-call | tf_op jit(solution)/shard_map/pallas_call | solution.py:404
  (50 shorter events, 5.8 us)
Async XLA Ops:
  0.6 41.9 %copy-start.8 = (s32[8]{0:T(128)S(1)}, s32[8]{0:T(128)}, u32[]{:S(2)}) copy-start(s32[8]{0:T(128)} %widths.9) | copy-start | bytes 100
  0.7 46.2 %copy-start.4 = (bf16[3,128,128]{2,1,0:T(8,128)(2,1)S(1)}, bf16[3,128,128]{2,1,0:T(8,128)(2,1)}, u32[]{:S(2)}) copy-start(bf16[3,128,128]{2,1,0:T(8,128)(2,1)} %right.3) | copy-start | bytes 294916
  4.6 42.3 %copy-start.1 = (bf16[2,128,512]{2,1,0:T(8,128)(2,1)S(1)}, bf16[2,128,512]{2,1,0:T(8,128)(2,1)}, u32[]{:S(2)}) copy-start(bf16[2,128,512]{2,1,0:T(8,128)(2,1)} %all_gather.7.amps) | copy-start | bytes 786436
  8.8 73.5 %copy-start.3 = (bf16[128,512]{1,0:T(8,128)(2,1)S(1)}, bf16[128,512]{1,0:T(8,128)(2,1)}, u32[]{:S(2)}) copy-start(bf16[128,512]{1,0:T(8,128)(2,1)} %get-tuple-element.37.stay) | copy-start | bytes 393220
  8.8 8.6 %collective-permute-start = (bf16[2,16,512]{2,1,0:T(8,128)(2,1)}, bf16[2,16,512]{2,1,0:T(8,128)(2,1)S(1)}, u32[]{:S(2)}, u32[]{:S(2)}) collective-permute-start(bf16[2,16,512]{2,1,0:T(8,128)(2,1)} %get-tuple-element.39), channel_id=1, source_target_pairs={{0,2},{2,0},{4,6},{6,4},{8,10},{10,8},{12,14},{14,12},{1,3},{3,1},... | collective-permute-start | bytes 98312 | tf_op jit(solution)/shard_map/ppermute | solution.py:331
  11.5 9.5 %collective-permute-start.1 = (bf16[2,16,512]{2,1,0:T(8,128)(2,1)}, bf16[2,16,512]{2,1,0:T(8,128)(2,1)S(1)}, u32[]{:S(2)}, u32[]{:S(2)}) collective-permute-start(bf16[2,16,512]{2,1,0:T(8,128)(2,1)} %get-tuple-element.40), channel_id=1, source_target_pairs={{0,4},{2,6},{4,0},{6,2},{8,12},{10,14},{12,8},{14,10},{1,5},{3,7},... | collective-permute-start | bytes 98312 | tf_op jit(solution)/shard_map/ppermute | solution.py:331
  13.1 7.9 %collective-permute-start.2 = (bf16[2,16,512]{2,1,0:T(8,128)(2,1)}, bf16[2,16,512]{2,1,0:T(8,128)(2,1)S(1)}, u32[]{:S(2)}, u32[]{:S(2)}) collective-permute-start(bf16[2,16,512]{2,1,0:T(8,128)(2,1)} %get-tuple-element.41), channel_id=1, source_target_pairs={{0,6},{2,4},{4,2},{6,0},{8,14},{10,12},{12,10},{14,8},{1,7},{3,5},... | collective-permute-start | bytes 98312 | tf_op jit(solution)/shard_map/ppermute | solution.py:331
  13.1 7.9 %collective-permute-start.3 = (bf16[2,16,512]{2,1,0:T(8,128)(2,1)}, bf16[2,16,512]{2,1,0:T(8,128)(2,1)S(1)}, u32[]{:S(2)}, u32[]{:S(2)}) collective-permute-start(bf16[2,16,512]{2,1,0:T(8,128)(2,1)} %get-tuple-element.42), channel_id=1, source_target_pairs={{0,8},{2,10},{4,12},{6,14},{8,0},{10,2},{12,4},{14,6},{1,9},{3,11}... | collective-permute-start | bytes 98312 | tf_op jit(solution)/shard_map/ppermute | solution.py:331
  16.1 5.9 %collective-permute-start.4 = (bf16[2,16,512]{2,1,0:T(8,128)(2,1)}, bf16[2,16,512]{2,1,0:T(8,128)(2,1)S(1)}, u32[]{:S(2)}, u32[]{:S(2)}) collective-permute-start(bf16[2,16,512]{2,1,0:T(8,128)(2,1)} %get-tuple-element.43), channel_id=1, source_target_pairs={{0,10},{2,8},{4,14},{6,12},{8,2},{10,0},{12,6},{14,4},{1,11},{3,9}... | collective-permute-start | bytes 98312 | tf_op jit(solution)/shard_map/ppermute | solution.py:331
  17.4 6.1 %collective-permute-start.5 = (bf16[2,16,512]{2,1,0:T(8,128)(2,1)}, bf16[2,16,512]{2,1,0:T(8,128)(2,1)S(1)}, u32[]{:S(2)}, u32[]{:S(2)}) collective-permute-start(bf16[2,16,512]{2,1,0:T(8,128)(2,1)} %get-tuple-element.44), channel_id=1, source_target_pairs={{0,12},{2,14},{4,8},{6,10},{8,4},{10,6},{12,0},{14,2},{1,13},{3,15... | collective-permute-start | bytes 98312 | tf_op jit(solution)/shard_map/ppermute | solution.py:331
  21.0 6.8 %collective-permute-start.6 = (bf16[2,16,512]{2,1,0:T(8,128)(2,1)}, bf16[2,16,512]{2,1,0:T(8,128)(2,1)S(1)}, u32[]{:S(2)}, u32[]{:S(2)}) collective-permute-start(bf16[2,16,512]{2,1,0:T(8,128)(2,1)} %get-tuple-element.45), channel_id=1, source_target_pairs={{0,14},{2,12},{4,10},{6,8},{8,6},{10,4},{12,2},{14,0},{1,15},{3,13... | collective-permute-start | bytes 98312 | tf_op jit(solution)/shard_map/ppermute | solution.py:331
  29.2 6.5 %collective-permute-start.7 = (bf16[16,512]{1,0:T(8,128)(2,1)S(1)}, bf16[16,512]{1,0:T(8,128)(2,1)S(1)}, u32[]{:S(2)}, u32[]{:S(2)}) collective-permute-start(bf16[16,512]{1,0:T(8,128)(2,1)S(1)} %get-tuple-element.47), channel_id=1, source_target_pairs={{0,2},{2,0},{4,6},{6,4},{8,10},{10,8},{12,14},{14,12},{1,3},{3,1},... | collective-permute-start | bytes 49160 | tf_op jit(solution)/shard_map/ppermute | solution.py:331
  29.8 6.2 %collective-permute-start.8 = (bf16[16,512]{1,0:T(8,128)(2,1)S(1)}, bf16[16,512]{1,0:T(8,128)(2,1)S(1)}, u32[]{:S(2)}, u32[]{:S(2)}) collective-permute-start(bf16[16,512]{1,0:T(8,128)(2,1)S(1)} %get-tuple-element.48), channel_id=1, source_target_pairs={{0,4},{2,6},{4,0},{6,2},{8,12},{10,14},{12,8},{14,10},{1,5},{3,7},... | collective-permute-start | bytes 49160 | tf_op jit(solution)/shard_map/ppermute | solution.py:331
  29.8 10.6 %collective-permute-start.9 = (bf16[16,512]{1,0:T(8,128)(2,1)S(1)}, bf16[16,512]{1,0:T(8,128)(2,1)S(1)}, u32[]{:S(2)}, u32[]{:S(2)}) collective-permute-start(bf16[16,512]{1,0:T(8,128)(2,1)S(1)} %get-tuple-element.49), channel_id=1, source_target_pairs={{0,6},{2,4},{4,2},{6,0},{8,14},{10,12},{12,10},{14,8},{1,7},{3,5},... | collective-permute-start | bytes 49160 | tf_op jit(solution)/shard_map/ppermute | solution.py:331
  32.8 7.7 %collective-permute-start.10 = (bf16[16,512]{1,0:T(8,128)(2,1)S(1)}, bf16[16,512]{1,0:T(8,128)(2,1)S(1)}, u32[]{:S(2)}, u32[]{:S(2)}) collective-permute-start(bf16[16,512]{1,0:T(8,128)(2,1)S(1)} %get-tuple-element.50), channel_id=1, source_target_pairs={{0,8},{2,10},{4,12},{6,14},{8,0},{10,2},{12,4},{14,6},{1,9},{3,11}... | collective-permute-start | bytes 49160 | tf_op jit(solution)/shard_map/ppermute | solution.py:331
  32.8 7.7 %collective-permute-start.11 = (bf16[16,512]{1,0:T(8,128)(2,1)S(1)}, bf16[16,512]{1,0:T(8,128)(2,1)S(1)}, u32[]{:S(2)}, u32[]{:S(2)}) collective-permute-start(bf16[16,512]{1,0:T(8,128)(2,1)S(1)} %get-tuple-element.51), channel_id=1, source_target_pairs={{0,10},{2,8},{4,14},{6,12},{8,2},{10,0},{12,6},{14,4},{1,11},{3,9}... | collective-permute-start | bytes 49160 | tf_op jit(solution)/shard_map/ppermute | solution.py:331
  35.7 5.5 %collective-permute-start.12 = (bf16[16,512]{1,0:T(8,128)(2,1)S(1)}, bf16[16,512]{1,0:T(8,128)(2,1)S(1)}, u32[]{:S(2)}, u32[]{:S(2)}) collective-permute-start(bf16[16,512]{1,0:T(8,128)(2,1)S(1)} %get-tuple-element.52), channel_id=1, source_target_pairs={{0,12},{2,14},{4,8},{6,10},{8,4},{10,6},{12,0},{14,2},{1,13},{3,15... | collective-permute-start | bytes 49160 | tf_op jit(solution)/shard_map/ppermute | solution.py:331
  36.1 6.4 %collective-permute-start.13 = (bf16[16,512]{1,0:T(8,128)(2,1)S(1)}, bf16[16,512]{1,0:T(8,128)(2,1)S(1)}, u32[]{:S(2)}, u32[]{:S(2)}) collective-permute-start(bf16[16,512]{1,0:T(8,128)(2,1)S(1)} %get-tuple-element.53), channel_id=1, source_target_pairs={{0,14},{2,12},{4,10},{6,8},{8,6},{10,4},{12,2},{14,0},{1,15},{3,13... | collective-permute-start | bytes 49160 | tf_op jit(solution)/shard_map/ppermute | solution.py:331
  50.6 7.2 %collective-permute-start.14 = (bf16[144,128]{1,0:T(8,128)(2,1)S(1)}, bf16[144,128]{1,0:T(8,128)(2,1)S(1)}, u32[]{:S(2)}, u32[]{:S(2)}) collective-permute-start(bf16[144,128]{1,0:T(8,128)(2,1)S(1)} %get-tuple-element.55), channel_id=1, source_target_pairs={{0,2},{2,0},{4,6},{6,4},{8,10},{10,8},{12,14},{14,12},{1,3},{3,1},... | collective-permute-start | bytes 110600 | tf_op jit(solution)/shard_map/ppermute | solution.py:331
  52.0 9.5 %collective-permute-start.15 = (bf16[144,128]{1,0:T(8,128)(2,1)S(1)}, bf16[144,128]{1,0:T(8,128)(2,1)S(1)}, u32[]{:S(2)}, u32[]{:S(2)}) collective-permute-start(bf16[144,128]{1,0:T(8,128)(2,1)S(1)} %get-tuple-element.56), channel_id=1, source_target_pairs={{0,4},{2,6},{4,0},{6,2},{8,12},{10,14},{12,8},{14,10},{1,5},{3,7},... | collective-permute-start | bytes 110600 | tf_op jit(solution)/shard_map/ppermute | solution.py:331
  52.0 9.8 %collective-permute-start.16 = (bf16[144,128]{1,0:T(8,128)(2,1)S(1)}, bf16[144,128]{1,0:T(8,128)(2,1)S(1)}, u32[]{:S(2)}, u32[]{:S(2)}) collective-permute-start(bf16[144,128]{1,0:T(8,128)(2,1)S(1)} %get-tuple-element.57), channel_id=1, source_target_pairs={{0,6},{2,4},{4,2},{6,0},{8,14},{10,12},{12,10},{14,8},{1,7},{3,5},... | collective-permute-start | bytes 110600 | tf_op jit(solution)/shard_map/ppermute | solution.py:331
  54.1 7.7 %collective-permute-start.17 = (bf16[144,128]{1,0:T(8,128)(2,1)S(1)}, bf16[144,128]{1,0:T(8,128)(2,1)S(1)}, u32[]{:S(2)}, u32[]{:S(2)}) collective-permute-start(bf16[144,128]{1,0:T(8,128)(2,1)S(1)} %get-tuple-element.58), channel_id=1, source_target_pairs={{0,8},{2,10},{4,12},{6,14},{8,0},{10,2},{12,4},{14,6},{1,9},{3,11}... | collective-permute-start | bytes 110600 | tf_op jit(solution)/shard_map/ppermute | solution.py:331
  56.2 6.1 %collective-permute-start.18 = (bf16[144,128]{1,0:T(8,128)(2,1)S(1)}, bf16[144,128]{1,0:T(8,128)(2,1)S(1)}, u32[]{:S(2)}, u32[]{:S(2)}) collective-permute-start(bf16[144,128]{1,0:T(8,128)(2,1)S(1)} %get-tuple-element.59), channel_id=1, source_target_pairs={{0,10},{2,8},{4,14},{6,12},{8,2},{10,0},{12,6},{14,4},{1,11},{3,9}... | collective-permute-start | bytes 110600 | tf_op jit(solution)/shard_map/ppermute | solution.py:331
  57.8 6.0 %collective-permute-start.19 = (bf16[144,128]{1,0:T(8,128)(2,1)S(1)}, bf16[144,128]{1,0:T(8,128)(2,1)S(1)}, u32[]{:S(2)}, u32[]{:S(2)}) collective-permute-start(bf16[144,128]{1,0:T(8,128)(2,1)S(1)} %get-tuple-element.60), channel_id=1, source_target_pairs={{0,12},{2,14},{4,8},{6,10},{8,4},{10,6},{12,0},{14,2},{1,13},{3,15... | collective-permute-start | bytes 110600 | tf_op jit(solution)/shard_map/ppermute | solution.py:331
  61.4 6.7 %collective-permute-start.20 = (bf16[144,128]{1,0:T(8,128)(2,1)S(1)}, bf16[144,128]{1,0:T(8,128)(2,1)S(1)}, u32[]{:S(2)}, u32[]{:S(2)}) collective-permute-start(bf16[144,128]{1,0:T(8,128)(2,1)S(1)} %get-tuple-element.61), channel_id=1, source_target_pairs={{0,14},{2,12},{4,10},{6,8},{8,6},{10,4},{12,2},{14,0},{1,15},{3,13... | collective-permute-start | bytes 110600 | tf_op jit(solution)/shard_map/ppermute | solution.py:331
  69.0 6.5 %collective-permute-start.21 = (bf16[16,512]{1,0:T(8,128)(2,1)S(1)}, bf16[16,512]{1,0:T(8,128)(2,1)S(1)}, u32[]{:S(2)}, u32[]{:S(2)}) collective-permute-start(bf16[16,512]{1,0:T(8,128)(2,1)S(1)} %get-tuple-element.65), channel_id=1, source_target_pairs={{0,2},{2,0},{4,6},{6,4},{8,10},{10,8},{12,14},{14,12},{1,3},{3,1},... | collective-permute-start | bytes 49160 | tf_op jit(solution)/shard_map/ppermute | solution.py:331
  69.6 6.3 %collective-permute-start.22 = (bf16[16,512]{1,0:T(8,128)(2,1)S(1)}, bf16[16,512]{1,0:T(8,128)(2,1)S(1)}, u32[]{:S(2)}, u32[]{:S(2)}) collective-permute-start(bf16[16,512]{1,0:T(8,128)(2,1)S(1)} %get-tuple-element.66), channel_id=1, source_target_pairs={{0,4},{2,6},{4,0},{6,2},{8,12},{10,14},{12,8},{14,10},{1,5},{3,7},... | collective-permute-start | bytes 49160 | tf_op jit(solution)/shard_map/ppermute | solution.py:331
  69.6 10.6 %collective-permute-start.23 = (bf16[16,512]{1,0:T(8,128)(2,1)S(1)}, bf16[16,512]{1,0:T(8,128)(2,1)S(1)}, u32[]{:S(2)}, u32[]{:S(2)}) collective-permute-start(bf16[16,512]{1,0:T(8,128)(2,1)S(1)} %get-tuple-element.67), channel_id=1, source_target_pairs={{0,6},{2,4},{4,2},{6,0},{8,14},{10,12},{12,10},{14,8},{1,7},{3,5},... | collective-permute-start | bytes 49160 | tf_op jit(solution)/shard_map/ppermute | solution.py:331
  72.6 7.7 %collective-permute-start.24 = (bf16[16,512]{1,0:T(8,128)(2,1)S(1)}, bf16[16,512]{1,0:T(8,128)(2,1)S(1)}, u32[]{:S(2)}, u32[]{:S(2)}) collective-permute-start(bf16[16,512]{1,0:T(8,128)(2,1)S(1)} %get-tuple-element.68), channel_id=1, source_target_pairs={{0,8},{2,10},{4,12},{6,14},{8,0},{10,2},{12,4},{14,6},{1,9},{3,11}... | collective-permute-start | bytes 49160 | tf_op jit(solution)/shard_map/ppermute | solution.py:331
  72.6 7.7 %collective-permute-start.25 = (bf16[16,512]{1,0:T(8,128)(2,1)S(1)}, bf16[16,512]{1,0:T(8,128)(2,1)S(1)}, u32[]{:S(2)}, u32[]{:S(2)}) collective-permute-start(bf16[16,512]{1,0:T(8,128)(2,1)S(1)} %get-tuple-element.69), channel_id=1, source_target_pairs={{0,10},{2,8},{4,14},{6,12},{8,2},{10,0},{12,6},{14,4},{1,11},{3,9}... | collective-permute-start | bytes 49160 | tf_op jit(solution)/shard_map/ppermute | solution.py:331
  75.5 5.5 %collective-permute-start.26 = (bf16[16,512]{1,0:T(8,128)(2,1)S(1)}, bf16[16,512]{1,0:T(8,128)(2,1)S(1)}, u32[]{:S(2)}, u32[]{:S(2)}) collective-permute-start(bf16[16,512]{1,0:T(8,128)(2,1)S(1)} %get-tuple-element.70), channel_id=1, source_target_pairs={{0,12},{2,14},{4,8},{6,10},{8,4},{10,6},{12,0},{14,2},{1,13},{3,15... | collective-permute-start | bytes 49160 | tf_op jit(solution)/shard_map/ppermute | solution.py:331
  75.9 6.4 %collective-permute-start.27 = (bf16[16,512]{1,0:T(8,128)(2,1)S(1)}, bf16[16,512]{1,0:T(8,128)(2,1)S(1)}, u32[]{:S(2)}, u32[]{:S(2)}) collective-permute-start(bf16[16,512]{1,0:T(8,128)(2,1)S(1)} %get-tuple-element.71), channel_id=1, source_target_pairs={{0,14},{2,12},{4,10},{6,8},{8,6},{10,4},{12,2},{14,0},{1,15},{3,13... | collective-permute-start | bytes 49160 | tf_op jit(solution)/shard_map/ppermute | solution.py:331
  (5 other events, 70.3 us)

commit v6 on v1

--- a/solution.py
+++ b/solution.py
@@ -1,6 +1,8 @@
 import jax
 import jax.numpy as jnp
 from jax import lax
+from jax.experimental import pallas as pl
+from jax.experimental.pallas import tpu as pltpu
 from jax.sharding import PartitionSpec as P
 
 QDOWN = 4
@@ -61,7 +63,7 @@
     return total
 
 
-def on_device(amplitudes, widths, holders, left_env, right_env):
+def on_device_any(amplitudes, widths, holders, left_env, right_env):
     slots_dev, right_dim, half_width = amplitudes.shape
     assert slots_dev == 1
     n_slots = holders.shape[0]
@@ -107,6 +109,228 @@
     return first[None], second[None]
 
 
+LANES = 128
+TAG = 16
+
+
+def live_columns(widths, holders, half):
+    width = widths[holders[lax.axis_index("sec")]]
+    first_column = lax.axis_index("env") * half
+    return first_column + lax.broadcasted_iota(jnp.int32, (1, half), 1) < width
+
+
+def apply_term(right, left, vector, term):
+    products = jnp.dot(right[term], vector, preferred_element_type=jnp.float32)
+    return jnp.dot(products.astype(jnp.bfloat16), left, preferred_element_type=jnp.float32)
+
+
+def mask_kernel(widths, holders, amps, start):
+    live = live_columns(widths, holders, amps.shape[1])
+    start[...] = jnp.where(live, amps[...], jnp.zeros_like(amps[...]))
+
+
+def first_kernel(start, right, left, message, stay):
+    slots, _, rows, _ = message.shape
+    vector = jnp.concatenate([start[0], start[1]], axis=1)
+    for term in (1, 2, 0):
+        block = apply_term(right, left[0, term], vector, term).astype(jnp.bfloat16)
+        if term == 0:
+            stay[...] = block
+        else:
+            for slot in range(slots):
+                message[slot, term - 1] = block[slot * rows : (slot + 1) * rows, :]
+
+
+def fill_slots(holders, slot_of):
+    for s in range(holders.shape[0]):
+        slot_of[holders[s]] = jnp.int32(s)
+
+
+def sources_of(holders, slot_of, target):
+    sector = holders[target]
+    has = (sector >= QDOWN, sector % QDOWN > 0)
+    source = (slot_of[sector & (QDOWN - 1)], slot_of[jnp.maximum(sector - 1, 0)])
+    return has, source
+
+
+def merge_kernel(holders, table, out, slot_of):
+    fill_slots(holders, slot_of)
+    for slot in range(holders.shape[0]):
+        has, source = sources_of(holders, slot_of, slot)
+        total = 0.0
+        for i in range(2):
+            block = table[source[i], i].astype(jnp.float32)
+            total = total + jnp.where(has[i], block, 0.0)
+        out[slot] = total.astype(jnp.bfloat16)
+
+
+def sum_kernel(widths, holders, stay, arrived, first):
+    live = live_columns(widths, holders, stay.shape[1])
+    total = stay[...].astype(jnp.float32) + arrived[...].astype(jnp.float32)
+    first[...] = jnp.where(live, total, 0.0).astype(jnp.bfloat16)
+
+
+def total_of(array):
+    return jnp.sum(jnp.sum(array, axis=0, keepdims=True), axis=1, keepdims=True)
+
+
+def make_tag(values, me):
+    row = lax.broadcasted_iota(jnp.int32, (TAG, LANES), 0)
+    lane = lax.broadcasted_iota(jnp.int32, (TAG, LANES), 1)
+    spread = jnp.zeros((TAG, LANES), jnp.float32)
+    for place, value in enumerate(values):
+        spread = jnp.where(row // 3 == place, value, spread)
+    high = spread.astype(jnp.bfloat16).astype(jnp.float32)
+    middle = (spread - high).astype(jnp.bfloat16).astype(jnp.float32)
+    low = spread - high - middle
+    parts = jnp.where(row % 3 == 0, high, jnp.where(row % 3 == 1, middle, low))
+    return jnp.where((lane == me) & (row < 3 * len(values)), parts, 0.0).astype(jnp.bfloat16)
+
+
+def second_kernel(start, first, right, left, message, stay):
+    slots = message.shape[0]
+    half = stay.shape[1]
+    rows = stay.shape[0] // slots
+    chunks = half // LANES
+    basis = [start[h].astype(jnp.float32) for h in range(2)]
+    firsts = [first[h].astype(jnp.float32) for h in range(2)]
+    overlap = total_of(basis[0] * firsts[0]) + total_of(basis[1] * firsts[1])
+    norm = total_of(basis[0] * basis[0]) + total_of(basis[1] * basis[1])
+    quotient = jnp.where(norm > 0, overlap / jnp.where(norm > 0, norm, 1.0), 0.0)
+    deflated = [firsts[h] - quotient * basis[h] for h in range(2)]
+    rest_norm = total_of(deflated[0] * deflated[0]) + total_of(deflated[1] * deflated[1])
+    vector = jnp.concatenate(deflated, axis=1).astype(jnp.bfloat16)
+    tag = make_tag((overlap, norm, quotient, rest_norm), lax.axis_index("sec"))
+    for slot in range(slots):
+        message[slot, pl.ds(2 * chunks * rows, TAG), :] = tag
+    for term in (1, 2, 0):
+        block = apply_term(right, left[0, term], vector, term)
+        if term == 0:
+            stay[...] = block
+        else:
+            block = block.astype(jnp.bfloat16)
+            for slot in range(slots):
+                for c in range(chunks):
+                    place = pl.ds(((term - 1) * chunks + c) * rows, rows)
+                    message[slot, place, :] = block[
+                        slot * rows : (slot + 1) * rows, c * LANES : (c + 1) * LANES
+                    ]
+
+
+def mix_kernel(widths, holders, old, new, out, factors, slot_of):
+    slots, rows, half = out.shape
+    chunks = half // LANES
+    fill_slots(holders, slot_of)
+    tag = jnp.zeros((TAG, LANES), jnp.float32)
+    total = jnp.int32(0)
+    for slot in range(slots):
+        tag = tag + new[slot, pl.ds(2 * chunks * rows, TAG), :].astype(jnp.float32)
+        total = total + widths[slot]
+    live_count = slots * rows * total.astype(jnp.float32)
+
+    def value(place):
+        parts = [tag[3 * place + i : 3 * place + i + 1, :] for i in range(3)]
+        return parts[0] + parts[1] + parts[2]
+
+    overlaps, norms, quotients, rests = (value(place) for place in range(4))
+    quotient = total_of(overlaps) / total_of(norms)
+    lane = lax.broadcasted_iota(jnp.int32, (1, LANES), 1)
+    shifts = jnp.where(lane < slots, quotients - quotient, 0.0)
+    resid_norm = total_of(rests + shifts * shifts * norms)
+    scale = lax.rsqrt(resid_norm / live_count + 1e-06)
+
+    def shift_of(slot):
+        return total_of(jnp.where(lane == slot, shifts, 0.0))
+
+    row = lax.broadcasted_iota(jnp.int32, factors.shape, 0)
+    factors[...] = jnp.where(row == 0, scale, scale * shift_of(lax.axis_index("sec")))
+    for slot in range(slots):
+        has, source = sources_of(holders, slot_of, slot)
+        total = 0.0
+        for i in range(2):
+            block = jnp.concatenate(
+                [
+                    new[source[i], pl.ds((i * chunks + c) * rows, rows), :]
+                    for c in range(chunks)
+                ],
+                axis=1,
+            ).astype(jnp.float32)
+            block = block + shift_of(source[i]) * old[source[i], i].astype(jnp.float32)
+            total = total + jnp.where(has[i], block, 0.0)
+        out[slot] = (scale * total).astype(jnp.bfloat16)
+
+
+def final_kernel(widths, holders, factors, stay, stay_2, arrived, second):
+    live = live_columns(widths, holders, stay.shape[1])
+    scale, shift = factors[0:1, 0:1], factors[1:2, 0:1]
+    total = scale * stay_2[...] + shift * stay[...].astype(jnp.float32)
+    total = total + arrived[...].astype(jnp.float32)
+    second[...] = jnp.where(live, total, 0.0).astype(jnp.bfloat16)
+
+
+SMEM = pl.BlockSpec(memory_space=pltpu.SMEM)
+VMEM = pl.BlockSpec(memory_space=pltpu.VMEM)
+
+
+def call(kernel, specs, outs, scratch=(), flops=0):
+    return pl.pallas_call(
+        kernel,
+        out_shape=outs,
+        in_specs=specs,
+        out_specs=jax.tree.map(lambda _: VMEM, outs),
+        scratch_shapes=scratch,
+        compiler_params=pltpu.CompilerParams(vmem_limit_bytes=16 * 1024 * 1024),
+        cost_estimate=pl.CostEstimate(flops=flops, bytes_accessed=1 << 18, transcendentals=0),
+    )
+
+
+def swap(pieces):
+    return lax.all_to_all(pieces, "sec", split_axis=0, concat_axis=0)
+
+
+def on_device(amplitudes, widths, holders, left_env, right_env):
+    slots_dev, right_dim, half = amplitudes.shape
+    slots = holders.shape[0]
+    assert slots_dev == 1
+    if slots != 2 * QDOWN:
+        return on_device_any(amplitudes, widths, holders, left_env, right_env)
+    rows = right_dim // slots
+    dots = 6 * right_dim * half * (right_dim + 2 * half)
+    block = jax.ShapeDtypeStruct((right_dim, half), jnp.bfloat16)
+    wide = jax.ShapeDtypeStruct((right_dim, half), jnp.float32)
+    pairs = jax.ShapeDtypeStruct((slots, 2, rows, half), jnp.bfloat16)
+    singles = jax.ShapeDtypeStruct((slots, rows, half), jnp.bfloat16)
+    tagged = jax.ShapeDtypeStruct((slots, 2 * rows * half // LANES + TAG, LANES), jnp.bfloat16)
+    factor_shape = jax.ShapeDtypeStruct((8, LANES), jnp.float32)
+    slot_table = [pltpu.SMEM((slots,), jnp.int32)]
+
+    start = call(mask_kernel, [SMEM, SMEM, VMEM], block, flops=dots)(
+        widths, holders, amplitudes[0]
+    )
+    start_full = lax.all_gather(start, "env")
+    message, stay = call(first_kernel, [VMEM] * 3, (pairs, block), flops=dots)(
+        start_full, right_env, left_env
+    )
+    old = swap(message)
+    merged = call(merge_kernel, [SMEM, VMEM], singles, slot_table)(holders, old)
+    arrived = swap(merged).reshape(right_dim, half)
+    first = call(sum_kernel, [SMEM, SMEM, VMEM, VMEM], block)(widths, holders, stay, arrived)
+
+    first_full = lax.all_gather(first, "env")
+    message, stay_2 = call(second_kernel, [VMEM] * 4, (tagged, wide), flops=dots)(
+        start_full, first_full, right_env, left_env
+    )
+    new = swap(message)
+    mixed, factors = call(
+        mix_kernel, [SMEM, SMEM, VMEM, VMEM], (singles, factor_shape), slot_table
+    )(widths, holders, old, new)
+    arrived = swap(mixed).reshape(right_dim, half)
+    second = call(final_kernel, [SMEM, SMEM] + [VMEM] * 4, block)(
+        widths, holders, factors, stay, stay_2, arrived
+    )
+    return first[None], second[None]
+
+
 def solution(mesh):
     in_specs = (
         P(("runs", "sec"), None, "env"),

time: 121 us -> 67.6 us (0.56); the launches traced: 119 us -> 67.2 us
  blocking collectives: 4.08 us -> 54.6 us
  starting transfers between devices: 29.4 us -> 0 us
  local copies, waits for them, and re-layouts: 31 us -> 5.07 us
  other arithmetic: 22.9 us -> 0 us
  waiting for transfers between devices: 18.9 us -> 0 us
  Pallas kernels: 0 us -> 6.82 us
  between operations: 7.35 us -> 0.7 us
  matrix products: 5.8 us -> 0 us
    all_to_all x0 -> x4, blocking collectives: none -> 50.2 us  [swap(): return lax.all_to_all(pieces, 'sec', split_axis=0, concat_axis=0)]
    all_to_all x4 -> x0, waiting for transfers between devices: 18.9 us -> none  [the longest x2 10.2 us: spread(): return lax.all_to_all(pieces, 'sec', split_axis=0, concat_axis=0)]
    all_to_all x4 -> x0, starting transfers between devices: 18.2 us -> none  [the longest x2 11.2 us: spread(): return lax.all_to_all(pieces, 'sec', split_axis=0, concat_axis=0)]
    ppermute x7 -> x0, starting transfers between devices: 11.2 us -> none  [share(): other = lax.ppermute(lanes, 'sec', pairs)]
    gather x6 -> x0, local copies, waits for them, and re-layouts: 9.57 us -> none  [the longest x4 8.29 us: merge(): picked = received[source, term]]
    convert_element_type x6 -> x0, other arithmetic: 7.96 us -> none  [the longest x1 1.89 us: on_device(): jnp.where(live, stay_2 + arrived_2.astype(jnp.float32), 0.0)]
    pallas_call x0 -> x7, Pallas kernels: none -> 6.82 us  [the longest x1 1.32 us: on_device(): call(final_kernel, [SMEM, SMEM] + [VMEM] * 4, block)]
    slice x4 -> x0, local copies, waits for them, and re-layouts: 6.24 us -> none  [the longest x2 3.45 us: on_device(): received = spread(outgoing[1:], n_slots)]
  transfers between devices with their start and end apart: 11 -> 0, of which waited for: 4 -> 0; matrix products, arithmetic and copies ran while one was open for 14% -> 0% of each run, Pallas kernels for 0% -> 0%
where the time goes in v6:
time: 67.6 us; the launch traced here: 67.2 us
  blocking collectives  54.6 us (81%)
  Pallas kernels  6.82 us (10%)
  local copies, waits for them, and re-layouts  5.07 us (8%)
  between operations  0.7 us (1%)
    all_to_all x4, blocking collectives, swap(): return lax.all_to_all(pieces, 'sec', split_axis=0, concat_axis=0)  50.2 us
    unnamed x18, local copies, waits for them, and re-layouts  5.07 us
    all_gather x1, blocking collectives, on_device(): start_full = lax.all_gather(start, 'env')  2.22 us
    all_gather x1, blocking collectives, on_device(): first_full = lax.all_gather(first, 'env')  2.19 us

profile of v6, /device:TPU:0, one launch (start us, length us, event | category | flops | bytes accessed | tf_op | source)
XLA Modules:
  0.0 67.2 jit_solution(9725727934126562115)
XLA Ops:
  0.6 0.0 copy-start.5
  0.6 0.0 copy-start.4
  0.6 0.7 %copy-done.4 = s32[8]{0:T(128)S(1)} copy-done((s32[8]{0:T(128)S(1)}, s32[8]{0:T(128)}, u32[]{:S(2)}) %copy-start.4) | copy-done | bytes 56
  1.4 0.0 copy-start.6
  1.4 0.7 copy-done.6
  2.0 0.0 copy-start.8
  2.0 0.9 %copy-done.8 = bf16[1,128,512]{2,1,0:T(8,128)(2,1)S(1)} copy-done((bf16[1,128,512]{2,1,0:T(8,128)(2,1)S(1)}, bf16[1,128,512]{2,1,0:T(8,128)(2,1)}, u32[]{:S(2)}) %copy-start.8) | copy-done | bytes 131096
  2.9 0.0 copy-start.7
  2.9 0.6 shard_map.68
  3.5 0.0 copy-start.3
  3.5 2.2 %all-gather = bf16[256,512]{1,0:T(8,128)(2,1)S(1)} all-gather(bf16[128,512]{1,0:T(8,128)(2,1)S(1)} %shard_map.68), channel_id=2, replica_groups=mesh['runs'=2,'sec'=8,'env'=2] {'env'}, dimensions={0}, use_global_device_ids=true | all-gather | bytes 393216 | tf_op jit(solution)/shard_map/all_gather | solution.py:310
  5.7 0.0 copy-start
  5.7 1.9 %copy-done = bf16[1,3,1024,512]{3,2,1,0:T(8,128)(2,1)S(1)} copy-done((bf16[1,3,1024,512]{3,2,1,0:T(8,128)(2,1)S(1)}, bf16[1,3,1024,512]{3,2,1,0:T(8,128)(2,1)}, u32[]{:S(2)}) %copy-start) | copy-done | bytes 3145752
  7.6 0.0 copy-start.2
  7.6 0.9 %copy-done.2 = bf16[3,128,128]{2,1,0:T(8,128)(2,1)S(1)} copy-done((bf16[3,128,128]{2,1,0:T(8,128)(2,1)S(1)}, bf16[3,128,128]{2,1,0:T(8,128)(2,1)}, u32[]{:S(2)}) %copy-start.2) | copy-done | bytes 98328
  8.5 0.0 copy-start.1
  8.5 1.0 %shard_map.69 = (bf16[8,2,16,512]{3,2,1,0:T(8,128)(2,1)S(1)}, bf16[128,512]{1,0:T(8,128)(2,1)S(1)}) custom-call(bf16[2,128,512]{2,1,0:T(8,128)(2,1)S(1)} %bitcast.7, bf16[3,128,128]{2,1,0:T(8,128)(2,1)S(1)} %copy-done.2, bf16[1,3,1024,512]{3,2,1,0:T(8,128)(2,1)S(1)} %copy-done), custom_call_target="tpu_custom_call" | custom-call | flops 452984832 | bytes 262144 | tf_op jit(solution)/shard_map/pallas_call | solution.py:311
  9.5 16.2 %all_to_all.20.table.old = bf16[8,2,16,512]{3,2,1,0:T(8,128)(2,1)S(1)} all-to-all(bf16[8,2,16,512]{3,2,1,0:T(8,128)(2,1)S(1)} %get-tuple-element.9), channel_id=1, replica_groups=mesh['runs'=2,'sec'=8,'env'=2] {'sec'}, dimensions={0} | all-to-all | bytes 524288 | tf_op jit(solution)/shard_map/all_to_all | solution.py:288
  25.7 0.0 copy-done.5
  25.7 0.6 shard_map.70
  26.3 10.7 %all_to_all.21 = bf16[8,16,512]{2,1,0:T(8,128)(2,1)S(1)} all-to-all(bf16[8,16,512]{2,1,0:T(8,128)(2,1)S(1)} %shard_map.70), channel_id=1, replica_groups=mesh['runs'=2,'sec'=8,'env'=2] {'sec'}, dimensions={0} | all-to-all | bytes 262144 | tf_op jit(solution)/shard_map/all_to_all | solution.py:288
  37.0 0.0 copy-done.7
  37.0 1.2 %shard_map.71 = bf16[128,512]{1,0:T(8,128)(2,1)} custom-call(s32[8]{0:T(128)S(1)} %copy-done.7, s32[8]{0:T(128)S(1)} %copy-done.5, bf16[128,512]{1,0:T(8,128)(2,1)S(1)} %get-tuple-element.8.stay, bf16[128,512]{1,0:T(8,128)(2,1)S(1)} %bitcast.11), custom_call_target="tpu_custom_call" | custom-call | bytes 262144 | tf_op jit(solution)/shard_map/pallas_call | solution.py:317
  38.3 2.2 %all-gather.1 = bf16[256,512]{1,0:T(8,128)(2,1)S(1)} all-gather(bf16[128,512]{1,0:T(8,128)(2,1)} %shard_map.71), channel_id=3, replica_groups=mesh['runs'=2,'sec'=8,'env'=2] {'env'}, dimensions={0}, use_global_device_ids=true | all-gather | bytes 393216 | tf_op jit(solution)/shard_map/all_gather | solution.py:319
  40.5 0.0 copy-done.3
  40.5 0.0 copy-done.1
  40.5 1.2 %shard_map.72 = (bf16[8,144,128]{2,1,0:T(8,128)(2,1)S(1)}, f32[128,512]{1,0:T(8,128)S(1)}) custom-call(bf16[2,128,512]{2,1,0:T(8,128)(2,1)S(1)} %bitcast.8, bf16[2,128,512]{2,1,0:T(8,128)(2,1)S(1)} %bitcast.9, bf16[3,128,128]{2,1,0:T(8,128)(2,1)S(1)} %copy-done.3, bf16[1,3,1024,512]{3,2,1,0:T(8,128)(2,1)S(1)} %copy-done.1), custom_call_target="tpu_custom_call" | custom-call | flops 452984832 | bytes 262144 | tf_op jit(solution)/shard_map/pallas_call | solution.py:320
  41.7 13.3 %all_to_all.22.new = bf16[8,144,128]{2,1,0:T(8,128)(2,1)S(1)} all-to-all(bf16[8,144,128]{2,1,0:T(8,128)(2,1)S(1)} %get-tuple-element.10), channel_id=1, replica_groups=mesh['runs'=2,'sec'=8,'env'=2] {'sec'}, dimensions={0} | all-to-all | bytes 589824 | tf_op jit(solution)/shard_map/all_to_all | solution.py:288
  55.0 0.9 %shard_map.73 = (bf16[8,16,512]{2,1,0:T(8,128)(2,1)S(1)}, f32[8,128]{1,0:T(8,128)S(1)}) custom-call(s32[8]{0:T(128)S(1)} %copy-done.7, s32[8]{0:T(128)S(1)} %copy-done.5, bf16[8,2,16,512]{3,2,1,0:T(8,128)(2,1)S(1)} %all_to_all.20.table.old, bf16[8,144,128]{2,1,0:T(8,128)(2,1)S(1)} %all_to_all.22.new), custom_call_target="tpu_custom_call" | custom-call | bytes 262144 | tf_op jit(solution)/shard_map/pallas_call | solution.py:324
  55.9 10.0 %all_to_all.23 = bf16[8,16,512]{2,1,0:T(8,128)(2,1)S(1)} all-to-all(bf16[8,16,512]{2,1,0:T(8,128)(2,1)S(1)} %get-tuple-element.13), channel_id=1, replica_groups=mesh['runs'=2,'sec'=8,'env'=2] {'sec'}, dimensions={0} | all-to-all | bytes 262144 | tf_op jit(solution)/shard_map/all_to_all | solution.py:288
  65.9 1.3 %shard_map.74 = bf16[128,512]{1,0:T(8,128)(2,1)} custom-call(s32[8]{0:T(128)S(1)} %copy-done.7, s32[8]{0:T(128)S(1)} %copy-done.5, f32[8,128]{1,0:T(8,128)S(1)} %get-tuple-element.11.factors, bf16[128,512]{1,0:T(8,128)(2,1)S(1)} %get-tuple-element.8.stay, f32[128,512]{1,0:T(8,128)S(1)} %get-tuple-element.12.stay_2, bf16[128,512]{1,0:T(8,128)(2,1)S(1)} %bitcast.10), custom_call_target="tpu_custom_call" | custom-call | bytes 262144 | tf_op jit(solution)/shard_map/pallas_call | solution.py:328
Async XLA Ops:
  0.6 25.1 %copy-start.5 = (s32[8]{0:T(128)S(1)}, s32[8]{0:T(128)}, u32[]{:S(2)}) copy-start(s32[8]{0:T(128)} %holders.9) | copy-start | bytes 100
  0.6 0.7 %copy-start.4 = (s32[8]{0:T(128)S(1)}, s32[8]{0:T(128)}, u32[]{:S(2)}) copy-start(s32[8]{0:T(128)} %holders.9) | copy-start | bytes 100
  1.4 0.7 copy-start.6
  2.0 0.9 %copy-start.8 = (bf16[1,128,512]{2,1,0:T(8,128)(2,1)S(1)}, bf16[1,128,512]{2,1,0:T(8,128)(2,1)}, u32[]{:S(2)}) copy-start(bf16[1,128,512]{2,1,0:T(8,128)(2,1)} %param.5) | copy-start | bytes 393220
  2.9 34.1 %copy-start.7 = (s32[8]{0:T(128)S(1)}, s32[8]{0:T(128)}, u32[]{:S(2)}) copy-start(s32[8]{0:T(128)} %widths.7) | copy-start | bytes 100
  3.5 37.0 %copy-start.3 = (bf16[3,128,128]{2,1,0:T(8,128)(2,1)S(1)}, bf16[3,128,128]{2,1,0:T(8,128)(2,1)}, u32[]{:S(2)}) copy-start(bf16[3,128,128]{2,1,0:T(8,128)(2,1)} %right.3) | copy-start | bytes 294916
  5.7 1.9 %copy-start = (bf16[1,3,1024,512]{3,2,1,0:T(8,128)(2,1)S(1)}, bf16[1,3,1024,512]{3,2,1,0:T(8,128)(2,1)}, u32[]{:S(2)}) copy-start(bf16[1,3,1024,512]{3,2,1,0:T(8,128)(2,1)} %left.3) | copy-start | bytes 9437188
  7.6 0.9 %copy-start.2 = (bf16[3,128,128]{2,1,0:T(8,128)(2,1)S(1)}, bf16[3,128,128]{2,1,0:T(8,128)(2,1)}, u32[]{:S(2)}) copy-start(bf16[3,128,128]{2,1,0:T(8,128)(2,1)} %right.3) | copy-start | bytes 294916
  8.5 32.0 %copy-start.1 = (bf16[1,3,1024,512]{3,2,1,0:T(8,128)(2,1)S(1)}, bf16[1,3,1024,512]{3,2,1,0:T(8,128)(2,1)}, u32[]{:S(2)}) copy-start(bf16[1,3,1024,512]{3,2,1,0:T(8,128)(2,1)} %left.3) | copy-start | bytes 9437188

commit v7 on v6

--- a/solution.py
+++ b/solution.py
@@ -124,16 +124,42 @@
     return jnp.dot(products.astype(jnp.bfloat16), left, preferred_element_type=jnp.float32)
 
 
-def mask_kernel(widths, holders, amps, start):
-    live = live_columns(widths, holders, amps.shape[1])
-    start[...] = jnp.where(live, amps[...], jnp.zeros_like(amps[...]))
-
-
-def first_kernel(start, right, left, message, stay):
-    slots, _, rows, _ = message.shape
+def first_kernel(
+    widths_in,
+    holders_in,
+    amps_in,
+    right_in,
+    left_in,
+    message,
+    stay,
+    start,
+    widths,
+    holders,
+    amps,
+    right,
+    left,
+    sems,
+):
+    slots, _, rows, half = message.shape
+    small = ((widths_in, widths), (holders_in, holders), (amps_in, amps), (right_in, right))
+    large = [(left_in.at[0, term], left.at[term]) for term in range(3)]
+    copies = [
+        pltpu.make_async_copy(source, target, sems.at[i])
+        for i, (source, target) in enumerate([*small, *large])
+    ]
+    for i in (0, 1, 2, 3, 5, 6, 4):
+        copies[i].start()
+    for copy in copies[:4]:
+        copy.wait()
+    width = widths[holders[lax.axis_index("sec")]]
+    columns = lax.broadcasted_iota(jnp.int32, (1, half), 1)
+    for h in range(2):
+        live = h * half + columns < width
+        start[h] = jnp.where(live, amps[h], jnp.zeros_like(amps[h]))
     vector = jnp.concatenate([start[0], start[1]], axis=1)
     for term in (1, 2, 0):
-        block = apply_term(right, left[0, term], vector, term).astype(jnp.bfloat16)
+        copies[4 + term].wait()
+        block = apply_term(right, left[term], vector, term).astype(jnp.bfloat16)
         if term == 0:
             stay[...] = block
         else:
@@ -260,7 +286,8 @@
         out[slot] = (scale * total).astype(jnp.bfloat16)
 
 
-def final_kernel(widths, holders, factors, stay, stay_2, arrived, second):
+def final_kernel(widths, holders, factors, stay, stay_2, arrived, first, second, first_out):
+    first_out[...] = first[...]
     live = live_columns(widths, holders, stay.shape[1])
     scale, shift = factors[0:1, 0:1], factors[1:2, 0:1]
     total = scale * stay_2[...] + shift * stay[...].astype(jnp.float32)
@@ -272,14 +299,17 @@
 VMEM = pl.BlockSpec(memory_space=pltpu.VMEM)
 
 
-def call(kernel, specs, outs, scratch=(), flops=0):
+ANY = pl.BlockSpec(memory_space=pl.ANY)
+
+
+def call(kernel, specs, outs, scratch=(), flops=0, vmem=16):
     return pl.pallas_call(
         kernel,
         out_shape=outs,
         in_specs=specs,
         out_specs=jax.tree.map(lambda _: VMEM, outs),
         scratch_shapes=scratch,
-        compiler_params=pltpu.CompilerParams(vmem_limit_bytes=16 * 1024 * 1024),
+        compiler_params=pltpu.CompilerParams(vmem_limit_bytes=vmem * 1024 * 1024),
         cost_estimate=pl.CostEstimate(flops=flops, bytes_accessed=1 << 18, transcendentals=0),
     )
 
@@ -304,13 +334,19 @@
     factor_shape = jax.ShapeDtypeStruct((8, LANES), jnp.float32)
     slot_table = [pltpu.SMEM((slots,), jnp.int32)]
 
-    start = call(mask_kernel, [SMEM, SMEM, VMEM], block, flops=dots)(
-        widths, holders, amplitudes[0]
-    )
-    start_full = lax.all_gather(start, "env")
-    message, stay = call(first_kernel, [VMEM] * 3, (pairs, block), flops=dots)(
-        start_full, right_env, left_env
-    )
+    amps_full = lax.all_gather(amplitudes[0], "env")
+    both = jax.ShapeDtypeStruct(amps_full.shape, jnp.bfloat16)
+    scratch = [
+        pltpu.SMEM((slots,), jnp.int32),
+        pltpu.SMEM((slots,), jnp.int32),
+        pltpu.VMEM(amps_full.shape, jnp.bfloat16),
+        pltpu.VMEM(right_env.shape, jnp.bfloat16),
+        pltpu.VMEM(left_env.shape[1:], jnp.bfloat16),
+        pltpu.SemaphoreType.DMA((7,)),
+    ]
+    message, stay, start_full = call(
+        first_kernel, [ANY] * 5, (pairs, block, both), scratch, dots, vmem=59
+    )(widths, holders, amps_full, right_env, left_env)
     old = swap(message)
     merged = call(merge_kernel, [SMEM, VMEM], singles, slot_table)(holders, old)
     arrived = swap(merged).reshape(right_dim, half)
@@ -325,8 +361,8 @@
         mix_kernel, [SMEM, SMEM, VMEM, VMEM], (singles, factor_shape), slot_table
     )(widths, holders, old, new)
     arrived = swap(mixed).reshape(right_dim, half)
-    second = call(final_kernel, [SMEM, SMEM] + [VMEM] * 4, block)(
-        widths, holders, factors, stay, stay_2, arrived
+    second, first = call(final_kernel, [SMEM, SMEM] + [VMEM] * 5, (block, block))(
+        widths, holders, factors, stay, stay_2, arrived, first
     )
     return first[None], second[None]
 

time: 67.6 us -> 67.7 us (level)
  local copies, waits for them, and re-layouts: 5.07 us -> 1.89 us
  blocking collectives: 54.6 us -> 56.7 us
  Pallas kernels: 6.82 us -> 8.05 us
    unnamed x18 -> x14, local copies, waits for them, and re-layouts: 5.07 us -> 1.89 us
    all_gather x1, blocking collectives: 2.22 us -> 4.13 us  [on_device(): amps_full = lax.all_gather(amplitudes[0], 'env')]
    pallas_call x3 -> x2, Pallas kernels: 2.87 us -> 4.75 us  [the longest x1 3.42 us: on_device(): call(first_kernel, [ANY] * 5, (pairs, block, both), scratch, dots, vmem=59)]
where the time goes in v7:
time: 67.7 us; the launch traced here: 67.3 us
  blocking collectives  56.7 us (84%)
  Pallas kernels  8.05 us (12%)
  local copies, waits for them, and re-layouts  1.89 us (3%)
  between operations  0.71 us (1%)
    all_to_all x4, blocking collectives, swap(): return lax.all_to_all(pieces, 'sec', split_axis=0, concat_axis=0)  50.5 us
    all_gather x1, blocking collectives, on_device(): amps_full = lax.all_gather(amplitudes[0], 'env')  4.13 us
    pallas_call x1, Pallas kernels, on_device(): call(first_kernel, [ANY] * 5, (pairs, block, both), scratch, dots, vmem=59)  3.42 us
    all_gather x1, blocking collectives, on_device(): first_full = lax.all_gather(first, 'env')  1.99 us
    unnamed x14, local copies, waits for them, and re-layouts  1.89 us

profile of v7, /device:TPU:0, one launch (start us, length us, event | category | flops | bytes accessed | tf_op | source)
XLA Modules:
  0.0 67.3 jit_solution(2443201160914751990)
XLA Ops:
  0.6 0.0 copy-start.5
  0.6 0.0 copy-start.6
  0.7 0.0 copy-start.3
  0.7 0.0 copy-start
  0.7 4.1 %all_gather.9.amps_in = bf16[2,128,512]{2,1,0:T(8,128)(2,1)} all-gather(bf16[1,128,512]{2,1,0:T(8,128)(2,1)} %param.5), channel_id=1, replica_groups=mesh['runs'=2,'sec'=8,'env'=2] {'env'}, dimensions={0}, use_global_device_ids=true | all-gather | bytes 393216 | tf_op jit(solution)/shard_map/all_gather | solution.py:337
  4.8 3.4 %shard_map.68 = (bf16[8,2,16,512]{3,2,1,0:T(8,128)(2,1)}, bf16[128,512]{1,0:T(8,128)(2,1)}, bf16[2,128,512]{2,1,0:T(8,128)(2,1)}) custom-call(s32[8]{0:T(128)} %widths.5, s32[8]{0:T(128)} %holders.7, bf16[2,128,512]{2,1,0:T(8,128)(2,1)} %all_gather.9.amps_in, bf16[3,128,128]{2,1,0:T(8,128)(2,1)} %right.1, bf16[1,3,1024,512]{3,2,1,0:T(8,128)(2,1)} %left.1), custom_call_target="tpu_custom_call" | custom-call | flops 452984832 | bytes 262144 | tf_op jit(solution)/shard_map/pallas_call | solution.py:347
  8.2 16.4 %all_to_all.20.table.old = bf16[8,2,16,512]{3,2,1,0:T(8,128)(2,1)S(1)} all-to-all(bf16[8,2,16,512]{3,2,1,0:T(8,128)(2,1)} %get-tuple-element.11), channel_id=1, replica_groups=mesh['runs'=2,'sec'=8,'env'=2] {'sec'}, dimensions={0} | all-to-all | bytes 524288 | tf_op jit(solution)/shard_map/all_to_all | solution.py:318
  24.6 0.0 copy-done.5
  24.6 0.6 shard_map.69
  25.2 0.0 copy-start.2
  25.3 10.9 %all_to_all.21 = bf16[8,16,512]{2,1,0:T(8,128)(2,1)S(1)} all-to-all(bf16[8,16,512]{2,1,0:T(8,128)(2,1)S(1)} %shard_map.69), channel_id=1, replica_groups=mesh['runs'=2,'sec'=8,'env'=2] {'sec'}, dimensions={0} | all-to-all | bytes 262144 | tf_op jit(solution)/shard_map/all_to_all | solution.py:318
  36.1 0.0 copy-done.6
  36.1 0.0 copy-start.1
  36.1 0.9 %copy-done.1 = bf16[128,512]{1,0:T(8,128)(2,1)S(1)} copy-done((bf16[128,512]{1,0:T(8,128)(2,1)S(1)}, bf16[128,512]{1,0:T(8,128)(2,1)}, u32[]{:S(2)}) %copy-start.1) | copy-done | bytes 131096
  37.0 0.6 shard_map.70.first
  37.6 2.0 %all-gather = bf16[256,512]{1,0:T(8,128)(2,1)S(1)} all-gather(bf16[128,512]{1,0:T(8,128)(2,1)S(1)} %shard_map.70.first), channel_id=2, replica_groups=mesh['runs'=2,'sec'=8,'env'=2] {'env'}, dimensions={0}, use_global_device_ids=true | all-gather | bytes 393216 | tf_op jit(solution)/shard_map/all_gather | solution.py:355
  39.6 0.0 copy-done.3
  39.6 0.0 copy-done
  39.6 0.0 copy-start.4
  39.6 0.9 %copy-done.4 = bf16[2,128,512]{2,1,0:T(8,128)(2,1)S(1)} copy-done((bf16[2,128,512]{2,1,0:T(8,128)(2,1)S(1)}, bf16[2,128,512]{2,1,0:T(8,128)(2,1)}, u32[]{:S(2)}) %copy-start.4) | copy-done | bytes 262168
  40.6 1.2 %shard_map.71 = (bf16[8,144,128]{2,1,0:T(8,128)(2,1)S(1)}, f32[128,512]{1,0:T(8,128)S(1)}) custom-call(bf16[2,128,512]{2,1,0:T(8,128)(2,1)S(1)} %copy-done.4, bf16[2,128,512]{2,1,0:T(8,128)(2,1)S(1)} %bitcast.5, bf16[3,128,128]{2,1,0:T(8,128)(2,1)S(1)} %copy-done.3, bf16[1,3,1024,512]{3,2,1,0:T(8,128)(2,1)S(1)} %copy-done), custom_call_target="tpu_custom_call" | custom-call | flops 452984832 | bytes 262144 | tf_op jit(solution)/shard_map/pallas_call | solution.py:356
  41.8 13.3 %all_to_all.22.new = bf16[8,144,128]{2,1,0:T(8,128)(2,1)S(1)} all-to-all(bf16[8,144,128]{2,1,0:T(8,128)(2,1)S(1)} %get-tuple-element.14), channel_id=1, replica_groups=mesh['runs'=2,'sec'=8,'env'=2] {'sec'}, dimensions={0} | all-to-all | bytes 589824 | tf_op jit(solution)/shard_map/all_to_all | solution.py:318
  55.1 0.9 %shard_map.72 = (bf16[8,16,512]{2,1,0:T(8,128)(2,1)S(1)}, f32[8,128]{1,0:T(8,128)S(1)}) custom-call(s32[8]{0:T(128)S(1)} %copy-done.6, s32[8]{0:T(128)S(1)} %copy-done.5, bf16[8,2,16,512]{3,2,1,0:T(8,128)(2,1)S(1)} %all_to_all.20.table.old, bf16[8,144,128]{2,1,0:T(8,128)(2,1)S(1)} %all_to_all.22.new), custom_call_target="tpu_custom_call" | custom-call | bytes 262144 | tf_op jit(solution)/shard_map/pallas_call | solution.py:360
  56.0 10.0 %all_to_all.23 = bf16[8,16,512]{2,1,0:T(8,128)(2,1)S(1)} all-to-all(bf16[8,16,512]{2,1,0:T(8,128)(2,1)S(1)} %get-tuple-element.17), channel_id=1, replica_groups=mesh['runs'=2,'sec'=8,'env'=2] {'sec'}, dimensions={0} | all-to-all | bytes 262144 | tf_op jit(solution)/shard_map/all_to_all | solution.py:318
  66.0 0.0 copy-done.2
  66.0 1.3 %shard_map.73 = (bf16[128,512]{1,0:T(8,128)(2,1)}, bf16[128,512]{1,0:T(8,128)(2,1)}) custom-call(s32[8]{0:T(128)S(1)} %copy-done.6, s32[8]{0:T(128)S(1)} %copy-done.5, f32[8,128]{1,0:T(8,128)S(1)} %get-tuple-element.15.factors, bf16[128,512]{1,0:T(8,128)(2,1)S(1)} %copy-done.2, f32[128,512]{1,0:T(8,128)S(1)} %get-tuple-element.16.stay_2, ...), custom_call_target="tpu_custom_call" | custom-call | bytes 262144 | tf_op jit(solution)/shard_map/pallas_call | solution.py:364
Async XLA Ops:
  0.6 24.0 %copy-start.5 = (s32[8]{0:T(128)S(1)}, s32[8]{0:T(128)}, u32[]{:S(2)}) copy-start(s32[8]{0:T(128)} %holders.7) | copy-start | bytes 100
  0.6 35.5 %copy-start.6 = (s32[8]{0:T(128)S(1)}, s32[8]{0:T(128)}, u32[]{:S(2)}) copy-start(s32[8]{0:T(128)} %widths.5) | copy-start | bytes 100
  0.7 39.0 %copy-start.3 = (bf16[3,128,128]{2,1,0:T(8,128)(2,1)S(1)}, bf16[3,128,128]{2,1,0:T(8,128)(2,1)}, u32[]{:S(2)}) copy-start(bf16[3,128,128]{2,1,0:T(8,128)(2,1)} %right.1) | copy-start | bytes 294916
  0.7 38.9 %copy-start = (bf16[1,3,1024,512]{3,2,1,0:T(8,128)(2,1)S(1)}, bf16[1,3,1024,512]{3,2,1,0:T(8,128)(2,1)}, u32[]{:S(2)}) copy-start(bf16[1,3,1024,512]{3,2,1,0:T(8,128)(2,1)} %left.1) | copy-start | bytes 9437188
  25.2 40.7 %copy-start.2 = (bf16[128,512]{1,0:T(8,128)(2,1)S(1)}, bf16[128,512]{1,0:T(8,128)(2,1)}, u32[]{:S(2)}) copy-start(bf16[128,512]{1,0:T(8,128)(2,1)} %get-tuple-element.13.stay) | copy-start | bytes 393220
  36.1 0.9 %copy-start.1 = (bf16[128,512]{1,0:T(8,128)(2,1)S(1)}, bf16[128,512]{1,0:T(8,128)(2,1)}, u32[]{:S(2)}) copy-start(bf16[128,512]{1,0:T(8,128)(2,1)} %get-tuple-element.13.stay) | copy-start | bytes 393220
  39.6 1.0 %copy-start.4 = (bf16[2,128,512]{2,1,0:T(8,128)(2,1)S(1)}, bf16[2,128,512]{2,1,0:T(8,128)(2,1)}, u32[]{:S(2)}) copy-start(bf16[2,128,512]{2,1,0:T(8,128)(2,1)} %get-tuple-element.12.start) | copy-start | bytes 786436

commit v8 on v6

--- a/solution.py
+++ b/solution.py
@@ -124,13 +124,17 @@
     return jnp.dot(products.astype(jnp.bfloat16), left, preferred_element_type=jnp.float32)
 
 
-def mask_kernel(widths, holders, amps, start):
-    live = live_columns(widths, holders, amps.shape[1])
-    start[...] = jnp.where(live, amps[...], jnp.zeros_like(amps[...]))
-
-
-def first_kernel(start, right, left, message, stay):
-    slots, _, rows, _ = message.shape
+def stage_kernel(amps, staged):
+    staged[...] = amps[...]
+
+
+def first_kernel(widths, holders, amps, right, left, message, stay, start):
+    slots, _, rows, half = message.shape
+    width = widths[holders[lax.axis_index("sec")]]
+    columns = lax.broadcasted_iota(jnp.int32, (1, half), 1)
+    for h in range(2):
+        live = h * half + columns < width
+        start[h] = jnp.where(live, amps[h], jnp.zeros_like(amps[h]))
     vector = jnp.concatenate([start[0], start[1]], axis=1)
     for term in (1, 2, 0):
         block = apply_term(right, left[0, term], vector, term).astype(jnp.bfloat16)
@@ -260,7 +264,8 @@
         out[slot] = (scale * total).astype(jnp.bfloat16)
 
 
-def final_kernel(widths, holders, factors, stay, stay_2, arrived, second):
+def final_kernel(widths, holders, factors, stay, stay_2, arrived, first, second, first_out):
+    first_out[...] = first[...]
     live = live_columns(widths, holders, stay.shape[1])
     scale, shift = factors[0:1, 0:1], factors[1:2, 0:1]
     total = scale * stay_2[...] + shift * stay[...].astype(jnp.float32)
@@ -304,13 +309,12 @@
     factor_shape = jax.ShapeDtypeStruct((8, LANES), jnp.float32)
     slot_table = [pltpu.SMEM((slots,), jnp.int32)]
 
-    start = call(mask_kernel, [SMEM, SMEM, VMEM], block, flops=dots)(
-        widths, holders, amplitudes[0]
-    )
-    start_full = lax.all_gather(start, "env")
-    message, stay = call(first_kernel, [VMEM] * 3, (pairs, block), flops=dots)(
-        start_full, right_env, left_env
-    )
+    staged = call(stage_kernel, [VMEM], block, flops=4 << 30)(amplitudes[0])
+    amps_full = lax.all_gather(staged, "env")
+    both = jax.ShapeDtypeStruct(amps_full.shape, jnp.bfloat16)
+    message, stay, start_full = call(
+        first_kernel, [SMEM, SMEM] + [VMEM] * 3, (pairs, block, both), flops=dots
+    )(widths, holders, amps_full, right_env, left_env)
     old = swap(message)
     merged = call(merge_kernel, [SMEM, VMEM], singles, slot_table)(holders, old)
     arrived = swap(merged).reshape(right_dim, half)
@@ -325,8 +329,8 @@
         mix_kernel, [SMEM, SMEM, VMEM, VMEM], (singles, factor_shape), slot_table
     )(widths, holders, old, new)
     arrived = swap(mixed).reshape(right_dim, half)
-    second = call(final_kernel, [SMEM, SMEM] + [VMEM] * 4, block)(
-        widths, holders, factors, stay, stay_2, arrived
+    second, first = call(final_kernel, [SMEM, SMEM] + [VMEM] * 5, (block, block))(
+        widths, holders, factors, stay, stay_2, arrived, first
     )
     return first[None], second[None]
 

time: 67.6 us -> 62.5 us (0.925)
  local copies, waits for them, and re-layouts: 5.07 us -> 0.91 us
    unnamed x18 -> x10, local copies, waits for them, and re-layouts: 5.07 us -> 0.91 us
where the time goes in v8:
time: 62.5 us; the launch traced here: 62.2 us
  blocking collectives  54.4 us (87%)
  Pallas kernels  6.18 us (10%)
  local copies, waits for them, and re-layouts  0.91 us (1%)
  between operations  0.7 us (1%)
    all_to_all x4, blocking collectives, swap(): return lax.all_to_all(pieces, 'sec', split_axis=0, concat_axis=0)  50.2 us
    all_gather x1, blocking collectives, on_device(): amps_full = lax.all_gather(staged, 'env')  2.22 us
    all_gather x1, blocking collectives, on_device(): first_full = lax.all_gather(first, 'env')  1.99 us
    pallas_call x1, Pallas kernels, on_device(): call(first_kernel, [SMEM, SMEM] + [VMEM] * 3, (pairs, block, both), flops...  1.53 us
    pallas_call x1, Pallas kernels, on_device(): call(final_kernel, [SMEM, SMEM] + [VMEM] * 5, (block, block))  1.33 us

profile of v8, /device:TPU:0, one launch (start us, length us, event | category | flops | bytes accessed | tf_op | source)
XLA Modules:
  0.0 62.2 jit_solution(679623017516005859)
XLA Ops:
  0.6 0.0 copy-start.4
  0.6 0.9 %copy-done.4 = bf16[1,128,512]{2,1,0:T(8,128)(2,1)S(1)} copy-done((bf16[1,128,512]{2,1,0:T(8,128)(2,1)S(1)}, bf16[1,128,512]{2,1,0:T(8,128)(2,1)}, u32[]{:S(2)}) %copy-start.4) | copy-done | bytes 131096
  1.5 0.0 copy-start
  1.5 0.0 copy-start.1
  1.5 0.0 copy-start.2
  1.5 0.0 copy-start.3
  1.6 2.2 %all-gather = bf16[256,512]{1,0:T(8,128)(2,1)S(1)} all-gather(bf16[128,512]{1,0:T(8,128)(2,1)S(1)} %shard_map.68), channel_id=2, replica_groups=mesh['runs'=2,'sec'=8,'env'=2] {'env'}, dimensions={0}, use_global_device_ids=true | all-gather | bytes 393216 | tf_op jit(solution)/shard_map/all_gather | solution.py:313
  3.8 0.0 copy-done
  3.8 0.0 copy-done.1
  3.8 0.0 copy-done.2
  3.8 0.0 copy-done.3
  3.8 1.5 %shard_map.69 = (bf16[8,2,16,512]{3,2,1,0:T(8,128)(2,1)S(1)}, bf16[128,512]{1,0:T(8,128)(2,1)S(1)}, bf16[2,128,512]{2,1,0:T(8,128)(2,1)S(1)}) custom-call(s32[8]{0:T(128)S(1)} %copy-done.3, s32[8]{0:T(128)S(1)} %copy-done.2, bf16[2,128,512]{2,1,0:T(8,128)(2,1)S(1)} %bitcast.8, bf16[3,128,128]{2,1,0:T(8,128)(2,1)S(1)} %copy-done.1, ...), custom_call_target="tpu_custom_call" | custom-call | flops 452984832 | bytes 262144 | tf_op jit(solution)/shard_map/pallas_call | solution.py:315
  5.3 16.2 %all_to_all.20.table.old = bf16[8,2,16,512]{3,2,1,0:T(8,128)(2,1)S(1)} all-to-all(bf16[8,2,16,512]{3,2,1,0:T(8,128)(2,1)S(1)} %get-tuple-element.11), channel_id=1, replica_groups=mesh['runs'=2,'sec'=8,'env'=2] {'sec'}, dimensions={0} | all-to-all | bytes 524288 | tf_op jit(solution)/shard_map/all_to_all | solution.py:293
  21.5 0.6 shard_map.70
  22.1 10.7 %all_to_all.21 = bf16[8,16,512]{2,1,0:T(8,128)(2,1)S(1)} all-to-all(bf16[8,16,512]{2,1,0:T(8,128)(2,1)S(1)} %shard_map.70), channel_id=1, replica_groups=mesh['runs'=2,'sec'=8,'env'=2] {'sec'}, dimensions={0} | all-to-all | bytes 262144 | tf_op jit(solution)/shard_map/all_to_all | solution.py:293
  32.9 0.6 shard_map.71.first
  33.5 2.0 %all-gather.1 = bf16[256,512]{1,0:T(8,128)(2,1)S(1)} all-gather(bf16[128,512]{1,0:T(8,128)(2,1)S(1)} %shard_map.71.first), channel_id=3, replica_groups=mesh['runs'=2,'sec'=8,'env'=2] {'env'}, dimensions={0}, use_global_device_ids=true | all-gather | bytes 393216 | tf_op jit(solution)/shard_map/all_gather | solution.py:323
  35.5 1.2 %shard_map.72 = (bf16[8,144,128]{2,1,0:T(8,128)(2,1)S(1)}, f32[128,512]{1,0:T(8,128)S(1)}) custom-call(bf16[2,128,512]{2,1,0:T(8,128)(2,1)S(1)} %get-tuple-element.12.start, bf16[2,128,512]{2,1,0:T(8,128)(2,1)S(1)} %bitcast.7, bf16[3,128,128]{2,1,0:T(8,128)(2,1)S(1)} %copy-done.1, bf16[1,3,1024,512]{3,2,1,0:T(8,128)(2,1)S(1)} %copy-done), custom_call_target="tpu_custom_call" | custom-call | flops 452984832 | bytes 262144 | tf_op jit(solution)/shard_map/pallas_call | solution.py:324
  36.7 13.3 %all_to_all.22.new = bf16[8,144,128]{2,1,0:T(8,128)(2,1)S(1)} all-to-all(bf16[8,144,128]{2,1,0:T(8,128)(2,1)S(1)} %get-tuple-element.14), channel_id=1, replica_groups=mesh['runs'=2,'sec'=8,'env'=2] {'sec'}, dimensions={0} | all-to-all | bytes 589824 | tf_op jit(solution)/shard_map/all_to_all | solution.py:293
  50.0 0.9 %shard_map.73 = (bf16[8,16,512]{2,1,0:T(8,128)(2,1)S(1)}, f32[8,128]{1,0:T(8,128)S(1)}) custom-call(s32[8]{0:T(128)S(1)} %copy-done.3, s32[8]{0:T(128)S(1)} %copy-done.2, bf16[8,2,16,512]{3,2,1,0:T(8,128)(2,1)S(1)} %all_to_all.20.table.old, bf16[8,144,128]{2,1,0:T(8,128)(2,1)S(1)} %all_to_all.22.new), custom_call_target="tpu_custom_call" | custom-call | bytes 262144 | tf_op jit(solution)/shard_map/pallas_call | solution.py:328
  50.9 10.0 %all_to_all.23 = bf16[8,16,512]{2,1,0:T(8,128)(2,1)S(1)} all-to-all(bf16[8,16,512]{2,1,0:T(8,128)(2,1)S(1)} %get-tuple-element.17), channel_id=1, replica_groups=mesh['runs'=2,'sec'=8,'env'=2] {'sec'}, dimensions={0} | all-to-all | bytes 262144 | tf_op jit(solution)/shard_map/all_to_all | solution.py:293
  60.9 1.3 %shard_map.74 = (bf16[128,512]{1,0:T(8,128)(2,1)}, bf16[128,512]{1,0:T(8,128)(2,1)}) custom-call(s32[8]{0:T(128)S(1)} %copy-done.3, s32[8]{0:T(128)S(1)} %copy-done.2, f32[8,128]{1,0:T(8,128)S(1)} %get-tuple-element.15.factors, bf16[128,512]{1,0:T(8,128)(2,1)S(1)} %get-tuple-element.13.stay, f32[128,512]{1,0:T(8,128)S(1)} %get-tuple-element.16.stay_2, ...), custom_call_target="tpu_custom_call" | custom-call | bytes 262144 | tf_op jit(solution)/shard_map/pallas_call | solution.py:332
  (1 shorter events, 0.0 us)
Async XLA Ops:
  0.6 0.9 %copy-start.4 = (bf16[1,128,512]{2,1,0:T(8,128)(2,1)S(1)}, bf16[1,128,512]{2,1,0:T(8,128)(2,1)}, u32[]{:S(2)}) copy-start(bf16[1,128,512]{2,1,0:T(8,128)(2,1)} %param.5) | copy-start | bytes 393220
  1.5 2.2 %copy-start = (bf16[1,3,1024,512]{3,2,1,0:T(8,128)(2,1)S(1)}, bf16[1,3,1024,512]{3,2,1,0:T(8,128)(2,1)}, u32[]{:S(2)}) copy-start(bf16[1,3,1024,512]{3,2,1,0:T(8,128)(2,1)} %left.3) | copy-start | bytes 9437188
  1.5 2.2 %copy-start.1 = (bf16[3,128,128]{2,1,0:T(8,128)(2,1)S(1)}, bf16[3,128,128]{2,1,0:T(8,128)(2,1)}, u32[]{:S(2)}) copy-start(bf16[3,128,128]{2,1,0:T(8,128)(2,1)} %right.3) | copy-start | bytes 294916
  1.5 2.2 %copy-start.2 = (s32[8]{0:T(128)S(1)}, s32[8]{0:T(128)}, u32[]{:S(2)}) copy-start(s32[8]{0:T(128)} %holders.9) | copy-start | bytes 100
  1.5 2.3 %copy-start.3 = (s32[8]{0:T(128)S(1)}, s32[8]{0:T(128)}, u32[]{:S(2)}) copy-start(s32[8]{0:T(128)} %widths.7) | copy-start | bytes 100

commit v9 on v8

--- a/solution.py
+++ b/solution.py
@@ -111,6 +111,7 @@
 
 LANES = 128
 TAG = 16
+LINES = 2
 
 
 def live_columns(widths, holders, half):
@@ -157,15 +158,28 @@
     return has, source
 
 
-def merge_kernel(holders, table, out, slot_of):
+def line_targets(holders, slot_of):
+    line = lax.axis_index("sec") % LINES
+    for place in range(holders.shape[0] // LINES):
+        for crossing in range(2):
+            has, source = sources_of(holders, slot_of, place * LINES + (line ^ crossing))
+            here = [has[i] & (source[i] % LINES == line) for i in range(2)]
+            yield place, crossing, here, source
+
+
+def merge_kernel(holders, table, keep, cross, slot_of):
     fill_slots(holders, slot_of)
-    for slot in range(holders.shape[0]):
-        has, source = sources_of(holders, slot_of, slot)
+    for place, crossing, here, source in line_targets(holders, slot_of):
         total = 0.0
         for i in range(2):
-            block = table[source[i], i].astype(jnp.float32)
-            total = total + jnp.where(has[i], block, 0.0)
-        out[slot] = total.astype(jnp.bfloat16)
+            block = table[source[i] // LINES, i].astype(jnp.float32)
+            total = total + jnp.where(here[i], block, 0.0)
+        (keep, cross)[crossing][place] = total.astype(jnp.bfloat16)
+
+
+def join_kernel(keep, arrived, out):
+    total = keep[...].astype(jnp.float32) + arrived[...].astype(jnp.float32)
+    out[...] = total.astype(jnp.bfloat16)
 
 
 def sum_kernel(widths, holders, stay, arrived, first):
@@ -221,47 +235,84 @@
                     ]
 
 
-def mix_kernel(widths, holders, old, new, out, factors, slot_of):
-    slots, rows, half = out.shape
+def read_tag(tag):
+    def value(place):
+        parts = [tag[3 * place + i : 3 * place + i + 1, :] for i in range(3)]
+        return parts[0] + parts[1] + parts[2]
+
+    return [value(place) for place in range(4)]
+
+
+def line_quotient(overlaps, norms, line):
+    inside = lax.broadcasted_iota(jnp.int32, (1, LANES), 1) % LINES == line
+    overlap = total_of(jnp.where(inside, overlaps, 0.0))
+    norm = total_of(jnp.where(inside, norms, 0.0))
+    return jnp.where(norm > 0, overlap / jnp.where(norm > 0, norm, 1.0), 0.0)
+
+
+def mix_kernel(holders, old, new, keep, cross, tag_out, slot_of):
+    places, rows, half = keep.shape
     chunks = half // LANES
     fill_slots(holders, slot_of)
     tag = jnp.zeros((TAG, LANES), jnp.float32)
+    for place in range(places):
+        tag = tag + new[place, pl.ds(2 * chunks * rows, TAG), :].astype(jnp.float32)
+    tag_out[...] = tag.astype(jnp.bfloat16)
+    cross[pl.ds(places * chunks * rows, TAG), :] = tag.astype(jnp.bfloat16)
+    overlaps, norms, quotients, _ = read_tag(tag)
+    shifts = quotients - line_quotient(overlaps, norms, lax.axis_index("sec") % LINES)
+    lane = lax.broadcasted_iota(jnp.int32, (1, LANES), 1)
+    for place, crossing, here, source in line_targets(holders, slot_of):
+        total = 0.0
+        for i in range(2):
+            where = source[i] // LINES
+            block = jnp.concatenate(
+                [new[where, pl.ds((i * chunks + c) * rows, rows), :] for c in range(chunks)],
+                axis=1,
+            ).astype(jnp.float32)
+            shift = total_of(jnp.where(lane == source[i], shifts, 0.0))
+            block = block + shift * old[where, i].astype(jnp.float32)
+            total = total + jnp.where(here[i], block, 0.0)
+        if crossing:
+            total = total.astype(jnp.bfloat16)
+            for c in range(chunks):
+                target = pl.ds((place * chunks + c) * rows, rows)
+                cross[target, :] = total[:, c * LANES : (c + 1) * LANES]
+        else:
+            keep[place] = total
+
+
+def join_mixed_kernel(widths, tag_line, keep, arrived, old_keep, old_arrived, out, factors):
+    places, rows, half = keep.shape
+    chunks = half // LANES
+    slots = widths.shape[0]
+    me = lax.axis_index("sec")
     total = jnp.int32(0)
     for slot in range(slots):
-        tag = tag + new[slot, pl.ds(2 * chunks * rows, TAG), :].astype(jnp.float32)
         total = total + widths[slot]
-    live_count = slots * rows * total.astype(jnp.float32)
-
-    def value(place):
-        parts = [tag[3 * place + i : 3 * place + i + 1, :] for i in range(3)]
-        return parts[0] + parts[1] + parts[2]
-
-    overlaps, norms, quotients, rests = (value(place) for place in range(4))
+    live_count = places * rows * total.astype(jnp.float32)
+    tag = tag_line[...].astype(jnp.float32)
+    tag = tag + arrived[pl.ds(places * chunks * rows, TAG), :].astype(jnp.float32)
+    overlaps, norms, quotients, rests = read_tag(tag)
     quotient = total_of(overlaps) / total_of(norms)
     lane = lax.broadcasted_iota(jnp.int32, (1, LANES), 1)
     shifts = jnp.where(lane < slots, quotients - quotient, 0.0)
     resid_norm = total_of(rests + shifts * shifts * norms)
     scale = lax.rsqrt(resid_norm / live_count + 1e-06)
-
-    def shift_of(slot):
-        return total_of(jnp.where(lane == slot, shifts, 0.0))
-
     row = lax.broadcasted_iota(jnp.int32, factors.shape, 0)
-    factors[...] = jnp.where(row == 0, scale, scale * shift_of(lax.axis_index("sec")))
-    for slot in range(slots):
-        has, source = sources_of(holders, slot_of, slot)
-        total = 0.0
-        for i in range(2):
-            block = jnp.concatenate(
-                [
-                    new[source[i], pl.ds((i * chunks + c) * rows, rows), :]
-                    for c in range(chunks)
-                ],
-                axis=1,
-            ).astype(jnp.float32)
-            block = block + shift_of(source[i]) * old[source[i], i].astype(jnp.float32)
-            total = total + jnp.where(has[i], block, 0.0)
-        out[slot] = (scale * total).astype(jnp.bfloat16)
+    own_shift = total_of(jnp.where(lane == me, shifts, 0.0))
+    factors[...] = jnp.where(row == 0, scale, scale * own_shift)
+    line = me % LINES
+    shift_here = line_quotient(overlaps, norms, line) - quotient
+    shift_there = line_quotient(overlaps, norms, 1 - line) - quotient
+    for place in range(places):
+        block = jnp.concatenate(
+            [arrived[pl.ds((place * chunks + c) * rows, rows), :] for c in range(chunks)],
+            axis=1,
+        ).astype(jnp.float32)
+        block = block + shift_there * old_arrived[place].astype(jnp.float32)
+        block = block + keep[place] + shift_here * old_keep[place].astype(jnp.float32)
+        out[place] = (scale * block).astype(jnp.bfloat16)
 
 
 def final_kernel(widths, holders, factors, stay, stay_2, arrived, first, second, first_out):
@@ -289,8 +340,14 @@
     )
 
 
-def swap(pieces):
-    return lax.all_to_all(pieces, "sec", split_axis=0, concat_axis=0)
+def along_line(pieces):
+    places = pieces.shape[0]
+    groups = [[place * LINES + line for place in range(places)] for line in range(LINES)]
+    return lax.all_to_all(pieces, "sec", 0, 0, axis_index_groups=groups)
+
+
+def across(piece, slots):
+    return lax.ppermute(piece, "sec", [(slot, slot ^ 1) for slot in range(slots)])
 
 
 def on_device(amplitudes, widths, holders, left_env, right_env):
@@ -299,13 +356,18 @@
     assert slots_dev == 1
     if slots != 2 * QDOWN:
         return on_device_any(amplitudes, widths, holders, left_env, right_env)
-    rows = right_dim // slots
+    places = slots // LINES
+    rows = right_dim // places
     dots = 6 * right_dim * half * (right_dim + 2 * half)
     block = jax.ShapeDtypeStruct((right_dim, half), jnp.bfloat16)
     wide = jax.ShapeDtypeStruct((right_dim, half), jnp.float32)
-    pairs = jax.ShapeDtypeStruct((slots, 2, rows, half), jnp.bfloat16)
-    singles = jax.ShapeDtypeStruct((slots, rows, half), jnp.bfloat16)
-    tagged = jax.ShapeDtypeStruct((slots, 2 * rows * half // LANES + TAG, LANES), jnp.bfloat16)
+    pairs = jax.ShapeDtypeStruct((places, 2, rows, half), jnp.bfloat16)
+    singles = jax.ShapeDtypeStruct((places, rows, half), jnp.bfloat16)
+    wides = jax.ShapeDtypeStruct((places, rows, half), jnp.float32)
+    chunked = rows * half // LANES
+    tagged = jax.ShapeDtypeStruct((places, 2 * chunked + TAG, LANES), jnp.bfloat16)
+    crossing = jax.ShapeDtypeStruct((places * chunked + TAG, LANES), jnp.bfloat16)
+    label = jax.ShapeDtypeStruct((TAG, LANES), jnp.bfloat16)
     factor_shape = jax.ShapeDtypeStruct((8, LANES), jnp.float32)
     slot_table = [pltpu.SMEM((slots,), jnp.int32)]
 
@@ -315,20 +377,25 @@
     message, stay, start_full = call(
         first_kernel, [SMEM, SMEM] + [VMEM] * 3, (pairs, block, both), flops=dots
     )(widths, holders, amps_full, right_env, left_env)
-    old = swap(message)
-    merged = call(merge_kernel, [SMEM, VMEM], singles, slot_table)(holders, old)
-    arrived = swap(merged).reshape(right_dim, half)
+    old = along_line(message)
+    old_keep, cross = call(merge_kernel, [SMEM, VMEM], (singles, singles), slot_table)(holders, old)
+    old_arrived = across(cross, slots)
+    joined = call(join_kernel, [VMEM, VMEM], singles)(old_keep, old_arrived)
+    arrived = along_line(joined).reshape(right_dim, half)
     first = call(sum_kernel, [SMEM, SMEM, VMEM, VMEM], block)(widths, holders, stay, arrived)
 
     first_full = lax.all_gather(first, "env")
     message, stay_2 = call(second_kernel, [VMEM] * 4, (tagged, wide), flops=dots)(
         start_full, first_full, right_env, left_env
     )
-    new = swap(message)
-    mixed, factors = call(
-        mix_kernel, [SMEM, SMEM, VMEM, VMEM], (singles, factor_shape), slot_table
-    )(widths, holders, old, new)
-    arrived = swap(mixed).reshape(right_dim, half)
+    new = along_line(message)
+    keep, cross, tag = call(
+        mix_kernel, [SMEM, VMEM, VMEM], (wides, crossing, label), slot_table
+    )(holders, old, new)
+    joined, factors = call(join_mixed_kernel, [SMEM] + [VMEM] * 5, (singles, factor_shape))(
+        widths, tag, keep, across(cross, slots), old_keep, old_arrived
+    )
+    arrived = along_line(joined).reshape(right_dim, half)
     second, first = call(final_kernel, [SMEM, SMEM] + [VMEM] * 5, (block, block))(
         widths, holders, factors, stay, stay_2, arrived, first
     )

time: 62.5 us -> 68.1 us (1.090)
  waiting for transfers between devices: 0 us -> 7.01 us
  blocking collectives: 54.4 us -> 48.7 us
  starting transfers between devices: 0 us -> 3.1 us
  Pallas kernels: 6.18 us -> 7.34 us
    ppermute x0 -> x2, waiting for transfers between devices: none -> 7.01 us  [across(): lax.ppermute(piece, 'sec', [(slot, slot ^ 1) for slot in range(slots)])]
    all_to_all x4, blocking collectives: 50.2 us -> 44.5 us  [along_line(): return lax.all_to_all(pieces, 'sec', 0, 0, axis_index_groups=groups)]
    ppermute x0 -> x2, starting transfers between devices: none -> 3.1 us  [across(): lax.ppermute(piece, 'sec', [(slot, slot ^ 1) for slot in range(slots)])]
    pallas_call x2 -> x4, Pallas kernels: 1.52 us -> 2.67 us  [the longest x1 0.99 us: on_device(): call(mix_kernel, [SMEM, VMEM, VMEM], (wides, crossing, label), slot_table)]
  transfers between devices with their start and end apart: 0 -> 2, of which waited for: 0 -> 2; matrix products, arithmetic and copies ran while one was open for 0% -> 0% of each run, Pallas kernels for 0% -> 0%
where the time goes in v9:
time: 68.1 us; the launch traced here: 67.8 us
  blocking collectives  48.7 us (72%)
  Pallas kernels  7.34 us (11%)
  waiting for transfers between devices  7.01 us (10%)
  starting transfers between devices  3.1 us (5%)
  local copies, waits for them, and re-layouts  0.91 us (1%)
  between operations  0.7 us (1%)
    all_to_all x4, blocking collectives, along_line(): return lax.all_to_all(pieces, 'sec', 0, 0, axis_index_groups=groups)  44.5 us
    ppermute x2, waiting for transfers between devices, across(): lax.ppermute(piece, 'sec', [(slot, slot ^ 1) for slot in range(slots)])  7.01 us
    ppermute x2, starting transfers between devices, across(): lax.ppermute(piece, 'sec', [(slot, slot ^ 1) for slot in range(slots)])  3.1 us
    all_gather x1, blocking collectives, on_device(): amps_full = lax.all_gather(staged, 'env')  2.22 us
    all_gather x1, blocking collectives, on_device(): first_full = lax.all_gather(first, 'env')  1.99 us
    pallas_call x1, Pallas kernels, on_device(): call(first_kernel, [SMEM, SMEM] + [VMEM] * 3, (pairs, block, both), flops...  1.53 us
  transfers between devices with their start and end apart: 2, of which 2 were waited for; matrix products, arithmetic and copies ran while one was open for 0% of the time, Pallas kernels for 0%

profile of v9, /device:TPU:0, one launch (start us, length us, event | category | flops | bytes accessed | tf_op | source)
XLA Modules:
  0.0 67.8 jit_solution(1729813490799322808)
XLA Ops:
  0.6 0.0 copy-start.4
  0.6 0.9 %copy-done.4 = bf16[1,128,512]{2,1,0:T(8,128)(2,1)S(1)} copy-done((bf16[1,128,512]{2,1,0:T(8,128)(2,1)S(1)}, bf16[1,128,512]{2,1,0:T(8,128)(2,1)}, u32[]{:S(2)}) %copy-start.4) | copy-done | bytes 131096
  1.5 0.0 copy-start
  1.5 0.0 copy-start.1
  1.5 0.0 copy-start.2
  1.5 0.0 copy-start.3
  1.6 2.2 %all-gather = bf16[256,512]{1,0:T(8,128)(2,1)S(1)} all-gather(bf16[128,512]{1,0:T(8,128)(2,1)S(1)} %shard_map.68), channel_id=2, replica_groups=mesh['runs'=2,'sec'=8,'env'=2] {'env'}, dimensions={0}, use_global_device_ids=true | all-gather | bytes 393216 | tf_op jit(solution)/shard_map/all_gather | solution.py:375
  3.8 0.0 copy-done
  3.8 0.0 copy-done.1
  3.8 0.0 copy-done.2
  3.8 0.0 copy-done.3
  3.8 1.5 %shard_map.69 = (bf16[4,2,32,512]{3,2,1,0:T(8,128)(2,1)S(1)}, bf16[128,512]{1,0:T(8,128)(2,1)S(1)}, bf16[2,128,512]{2,1,0:T(8,128)(2,1)S(1)}) custom-call(s32[8]{0:T(128)S(1)} %copy-done.3, s32[8]{0:T(128)S(1)} %copy-done.2, bf16[2,128,512]{2,1,0:T(8,128)(2,1)S(1)} %bitcast.8, bf16[3,128,128]{2,1,0:T(8,128)(2,1)S(1)} %copy-done.1, ...), custom_call_target="tpu_custom_call" | custom-call | flops 452984832 | bytes 262144 | tf_op jit(solution)/shard_map/pallas_call | solution.py:377
  5.3 15.2 %all_to_all.20.table.old = bf16[4,2,32,512]{3,2,1,0:T(8,128)(2,1)S(1)} all-to-all(bf16[4,2,32,512]{3,2,1,0:T(8,128)(2,1)S(1)} %get-tuple-element.16), channel_id=1, replica_groups={{0,4,8,12},{2,6,10,14},{1,5,9,13},{3,7,11,15},{16,20,24,28},{18,22,26,3..., dimensions={0} | all-to-all | bytes 524288 | tf_op jit(solution)/shard_map/all_to_all | solution.py:346
  20.6 0.7 %shard_map.70 = (bf16[4,32,512]{2,1,0:T(8,128)(2,1)S(1)}, bf16[4,32,512]{2,1,0:T(8,128)(2,1)S(1)}) custom-call(s32[8]{0:T(128)S(1)} %copy-done.2, bf16[4,2,32,512]{3,2,1,0:T(8,128)(2,1)S(1)} %all_to_all.20.table.old), custom_call_target="tpu_custom_call" | custom-call | bytes 262144 | tf_op jit(solution)/shard_map/pallas_call | solution.py:381
  21.3 1.6 %collective-permute-start = (bf16[4,32,512]{2,1,0:T(8,128)(2,1)S(1)}, bf16[4,32,512]{2,1,0:T(8,128)(2,1)S(1)}, u32[]{:S(2)}, u32[]{:S(2)}) collective-permute-start(bf16[4,32,512]{2,1,0:T(8,128)(2,1)S(1)} %get-tuple-element.20), channel_id=1, source_target_pairs={{0,2},{2,0},{4,6},{6,4},{8,10},{10,8},{12,14},{14,12},{1,3},{3,1},... | collective-permute-start | bytes 393224 | tf_op jit(solution)/shard_map/ppermute | solution.py:350
  22.8 3.5 %collective-permute-done.arrived.old_arrived = bf16[4,32,512]{2,1,0:T(8,128)(2,1)S(1)} collective-permute-done((bf16[4,32,512]{2,1,0:T(8,128)(2,1)S(1)}, bf16[4,32,512]{2,1,0:T(8,128)(2,1)S(1)}, u32[]{:S(2)}, u32[]{:S(2)}) %collective-permute-start) | collective-permute-done | bytes 131104 | tf_op jit(solution)/shard_map/ppermute | solution.py:350
  26.4 8.5 %all_to_all.21 = bf16[4,32,512]{2,1,0:T(8,128)(2,1)S(1)} all-to-all(bf16[4,32,512]{2,1,0:T(8,128)(2,1)S(1)} %shard_map.71), channel_id=1, replica_groups={{0,4,8,12},{2,6,10,14},{1,5,9,13},{3,7,11,15},{16,20,24,28},{18,22,26,3..., dimensions={0} | all-to-all | bytes 262144 | tf_op jit(solution)/shard_map/all_to_all | solution.py:346
  34.8 0.6 shard_map.72.first
  35.4 2.0 %all-gather.1 = bf16[256,512]{1,0:T(8,128)(2,1)S(1)} all-gather(bf16[128,512]{1,0:T(8,128)(2,1)S(1)} %shard_map.72.first), channel_id=3, replica_groups=mesh['runs'=2,'sec'=8,'env'=2] {'env'}, dimensions={0}, use_global_device_ids=true | all-gather | bytes 393216 | tf_op jit(solution)/shard_map/all_gather | solution.py:387
  37.4 1.2 %shard_map.73 = (bf16[4,272,128]{2,1,0:T(8,128)(2,1)S(1)}, f32[128,512]{1,0:T(8,128)S(1)}) custom-call(bf16[2,128,512]{2,1,0:T(8,128)(2,1)S(1)} %get-tuple-element.17.start, bf16[2,128,512]{2,1,0:T(8,128)(2,1)S(1)} %bitcast.7, bf16[3,128,128]{2,1,0:T(8,128)(2,1)S(1)} %copy-done.1, bf16[1,3,1024,512]{3,2,1,0:T(8,128)(2,1)S(1)} %copy-done), custom_call_target="tpu_custom_call" | custom-call | flops 452984832 | bytes 262144 | tf_op jit(solution)/shard_map/pallas_call | solution.py:388
  38.6 12.2 %all_to_all.22.new = bf16[4,272,128]{2,1,0:T(8,128)(2,1)S(1)} all-to-all(bf16[4,272,128]{2,1,0:T(8,128)(2,1)S(1)} %get-tuple-element.21), channel_id=1, replica_groups={{0,4,8,12},{2,6,10,14},{1,5,9,13},{3,7,11,15},{16,20,24,28},{18,22,26,3..., dimensions={0} | all-to-all | bytes 557056 | tf_op jit(solution)/shard_map/all_to_all | solution.py:346
  50.8 1.0 %shard_map.74 = (f32[4,32,512]{2,1,0:T(8,128)S(1)}, bf16[528,128]{1,0:T(8,128)(2,1)S(1)}, bf16[16,128]{1,0:T(8,128)(2,1)S(1)}) custom-call(s32[8]{0:T(128)S(1)} %copy-done.2, bf16[4,2,32,512]{3,2,1,0:T(8,128)(2,1)S(1)} %all_to_all.20.table.old, bf16[4,272,128]{2,1,0:T(8,128)(2,1)S(1)} %all_to_all.22.new), custom_call_target="tpu_custom_call" | custom-call | bytes 262144 | tf_op jit(solution)/shard_map/pallas_call | solution.py:392
  51.8 1.6 %collective-permute-start.1 = (bf16[528,128]{1,0:T(8,128)(2,1)S(1)}, bf16[528,128]{1,0:T(8,128)(2,1)S(1)}, u32[]{:S(2)}, u32[]{:S(2)}) collective-permute-start(bf16[528,128]{1,0:T(8,128)(2,1)S(1)} %get-tuple-element.24), channel_id=1, source_target_pairs={{0,2},{2,0},{4,6},{6,4},{8,10},{10,8},{12,14},{14,12},{1,3},{3,1},... | collective-permute-start | bytes 405512 | tf_op jit(solution)/shard_map/ppermute | solution.py:350
  53.3 3.5 %collective-permute-done.1.arrived = bf16[528,128]{1,0:T(8,128)(2,1)S(1)} collective-permute-done((bf16[528,128]{1,0:T(8,128)(2,1)S(1)}, bf16[528,128]{1,0:T(8,128)(2,1)S(1)}, u32[]{:S(2)}, u32[]{:S(2)}) %collective-permute-start.1) | collective-permute-done | bytes 135200 | tf_op jit(solution)/shard_map/ppermute | solution.py:350
  56.9 0.9 %shard_map.75 = (bf16[4,32,512]{2,1,0:T(8,128)(2,1)S(1)}, f32[8,128]{1,0:T(8,128)S(1)}) custom-call(s32[8]{0:T(128)S(1)} %copy-done.3, bf16[16,128]{1,0:T(8,128)(2,1)S(1)} %get-tuple-element.22.tag_line, f32[4,32,512]{2,1,0:T(8,128)S(1)} %get-tuple-element.23.keep, bf16[528,128]{1,0:T(8,128)(2,1)S(1)} %collective-permute-done.1.arrived, ...), custom_call_target="tpu_custom_call" | custom-call | bytes 262144 | tf_op jit(solution)/shard_map/pallas_call | solution.py:395
  57.8 8.7 %all_to_all.23 = bf16[4,32,512]{2,1,0:T(8,128)(2,1)S(1)} all-to-all(bf16[4,32,512]{2,1,0:T(8,128)(2,1)S(1)} %get-tuple-element.27), channel_id=1, replica_groups={{0,4,8,12},{2,6,10,14},{1,5,9,13},{3,7,11,15},{16,20,24,28},{18,22,26,3..., dimensions={0} | all-to-all | bytes 262144 | tf_op jit(solution)/shard_map/all_to_all | solution.py:346
  66.4 1.3 %shard_map.76 = (bf16[128,512]{1,0:T(8,128)(2,1)}, bf16[128,512]{1,0:T(8,128)(2,1)}) custom-call(s32[8]{0:T(128)S(1)} %copy-done.3, s32[8]{0:T(128)S(1)} %copy-done.2, f32[8,128]{1,0:T(8,128)S(1)} %get-tuple-element.25.factors, bf16[128,512]{1,0:T(8,128)(2,1)S(1)} %get-tuple-element.18.stay, f32[128,512]{1,0:T(8,128)S(1)} %get-tuple-element.26.stay_2, ...), custom_call_target="tpu_custom_call" | custom-call | bytes 262144 | tf_op jit(solution)/shard_map/pallas_call | solution.py:399
  (2 shorter events, 0.0 us)
Async XLA Ops:
  0.6 0.9 %copy-start.4 = (bf16[1,128,512]{2,1,0:T(8,128)(2,1)S(1)}, bf16[1,128,512]{2,1,0:T(8,128)(2,1)}, u32[]{:S(2)}) copy-start(bf16[1,128,512]{2,1,0:T(8,128)(2,1)} %param.5) | copy-start | bytes 393220
  1.5 2.2 %copy-start = (bf16[1,3,1024,512]{3,2,1,0:T(8,128)(2,1)S(1)}, bf16[1,3,1024,512]{3,2,1,0:T(8,128)(2,1)}, u32[]{:S(2)}) copy-start(bf16[1,3,1024,512]{3,2,1,0:T(8,128)(2,1)} %left.3) | copy-start | bytes 9437188
  1.5 2.2 %copy-start.1 = (bf16[3,128,128]{2,1,0:T(8,128)(2,1)S(1)}, bf16[3,128,128]{2,1,0:T(8,128)(2,1)}, u32[]{:S(2)}) copy-start(bf16[3,128,128]{2,1,0:T(8,128)(2,1)} %right.3) | copy-start | bytes 294916
  1.5 2.2 %copy-start.2 = (s32[8]{0:T(128)S(1)}, s32[8]{0:T(128)}, u32[]{:S(2)}) copy-start(s32[8]{0:T(128)} %holders.9) | copy-start | bytes 100
  1.5 2.3 %copy-start.3 = (s32[8]{0:T(128)S(1)}, s32[8]{0:T(128)}, u32[]{:S(2)}) copy-start(s32[8]{0:T(128)} %widths.7) | copy-start | bytes 100
  21.3 5.0 %collective-permute-start = (bf16[4,32,512]{2,1,0:T(8,128)(2,1)S(1)}, bf16[4,32,512]{2,1,0:T(8,128)(2,1)S(1)}, u32[]{:S(2)}, u32[]{:S(2)}) collective-permute-start(bf16[4,32,512]{2,1,0:T(8,128)(2,1)S(1)} %get-tuple-element.20), channel_id=1, source_target_pairs={{0,2},{2,0},{4,6},{6,4},{8,10},{10,8},{12,14},{14,12},{1,3},{3,1},... | collective-permute-start | bytes 393224 | tf_op jit(solution)/shard_map/ppermute | solution.py:350
  51.8 5.1 %collective-permute-start.1 = (bf16[528,128]{1,0:T(8,128)(2,1)S(1)}, bf16[528,128]{1,0:T(8,128)(2,1)S(1)}, u32[]{:S(2)}, u32[]{:S(2)}) collective-permute-start(bf16[528,128]{1,0:T(8,128)(2,1)S(1)} %get-tuple-element.24), channel_id=1, source_target_pairs={{0,2},{2,0},{4,6},{6,4},{8,10},{10,8},{12,14},{14,12},{1,3},{3,1},... | collective-permute-start | bytes 405512 | tf_op jit(solution)/shard_map/ppermute | solution.py:350

commit v10 on v6

--- a/solution.py
+++ b/solution.py
@@ -124,14 +124,22 @@
     return jnp.dot(products.astype(jnp.bfloat16), left, preferred_element_type=jnp.float32)
 
 
-def mask_kernel(widths, holders, amps, start):
-    live = live_columns(widths, holders, amps.shape[1])
-    start[...] = jnp.where(live, amps[...], jnp.zeros_like(amps[...]))
-
-
-def first_kernel(start, right, left, message, stay):
-    slots, _, rows, _ = message.shape
-    vector = jnp.concatenate([start[0], start[1]], axis=1)
+def columns_kernel(columns):
+    columns[...] = lax.broadcasted_iota(jnp.int32, columns.shape, 1)
+
+
+def masked(widths, holders, columns, amps):
+    half = amps.shape[2]
+    width = widths[holders[lax.axis_index("sec")]]
+    return [
+        jnp.where(columns[0:1, :] < width - h * half, amps[h], jnp.zeros_like(amps[h]))
+        for h in range(2)
+    ]
+
+
+def first_kernel(widths, holders, columns, amps, right, left, message, stay):
+    slots, _, rows, half = message.shape
+    vector = jnp.concatenate(masked(widths, holders, columns, amps), axis=1)
     for term in (1, 2, 0):
         block = apply_term(right, left[0, term], vector, term).astype(jnp.bfloat16)
         if term == 0:
@@ -187,12 +195,12 @@
     return jnp.where((lane == me) & (row < 3 * len(values)), parts, 0.0).astype(jnp.bfloat16)
 
 
-def second_kernel(start, first, right, left, message, stay):
+def second_kernel(widths, holders, columns, amps, first, right, left, message, stay):
     slots = message.shape[0]
     half = stay.shape[1]
     rows = stay.shape[0] // slots
     chunks = half // LANES
-    basis = [start[h].astype(jnp.float32) for h in range(2)]
+    basis = [part.astype(jnp.float32) for part in masked(widths, holders, columns, amps)]
     firsts = [first[h].astype(jnp.float32) for h in range(2)]
     overlap = total_of(basis[0] * firsts[0]) + total_of(basis[1] * firsts[1])
     norm = total_of(basis[0] * basis[0]) + total_of(basis[1] * basis[1])
@@ -243,7 +251,11 @@
         return total_of(jnp.where(lane == slot, shifts, 0.0))
 
     row = lax.broadcasted_iota(jnp.int32, factors.shape, 0)
-    factors[...] = jnp.where(row == 0, scale, scale * shift_of(lax.axis_index("sec")))
+    me = lax.axis_index("sec")
+    bound = widths[holders[me]] - lax.axis_index("env") * half
+    factors[...] = jnp.where(
+        row == 0, scale, jnp.where(row == 1, scale * shift_of(me), bound.astype(jnp.float32))
+    )
     for slot in range(slots):
         has, source = sources_of(holders, slot_of, slot)
         total = 0.0
@@ -258,14 +270,6 @@
             block = block + shift_of(source[i]) * old[source[i], i].astype(jnp.float32)
             total = total + jnp.where(has[i], block, 0.0)
         out[slot] = (scale * total).astype(jnp.bfloat16)
-
-
-def final_kernel(widths, holders, factors, stay, stay_2, arrived, second):
-    live = live_columns(widths, holders, stay.shape[1])
-    scale, shift = factors[0:1, 0:1], factors[1:2, 0:1]
-    total = scale * stay_2[...] + shift * stay[...].astype(jnp.float32)
-    total = total + arrived[...].astype(jnp.float32)
-    second[...] = jnp.where(live, total, 0.0).astype(jnp.bfloat16)
 
 
 SMEM = pl.BlockSpec(memory_space=pltpu.SMEM)
@@ -304,12 +308,12 @@
     factor_shape = jax.ShapeDtypeStruct((8, LANES), jnp.float32)
     slot_table = [pltpu.SMEM((slots,), jnp.int32)]
 
-    start = call(mask_kernel, [SMEM, SMEM, VMEM], block, flops=dots)(
-        widths, holders, amplitudes[0]
-    )
-    start_full = lax.all_gather(start, "env")
-    message, stay = call(first_kernel, [VMEM] * 3, (pairs, block), flops=dots)(
-        start_full, right_env, left_env
+    number = jax.ShapeDtypeStruct((8, half), jnp.int32)
+    columns = call(columns_kernel, [], number, flops=4 << 30)()
+    columns, amps = lax.optimization_barrier((columns, amplitudes[0]))
+    amps_full = lax.all_gather(amps, "env")
+    message, stay = call(first_kernel, [SMEM, SMEM] + [VMEM] * 4, (pairs, block), flops=dots)(
+        widths, holders, columns, amps_full, right_env, left_env
     )
     old = swap(message)
     merged = call(merge_kernel, [SMEM, VMEM], singles, slot_table)(holders, old)
@@ -317,17 +321,19 @@
     first = call(sum_kernel, [SMEM, SMEM, VMEM, VMEM], block)(widths, holders, stay, arrived)
 
     first_full = lax.all_gather(first, "env")
-    message, stay_2 = call(second_kernel, [VMEM] * 4, (tagged, wide), flops=dots)(
-        start_full, first_full, right_env, left_env
-    )
+    message, stay_2 = call(
+        second_kernel, [SMEM, SMEM] + [VMEM] * 5, (tagged, wide), flops=dots
+    )(widths, holders, columns, amps_full, first_full, right_env, left_env)
     new = swap(message)
     mixed, factors = call(
         mix_kernel, [SMEM, SMEM, VMEM, VMEM], (singles, factor_shape), slot_table
     )(widths, holders, old, new)
     arrived = swap(mixed).reshape(right_dim, half)
-    second = call(final_kernel, [SMEM, SMEM] + [VMEM] * 4, block)(
-        widths, holders, factors, stay, stay_2, arrived
-    )
+    total = factors[0:1, 0:1] * stay_2 + factors[1:2, 0:1] * stay.astype(jnp.float32)
+    total = total + arrived.astype(jnp.float32)
+    live = lax.broadcasted_iota(jnp.int32, (right_dim, half), 1).astype(jnp.float32) < factors[2:3, 0:1]
+    second = jnp.where(live, total, 0.0).astype(jnp.bfloat16)
+    first = jnp.where(live, first, jnp.zeros_like(first))
     return first[None], second[None]
 
 

time: 67.6 us -> 66.3 us (0.981)
  blocking collectives: 54.6 us -> 44.4 us
  waiting for transfers between devices: 0 us -> 6.61 us
  local copies, waits for them, and re-layouts: 5.07 us -> 1.44 us
  starting transfers between devices: 0 us -> 3.38 us
  other arithmetic: 0 us -> 3.3 us
  Pallas kernels: 6.82 us -> 6.06 us
    all_to_all x4 -> x3, blocking collectives: 50.2 us -> 40.2 us  [swap(): return lax.all_to_all(pieces, 'sec', split_axis=0, concat_axis=0)]
    all_to_all x0 -> x1, waiting for transfers between devices: none -> 6.61 us  [swap(): return lax.all_to_all(pieces, 'sec', split_axis=0, concat_axis=0)]
    unnamed x18 -> x10, local copies, waits for them, and re-layouts: 5.07 us -> 0.86 us
    all_to_all x0 -> x1, starting transfers between devices: none -> 3.38 us  [swap(): return lax.all_to_all(pieces, 'sec', split_axis=0, concat_axis=0)]
    broadcast_in_dim x0 -> x2, other arithmetic: none -> 2.65 us  [on_device(): return (first[None], second[None])]
    pallas_call x4 -> x3, Pallas kernels: 4.06 us -> 3.29 us  [the longest x1 1.74 us: on_device(): call(second_kernel, [SMEM, SMEM] + [VMEM] * 5, (tagged, wide), flops=dots)]
  transfers between devices with their start and end apart: 0 -> 1, of which waited for: 0 -> 1; matrix products, arithmetic and copies ran while one was open for 0% -> 1% of each run, Pallas kernels for 0% -> 0%
where the time goes in v10:
time: 66.3 us; the launch traced here: 66 us
  blocking collectives  44.4 us (67%)
  waiting for transfers between devices  6.61 us (10%)
  Pallas kernels  6.06 us (9%)
  starting transfers between devices  3.38 us (5%)
  other arithmetic  3.3 us (5%)
  local copies, waits for them, and re-layouts  1.44 us (2%)
  between operations  0.73 us (1%)
    all_to_all x3, blocking collectives, swap(): return lax.all_to_all(pieces, 'sec', split_axis=0, concat_axis=0)  40.2 us
    all_to_all x1, waiting for transfers between devices, swap(): return lax.all_to_all(pieces, 'sec', split_axis=0, concat_axis=0)  6.61 us
    all_to_all x1, starting transfers between devices, swap(): return lax.all_to_all(pieces, 'sec', split_axis=0, concat_axis=0)  3.38 us
    broadcast_in_dim x2, other arithmetic, on_device(): return (first[None], second[None])  2.65 us
    all_gather x1, blocking collectives, on_device(): amps_full = lax.all_gather(amps, 'env')  2.2 us
    all_gather x1, blocking collectives, on_device(): first_full = lax.all_gather(first, 'env')  1.99 us
    pallas_call x1, Pallas kernels, on_device(): call(second_kernel, [SMEM, SMEM] + [VMEM] * 5, (tagged, wide), flops=dots)  1.74 us
    pallas_call x1, Pallas kernels, on_device(): call(mix_kernel, [SMEM, SMEM, VMEM, VMEM], (singles, factor_shape), slot_...  1.57 us
  transfers between devices with their start and end apart: 1, of which 1 were waited for; matrix products, arithmetic and copies ran while one was open for 1% of the time, Pallas kernels for 0%

profile of v10, /device:TPU:0, one launch (start us, length us, event | category | flops | bytes accessed | tf_op | source)
XLA Modules:
  0.0 66.0 jit_solution(14244204936677557869)
XLA Ops:
  0.6 0.0 copy-start.4
  0.6 0.0 copy-start.2
  0.7 0.0 copy-start.3
  0.7 0.0 copy-start.1
  0.7 0.0 copy-start
  0.7 0.8 %copy-done.4 = bf16[1,128,512]{2,1,0:T(8,128)(2,1)S(1)} copy-done((bf16[1,128,512]{2,1,0:T(8,128)(2,1)S(1)}, bf16[1,128,512]{2,1,0:T(8,128)(2,1)}, u32[]{:S(2)}) %copy-start.4) | copy-done | bytes 131096
  1.5 2.2 %all-gather = bf16[256,512]{1,0:T(8,128)(2,1)S(1)} all-gather(bf16[128,512]{1,0:T(8,128)(2,1)S(1)} %bitcast.18), channel_id=2, replica_groups=mesh['runs'=2,'sec'=8,'env'=2] {'env'}, dimensions={0}, use_global_device_ids=true | all-gather | bytes 393216 | tf_op jit(solution)/shard_map/all_gather | solution.py:314
  3.7 0.0 copy-done.2
  3.7 0.0 copy-done.3
  3.7 0.0 copy-done.1
  3.7 0.0 copy-done
  3.8 1.5 %shard_map.69 = (bf16[8,2,16,512]{3,2,1,0:T(8,128)(2,1)S(1)}, bf16[128,512]{1,0:T(8,128)(2,1)S(1)}) custom-call(s32[8]{0:T(128)S(1)} %copy-done.3, s32[8]{0:T(128)S(1)} %copy-done.2, s32[8,512]{1,0:T(8,128)S(1)} %shard_map.68.columns, bf16[2,128,512]{2,1,0:T(8,128)(2,1)S(1)} %bitcast.14, bf16[3,128,128]{2,1,0:T(8,128)(2,1)S(1)} %copy-done.1, ...), custom_call_target="tpu_custom_call" | custom-call | flops 452984832 | bytes 262144 | tf_op jit(solution)/shard_map/pallas_call | solution.py:315
  5.3 16.2 %all_to_all.20.table.old = bf16[8,2,16,512]{3,2,1,0:T(8,128)(2,1)S(1)} all-to-all(bf16[8,2,16,512]{3,2,1,0:T(8,128)(2,1)S(1)} %get-tuple-element.12), channel_id=1, replica_groups=mesh['runs'=2,'sec'=8,'env'=2] {'sec'}, dimensions={0} | all-to-all | bytes 524288 | tf_op jit(solution)/shard_map/all_to_all | solution.py:292
  21.5 0.6 shard_map.70
  22.1 10.7 %all_to_all.21 = bf16[8,16,512]{2,1,0:T(8,128)(2,1)S(1)} all-to-all(bf16[8,16,512]{2,1,0:T(8,128)(2,1)S(1)} %shard_map.70), channel_id=1, replica_groups=mesh['runs'=2,'sec'=8,'env'=2] {'sec'}, dimensions={0} | all-to-all | bytes 262144 | tf_op jit(solution)/shard_map/all_to_all | solution.py:292
  32.8 0.6 shard_map.71
  33.4 2.0 %all-gather.1 = bf16[256,512]{1,0:T(8,128)(2,1)S(1)} all-gather(bf16[128,512]{1,0:T(8,128)(2,1)S(1)} %shard_map.71), channel_id=3, replica_groups=mesh['runs'=2,'sec'=8,'env'=2] {'env'}, dimensions={0}, use_global_device_ids=true | all-gather | bytes 393216 | tf_op jit(solution)/shard_map/all_gather | solution.py:323
  35.4 1.7 %shard_map.72 = (bf16[8,144,128]{2,1,0:T(8,128)(2,1)S(1)}, f32[128,512]{1,0:T(8,128)S(1)}) custom-call(s32[8]{0:T(128)S(1)} %copy-done.3, s32[8]{0:T(128)S(1)} %copy-done.2, s32[8,512]{1,0:T(8,128)S(1)} %shard_map.68.columns, bf16[2,128,512]{2,1,0:T(8,128)(2,1)S(1)} %bitcast.15, bf16[2,128,512]{2,1,0:T(8,128)(2,1)S(1)} %bitcast.16, ...), custom_call_target="tpu_custom_call" | custom-call | flops 452984832 | bytes 262144 | tf_op jit(solution)/shard_map/pallas_call | solution.py:324
  37.2 13.3 %all_to_all.22.new = bf16[8,144,128]{2,1,0:T(8,128)(2,1)S(1)} all-to-all(bf16[8,144,128]{2,1,0:T(8,128)(2,1)S(1)} %get-tuple-element.14), channel_id=1, replica_groups=mesh['runs'=2,'sec'=8,'env'=2] {'sec'}, dimensions={0} | all-to-all | bytes 589824 | tf_op jit(solution)/shard_map/all_to_all | solution.py:292
  50.5 1.6 %shard_map.73 = (bf16[8,16,512]{2,1,0:T(8,128)(2,1)}, f32[8,128]{1,0:T(8,128)S(1)}) custom-call(s32[8]{0:T(128)S(1)} %copy-done.3, s32[8]{0:T(128)S(1)} %copy-done.2, bf16[8,2,16,512]{3,2,1,0:T(8,128)(2,1)S(1)} %all_to_all.20.table.old, bf16[8,144,128]{2,1,0:T(8,128)(2,1)S(1)} %all_to_all.22.new), custom_call_target="tpu_custom_call" | custom-call | bytes 262144 | tf_op jit(solution)/shard_map/pallas_call | solution.py:328
  52.1 0.6 fusion.3
  52.6 0.7 convert_compare_fusion
  53.3 3.4 %all-to-all-start.3 = ((bf16[8,16,512]{2,1,0:T(8,128)(2,1)}), bf16[8,16,512]{2,1,0:T(8,128)(2,1)S(1)}, u32[]{:S(2)}, u32[]{:S(2)}) async-start(bf16[8,16,512]{2,1,0:T(8,128)(2,1)} %get-tuple-element.17), calls=%async_computation.3 | async-start | bytes 262144 | tf_op jit(solution)/shard_map/all_to_all | solution.py:292
  56.7 0.7 %select_bitcast_fusion = bf16[1,128,512]{2,1,0:T(8,128)(2,1)} fusion(bf16[128,512]{1,0:T(8,128)(2,1)S(1)} %shard_map.71, pred[512]{0:T(512)(128)(4,1)S(1)} %convert_compare_fusion), kind=kLoop, calls=%fused_computation.4 | loop fusion | flops 65536 | bytes 262656 | tf_op jit(solution)/shard_map/broadcast_in_dim | solution.py:337
  57.4 6.6 %all-to-all-done.3 = bf16[8,16,512]{2,1,0:T(8,128)(2,1)S(1)} async-done(((bf16[8,16,512]{2,1,0:T(8,128)(2,1)}), bf16[8,16,512]{2,1,0:T(8,128)(2,1)S(1)}, u32[]{:S(2)}, u32[]{:S(2)}) %all-to-all-start.3) | async-done | bytes 131104 | tf_op jit(solution)/shard_map/all_to_all | solution.py:292
  64.0 2.0 %fusion.2 = bf16[1,128,512]{2,1,0:T(8,128)(2,1)} fusion(bf16[128,512]{1,0:T(8,128)(2,1)S(1)} %get-tuple-element.13.stay, f32[128,512]{1,0:T(8,128)S(1)} %get-tuple-element.16, bf16[8,16,512]{2,1,0:T(8,128)(2,1)S(1)} %all-to-all-done.3, f32[]{:T(128)} %bitcast.7, f32[]{:T(128)} %bitcast.6, pred[512]{0:T(512)(128)(4,1)S(1)} %convert_compare_fusion), kind=kLoop, calls=%fused_computation.3 | loop fusion | flops 524288 | bytes 655880 | tf_op jit(solution)/shard_map/broadcast_in_dim | solution.py:337
  (1 shorter events, 0.0 us)
Async XLA Ops:
  0.6 0.9 %copy-start.4 = (bf16[1,128,512]{2,1,0:T(8,128)(2,1)S(1)}, bf16[1,128,512]{2,1,0:T(8,128)(2,1)}, u32[]{:S(2)}) copy-start(bf16[1,128,512]{2,1,0:T(8,128)(2,1)} %param.5) | copy-start | bytes 393220
  0.6 3.1 %copy-start.2 = (s32[8]{0:T(128)S(1)}, s32[8]{0:T(128)}, u32[]{:S(2)}) copy-start(s32[8]{0:T(128)} %holders.9) | copy-start | bytes 100
  0.7 3.1 %copy-start.3 = (s32[8]{0:T(128)S(1)}, s32[8]{0:T(128)}, u32[]{:S(2)}) copy-start(s32[8]{0:T(128)} %widths.7) | copy-start | bytes 100
  0.7 3.1 %copy-start.1 = (bf16[3,128,128]{2,1,0:T(8,128)(2,1)S(1)}, bf16[3,128,128]{2,1,0:T(8,128)(2,1)}, u32[]{:S(2)}) copy-start(bf16[3,128,128]{2,1,0:T(8,128)(2,1)} %right.3) | copy-start | bytes 294916
  0.7 3.1 %copy-start = (bf16[1,3,1024,512]{3,2,1,0:T(8,128)(2,1)S(1)}, bf16[1,3,1024,512]{3,2,1,0:T(8,128)(2,1)}, u32[]{:S(2)}) copy-start(bf16[1,3,1024,512]{3,2,1,0:T(8,128)(2,1)} %left.3) | copy-start | bytes 9437188
  53.3 10.7 %all-to-all-start.3 = ((bf16[8,16,512]{2,1,0:T(8,128)(2,1)}), bf16[8,16,512]{2,1,0:T(8,128)(2,1)S(1)}, u32[]{:S(2)}, u32[]{:S(2)}) async-start(bf16[8,16,512]{2,1,0:T(8,128)(2,1)} %get-tuple-element.17), calls=%async_computation.3 | async-start | bytes 262144 | tf_op jit(solution)/shard_map/all_to_all | solution.py:292

commit v11 on v9

--- a/solution.py
+++ b/solution.py
@@ -129,8 +129,13 @@
     staged[...] = amps[...]
 
 
-def first_kernel(widths, holders, amps, right, left, message, stay, start):
-    slots, _, rows, half = message.shape
+def own_place():
+    return lax.axis_index("sec") // LINES
+
+
+def first_kernel(widths, holders, amps, right, left, *rest):
+    *pieces, stay, start, block_vmem = rest
+    half = stay.shape[1]
     width = widths[holders[lax.axis_index("sec")]]
     columns = lax.broadcasted_iota(jnp.int32, (1, half), 1)
     for h in range(2):
@@ -142,8 +147,9 @@
         if term == 0:
             stay[...] = block
         else:
-            for slot in range(slots):
-                message[slot, term - 1] = block[slot * rows : (slot + 1) * rows, :]
+            block_vmem[...] = block.reshape(block_vmem.shape)
+            for step, piece in enumerate(pieces):
+                piece[term - 1] = block_vmem[own_place() ^ step]
 
 
 def fill_slots(holders, slot_of):
@@ -167,8 +173,11 @@
             yield place, crossing, here, source
 
 
-def merge_kernel(holders, table, keep, cross, slot_of):
+def merge_kernel(holders, *rest):
+    *pieces, keep, cross, table, slot_of = rest
     fill_slots(holders, slot_of)
+    for step, piece in enumerate(pieces):
+        table[own_place() ^ step] = piece[...]
     for place, crossing, here, source in line_targets(holders, slot_of):
         total = 0.0
         for i in range(2):
@@ -177,15 +186,24 @@
         (keep, cross)[crossing][place] = total.astype(jnp.bfloat16)
 
 
-def join_kernel(keep, arrived, out):
-    total = keep[...].astype(jnp.float32) + arrived[...].astype(jnp.float32)
-    out[...] = total.astype(jnp.bfloat16)
-
-
-def sum_kernel(widths, holders, stay, arrived, first):
+def join_kernel(keep, arrived, *outs):
+    for step, out in enumerate(outs):
+        place = own_place() ^ step
+        total = keep[place].astype(jnp.float32) + arrived[place].astype(jnp.float32)
+        out[...] = total.astype(jnp.bfloat16)
+
+
+def piece_rows(step, rows):
+    return pl.ds(pl.multiple_of((own_place() ^ step) * rows, rows), rows)
+
+
+def sum_kernel(widths, holders, stay, *rest):
+    *pieces, first = rest
     live = live_columns(widths, holders, stay.shape[1])
-    total = stay[...].astype(jnp.float32) + arrived[...].astype(jnp.float32)
-    first[...] = jnp.where(live, total, 0.0).astype(jnp.bfloat16)
+    for step, piece in enumerate(pieces):
+        place = piece_rows(step, piece.shape[0])
+        total = stay[place, :].astype(jnp.float32) + piece[...].astype(jnp.float32)
+        first[place, :] = jnp.where(live, total, 0.0).astype(jnp.bfloat16)
 
 
 def total_of(array):
@@ -205,10 +223,10 @@
     return jnp.where((lane == me) & (row < 3 * len(values)), parts, 0.0).astype(jnp.bfloat16)
 
 
-def second_kernel(start, first, right, left, message, stay):
-    slots = message.shape[0]
+def second_kernel(start, first, right, left, *rest):
+    *pieces, stay, block_vmem = rest
     half = stay.shape[1]
-    rows = stay.shape[0] // slots
+    rows = block_vmem.shape[1]
     chunks = half // LANES
     basis = [start[h].astype(jnp.float32) for h in range(2)]
     firsts = [first[h].astype(jnp.float32) for h in range(2)]
@@ -219,20 +237,19 @@
     rest_norm = total_of(deflated[0] * deflated[0]) + total_of(deflated[1] * deflated[1])
     vector = jnp.concatenate(deflated, axis=1).astype(jnp.bfloat16)
     tag = make_tag((overlap, norm, quotient, rest_norm), lax.axis_index("sec"))
-    for slot in range(slots):
-        message[slot, pl.ds(2 * chunks * rows, TAG), :] = tag
+    for piece in pieces:
+        piece[pl.ds(2 * chunks * rows, TAG), :] = tag
     for term in (1, 2, 0):
         block = apply_term(right, left[0, term], vector, term)
         if term == 0:
             stay[...] = block
         else:
-            block = block.astype(jnp.bfloat16)
-            for slot in range(slots):
+            block_vmem[...] = block.astype(jnp.bfloat16).reshape(block_vmem.shape)
+            for step, piece in enumerate(pieces):
+                part = block_vmem[own_place() ^ step]
                 for c in range(chunks):
                     place = pl.ds(((term - 1) * chunks + c) * rows, rows)
-                    message[slot, place, :] = block[
-                        slot * rows : (slot + 1) * rows, c * LANES : (c + 1) * LANES
-                    ]
+                    piece[place, :] = part[:, c * LANES : (c + 1) * LANES]
 
 
 def read_tag(tag):
@@ -250,13 +267,17 @@
     return jnp.where(norm > 0, overlap / jnp.where(norm > 0, norm, 1.0), 0.0)
 
 
-def mix_kernel(holders, old, new, keep, cross, tag_out, slot_of):
+def mix_kernel(holders, *rest):
+    keep, cross, tag_out, old, new, slot_of = rest[-6:]
     places, rows, half = keep.shape
     chunks = half // LANES
     fill_slots(holders, slot_of)
     tag = jnp.zeros((TAG, LANES), jnp.float32)
-    for place in range(places):
-        tag = tag + new[place, pl.ds(2 * chunks * rows, TAG), :].astype(jnp.float32)
+    for step in range(places):
+        old[own_place() ^ step] = rest[step][...]
+        new[own_place() ^ step] = rest[places + step][...]
+        label = rest[places + step][pl.ds(2 * chunks * rows, TAG), :]
+        tag = tag + label.astype(jnp.float32)
     tag_out[...] = tag.astype(jnp.bfloat16)
     cross[pl.ds(places * chunks * rows, TAG), :] = tag.astype(jnp.bfloat16)
     overlaps, norms, quotients, _ = read_tag(tag)
@@ -282,7 +303,8 @@
             keep[place] = total
 
 
-def join_mixed_kernel(widths, tag_line, keep, arrived, old_keep, old_arrived, out, factors):
+def join_mixed_kernel(widths, tag_line, keep, arrived, old_keep, old_arrived, *rest):
+    *outs, factors = rest
     places, rows, half = keep.shape
     chunks = half // LANES
     slots = widths.shape[0]
@@ -305,23 +327,27 @@
     line = me % LINES
     shift_here = line_quotient(overlaps, norms, line) - quotient
     shift_there = line_quotient(overlaps, norms, 1 - line) - quotient
-    for place in range(places):
+    for step, out in enumerate(outs):
+        place = own_place() ^ step
+        starts = [pl.multiple_of((place * chunks + c) * rows, rows) for c in range(chunks)]
         block = jnp.concatenate(
-            [arrived[pl.ds((place * chunks + c) * rows, rows), :] for c in range(chunks)],
-            axis=1,
+            [arrived[pl.ds(start, rows), :] for start in starts], axis=1
         ).astype(jnp.float32)
         block = block + shift_there * old_arrived[place].astype(jnp.float32)
         block = block + keep[place] + shift_here * old_keep[place].astype(jnp.float32)
-        out[place] = (scale * block).astype(jnp.bfloat16)
-
-
-def final_kernel(widths, holders, factors, stay, stay_2, arrived, first, second, first_out):
+        out[...] = (scale * block).astype(jnp.bfloat16)
+
+
+def final_kernel(widths, holders, factors, stay, stay_2, first, *rest):
+    *pieces, second, first_out = rest
     first_out[...] = first[...]
     live = live_columns(widths, holders, stay.shape[1])
     scale, shift = factors[0:1, 0:1], factors[1:2, 0:1]
-    total = scale * stay_2[...] + shift * stay[...].astype(jnp.float32)
-    total = total + arrived[...].astype(jnp.float32)
-    second[...] = jnp.where(live, total, 0.0).astype(jnp.bfloat16)
+    for step, piece in enumerate(pieces):
+        place = piece_rows(step, piece.shape[0])
+        total = scale * stay_2[place, :] + shift * stay[place, :].astype(jnp.float32)
+        total = total + piece[...].astype(jnp.float32)
+        second[place, :] = jnp.where(live, total, 0.0).astype(jnp.bfloat16)
 
 
 SMEM = pl.BlockSpec(memory_space=pltpu.SMEM)
@@ -340,10 +366,12 @@
     )
 
 
-def along_line(pieces):
-    places = pieces.shape[0]
-    groups = [[place * LINES + line for place in range(places)] for line in range(LINES)]
-    return lax.all_to_all(pieces, "sec", 0, 0, axis_index_groups=groups)
+def along_line(pieces, slots):
+    sent = [pieces[0]]
+    for step in range(1, len(pieces)):
+        pairs = [(slot, slot ^ (step * LINES)) for slot in range(slots)]
+        sent.append(lax.ppermute(pieces[step], "sec", pairs))
+    return sent
 
 
 def across(piece, slots):
@@ -361,43 +389,51 @@
     dots = 6 * right_dim * half * (right_dim + 2 * half)
     block = jax.ShapeDtypeStruct((right_dim, half), jnp.bfloat16)
     wide = jax.ShapeDtypeStruct((right_dim, half), jnp.float32)
-    pairs = jax.ShapeDtypeStruct((places, 2, rows, half), jnp.bfloat16)
+    pair = jax.ShapeDtypeStruct((2, rows, half), jnp.bfloat16)
+    single = jax.ShapeDtypeStruct((rows, half), jnp.bfloat16)
     singles = jax.ShapeDtypeStruct((places, rows, half), jnp.bfloat16)
     wides = jax.ShapeDtypeStruct((places, rows, half), jnp.float32)
     chunked = rows * half // LANES
-    tagged = jax.ShapeDtypeStruct((places, 2 * chunked + TAG, LANES), jnp.bfloat16)
+    tagged = jax.ShapeDtypeStruct((2 * chunked + TAG, LANES), jnp.bfloat16)
     crossing = jax.ShapeDtypeStruct((places * chunked + TAG, LANES), jnp.bfloat16)
     label = jax.ShapeDtypeStruct((TAG, LANES), jnp.bfloat16)
     factor_shape = jax.ShapeDtypeStruct((8, LANES), jnp.float32)
-    slot_table = [pltpu.SMEM((slots,), jnp.int32)]
+    slot_table = pltpu.SMEM((slots,), jnp.int32)
+    split = [pltpu.VMEM((places, rows, half), jnp.bfloat16)]
+    tables = [pltpu.VMEM((places, *shape.shape), jnp.bfloat16) for shape in (pair, tagged)]
 
     staged = call(stage_kernel, [VMEM], block, flops=4 << 30)(amplitudes[0])
     amps_full = lax.all_gather(staged, "env")
     both = jax.ShapeDtypeStruct(amps_full.shape, jnp.bfloat16)
-    message, stay, start_full = call(
-        first_kernel, [SMEM, SMEM] + [VMEM] * 3, (pairs, block, both), flops=dots
+    *pieces, stay, start_full = call(
+        first_kernel, [SMEM, SMEM] + [VMEM] * 3, (pair,) * places + (block, both), split, dots
     )(widths, holders, amps_full, right_env, left_env)
-    old = along_line(message)
-    old_keep, cross = call(merge_kernel, [SMEM, VMEM], (singles, singles), slot_table)(holders, old)
+    old = along_line(pieces, slots)
+    old_keep, cross = call(
+        merge_kernel, [SMEM] + [VMEM] * places, (singles, singles), [tables[0], slot_table]
+    )(holders, *old)
     old_arrived = across(cross, slots)
-    joined = call(join_kernel, [VMEM, VMEM], singles)(old_keep, old_arrived)
-    arrived = along_line(joined).reshape(right_dim, half)
-    first = call(sum_kernel, [SMEM, SMEM, VMEM, VMEM], block)(widths, holders, stay, arrived)
+    joined = call(join_kernel, [VMEM, VMEM], (single,) * places)(old_keep, old_arrived)
+    first = call(sum_kernel, [SMEM, SMEM] + [VMEM] * (1 + places), block)(
+        widths, holders, stay, *along_line(joined, slots)
+    )
 
     first_full = lax.all_gather(first, "env")
-    message, stay_2 = call(second_kernel, [VMEM] * 4, (tagged, wide), flops=dots)(
-        start_full, first_full, right_env, left_env
-    )
-    new = along_line(message)
+    *pieces, stay_2 = call(
+        second_kernel, [VMEM] * 4, (tagged,) * places + (wide,), split, dots
+    )(start_full, first_full, right_env, left_env)
+    new = along_line(pieces, slots)
     keep, cross, tag = call(
-        mix_kernel, [SMEM, VMEM, VMEM], (wides, crossing, label), slot_table
-    )(holders, old, new)
-    joined, factors = call(join_mixed_kernel, [SMEM] + [VMEM] * 5, (singles, factor_shape))(
-        widths, tag, keep, across(cross, slots), old_keep, old_arrived
-    )
-    arrived = along_line(joined).reshape(right_dim, half)
-    second, first = call(final_kernel, [SMEM, SMEM] + [VMEM] * 5, (block, block))(
-        widths, holders, factors, stay, stay_2, arrived, first
+        mix_kernel,
+        [SMEM] + [VMEM] * (2 * places),
+        (wides, crossing, label),
+        [*tables, slot_table],
+    )(holders, *old, *new)
+    *joined, factors = call(
+        join_mixed_kernel, [SMEM] + [VMEM] * 5, (single,) * places + (factor_shape,)
+    )(widths, tag, keep, across(cross, slots), old_keep, old_arrived)
+    second, first = call(final_kernel, [SMEM, SMEM] + [VMEM] * (4 + places), (block, block))(
+        widths, holders, factors, stay, stay_2, first, *along_line(joined, slots)
     )
     return first[None], second[None]
 

time: 68.1 us -> 60.8 us (0.89)
  blocking collectives: 48.7 us -> 4.21 us
  starting transfers between devices: 3.1 us -> 22.1 us
  waiting for transfers between devices: 7.01 us -> 25.4 us
    all_to_all x4 -> x0, blocking collectives: 44.5 us -> none  [along_line(): return lax.all_to_all(pieces, 'sec', 0, 0, axis_index_groups=groups)]
    ppermute x0 -> x12, starting transfers between devices: none -> 18.9 us  [along_line(): sent.append(lax.ppermute(pieces[step], 'sec', pairs))]
    ppermute x0 -> x12, waiting for transfers between devices: none -> 18.4 us  [along_line(): sent.append(lax.ppermute(pieces[step], 'sec', pairs))]
  transfers between devices with their start and end apart: 2 -> 14, of which waited for: 2 -> 10; matrix products, arithmetic and copies ran while one was open for 0% -> 0% of each run, Pallas kernels for 0% -> 0%
where the time goes in v11:
time: 60.8 us; the launch traced here: 60.6 us
  waiting for transfers between devices  25.4 us (42%)
  starting transfers between devices  22.1 us (36%)
  Pallas kernels  7.36 us (12%)
  blocking collectives  4.21 us (7%)
  local copies, waits for them, and re-layouts  0.91 us (1%)
  between operations  0.72 us (1%)
    ppermute x12, starting transfers between devices, along_line(): sent.append(lax.ppermute(pieces[step], 'sec', pairs))  18.9 us
    ppermute x12, waiting for transfers between devices, along_line(): sent.append(lax.ppermute(pieces[step], 'sec', pairs))  18.4 us
    ppermute x2, waiting for transfers between devices, across(): lax.ppermute(piece, 'sec', [(slot, slot ^ 1) for slot in range(slots)])  6.99 us
    ppermute x2, starting transfers between devices, across(): lax.ppermute(piece, 'sec', [(slot, slot ^ 1) for slot in range(slots)])  3.12 us
    all_gather x1, blocking collectives, on_device(): amps_full = lax.all_gather(staged, 'env')  2.22 us
    all_gather x1, blocking collectives, on_device(): first_full = lax.all_gather(first, 'env')  1.99 us
    pallas_call x1, Pallas kernels, on_device(): call(first_kernel, [SMEM, SMEM] + [VMEM] * 3, (pair,) * places + (block,...  1.54 us
    pallas_call x1, Pallas kernels, on_device(): call(final_kernel, [SMEM, SMEM] + [VMEM] * (4 + places), (block, block))  1.31 us
  transfers between devices with their start and end apart: 14, of which 10 were waited for; matrix products, arithmetic and copies ran while one was open for 0% of the time, Pallas kernels for 0%

profile of v11, /device:TPU:0, one launch (start us, length us, event | category | flops | bytes accessed | tf_op | source)
XLA Modules:
  0.0 60.6 jit_solution(7788618198463115860)
XLA Ops:
  0.6 0.9 %copy-done.4 = bf16[1,128,512]{2,1,0:T(8,128)(2,1)S(1)} copy-done((bf16[1,128,512]{2,1,0:T(8,128)(2,1)S(1)}, bf16[1,128,512]{2,1,0:T(8,128)(2,1)}, u32[]{:S(2)}) %copy-start.4) | copy-done | bytes 131096
  1.6 2.2 %all-gather = bf16[256,512]{1,0:T(8,128)(2,1)S(1)} all-gather(bf16[128,512]{1,0:T(8,128)(2,1)S(1)} %shard_map.68), channel_id=2, replica_groups=mesh['runs'=2,'sec'=8,'env'=2] {'env'}, dimensions={0}, use_global_device_ids=true | all-gather | bytes 393216 | tf_op jit(solution)/shard_map/all_gather | solution.py:406
  3.8 1.5 %shard_map.69 = (bf16[2,32,512]{2,1,0:T(8,128)(2,1)S(1)}, bf16[2,32,512]{2,1,0:T(8,128)(2,1)S(1)}, bf16[2,32,512]{2,1,0:T(8,128)(2,1)S(1)}, bf16[2,32,512]{2,1,0...) custom-call(s32[8]{0:T(128)S(1)} %copy-done.3, s32[8]{0:T(128)S(1)} %copy-done.2, ...), custom_call_target="tpu_custom_call" | custom-call | flops 452984832 | bytes 262144 | tf_op jit(solution)/shard_map/pallas_call | solution.py:408
  5.3 3.0 %collective-permute-start = (bf16[2,32,512]{2,1,0:T(8,128)(2,1)S(1)}, bf16[2,32,512]{2,1,0:T(8,128)(2,1)S(1)}, u32[]{:S(2)}, u32[]{:S(2)}) collective-permute-start(bf16[2,32,512]{2,1,0:T(8,128)(2,1)S(1)} %get-tuple-element.30), channel_id=1, source_target_pairs={{0,4},{2,6},{4,0},{6,2},{8,12},{10,14},{12,8},{14,10},{1,5},{3,7},... | collective-permute-start | bytes 196616 | tf_op jit(solution)/shard_map/ppermute | solution.py:373
  8.4 2.6 %collective-permute-start.1 = (bf16[2,32,512]{2,1,0:T(8,128)(2,1)S(1)}, bf16[2,32,512]{2,1,0:T(8,128)(2,1)S(1)}, u32[]{:S(2)}, u32[]{:S(2)}) collective-permute-start(bf16[2,32,512]{2,1,0:T(8,128)(2,1)S(1)} %get-tuple-element.31), channel_id=1, source_target_pairs={{0,8},{2,10},{4,12},{6,14},{8,0},{10,2},{12,4},{14,6},{1,9},{3,11}... | collective-permute-start | bytes 196616 | tf_op jit(solution)/shard_map/ppermute | solution.py:373
  10.9 4.9 %collective-permute-done.1.rest_2_ = bf16[2,32,512]{2,1,0:T(8,128)(2,1)S(1)} collective-permute-done((bf16[2,32,512]{2,1,0:T(8,128)(2,1)S(1)}, bf16[2,32,512]{2,1,0:T(8,128)(2,1)S(1)}, u32[]{:S(2)}, u32[]{:S(2)}) %collective-permute-start.1) | collective-permute-done | bytes 65568 | tf_op jit(solution)/shard_map/ppermute | solution.py:373
  15.9 1.2 %collective-permute-done.2.rest_3_ = bf16[2,32,512]{2,1,0:T(8,128)(2,1)S(1)} collective-permute-done((bf16[2,32,512]{2,1,0:T(8,128)(2,1)S(1)}, bf16[2,32,512]{2,1,0:T(8,128)(2,1)S(1)}, u32[]{:S(2)}, u32[]{:S(2)}) %collective-permute-start.2) | collective-permute-done | bytes 65568 | tf_op jit(solution)/shard_map/ppermute | solution.py:373
  17.1 0.7 %shard_map.70 = (bf16[4,32,512]{2,1,0:T(8,128)(2,1)S(1)}, bf16[4,32,512]{2,1,0:T(8,128)(2,1)S(1)}) custom-call(s32[8]{0:T(128)S(1)} %copy-done.2, bf16[2,32,512]{2,1,0:T(8,128)(2,1)S(1)} %get-tuple-element.29.rest_0_, bf16[2,32,512]{2,1,0:T(8,128)(2,1)S(1)} %collective-permute-done.rest_1_, bf16[2,32,512]{2,1,0:T(8,128)(2,1)S(1)} %collective-permute-done.1.rest_2_, ...), custom_call_target="tpu_custom_call" | custom-call | bytes 262144 | tf_op jit(solution)/shard_map/pallas_call | solution.py:412
  17.8 1.6 %collective-permute-start.3 = (bf16[4,32,512]{2,1,0:T(8,128)(2,1)S(1)}, bf16[4,32,512]{2,1,0:T(8,128)(2,1)S(1)}, u32[]{:S(2)}, u32[]{:S(2)}) collective-permute-start(bf16[4,32,512]{2,1,0:T(8,128)(2,1)S(1)} %get-tuple-element.36), channel_id=1, source_target_pairs={{0,2},{2,0},{4,6},{6,4},{8,10},{10,8},{12,14},{14,12},{1,3},{3,1},... | collective-permute-start | bytes 393224 | tf_op jit(solution)/shard_map/ppermute | solution.py:378
  19.4 3.5 %collective-permute-done.3.arrived.old_arrived = bf16[4,32,512]{2,1,0:T(8,128)(2,1)S(1)} collective-permute-done((bf16[4,32,512]{2,1,0:T(8,128)(2,1)S(1)}, bf16[4,32,512]{2,1,0:T(8,128)(2,1)S(1)}, u32[]{:S(2)}, u32[]{:S(2)}) %collective-permute-start.3) | collective-permute-done | bytes 131104 | tf_op jit(solution)/shard_map/ppermute | solution.py:378
  22.9 0.9 %collective-permute-start.4 = (bf16[32,512]{1,0:T(8,128)(2,1)S(1)}, bf16[32,512]{1,0:T(8,128)(2,1)S(1)}, u32[]{:S(2)}, u32[]{:S(2)}) collective-permute-start(bf16[32,512]{1,0:T(8,128)(2,1)S(1)} %get-tuple-element.38), channel_id=1, source_target_pairs={{0,4},{2,6},{4,0},{6,2},{8,12},{10,14},{12,8},{14,10},{1,5},{3,7},... | collective-permute-start | bytes 98312 | tf_op jit(solution)/shard_map/ppermute | solution.py:373
  23.8 1.7 %collective-permute-start.5 = (bf16[32,512]{1,0:T(8,128)(2,1)S(1)}, bf16[32,512]{1,0:T(8,128)(2,1)S(1)}, u32[]{:S(2)}, u32[]{:S(2)}) collective-permute-start(bf16[32,512]{1,0:T(8,128)(2,1)S(1)} %get-tuple-element.39), channel_id=1, source_target_pairs={{0,8},{2,10},{4,12},{6,14},{8,0},{10,2},{12,4},{14,6},{1,9},{3,11}... | collective-permute-start | bytes 98312 | tf_op jit(solution)/shard_map/ppermute | solution.py:373
  25.5 1.8 %collective-permute-start.6 = (bf16[32,512]{1,0:T(8,128)(2,1)S(1)}, bf16[32,512]{1,0:T(8,128)(2,1)S(1)}, u32[]{:S(2)}, u32[]{:S(2)}) collective-permute-start(bf16[32,512]{1,0:T(8,128)(2,1)S(1)} %get-tuple-element.40), channel_id=1, source_target_pairs={{0,12},{2,14},{4,8},{6,10},{8,4},{10,6},{12,0},{14,2},{1,13},{3,15... | collective-permute-start | bytes 98312 | tf_op jit(solution)/shard_map/ppermute | solution.py:373
  27.4 1.3 %collective-permute-done.5.rest_2_ = bf16[32,512]{1,0:T(8,128)(2,1)S(1)} collective-permute-done((bf16[32,512]{1,0:T(8,128)(2,1)S(1)}, bf16[32,512]{1,0:T(8,128)(2,1)S(1)}, u32[]{:S(2)}, u32[]{:S(2)}) %collective-permute-start.5) | collective-permute-done | bytes 32800 | tf_op jit(solution)/shard_map/ppermute | solution.py:373
  28.6 2.6 %collective-permute-done.6.rest_3_ = bf16[32,512]{1,0:T(8,128)(2,1)S(1)} collective-permute-done((bf16[32,512]{1,0:T(8,128)(2,1)S(1)}, bf16[32,512]{1,0:T(8,128)(2,1)S(1)}, u32[]{:S(2)}, u32[]{:S(2)}) %collective-permute-start.6) | collective-permute-done | bytes 32800 | tf_op jit(solution)/shard_map/ppermute | solution.py:373
  31.2 0.6 shard_map.72.first
  31.9 2.0 %all-gather.1 = bf16[256,512]{1,0:T(8,128)(2,1)S(1)} all-gather(bf16[128,512]{1,0:T(8,128)(2,1)S(1)} %shard_map.72.first), channel_id=3, replica_groups=mesh['runs'=2,'sec'=8,'env'=2] {'env'}, dimensions={0}, use_global_device_ids=true | all-gather | bytes 393216 | tf_op jit(solution)/shard_map/all_gather | solution.py:421
  33.9 1.2 %shard_map.73 = (bf16[272,128]{1,0:T(8,128)(2,1)S(1)}, bf16[272,128]{1,0:T(8,128)(2,1)S(1)}, bf16[272,128]{1,0:T(8,128)(2,1)S(1)}, bf16[272,128]{1,0:T(8,128)(2,1)S(1)}, f32[128,512]{1,0:T(8,128)S(1)}) custom-call(bf16[2,128,512]{2,1,0:T(8,128)(2,1)S(1)} %get-tuple-element.33.start, bf16[2,128,512]{2,1,0:T(8,128)(2,1)S(1)} %bitcast.5, ...), custom_call_target="tpu_custom_call" | custom-call | flops 452984832 | bytes 262144 | tf_op jit(solution)/shard_map/pallas_call | solution.py:422
  35.2 2.4 %collective-permute-start.8 = (bf16[272,128]{1,0:T(8,128)(2,1)S(1)}, bf16[272,128]{1,0:T(8,128)(2,1)S(1)}, u32[]{:S(2)}, u32[]{:S(2)}) collective-permute-start(bf16[272,128]{1,0:T(8,128)(2,1)S(1)} %get-tuple-element.43), channel_id=1, source_target_pairs={{0,8},{2,10},{4,12},{6,14},{8,0},{10,2},{12,4},{14,6},{1,9},{3,11}... | collective-permute-start | bytes 208904 | tf_op jit(solution)/shard_map/ppermute | solution.py:373
  37.6 2.0 %collective-permute-start.9 = (bf16[272,128]{1,0:T(8,128)(2,1)S(1)}, bf16[272,128]{1,0:T(8,128)(2,1)S(1)}, u32[]{:S(2)}, u32[]{:S(2)}) collective-permute-start(bf16[272,128]{1,0:T(8,128)(2,1)S(1)} %get-tuple-element.44), channel_id=1, source_target_pairs={{0,12},{2,14},{4,8},{6,10},{8,4},{10,6},{12,0},{14,2},{1,13},{3,15... | collective-permute-start | bytes 208904 | tf_op jit(solution)/shard_map/ppermute | solution.py:373
  39.6 0.9 %collective-permute-done.7.rest_5_ = bf16[272,128]{1,0:T(8,128)(2,1)S(1)} collective-permute-done((bf16[272,128]{1,0:T(8,128)(2,1)S(1)}, bf16[272,128]{1,0:T(8,128)(2,1)S(1)}, u32[]{:S(2)}, u32[]{:S(2)}) %collective-permute-start.7) | collective-permute-done | bytes 69664 | tf_op jit(solution)/shard_map/ppermute | solution.py:373
  40.4 3.7 %collective-permute-done.8.rest_6_ = bf16[272,128]{1,0:T(8,128)(2,1)S(1)} collective-permute-done((bf16[272,128]{1,0:T(8,128)(2,1)S(1)}, bf16[272,128]{1,0:T(8,128)(2,1)S(1)}, u32[]{:S(2)}, u32[]{:S(2)}) %collective-permute-start.8) | collective-permute-done | bytes 69664 | tf_op jit(solution)/shard_map/ppermute | solution.py:373
  44.1 1.0 %shard_map.74 = (f32[4,32,512]{2,1,0:T(8,128)S(1)}, bf16[528,128]{1,0:T(8,128)(2,1)S(1)}, bf16[16,128]{1,0:T(8,128)(2,1)S(1)}) custom-call(s32[8]{0:T(128)S(1)} %copy-done.2, bf16[2,32,512]{2,1,0:T(8,128)(2,1)S(1)} %get-tuple-element.29.rest_0_, bf16[2,32,512]{2,1,0:T(8,128)(2,1)S(1)} %collective-permute-done.rest_1_, ...), custom_call_target="tpu_custom_call" | custom-call | bytes 262144 | tf_op jit(solution)/shard_map/pallas_call | solution.py:426
  45.1 1.6 %collective-permute-start.10 = (bf16[528,128]{1,0:T(8,128)(2,1)S(1)}, bf16[528,128]{1,0:T(8,128)(2,1)S(1)}, u32[]{:S(2)}, u32[]{:S(2)}) collective-permute-start(bf16[528,128]{1,0:T(8,128)(2,1)S(1)} %get-tuple-element.47), channel_id=1, source_target_pairs={{0,2},{2,0},{4,6},{6,4},{8,10},{10,8},{12,14},{14,12},{1,3},{3,1},... | collective-permute-start | bytes 405512 | tf_op jit(solution)/shard_map/ppermute | solution.py:378
  46.6 3.5 %collective-permute-done.10.arrived = bf16[528,128]{1,0:T(8,128)(2,1)S(1)} collective-permute-done((bf16[528,128]{1,0:T(8,128)(2,1)S(1)}, bf16[528,128]{1,0:T(8,128)(2,1)S(1)}, u32[]{:S(2)}, u32[]{:S(2)}) %collective-permute-start.10) | collective-permute-done | bytes 135200 | tf_op jit(solution)/shard_map/ppermute | solution.py:378
  50.2 0.9 %shard_map.75 = (bf16[32,512]{1,0:T(8,128)(2,1)S(1)}, bf16[32,512]{1,0:T(8,128)(2,1)S(1)}, bf16[32,512]{1,0:T(8,128)(2,1)S(1)}, bf16[32,512]{1,0:T(8,128)(2,1)S(1)}, f32[8,128]{1,0:T(8,128)S(1)}) custom-call(s32[8]{0:T(128)S(1)} %copy-done.3, bf16[16,128]{1,0:T(8,128)(2,1)S(1)} %get-tuple-element.45.tag_line, f32[4,32,512]{2,1,0:T(8,128)S(1)} %get-tuple-element.46.keep, ...), custom_call_target="tpu_custom_call" | custom-call | bytes 262144 | tf_op jit(solution)/shard_map/pallas_call | solution.py:432
  51.1 1.4 %collective-permute-start.11 = (bf16[32,512]{1,0:T(8,128)(2,1)S(1)}, bf16[32,512]{1,0:T(8,128)(2,1)S(1)}, u32[]{:S(2)}, u32[]{:S(2)}) collective-permute-start(bf16[32,512]{1,0:T(8,128)(2,1)S(1)} %get-tuple-element.51), channel_id=1, source_target_pairs={{0,4},{2,6},{4,0},{6,2},{8,12},{10,14},{12,8},{14,10},{1,5},{3,7},... | collective-permute-start | bytes 98312 | tf_op jit(solution)/shard_map/ppermute | solution.py:373
  52.5 1.2 %collective-permute-start.12 = (bf16[32,512]{1,0:T(8,128)(2,1)S(1)}, bf16[32,512]{1,0:T(8,128)(2,1)S(1)}, u32[]{:S(2)}, u32[]{:S(2)}) collective-permute-start(bf16[32,512]{1,0:T(8,128)(2,1)S(1)} %get-tuple-element.52), channel_id=1, source_target_pairs={{0,8},{2,10},{4,12},{6,14},{8,0},{10,2},{12,4},{14,6},{1,9},{3,11}... | collective-permute-start | bytes 98312 | tf_op jit(solution)/shard_map/ppermute | solution.py:373
  53.6 1.9 %collective-permute-start.13 = (bf16[32,512]{1,0:T(8,128)(2,1)S(1)}, bf16[32,512]{1,0:T(8,128)(2,1)S(1)}, u32[]{:S(2)}, u32[]{:S(2)}) collective-permute-start(bf16[32,512]{1,0:T(8,128)(2,1)S(1)} %get-tuple-element.53), channel_id=1, source_target_pairs={{0,12},{2,14},{4,8},{6,10},{8,4},{10,6},{12,0},{14,2},{1,13},{3,15... | collective-permute-start | bytes 98312 | tf_op jit(solution)/shard_map/ppermute | solution.py:373
  55.5 2.1 %collective-permute-done.12.rest_2_ = bf16[32,512]{1,0:T(8,128)(2,1)S(1)} collective-permute-done((bf16[32,512]{1,0:T(8,128)(2,1)S(1)}, bf16[32,512]{1,0:T(8,128)(2,1)S(1)}, u32[]{:S(2)}, u32[]{:S(2)}) %collective-permute-start.12) | collective-permute-done | bytes 32800 | tf_op jit(solution)/shard_map/ppermute | solution.py:373
  57.6 1.7 %collective-permute-done.13.rest_3_ = bf16[32,512]{1,0:T(8,128)(2,1)S(1)} collective-permute-done((bf16[32,512]{1,0:T(8,128)(2,1)S(1)}, bf16[32,512]{1,0:T(8,128)(2,1)S(1)}, u32[]{:S(2)}, u32[]{:S(2)}) %collective-permute-start.13) | collective-permute-done | bytes 32800 | tf_op jit(solution)/shard_map/ppermute | solution.py:373
  59.3 1.3 %shard_map.76 = (bf16[128,512]{1,0:T(8,128)(2,1)}, bf16[128,512]{1,0:T(8,128)(2,1)}) custom-call(s32[8]{0:T(128)S(1)} %copy-done.3, s32[8]{0:T(128)S(1)} %copy-done.2, f32[8,128]{1,0:T(8,128)S(1)} %get-tuple-element.48.factors, bf16[128,512]{1,0:T(8,128)(2,1)S(1)} %get-tuple-element.34.stay, f32[128,512]{1,0:T(8,128)S(1)} %get-tuple-element.49.stay_2, ...), custom_call_target="tpu_custom_call" | custom-call | bytes 262144 | tf_op jit(solution)/shard_map/pallas_call | solution.py:435
  (17 shorter events, 0.1 us)
Async XLA Ops:
  0.6 0.9 %copy-start.4 = (bf16[1,128,512]{2,1,0:T(8,128)(2,1)S(1)}, bf16[1,128,512]{2,1,0:T(8,128)(2,1)}, u32[]{:S(2)}) copy-start(bf16[1,128,512]{2,1,0:T(8,128)(2,1)} %param.5) | copy-start | bytes 393220
  1.5 2.2 %copy-start = (bf16[1,3,1024,512]{3,2,1,0:T(8,128)(2,1)S(1)}, bf16[1,3,1024,512]{3,2,1,0:T(8,128)(2,1)}, u32[]{:S(2)}) copy-start(bf16[1,3,1024,512]{3,2,1,0:T(8,128)(2,1)} %left.3) | copy-start | bytes 9437188
  1.5 2.2 %copy-start.1 = (bf16[3,128,128]{2,1,0:T(8,128)(2,1)S(1)}, bf16[3,128,128]{2,1,0:T(8,128)(2,1)}, u32[]{:S(2)}) copy-start(bf16[3,128,128]{2,1,0:T(8,128)(2,1)} %right.3) | copy-start | bytes 294916
  1.5 2.2 %copy-start.2 = (s32[8]{0:T(128)S(1)}, s32[8]{0:T(128)}, u32[]{:S(2)}) copy-start(s32[8]{0:T(128)} %holders.9) | copy-start | bytes 100
  1.5 2.3 %copy-start.3 = (s32[8]{0:T(128)S(1)}, s32[8]{0:T(128)}, u32[]{:S(2)}) copy-start(s32[8]{0:T(128)} %widths.7) | copy-start | bytes 100
  5.3 5.6 %collective-permute-start = (bf16[2,32,512]{2,1,0:T(8,128)(2,1)S(1)}, bf16[2,32,512]{2,1,0:T(8,128)(2,1)S(1)}, u32[]{:S(2)}, u32[]{:S(2)}) collective-permute-start(bf16[2,32,512]{2,1,0:T(8,128)(2,1)S(1)} %get-tuple-element.30), channel_id=1, source_target_pairs={{0,4},{2,6},{4,0},{6,2},{8,12},{10,14},{12,8},{14,10},{1,5},{3,7},... | collective-permute-start | bytes 196616 | tf_op jit(solution)/shard_map/ppermute | solution.py:373
  8.4 7.5 %collective-permute-start.1 = (bf16[2,32,512]{2,1,0:T(8,128)(2,1)S(1)}, bf16[2,32,512]{2,1,0:T(8,128)(2,1)S(1)}, u32[]{:S(2)}, u32[]{:S(2)}) collective-permute-start(bf16[2,32,512]{2,1,0:T(8,128)(2,1)S(1)} %get-tuple-element.31), channel_id=1, source_target_pairs={{0,8},{2,10},{4,12},{6,14},{8,0},{10,2},{12,4},{14,6},{1,9},{3,11}... | collective-permute-start | bytes 196616 | tf_op jit(solution)/shard_map/ppermute | solution.py:373
  10.9 6.2 %collective-permute-start.2 = (bf16[2,32,512]{2,1,0:T(8,128)(2,1)S(1)}, bf16[2,32,512]{2,1,0:T(8,128)(2,1)S(1)}, u32[]{:S(2)}, u32[]{:S(2)}) collective-permute-start(bf16[2,32,512]{2,1,0:T(8,128)(2,1)S(1)} %get-tuple-element.32), channel_id=1, source_target_pairs={{0,12},{2,14},{4,8},{6,10},{8,4},{10,6},{12,0},{14,2},{1,13},{3,15... | collective-permute-start | bytes 196616 | tf_op jit(solution)/shard_map/ppermute | solution.py:373
  17.8 5.0 %collective-permute-start.3 = (bf16[4,32,512]{2,1,0:T(8,128)(2,1)S(1)}, bf16[4,32,512]{2,1,0:T(8,128)(2,1)S(1)}, u32[]{:S(2)}, u32[]{:S(2)}) collective-permute-start(bf16[4,32,512]{2,1,0:T(8,128)(2,1)S(1)} %get-tuple-element.36), channel_id=1, source_target_pairs={{0,2},{2,0},{4,6},{6,4},{8,10},{10,8},{12,14},{14,12},{1,3},{3,1},... | collective-permute-start | bytes 393224 | tf_op jit(solution)/shard_map/ppermute | solution.py:378
  22.9 4.5 %collective-permute-start.4 = (bf16[32,512]{1,0:T(8,128)(2,1)S(1)}, bf16[32,512]{1,0:T(8,128)(2,1)S(1)}, u32[]{:S(2)}, u32[]{:S(2)}) collective-permute-start(bf16[32,512]{1,0:T(8,128)(2,1)S(1)} %get-tuple-element.38), channel_id=1, source_target_pairs={{0,4},{2,6},{4,0},{6,2},{8,12},{10,14},{12,8},{14,10},{1,5},{3,7},... | collective-permute-start | bytes 98312 | tf_op jit(solution)/shard_map/ppermute | solution.py:373
  23.8 4.8 %collective-permute-start.5 = (bf16[32,512]{1,0:T(8,128)(2,1)S(1)}, bf16[32,512]{1,0:T(8,128)(2,1)S(1)}, u32[]{:S(2)}, u32[]{:S(2)}) collective-permute-start(bf16[32,512]{1,0:T(8,128)(2,1)S(1)} %get-tuple-element.39), channel_id=1, source_target_pairs={{0,8},{2,10},{4,12},{6,14},{8,0},{10,2},{12,4},{14,6},{1,9},{3,11}... | collective-permute-start | bytes 98312 | tf_op jit(solution)/shard_map/ppermute | solution.py:373
  25.5 5.7 %collective-permute-start.6 = (bf16[32,512]{1,0:T(8,128)(2,1)S(1)}, bf16[32,512]{1,0:T(8,128)(2,1)S(1)}, u32[]{:S(2)}, u32[]{:S(2)}) collective-permute-start(bf16[32,512]{1,0:T(8,128)(2,1)S(1)} %get-tuple-element.40), channel_id=1, source_target_pairs={{0,12},{2,14},{4,8},{6,10},{8,4},{10,6},{12,0},{14,2},{1,13},{3,15... | collective-permute-start | bytes 98312 | tf_op jit(solution)/shard_map/ppermute | solution.py:373
  35.1 5.3 %collective-permute-start.7 = (bf16[272,128]{1,0:T(8,128)(2,1)S(1)}, bf16[272,128]{1,0:T(8,128)(2,1)S(1)}, u32[]{:S(2)}, u32[]{:S(2)}) collective-permute-start(bf16[272,128]{1,0:T(8,128)(2,1)S(1)} %get-tuple-element.42), channel_id=1, source_target_pairs={{0,4},{2,6},{4,0},{6,2},{8,12},{10,14},{12,8},{14,10},{1,5},{3,7},... | collective-permute-start | bytes 208904 | tf_op jit(solution)/shard_map/ppermute | solution.py:373
  35.2 8.9 %collective-permute-start.8 = (bf16[272,128]{1,0:T(8,128)(2,1)S(1)}, bf16[272,128]{1,0:T(8,128)(2,1)S(1)}, u32[]{:S(2)}, u32[]{:S(2)}) collective-permute-start(bf16[272,128]{1,0:T(8,128)(2,1)S(1)} %get-tuple-element.43), channel_id=1, source_target_pairs={{0,8},{2,10},{4,12},{6,14},{8,0},{10,2},{12,4},{14,6},{1,9},{3,11}... | collective-permute-start | bytes 208904 | tf_op jit(solution)/shard_map/ppermute | solution.py:373
  37.6 6.5 %collective-permute-start.9 = (bf16[272,128]{1,0:T(8,128)(2,1)S(1)}, bf16[272,128]{1,0:T(8,128)(2,1)S(1)}, u32[]{:S(2)}, u32[]{:S(2)}) collective-permute-start(bf16[272,128]{1,0:T(8,128)(2,1)S(1)} %get-tuple-element.44), channel_id=1, source_target_pairs={{0,12},{2,14},{4,8},{6,10},{8,4},{10,6},{12,0},{14,2},{1,13},{3,15... | collective-permute-start | bytes 208904 | tf_op jit(solution)/shard_map/ppermute | solution.py:373
  45.1 5.1 %collective-permute-start.10 = (bf16[528,128]{1,0:T(8,128)(2,1)S(1)}, bf16[528,128]{1,0:T(8,128)(2,1)S(1)}, u32[]{:S(2)}, u32[]{:S(2)}) collective-permute-start(bf16[528,128]{1,0:T(8,128)(2,1)S(1)} %get-tuple-element.47), channel_id=1, source_target_pairs={{0,2},{2,0},{4,6},{6,4},{8,10},{10,8},{12,14},{14,12},{1,3},{3,1},... | collective-permute-start | bytes 405512 | tf_op jit(solution)/shard_map/ppermute | solution.py:378
  51.1 4.5 %collective-permute-start.11 = (bf16[32,512]{1,0:T(8,128)(2,1)S(1)}, bf16[32,512]{1,0:T(8,128)(2,1)S(1)}, u32[]{:S(2)}, u32[]{:S(2)}) collective-permute-start(bf16[32,512]{1,0:T(8,128)(2,1)S(1)} %get-tuple-element.51), channel_id=1, source_target_pairs={{0,4},{2,6},{4,0},{6,2},{8,12},{10,14},{12,8},{14,10},{1,5},{3,7},... | collective-permute-start | bytes 98312 | tf_op jit(solution)/shard_map/ppermute | solution.py:373
  52.5 5.2 %collective-permute-start.12 = (bf16[32,512]{1,0:T(8,128)(2,1)S(1)}, bf16[32,512]{1,0:T(8,128)(2,1)S(1)}, u32[]{:S(2)}, u32[]{:S(2)}) collective-permute-start(bf16[32,512]{1,0:T(8,128)(2,1)S(1)} %get-tuple-element.52), channel_id=1, source_target_pairs={{0,8},{2,10},{4,12},{6,14},{8,0},{10,2},{12,4},{14,6},{1,9},{3,11}... | collective-permute-start | bytes 98312 | tf_op jit(solution)/shard_map/ppermute | solution.py:373
  53.6 5.7 %collective-permute-start.13 = (bf16[32,512]{1,0:T(8,128)(2,1)S(1)}, bf16[32,512]{1,0:T(8,128)(2,1)S(1)}, u32[]{:S(2)}, u32[]{:S(2)}) collective-permute-start(bf16[32,512]{1,0:T(8,128)(2,1)S(1)} %get-tuple-element.53), channel_id=1, source_target_pairs={{0,12},{2,14},{4,8},{6,10},{8,4},{10,6},{12,0},{14,2},{1,13},{3,15... | collective-permute-start | bytes 98312 | tf_op jit(solution)/shard_map/ppermute | solution.py:373

commit v12 on v11

--- a/solution.py
+++ b/solution.py
@@ -367,11 +367,12 @@
 
 
 def along_line(pieces, slots):
-    sent = [pieces[0]]
-    for step in range(1, len(pieces)):
+    places = len(pieces)
+    sent = {0: pieces[0]}
+    for step in sorted(range(1, places), key=lambda step: step < places // 2):
         pairs = [(slot, slot ^ (step * LINES)) for slot in range(slots)]
-        sent.append(lax.ppermute(pieces[step], "sec", pairs))
-    return sent
+        sent[step] = lax.ppermute(pieces[step], "sec", pairs)
+    return [sent[step] for step in range(places)]
 
 
 def across(piece, slots):

time: 60.8 us -> 60.8 us (level)
  no operation moved by 1% of the time
where the time goes in v12:
time: 60.8 us; the launch traced here: 60.6 us
  waiting for transfers between devices  25.4 us (42%)
  starting transfers between devices  22.1 us (36%)
  Pallas kernels  7.36 us (12%)
  blocking collectives  4.21 us (7%)
  local copies, waits for them, and re-layouts  0.91 us (1%)
  between operations  0.72 us (1%)
    ppermute x12, starting transfers between devices, along_line(): sent[step] = lax.ppermute(pieces[step], 'sec', pairs)  18.9 us
    ppermute x12, waiting for transfers between devices, along_line(): sent[step] = lax.ppermute(pieces[step], 'sec', pairs)  18.4 us
    ppermute x2, waiting for transfers between devices, across(): lax.ppermute(piece, 'sec', [(slot, slot ^ 1) for slot in range(slots)])  6.99 us
    ppermute x2, starting transfers between devices, across(): lax.ppermute(piece, 'sec', [(slot, slot ^ 1) for slot in range(slots)])  3.12 us
    all_gather x1, blocking collectives, on_device(): amps_full = lax.all_gather(staged, 'env')  2.22 us
    all_gather x1, blocking collectives, on_device(): first_full = lax.all_gather(first, 'env')  1.99 us
    pallas_call x1, Pallas kernels, on_device(): call(first_kernel, [SMEM, SMEM] + [VMEM] * 3, (pair,) * places + (block,...  1.54 us
    pallas_call x1, Pallas kernels, on_device(): call(final_kernel, [SMEM, SMEM] + [VMEM] * (4 + places), (block, block))  1.31 us
  transfers between devices with their start and end apart: 14, of which 10 were waited for; matrix products, arithmetic and copies ran while one was open for 0% of the time, Pallas kernels for 0%

profile of v12, /device:TPU:0, one launch (start us, length us, event | category | flops | bytes accessed | tf_op | source)
XLA Modules:
  0.0 60.6 jit_solution(7788618198463115860)
XLA Ops:
  0.6 0.9 %copy-done.4 = bf16[1,128,512]{2,1,0:T(8,128)(2,1)S(1)} copy-done((bf16[1,128,512]{2,1,0:T(8,128)(2,1)S(1)}, bf16[1,128,512]{2,1,0:T(8,128)(2,1)}, u32[]{:S(2)}) %copy-start.4) | copy-done | bytes 131096
  1.6 2.2 %all-gather = bf16[256,512]{1,0:T(8,128)(2,1)S(1)} all-gather(bf16[128,512]{1,0:T(8,128)(2,1)S(1)} %shard_map.68), channel_id=2, replica_groups=mesh['runs'=2,'sec'=8,'env'=2] {'env'}, dimensions={0}, use_global_device_ids=true | all-gather | bytes 393216 | tf_op jit(solution)/shard_map/all_gather | solution.py:407
  3.8 1.5 %shard_map.69 = (bf16[2,32,512]{2,1,0:T(8,128)(2,1)S(1)}, bf16[2,32,512]{2,1,0:T(8,128)(2,1)S(1)}, bf16[2,32,512]{2,1,0:T(8,128)(2,1)S(1)}, bf16[2,32,512]{2,1,0...) custom-call(s32[8]{0:T(128)S(1)} %copy-done.3, s32[8]{0:T(128)S(1)} %copy-done.2, ...), custom_call_target="tpu_custom_call" | custom-call | flops 452984832 | bytes 262144 | tf_op jit(solution)/shard_map/pallas_call | solution.py:409
  5.3 3.0 %collective-permute-start = (bf16[2,32,512]{2,1,0:T(8,128)(2,1)S(1)}, bf16[2,32,512]{2,1,0:T(8,128)(2,1)S(1)}, u32[]{:S(2)}, u32[]{:S(2)}) collective-permute-start(bf16[2,32,512]{2,1,0:T(8,128)(2,1)S(1)} %get-tuple-element.30), channel_id=1, source_target_pairs={{0,4},{2,6},{4,0},{6,2},{8,12},{10,14},{12,8},{14,10},{1,5},{3,7},... | collective-permute-start | bytes 196616 | tf_op jit(solution)/shard_map/ppermute | solution.py:374
  8.4 2.6 %collective-permute-start.1 = (bf16[2,32,512]{2,1,0:T(8,128)(2,1)S(1)}, bf16[2,32,512]{2,1,0:T(8,128)(2,1)S(1)}, u32[]{:S(2)}, u32[]{:S(2)}) collective-permute-start(bf16[2,32,512]{2,1,0:T(8,128)(2,1)S(1)} %get-tuple-element.31), channel_id=1, source_target_pairs={{0,8},{2,10},{4,12},{6,14},{8,0},{10,2},{12,4},{14,6},{1,9},{3,11}... | collective-permute-start | bytes 196616 | tf_op jit(solution)/shard_map/ppermute | solution.py:374
  10.9 4.9 %collective-permute-done.1.rest_2_ = bf16[2,32,512]{2,1,0:T(8,128)(2,1)S(1)} collective-permute-done((bf16[2,32,512]{2,1,0:T(8,128)(2,1)S(1)}, bf16[2,32,512]{2,1,0:T(8,128)(2,1)S(1)}, u32[]{:S(2)}, u32[]{:S(2)}) %collective-permute-start.1) | collective-permute-done | bytes 65568 | tf_op jit(solution)/shard_map/ppermute | solution.py:374
  15.9 1.2 %collective-permute-done.2.rest_3_ = bf16[2,32,512]{2,1,0:T(8,128)(2,1)S(1)} collective-permute-done((bf16[2,32,512]{2,1,0:T(8,128)(2,1)S(1)}, bf16[2,32,512]{2,1,0:T(8,128)(2,1)S(1)}, u32[]{:S(2)}, u32[]{:S(2)}) %collective-permute-start.2) | collective-permute-done | bytes 65568 | tf_op jit(solution)/shard_map/ppermute | solution.py:374
  17.1 0.7 %shard_map.70 = (bf16[4,32,512]{2,1,0:T(8,128)(2,1)S(1)}, bf16[4,32,512]{2,1,0:T(8,128)(2,1)S(1)}) custom-call(s32[8]{0:T(128)S(1)} %copy-done.2, bf16[2,32,512]{2,1,0:T(8,128)(2,1)S(1)} %get-tuple-element.29.rest_0_, bf16[2,32,512]{2,1,0:T(8,128)(2,1)S(1)} %collective-permute-done.rest_1_, bf16[2,32,512]{2,1,0:T(8,128)(2,1)S(1)} %collective-permute-done.1.rest_2_, ...), custom_call_target="tpu_custom_call" | custom-call | bytes 262144 | tf_op jit(solution)/shard_map/pallas_call | solution.py:413
  17.8 1.6 %collective-permute-start.3 = (bf16[4,32,512]{2,1,0:T(8,128)(2,1)S(1)}, bf16[4,32,512]{2,1,0:T(8,128)(2,1)S(1)}, u32[]{:S(2)}, u32[]{:S(2)}) collective-permute-start(bf16[4,32,512]{2,1,0:T(8,128)(2,1)S(1)} %get-tuple-element.36), channel_id=1, source_target_pairs={{0,2},{2,0},{4,6},{6,4},{8,10},{10,8},{12,14},{14,12},{1,3},{3,1},... | collective-permute-start | bytes 393224 | tf_op jit(solution)/shard_map/ppermute | solution.py:379
  19.4 3.5 %collective-permute-done.3.arrived.old_arrived = bf16[4,32,512]{2,1,0:T(8,128)(2,1)S(1)} collective-permute-done((bf16[4,32,512]{2,1,0:T(8,128)(2,1)S(1)}, bf16[4,32,512]{2,1,0:T(8,128)(2,1)S(1)}, u32[]{:S(2)}, u32[]{:S(2)}) %collective-permute-start.3) | collective-permute-done | bytes 131104 | tf_op jit(solution)/shard_map/ppermute | solution.py:379
  22.9 0.9 %collective-permute-start.4 = (bf16[32,512]{1,0:T(8,128)(2,1)S(1)}, bf16[32,512]{1,0:T(8,128)(2,1)S(1)}, u32[]{:S(2)}, u32[]{:S(2)}) collective-permute-start(bf16[32,512]{1,0:T(8,128)(2,1)S(1)} %get-tuple-element.38), channel_id=1, source_target_pairs={{0,4},{2,6},{4,0},{6,2},{8,12},{10,14},{12,8},{14,10},{1,5},{3,7},... | collective-permute-start | bytes 98312 | tf_op jit(solution)/shard_map/ppermute | solution.py:374
  23.8 1.7 %collective-permute-start.5 = (bf16[32,512]{1,0:T(8,128)(2,1)S(1)}, bf16[32,512]{1,0:T(8,128)(2,1)S(1)}, u32[]{:S(2)}, u32[]{:S(2)}) collective-permute-start(bf16[32,512]{1,0:T(8,128)(2,1)S(1)} %get-tuple-element.39), channel_id=1, source_target_pairs={{0,8},{2,10},{4,12},{6,14},{8,0},{10,2},{12,4},{14,6},{1,9},{3,11}... | collective-permute-start | bytes 98312 | tf_op jit(solution)/shard_map/ppermute | solution.py:374
  25.5 1.8 %collective-permute-start.6 = (bf16[32,512]{1,0:T(8,128)(2,1)S(1)}, bf16[32,512]{1,0:T(8,128)(2,1)S(1)}, u32[]{:S(2)}, u32[]{:S(2)}) collective-permute-start(bf16[32,512]{1,0:T(8,128)(2,1)S(1)} %get-tuple-element.40), channel_id=1, source_target_pairs={{0,12},{2,14},{4,8},{6,10},{8,4},{10,6},{12,0},{14,2},{1,13},{3,15... | collective-permute-start | bytes 98312 | tf_op jit(solution)/shard_map/ppermute | solution.py:374
  27.4 1.3 %collective-permute-done.5.rest_2_ = bf16[32,512]{1,0:T(8,128)(2,1)S(1)} collective-permute-done((bf16[32,512]{1,0:T(8,128)(2,1)S(1)}, bf16[32,512]{1,0:T(8,128)(2,1)S(1)}, u32[]{:S(2)}, u32[]{:S(2)}) %collective-permute-start.5) | collective-permute-done | bytes 32800 | tf_op jit(solution)/shard_map/ppermute | solution.py:374
  28.6 2.6 %collective-permute-done.6.rest_3_ = bf16[32,512]{1,0:T(8,128)(2,1)S(1)} collective-permute-done((bf16[32,512]{1,0:T(8,128)(2,1)S(1)}, bf16[32,512]{1,0:T(8,128)(2,1)S(1)}, u32[]{:S(2)}, u32[]{:S(2)}) %collective-permute-start.6) | collective-permute-done | bytes 32800 | tf_op jit(solution)/shard_map/ppermute | solution.py:374
  31.2 0.6 shard_map.72.first
  31.9 2.0 %all-gather.1 = bf16[256,512]{1,0:T(8,128)(2,1)S(1)} all-gather(bf16[128,512]{1,0:T(8,128)(2,1)S(1)} %shard_map.72.first), channel_id=3, replica_groups=mesh['runs'=2,'sec'=8,'env'=2] {'env'}, dimensions={0}, use_global_device_ids=true | all-gather | bytes 393216 | tf_op jit(solution)/shard_map/all_gather | solution.py:422
  33.9 1.2 %shard_map.73 = (bf16[272,128]{1,0:T(8,128)(2,1)S(1)}, bf16[272,128]{1,0:T(8,128)(2,1)S(1)}, bf16[272,128]{1,0:T(8,128)(2,1)S(1)}, bf16[272,128]{1,0:T(8,128)(2,1)S(1)}, f32[128,512]{1,0:T(8,128)S(1)}) custom-call(bf16[2,128,512]{2,1,0:T(8,128)(2,1)S(1)} %get-tuple-element.33.start, bf16[2,128,512]{2,1,0:T(8,128)(2,1)S(1)} %bitcast.5, ...), custom_call_target="tpu_custom_call" | custom-call | flops 452984832 | bytes 262144 | tf_op jit(solution)/shard_map/pallas_call | solution.py:423
  35.2 2.4 %collective-permute-start.8 = (bf16[272,128]{1,0:T(8,128)(2,1)S(1)}, bf16[272,128]{1,0:T(8,128)(2,1)S(1)}, u32[]{:S(2)}, u32[]{:S(2)}) collective-permute-start(bf16[272,128]{1,0:T(8,128)(2,1)S(1)} %get-tuple-element.43), channel_id=1, source_target_pairs={{0,8},{2,10},{4,12},{6,14},{8,0},{10,2},{12,4},{14,6},{1,9},{3,11}... | collective-permute-start | bytes 208904 | tf_op jit(solution)/shard_map/ppermute | solution.py:374
  37.6 2.0 %collective-permute-start.9 = (bf16[272,128]{1,0:T(8,128)(2,1)S(1)}, bf16[272,128]{1,0:T(8,128)(2,1)S(1)}, u32[]{:S(2)}, u32[]{:S(2)}) collective-permute-start(bf16[272,128]{1,0:T(8,128)(2,1)S(1)} %get-tuple-element.44), channel_id=1, source_target_pairs={{0,12},{2,14},{4,8},{6,10},{8,4},{10,6},{12,0},{14,2},{1,13},{3,15... | collective-permute-start | bytes 208904 | tf_op jit(solution)/shard_map/ppermute | solution.py:374
  39.6 0.9 %collective-permute-done.7.rest_5_ = bf16[272,128]{1,0:T(8,128)(2,1)S(1)} collective-permute-done((bf16[272,128]{1,0:T(8,128)(2,1)S(1)}, bf16[272,128]{1,0:T(8,128)(2,1)S(1)}, u32[]{:S(2)}, u32[]{:S(2)}) %collective-permute-start.7) | collective-permute-done | bytes 69664 | tf_op jit(solution)/shard_map/ppermute | solution.py:374
  40.4 3.7 %collective-permute-done.8.rest_6_ = bf16[272,128]{1,0:T(8,128)(2,1)S(1)} collective-permute-done((bf16[272,128]{1,0:T(8,128)(2,1)S(1)}, bf16[272,128]{1,0:T(8,128)(2,1)S(1)}, u32[]{:S(2)}, u32[]{:S(2)}) %collective-permute-start.8) | collective-permute-done | bytes 69664 | tf_op jit(solution)/shard_map/ppermute | solution.py:374
  44.1 1.0 %shard_map.74 = (f32[4,32,512]{2,1,0:T(8,128)S(1)}, bf16[528,128]{1,0:T(8,128)(2,1)S(1)}, bf16[16,128]{1,0:T(8,128)(2,1)S(1)}) custom-call(s32[8]{0:T(128)S(1)} %copy-done.2, bf16[2,32,512]{2,1,0:T(8,128)(2,1)S(1)} %get-tuple-element.29.rest_0_, bf16[2,32,512]{2,1,0:T(8,128)(2,1)S(1)} %collective-permute-done.rest_1_, ...), custom_call_target="tpu_custom_call" | custom-call | bytes 262144 | tf_op jit(solution)/shard_map/pallas_call | solution.py:427
  45.1 1.6 %collective-permute-start.10 = (bf16[528,128]{1,0:T(8,128)(2,1)S(1)}, bf16[528,128]{1,0:T(8,128)(2,1)S(1)}, u32[]{:S(2)}, u32[]{:S(2)}) collective-permute-start(bf16[528,128]{1,0:T(8,128)(2,1)S(1)} %get-tuple-element.47), channel_id=1, source_target_pairs={{0,2},{2,0},{4,6},{6,4},{8,10},{10,8},{12,14},{14,12},{1,3},{3,1},... | collective-permute-start | bytes 405512 | tf_op jit(solution)/shard_map/ppermute | solution.py:379
  46.6 3.5 %collective-permute-done.10.arrived = bf16[528,128]{1,0:T(8,128)(2,1)S(1)} collective-permute-done((bf16[528,128]{1,0:T(8,128)(2,1)S(1)}, bf16[528,128]{1,0:T(8,128)(2,1)S(1)}, u32[]{:S(2)}, u32[]{:S(2)}) %collective-permute-start.10) | collective-permute-done | bytes 135200 | tf_op jit(solution)/shard_map/ppermute | solution.py:379
  50.2 0.9 %shard_map.75 = (bf16[32,512]{1,0:T(8,128)(2,1)S(1)}, bf16[32,512]{1,0:T(8,128)(2,1)S(1)}, bf16[32,512]{1,0:T(8,128)(2,1)S(1)}, bf16[32,512]{1,0:T(8,128)(2,1)S(1)}, f32[8,128]{1,0:T(8,128)S(1)}) custom-call(s32[8]{0:T(128)S(1)} %copy-done.3, bf16[16,128]{1,0:T(8,128)(2,1)S(1)} %get-tuple-element.45.tag_line, f32[4,32,512]{2,1,0:T(8,128)S(1)} %get-tuple-element.46.keep, ...), custom_call_target="tpu_custom_call" | custom-call | bytes 262144 | tf_op jit(solution)/shard_map/pallas_call | solution.py:433
  51.1 1.4 %collective-permute-start.11 = (bf16[32,512]{1,0:T(8,128)(2,1)S(1)}, bf16[32,512]{1,0:T(8,128)(2,1)S(1)}, u32[]{:S(2)}, u32[]{:S(2)}) collective-permute-start(bf16[32,512]{1,0:T(8,128)(2,1)S(1)} %get-tuple-element.51), channel_id=1, source_target_pairs={{0,4},{2,6},{4,0},{6,2},{8,12},{10,14},{12,8},{14,10},{1,5},{3,7},... | collective-permute-start | bytes 98312 | tf_op jit(solution)/shard_map/ppermute | solution.py:374
  52.5 1.2 %collective-permute-start.12 = (bf16[32,512]{1,0:T(8,128)(2,1)S(1)}, bf16[32,512]{1,0:T(8,128)(2,1)S(1)}, u32[]{:S(2)}, u32[]{:S(2)}) collective-permute-start(bf16[32,512]{1,0:T(8,128)(2,1)S(1)} %get-tuple-element.52), channel_id=1, source_target_pairs={{0,8},{2,10},{4,12},{6,14},{8,0},{10,2},{12,4},{14,6},{1,9},{3,11}... | collective-permute-start | bytes 98312 | tf_op jit(solution)/shard_map/ppermute | solution.py:374
  53.6 1.9 %collective-permute-start.13 = (bf16[32,512]{1,0:T(8,128)(2,1)S(1)}, bf16[32,512]{1,0:T(8,128)(2,1)S(1)}, u32[]{:S(2)}, u32[]{:S(2)}) collective-permute-start(bf16[32,512]{1,0:T(8,128)(2,1)S(1)} %get-tuple-element.53), channel_id=1, source_target_pairs={{0,12},{2,14},{4,8},{6,10},{8,4},{10,6},{12,0},{14,2},{1,13},{3,15... | collective-permute-start | bytes 98312 | tf_op jit(solution)/shard_map/ppermute | solution.py:374
  55.5 2.1 %collective-permute-done.12.rest_2_ = bf16[32,512]{1,0:T(8,128)(2,1)S(1)} collective-permute-done((bf16[32,512]{1,0:T(8,128)(2,1)S(1)}, bf16[32,512]{1,0:T(8,128)(2,1)S(1)}, u32[]{:S(2)}, u32[]{:S(2)}) %collective-permute-start.12) | collective-permute-done | bytes 32800 | tf_op jit(solution)/shard_map/ppermute | solution.py:374
  57.6 1.7 %collective-permute-done.13.rest_3_ = bf16[32,512]{1,0:T(8,128)(2,1)S(1)} collective-permute-done((bf16[32,512]{1,0:T(8,128)(2,1)S(1)}, bf16[32,512]{1,0:T(8,128)(2,1)S(1)}, u32[]{:S(2)}, u32[]{:S(2)}) %collective-permute-start.13) | collective-permute-done | bytes 32800 | tf_op jit(solution)/shard_map/ppermute | solution.py:374
  59.3 1.3 %shard_map.76 = (bf16[128,512]{1,0:T(8,128)(2,1)}, bf16[128,512]{1,0:T(8,128)(2,1)}) custom-call(s32[8]{0:T(128)S(1)} %copy-done.3, s32[8]{0:T(128)S(1)} %copy-done.2, f32[8,128]{1,0:T(8,128)S(1)} %get-tuple-element.48.factors, bf16[128,512]{1,0:T(8,128)(2,1)S(1)} %get-tuple-element.34.stay, f32[128,512]{1,0:T(8,128)S(1)} %get-tuple-element.49.stay_2, ...), custom_call_target="tpu_custom_call" | custom-call | bytes 262144 | tf_op jit(solution)/shard_map/pallas_call | solution.py:436
  (17 shorter events, 0.1 us)
Async XLA Ops:
  0.6 0.9 %copy-start.4 = (bf16[1,128,512]{2,1,0:T(8,128)(2,1)S(1)}, bf16[1,128,512]{2,1,0:T(8,128)(2,1)}, u32[]{:S(2)}) copy-start(bf16[1,128,512]{2,1,0:T(8,128)(2,1)} %param.5) | copy-start | bytes 393220
  1.5 2.2 %copy-start = (bf16[1,3,1024,512]{3,2,1,0:T(8,128)(2,1)S(1)}, bf16[1,3,1024,512]{3,2,1,0:T(8,128)(2,1)}, u32[]{:S(2)}) copy-start(bf16[1,3,1024,512]{3,2,1,0:T(8,128)(2,1)} %left.3) | copy-start | bytes 9437188
  1.5 2.2 %copy-start.1 = (bf16[3,128,128]{2,1,0:T(8,128)(2,1)S(1)}, bf16[3,128,128]{2,1,0:T(8,128)(2,1)}, u32[]{:S(2)}) copy-start(bf16[3,128,128]{2,1,0:T(8,128)(2,1)} %right.3) | copy-start | bytes 294916
  1.5 2.2 %copy-start.2 = (s32[8]{0:T(128)S(1)}, s32[8]{0:T(128)}, u32[]{:S(2)}) copy-start(s32[8]{0:T(128)} %holders.9) | copy-start | bytes 100
  1.5 2.3 %copy-start.3 = (s32[8]{0:T(128)S(1)}, s32[8]{0:T(128)}, u32[]{:S(2)}) copy-start(s32[8]{0:T(128)} %widths.7) | copy-start | bytes 100
  5.3 5.6 %collective-permute-start = (bf16[2,32,512]{2,1,0:T(8,128)(2,1)S(1)}, bf16[2,32,512]{2,1,0:T(8,128)(2,1)S(1)}, u32[]{:S(2)}, u32[]{:S(2)}) collective-permute-start(bf16[2,32,512]{2,1,0:T(8,128)(2,1)S(1)} %get-tuple-element.30), channel_id=1, source_target_pairs={{0,4},{2,6},{4,0},{6,2},{8,12},{10,14},{12,8},{14,10},{1,5},{3,7},... | collective-permute-start | bytes 196616 | tf_op jit(solution)/shard_map/ppermute | solution.py:374
  8.4 7.5 %collective-permute-start.1 = (bf16[2,32,512]{2,1,0:T(8,128)(2,1)S(1)}, bf16[2,32,512]{2,1,0:T(8,128)(2,1)S(1)}, u32[]{:S(2)}, u32[]{:S(2)}) collective-permute-start(bf16[2,32,512]{2,1,0:T(8,128)(2,1)S(1)} %get-tuple-element.31), channel_id=1, source_target_pairs={{0,8},{2,10},{4,12},{6,14},{8,0},{10,2},{12,4},{14,6},{1,9},{3,11}... | collective-permute-start | bytes 196616 | tf_op jit(solution)/shard_map/ppermute | solution.py:374
  10.9 6.2 %collective-permute-start.2 = (bf16[2,32,512]{2,1,0:T(8,128)(2,1)S(1)}, bf16[2,32,512]{2,1,0:T(8,128)(2,1)S(1)}, u32[]{:S(2)}, u32[]{:S(2)}) collective-permute-start(bf16[2,32,512]{2,1,0:T(8,128)(2,1)S(1)} %get-tuple-element.32), channel_id=1, source_target_pairs={{0,12},{2,14},{4,8},{6,10},{8,4},{10,6},{12,0},{14,2},{1,13},{3,15... | collective-permute-start | bytes 196616 | tf_op jit(solution)/shard_map/ppermute | solution.py:374
  17.8 5.0 %collective-permute-start.3 = (bf16[4,32,512]{2,1,0:T(8,128)(2,1)S(1)}, bf16[4,32,512]{2,1,0:T(8,128)(2,1)S(1)}, u32[]{:S(2)}, u32[]{:S(2)}) collective-permute-start(bf16[4,32,512]{2,1,0:T(8,128)(2,1)S(1)} %get-tuple-element.36), channel_id=1, source_target_pairs={{0,2},{2,0},{4,6},{6,4},{8,10},{10,8},{12,14},{14,12},{1,3},{3,1},... | collective-permute-start | bytes 393224 | tf_op jit(solution)/shard_map/ppermute | solution.py:379
  22.9 4.5 %collective-permute-start.4 = (bf16[32,512]{1,0:T(8,128)(2,1)S(1)}, bf16[32,512]{1,0:T(8,128)(2,1)S(1)}, u32[]{:S(2)}, u32[]{:S(2)}) collective-permute-start(bf16[32,512]{1,0:T(8,128)(2,1)S(1)} %get-tuple-element.38), channel_id=1, source_target_pairs={{0,4},{2,6},{4,0},{6,2},{8,12},{10,14},{12,8},{14,10},{1,5},{3,7},... | collective-permute-start | bytes 98312 | tf_op jit(solution)/shard_map/ppermute | solution.py:374
  23.8 4.8 %collective-permute-start.5 = (bf16[32,512]{1,0:T(8,128)(2,1)S(1)}, bf16[32,512]{1,0:T(8,128)(2,1)S(1)}, u32[]{:S(2)}, u32[]{:S(2)}) collective-permute-start(bf16[32,512]{1,0:T(8,128)(2,1)S(1)} %get-tuple-element.39), channel_id=1, source_target_pairs={{0,8},{2,10},{4,12},{6,14},{8,0},{10,2},{12,4},{14,6},{1,9},{3,11}... | collective-permute-start | bytes 98312 | tf_op jit(solution)/shard_map/ppermute | solution.py:374
  25.5 5.7 %collective-permute-start.6 = (bf16[32,512]{1,0:T(8,128)(2,1)S(1)}, bf16[32,512]{1,0:T(8,128)(2,1)S(1)}, u32[]{:S(2)}, u32[]{:S(2)}) collective-permute-start(bf16[32,512]{1,0:T(8,128)(2,1)S(1)} %get-tuple-element.40), channel_id=1, source_target_pairs={{0,12},{2,14},{4,8},{6,10},{8,4},{10,6},{12,0},{14,2},{1,13},{3,15... | collective-permute-start | bytes 98312 | tf_op jit(solution)/shard_map/ppermute | solution.py:374
  35.1 5.3 %collective-permute-start.7 = (bf16[272,128]{1,0:T(8,128)(2,1)S(1)}, bf16[272,128]{1,0:T(8,128)(2,1)S(1)}, u32[]{:S(2)}, u32[]{:S(2)}) collective-permute-start(bf16[272,128]{1,0:T(8,128)(2,1)S(1)} %get-tuple-element.42), channel_id=1, source_target_pairs={{0,4},{2,6},{4,0},{6,2},{8,12},{10,14},{12,8},{14,10},{1,5},{3,7},... | collective-permute-start | bytes 208904 | tf_op jit(solution)/shard_map/ppermute | solution.py:374
  35.2 8.9 %collective-permute-start.8 = (bf16[272,128]{1,0:T(8,128)(2,1)S(1)}, bf16[272,128]{1,0:T(8,128)(2,1)S(1)}, u32[]{:S(2)}, u32[]{:S(2)}) collective-permute-start(bf16[272,128]{1,0:T(8,128)(2,1)S(1)} %get-tuple-element.43), channel_id=1, source_target_pairs={{0,8},{2,10},{4,12},{6,14},{8,0},{10,2},{12,4},{14,6},{1,9},{3,11}... | collective-permute-start | bytes 208904 | tf_op jit(solution)/shard_map/ppermute | solution.py:374
  37.6 6.5 %collective-permute-start.9 = (bf16[272,128]{1,0:T(8,128)(2,1)S(1)}, bf16[272,128]{1,0:T(8,128)(2,1)S(1)}, u32[]{:S(2)}, u32[]{:S(2)}) collective-permute-start(bf16[272,128]{1,0:T(8,128)(2,1)S(1)} %get-tuple-element.44), channel_id=1, source_target_pairs={{0,12},{2,14},{4,8},{6,10},{8,4},{10,6},{12,0},{14,2},{1,13},{3,15... | collective-permute-start | bytes 208904 | tf_op jit(solution)/shard_map/ppermute | solution.py:374
  45.1 5.1 %collective-permute-start.10 = (bf16[528,128]{1,0:T(8,128)(2,1)S(1)}, bf16[528,128]{1,0:T(8,128)(2,1)S(1)}, u32[]{:S(2)}, u32[]{:S(2)}) collective-permute-start(bf16[528,128]{1,0:T(8,128)(2,1)S(1)} %get-tuple-element.47), channel_id=1, source_target_pairs={{0,2},{2,0},{4,6},{6,4},{8,10},{10,8},{12,14},{14,12},{1,3},{3,1},... | collective-permute-start | bytes 405512 | tf_op jit(solution)/shard_map/ppermute | solution.py:379
  51.1 4.5 %collective-permute-start.11 = (bf16[32,512]{1,0:T(8,128)(2,1)S(1)}, bf16[32,512]{1,0:T(8,128)(2,1)S(1)}, u32[]{:S(2)}, u32[]{:S(2)}) collective-permute-start(bf16[32,512]{1,0:T(8,128)(2,1)S(1)} %get-tuple-element.51), channel_id=1, source_target_pairs={{0,4},{2,6},{4,0},{6,2},{8,12},{10,14},{12,8},{14,10},{1,5},{3,7},... | collective-permute-start | bytes 98312 | tf_op jit(solution)/shard_map/ppermute | solution.py:374
  52.5 5.2 %collective-permute-start.12 = (bf16[32,512]{1,0:T(8,128)(2,1)S(1)}, bf16[32,512]{1,0:T(8,128)(2,1)S(1)}, u32[]{:S(2)}, u32[]{:S(2)}) collective-permute-start(bf16[32,512]{1,0:T(8,128)(2,1)S(1)} %get-tuple-element.52), channel_id=1, source_target_pairs={{0,8},{2,10},{4,12},{6,14},{8,0},{10,2},{12,4},{14,6},{1,9},{3,11}... | collective-permute-start | bytes 98312 | tf_op jit(solution)/shard_map/ppermute | solution.py:374
  53.6 5.7 %collective-permute-start.13 = (bf16[32,512]{1,0:T(8,128)(2,1)S(1)}, bf16[32,512]{1,0:T(8,128)(2,1)S(1)}, u32[]{:S(2)}, u32[]{:S(2)}) collective-permute-start(bf16[32,512]{1,0:T(8,128)(2,1)S(1)} %get-tuple-element.53), channel_id=1, source_target_pairs={{0,12},{2,14},{4,8},{6,10},{8,4},{10,6},{12,0},{14,2},{1,13},{3,15... | collective-permute-start | bytes 98312 | tf_op jit(solution)/shard_map/ppermute | solution.py:374

commit v13 on v11

--- a/solution.py
+++ b/solution.py
@@ -112,6 +112,7 @@
 LANES = 128
 TAG = 16
 LINES = 2
+STEPS = (0, 2, 3, 1)
 
 
 def live_columns(widths, holders, half):
@@ -148,7 +149,7 @@
             stay[...] = block
         else:
             block_vmem[...] = block.reshape(block_vmem.shape)
-            for step, piece in enumerate(pieces):
+            for step, piece in zip(STEPS, pieces):
                 piece[term - 1] = block_vmem[own_place() ^ step]
 
 
@@ -176,7 +177,7 @@
 def merge_kernel(holders, *rest):
     *pieces, keep, cross, table, slot_of = rest
     fill_slots(holders, slot_of)
-    for step, piece in enumerate(pieces):
+    for step, piece in zip(STEPS, pieces):
         table[own_place() ^ step] = piece[...]
     for place, crossing, here, source in line_targets(holders, slot_of):
         total = 0.0
@@ -187,7 +188,7 @@
 
 
 def join_kernel(keep, arrived, *outs):
-    for step, out in enumerate(outs):
+    for step, out in zip(STEPS, outs):
         place = own_place() ^ step
         total = keep[place].astype(jnp.float32) + arrived[place].astype(jnp.float32)
         out[...] = total.astype(jnp.bfloat16)
@@ -200,7 +201,7 @@
 def sum_kernel(widths, holders, stay, *rest):
     *pieces, first = rest
     live = live_columns(widths, holders, stay.shape[1])
-    for step, piece in enumerate(pieces):
+    for step, piece in zip(STEPS, pieces):
         place = piece_rows(step, piece.shape[0])
         total = stay[place, :].astype(jnp.float32) + piece[...].astype(jnp.float32)
         first[place, :] = jnp.where(live, total, 0.0).astype(jnp.bfloat16)
@@ -245,7 +246,7 @@
             stay[...] = block
         else:
             block_vmem[...] = block.astype(jnp.bfloat16).reshape(block_vmem.shape)
-            for step, piece in enumerate(pieces):
+            for step, piece in zip(STEPS, pieces):
                 part = block_vmem[own_place() ^ step]
                 for c in range(chunks):
                     place = pl.ds(((term - 1) * chunks + c) * rows, rows)
@@ -273,10 +274,10 @@
     chunks = half // LANES
     fill_slots(holders, slot_of)
     tag = jnp.zeros((TAG, LANES), jnp.float32)
-    for step in range(places):
-        old[own_place() ^ step] = rest[step][...]
-        new[own_place() ^ step] = rest[places + step][...]
-        label = rest[places + step][pl.ds(2 * chunks * rows, TAG), :]
+    for i, step in enumerate(STEPS):
+        old[own_place() ^ step] = rest[i][...]
+        new[own_place() ^ step] = rest[places + i][...]
+        label = rest[places + i][pl.ds(2 * chunks * rows, TAG), :]
         tag = tag + label.astype(jnp.float32)
     tag_out[...] = tag.astype(jnp.bfloat16)
     cross[pl.ds(places * chunks * rows, TAG), :] = tag.astype(jnp.bfloat16)
@@ -327,7 +328,7 @@
     line = me % LINES
     shift_here = line_quotient(overlaps, norms, line) - quotient
     shift_there = line_quotient(overlaps, norms, 1 - line) - quotient
-    for step, out in enumerate(outs):
+    for step, out in zip(STEPS, outs):
         place = own_place() ^ step
         starts = [pl.multiple_of((place * chunks + c) * rows, rows) for c in range(chunks)]
         block = jnp.concatenate(
@@ -343,7 +344,7 @@
     first_out[...] = first[...]
     live = live_columns(widths, holders, stay.shape[1])
     scale, shift = factors[0:1, 0:1], factors[1:2, 0:1]
-    for step, piece in enumerate(pieces):
+    for step, piece in zip(STEPS, pieces):
         place = piece_rows(step, piece.shape[0])
         total = scale * stay_2[place, :] + shift * stay[place, :].astype(jnp.float32)
         total = total + piece[...].astype(jnp.float32)
@@ -367,10 +368,10 @@
 
 
 def along_line(pieces, slots):
-    sent = [pieces[0]]
-    for step in range(1, len(pieces)):
+    sent = []
+    for step, piece in zip(STEPS, pieces):
         pairs = [(slot, slot ^ (step * LINES)) for slot in range(slots)]
-        sent.append(lax.ppermute(pieces[step], "sec", pairs))
+        sent.append(lax.ppermute(piece, "sec", pairs) if step else piece)
     return sent
 
 

time: 60.8 us -> 59.9 us (0.985)
  starting transfers between devices: 22.1 us -> 20.1 us
  waiting for transfers between devices: 25.4 us -> 26.4 us
    ppermute x12, starting transfers between devices: 18.9 us -> 16.8 us  [along_line(): sent.append(lax.ppermute(piece, 'sec', pairs) if step else piece)]
    ppermute x12, waiting for transfers between devices: 18.4 us -> 19.2 us  [along_line(): sent.append(lax.ppermute(piece, 'sec', pairs) if step else piece)]
  transfers between devices with their start and end apart: 14 -> 14, of which waited for: 10 -> 11; matrix products, arithmetic and copies ran while one was open for 0% -> 0% of each run, Pallas kernels for 0% -> 0%
where the time goes in v13:
time: 59.9 us; the launch traced here: 59.7 us
  waiting for transfers between devices  26.4 us (44%)
  starting transfers between devices  20.1 us (34%)
  Pallas kernels  7.36 us (12%)
  blocking collectives  4.21 us (7%)
  local copies, waits for them, and re-layouts  0.91 us (2%)
  between operations  0.71 us (1%)
    ppermute x12, waiting for transfers between devices, along_line(): sent.append(lax.ppermute(piece, 'sec', pairs) if step else piece)  19.2 us
    ppermute x12, starting transfers between devices, along_line(): sent.append(lax.ppermute(piece, 'sec', pairs) if step else piece)  16.8 us
    ppermute x2, waiting for transfers between devices, across(): lax.ppermute(piece, 'sec', [(slot, slot ^ 1) for slot in range(slots)])  7.26 us
    ppermute x2, starting transfers between devices, across(): lax.ppermute(piece, 'sec', [(slot, slot ^ 1) for slot in range(slots)])  3.3 us
    all_gather x1, blocking collectives, on_device(): amps_full = lax.all_gather(staged, 'env')  2.22 us
    all_gather x1, blocking collectives, on_device(): first_full = lax.all_gather(first, 'env')  1.99 us
    pallas_call x1, Pallas kernels, on_device(): call(first_kernel, [SMEM, SMEM] + [VMEM] * 3, (pair,) * places + (block,...  1.54 us
    pallas_call x1, Pallas kernels, on_device(): call(final_kernel, [SMEM, SMEM] + [VMEM] * (4 + places), (block, block))  1.31 us
  transfers between devices with their start and end apart: 14, of which 11 were waited for; matrix products, arithmetic and copies ran while one was open for 0% of the time, Pallas kernels for 0%

profile of v13, /device:TPU:0, one launch (start us, length us, event | category | flops | bytes accessed | tf_op | source)
XLA Modules:
  0.0 59.7 jit_solution(7519068510677694822)
XLA Ops:
  0.6 0.9 %copy-done.4 = bf16[1,128,512]{2,1,0:T(8,128)(2,1)S(1)} copy-done((bf16[1,128,512]{2,1,0:T(8,128)(2,1)S(1)}, bf16[1,128,512]{2,1,0:T(8,128)(2,1)}, u32[]{:S(2)}) %copy-start.4) | copy-done | bytes 131096
  1.6 2.2 %all-gather = bf16[256,512]{1,0:T(8,128)(2,1)S(1)} all-gather(bf16[128,512]{1,0:T(8,128)(2,1)S(1)} %shard_map.68), channel_id=2, replica_groups=mesh['runs'=2,'sec'=8,'env'=2] {'env'}, dimensions={0}, use_global_device_ids=true | all-gather | bytes 393216 | tf_op jit(solution)/shard_map/all_gather | solution.py:407
  3.8 1.5 %shard_map.69 = (bf16[2,32,512]{2,1,0:T(8,128)(2,1)S(1)}, bf16[2,32,512]{2,1,0:T(8,128)(2,1)S(1)}, bf16[2,32,512]{2,1,0:T(8,128)(2,1)S(1)}, bf16[2,32,512]{2,1,0...) custom-call(s32[8]{0:T(128)S(1)} %copy-done.3, s32[8]{0:T(128)S(1)} %copy-done.2, ...), custom_call_target="tpu_custom_call" | custom-call | flops 452984832 | bytes 262144 | tf_op jit(solution)/shard_map/pallas_call | solution.py:409
  5.3 4.0 %collective-permute-start = (bf16[2,32,512]{2,1,0:T(8,128)(2,1)S(1)}, bf16[2,32,512]{2,1,0:T(8,128)(2,1)S(1)}, u32[]{:S(2)}, u32[]{:S(2)}) collective-permute-start(bf16[2,32,512]{2,1,0:T(8,128)(2,1)S(1)} %get-tuple-element.30), channel_id=1, source_target_pairs={{0,8},{2,10},{4,12},{6,14},{8,0},{10,2},{12,4},{14,6},{1,9},{3,11}... | collective-permute-start | bytes 196616 | tf_op jit(solution)/shard_map/ppermute | solution.py:374
  9.4 1.3 %collective-permute-start.1 = (bf16[2,32,512]{2,1,0:T(8,128)(2,1)S(1)}, bf16[2,32,512]{2,1,0:T(8,128)(2,1)S(1)}, u32[]{:S(2)}, u32[]{:S(2)}) collective-permute-start(bf16[2,32,512]{2,1,0:T(8,128)(2,1)S(1)} %get-tuple-element.31), channel_id=1, source_target_pairs={{0,12},{2,14},{4,8},{6,10},{8,4},{10,6},{12,0},{14,2},{1,13},{3,15... | collective-permute-start | bytes 196616 | tf_op jit(solution)/shard_map/ppermute | solution.py:374
  10.9 2.4 %collective-permute-done.rest_1_ = bf16[2,32,512]{2,1,0:T(8,128)(2,1)S(1)} collective-permute-done((bf16[2,32,512]{2,1,0:T(8,128)(2,1)S(1)}, bf16[2,32,512]{2,1,0:T(8,128)(2,1)S(1)}, u32[]{:S(2)}, u32[]{:S(2)}) %collective-permute-start) | collective-permute-done | bytes 65568 | tf_op jit(solution)/shard_map/ppermute | solution.py:374
  13.3 2.5 %collective-permute-done.1.rest_2_ = bf16[2,32,512]{2,1,0:T(8,128)(2,1)S(1)} collective-permute-done((bf16[2,32,512]{2,1,0:T(8,128)(2,1)S(1)}, bf16[2,32,512]{2,1,0:T(8,128)(2,1)S(1)}, u32[]{:S(2)}, u32[]{:S(2)}) %collective-permute-start.1) | collective-permute-done | bytes 65568 | tf_op jit(solution)/shard_map/ppermute | solution.py:374
  15.9 0.7 %shard_map.70 = (bf16[4,32,512]{2,1,0:T(8,128)(2,1)S(1)}, bf16[4,32,512]{2,1,0:T(8,128)(2,1)S(1)}) custom-call(s32[8]{0:T(128)S(1)} %copy-done.2, bf16[2,32,512]{2,1,0:T(8,128)(2,1)S(1)} %get-tuple-element.29.rest_0_, bf16[2,32,512]{2,1,0:T(8,128)(2,1)S(1)} %collective-permute-done.rest_1_, bf16[2,32,512]{2,1,0:T(8,128)(2,1)S(1)} %collective-permute-done.1.rest_2_, ...), custom_call_target="tpu_custom_call" | custom-call | bytes 262144 | tf_op jit(solution)/shard_map/pallas_call | solution.py:413
  16.7 1.7 %collective-permute-start.3 = (bf16[4,32,512]{2,1,0:T(8,128)(2,1)S(1)}, bf16[4,32,512]{2,1,0:T(8,128)(2,1)S(1)}, u32[]{:S(2)}, u32[]{:S(2)}) collective-permute-start(bf16[4,32,512]{2,1,0:T(8,128)(2,1)S(1)} %get-tuple-element.36), channel_id=1, source_target_pairs={{0,2},{2,0},{4,6},{6,4},{8,10},{10,8},{12,14},{14,12},{1,3},{3,1},... | collective-permute-start | bytes 393224 | tf_op jit(solution)/shard_map/ppermute | solution.py:379
  18.4 3.3 %collective-permute-done.3.arrived.old_arrived = bf16[4,32,512]{2,1,0:T(8,128)(2,1)S(1)} collective-permute-done((bf16[4,32,512]{2,1,0:T(8,128)(2,1)S(1)}, bf16[4,32,512]{2,1,0:T(8,128)(2,1)S(1)}, u32[]{:S(2)}, u32[]{:S(2)}) %collective-permute-start.3) | collective-permute-done | bytes 131104 | tf_op jit(solution)/shard_map/ppermute | solution.py:379
  21.7 3.2 %collective-permute-start.4 = (bf16[32,512]{1,0:T(8,128)(2,1)S(1)}, bf16[32,512]{1,0:T(8,128)(2,1)S(1)}, u32[]{:S(2)}, u32[]{:S(2)}) collective-permute-start(bf16[32,512]{1,0:T(8,128)(2,1)S(1)} %get-tuple-element.38), channel_id=1, source_target_pairs={{0,8},{2,10},{4,12},{6,14},{8,0},{10,2},{12,4},{14,6},{1,9},{3,11}... | collective-permute-start | bytes 98312 | tf_op jit(solution)/shard_map/ppermute | solution.py:374
  24.9 0.4 collective-permute-start.5
  25.4 0.4 collective-permute-start.6
  25.8 1.6 %collective-permute-done.4.rest_1_ = bf16[32,512]{1,0:T(8,128)(2,1)S(1)} collective-permute-done((bf16[32,512]{1,0:T(8,128)(2,1)S(1)}, bf16[32,512]{1,0:T(8,128)(2,1)S(1)}, u32[]{:S(2)}, u32[]{:S(2)}) %collective-permute-start.4) | collective-permute-done | bytes 32800 | tf_op jit(solution)/shard_map/ppermute | solution.py:374
  27.4 3.2 %collective-permute-done.5.rest_2_ = bf16[32,512]{1,0:T(8,128)(2,1)S(1)} collective-permute-done((bf16[32,512]{1,0:T(8,128)(2,1)S(1)}, bf16[32,512]{1,0:T(8,128)(2,1)S(1)}, u32[]{:S(2)}, u32[]{:S(2)}) %collective-permute-start.5) | collective-permute-done | bytes 32800 | tf_op jit(solution)/shard_map/ppermute | solution.py:374
  30.7 0.6 %shard_map.72.first = bf16[128,512]{1,0:T(8,128)(2,1)S(1)} custom-call(s32[8]{0:T(128)S(1)} %copy-done.3, s32[8]{0:T(128)S(1)} %copy-done.2, bf16[128,512]{1,0:T(8,128)(2,1)S(1)} %get-tuple-element.34.stay, bf16[32,512]{1,0:T(8,128)(2,1)S(1)} %get-tuple-element.37.rest_0_, bf16[32,512]{1,0:T(8,128)(2,1)S(1)} %collective-permute-done.4.rest_1_, ...), custom_call_target="tpu_custom_call" | custom-call | bytes 262144 | tf_op jit(solution)/shard_map/pallas_call | solution.py:418
  31.3 2.0 %all-gather.1 = bf16[256,512]{1,0:T(8,128)(2,1)S(1)} all-gather(bf16[128,512]{1,0:T(8,128)(2,1)S(1)} %shard_map.72.first), channel_id=3, replica_groups=mesh['runs'=2,'sec'=8,'env'=2] {'env'}, dimensions={0}, use_global_device_ids=true | all-gather | bytes 393216 | tf_op jit(solution)/shard_map/all_gather | solution.py:422
  33.3 1.2 %shard_map.73 = (bf16[272,128]{1,0:T(8,128)(2,1)S(1)}, bf16[272,128]{1,0:T(8,128)(2,1)S(1)}, bf16[272,128]{1,0:T(8,128)(2,1)S(1)}, bf16[272,128]{1,0:T(8,128)(2,1)S(1)}, f32[128,512]{1,0:T(8,128)S(1)}) custom-call(bf16[2,128,512]{2,1,0:T(8,128)(2,1)S(1)} %get-tuple-element.33.start, bf16[2,128,512]{2,1,0:T(8,128)(2,1)S(1)} %bitcast.5, ...), custom_call_target="tpu_custom_call" | custom-call | flops 452984832 | bytes 262144 | tf_op jit(solution)/shard_map/pallas_call | solution.py:423
  34.5 1.0 %collective-permute-start.7 = (bf16[272,128]{1,0:T(8,128)(2,1)S(1)}, bf16[272,128]{1,0:T(8,128)(2,1)S(1)}, u32[]{:S(2)}, u32[]{:S(2)}) collective-permute-start(bf16[272,128]{1,0:T(8,128)(2,1)S(1)} %get-tuple-element.42), channel_id=1, source_target_pairs={{0,8},{2,10},{4,12},{6,14},{8,0},{10,2},{12,4},{14,6},{1,9},{3,11}... | collective-permute-start | bytes 208904 | tf_op jit(solution)/shard_map/ppermute | solution.py:374
  35.5 1.2 %collective-permute-start.8 = (bf16[272,128]{1,0:T(8,128)(2,1)S(1)}, bf16[272,128]{1,0:T(8,128)(2,1)S(1)}, u32[]{:S(2)}, u32[]{:S(2)}) collective-permute-start(bf16[272,128]{1,0:T(8,128)(2,1)S(1)} %get-tuple-element.43), channel_id=1, source_target_pairs={{0,12},{2,14},{4,8},{6,10},{8,4},{10,6},{12,0},{14,2},{1,13},{3,15... | collective-permute-start | bytes 208904 | tf_op jit(solution)/shard_map/ppermute | solution.py:374
  36.7 1.4 %collective-permute-start.9 = (bf16[272,128]{1,0:T(8,128)(2,1)S(1)}, bf16[272,128]{1,0:T(8,128)(2,1)S(1)}, u32[]{:S(2)}, u32[]{:S(2)}) collective-permute-start(bf16[272,128]{1,0:T(8,128)(2,1)S(1)} %get-tuple-element.44), channel_id=1, source_target_pairs={{0,4},{2,6},{4,0},{6,2},{8,12},{10,14},{12,8},{14,10},{1,5},{3,7},... | collective-permute-start | bytes 208904 | tf_op jit(solution)/shard_map/ppermute | solution.py:374
  38.1 4.1 %collective-permute-done.7.rest_5_ = bf16[272,128]{1,0:T(8,128)(2,1)S(1)} collective-permute-done((bf16[272,128]{1,0:T(8,128)(2,1)S(1)}, bf16[272,128]{1,0:T(8,128)(2,1)S(1)}, u32[]{:S(2)}, u32[]{:S(2)}) %collective-permute-start.7) | collective-permute-done | bytes 69664 | tf_op jit(solution)/shard_map/ppermute | solution.py:374
  42.2 1.3 %collective-permute-done.9.rest_7_ = bf16[272,128]{1,0:T(8,128)(2,1)S(1)} collective-permute-done((bf16[272,128]{1,0:T(8,128)(2,1)S(1)}, bf16[272,128]{1,0:T(8,128)(2,1)S(1)}, u32[]{:S(2)}, u32[]{:S(2)}) %collective-permute-start.9) | collective-permute-done | bytes 69664 | tf_op jit(solution)/shard_map/ppermute | solution.py:374
  43.5 1.0 %shard_map.74 = (f32[4,32,512]{2,1,0:T(8,128)S(1)}, bf16[528,128]{1,0:T(8,128)(2,1)S(1)}, bf16[16,128]{1,0:T(8,128)(2,1)S(1)}) custom-call(s32[8]{0:T(128)S(1)} %copy-done.2, bf16[2,32,512]{2,1,0:T(8,128)(2,1)S(1)} %get-tuple-element.29.rest_0_, bf16[2,32,512]{2,1,0:T(8,128)(2,1)S(1)} %collective-permute-done.rest_1_, ...), custom_call_target="tpu_custom_call" | custom-call | bytes 262144 | tf_op jit(solution)/shard_map/pallas_call | solution.py:427
  44.5 1.6 %collective-permute-start.10 = (bf16[528,128]{1,0:T(8,128)(2,1)S(1)}, bf16[528,128]{1,0:T(8,128)(2,1)S(1)}, u32[]{:S(2)}, u32[]{:S(2)}) collective-permute-start(bf16[528,128]{1,0:T(8,128)(2,1)S(1)} %get-tuple-element.47), channel_id=1, source_target_pairs={{0,2},{2,0},{4,6},{6,4},{8,10},{10,8},{12,14},{14,12},{1,3},{3,1},... | collective-permute-start | bytes 405512 | tf_op jit(solution)/shard_map/ppermute | solution.py:379
  46.1 4.0 %collective-permute-done.10.arrived = bf16[528,128]{1,0:T(8,128)(2,1)S(1)} collective-permute-done((bf16[528,128]{1,0:T(8,128)(2,1)S(1)}, bf16[528,128]{1,0:T(8,128)(2,1)S(1)}, u32[]{:S(2)}, u32[]{:S(2)}) %collective-permute-start.10) | collective-permute-done | bytes 135200 | tf_op jit(solution)/shard_map/ppermute | solution.py:379
  50.0 0.9 %shard_map.75 = (bf16[32,512]{1,0:T(8,128)(2,1)S(1)}, bf16[32,512]{1,0:T(8,128)(2,1)S(1)}, bf16[32,512]{1,0:T(8,128)(2,1)S(1)}, bf16[32,512]{1,0:T(8,128)(2,1)S(1)}, f32[8,128]{1,0:T(8,128)S(1)}) custom-call(s32[8]{0:T(128)S(1)} %copy-done.3, bf16[16,128]{1,0:T(8,128)(2,1)S(1)} %get-tuple-element.45.tag_line, f32[4,32,512]{2,1,0:T(8,128)S(1)} %get-tuple-element.46.keep, ...), custom_call_target="tpu_custom_call" | custom-call | bytes 262144 | tf_op jit(solution)/shard_map/pallas_call | solution.py:433
  51.0 1.7 %collective-permute-start.11 = (bf16[32,512]{1,0:T(8,128)(2,1)S(1)}, bf16[32,512]{1,0:T(8,128)(2,1)S(1)}, u32[]{:S(2)}, u32[]{:S(2)}) collective-permute-start(bf16[32,512]{1,0:T(8,128)(2,1)S(1)} %get-tuple-element.51), channel_id=1, source_target_pairs={{0,8},{2,10},{4,12},{6,14},{8,0},{10,2},{12,4},{14,6},{1,9},{3,11}... | collective-permute-start | bytes 98312 | tf_op jit(solution)/shard_map/ppermute | solution.py:374
  52.7 1.4 %collective-permute-start.12 = (bf16[32,512]{1,0:T(8,128)(2,1)S(1)}, bf16[32,512]{1,0:T(8,128)(2,1)S(1)}, u32[]{:S(2)}, u32[]{:S(2)}) collective-permute-start(bf16[32,512]{1,0:T(8,128)(2,1)S(1)} %get-tuple-element.52), channel_id=1, source_target_pairs={{0,12},{2,14},{4,8},{6,10},{8,4},{10,6},{12,0},{14,2},{1,13},{3,15... | collective-permute-start | bytes 98312 | tf_op jit(solution)/shard_map/ppermute | solution.py:374
  54.5 2.0 %collective-permute-done.11.rest_1_ = bf16[32,512]{1,0:T(8,128)(2,1)S(1)} collective-permute-done((bf16[32,512]{1,0:T(8,128)(2,1)S(1)}, bf16[32,512]{1,0:T(8,128)(2,1)S(1)}, u32[]{:S(2)}, u32[]{:S(2)}) %collective-permute-start.11) | collective-permute-done | bytes 32800 | tf_op jit(solution)/shard_map/ppermute | solution.py:374
  56.5 1.9 %collective-permute-done.12.rest_2_ = bf16[32,512]{1,0:T(8,128)(2,1)S(1)} collective-permute-done((bf16[32,512]{1,0:T(8,128)(2,1)S(1)}, bf16[32,512]{1,0:T(8,128)(2,1)S(1)}, u32[]{:S(2)}, u32[]{:S(2)}) %collective-permute-start.12) | collective-permute-done | bytes 32800 | tf_op jit(solution)/shard_map/ppermute | solution.py:374
  58.4 1.3 %shard_map.76 = (bf16[128,512]{1,0:T(8,128)(2,1)}, bf16[128,512]{1,0:T(8,128)(2,1)}) custom-call(s32[8]{0:T(128)S(1)} %copy-done.3, s32[8]{0:T(128)S(1)} %copy-done.2, f32[8,128]{1,0:T(8,128)S(1)} %get-tuple-element.48.factors, bf16[128,512]{1,0:T(8,128)(2,1)S(1)} %get-tuple-element.34.stay, f32[128,512]{1,0:T(8,128)S(1)} %get-tuple-element.49.stay_2, ...), custom_call_target="tpu_custom_call" | custom-call | bytes 262144 | tf_op jit(solution)/shard_map/pallas_call | solution.py:436
  (17 shorter events, 0.9 us)
Async XLA Ops:
  0.6 0.9 %copy-start.4 = (bf16[1,128,512]{2,1,0:T(8,128)(2,1)S(1)}, bf16[1,128,512]{2,1,0:T(8,128)(2,1)}, u32[]{:S(2)}) copy-start(bf16[1,128,512]{2,1,0:T(8,128)(2,1)} %param.5) | copy-start | bytes 393220
  1.5 2.2 %copy-start = (bf16[1,3,1024,512]{3,2,1,0:T(8,128)(2,1)S(1)}, bf16[1,3,1024,512]{3,2,1,0:T(8,128)(2,1)}, u32[]{:S(2)}) copy-start(bf16[1,3,1024,512]{3,2,1,0:T(8,128)(2,1)} %left.3) | copy-start | bytes 9437188
  1.5 2.2 %copy-start.1 = (bf16[3,128,128]{2,1,0:T(8,128)(2,1)S(1)}, bf16[3,128,128]{2,1,0:T(8,128)(2,1)}, u32[]{:S(2)}) copy-start(bf16[3,128,128]{2,1,0:T(8,128)(2,1)} %right.3) | copy-start | bytes 294916
  1.5 2.2 %copy-start.2 = (s32[8]{0:T(128)S(1)}, s32[8]{0:T(128)}, u32[]{:S(2)}) copy-start(s32[8]{0:T(128)} %holders.9) | copy-start | bytes 100
  1.5 2.3 %copy-start.3 = (s32[8]{0:T(128)S(1)}, s32[8]{0:T(128)}, u32[]{:S(2)}) copy-start(s32[8]{0:T(128)} %widths.7) | copy-start | bytes 100
  5.3 8.0 %collective-permute-start = (bf16[2,32,512]{2,1,0:T(8,128)(2,1)S(1)}, bf16[2,32,512]{2,1,0:T(8,128)(2,1)S(1)}, u32[]{:S(2)}, u32[]{:S(2)}) collective-permute-start(bf16[2,32,512]{2,1,0:T(8,128)(2,1)S(1)} %get-tuple-element.30), channel_id=1, source_target_pairs={{0,8},{2,10},{4,12},{6,14},{8,0},{10,2},{12,4},{14,6},{1,9},{3,11}... | collective-permute-start | bytes 196616 | tf_op jit(solution)/shard_map/ppermute | solution.py:374
  9.4 6.4 %collective-permute-start.1 = (bf16[2,32,512]{2,1,0:T(8,128)(2,1)S(1)}, bf16[2,32,512]{2,1,0:T(8,128)(2,1)S(1)}, u32[]{:S(2)}, u32[]{:S(2)}) collective-permute-start(bf16[2,32,512]{2,1,0:T(8,128)(2,1)S(1)} %get-tuple-element.31), channel_id=1, source_target_pairs={{0,12},{2,14},{4,8},{6,10},{8,4},{10,6},{12,0},{14,2},{1,13},{3,15... | collective-permute-start | bytes 196616 | tf_op jit(solution)/shard_map/ppermute | solution.py:374
  10.7 5.2 %collective-permute-start.2 = (bf16[2,32,512]{2,1,0:T(8,128)(2,1)S(1)}, bf16[2,32,512]{2,1,0:T(8,128)(2,1)S(1)}, u32[]{:S(2)}, u32[]{:S(2)}) collective-permute-start(bf16[2,32,512]{2,1,0:T(8,128)(2,1)S(1)} %get-tuple-element.32), channel_id=1, source_target_pairs={{0,4},{2,6},{4,0},{6,2},{8,12},{10,14},{12,8},{14,10},{1,5},{3,7},... | collective-permute-start | bytes 196616 | tf_op jit(solution)/shard_map/ppermute | solution.py:374
  16.7 5.0 %collective-permute-start.3 = (bf16[4,32,512]{2,1,0:T(8,128)(2,1)S(1)}, bf16[4,32,512]{2,1,0:T(8,128)(2,1)S(1)}, u32[]{:S(2)}, u32[]{:S(2)}) collective-permute-start(bf16[4,32,512]{2,1,0:T(8,128)(2,1)S(1)} %get-tuple-element.36), channel_id=1, source_target_pairs={{0,2},{2,0},{4,6},{6,4},{8,10},{10,8},{12,14},{14,12},{1,3},{3,1},... | collective-permute-start | bytes 393224 | tf_op jit(solution)/shard_map/ppermute | solution.py:379
  21.7 5.7 %collective-permute-start.4 = (bf16[32,512]{1,0:T(8,128)(2,1)S(1)}, bf16[32,512]{1,0:T(8,128)(2,1)S(1)}, u32[]{:S(2)}, u32[]{:S(2)}) collective-permute-start(bf16[32,512]{1,0:T(8,128)(2,1)S(1)} %get-tuple-element.38), channel_id=1, source_target_pairs={{0,8},{2,10},{4,12},{6,14},{8,0},{10,2},{12,4},{14,6},{1,9},{3,11}... | collective-permute-start | bytes 98312 | tf_op jit(solution)/shard_map/ppermute | solution.py:374
  24.9 5.7 %collective-permute-start.5 = (bf16[32,512]{1,0:T(8,128)(2,1)S(1)}, bf16[32,512]{1,0:T(8,128)(2,1)S(1)}, u32[]{:S(2)}, u32[]{:S(2)}) collective-permute-start(bf16[32,512]{1,0:T(8,128)(2,1)S(1)} %get-tuple-element.39), channel_id=1, source_target_pairs={{0,12},{2,14},{4,8},{6,10},{8,4},{10,6},{12,0},{14,2},{1,13},{3,15... | collective-permute-start | bytes 98312 | tf_op jit(solution)/shard_map/ppermute | solution.py:374
  25.4 5.3 %collective-permute-start.6 = (bf16[32,512]{1,0:T(8,128)(2,1)S(1)}, bf16[32,512]{1,0:T(8,128)(2,1)S(1)}, u32[]{:S(2)}, u32[]{:S(2)}) collective-permute-start(bf16[32,512]{1,0:T(8,128)(2,1)S(1)} %get-tuple-element.40), channel_id=1, source_target_pairs={{0,4},{2,6},{4,0},{6,2},{8,12},{10,14},{12,8},{14,10},{1,5},{3,7},... | collective-permute-start | bytes 98312 | tf_op jit(solution)/shard_map/ppermute | solution.py:374
  34.5 7.7 %collective-permute-start.7 = (bf16[272,128]{1,0:T(8,128)(2,1)S(1)}, bf16[272,128]{1,0:T(8,128)(2,1)S(1)}, u32[]{:S(2)}, u32[]{:S(2)}) collective-permute-start(bf16[272,128]{1,0:T(8,128)(2,1)S(1)} %get-tuple-element.42), channel_id=1, source_target_pairs={{0,8},{2,10},{4,12},{6,14},{8,0},{10,2},{12,4},{14,6},{1,9},{3,11}... | collective-permute-start | bytes 208904 | tf_op jit(solution)/shard_map/ppermute | solution.py:374
  35.5 6.7 %collective-permute-start.8 = (bf16[272,128]{1,0:T(8,128)(2,1)S(1)}, bf16[272,128]{1,0:T(8,128)(2,1)S(1)}, u32[]{:S(2)}, u32[]{:S(2)}) collective-permute-start(bf16[272,128]{1,0:T(8,128)(2,1)S(1)} %get-tuple-element.43), channel_id=1, source_target_pairs={{0,12},{2,14},{4,8},{6,10},{8,4},{10,6},{12,0},{14,2},{1,13},{3,15... | collective-permute-start | bytes 208904 | tf_op jit(solution)/shard_map/ppermute | solution.py:374
  36.7 6.8 %collective-permute-start.9 = (bf16[272,128]{1,0:T(8,128)(2,1)S(1)}, bf16[272,128]{1,0:T(8,128)(2,1)S(1)}, u32[]{:S(2)}, u32[]{:S(2)}) collective-permute-start(bf16[272,128]{1,0:T(8,128)(2,1)S(1)} %get-tuple-element.44), channel_id=1, source_target_pairs={{0,4},{2,6},{4,0},{6,2},{8,12},{10,14},{12,8},{14,10},{1,5},{3,7},... | collective-permute-start | bytes 208904 | tf_op jit(solution)/shard_map/ppermute | solution.py:374
  44.5 5.5 %collective-permute-start.10 = (bf16[528,128]{1,0:T(8,128)(2,1)S(1)}, bf16[528,128]{1,0:T(8,128)(2,1)S(1)}, u32[]{:S(2)}, u32[]{:S(2)}) collective-permute-start(bf16[528,128]{1,0:T(8,128)(2,1)S(1)} %get-tuple-element.47), channel_id=1, source_target_pairs={{0,2},{2,0},{4,6},{6,4},{8,10},{10,8},{12,14},{14,12},{1,3},{3,1},... | collective-permute-start | bytes 405512 | tf_op jit(solution)/shard_map/ppermute | solution.py:379
  51.0 5.6 %collective-permute-start.11 = (bf16[32,512]{1,0:T(8,128)(2,1)S(1)}, bf16[32,512]{1,0:T(8,128)(2,1)S(1)}, u32[]{:S(2)}, u32[]{:S(2)}) collective-permute-start(bf16[32,512]{1,0:T(8,128)(2,1)S(1)} %get-tuple-element.51), channel_id=1, source_target_pairs={{0,8},{2,10},{4,12},{6,14},{8,0},{10,2},{12,4},{14,6},{1,9},{3,11}... | collective-permute-start | bytes 98312 | tf_op jit(solution)/shard_map/ppermute | solution.py:374
  52.7 5.7 %collective-permute-start.12 = (bf16[32,512]{1,0:T(8,128)(2,1)S(1)}, bf16[32,512]{1,0:T(8,128)(2,1)S(1)}, u32[]{:S(2)}, u32[]{:S(2)}) collective-permute-start(bf16[32,512]{1,0:T(8,128)(2,1)S(1)} %get-tuple-element.52), channel_id=1, source_target_pairs={{0,12},{2,14},{4,8},{6,10},{8,4},{10,6},{12,0},{14,2},{1,13},{3,15... | collective-permute-start | bytes 98312 | tf_op jit(solution)/shard_map/ppermute | solution.py:374
  54.1 4.3 %collective-permute-start.13 = (bf16[32,512]{1,0:T(8,128)(2,1)S(1)}, bf16[32,512]{1,0:T(8,128)(2,1)S(1)}, u32[]{:S(2)}, u32[]{:S(2)}) collective-permute-start(bf16[32,512]{1,0:T(8,128)(2,1)S(1)} %get-tuple-element.53), channel_id=1, source_target_pairs={{0,4},{2,6},{4,0},{6,2},{8,12},{10,14},{12,8},{14,10},{1,5},{3,7},... | collective-permute-start | bytes 98312 | tf_op jit(solution)/shard_map/ppermute | solution.py:374

commit v14 on v13

--- a/solution.py
+++ b/solution.py
@@ -115,10 +115,30 @@
 STEPS = (0, 2, 3, 1)
 
 
-def live_columns(widths, holders, half):
-    width = widths[holders[lax.axis_index("sec")]]
+def plan_kernel(widths, holders, plan, slot_of):
+    slots = holders.shape[0]
+    me = lax.axis_index("sec")
+    total = jnp.int32(0)
+    for s in range(slots):
+        slot_of[holders[s]] = jnp.int32(s)
+        total = total + widths[s]
+    codes = [jnp.int32(0), jnp.int32(0)]
+    for target in range(slots):
+        sector = holders[target]
+        has = (sector >= QDOWN, sector % QDOWN > 0)
+        source = (slot_of[sector & (QDOWN - 1)], slot_of[jnp.maximum(sector - 1, 0)])
+        for i in range(2):
+            entry = jnp.where(has[i], source[i] + slots, 0)
+            codes[i] = codes[i] | (entry << (target * 4))
+    row = lax.broadcasted_iota(jnp.int32, plan.shape, 0)
+    values = jnp.where(row == 0, widths[holders[me]], total)
+    values = jnp.where(row == 2, codes[0], values)
+    plan[...] = jnp.where(row == 3, codes[1], values)
+
+
+def live_columns(plan, half):
     first_column = lax.axis_index("env") * half
-    return first_column + lax.broadcasted_iota(jnp.int32, (1, half), 1) < width
+    return first_column + lax.broadcasted_iota(jnp.int32, (1, half), 1) < plan[0:1, 0:1]
 
 
 def apply_term(right, left, vector, term):
@@ -137,7 +157,10 @@
 def first_kernel(widths, holders, amps, right, left, *rest):
     *pieces, stay, start, block_vmem = rest
     half = stay.shape[1]
-    width = widths[holders[lax.axis_index("sec")]]
+    slot = lax.broadcasted_iota(jnp.int32, widths.shape, 1)
+    mine = jnp.where(slot == lax.axis_index("sec"), holders[...], 0)
+    sector = jnp.sum(mine, axis=1, keepdims=True)
+    width = jnp.sum(jnp.where(slot == sector, widths[...], 0), axis=1, keepdims=True)
     columns = lax.broadcasted_iota(jnp.int32, (1, half), 1)
     for h in range(2):
         live = h * half + columns < width
@@ -153,33 +176,26 @@
                 piece[term - 1] = block_vmem[own_place() ^ step]
 
 
-def fill_slots(holders, slot_of):
-    for s in range(holders.shape[0]):
-        slot_of[holders[s]] = jnp.int32(s)
-
-
-def sources_of(holders, slot_of, target):
-    sector = holders[target]
-    has = (sector >= QDOWN, sector % QDOWN > 0)
-    source = (slot_of[sector & (QDOWN - 1)], slot_of[jnp.maximum(sector - 1, 0)])
-    return has, source
-
-
-def line_targets(holders, slot_of):
+def line_targets(plan, places):
     line = lax.axis_index("sec") % LINES
-    for place in range(holders.shape[0] // LINES):
+    codes = [jnp.max(plan[2 + i : 3 + i, :]) for i in range(2)]
+    for place in range(places):
         for crossing in range(2):
-            has, source = sources_of(holders, slot_of, place * LINES + (line ^ crossing))
-            here = [has[i] & (source[i] % LINES == line) for i in range(2)]
+            target = place * LINES + (line ^ crossing)
+            entries = [(code >> (target * 4)) & (2 * LINES * places - 1) for code in codes]
+            source = [entry & (LINES * places - 1) for entry in entries]
+            here = [
+                (entry >= LINES * places) & (slot % LINES == line)
+                for entry, slot in zip(entries, source)
+            ]
             yield place, crossing, here, source
 
 
-def merge_kernel(holders, *rest):
-    *pieces, keep, cross, table, slot_of = rest
-    fill_slots(holders, slot_of)
+def merge_kernel(plan, *rest):
+    *pieces, keep, cross, table = rest
     for step, piece in zip(STEPS, pieces):
         table[own_place() ^ step] = piece[...]
-    for place, crossing, here, source in line_targets(holders, slot_of):
+    for place, crossing, here, source in line_targets(plan, keep.shape[0]):
         total = 0.0
         for i in range(2):
             block = table[source[i] // LINES, i].astype(jnp.float32)
@@ -198,9 +214,9 @@
     return pl.ds(pl.multiple_of((own_place() ^ step) * rows, rows), rows)
 
 
-def sum_kernel(widths, holders, stay, *rest):
+def sum_kernel(plan, stay, *rest):
     *pieces, first = rest
-    live = live_columns(widths, holders, stay.shape[1])
+    live = live_columns(plan, stay.shape[1])
     for step, piece in zip(STEPS, pieces):
         place = piece_rows(step, piece.shape[0])
         total = stay[place, :].astype(jnp.float32) + piece[...].astype(jnp.float32)
@@ -268,11 +284,10 @@
     return jnp.where(norm > 0, overlap / jnp.where(norm > 0, norm, 1.0), 0.0)
 
 
-def mix_kernel(holders, *rest):
-    keep, cross, tag_out, old, new, slot_of = rest[-6:]
+def mix_kernel(plan, *rest):
+    keep, cross, tag_out, old, new = rest[-5:]
     places, rows, half = keep.shape
     chunks = half // LANES
-    fill_slots(holders, slot_of)
     tag = jnp.zeros((TAG, LANES), jnp.float32)
     for i, step in enumerate(STEPS):
         old[own_place() ^ step] = rest[i][...]
@@ -284,7 +299,7 @@
     overlaps, norms, quotients, _ = read_tag(tag)
     shifts = quotients - line_quotient(overlaps, norms, lax.axis_index("sec") % LINES)
     lane = lax.broadcasted_iota(jnp.int32, (1, LANES), 1)
-    for place, crossing, here, source in line_targets(holders, slot_of):
+    for place, crossing, here, source in line_targets(plan, keep.shape[0]):
         total = 0.0
         for i in range(2):
             where = source[i] // LINES
@@ -304,16 +319,13 @@
             keep[place] = total
 
 
-def join_mixed_kernel(widths, tag_line, keep, arrived, old_keep, old_arrived, *rest):
+def join_mixed_kernel(plan, tag_line, keep, arrived, old_keep, old_arrived, *rest):
     *outs, factors = rest
     places, rows, half = keep.shape
     chunks = half // LANES
-    slots = widths.shape[0]
+    slots = places * LINES
     me = lax.axis_index("sec")
-    total = jnp.int32(0)
-    for slot in range(slots):
-        total = total + widths[slot]
-    live_count = places * rows * total.astype(jnp.float32)
+    live_count = places * rows * plan[1:2, 0:1].astype(jnp.float32)
     tag = tag_line[...].astype(jnp.float32)
     tag = tag + arrived[pl.ds(places * chunks * rows, TAG), :].astype(jnp.float32)
     overlaps, norms, quotients, rests = read_tag(tag)
@@ -339,10 +351,10 @@
         out[...] = (scale * block).astype(jnp.bfloat16)
 
 
-def final_kernel(widths, holders, factors, stay, stay_2, first, *rest):
+def final_kernel(plan, factors, stay, stay_2, first, *rest):
     *pieces, second, first_out = rest
     first_out[...] = first[...]
-    live = live_columns(widths, holders, stay.shape[1])
+    live = live_columns(plan, stay.shape[1])
     scale, shift = factors[0:1, 0:1], factors[1:2, 0:1]
     for step, piece in zip(STEPS, pieces):
         place = piece_rows(step, piece.shape[0])
@@ -399,24 +411,26 @@
     crossing = jax.ShapeDtypeStruct((places * chunked + TAG, LANES), jnp.bfloat16)
     label = jax.ShapeDtypeStruct((TAG, LANES), jnp.bfloat16)
     factor_shape = jax.ShapeDtypeStruct((8, LANES), jnp.float32)
-    slot_table = pltpu.SMEM((slots,), jnp.int32)
+    plan_shape = jax.ShapeDtypeStruct((8, LANES), jnp.int32)
     split = [pltpu.VMEM((places, rows, half), jnp.bfloat16)]
     tables = [pltpu.VMEM((places, *shape.shape), jnp.bfloat16) for shape in (pair, tagged)]
 
+    slot_table = [pltpu.SMEM((slots,), jnp.int32)]
+    plan = call(plan_kernel, [SMEM, SMEM], plan_shape, slot_table)(widths, holders)
     staged = call(stage_kernel, [VMEM], block, flops=4 << 30)(amplitudes[0])
     amps_full = lax.all_gather(staged, "env")
     both = jax.ShapeDtypeStruct(amps_full.shape, jnp.bfloat16)
     *pieces, stay, start_full = call(
-        first_kernel, [SMEM, SMEM] + [VMEM] * 3, (pair,) * places + (block, both), split, dots
-    )(widths, holders, amps_full, right_env, left_env)
+        first_kernel, [VMEM] * 5, (pair,) * places + (block, both), split, dots
+    )(widths[None], holders[None], amps_full, right_env, left_env)
     old = along_line(pieces, slots)
     old_keep, cross = call(
-        merge_kernel, [SMEM] + [VMEM] * places, (singles, singles), [tables[0], slot_table]
-    )(holders, *old)
+        merge_kernel, [VMEM] * (1 + places), (singles, singles), tables[:1]
+    )(plan, *old)
     old_arrived = across(cross, slots)
     joined = call(join_kernel, [VMEM, VMEM], (single,) * places)(old_keep, old_arrived)
-    first = call(sum_kernel, [SMEM, SMEM] + [VMEM] * (1 + places), block)(
-        widths, holders, stay, *along_line(joined, slots)
+    first = call(sum_kernel, [VMEM] * (2 + places), block)(
+        plan, stay, *along_line(joined, slots)
     )
 
     first_full = lax.all_gather(first, "env")
@@ -425,16 +439,13 @@
     )(start_full, first_full, right_env, left_env)
     new = along_line(pieces, slots)
     keep, cross, tag = call(
-        mix_kernel,
-        [SMEM] + [VMEM] * (2 * places),
-        (wides, crossing, label),
-        [*tables, slot_table],
-    )(holders, *old, *new)
+        mix_kernel, [VMEM] * (1 + 2 * places), (wides, crossing, label), tables
+    )(plan, *old, *new)
     *joined, factors = call(
-        join_mixed_kernel, [SMEM] + [VMEM] * 5, (single,) * places + (factor_shape,)
-    )(widths, tag, keep, across(cross, slots), old_keep, old_arrived)
-    second, first = call(final_kernel, [SMEM, SMEM] + [VMEM] * (4 + places), (block, block))(
-        widths, holders, factors, stay, stay_2, first, *along_line(joined, slots)
+        join_mixed_kernel, [VMEM] * 6, (single,) * places + (factor_shape,)
+    )(plan, tag, keep, across(cross, slots), old_keep, old_arrived)
+    second, first = call(final_kernel, [VMEM] * (5 + places), (block, block))(
+        plan, factors, stay, stay_2, first, *along_line(joined, slots)
     )
     return first[None], second[None]
 

time: 59.9 us -> 57 us (0.952)
  Pallas kernels: 7.36 us -> 5.1 us
  waiting for transfers between devices: 26.4 us -> 25.8 us
    pallas_call x6 -> x7, Pallas kernels: 6.07 us -> 3.82 us  [the longest x1 1.17 us: on_device(): call(first_kernel, [VMEM] * 5, (pair,) * places + (block, both), split, d...]
    ppermute x12, waiting for transfers between devices: 19.2 us -> 18.5 us  [along_line(): sent.append(lax.ppermute(piece, 'sec', pairs) if step else piece)]
  transfers between devices with their start and end apart: 14 -> 14, of which waited for: 11 -> 11; matrix products, arithmetic and copies ran while one was open for 0% -> 0% of each run, Pallas kernels for 0% -> 1%
where the time goes in v14:
time: 57 us; the launch traced here: 56.9 us
  waiting for transfers between devices  25.8 us (45%)
  starting transfers between devices  20.1 us (35%)
  Pallas kernels  5.1 us (9%)
  blocking collectives  4.21 us (7%)
  local copies, waits for them, and re-layouts  0.91 us (2%)
  between operations  0.72 us (1%)
    ppermute x12, waiting for transfers between devices, along_line(): sent.append(lax.ppermute(piece, 'sec', pairs) if step else piece)  18.5 us
    ppermute x12, starting transfers between devices, along_line(): sent.append(lax.ppermute(piece, 'sec', pairs) if step else piece)  16.8 us
    ppermute x2, waiting for transfers between devices, across(): lax.ppermute(piece, 'sec', [(slot, slot ^ 1) for slot in range(slots)])  7.27 us
    ppermute x2, starting transfers between devices, across(): lax.ppermute(piece, 'sec', [(slot, slot ^ 1) for slot in range(slots)])  3.29 us
    all_gather x1, blocking collectives, on_device(): amps_full = lax.all_gather(staged, 'env')  2.22 us
    all_gather x1, blocking collectives, on_device(): first_full = lax.all_gather(first, 'env')  1.99 us
    pallas_call x1, Pallas kernels, on_device(): call(second_kernel, [VMEM] * 4, (tagged,) * places + (wide,), split, dots)  1.24 us
    pallas_call x1, Pallas kernels, on_device(): call(first_kernel, [VMEM] * 5, (pair,) * places + (block, both), split, d...  1.17 us
  transfers between devices with their start and end apart: 14, of which 11 were waited for; matrix products, arithmetic and copies ran while one was open for 0% of the time, Pallas kernels for 1%

profile of v14, /device:TPU:0, one launch (start us, length us, event | category | flops | bytes accessed | tf_op | source)
XLA Modules:
  0.0 56.9 jit_solution(13558599669377491550)
XLA Ops:
  0.6 0.9 %copy-done.4 = bf16[1,128,512]{2,1,0:T(8,128)(2,1)S(1)} copy-done((bf16[1,128,512]{2,1,0:T(8,128)(2,1)S(1)}, bf16[1,128,512]{2,1,0:T(8,128)(2,1)}, u32[]{:S(2)}) %copy-start.4) | copy-done | bytes 131096
  1.6 2.2 %all-gather = bf16[256,512]{1,0:T(8,128)(2,1)S(1)} all-gather(bf16[128,512]{1,0:T(8,128)(2,1)S(1)} %shard_map.69), channel_id=2, replica_groups=mesh['runs'=2,'sec'=8,'env'=2] {'env'}, dimensions={0}, use_global_device_ids=true | all-gather | bytes 393216 | tf_op jit(solution)/shard_map/all_gather | solution.py:421
  3.8 1.2 %shard_map.70 = (bf16[2,32,512]{2,1,0:T(8,128)(2,1)S(1)}, bf16[2,32,512]{2,1,0:T(8,128)(2,1)S(1)}, bf16[2,32,512]{2,1,0:T(8,128)(2,1)S(1)}, bf16[2,32,512]{2,1,0...) custom-call(s32[1,8]{1,0:T(1,128)S(1)} %bitcast.9, s32[1,8]{1,0:T(1,128)S(1)} %bitcast.10, ...), custom_call_target="tpu_custom_call" | custom-call | flops 452984832 | bytes 262144 | tf_op jit(solution)/shard_map/pallas_call | solution.py:423
  5.0 4.0 %collective-permute-start = (bf16[2,32,512]{2,1,0:T(8,128)(2,1)S(1)}, bf16[2,32,512]{2,1,0:T(8,128)(2,1)S(1)}, u32[]{:S(2)}, u32[]{:S(2)}) collective-permute-start(bf16[2,32,512]{2,1,0:T(8,128)(2,1)S(1)} %get-tuple-element.30), channel_id=1, source_target_pairs={{0,8},{2,10},{4,12},{6,14},{8,0},{10,2},{12,4},{14,6},{1,9},{3,11}... | collective-permute-start | bytes 196616 | tf_op jit(solution)/shard_map/ppermute | solution.py:386
  9.0 1.3 %collective-permute-start.1 = (bf16[2,32,512]{2,1,0:T(8,128)(2,1)S(1)}, bf16[2,32,512]{2,1,0:T(8,128)(2,1)S(1)}, u32[]{:S(2)}, u32[]{:S(2)}) collective-permute-start(bf16[2,32,512]{2,1,0:T(8,128)(2,1)S(1)} %get-tuple-element.31), channel_id=1, source_target_pairs={{0,12},{2,14},{4,8},{6,10},{8,4},{10,6},{12,0},{14,2},{1,13},{3,15... | collective-permute-start | bytes 196616 | tf_op jit(solution)/shard_map/ppermute | solution.py:386
  10.6 0.6 %shard_map.68.plan = s32[8,128]{1,0:T(8,128)S(1)} custom-call(s32[8]{0:T(128)S(1)} %copy-done.2, s32[8]{0:T(128)S(1)} %copy-done.3), custom_call_target="tpu_custom_call" | custom-call | bytes 262144 | tf_op jit(solution)/shard_map/pallas_call | solution.py:419
  11.2 1.7 %collective-permute-done.rest_1_ = bf16[2,32,512]{2,1,0:T(8,128)(2,1)S(1)} collective-permute-done((bf16[2,32,512]{2,1,0:T(8,128)(2,1)S(1)}, bf16[2,32,512]{2,1,0:T(8,128)(2,1)S(1)}, u32[]{:S(2)}, u32[]{:S(2)}) %collective-permute-start) | collective-permute-done | bytes 65568 | tf_op jit(solution)/shard_map/ppermute | solution.py:386
  12.9 2.5 %collective-permute-done.1.rest_2_ = bf16[2,32,512]{2,1,0:T(8,128)(2,1)S(1)} collective-permute-done((bf16[2,32,512]{2,1,0:T(8,128)(2,1)S(1)}, bf16[2,32,512]{2,1,0:T(8,128)(2,1)S(1)}, u32[]{:S(2)}, u32[]{:S(2)}) %collective-permute-start.1) | collective-permute-done | bytes 65568 | tf_op jit(solution)/shard_map/ppermute | solution.py:386
  15.9 1.7 %collective-permute-start.3 = (bf16[4,32,512]{2,1,0:T(8,128)(2,1)S(1)}, bf16[4,32,512]{2,1,0:T(8,128)(2,1)S(1)}, u32[]{:S(2)}, u32[]{:S(2)}) collective-permute-start(bf16[4,32,512]{2,1,0:T(8,128)(2,1)S(1)} %get-tuple-element.36), channel_id=1, source_target_pairs={{0,2},{2,0},{4,6},{6,4},{8,10},{10,8},{12,14},{14,12},{1,3},{3,1},... | collective-permute-start | bytes 393224 | tf_op jit(solution)/shard_map/ppermute | solution.py:391
  17.6 3.3 %collective-permute-done.3.arrived.old_arrived = bf16[4,32,512]{2,1,0:T(8,128)(2,1)S(1)} collective-permute-done((bf16[4,32,512]{2,1,0:T(8,128)(2,1)S(1)}, bf16[4,32,512]{2,1,0:T(8,128)(2,1)S(1)}, u32[]{:S(2)}, u32[]{:S(2)}) %collective-permute-start.3) | collective-permute-done | bytes 131104 | tf_op jit(solution)/shard_map/ppermute | solution.py:391
  20.9 3.2 %collective-permute-start.4 = (bf16[32,512]{1,0:T(8,128)(2,1)S(1)}, bf16[32,512]{1,0:T(8,128)(2,1)S(1)}, u32[]{:S(2)}, u32[]{:S(2)}) collective-permute-start(bf16[32,512]{1,0:T(8,128)(2,1)S(1)} %get-tuple-element.38), channel_id=1, source_target_pairs={{0,8},{2,10},{4,12},{6,14},{8,0},{10,2},{12,4},{14,6},{1,9},{3,11}... | collective-permute-start | bytes 98312 | tf_op jit(solution)/shard_map/ppermute | solution.py:386
  24.2 0.4 collective-permute-start.5
  24.6 0.4 collective-permute-start.6
  25.1 1.6 %collective-permute-done.4.rest_1_ = bf16[32,512]{1,0:T(8,128)(2,1)S(1)} collective-permute-done((bf16[32,512]{1,0:T(8,128)(2,1)S(1)}, bf16[32,512]{1,0:T(8,128)(2,1)S(1)}, u32[]{:S(2)}, u32[]{:S(2)}) %collective-permute-start.4) | collective-permute-done | bytes 32800 | tf_op jit(solution)/shard_map/ppermute | solution.py:386
  26.7 3.2 %collective-permute-done.5.rest_2_ = bf16[32,512]{1,0:T(8,128)(2,1)S(1)} collective-permute-done((bf16[32,512]{1,0:T(8,128)(2,1)S(1)}, bf16[32,512]{1,0:T(8,128)(2,1)S(1)}, u32[]{:S(2)}, u32[]{:S(2)}) %collective-permute-start.5) | collective-permute-done | bytes 32800 | tf_op jit(solution)/shard_map/ppermute | solution.py:386
  30.0 2.0 %all-gather.1 = bf16[256,512]{1,0:T(8,128)(2,1)S(1)} all-gather(bf16[128,512]{1,0:T(8,128)(2,1)S(1)} %shard_map.73.first), channel_id=3, replica_groups=mesh['runs'=2,'sec'=8,'env'=2] {'env'}, dimensions={0}, use_global_device_ids=true | all-gather | bytes 393216 | tf_op jit(solution)/shard_map/all_gather | solution.py:436
  32.0 1.2 %shard_map.74 = (bf16[272,128]{1,0:T(8,128)(2,1)S(1)}, bf16[272,128]{1,0:T(8,128)(2,1)S(1)}, bf16[272,128]{1,0:T(8,128)(2,1)S(1)}, bf16[272,128]{1,0:T(8,128)(2,1)S(1)}, f32[128,512]{1,0:T(8,128)S(1)}) custom-call(bf16[2,128,512]{2,1,0:T(8,128)(2,1)S(1)} %get-tuple-element.33.start, bf16[2,128,512]{2,1,0:T(8,128)(2,1)S(1)} %bitcast.7, ...), custom_call_target="tpu_custom_call" | custom-call | flops 452984832 | bytes 262144 | tf_op jit(solution)/shard_map/pallas_call | solution.py:437
  33.2 1.0 %collective-permute-start.7 = (bf16[272,128]{1,0:T(8,128)(2,1)S(1)}, bf16[272,128]{1,0:T(8,128)(2,1)S(1)}, u32[]{:S(2)}, u32[]{:S(2)}) collective-permute-start(bf16[272,128]{1,0:T(8,128)(2,1)S(1)} %get-tuple-element.42), channel_id=1, source_target_pairs={{0,8},{2,10},{4,12},{6,14},{8,0},{10,2},{12,4},{14,6},{1,9},{3,11}... | collective-permute-start | bytes 208904 | tf_op jit(solution)/shard_map/ppermute | solution.py:386
  34.2 1.2 %collective-permute-start.8 = (bf16[272,128]{1,0:T(8,128)(2,1)S(1)}, bf16[272,128]{1,0:T(8,128)(2,1)S(1)}, u32[]{:S(2)}, u32[]{:S(2)}) collective-permute-start(bf16[272,128]{1,0:T(8,128)(2,1)S(1)} %get-tuple-element.43), channel_id=1, source_target_pairs={{0,12},{2,14},{4,8},{6,10},{8,4},{10,6},{12,0},{14,2},{1,13},{3,15... | collective-permute-start | bytes 208904 | tf_op jit(solution)/shard_map/ppermute | solution.py:386
  35.4 1.4 %collective-permute-start.9 = (bf16[272,128]{1,0:T(8,128)(2,1)S(1)}, bf16[272,128]{1,0:T(8,128)(2,1)S(1)}, u32[]{:S(2)}, u32[]{:S(2)}) collective-permute-start(bf16[272,128]{1,0:T(8,128)(2,1)S(1)} %get-tuple-element.44), channel_id=1, source_target_pairs={{0,4},{2,6},{4,0},{6,2},{8,12},{10,14},{12,8},{14,10},{1,5},{3,7},... | collective-permute-start | bytes 208904 | tf_op jit(solution)/shard_map/ppermute | solution.py:386
  36.8 4.1 %collective-permute-done.7.rest_5_ = bf16[272,128]{1,0:T(8,128)(2,1)S(1)} collective-permute-done((bf16[272,128]{1,0:T(8,128)(2,1)S(1)}, bf16[272,128]{1,0:T(8,128)(2,1)S(1)}, u32[]{:S(2)}, u32[]{:S(2)}) %collective-permute-start.7) | collective-permute-done | bytes 69664 | tf_op jit(solution)/shard_map/ppermute | solution.py:386
  40.9 1.3 %collective-permute-done.9.rest_7_ = bf16[272,128]{1,0:T(8,128)(2,1)S(1)} collective-permute-done((bf16[272,128]{1,0:T(8,128)(2,1)S(1)}, bf16[272,128]{1,0:T(8,128)(2,1)S(1)}, u32[]{:S(2)}, u32[]{:S(2)}) %collective-permute-start.9) | collective-permute-done | bytes 69664 | tf_op jit(solution)/shard_map/ppermute | solution.py:386
  42.2 0.5 shard_map.75
  42.7 1.6 %collective-permute-start.10 = (bf16[528,128]{1,0:T(8,128)(2,1)S(1)}, bf16[528,128]{1,0:T(8,128)(2,1)S(1)}, u32[]{:S(2)}, u32[]{:S(2)}) collective-permute-start(bf16[528,128]{1,0:T(8,128)(2,1)S(1)} %get-tuple-element.47), channel_id=1, source_target_pairs={{0,2},{2,0},{4,6},{6,4},{8,10},{10,8},{12,14},{14,12},{1,3},{3,1},... | collective-permute-start | bytes 405512 | tf_op jit(solution)/shard_map/ppermute | solution.py:391
  44.3 4.0 %collective-permute-done.10.arrived = bf16[528,128]{1,0:T(8,128)(2,1)S(1)} collective-permute-done((bf16[528,128]{1,0:T(8,128)(2,1)S(1)}, bf16[528,128]{1,0:T(8,128)(2,1)S(1)}, u32[]{:S(2)}, u32[]{:S(2)}) %collective-permute-start.10) | collective-permute-done | bytes 135200 | tf_op jit(solution)/shard_map/ppermute | solution.py:391
  48.3 0.4 shard_map.76
  48.6 1.7 %collective-permute-start.11 = (bf16[32,512]{1,0:T(8,128)(2,1)S(1)}, bf16[32,512]{1,0:T(8,128)(2,1)S(1)}, u32[]{:S(2)}, u32[]{:S(2)}) collective-permute-start(bf16[32,512]{1,0:T(8,128)(2,1)S(1)} %get-tuple-element.51), channel_id=1, source_target_pairs={{0,8},{2,10},{4,12},{6,14},{8,0},{10,2},{12,4},{14,6},{1,9},{3,11}... | collective-permute-start | bytes 98312 | tf_op jit(solution)/shard_map/ppermute | solution.py:386
  50.4 1.4 %collective-permute-start.12 = (bf16[32,512]{1,0:T(8,128)(2,1)S(1)}, bf16[32,512]{1,0:T(8,128)(2,1)S(1)}, u32[]{:S(2)}, u32[]{:S(2)}) collective-permute-start(bf16[32,512]{1,0:T(8,128)(2,1)S(1)} %get-tuple-element.52), channel_id=1, source_target_pairs={{0,12},{2,14},{4,8},{6,10},{8,4},{10,6},{12,0},{14,2},{1,13},{3,15... | collective-permute-start | bytes 98312 | tf_op jit(solution)/shard_map/ppermute | solution.py:386
  51.8 0.4 collective-permute-start.13
  52.2 2.0 %collective-permute-done.11.rest_1_ = bf16[32,512]{1,0:T(8,128)(2,1)S(1)} collective-permute-done((bf16[32,512]{1,0:T(8,128)(2,1)S(1)}, bf16[32,512]{1,0:T(8,128)(2,1)S(1)}, u32[]{:S(2)}, u32[]{:S(2)}) %collective-permute-start.11) | collective-permute-done | bytes 32800 | tf_op jit(solution)/shard_map/ppermute | solution.py:386
  54.2 1.9 %collective-permute-done.12.rest_2_ = bf16[32,512]{1,0:T(8,128)(2,1)S(1)} collective-permute-done((bf16[32,512]{1,0:T(8,128)(2,1)S(1)}, bf16[32,512]{1,0:T(8,128)(2,1)S(1)}, u32[]{:S(2)}, u32[]{:S(2)}) %collective-permute-start.12) | collective-permute-done | bytes 32800 | tf_op jit(solution)/shard_map/ppermute | solution.py:386
  56.1 0.8 %shard_map.77 = (bf16[128,512]{1,0:T(8,128)(2,1)}, bf16[128,512]{1,0:T(8,128)(2,1)}) custom-call(s32[8,128]{1,0:T(8,128)S(1)} %shard_map.68.plan, f32[8,128]{1,0:T(8,128)S(1)} %get-tuple-element.48.factors, bf16[128,512]{1,0:T(8,128)(2,1)S(1)} %get-tuple-element.34.stay, f32[128,512]{1,0:T(8,128)S(1)} %get-tuple-element.49.stay_2, ...), custom_call_target="tpu_custom_call" | custom-call | bytes 262144 | tf_op jit(solution)/shard_map/pallas_call | solution.py:447
  (18 shorter events, 0.9 us)
Async XLA Ops:
  0.6 0.9 %copy-start.4 = (bf16[1,128,512]{2,1,0:T(8,128)(2,1)S(1)}, bf16[1,128,512]{2,1,0:T(8,128)(2,1)}, u32[]{:S(2)}) copy-start(bf16[1,128,512]{2,1,0:T(8,128)(2,1)} %param.5) | copy-start | bytes 393220
  1.5 2.2 %copy-start = (bf16[1,3,1024,512]{3,2,1,0:T(8,128)(2,1)S(1)}, bf16[1,3,1024,512]{3,2,1,0:T(8,128)(2,1)}, u32[]{:S(2)}) copy-start(bf16[1,3,1024,512]{3,2,1,0:T(8,128)(2,1)} %left.3) | copy-start | bytes 9437188
  1.5 2.2 %copy-start.1 = (bf16[3,128,128]{2,1,0:T(8,128)(2,1)S(1)}, bf16[3,128,128]{2,1,0:T(8,128)(2,1)}, u32[]{:S(2)}) copy-start(bf16[3,128,128]{2,1,0:T(8,128)(2,1)} %right.3) | copy-start | bytes 294916
  1.5 2.2 %copy-start.2 = (s32[8]{0:T(128)S(1)}, s32[8]{0:T(128)}, u32[]{:S(2)}) copy-start(s32[8]{0:T(128)} %widths.1) | copy-start | bytes 100
  1.5 2.3 %copy-start.3 = (s32[8]{0:T(128)S(1)}, s32[8]{0:T(128)}, u32[]{:S(2)}) copy-start(s32[8]{0:T(128)} %holders.1) | copy-start | bytes 100
  5.0 8.0 %collective-permute-start = (bf16[2,32,512]{2,1,0:T(8,128)(2,1)S(1)}, bf16[2,32,512]{2,1,0:T(8,128)(2,1)S(1)}, u32[]{:S(2)}, u32[]{:S(2)}) collective-permute-start(bf16[2,32,512]{2,1,0:T(8,128)(2,1)S(1)} %get-tuple-element.30), channel_id=1, source_target_pairs={{0,8},{2,10},{4,12},{6,14},{8,0},{10,2},{12,4},{14,6},{1,9},{3,11}... | collective-permute-start | bytes 196616 | tf_op jit(solution)/shard_map/ppermute | solution.py:386
  9.0 6.4 %collective-permute-start.1 = (bf16[2,32,512]{2,1,0:T(8,128)(2,1)S(1)}, bf16[2,32,512]{2,1,0:T(8,128)(2,1)S(1)}, u32[]{:S(2)}, u32[]{:S(2)}) collective-permute-start(bf16[2,32,512]{2,1,0:T(8,128)(2,1)S(1)} %get-tuple-element.31), channel_id=1, source_target_pairs={{0,12},{2,14},{4,8},{6,10},{8,4},{10,6},{12,0},{14,2},{1,13},{3,15... | collective-permute-start | bytes 196616 | tf_op jit(solution)/shard_map/ppermute | solution.py:386
  10.3 5.2 %collective-permute-start.2 = (bf16[2,32,512]{2,1,0:T(8,128)(2,1)S(1)}, bf16[2,32,512]{2,1,0:T(8,128)(2,1)S(1)}, u32[]{:S(2)}, u32[]{:S(2)}) collective-permute-start(bf16[2,32,512]{2,1,0:T(8,128)(2,1)S(1)} %get-tuple-element.32), channel_id=1, source_target_pairs={{0,4},{2,6},{4,0},{6,2},{8,12},{10,14},{12,8},{14,10},{1,5},{3,7},... | collective-permute-start | bytes 196616 | tf_op jit(solution)/shard_map/ppermute | solution.py:386
  15.9 5.0 %collective-permute-start.3 = (bf16[4,32,512]{2,1,0:T(8,128)(2,1)S(1)}, bf16[4,32,512]{2,1,0:T(8,128)(2,1)S(1)}, u32[]{:S(2)}, u32[]{:S(2)}) collective-permute-start(bf16[4,32,512]{2,1,0:T(8,128)(2,1)S(1)} %get-tuple-element.36), channel_id=1, source_target_pairs={{0,2},{2,0},{4,6},{6,4},{8,10},{10,8},{12,14},{14,12},{1,3},{3,1},... | collective-permute-start | bytes 393224 | tf_op jit(solution)/shard_map/ppermute | solution.py:391
  20.9 5.7 %collective-permute-start.4 = (bf16[32,512]{1,0:T(8,128)(2,1)S(1)}, bf16[32,512]{1,0:T(8,128)(2,1)S(1)}, u32[]{:S(2)}, u32[]{:S(2)}) collective-permute-start(bf16[32,512]{1,0:T(8,128)(2,1)S(1)} %get-tuple-element.38), channel_id=1, source_target_pairs={{0,8},{2,10},{4,12},{6,14},{8,0},{10,2},{12,4},{14,6},{1,9},{3,11}... | collective-permute-start | bytes 98312 | tf_op jit(solution)/shard_map/ppermute | solution.py:386
  24.2 5.7 %collective-permute-start.5 = (bf16[32,512]{1,0:T(8,128)(2,1)S(1)}, bf16[32,512]{1,0:T(8,128)(2,1)S(1)}, u32[]{:S(2)}, u32[]{:S(2)}) collective-permute-start(bf16[32,512]{1,0:T(8,128)(2,1)S(1)} %get-tuple-element.39), channel_id=1, source_target_pairs={{0,12},{2,14},{4,8},{6,10},{8,4},{10,6},{12,0},{14,2},{1,13},{3,15... | collective-permute-start | bytes 98312 | tf_op jit(solution)/shard_map/ppermute | solution.py:386
  24.6 5.3 %collective-permute-start.6 = (bf16[32,512]{1,0:T(8,128)(2,1)S(1)}, bf16[32,512]{1,0:T(8,128)(2,1)S(1)}, u32[]{:S(2)}, u32[]{:S(2)}) collective-permute-start(bf16[32,512]{1,0:T(8,128)(2,1)S(1)} %get-tuple-element.40), channel_id=1, source_target_pairs={{0,4},{2,6},{4,0},{6,2},{8,12},{10,14},{12,8},{14,10},{1,5},{3,7},... | collective-permute-start | bytes 98312 | tf_op jit(solution)/shard_map/ppermute | solution.py:386
  33.2 7.7 %collective-permute-start.7 = (bf16[272,128]{1,0:T(8,128)(2,1)S(1)}, bf16[272,128]{1,0:T(8,128)(2,1)S(1)}, u32[]{:S(2)}, u32[]{:S(2)}) collective-permute-start(bf16[272,128]{1,0:T(8,128)(2,1)S(1)} %get-tuple-element.42), channel_id=1, source_target_pairs={{0,8},{2,10},{4,12},{6,14},{8,0},{10,2},{12,4},{14,6},{1,9},{3,11}... | collective-permute-start | bytes 208904 | tf_op jit(solution)/shard_map/ppermute | solution.py:386
  34.2 6.7 %collective-permute-start.8 = (bf16[272,128]{1,0:T(8,128)(2,1)S(1)}, bf16[272,128]{1,0:T(8,128)(2,1)S(1)}, u32[]{:S(2)}, u32[]{:S(2)}) collective-permute-start(bf16[272,128]{1,0:T(8,128)(2,1)S(1)} %get-tuple-element.43), channel_id=1, source_target_pairs={{0,12},{2,14},{4,8},{6,10},{8,4},{10,6},{12,0},{14,2},{1,13},{3,15... | collective-permute-start | bytes 208904 | tf_op jit(solution)/shard_map/ppermute | solution.py:386
  35.4 6.8 %collective-permute-start.9 = (bf16[272,128]{1,0:T(8,128)(2,1)S(1)}, bf16[272,128]{1,0:T(8,128)(2,1)S(1)}, u32[]{:S(2)}, u32[]{:S(2)}) collective-permute-start(bf16[272,128]{1,0:T(8,128)(2,1)S(1)} %get-tuple-element.44), channel_id=1, source_target_pairs={{0,4},{2,6},{4,0},{6,2},{8,12},{10,14},{12,8},{14,10},{1,5},{3,7},... | collective-permute-start | bytes 208904 | tf_op jit(solution)/shard_map/ppermute | solution.py:386
  42.7 5.5 %collective-permute-start.10 = (bf16[528,128]{1,0:T(8,128)(2,1)S(1)}, bf16[528,128]{1,0:T(8,128)(2,1)S(1)}, u32[]{:S(2)}, u32[]{:S(2)}) collective-permute-start(bf16[528,128]{1,0:T(8,128)(2,1)S(1)} %get-tuple-element.47), channel_id=1, source_target_pairs={{0,2},{2,0},{4,6},{6,4},{8,10},{10,8},{12,14},{14,12},{1,3},{3,1},... | collective-permute-start | bytes 405512 | tf_op jit(solution)/shard_map/ppermute | solution.py:391
  48.6 5.6 %collective-permute-start.11 = (bf16[32,512]{1,0:T(8,128)(2,1)S(1)}, bf16[32,512]{1,0:T(8,128)(2,1)S(1)}, u32[]{:S(2)}, u32[]{:S(2)}) collective-permute-start(bf16[32,512]{1,0:T(8,128)(2,1)S(1)} %get-tuple-element.51), channel_id=1, source_target_pairs={{0,8},{2,10},{4,12},{6,14},{8,0},{10,2},{12,4},{14,6},{1,9},{3,11}... | collective-permute-start | bytes 98312 | tf_op jit(solution)/shard_map/ppermute | solution.py:386
  50.4 5.7 %collective-permute-start.12 = (bf16[32,512]{1,0:T(8,128)(2,1)S(1)}, bf16[32,512]{1,0:T(8,128)(2,1)S(1)}, u32[]{:S(2)}, u32[]{:S(2)}) collective-permute-start(bf16[32,512]{1,0:T(8,128)(2,1)S(1)} %get-tuple-element.52), channel_id=1, source_target_pairs={{0,12},{2,14},{4,8},{6,10},{8,4},{10,6},{12,0},{14,2},{1,13},{3,15... | collective-permute-start | bytes 98312 | tf_op jit(solution)/shard_map/ppermute | solution.py:386
  51.8 4.3 %collective-permute-start.13 = (bf16[32,512]{1,0:T(8,128)(2,1)S(1)}, bf16[32,512]{1,0:T(8,128)(2,1)S(1)}, u32[]{:S(2)}, u32[]{:S(2)}) collective-permute-start(bf16[32,512]{1,0:T(8,128)(2,1)S(1)} %get-tuple-element.53), channel_id=1, source_target_pairs={{0,4},{2,6},{4,0},{6,2},{8,12},{10,14},{12,8},{14,10},{1,5},{3,7},... | collective-permute-start | bytes 98312 | tf_op jit(solution)/shard_map/ppermute | solution.py:386

commit v15 on v14

--- a/solution.py
+++ b/solution.py
@@ -146,15 +146,16 @@
     return jnp.dot(products.astype(jnp.bfloat16), left, preferred_element_type=jnp.float32)
 
 
-def stage_kernel(amps, staged):
-    staged[...] = amps[...]
+def in_order(own, other):
+    upper = lax.axis_index("env") > 0
+    return [jnp.where(upper, other, own), jnp.where(upper, own, other)]
 
 
 def own_place():
     return lax.axis_index("sec") // LINES
 
 
-def first_kernel(widths, holders, amps, right, left, *rest):
+def first_kernel(widths, holders, own, other, right, left, *rest):
     *pieces, stay, start, block_vmem = rest
     half = stay.shape[1]
     slot = lax.broadcasted_iota(jnp.int32, widths.shape, 1)
@@ -162,9 +163,9 @@
     sector = jnp.sum(mine, axis=1, keepdims=True)
     width = jnp.sum(jnp.where(slot == sector, widths[...], 0), axis=1, keepdims=True)
     columns = lax.broadcasted_iota(jnp.int32, (1, half), 1)
-    for h in range(2):
+    for h, part in enumerate(in_order(own[...], other[...])):
         live = h * half + columns < width
-        start[h] = jnp.where(live, amps[h], jnp.zeros_like(amps[h]))
+        start[h] = jnp.where(live, part, jnp.zeros_like(part))
     vector = jnp.concatenate([start[0], start[1]], axis=1)
     for term in (1, 2, 0):
         block = apply_term(right, left[0, term], vector, term).astype(jnp.bfloat16)
@@ -240,13 +241,13 @@
     return jnp.where((lane == me) & (row < 3 * len(values)), parts, 0.0).astype(jnp.bfloat16)
 
 
-def second_kernel(start, first, right, left, *rest):
+def second_kernel(start, own, other, right, left, *rest):
     *pieces, stay, block_vmem = rest
     half = stay.shape[1]
     rows = block_vmem.shape[1]
     chunks = half // LANES
     basis = [start[h].astype(jnp.float32) for h in range(2)]
-    firsts = [first[h].astype(jnp.float32) for h in range(2)]
+    firsts = [part.astype(jnp.float32) for part in in_order(own[...], other[...])]
     overlap = total_of(basis[0] * firsts[0]) + total_of(basis[1] * firsts[1])
     norm = total_of(basis[0] * basis[0]) + total_of(basis[1] * basis[1])
     quotient = jnp.where(norm > 0, overlap / jnp.where(norm > 0, norm, 1.0), 0.0)
@@ -387,6 +388,10 @@
     return sent
 
 
+def other_core(block):
+    return lax.ppermute(block, "env", [(0, 1), (1, 0)])
+
+
 def across(piece, slots):
     return lax.ppermute(piece, "sec", [(slot, slot ^ 1) for slot in range(slots)])
 
@@ -417,12 +422,10 @@
 
     slot_table = [pltpu.SMEM((slots,), jnp.int32)]
     plan = call(plan_kernel, [SMEM, SMEM], plan_shape, slot_table)(widths, holders)
-    staged = call(stage_kernel, [VMEM], block, flops=4 << 30)(amplitudes[0])
-    amps_full = lax.all_gather(staged, "env")
-    both = jax.ShapeDtypeStruct(amps_full.shape, jnp.bfloat16)
+    both = jax.ShapeDtypeStruct((2, right_dim, half), jnp.bfloat16)
     *pieces, stay, start_full = call(
-        first_kernel, [VMEM] * 5, (pair,) * places + (block, both), split, dots
-    )(widths[None], holders[None], amps_full, right_env, left_env)
+        first_kernel, [VMEM] * 6, (pair,) * places + (block, both), split, dots
+    )(widths[None], holders[None], amplitudes[0], other_core(amplitudes[0]), right_env, left_env)
     old = along_line(pieces, slots)
     old_keep, cross = call(
         merge_kernel, [VMEM] * (1 + places), (singles, singles), tables[:1]
@@ -433,10 +436,9 @@
         plan, stay, *along_line(joined, slots)
     )
 
-    first_full = lax.all_gather(first, "env")
     *pieces, stay_2 = call(
-        second_kernel, [VMEM] * 4, (tagged,) * places + (wide,), split, dots
-    )(start_full, first_full, right_env, left_env)
+        second_kernel, [VMEM] * 5, (tagged,) * places + (wide,), split, dots
+    )(start_full, first, other_core(first), right_env, left_env)
     new = along_line(pieces, slots)
     keep, cross, tag = call(
         mix_kernel, [VMEM] * (1 + 2 * places), (wides, crossing, label), tables

time: 57 us -> 60 us (1.053)
  blocking collectives: 4.21 us -> 0 us
  local copies, waits for them, and re-layouts: 0.91 us -> 5 us
  waiting for transfers between devices: 25.8 us -> 28.3 us
    all_gather x2 -> x0, blocking collectives: 4.21 us -> none  [the longest x1 2.22 us: on_device(): amps_full = lax.all_gather(staged, 'env')]
    unnamed x10 -> x14, local copies, waits for them, and re-layouts: 0.91 us -> 5 us
    ppermute x0 -> x2, waiting for transfers between devices: none -> 2.53 us  [other_core(): return lax.ppermute(block, 'env', [(0, 1), (1, 0)])]
    pallas_call x3 -> x2, Pallas kernels: 2.41 us -> 2.39 us  [the longest x1 1.22 us: on_device(): call(second_kernel, [VMEM] * 5, (tagged,) * places + (wide,), split, dots)]
  transfers between devices with their start and end apart: 14 -> 16, of which waited for: 11 -> 13; matrix products, arithmetic and copies ran while one was open for 0% -> 0% of each run, Pallas kernels for 1% -> 1%
where the time goes in v15:
time: 60 us; the launch traced here: 59.8 us
  waiting for transfers between devices  28.3 us (47%)
  starting transfers between devices  20.7 us (34%)
  Pallas kernels  5.08 us (8%)
  local copies, waits for them, and re-layouts  5 us (8%)
  between operations  0.71 us (1%)
    ppermute x12, waiting for transfers between devices, along_line(): sent.append(lax.ppermute(piece, 'sec', pairs) if step else piece)  18.5 us
    ppermute x12, starting transfers between devices, along_line(): sent.append(lax.ppermute(piece, 'sec', pairs) if step else piece)  16.9 us
    ppermute x2, waiting for transfers between devices, across(): lax.ppermute(piece, 'sec', [(slot, slot ^ 1) for slot in range(slots)])  7.27 us
    unnamed x14, local copies, waits for them, and re-layouts  5 us
    ppermute x2, starting transfers between devices, across(): lax.ppermute(piece, 'sec', [(slot, slot ^ 1) for slot in range(slots)])  3.29 us
    ppermute x2, waiting for transfers between devices, other_core(): return lax.ppermute(block, 'env', [(0, 1), (1, 0)])  2.53 us
    pallas_call x1, Pallas kernels, on_device(): call(second_kernel, [VMEM] * 5, (tagged,) * places + (wide,), split, dots)  1.22 us
  transfers between devices with their start and end apart: 16, of which 13 were waited for; matrix products, arithmetic and copies ran while one was open for 0% of the time, Pallas kernels for 1%

profile of v15, /device:TPU:0, one launch (start us, length us, event | category | flops | bytes accessed | tf_op | source)
XLA Modules:
  0.0 59.8 jit_solution(5755081429111767666)
XLA Ops:
  0.6 0.5 collective-permute-start
  1.1 1.2 %collective-permute-done.other = bf16[128,512]{1,0:T(8,128)(2,1)S(1)} collective-permute-done((bf16[128,512]{1,0:T(8,128)(2,1)}, bf16[128,512]{1,0:T(8,128)(2,1)S(1)}, u32[]{:S(2)}, u32[]{:S(2)}) %collective-permute-start) | collective-permute-done | bytes 131104 | tf_op jit(solution)/shard_map/ppermute | solution.py:392
  2.3 1.9 %copy-done = bf16[1,3,1024,512]{3,2,1,0:T(8,128)(2,1)S(1)} copy-done((bf16[1,3,1024,512]{3,2,1,0:T(8,128)(2,1)S(1)}, bf16[1,3,1024,512]{3,2,1,0:T(8,128)(2,1)}, u32[]{:S(2)}) %copy-start) | copy-done | bytes 3145752
  4.2 0.9 %copy-done.2 = bf16[3,128,128]{2,1,0:T(8,128)(2,1)S(1)} copy-done((bf16[3,128,128]{2,1,0:T(8,128)(2,1)S(1)}, bf16[3,128,128]{2,1,0:T(8,128)(2,1)}, u32[]{:S(2)}) %copy-start.2) | copy-done | bytes 98328
  5.1 0.9 %copy-done.4 = bf16[1,128,512]{2,1,0:T(8,128)(2,1)S(1)} copy-done((bf16[1,128,512]{2,1,0:T(8,128)(2,1)S(1)}, bf16[1,128,512]{2,1,0:T(8,128)(2,1)}, u32[]{:S(2)}) %copy-start.4) | copy-done | bytes 131096
  6.0 0.7 %copy-done.5 = s32[8]{0:T(128)S(1)} copy-done((s32[8]{0:T(128)S(1)}, s32[8]{0:T(128)}, u32[]{:S(2)}) %copy-start.5) | copy-done | bytes 56
  6.7 0.7 %copy-done.6 = s32[8]{0:T(128)S(1)} copy-done((s32[8]{0:T(128)S(1)}, s32[8]{0:T(128)}, u32[]{:S(2)}) %copy-start.6) | copy-done | bytes 56
  7.3 1.2 %shard_map.69 = (bf16[2,32,512]{2,1,0:T(8,128)(2,1)S(1)}, bf16[2,32,512]{2,1,0:T(8,128)(2,1)S(1)}, bf16[2,32,512]{2,1,0:T(8,128)(2,1)S(1)}, bf16[2,32,512]{2,1,0...) custom-call(s32[1,8]{1,0:T(1,128)S(1)} %bitcast.7, s32[1,8]{1,0:T(1,128)S(1)} %bitcast.8, ...), custom_call_target="tpu_custom_call" | custom-call | flops 452984832 | bytes 262144 | tf_op jit(solution)/shard_map/pallas_call | solution.py:426
  8.5 4.0 %collective-permute-start.1 = (bf16[2,32,512]{2,1,0:T(8,128)(2,1)S(1)}, bf16[2,32,512]{2,1,0:T(8,128)(2,1)S(1)}, u32[]{:S(2)}, u32[]{:S(2)}) collective-permute-start(bf16[2,32,512]{2,1,0:T(8,128)(2,1)S(1)} %get-tuple-element.30), channel_id=1, source_target_pairs={{0,8},{2,10},{4,12},{6,14},{8,0},{10,2},{12,4},{14,6},{1,9},{3,11}... | collective-permute-start | bytes 196616 | tf_op jit(solution)/shard_map/ppermute | solution.py:387
  12.5 1.4 %collective-permute-start.2 = (bf16[2,32,512]{2,1,0:T(8,128)(2,1)S(1)}, bf16[2,32,512]{2,1,0:T(8,128)(2,1)S(1)}, u32[]{:S(2)}, u32[]{:S(2)}) collective-permute-start(bf16[2,32,512]{2,1,0:T(8,128)(2,1)S(1)} %get-tuple-element.31), channel_id=1, source_target_pairs={{0,12},{2,14},{4,8},{6,10},{8,4},{10,6},{12,0},{14,2},{1,13},{3,15... | collective-permute-start | bytes 196616 | tf_op jit(solution)/shard_map/ppermute | solution.py:387
  14.1 0.6 %shard_map.68.plan = s32[8,128]{1,0:T(8,128)S(1)} custom-call(s32[8]{0:T(128)S(1)} %copy-done.5, s32[8]{0:T(128)S(1)} %copy-done.6), custom_call_target="tpu_custom_call" | custom-call | bytes 262144 | tf_op jit(solution)/shard_map/pallas_call | solution.py:424
  14.7 1.8 %collective-permute-done.1.rest_1_ = bf16[2,32,512]{2,1,0:T(8,128)(2,1)S(1)} collective-permute-done((bf16[2,32,512]{2,1,0:T(8,128)(2,1)S(1)}, bf16[2,32,512]{2,1,0:T(8,128)(2,1)S(1)}, u32[]{:S(2)}, u32[]{:S(2)}) %collective-permute-start.1) | collective-permute-done | bytes 65568 | tf_op jit(solution)/shard_map/ppermute | solution.py:387
  16.5 2.5 %collective-permute-done.2.rest_2_ = bf16[2,32,512]{2,1,0:T(8,128)(2,1)S(1)} collective-permute-done((bf16[2,32,512]{2,1,0:T(8,128)(2,1)S(1)}, bf16[2,32,512]{2,1,0:T(8,128)(2,1)S(1)}, u32[]{:S(2)}, u32[]{:S(2)}) %collective-permute-start.2) | collective-permute-done | bytes 65568 | tf_op jit(solution)/shard_map/ppermute | solution.py:387
  19.4 1.7 %collective-permute-start.4 = (bf16[4,32,512]{2,1,0:T(8,128)(2,1)S(1)}, bf16[4,32,512]{2,1,0:T(8,128)(2,1)S(1)}, u32[]{:S(2)}, u32[]{:S(2)}) collective-permute-start(bf16[4,32,512]{2,1,0:T(8,128)(2,1)S(1)} %get-tuple-element.36), channel_id=1, source_target_pairs={{0,2},{2,0},{4,6},{6,4},{8,10},{10,8},{12,14},{14,12},{1,3},{3,1},... | collective-permute-start | bytes 393224 | tf_op jit(solution)/shard_map/ppermute | solution.py:396
  21.2 3.3 %collective-permute-done.4.arrived.old_arrived = bf16[4,32,512]{2,1,0:T(8,128)(2,1)S(1)} collective-permute-done((bf16[4,32,512]{2,1,0:T(8,128)(2,1)S(1)}, bf16[4,32,512]{2,1,0:T(8,128)(2,1)S(1)}, u32[]{:S(2)}, u32[]{:S(2)}) %collective-permute-start.4) | collective-permute-done | bytes 131104 | tf_op jit(solution)/shard_map/ppermute | solution.py:396
  24.5 3.2 %collective-permute-start.5 = (bf16[32,512]{1,0:T(8,128)(2,1)S(1)}, bf16[32,512]{1,0:T(8,128)(2,1)S(1)}, u32[]{:S(2)}, u32[]{:S(2)}) collective-permute-start(bf16[32,512]{1,0:T(8,128)(2,1)S(1)} %get-tuple-element.38), channel_id=1, source_target_pairs={{0,8},{2,10},{4,12},{6,14},{8,0},{10,2},{12,4},{14,6},{1,9},{3,11}... | collective-permute-start | bytes 98312 | tf_op jit(solution)/shard_map/ppermute | solution.py:387
  28.7 1.6 %collective-permute-done.5.rest_1_ = bf16[32,512]{1,0:T(8,128)(2,1)S(1)} collective-permute-done((bf16[32,512]{1,0:T(8,128)(2,1)S(1)}, bf16[32,512]{1,0:T(8,128)(2,1)S(1)}, u32[]{:S(2)}, u32[]{:S(2)}) %collective-permute-start.5) | collective-permute-done | bytes 32800 | tf_op jit(solution)/shard_map/ppermute | solution.py:387
  30.3 3.2 %collective-permute-done.6.rest_2_ = bf16[32,512]{1,0:T(8,128)(2,1)S(1)} collective-permute-done((bf16[32,512]{1,0:T(8,128)(2,1)S(1)}, bf16[32,512]{1,0:T(8,128)(2,1)S(1)}, u32[]{:S(2)}, u32[]{:S(2)}) %collective-permute-start.6) | collective-permute-done | bytes 32800 | tf_op jit(solution)/shard_map/ppermute | solution.py:387
  33.6 1.3 %collective-permute-done.8.other = bf16[128,512]{1,0:T(8,128)(2,1)S(1)} collective-permute-done((bf16[128,512]{1,0:T(8,128)(2,1)S(1)}, bf16[128,512]{1,0:T(8,128)(2,1)S(1)}, u32[]{:S(2)}, u32[]{:S(2)}) %collective-permute-start.8) | collective-permute-done | bytes 131104 | tf_op jit(solution)/shard_map/ppermute | solution.py:392
  35.0 1.2 %shard_map.73 = (bf16[272,128]{1,0:T(8,128)(2,1)S(1)}, bf16[272,128]{1,0:T(8,128)(2,1)S(1)}, bf16[272,128]{1,0:T(8,128)(2,1)S(1)}, bf16[272,128]{1,0:T(8,128)(2,1)S(1)}, f32[128,512]{1,0:T(8,128)S(1)}) custom-call(bf16[2,128,512]{2,1,0:T(8,128)(2,1)S(1)} %get-tuple-element.33.start, bf16[128,512]{1,0:T(8,128)(2,1)S(1)} %shard_map.72.own.first, ...), custom_call_target="tpu_custom_call" | custom-call | flops 452984832 | bytes 262144 | tf_op jit(solution)/shard_map/pallas_call | solution.py:439
  36.2 1.0 %collective-permute-start.9 = (bf16[272,128]{1,0:T(8,128)(2,1)S(1)}, bf16[272,128]{1,0:T(8,128)(2,1)S(1)}, u32[]{:S(2)}, u32[]{:S(2)}) collective-permute-start(bf16[272,128]{1,0:T(8,128)(2,1)S(1)} %get-tuple-element.42), channel_id=1, source_target_pairs={{0,8},{2,10},{4,12},{6,14},{8,0},{10,2},{12,4},{14,6},{1,9},{3,11}... | collective-permute-start | bytes 208904 | tf_op jit(solution)/shard_map/ppermute | solution.py:387
  37.2 1.2 %collective-permute-start.10 = (bf16[272,128]{1,0:T(8,128)(2,1)S(1)}, bf16[272,128]{1,0:T(8,128)(2,1)S(1)}, u32[]{:S(2)}, u32[]{:S(2)}) collective-permute-start(bf16[272,128]{1,0:T(8,128)(2,1)S(1)} %get-tuple-element.43), channel_id=1, source_target_pairs={{0,12},{2,14},{4,8},{6,10},{8,4},{10,6},{12,0},{14,2},{1,13},{3,15... | collective-permute-start | bytes 208904 | tf_op jit(solution)/shard_map/ppermute | solution.py:387
  38.4 1.4 %collective-permute-start.11 = (bf16[272,128]{1,0:T(8,128)(2,1)S(1)}, bf16[272,128]{1,0:T(8,128)(2,1)S(1)}, u32[]{:S(2)}, u32[]{:S(2)}) collective-permute-start(bf16[272,128]{1,0:T(8,128)(2,1)S(1)} %get-tuple-element.44), channel_id=1, source_target_pairs={{0,4},{2,6},{4,0},{6,2},{8,12},{10,14},{12,8},{14,10},{1,5},{3,7},... | collective-permute-start | bytes 208904 | tf_op jit(solution)/shard_map/ppermute | solution.py:387
  39.7 4.1 %collective-permute-done.9.rest_5_ = bf16[272,128]{1,0:T(8,128)(2,1)S(1)} collective-permute-done((bf16[272,128]{1,0:T(8,128)(2,1)S(1)}, bf16[272,128]{1,0:T(8,128)(2,1)S(1)}, u32[]{:S(2)}, u32[]{:S(2)}) %collective-permute-start.9) | collective-permute-done | bytes 69664 | tf_op jit(solution)/shard_map/ppermute | solution.py:387
  43.9 1.3 %collective-permute-done.11.rest_7_ = bf16[272,128]{1,0:T(8,128)(2,1)S(1)} collective-permute-done((bf16[272,128]{1,0:T(8,128)(2,1)S(1)}, bf16[272,128]{1,0:T(8,128)(2,1)S(1)}, u32[]{:S(2)}, u32[]{:S(2)}) %collective-permute-start.11) | collective-permute-done | bytes 69664 | tf_op jit(solution)/shard_map/ppermute | solution.py:387
  45.7 1.6 %collective-permute-start.12 = (bf16[528,128]{1,0:T(8,128)(2,1)S(1)}, bf16[528,128]{1,0:T(8,128)(2,1)S(1)}, u32[]{:S(2)}, u32[]{:S(2)}) collective-permute-start(bf16[528,128]{1,0:T(8,128)(2,1)S(1)} %get-tuple-element.47), channel_id=1, source_target_pairs={{0,2},{2,0},{4,6},{6,4},{8,10},{10,8},{12,14},{14,12},{1,3},{3,1},... | collective-permute-start | bytes 405512 | tf_op jit(solution)/shard_map/ppermute | solution.py:396
  47.3 4.0 %collective-permute-done.12.arrived = bf16[528,128]{1,0:T(8,128)(2,1)S(1)} collective-permute-done((bf16[528,128]{1,0:T(8,128)(2,1)S(1)}, bf16[528,128]{1,0:T(8,128)(2,1)S(1)}, u32[]{:S(2)}, u32[]{:S(2)}) %collective-permute-start.12) | collective-permute-done | bytes 135200 | tf_op jit(solution)/shard_map/ppermute | solution.py:396
  51.6 1.7 %collective-permute-start.13 = (bf16[32,512]{1,0:T(8,128)(2,1)S(1)}, bf16[32,512]{1,0:T(8,128)(2,1)S(1)}, u32[]{:S(2)}, u32[]{:S(2)}) collective-permute-start(bf16[32,512]{1,0:T(8,128)(2,1)S(1)} %get-tuple-element.51), channel_id=1, source_target_pairs={{0,8},{2,10},{4,12},{6,14},{8,0},{10,2},{12,4},{14,6},{1,9},{3,11}... | collective-permute-start | bytes 98312 | tf_op jit(solution)/shard_map/ppermute | solution.py:387
  53.3 1.4 %collective-permute-start.14 = (bf16[32,512]{1,0:T(8,128)(2,1)S(1)}, bf16[32,512]{1,0:T(8,128)(2,1)S(1)}, u32[]{:S(2)}, u32[]{:S(2)}) collective-permute-start(bf16[32,512]{1,0:T(8,128)(2,1)S(1)} %get-tuple-element.52), channel_id=1, source_target_pairs={{0,12},{2,14},{4,8},{6,10},{8,4},{10,6},{12,0},{14,2},{1,13},{3,15... | collective-permute-start | bytes 98312 | tf_op jit(solution)/shard_map/ppermute | solution.py:387
  55.2 2.0 %collective-permute-done.13.rest_1_ = bf16[32,512]{1,0:T(8,128)(2,1)S(1)} collective-permute-done((bf16[32,512]{1,0:T(8,128)(2,1)S(1)}, bf16[32,512]{1,0:T(8,128)(2,1)S(1)}, u32[]{:S(2)}, u32[]{:S(2)}) %collective-permute-start.13) | collective-permute-done | bytes 32800 | tf_op jit(solution)/shard_map/ppermute | solution.py:387
  57.2 1.9 %collective-permute-done.14.rest_2_ = bf16[32,512]{1,0:T(8,128)(2,1)S(1)} collective-permute-done((bf16[32,512]{1,0:T(8,128)(2,1)S(1)}, bf16[32,512]{1,0:T(8,128)(2,1)S(1)}, u32[]{:S(2)}, u32[]{:S(2)}) %collective-permute-start.14) | collective-permute-done | bytes 32800 | tf_op jit(solution)/shard_map/ppermute | solution.py:387
  59.1 0.8 %shard_map.76 = (bf16[128,512]{1,0:T(8,128)(2,1)}, bf16[128,512]{1,0:T(8,128)(2,1)}) custom-call(s32[8,128]{1,0:T(8,128)S(1)} %shard_map.68.plan, f32[8,128]{1,0:T(8,128)S(1)} %get-tuple-element.48.factors, bf16[128,512]{1,0:T(8,128)(2,1)S(1)} %get-tuple-element.34.stay, f32[128,512]{1,0:T(8,128)S(1)} %get-tuple-element.49.stay_2, ...), custom_call_target="tpu_custom_call" | custom-call | bytes 262144 | tf_op jit(solution)/shard_map/pallas_call | solution.py:449
  (23 shorter events, 3.1 us)
Async XLA Ops:
  0.6 1.7 %collective-permute-start = (bf16[128,512]{1,0:T(8,128)(2,1)}, bf16[128,512]{1,0:T(8,128)(2,1)S(1)}, u32[]{:S(2)}, u32[]{:S(2)}) collective-permute-start(bf16[128,512]{1,0:T(8,128)(2,1)} %bitcast.5), channel_id=1, source_target_pairs={{0,1},{1,0},{2,3},{3,2},{4,5},{5,4},{6,7},{7,6},{8,9},{9,8},{10,11... | collective-permute-start | bytes 393224 | tf_op jit(solution)/shard_map/ppermute | solution.py:392
  2.3 1.9 %copy-start = (bf16[1,3,1024,512]{3,2,1,0:T(8,128)(2,1)S(1)}, bf16[1,3,1024,512]{3,2,1,0:T(8,128)(2,1)}, u32[]{:S(2)}) copy-start(bf16[1,3,1024,512]{3,2,1,0:T(8,128)(2,1)} %left.3) | copy-start | bytes 9437188
  4.2 0.9 %copy-start.2 = (bf16[3,128,128]{2,1,0:T(8,128)(2,1)S(1)}, bf16[3,128,128]{2,1,0:T(8,128)(2,1)}, u32[]{:S(2)}) copy-start(bf16[3,128,128]{2,1,0:T(8,128)(2,1)} %right.3) | copy-start | bytes 294916
  5.1 0.9 %copy-start.4 = (bf16[1,128,512]{2,1,0:T(8,128)(2,1)S(1)}, bf16[1,128,512]{2,1,0:T(8,128)(2,1)}, u32[]{:S(2)}) copy-start(bf16[1,128,512]{2,1,0:T(8,128)(2,1)} %param.5) | copy-start | bytes 393220
  6.0 0.7 %copy-start.5 = (s32[8]{0:T(128)S(1)}, s32[8]{0:T(128)}, u32[]{:S(2)}) copy-start(s32[8]{0:T(128)} %widths.1) | copy-start | bytes 100
  6.7 0.7 %copy-start.6 = (s32[8]{0:T(128)S(1)}, s32[8]{0:T(128)}, u32[]{:S(2)}) copy-start(s32[8]{0:T(128)} %holders.1) | copy-start | bytes 100
  7.3 27.6 %copy-start.1 = (bf16[1,3,1024,512]{3,2,1,0:T(8,128)(2,1)S(1)}, bf16[1,3,1024,512]{3,2,1,0:T(8,128)(2,1)}, u32[]{:S(2)}) copy-start(bf16[1,3,1024,512]{3,2,1,0:T(8,128)(2,1)} %left.3) | copy-start | bytes 9437188
  7.3 27.6 %copy-start.3 = (bf16[3,128,128]{2,1,0:T(8,128)(2,1)S(1)}, bf16[3,128,128]{2,1,0:T(8,128)(2,1)}, u32[]{:S(2)}) copy-start(bf16[3,128,128]{2,1,0:T(8,128)(2,1)} %right.3) | copy-start | bytes 294916
  8.5 8.0 %collective-permute-start.1 = (bf16[2,32,512]{2,1,0:T(8,128)(2,1)S(1)}, bf16[2,32,512]{2,1,0:T(8,128)(2,1)S(1)}, u32[]{:S(2)}, u32[]{:S(2)}) collective-permute-start(bf16[2,32,512]{2,1,0:T(8,128)(2,1)S(1)} %get-tuple-element.30), channel_id=1, source_target_pairs={{0,8},{2,10},{4,12},{6,14},{8,0},{10,2},{12,4},{14,6},{1,9},{3,11}... | collective-permute-start | bytes 196616 | tf_op jit(solution)/shard_map/ppermute | solution.py:387
  12.5 6.4 %collective-permute-start.2 = (bf16[2,32,512]{2,1,0:T(8,128)(2,1)S(1)}, bf16[2,32,512]{2,1,0:T(8,128)(2,1)S(1)}, u32[]{:S(2)}, u32[]{:S(2)}) collective-permute-start(bf16[2,32,512]{2,1,0:T(8,128)(2,1)S(1)} %get-tuple-element.31), channel_id=1, source_target_pairs={{0,12},{2,14},{4,8},{6,10},{8,4},{10,6},{12,0},{14,2},{1,13},{3,15... | collective-permute-start | bytes 196616 | tf_op jit(solution)/shard_map/ppermute | solution.py:387
  13.9 5.2 %collective-permute-start.3 = (bf16[2,32,512]{2,1,0:T(8,128)(2,1)S(1)}, bf16[2,32,512]{2,1,0:T(8,128)(2,1)S(1)}, u32[]{:S(2)}, u32[]{:S(2)}) collective-permute-start(bf16[2,32,512]{2,1,0:T(8,128)(2,1)S(1)} %get-tuple-element.32), channel_id=1, source_target_pairs={{0,4},{2,6},{4,0},{6,2},{8,12},{10,14},{12,8},{14,10},{1,5},{3,7},... | collective-permute-start | bytes 196616 | tf_op jit(solution)/shard_map/ppermute | solution.py:387
  19.4 5.0 %collective-permute-start.4 = (bf16[4,32,512]{2,1,0:T(8,128)(2,1)S(1)}, bf16[4,32,512]{2,1,0:T(8,128)(2,1)S(1)}, u32[]{:S(2)}, u32[]{:S(2)}) collective-permute-start(bf16[4,32,512]{2,1,0:T(8,128)(2,1)S(1)} %get-tuple-element.36), channel_id=1, source_target_pairs={{0,2},{2,0},{4,6},{6,4},{8,10},{10,8},{12,14},{14,12},{1,3},{3,1},... | collective-permute-start | bytes 393224 | tf_op jit(solution)/shard_map/ppermute | solution.py:396
  24.5 5.8 %collective-permute-start.5 = (bf16[32,512]{1,0:T(8,128)(2,1)S(1)}, bf16[32,512]{1,0:T(8,128)(2,1)S(1)}, u32[]{:S(2)}, u32[]{:S(2)}) collective-permute-start(bf16[32,512]{1,0:T(8,128)(2,1)S(1)} %get-tuple-element.38), channel_id=1, source_target_pairs={{0,8},{2,10},{4,12},{6,14},{8,0},{10,2},{12,4},{14,6},{1,9},{3,11}... | collective-permute-start | bytes 98312 | tf_op jit(solution)/shard_map/ppermute | solution.py:387
  27.7 5.7 %collective-permute-start.6 = (bf16[32,512]{1,0:T(8,128)(2,1)S(1)}, bf16[32,512]{1,0:T(8,128)(2,1)S(1)}, u32[]{:S(2)}, u32[]{:S(2)}) collective-permute-start(bf16[32,512]{1,0:T(8,128)(2,1)S(1)} %get-tuple-element.39), channel_id=1, source_target_pairs={{0,12},{2,14},{4,8},{6,10},{8,4},{10,6},{12,0},{14,2},{1,13},{3,15... | collective-permute-start | bytes 98312 | tf_op jit(solution)/shard_map/ppermute | solution.py:387
  28.2 5.3 %collective-permute-start.7 = (bf16[32,512]{1,0:T(8,128)(2,1)S(1)}, bf16[32,512]{1,0:T(8,128)(2,1)S(1)}, u32[]{:S(2)}, u32[]{:S(2)}) collective-permute-start(bf16[32,512]{1,0:T(8,128)(2,1)S(1)} %get-tuple-element.40), channel_id=1, source_target_pairs={{0,4},{2,6},{4,0},{6,2},{8,12},{10,14},{12,8},{14,10},{1,5},{3,7},... | collective-permute-start | bytes 98312 | tf_op jit(solution)/shard_map/ppermute | solution.py:387
  33.5 1.4 %collective-permute-start.8 = (bf16[128,512]{1,0:T(8,128)(2,1)S(1)}, bf16[128,512]{1,0:T(8,128)(2,1)S(1)}, u32[]{:S(2)}, u32[]{:S(2)}) collective-permute-start(bf16[128,512]{1,0:T(8,128)(2,1)S(1)} %shard_map.72.own.first), channel_id=1, source_target_pairs={{0,1},{1,0},{2,3},{3,2},{4,5},{5,4},{6,7},{7,6},{8,9},{9,8},{10,11... | collective-permute-start | bytes 393224 | tf_op jit(solution)/shard_map/ppermute | solution.py:392
  36.2 7.7 %collective-permute-start.9 = (bf16[272,128]{1,0:T(8,128)(2,1)S(1)}, bf16[272,128]{1,0:T(8,128)(2,1)S(1)}, u32[]{:S(2)}, u32[]{:S(2)}) collective-permute-start(bf16[272,128]{1,0:T(8,128)(2,1)S(1)} %get-tuple-element.42), channel_id=1, source_target_pairs={{0,8},{2,10},{4,12},{6,14},{8,0},{10,2},{12,4},{14,6},{1,9},{3,11}... | collective-permute-start | bytes 208904 | tf_op jit(solution)/shard_map/ppermute | solution.py:387
  37.2 6.7 %collective-permute-start.10 = (bf16[272,128]{1,0:T(8,128)(2,1)S(1)}, bf16[272,128]{1,0:T(8,128)(2,1)S(1)}, u32[]{:S(2)}, u32[]{:S(2)}) collective-permute-start(bf16[272,128]{1,0:T(8,128)(2,1)S(1)} %get-tuple-element.43), channel_id=1, source_target_pairs={{0,12},{2,14},{4,8},{6,10},{8,4},{10,6},{12,0},{14,2},{1,13},{3,15... | collective-permute-start | bytes 208904 | tf_op jit(solution)/shard_map/ppermute | solution.py:387
  38.4 6.8 %collective-permute-start.11 = (bf16[272,128]{1,0:T(8,128)(2,1)S(1)}, bf16[272,128]{1,0:T(8,128)(2,1)S(1)}, u32[]{:S(2)}, u32[]{:S(2)}) collective-permute-start(bf16[272,128]{1,0:T(8,128)(2,1)S(1)} %get-tuple-element.44), channel_id=1, source_target_pairs={{0,4},{2,6},{4,0},{6,2},{8,12},{10,14},{12,8},{14,10},{1,5},{3,7},... | collective-permute-start | bytes 208904 | tf_op jit(solution)/shard_map/ppermute | solution.py:387
  45.7 5.5 %collective-permute-start.12 = (bf16[528,128]{1,0:T(8,128)(2,1)S(1)}, bf16[528,128]{1,0:T(8,128)(2,1)S(1)}, u32[]{:S(2)}, u32[]{:S(2)}) collective-permute-start(bf16[528,128]{1,0:T(8,128)(2,1)S(1)} %get-tuple-element.47), channel_id=1, source_target_pairs={{0,2},{2,0},{4,6},{6,4},{8,10},{10,8},{12,14},{14,12},{1,3},{3,1},... | collective-permute-start | bytes 405512 | tf_op jit(solution)/shard_map/ppermute | solution.py:396
  51.6 5.6 %collective-permute-start.13 = (bf16[32,512]{1,0:T(8,128)(2,1)S(1)}, bf16[32,512]{1,0:T(8,128)(2,1)S(1)}, u32[]{:S(2)}, u32[]{:S(2)}) collective-permute-start(bf16[32,512]{1,0:T(8,128)(2,1)S(1)} %get-tuple-element.51), channel_id=1, source_target_pairs={{0,8},{2,10},{4,12},{6,14},{8,0},{10,2},{12,4},{14,6},{1,9},{3,11}... | collective-permute-start | bytes 98312 | tf_op jit(solution)/shard_map/ppermute | solution.py:387
  53.3 5.7 %collective-permute-start.14 = (bf16[32,512]{1,0:T(8,128)(2,1)S(1)}, bf16[32,512]{1,0:T(8,128)(2,1)S(1)}, u32[]{:S(2)}, u32[]{:S(2)}) collective-permute-start(bf16[32,512]{1,0:T(8,128)(2,1)S(1)} %get-tuple-element.52), channel_id=1, source_target_pairs={{0,12},{2,14},{4,8},{6,10},{8,4},{10,6},{12,0},{14,2},{1,13},{3,15... | collective-permute-start | bytes 98312 | tf_op jit(solution)/shard_map/ppermute | solution.py:387
  54.8 4.3 %collective-permute-start.15 = (bf16[32,512]{1,0:T(8,128)(2,1)S(1)}, bf16[32,512]{1,0:T(8,128)(2,1)S(1)}, u32[]{:S(2)}, u32[]{:S(2)}) collective-permute-start(bf16[32,512]{1,0:T(8,128)(2,1)S(1)} %get-tuple-element.53), channel_id=1, source_target_pairs={{0,4},{2,6},{4,0},{6,2},{8,12},{10,14},{12,8},{14,10},{1,5},{3,7},... | collective-permute-start | bytes 98312 | tf_op jit(solution)/shard_map/ppermute | solution.py:387

commit v16 on v15

--- a/solution.py
+++ b/solution.py
@@ -155,16 +155,19 @@
     return lax.axis_index("sec") // LINES
 
 
-def first_kernel(widths, holders, own, other, right, left, *rest):
+def columns_kernel(columns):
+    columns[...] = lax.broadcasted_iota(jnp.int32, columns.shape, 1)
+
+
+def first_kernel(columns, widths, holders, own, other, right, left, *rest):
     *pieces, stay, start, block_vmem = rest
     half = stay.shape[1]
     slot = lax.broadcasted_iota(jnp.int32, widths.shape, 1)
     mine = jnp.where(slot == lax.axis_index("sec"), holders[...], 0)
     sector = jnp.sum(mine, axis=1, keepdims=True)
     width = jnp.sum(jnp.where(slot == sector, widths[...], 0), axis=1, keepdims=True)
-    columns = lax.broadcasted_iota(jnp.int32, (1, half), 1)
     for h, part in enumerate(in_order(own[...], other[...])):
-        live = h * half + columns < width
+        live = h * half + columns[0:1, :] < width
         start[h] = jnp.where(live, part, jnp.zeros_like(part))
     vector = jnp.concatenate([start[0], start[1]], axis=1)
     for term in (1, 2, 0):
@@ -423,9 +426,19 @@
     slot_table = [pltpu.SMEM((slots,), jnp.int32)]
     plan = call(plan_kernel, [SMEM, SMEM], plan_shape, slot_table)(widths, holders)
     both = jax.ShapeDtypeStruct((2, right_dim, half), jnp.bfloat16)
+    number = jax.ShapeDtypeStruct((8, half), jnp.int32)
+    columns = call(columns_kernel, [], number, flops=4 << 30)()
     *pieces, stay, start_full = call(
-        first_kernel, [VMEM] * 6, (pair,) * places + (block, both), split, dots
-    )(widths[None], holders[None], amplitudes[0], other_core(amplitudes[0]), right_env, left_env)
+        first_kernel, [VMEM] * 7, (pair,) * places + (block, both), split, dots
+    )(
+        columns,
+        widths[None],
+        holders[None],
+        amplitudes[0],
+        other_core(amplitudes[0]),
+        right_env,
+        left_env,
+    )
     old = along_line(pieces, slots)
     old_keep, cross = call(
         merge_kernel, [VMEM] * (1 + places), (singles, singles), tables[:1]

time: 60 us -> 54.8 us (0.913)
  local copies, waits for them, and re-layouts: 5 us -> 0.14 us
    unnamed x14 -> x10, local copies, waits for them, and re-layouts: 5 us -> 0.14 us
  transfers between devices with their start and end apart: 16 -> 16, of which waited for: 13 -> 12; matrix products, arithmetic and copies ran while one was open for 0% -> 0% of each run, Pallas kernels for 1% -> 1%
where the time goes in v16:
time: 54.8 us; the launch traced here: 54.7 us
  waiting for transfers between devices  28.2 us (51%)
  starting transfers between devices  20.5 us (37%)
  Pallas kernels  5.09 us (9%)
  between operations  0.75 us (1%)
    ppermute x12, waiting for transfers between devices, along_line(): sent.append(lax.ppermute(piece, 'sec', pairs) if step else piece)  18.4 us
    ppermute x12, starting transfers between devices, along_line(): sent.append(lax.ppermute(piece, 'sec', pairs) if step else piece)  16.6 us
    ppermute x2, waiting for transfers between devices, across(): lax.ppermute(piece, 'sec', [(slot, slot ^ 1) for slot in range(slots)])  7.21 us
    ppermute x2, starting transfers between devices, across(): lax.ppermute(piece, 'sec', [(slot, slot ^ 1) for slot in range(slots)])  3.35 us
    ppermute x2, waiting for transfers between devices, other_core(): return lax.ppermute(block, 'env', [(0, 1), (1, 0)])  2.53 us
    pallas_call x1, Pallas kernels, on_device(): call(second_kernel, [VMEM] * 5, (tagged,) * places + (wide,), split, dots)  1.23 us
    pallas_call x1, Pallas kernels, on_device(): call(first_kernel, [VMEM] * 7, (pair,) * places + (block, both), split, d...  1.17 us
  transfers between devices with their start and end apart: 16, of which 12 were waited for; matrix products, arithmetic and copies ran while one was open for 0% of the time, Pallas kernels for 1%

profile of v16, /device:TPU:0, one launch (start us, length us, event | category | flops | bytes accessed | tf_op | source)
XLA Modules:
  0.0 54.7 jit_solution(10179779066597340124)
XLA Ops:
  0.7 0.5 collective-permute-start
  1.2 1.2 %collective-permute-done.other = bf16[128,512]{1,0:T(8,128)(2,1)S(1)} collective-permute-done((bf16[128,512]{1,0:T(8,128)(2,1)}, bf16[128,512]{1,0:T(8,128)(2,1)S(1)}, u32[]{:S(2)}, u32[]{:S(2)}) %collective-permute-start) | collective-permute-done | bytes 131104 | tf_op jit(solution)/shard_map/ppermute | solution.py:395
  2.5 1.2 %shard_map.70 = (bf16[2,32,512]{2,1,0:T(8,128)(2,1)S(1)}, bf16[2,32,512]{2,1,0:T(8,128)(2,1)S(1)}, bf16[2,32,512]{2,1,0:T(8,128)(2,1)S(1)}, bf16[2,32,512]{2,1,0...) custom-call(s32[8,512]{1,0:T(8,128)S(1)} %shard_map.69.columns, s32[1,8]{1,0:T(1,128)S(1)} %bitcast.7, ...), custom_call_target="tpu_custom_call" | custom-call | flops 452984832 | bytes 262144 | tf_op jit(solution)/shard_map/pallas_call | solution.py:431
  3.7 4.1 %collective-permute-start.1 = (bf16[2,32,512]{2,1,0:T(8,128)(2,1)S(1)}, bf16[2,32,512]{2,1,0:T(8,128)(2,1)S(1)}, u32[]{:S(2)}, u32[]{:S(2)}) collective-permute-start(bf16[2,32,512]{2,1,0:T(8,128)(2,1)S(1)} %get-tuple-element.30), channel_id=1, source_target_pairs={{0,8},{2,10},{4,12},{6,14},{8,0},{10,2},{12,4},{14,6},{1,9},{3,11}... | collective-permute-start | bytes 196616 | tf_op jit(solution)/shard_map/ppermute | solution.py:390
  7.8 1.3 %collective-permute-start.2 = (bf16[2,32,512]{2,1,0:T(8,128)(2,1)S(1)}, bf16[2,32,512]{2,1,0:T(8,128)(2,1)S(1)}, u32[]{:S(2)}, u32[]{:S(2)}) collective-permute-start(bf16[2,32,512]{2,1,0:T(8,128)(2,1)S(1)} %get-tuple-element.31), channel_id=1, source_target_pairs={{0,12},{2,14},{4,8},{6,10},{8,4},{10,6},{12,0},{14,2},{1,13},{3,15... | collective-permute-start | bytes 196616 | tf_op jit(solution)/shard_map/ppermute | solution.py:390
  9.4 0.6 %shard_map.68.plan = s32[8,128]{1,0:T(8,128)S(1)} custom-call(s32[8]{0:T(128)S(1)} %copy-done.3, s32[8]{0:T(128)S(1)} %copy-done.4), custom_call_target="tpu_custom_call" | custom-call | bytes 262144 | tf_op jit(solution)/shard_map/pallas_call | solution.py:427
  10.0 1.6 %collective-permute-done.1.rest_1_ = bf16[2,32,512]{2,1,0:T(8,128)(2,1)S(1)} collective-permute-done((bf16[2,32,512]{2,1,0:T(8,128)(2,1)S(1)}, bf16[2,32,512]{2,1,0:T(8,128)(2,1)S(1)}, u32[]{:S(2)}, u32[]{:S(2)}) %collective-permute-start.1) | collective-permute-done | bytes 65568 | tf_op jit(solution)/shard_map/ppermute | solution.py:390
  11.6 2.5 %collective-permute-done.2.rest_2_ = bf16[2,32,512]{2,1,0:T(8,128)(2,1)S(1)} collective-permute-done((bf16[2,32,512]{2,1,0:T(8,128)(2,1)S(1)}, bf16[2,32,512]{2,1,0:T(8,128)(2,1)S(1)}, u32[]{:S(2)}, u32[]{:S(2)}) %collective-permute-start.2) | collective-permute-done | bytes 65568 | tf_op jit(solution)/shard_map/ppermute | solution.py:390
  14.1 0.3 shard_map.71
  14.5 1.8 %collective-permute-start.4 = (bf16[4,32,512]{2,1,0:T(8,128)(2,1)S(1)}, bf16[4,32,512]{2,1,0:T(8,128)(2,1)S(1)}, u32[]{:S(2)}, u32[]{:S(2)}) collective-permute-start(bf16[4,32,512]{2,1,0:T(8,128)(2,1)S(1)} %get-tuple-element.36), channel_id=1, source_target_pairs={{0,2},{2,0},{4,6},{6,4},{8,10},{10,8},{12,14},{14,12},{1,3},{3,1},... | collective-permute-start | bytes 393224 | tf_op jit(solution)/shard_map/ppermute | solution.py:399
  16.2 3.3 %collective-permute-done.4.arrived.old_arrived = bf16[4,32,512]{2,1,0:T(8,128)(2,1)S(1)} collective-permute-done((bf16[4,32,512]{2,1,0:T(8,128)(2,1)S(1)}, bf16[4,32,512]{2,1,0:T(8,128)(2,1)S(1)}, u32[]{:S(2)}, u32[]{:S(2)}) %collective-permute-start.4) | collective-permute-done | bytes 131104 | tf_op jit(solution)/shard_map/ppermute | solution.py:399
  19.5 3.1 %collective-permute-start.5 = (bf16[32,512]{1,0:T(8,128)(2,1)S(1)}, bf16[32,512]{1,0:T(8,128)(2,1)S(1)}, u32[]{:S(2)}, u32[]{:S(2)}) collective-permute-start(bf16[32,512]{1,0:T(8,128)(2,1)S(1)} %get-tuple-element.38), channel_id=1, source_target_pairs={{0,8},{2,10},{4,12},{6,14},{8,0},{10,2},{12,4},{14,6},{1,9},{3,11}... | collective-permute-start | bytes 98312 | tf_op jit(solution)/shard_map/ppermute | solution.py:390
  22.6 0.4 collective-permute-start.6
  23.3 1.3 %collective-permute-done.5.rest_1_ = bf16[32,512]{1,0:T(8,128)(2,1)S(1)} collective-permute-done((bf16[32,512]{1,0:T(8,128)(2,1)S(1)}, bf16[32,512]{1,0:T(8,128)(2,1)S(1)}, u32[]{:S(2)}, u32[]{:S(2)}) %collective-permute-start.5) | collective-permute-done | bytes 32800 | tf_op jit(solution)/shard_map/ppermute | solution.py:390
  24.6 3.7 %collective-permute-done.6.rest_2_ = bf16[32,512]{1,0:T(8,128)(2,1)S(1)} collective-permute-done((bf16[32,512]{1,0:T(8,128)(2,1)S(1)}, bf16[32,512]{1,0:T(8,128)(2,1)S(1)}, u32[]{:S(2)}, u32[]{:S(2)}) %collective-permute-start.6) | collective-permute-done | bytes 32800 | tf_op jit(solution)/shard_map/ppermute | solution.py:390
  28.5 1.3 %collective-permute-done.8.other = bf16[128,512]{1,0:T(8,128)(2,1)S(1)} collective-permute-done((bf16[128,512]{1,0:T(8,128)(2,1)S(1)}, bf16[128,512]{1,0:T(8,128)(2,1)S(1)}, u32[]{:S(2)}, u32[]{:S(2)}) %collective-permute-start.8) | collective-permute-done | bytes 131104 | tf_op jit(solution)/shard_map/ppermute | solution.py:395
  29.8 1.2 %shard_map.74 = (bf16[272,128]{1,0:T(8,128)(2,1)S(1)}, bf16[272,128]{1,0:T(8,128)(2,1)S(1)}, bf16[272,128]{1,0:T(8,128)(2,1)S(1)}, bf16[272,128]{1,0:T(8,128)(2,1)S(1)}, f32[128,512]{1,0:T(8,128)S(1)}) custom-call(bf16[2,128,512]{2,1,0:T(8,128)(2,1)S(1)} %get-tuple-element.33.start, bf16[128,512]{1,0:T(8,128)(2,1)S(1)} %shard_map.73.own.first, ...), custom_call_target="tpu_custom_call" | custom-call | flops 452984832 | bytes 262144 | tf_op jit(solution)/shard_map/pallas_call | solution.py:452
  31.0 1.0 %collective-permute-start.9 = (bf16[272,128]{1,0:T(8,128)(2,1)S(1)}, bf16[272,128]{1,0:T(8,128)(2,1)S(1)}, u32[]{:S(2)}, u32[]{:S(2)}) collective-permute-start(bf16[272,128]{1,0:T(8,128)(2,1)S(1)} %get-tuple-element.42), channel_id=1, source_target_pairs={{0,8},{2,10},{4,12},{6,14},{8,0},{10,2},{12,4},{14,6},{1,9},{3,11}... | collective-permute-start | bytes 208904 | tf_op jit(solution)/shard_map/ppermute | solution.py:390
  32.0 1.2 %collective-permute-start.10 = (bf16[272,128]{1,0:T(8,128)(2,1)S(1)}, bf16[272,128]{1,0:T(8,128)(2,1)S(1)}, u32[]{:S(2)}, u32[]{:S(2)}) collective-permute-start(bf16[272,128]{1,0:T(8,128)(2,1)S(1)} %get-tuple-element.43), channel_id=1, source_target_pairs={{0,12},{2,14},{4,8},{6,10},{8,4},{10,6},{12,0},{14,2},{1,13},{3,15... | collective-permute-start | bytes 208904 | tf_op jit(solution)/shard_map/ppermute | solution.py:390
  33.2 1.4 %collective-permute-start.11 = (bf16[272,128]{1,0:T(8,128)(2,1)S(1)}, bf16[272,128]{1,0:T(8,128)(2,1)S(1)}, u32[]{:S(2)}, u32[]{:S(2)}) collective-permute-start(bf16[272,128]{1,0:T(8,128)(2,1)S(1)} %get-tuple-element.44), channel_id=1, source_target_pairs={{0,4},{2,6},{4,0},{6,2},{8,12},{10,14},{12,8},{14,10},{1,5},{3,7},... | collective-permute-start | bytes 208904 | tf_op jit(solution)/shard_map/ppermute | solution.py:390
  34.6 4.1 %collective-permute-done.9.rest_5_ = bf16[272,128]{1,0:T(8,128)(2,1)S(1)} collective-permute-done((bf16[272,128]{1,0:T(8,128)(2,1)S(1)}, bf16[272,128]{1,0:T(8,128)(2,1)S(1)}, u32[]{:S(2)}, u32[]{:S(2)}) %collective-permute-start.9) | collective-permute-done | bytes 69664 | tf_op jit(solution)/shard_map/ppermute | solution.py:390
  38.7 1.3 %collective-permute-done.11.rest_7_ = bf16[272,128]{1,0:T(8,128)(2,1)S(1)} collective-permute-done((bf16[272,128]{1,0:T(8,128)(2,1)S(1)}, bf16[272,128]{1,0:T(8,128)(2,1)S(1)}, u32[]{:S(2)}, u32[]{:S(2)}) %collective-permute-start.11) | collective-permute-done | bytes 69664 | tf_op jit(solution)/shard_map/ppermute | solution.py:390
  40.1 0.5 shard_map.75
  40.6 1.6 %collective-permute-start.12 = (bf16[528,128]{1,0:T(8,128)(2,1)S(1)}, bf16[528,128]{1,0:T(8,128)(2,1)S(1)}, u32[]{:S(2)}, u32[]{:S(2)}) collective-permute-start(bf16[528,128]{1,0:T(8,128)(2,1)S(1)} %get-tuple-element.47), channel_id=1, source_target_pairs={{0,2},{2,0},{4,6},{6,4},{8,10},{10,8},{12,14},{14,12},{1,3},{3,1},... | collective-permute-start | bytes 405512 | tf_op jit(solution)/shard_map/ppermute | solution.py:399
  42.1 3.9 %collective-permute-done.12.arrived = bf16[528,128]{1,0:T(8,128)(2,1)S(1)} collective-permute-done((bf16[528,128]{1,0:T(8,128)(2,1)S(1)}, bf16[528,128]{1,0:T(8,128)(2,1)S(1)}, u32[]{:S(2)}, u32[]{:S(2)}) %collective-permute-start.12) | collective-permute-done | bytes 135200 | tf_op jit(solution)/shard_map/ppermute | solution.py:399
  46.1 0.4 shard_map.76
  46.5 1.7 %collective-permute-start.13 = (bf16[32,512]{1,0:T(8,128)(2,1)S(1)}, bf16[32,512]{1,0:T(8,128)(2,1)S(1)}, u32[]{:S(2)}, u32[]{:S(2)}) collective-permute-start(bf16[32,512]{1,0:T(8,128)(2,1)S(1)} %get-tuple-element.51), channel_id=1, source_target_pairs={{0,8},{2,10},{4,12},{6,14},{8,0},{10,2},{12,4},{14,6},{1,9},{3,11}... | collective-permute-start | bytes 98312 | tf_op jit(solution)/shard_map/ppermute | solution.py:390
  48.2 1.4 %collective-permute-start.14 = (bf16[32,512]{1,0:T(8,128)(2,1)S(1)}, bf16[32,512]{1,0:T(8,128)(2,1)S(1)}, u32[]{:S(2)}, u32[]{:S(2)}) collective-permute-start(bf16[32,512]{1,0:T(8,128)(2,1)S(1)} %get-tuple-element.52), channel_id=1, source_target_pairs={{0,12},{2,14},{4,8},{6,10},{8,4},{10,6},{12,0},{14,2},{1,13},{3,15... | collective-permute-start | bytes 98312 | tf_op jit(solution)/shard_map/ppermute | solution.py:390
  49.6 0.4 collective-permute-start.15
  50.0 2.0 %collective-permute-done.13.rest_1_ = bf16[32,512]{1,0:T(8,128)(2,1)S(1)} collective-permute-done((bf16[32,512]{1,0:T(8,128)(2,1)S(1)}, bf16[32,512]{1,0:T(8,128)(2,1)S(1)}, u32[]{:S(2)}, u32[]{:S(2)}) %collective-permute-start.13) | collective-permute-done | bytes 32800 | tf_op jit(solution)/shard_map/ppermute | solution.py:390
  52.1 1.8 %collective-permute-done.14.rest_2_ = bf16[32,512]{1,0:T(8,128)(2,1)S(1)} collective-permute-done((bf16[32,512]{1,0:T(8,128)(2,1)S(1)}, bf16[32,512]{1,0:T(8,128)(2,1)S(1)}, u32[]{:S(2)}, u32[]{:S(2)}) %collective-permute-start.14) | collective-permute-done | bytes 32800 | tf_op jit(solution)/shard_map/ppermute | solution.py:390
  53.9 0.8 %shard_map.77 = (bf16[128,512]{1,0:T(8,128)(2,1)}, bf16[128,512]{1,0:T(8,128)(2,1)}) custom-call(s32[8,128]{1,0:T(8,128)S(1)} %shard_map.68.plan, f32[8,128]{1,0:T(8,128)S(1)} %get-tuple-element.48.factors, bf16[128,512]{1,0:T(8,128)(2,1)S(1)} %get-tuple-element.34.stay, f32[128,512]{1,0:T(8,128)S(1)} %get-tuple-element.49.stay_2, ...), custom_call_target="tpu_custom_call" | custom-call | bytes 262144 | tf_op jit(solution)/shard_map/pallas_call | solution.py:462
  (20 shorter events, 0.9 us)
Async XLA Ops:
  0.6 1.9 %copy-start = (bf16[1,3,1024,512]{3,2,1,0:T(8,128)(2,1)S(1)}, bf16[1,3,1024,512]{3,2,1,0:T(8,128)(2,1)}, u32[]{:S(2)}) copy-start(bf16[1,3,1024,512]{3,2,1,0:T(8,128)(2,1)} %left.3) | copy-start | bytes 9437188
  0.6 1.9 %copy-start.1 = (bf16[3,128,128]{2,1,0:T(8,128)(2,1)S(1)}, bf16[3,128,128]{2,1,0:T(8,128)(2,1)}, u32[]{:S(2)}) copy-start(bf16[3,128,128]{2,1,0:T(8,128)(2,1)} %right.3) | copy-start | bytes 294916
  0.7 1.9 %copy-start.2 = (bf16[1,128,512]{2,1,0:T(8,128)(2,1)S(1)}, bf16[1,128,512]{2,1,0:T(8,128)(2,1)}, u32[]{:S(2)}) copy-start(bf16[1,128,512]{2,1,0:T(8,128)(2,1)} %param.5) | copy-start | bytes 393220
  0.7 1.9 %copy-start.3 = (s32[8]{0:T(128)S(1)}, s32[8]{0:T(128)}, u32[]{:S(2)}) copy-start(s32[8]{0:T(128)} %widths.1) | copy-start | bytes 100
  0.7 1.9 %copy-start.4 = (s32[8]{0:T(128)S(1)}, s32[8]{0:T(128)}, u32[]{:S(2)}) copy-start(s32[8]{0:T(128)} %holders.1) | copy-start | bytes 100
  0.7 1.7 %collective-permute-start = (bf16[128,512]{1,0:T(8,128)(2,1)}, bf16[128,512]{1,0:T(8,128)(2,1)S(1)}, u32[]{:S(2)}, u32[]{:S(2)}) collective-permute-start(bf16[128,512]{1,0:T(8,128)(2,1)} %bitcast.5), channel_id=1, source_target_pairs={{0,1},{1,0},{2,3},{3,2},{4,5},{5,4},{6,7},{7,6},{8,9},{9,8},{10,11... | collective-permute-start | bytes 393224 | tf_op jit(solution)/shard_map/ppermute | solution.py:395
  3.7 7.9 %collective-permute-start.1 = (bf16[2,32,512]{2,1,0:T(8,128)(2,1)S(1)}, bf16[2,32,512]{2,1,0:T(8,128)(2,1)S(1)}, u32[]{:S(2)}, u32[]{:S(2)}) collective-permute-start(bf16[2,32,512]{2,1,0:T(8,128)(2,1)S(1)} %get-tuple-element.30), channel_id=1, source_target_pairs={{0,8},{2,10},{4,12},{6,14},{8,0},{10,2},{12,4},{14,6},{1,9},{3,11}... | collective-permute-start | bytes 196616 | tf_op jit(solution)/shard_map/ppermute | solution.py:390
  7.8 6.3 %collective-permute-start.2 = (bf16[2,32,512]{2,1,0:T(8,128)(2,1)S(1)}, bf16[2,32,512]{2,1,0:T(8,128)(2,1)S(1)}, u32[]{:S(2)}, u32[]{:S(2)}) collective-permute-start(bf16[2,32,512]{2,1,0:T(8,128)(2,1)S(1)} %get-tuple-element.31), channel_id=1, source_target_pairs={{0,12},{2,14},{4,8},{6,10},{8,4},{10,6},{12,0},{14,2},{1,13},{3,15... | collective-permute-start | bytes 196616 | tf_op jit(solution)/shard_map/ppermute | solution.py:390
  9.2 5.0 %collective-permute-start.3 = (bf16[2,32,512]{2,1,0:T(8,128)(2,1)S(1)}, bf16[2,32,512]{2,1,0:T(8,128)(2,1)S(1)}, u32[]{:S(2)}, u32[]{:S(2)}) collective-permute-start(bf16[2,32,512]{2,1,0:T(8,128)(2,1)S(1)} %get-tuple-element.32), channel_id=1, source_target_pairs={{0,4},{2,6},{4,0},{6,2},{8,12},{10,14},{12,8},{14,10},{1,5},{3,7},... | collective-permute-start | bytes 196616 | tf_op jit(solution)/shard_map/ppermute | solution.py:390
  14.5 5.0 %collective-permute-start.4 = (bf16[4,32,512]{2,1,0:T(8,128)(2,1)S(1)}, bf16[4,32,512]{2,1,0:T(8,128)(2,1)S(1)}, u32[]{:S(2)}, u32[]{:S(2)}) collective-permute-start(bf16[4,32,512]{2,1,0:T(8,128)(2,1)S(1)} %get-tuple-element.36), channel_id=1, source_target_pairs={{0,2},{2,0},{4,6},{6,4},{8,10},{10,8},{12,14},{14,12},{1,3},{3,1},... | collective-permute-start | bytes 393224 | tf_op jit(solution)/shard_map/ppermute | solution.py:399
  19.5 5.1 %collective-permute-start.5 = (bf16[32,512]{1,0:T(8,128)(2,1)S(1)}, bf16[32,512]{1,0:T(8,128)(2,1)S(1)}, u32[]{:S(2)}, u32[]{:S(2)}) collective-permute-start(bf16[32,512]{1,0:T(8,128)(2,1)S(1)} %get-tuple-element.38), channel_id=1, source_target_pairs={{0,8},{2,10},{4,12},{6,14},{8,0},{10,2},{12,4},{14,6},{1,9},{3,11}... | collective-permute-start | bytes 98312 | tf_op jit(solution)/shard_map/ppermute | solution.py:390
  22.6 5.7 %collective-permute-start.6 = (bf16[32,512]{1,0:T(8,128)(2,1)S(1)}, bf16[32,512]{1,0:T(8,128)(2,1)S(1)}, u32[]{:S(2)}, u32[]{:S(2)}) collective-permute-start(bf16[32,512]{1,0:T(8,128)(2,1)S(1)} %get-tuple-element.39), channel_id=1, source_target_pairs={{0,12},{2,14},{4,8},{6,10},{8,4},{10,6},{12,0},{14,2},{1,13},{3,15... | collective-permute-start | bytes 98312 | tf_op jit(solution)/shard_map/ppermute | solution.py:390
  23.0 5.3 %collective-permute-start.7 = (bf16[32,512]{1,0:T(8,128)(2,1)S(1)}, bf16[32,512]{1,0:T(8,128)(2,1)S(1)}, u32[]{:S(2)}, u32[]{:S(2)}) collective-permute-start(bf16[32,512]{1,0:T(8,128)(2,1)S(1)} %get-tuple-element.40), channel_id=1, source_target_pairs={{0,4},{2,6},{4,0},{6,2},{8,12},{10,14},{12,8},{14,10},{1,5},{3,7},... | collective-permute-start | bytes 98312 | tf_op jit(solution)/shard_map/ppermute | solution.py:390
  28.4 1.4 %collective-permute-start.8 = (bf16[128,512]{1,0:T(8,128)(2,1)S(1)}, bf16[128,512]{1,0:T(8,128)(2,1)S(1)}, u32[]{:S(2)}, u32[]{:S(2)}) collective-permute-start(bf16[128,512]{1,0:T(8,128)(2,1)S(1)} %shard_map.73.own.first), channel_id=1, source_target_pairs={{0,1},{1,0},{2,3},{3,2},{4,5},{5,4},{6,7},{7,6},{8,9},{9,8},{10,11... | collective-permute-start | bytes 393224 | tf_op jit(solution)/shard_map/ppermute | solution.py:395
  31.0 7.7 %collective-permute-start.9 = (bf16[272,128]{1,0:T(8,128)(2,1)S(1)}, bf16[272,128]{1,0:T(8,128)(2,1)S(1)}, u32[]{:S(2)}, u32[]{:S(2)}) collective-permute-start(bf16[272,128]{1,0:T(8,128)(2,1)S(1)} %get-tuple-element.42), channel_id=1, source_target_pairs={{0,8},{2,10},{4,12},{6,14},{8,0},{10,2},{12,4},{14,6},{1,9},{3,11}... | collective-permute-start | bytes 208904 | tf_op jit(solution)/shard_map/ppermute | solution.py:390
  32.0 6.7 %collective-permute-start.10 = (bf16[272,128]{1,0:T(8,128)(2,1)S(1)}, bf16[272,128]{1,0:T(8,128)(2,1)S(1)}, u32[]{:S(2)}, u32[]{:S(2)}) collective-permute-start(bf16[272,128]{1,0:T(8,128)(2,1)S(1)} %get-tuple-element.43), channel_id=1, source_target_pairs={{0,12},{2,14},{4,8},{6,10},{8,4},{10,6},{12,0},{14,2},{1,13},{3,15... | collective-permute-start | bytes 208904 | tf_op jit(solution)/shard_map/ppermute | solution.py:390
  33.2 6.8 %collective-permute-start.11 = (bf16[272,128]{1,0:T(8,128)(2,1)S(1)}, bf16[272,128]{1,0:T(8,128)(2,1)S(1)}, u32[]{:S(2)}, u32[]{:S(2)}) collective-permute-start(bf16[272,128]{1,0:T(8,128)(2,1)S(1)} %get-tuple-element.44), channel_id=1, source_target_pairs={{0,4},{2,6},{4,0},{6,2},{8,12},{10,14},{12,8},{14,10},{1,5},{3,7},... | collective-permute-start | bytes 208904 | tf_op jit(solution)/shard_map/ppermute | solution.py:390
  40.6 5.5 %collective-permute-start.12 = (bf16[528,128]{1,0:T(8,128)(2,1)S(1)}, bf16[528,128]{1,0:T(8,128)(2,1)S(1)}, u32[]{:S(2)}, u32[]{:S(2)}) collective-permute-start(bf16[528,128]{1,0:T(8,128)(2,1)S(1)} %get-tuple-element.47), channel_id=1, source_target_pairs={{0,2},{2,0},{4,6},{6,4},{8,10},{10,8},{12,14},{14,12},{1,3},{3,1},... | collective-permute-start | bytes 405512 | tf_op jit(solution)/shard_map/ppermute | solution.py:399
  46.5 5.6 %collective-permute-start.13 = (bf16[32,512]{1,0:T(8,128)(2,1)S(1)}, bf16[32,512]{1,0:T(8,128)(2,1)S(1)}, u32[]{:S(2)}, u32[]{:S(2)}) collective-permute-start(bf16[32,512]{1,0:T(8,128)(2,1)S(1)} %get-tuple-element.51), channel_id=1, source_target_pairs={{0,8},{2,10},{4,12},{6,14},{8,0},{10,2},{12,4},{14,6},{1,9},{3,11}... | collective-permute-start | bytes 98312 | tf_op jit(solution)/shard_map/ppermute | solution.py:390
  48.2 5.7 %collective-permute-start.14 = (bf16[32,512]{1,0:T(8,128)(2,1)S(1)}, bf16[32,512]{1,0:T(8,128)(2,1)S(1)}, u32[]{:S(2)}, u32[]{:S(2)}) collective-permute-start(bf16[32,512]{1,0:T(8,128)(2,1)S(1)} %get-tuple-element.52), channel_id=1, source_target_pairs={{0,12},{2,14},{4,8},{6,10},{8,4},{10,6},{12,0},{14,2},{1,13},{3,15... | collective-permute-start | bytes 98312 | tf_op jit(solution)/shard_map/ppermute | solution.py:390
  49.6 4.3 %collective-permute-start.15 = (bf16[32,512]{1,0:T(8,128)(2,1)S(1)}, bf16[32,512]{1,0:T(8,128)(2,1)S(1)}, u32[]{:S(2)}, u32[]{:S(2)}) collective-permute-start(bf16[32,512]{1,0:T(8,128)(2,1)S(1)} %get-tuple-element.53), channel_id=1, source_target_pairs={{0,4},{2,6},{4,0},{6,2},{8,12},{10,14},{12,8},{14,10},{1,5},{3,7},... | collective-permute-start | bytes 98312 | tf_op jit(solution)/shard_map/ppermute | solution.py:390

commit v17 on v16

--- a/solution.py
+++ b/solution.py
@@ -112,7 +112,7 @@
 LANES = 128
 TAG = 16
 LINES = 2
-STEPS = (0, 2, 3, 1)
+STEPS = (0, 3, 2, 1)
 
 
 def plan_kernel(widths, holders, plan, slot_of):

time: 54.8 us -> 53.7 us (0.980)
  waiting for transfers between devices: 28.2 us -> 24.6 us
  starting transfers between devices: 20.5 us -> 22.9 us
    ppermute x12, waiting for transfers between devices: 18.4 us -> 14.5 us  [along_line(): sent.append(lax.ppermute(piece, 'sec', pairs) if step else piece)]
    ppermute x12, starting transfers between devices: 16.6 us -> 19.1 us  [along_line(): sent.append(lax.ppermute(piece, 'sec', pairs) if step else piece)]
where the time goes in v17:
time: 53.7 us; the launch traced here: 53.5 us
  waiting for transfers between devices  24.6 us (46%)
  starting transfers between devices  22.9 us (43%)
  Pallas kernels  5.1 us (9%)
  between operations  0.75 us (1%)
    ppermute x12, starting transfers between devices, along_line(): sent.append(lax.ppermute(piece, 'sec', pairs) if step else piece)  19.1 us
    ppermute x12, waiting for transfers between devices, along_line(): sent.append(lax.ppermute(piece, 'sec', pairs) if step else piece)  14.5 us
    ppermute x2, waiting for transfers between devices, across(): lax.ppermute(piece, 'sec', [(slot, slot ^ 1) for slot in range(slots)])  7.61 us
    ppermute x2, starting transfers between devices, across(): lax.ppermute(piece, 'sec', [(slot, slot ^ 1) for slot in range(slots)])  3.19 us
    ppermute x2, waiting for transfers between devices, other_core(): return lax.ppermute(block, 'env', [(0, 1), (1, 0)])  2.53 us
    pallas_call x1, Pallas kernels, on_device(): call(second_kernel, [VMEM] * 5, (tagged,) * places + (wide,), split, dots)  1.23 us
    pallas_call x1, Pallas kernels, on_device(): call(first_kernel, [VMEM] * 7, (pair,) * places + (block, both), split, d...  1.17 us
  transfers between devices with their start and end apart: 16, of which 12 were waited for; matrix products, arithmetic and copies ran while one was open for 0% of the time, Pallas kernels for 1%

profile of v17, /device:TPU:0, one launch (start us, length us, event | category | flops | bytes accessed | tf_op | source)
XLA Modules:
  0.0 53.5 jit_solution(3990955868674949321)
XLA Ops:
  0.7 0.5 collective-permute-start
  1.2 1.2 %collective-permute-done.other = bf16[128,512]{1,0:T(8,128)(2,1)S(1)} collective-permute-done((bf16[128,512]{1,0:T(8,128)(2,1)}, bf16[128,512]{1,0:T(8,128)(2,1)S(1)}, u32[]{:S(2)}, u32[]{:S(2)}) %collective-permute-start) | collective-permute-done | bytes 131104 | tf_op jit(solution)/shard_map/ppermute | solution.py:395
  2.4 0.1 copy-done
  2.5 1.2 %shard_map.70 = (bf16[2,32,512]{2,1,0:T(8,128)(2,1)S(1)}, bf16[2,32,512]{2,1,0:T(8,128)(2,1)S(1)}, bf16[2,32,512]{2,1,0:T(8,128)(2,1)S(1)}, bf16[2,32,512]{2,1,0...) custom-call(s32[8,512]{1,0:T(8,128)S(1)} %shard_map.69.columns, s32[1,8]{1,0:T(1,128)S(1)} %bitcast.7, ...), custom_call_target="tpu_custom_call" | custom-call | flops 452984832 | bytes 262144 | tf_op jit(solution)/shard_map/pallas_call | solution.py:431
  3.7 5.1 %collective-permute-start.1 = (bf16[2,32,512]{2,1,0:T(8,128)(2,1)S(1)}, bf16[2,32,512]{2,1,0:T(8,128)(2,1)S(1)}, u32[]{:S(2)}, u32[]{:S(2)}) collective-permute-start(bf16[2,32,512]{2,1,0:T(8,128)(2,1)S(1)} %get-tuple-element.30), channel_id=1, source_target_pairs={{0,12},{2,14},{4,8},{6,10},{8,4},{10,6},{12,0},{14,2},{1,13},{3,15... | collective-permute-start | bytes 196616 | tf_op jit(solution)/shard_map/ppermute | solution.py:390
  8.8 0.6 %collective-permute-start.3 = (bf16[2,32,512]{2,1,0:T(8,128)(2,1)S(1)}, bf16[2,32,512]{2,1,0:T(8,128)(2,1)S(1)}, u32[]{:S(2)}, u32[]{:S(2)}) collective-permute-start(bf16[2,32,512]{2,1,0:T(8,128)(2,1)S(1)} %get-tuple-element.32), channel_id=1, source_target_pairs={{0,4},{2,6},{4,0},{6,2},{8,12},{10,14},{12,8},{14,10},{1,5},{3,7},... | collective-permute-start | bytes 196616 | tf_op jit(solution)/shard_map/ppermute | solution.py:390
  9.5 0.6 %shard_map.68.plan = s32[8,128]{1,0:T(8,128)S(1)} custom-call(s32[8]{0:T(128)S(1)} %copy-done.3, s32[8]{0:T(128)S(1)} %copy-done.4), custom_call_target="tpu_custom_call" | custom-call | bytes 262144 | tf_op jit(solution)/shard_map/pallas_call | solution.py:427
  10.1 1.2 %collective-permute-done.1.rest_1_ = bf16[2,32,512]{2,1,0:T(8,128)(2,1)S(1)} collective-permute-done((bf16[2,32,512]{2,1,0:T(8,128)(2,1)S(1)}, bf16[2,32,512]{2,1,0:T(8,128)(2,1)S(1)}, u32[]{:S(2)}, u32[]{:S(2)}) %collective-permute-start.1) | collective-permute-done | bytes 65568 | tf_op jit(solution)/shard_map/ppermute | solution.py:390
  11.3 3.2 %collective-permute-done.2.rest_2_ = bf16[2,32,512]{2,1,0:T(8,128)(2,1)S(1)} collective-permute-done((bf16[2,32,512]{2,1,0:T(8,128)(2,1)S(1)}, bf16[2,32,512]{2,1,0:T(8,128)(2,1)S(1)}, u32[]{:S(2)}, u32[]{:S(2)}) %collective-permute-start.2) | collective-permute-done | bytes 65568 | tf_op jit(solution)/shard_map/ppermute | solution.py:390
  14.5 0.3 shard_map.71
  14.9 1.6 %collective-permute-start.4 = (bf16[4,32,512]{2,1,0:T(8,128)(2,1)S(1)}, bf16[4,32,512]{2,1,0:T(8,128)(2,1)S(1)}, u32[]{:S(2)}, u32[]{:S(2)}) collective-permute-start(bf16[4,32,512]{2,1,0:T(8,128)(2,1)S(1)} %get-tuple-element.36), channel_id=1, source_target_pairs={{0,2},{2,0},{4,6},{6,4},{8,10},{10,8},{12,14},{14,12},{1,3},{3,1},... | collective-permute-start | bytes 393224 | tf_op jit(solution)/shard_map/ppermute | solution.py:399
  16.4 3.6 %collective-permute-done.4.arrived.old_arrived = bf16[4,32,512]{2,1,0:T(8,128)(2,1)S(1)} collective-permute-done((bf16[4,32,512]{2,1,0:T(8,128)(2,1)S(1)}, bf16[4,32,512]{2,1,0:T(8,128)(2,1)S(1)}, u32[]{:S(2)}, u32[]{:S(2)}) %collective-permute-start.4) | collective-permute-done | bytes 131104 | tf_op jit(solution)/shard_map/ppermute | solution.py:399
  20.0 2.6 %collective-permute-start.5 = (bf16[32,512]{1,0:T(8,128)(2,1)S(1)}, bf16[32,512]{1,0:T(8,128)(2,1)S(1)}, u32[]{:S(2)}, u32[]{:S(2)}) collective-permute-start(bf16[32,512]{1,0:T(8,128)(2,1)S(1)} %get-tuple-element.38), channel_id=1, source_target_pairs={{0,12},{2,14},{4,8},{6,10},{8,4},{10,6},{12,0},{14,2},{1,13},{3,15... | collective-permute-start | bytes 98312 | tf_op jit(solution)/shard_map/ppermute | solution.py:390
  22.7 1.8 %collective-permute-start.7 = (bf16[32,512]{1,0:T(8,128)(2,1)S(1)}, bf16[32,512]{1,0:T(8,128)(2,1)S(1)}, u32[]{:S(2)}, u32[]{:S(2)}) collective-permute-start(bf16[32,512]{1,0:T(8,128)(2,1)S(1)} %get-tuple-element.40), channel_id=1, source_target_pairs={{0,4},{2,6},{4,0},{6,2},{8,12},{10,14},{12,8},{14,10},{1,5},{3,7},... | collective-permute-start | bytes 98312 | tf_op jit(solution)/shard_map/ppermute | solution.py:390
  24.5 1.3 %collective-permute-done.5.rest_1_ = bf16[32,512]{1,0:T(8,128)(2,1)S(1)} collective-permute-done((bf16[32,512]{1,0:T(8,128)(2,1)S(1)}, bf16[32,512]{1,0:T(8,128)(2,1)S(1)}, u32[]{:S(2)}, u32[]{:S(2)}) %collective-permute-start.5) | collective-permute-done | bytes 32800 | tf_op jit(solution)/shard_map/ppermute | solution.py:390
  25.8 1.7 %collective-permute-done.6.rest_2_ = bf16[32,512]{1,0:T(8,128)(2,1)S(1)} collective-permute-done((bf16[32,512]{1,0:T(8,128)(2,1)S(1)}, bf16[32,512]{1,0:T(8,128)(2,1)S(1)}, u32[]{:S(2)}, u32[]{:S(2)}) %collective-permute-start.6) | collective-permute-done | bytes 32800 | tf_op jit(solution)/shard_map/ppermute | solution.py:390
  27.7 1.3 %collective-permute-done.8.other = bf16[128,512]{1,0:T(8,128)(2,1)S(1)} collective-permute-done((bf16[128,512]{1,0:T(8,128)(2,1)S(1)}, bf16[128,512]{1,0:T(8,128)(2,1)S(1)}, u32[]{:S(2)}, u32[]{:S(2)}) %collective-permute-start.8) | collective-permute-done | bytes 131104 | tf_op jit(solution)/shard_map/ppermute | solution.py:395
  29.0 1.2 %shard_map.74 = (bf16[272,128]{1,0:T(8,128)(2,1)S(1)}, bf16[272,128]{1,0:T(8,128)(2,1)S(1)}, bf16[272,128]{1,0:T(8,128)(2,1)S(1)}, bf16[272,128]{1,0:T(8,128)(2,1)S(1)}, f32[128,512]{1,0:T(8,128)S(1)}) custom-call(bf16[2,128,512]{2,1,0:T(8,128)(2,1)S(1)} %get-tuple-element.33.start, bf16[128,512]{1,0:T(8,128)(2,1)S(1)} %shard_map.73.own.first, ...), custom_call_target="tpu_custom_call" | custom-call | flops 452984832 | bytes 262144 | tf_op jit(solution)/shard_map/pallas_call | solution.py:452
  30.2 1.9 %collective-permute-start.9 = (bf16[272,128]{1,0:T(8,128)(2,1)S(1)}, bf16[272,128]{1,0:T(8,128)(2,1)S(1)}, u32[]{:S(2)}, u32[]{:S(2)}) collective-permute-start(bf16[272,128]{1,0:T(8,128)(2,1)S(1)} %get-tuple-element.42), channel_id=1, source_target_pairs={{0,12},{2,14},{4,8},{6,10},{8,4},{10,6},{12,0},{14,2},{1,13},{3,15... | collective-permute-start | bytes 208904 | tf_op jit(solution)/shard_map/ppermute | solution.py:390
  32.1 0.6 %collective-permute-start.10 = (bf16[272,128]{1,0:T(8,128)(2,1)S(1)}, bf16[272,128]{1,0:T(8,128)(2,1)S(1)}, u32[]{:S(2)}, u32[]{:S(2)}) collective-permute-start(bf16[272,128]{1,0:T(8,128)(2,1)S(1)} %get-tuple-element.43), channel_id=1, source_target_pairs={{0,8},{2,10},{4,12},{6,14},{8,0},{10,2},{12,4},{14,6},{1,9},{3,11}... | collective-permute-start | bytes 208904 | tf_op jit(solution)/shard_map/ppermute | solution.py:390
  32.7 2.0 %collective-permute-start.11 = (bf16[272,128]{1,0:T(8,128)(2,1)S(1)}, bf16[272,128]{1,0:T(8,128)(2,1)S(1)}, u32[]{:S(2)}, u32[]{:S(2)}) collective-permute-start(bf16[272,128]{1,0:T(8,128)(2,1)S(1)} %get-tuple-element.44), channel_id=1, source_target_pairs={{0,4},{2,6},{4,0},{6,2},{8,12},{10,14},{12,8},{14,10},{1,5},{3,7},... | collective-permute-start | bytes 208904 | tf_op jit(solution)/shard_map/ppermute | solution.py:390
  34.7 2.5 %collective-permute-done.9.rest_5_ = bf16[272,128]{1,0:T(8,128)(2,1)S(1)} collective-permute-done((bf16[272,128]{1,0:T(8,128)(2,1)S(1)}, bf16[272,128]{1,0:T(8,128)(2,1)S(1)}, u32[]{:S(2)}, u32[]{:S(2)}) %collective-permute-start.9) | collective-permute-done | bytes 69664 | tf_op jit(solution)/shard_map/ppermute | solution.py:390
  37.2 2.3 %collective-permute-done.10.rest_6_ = bf16[272,128]{1,0:T(8,128)(2,1)S(1)} collective-permute-done((bf16[272,128]{1,0:T(8,128)(2,1)S(1)}, bf16[272,128]{1,0:T(8,128)(2,1)S(1)}, u32[]{:S(2)}, u32[]{:S(2)}) %collective-permute-start.10) | collective-permute-done | bytes 69664 | tf_op jit(solution)/shard_map/ppermute | solution.py:390
  39.4 0.5 shard_map.75
  39.9 1.6 %collective-permute-start.12 = (bf16[528,128]{1,0:T(8,128)(2,1)S(1)}, bf16[528,128]{1,0:T(8,128)(2,1)S(1)}, u32[]{:S(2)}, u32[]{:S(2)}) collective-permute-start(bf16[528,128]{1,0:T(8,128)(2,1)S(1)} %get-tuple-element.47), channel_id=1, source_target_pairs={{0,2},{2,0},{4,6},{6,4},{8,10},{10,8},{12,14},{14,12},{1,3},{3,1},... | collective-permute-start | bytes 405512 | tf_op jit(solution)/shard_map/ppermute | solution.py:399
  41.6 4.0 %collective-permute-done.12.arrived = bf16[528,128]{1,0:T(8,128)(2,1)S(1)} collective-permute-done((bf16[528,128]{1,0:T(8,128)(2,1)S(1)}, bf16[528,128]{1,0:T(8,128)(2,1)S(1)}, u32[]{:S(2)}, u32[]{:S(2)}) %collective-permute-start.12) | collective-permute-done | bytes 135200 | tf_op jit(solution)/shard_map/ppermute | solution.py:399
  45.6 0.4 shard_map.76
  46.0 2.0 %collective-permute-start.13 = (bf16[32,512]{1,0:T(8,128)(2,1)S(1)}, bf16[32,512]{1,0:T(8,128)(2,1)S(1)}, u32[]{:S(2)}, u32[]{:S(2)}) collective-permute-start(bf16[32,512]{1,0:T(8,128)(2,1)S(1)} %get-tuple-element.51), channel_id=1, source_target_pairs={{0,12},{2,14},{4,8},{6,10},{8,4},{10,6},{12,0},{14,2},{1,13},{3,15... | collective-permute-start | bytes 98312 | tf_op jit(solution)/shard_map/ppermute | solution.py:390
  48.0 2.5 %collective-permute-start.15 = (bf16[32,512]{1,0:T(8,128)(2,1)S(1)}, bf16[32,512]{1,0:T(8,128)(2,1)S(1)}, u32[]{:S(2)}, u32[]{:S(2)}) collective-permute-start(bf16[32,512]{1,0:T(8,128)(2,1)S(1)} %get-tuple-element.53), channel_id=1, source_target_pairs={{0,4},{2,6},{4,0},{6,2},{8,12},{10,14},{12,8},{14,10},{1,5},{3,7},... | collective-permute-start | bytes 98312 | tf_op jit(solution)/shard_map/ppermute | solution.py:390
  50.4 1.3 %collective-permute-done.13.rest_1_ = bf16[32,512]{1,0:T(8,128)(2,1)S(1)} collective-permute-done((bf16[32,512]{1,0:T(8,128)(2,1)S(1)}, bf16[32,512]{1,0:T(8,128)(2,1)S(1)}, u32[]{:S(2)}, u32[]{:S(2)}) %collective-permute-start.13) | collective-permute-done | bytes 32800 | tf_op jit(solution)/shard_map/ppermute | solution.py:390
  51.8 1.0 %collective-permute-done.14.rest_2_ = bf16[32,512]{1,0:T(8,128)(2,1)S(1)} collective-permute-done((bf16[32,512]{1,0:T(8,128)(2,1)S(1)}, bf16[32,512]{1,0:T(8,128)(2,1)S(1)}, u32[]{:S(2)}, u32[]{:S(2)}) %collective-permute-start.14) | collective-permute-done | bytes 32800 | tf_op jit(solution)/shard_map/ppermute | solution.py:390
  52.8 0.8 %shard_map.77 = (bf16[128,512]{1,0:T(8,128)(2,1)}, bf16[128,512]{1,0:T(8,128)(2,1)}) custom-call(s32[8,128]{1,0:T(8,128)S(1)} %shard_map.68.plan, f32[8,128]{1,0:T(8,128)S(1)} %get-tuple-element.48.factors, bf16[128,512]{1,0:T(8,128)(2,1)S(1)} %get-tuple-element.34.stay, f32[128,512]{1,0:T(8,128)S(1)} %get-tuple-element.49.stay_2, ...), custom_call_target="tpu_custom_call" | custom-call | bytes 262144 | tf_op jit(solution)/shard_map/pallas_call | solution.py:462
  (20 shorter events, 0.2 us)
Async XLA Ops:
  0.6 1.9 %copy-start = (bf16[1,3,1024,512]{3,2,1,0:T(8,128)(2,1)S(1)}, bf16[1,3,1024,512]{3,2,1,0:T(8,128)(2,1)}, u32[]{:S(2)}) copy-start(bf16[1,3,1024,512]{3,2,1,0:T(8,128)(2,1)} %left.3) | copy-start | bytes 9437188
  0.6 1.9 %copy-start.1 = (bf16[3,128,128]{2,1,0:T(8,128)(2,1)S(1)}, bf16[3,128,128]{2,1,0:T(8,128)(2,1)}, u32[]{:S(2)}) copy-start(bf16[3,128,128]{2,1,0:T(8,128)(2,1)} %right.3) | copy-start | bytes 294916
  0.7 1.9 %copy-start.2 = (bf16[1,128,512]{2,1,0:T(8,128)(2,1)S(1)}, bf16[1,128,512]{2,1,0:T(8,128)(2,1)}, u32[]{:S(2)}) copy-start(bf16[1,128,512]{2,1,0:T(8,128)(2,1)} %param.5) | copy-start | bytes 393220
  0.7 1.9 %copy-start.3 = (s32[8]{0:T(128)S(1)}, s32[8]{0:T(128)}, u32[]{:S(2)}) copy-start(s32[8]{0:T(128)} %widths.1) | copy-start | bytes 100
  0.7 1.9 %copy-start.4 = (s32[8]{0:T(128)S(1)}, s32[8]{0:T(128)}, u32[]{:S(2)}) copy-start(s32[8]{0:T(128)} %holders.1) | copy-start | bytes 100
  0.7 1.7 %collective-permute-start = (bf16[128,512]{1,0:T(8,128)(2,1)}, bf16[128,512]{1,0:T(8,128)(2,1)S(1)}, u32[]{:S(2)}, u32[]{:S(2)}) collective-permute-start(bf16[128,512]{1,0:T(8,128)(2,1)} %bitcast.5), channel_id=1, source_target_pairs={{0,1},{1,0},{2,3},{3,2},{4,5},{5,4},{6,7},{7,6},{8,9},{9,8},{10,11... | collective-permute-start | bytes 393224 | tf_op jit(solution)/shard_map/ppermute | solution.py:395
  3.7 7.6 %collective-permute-start.1 = (bf16[2,32,512]{2,1,0:T(8,128)(2,1)S(1)}, bf16[2,32,512]{2,1,0:T(8,128)(2,1)S(1)}, u32[]{:S(2)}, u32[]{:S(2)}) collective-permute-start(bf16[2,32,512]{2,1,0:T(8,128)(2,1)S(1)} %get-tuple-element.30), channel_id=1, source_target_pairs={{0,12},{2,14},{4,8},{6,10},{8,4},{10,6},{12,0},{14,2},{1,13},{3,15... | collective-permute-start | bytes 196616 | tf_op jit(solution)/shard_map/ppermute | solution.py:390
  8.8 5.7 %collective-permute-start.2 = (bf16[2,32,512]{2,1,0:T(8,128)(2,1)S(1)}, bf16[2,32,512]{2,1,0:T(8,128)(2,1)S(1)}, u32[]{:S(2)}, u32[]{:S(2)}) collective-permute-start(bf16[2,32,512]{2,1,0:T(8,128)(2,1)S(1)} %get-tuple-element.31), channel_id=1, source_target_pairs={{0,8},{2,10},{4,12},{6,14},{8,0},{10,2},{12,4},{14,6},{1,9},{3,11}... | collective-permute-start | bytes 196616 | tf_op jit(solution)/shard_map/ppermute | solution.py:390
  8.8 5.7 %collective-permute-start.3 = (bf16[2,32,512]{2,1,0:T(8,128)(2,1)S(1)}, bf16[2,32,512]{2,1,0:T(8,128)(2,1)S(1)}, u32[]{:S(2)}, u32[]{:S(2)}) collective-permute-start(bf16[2,32,512]{2,1,0:T(8,128)(2,1)S(1)} %get-tuple-element.32), channel_id=1, source_target_pairs={{0,4},{2,6},{4,0},{6,2},{8,12},{10,14},{12,8},{14,10},{1,5},{3,7},... | collective-permute-start | bytes 196616 | tf_op jit(solution)/shard_map/ppermute | solution.py:390
  14.9 5.1 %collective-permute-start.4 = (bf16[4,32,512]{2,1,0:T(8,128)(2,1)S(1)}, bf16[4,32,512]{2,1,0:T(8,128)(2,1)S(1)}, u32[]{:S(2)}, u32[]{:S(2)}) collective-permute-start(bf16[4,32,512]{2,1,0:T(8,128)(2,1)S(1)} %get-tuple-element.36), channel_id=1, source_target_pairs={{0,2},{2,0},{4,6},{6,4},{8,10},{10,8},{12,14},{14,12},{1,3},{3,1},... | collective-permute-start | bytes 393224 | tf_op jit(solution)/shard_map/ppermute | solution.py:399
  20.0 5.8 %collective-permute-start.5 = (bf16[32,512]{1,0:T(8,128)(2,1)S(1)}, bf16[32,512]{1,0:T(8,128)(2,1)S(1)}, u32[]{:S(2)}, u32[]{:S(2)}) collective-permute-start(bf16[32,512]{1,0:T(8,128)(2,1)S(1)} %get-tuple-element.38), channel_id=1, source_target_pairs={{0,12},{2,14},{4,8},{6,10},{8,4},{10,6},{12,0},{14,2},{1,13},{3,15... | collective-permute-start | bytes 98312 | tf_op jit(solution)/shard_map/ppermute | solution.py:390
  22.7 4.8 %collective-permute-start.6 = (bf16[32,512]{1,0:T(8,128)(2,1)S(1)}, bf16[32,512]{1,0:T(8,128)(2,1)S(1)}, u32[]{:S(2)}, u32[]{:S(2)}) collective-permute-start(bf16[32,512]{1,0:T(8,128)(2,1)S(1)} %get-tuple-element.39), channel_id=1, source_target_pairs={{0,8},{2,10},{4,12},{6,14},{8,0},{10,2},{12,4},{14,6},{1,9},{3,11}... | collective-permute-start | bytes 98312 | tf_op jit(solution)/shard_map/ppermute | solution.py:390
  22.7 4.8 %collective-permute-start.7 = (bf16[32,512]{1,0:T(8,128)(2,1)S(1)}, bf16[32,512]{1,0:T(8,128)(2,1)S(1)}, u32[]{:S(2)}, u32[]{:S(2)}) collective-permute-start(bf16[32,512]{1,0:T(8,128)(2,1)S(1)} %get-tuple-element.40), channel_id=1, source_target_pairs={{0,4},{2,6},{4,0},{6,2},{8,12},{10,14},{12,8},{14,10},{1,5},{3,7},... | collective-permute-start | bytes 98312 | tf_op jit(solution)/shard_map/ppermute | solution.py:390
  27.6 1.4 %collective-permute-start.8 = (bf16[128,512]{1,0:T(8,128)(2,1)S(1)}, bf16[128,512]{1,0:T(8,128)(2,1)S(1)}, u32[]{:S(2)}, u32[]{:S(2)}) collective-permute-start(bf16[128,512]{1,0:T(8,128)(2,1)S(1)} %shard_map.73.own.first), channel_id=1, source_target_pairs={{0,1},{1,0},{2,3},{3,2},{4,5},{5,4},{6,7},{7,6},{8,9},{9,8},{10,11... | collective-permute-start | bytes 393224 | tf_op jit(solution)/shard_map/ppermute | solution.py:395
  30.2 6.9 %collective-permute-start.9 = (bf16[272,128]{1,0:T(8,128)(2,1)S(1)}, bf16[272,128]{1,0:T(8,128)(2,1)S(1)}, u32[]{:S(2)}, u32[]{:S(2)}) collective-permute-start(bf16[272,128]{1,0:T(8,128)(2,1)S(1)} %get-tuple-element.42), channel_id=1, source_target_pairs={{0,12},{2,14},{4,8},{6,10},{8,4},{10,6},{12,0},{14,2},{1,13},{3,15... | collective-permute-start | bytes 208904 | tf_op jit(solution)/shard_map/ppermute | solution.py:390
  32.1 7.3 %collective-permute-start.10 = (bf16[272,128]{1,0:T(8,128)(2,1)S(1)}, bf16[272,128]{1,0:T(8,128)(2,1)S(1)}, u32[]{:S(2)}, u32[]{:S(2)}) collective-permute-start(bf16[272,128]{1,0:T(8,128)(2,1)S(1)} %get-tuple-element.43), channel_id=1, source_target_pairs={{0,8},{2,10},{4,12},{6,14},{8,0},{10,2},{12,4},{14,6},{1,9},{3,11}... | collective-permute-start | bytes 208904 | tf_op jit(solution)/shard_map/ppermute | solution.py:390
  32.7 6.8 %collective-permute-start.11 = (bf16[272,128]{1,0:T(8,128)(2,1)S(1)}, bf16[272,128]{1,0:T(8,128)(2,1)S(1)}, u32[]{:S(2)}, u32[]{:S(2)}) collective-permute-start(bf16[272,128]{1,0:T(8,128)(2,1)S(1)} %get-tuple-element.44), channel_id=1, source_target_pairs={{0,4},{2,6},{4,0},{6,2},{8,12},{10,14},{12,8},{14,10},{1,5},{3,7},... | collective-permute-start | bytes 208904 | tf_op jit(solution)/shard_map/ppermute | solution.py:390
  39.9 5.7 %collective-permute-start.12 = (bf16[528,128]{1,0:T(8,128)(2,1)S(1)}, bf16[528,128]{1,0:T(8,128)(2,1)S(1)}, u32[]{:S(2)}, u32[]{:S(2)}) collective-permute-start(bf16[528,128]{1,0:T(8,128)(2,1)S(1)} %get-tuple-element.47), channel_id=1, source_target_pairs={{0,2},{2,0},{4,6},{6,4},{8,10},{10,8},{12,14},{14,12},{1,3},{3,1},... | collective-permute-start | bytes 405512 | tf_op jit(solution)/shard_map/ppermute | solution.py:399
  46.0 5.8 %collective-permute-start.13 = (bf16[32,512]{1,0:T(8,128)(2,1)S(1)}, bf16[32,512]{1,0:T(8,128)(2,1)S(1)}, u32[]{:S(2)}, u32[]{:S(2)}) collective-permute-start(bf16[32,512]{1,0:T(8,128)(2,1)S(1)} %get-tuple-element.51), channel_id=1, source_target_pairs={{0,12},{2,14},{4,8},{6,10},{8,4},{10,6},{12,0},{14,2},{1,13},{3,15... | collective-permute-start | bytes 98312 | tf_op jit(solution)/shard_map/ppermute | solution.py:390
  47.9 4.8 %collective-permute-start.14 = (bf16[32,512]{1,0:T(8,128)(2,1)S(1)}, bf16[32,512]{1,0:T(8,128)(2,1)S(1)}, u32[]{:S(2)}, u32[]{:S(2)}) collective-permute-start(bf16[32,512]{1,0:T(8,128)(2,1)S(1)} %get-tuple-element.52), channel_id=1, source_target_pairs={{0,8},{2,10},{4,12},{6,14},{8,0},{10,2},{12,4},{14,6},{1,9},{3,11}... | collective-permute-start | bytes 98312 | tf_op jit(solution)/shard_map/ppermute | solution.py:390
  48.0 4.8 %collective-permute-start.15 = (bf16[32,512]{1,0:T(8,128)(2,1)S(1)}, bf16[32,512]{1,0:T(8,128)(2,1)S(1)}, u32[]{:S(2)}, u32[]{:S(2)}) collective-permute-start(bf16[32,512]{1,0:T(8,128)(2,1)S(1)} %get-tuple-element.53), channel_id=1, source_target_pairs={{0,4},{2,6},{4,0},{6,2},{8,12},{10,14},{12,8},{14,10},{1,5},{3,7},... | collective-permute-start | bytes 98312 | tf_op jit(solution)/shard_map/ppermute | solution.py:390

commit v18 on v17

--- a/solution.py
+++ b/solution.py
@@ -160,8 +160,8 @@
 
 
 def first_kernel(columns, widths, holders, own, other, right, left, *rest):
-    *pieces, stay, start, block_vmem = rest
-    half = stay.shape[1]
+    *pieces, start, block_vmem = rest
+    half = start.shape[2]
     slot = lax.broadcasted_iota(jnp.int32, widths.shape, 1)
     mine = jnp.where(slot == lax.axis_index("sec"), holders[...], 0)
     sector = jnp.sum(mine, axis=1, keepdims=True)
@@ -170,14 +170,16 @@
         live = h * half + columns[0:1, :] < width
         start[h] = jnp.where(live, part, jnp.zeros_like(part))
     vector = jnp.concatenate([start[0], start[1]], axis=1)
-    for term in (1, 2, 0):
+    for term in (1, 2):
         block = apply_term(right, left[0, term], vector, term).astype(jnp.bfloat16)
-        if term == 0:
-            stay[...] = block
-        else:
-            block_vmem[...] = block.reshape(block_vmem.shape)
-            for step, piece in zip(STEPS, pieces):
-                piece[term - 1] = block_vmem[own_place() ^ step]
+        block_vmem[...] = block.reshape(block_vmem.shape)
+        for step, piece in zip(STEPS, pieces):
+            piece[term - 1] = block_vmem[own_place() ^ step]
+
+
+def stay_kernel(vector, right, left, stay):
+    block = apply_term(right, left[0, 0], jnp.concatenate([vector[0], vector[1]], axis=1), 0)
+    stay[...] = block.astype(stay.dtype)
 
 
 def line_targets(plan, places):
@@ -245,8 +247,8 @@
 
 
 def second_kernel(start, own, other, right, left, *rest):
-    *pieces, stay, block_vmem = rest
-    half = stay.shape[1]
+    *pieces, deflated_out, block_vmem = rest
+    half = start.shape[2]
     rows = block_vmem.shape[1]
     chunks = half // LANES
     basis = [start[h].astype(jnp.float32) for h in range(2)]
@@ -256,21 +258,20 @@
     quotient = jnp.where(norm > 0, overlap / jnp.where(norm > 0, norm, 1.0), 0.0)
     deflated = [firsts[h] - quotient * basis[h] for h in range(2)]
     rest_norm = total_of(deflated[0] * deflated[0]) + total_of(deflated[1] * deflated[1])
+    for h in range(2):
+        deflated_out[h] = deflated[h].astype(jnp.bfloat16)
     vector = jnp.concatenate(deflated, axis=1).astype(jnp.bfloat16)
     tag = make_tag((overlap, norm, quotient, rest_norm), lax.axis_index("sec"))
     for piece in pieces:
         piece[pl.ds(2 * chunks * rows, TAG), :] = tag
-    for term in (1, 2, 0):
+    for term in (1, 2):
         block = apply_term(right, left[0, term], vector, term)
-        if term == 0:
-            stay[...] = block
-        else:
-            block_vmem[...] = block.astype(jnp.bfloat16).reshape(block_vmem.shape)
-            for step, piece in zip(STEPS, pieces):
-                part = block_vmem[own_place() ^ step]
-                for c in range(chunks):
-                    place = pl.ds(((term - 1) * chunks + c) * rows, rows)
-                    piece[place, :] = part[:, c * LANES : (c + 1) * LANES]
+        block_vmem[...] = block.astype(jnp.bfloat16).reshape(block_vmem.shape)
+        for step, piece in zip(STEPS, pieces):
+            part = block_vmem[own_place() ^ step]
+            for c in range(chunks):
+                place = pl.ds(((term - 1) * chunks + c) * rows, rows)
+                piece[place, :] = part[:, c * LANES : (c + 1) * LANES]
 
 
 def read_tag(tag):
@@ -428,8 +429,8 @@
     both = jax.ShapeDtypeStruct((2, right_dim, half), jnp.bfloat16)
     number = jax.ShapeDtypeStruct((8, half), jnp.int32)
     columns = call(columns_kernel, [], number, flops=4 << 30)()
-    *pieces, stay, start_full = call(
-        first_kernel, [VMEM] * 7, (pair,) * places + (block, both), split, dots
+    *pieces, start_full = call(
+        first_kernel, [VMEM] * 7, (pair,) * places + (both,), split, dots
     )(
         columns,
         widths[None],
@@ -440,6 +441,7 @@
         left_env,
     )
     old = along_line(pieces, slots)
+    stay = call(stay_kernel, [VMEM] * 3, block, flops=dots // 3)(start_full, right_env, left_env)
     old_keep, cross = call(
         merge_kernel, [VMEM] * (1 + places), (singles, singles), tables[:1]
     )(plan, *old)
@@ -449,10 +451,11 @@
         plan, stay, *along_line(joined, slots)
     )
 
-    *pieces, stay_2 = call(
-        second_kernel, [VMEM] * 5, (tagged,) * places + (wide,), split, dots
+    *pieces, deflated = call(
+        second_kernel, [VMEM] * 5, (tagged,) * places + (both,), split, dots
     )(start_full, first, other_core(first), right_env, left_env)
     new = along_line(pieces, slots)
+    stay_2 = call(stay_kernel, [VMEM] * 3, wide, flops=dots // 3)(deflated, right_env, left_env)
     keep, cross, tag = call(
         mix_kernel, [VMEM] * (1 + 2 * places), (wides, crossing, label), tables
     )(plan, *old, *new)

time: 53.7 us -> 53.2 us (level)
  waiting for transfers between devices: 24.6 us -> 23.8 us
    ppermute x12, waiting for transfers between devices: 14.5 us -> 13.7 us  [along_line(): sent.append(lax.ppermute(piece, 'sec', pairs) if step else piece)]
    pallas_call x2 -> x4, Pallas kernels: 2.41 us -> 2.75 us  [the longest x1 1.03 us: on_device(): call(second_kernel, [VMEM] * 5, (tagged,) * places + (both,), split, dots)]
  transfers between devices with their start and end apart: 16 -> 16, of which waited for: 12 -> 12; matrix products, arithmetic and copies ran while one was open for 0% -> 0% of each run, Pallas kernels for 1% -> 3%
where the time goes in v18:
time: 53.2 us; the launch traced here: 53.1 us
  waiting for transfers between devices  23.8 us (45%)
  starting transfers between devices  22.9 us (43%)
  Pallas kernels  5.45 us (10%)
  between operations  0.76 us (1%)
    ppermute x12, starting transfers between devices, along_line(): sent.append(lax.ppermute(piece, 'sec', pairs) if step else piece)  19.1 us
    ppermute x12, waiting for transfers between devices, along_line(): sent.append(lax.ppermute(piece, 'sec', pairs) if step else piece)  13.7 us
    ppermute x2, waiting for transfers between devices, across(): lax.ppermute(piece, 'sec', [(slot, slot ^ 1) for slot in range(slots)])  7.63 us
    ppermute x2, starting transfers between devices, across(): lax.ppermute(piece, 'sec', [(slot, slot ^ 1) for slot in range(slots)])  3.17 us
    ppermute x2, waiting for transfers between devices, other_core(): return lax.ppermute(block, 'env', [(0, 1), (1, 0)])  2.53 us
  transfers between devices with their start and end apart: 16, of which 12 were waited for; matrix products, arithmetic and copies ran while one was open for 0% of the time, Pallas kernels for 3%

profile of v18, /device:TPU:0, one launch (start us, length us, event | category | flops | bytes accessed | tf_op | source)
XLA Modules:
  0.0 53.1 jit_solution(17059525199530713112)
XLA Ops:
  0.7 0.5 collective-permute-start
  1.2 1.2 %collective-permute-done.other = bf16[128,512]{1,0:T(8,128)(2,1)S(1)} collective-permute-done((bf16[128,512]{1,0:T(8,128)(2,1)}, bf16[128,512]{1,0:T(8,128)(2,1)S(1)}, u32[]{:S(2)}, u32[]{:S(2)}) %collective-permute-start) | collective-permute-done | bytes 131104 | tf_op jit(solution)/shard_map/ppermute | solution.py:396
  2.5 0.9 %shard_map.70 = (bf16[2,32,512]{2,1,0:T(8,128)(2,1)S(1)}, bf16[2,32,512]{2,1,0:T(8,128)(2,1)S(1)}, bf16[2,32,512]{2,1,0:T(8,128)(2,1)S(1)}, bf16[2,32,512]{2,1,0:T(8,128)(2,1)S(1)}, bf16[2,128,512]{2,1,0:T(8,128)(2,1)S(1)}) custom-call(s32[8,512]{1,0:T(8,128)S(1)} %shard_map.69.columns, s32[1,8]{1,0:T(1,128)S(1)} %bitcast.7, s32[1,8]{1,0:T(1,128)S(1)} %bitcast.8, ...), custom_call_target="tpu_custom_call" | custom-call | flops 452984832 | bytes 262144 | tf_op jit(solution)/shard_map/pallas_call | solution.py:432
  3.4 5.1 %collective-permute-start.1 = (bf16[2,32,512]{2,1,0:T(8,128)(2,1)S(1)}, bf16[2,32,512]{2,1,0:T(8,128)(2,1)S(1)}, u32[]{:S(2)}, u32[]{:S(2)}) collective-permute-start(bf16[2,32,512]{2,1,0:T(8,128)(2,1)S(1)} %get-tuple-element.29), channel_id=1, source_target_pairs={{0,12},{2,14},{4,8},{6,10},{8,4},{10,6},{12,0},{14,2},{1,13},{3,15... | collective-permute-start | bytes 196616 | tf_op jit(solution)/shard_map/ppermute | solution.py:391
  8.6 0.6 %collective-permute-start.3 = (bf16[2,32,512]{2,1,0:T(8,128)(2,1)S(1)}, bf16[2,32,512]{2,1,0:T(8,128)(2,1)S(1)}, u32[]{:S(2)}, u32[]{:S(2)}) collective-permute-start(bf16[2,32,512]{2,1,0:T(8,128)(2,1)S(1)} %get-tuple-element.31), channel_id=1, source_target_pairs={{0,4},{2,6},{4,0},{6,2},{8,12},{10,14},{12,8},{14,10},{1,5},{3,7},... | collective-permute-start | bytes 196616 | tf_op jit(solution)/shard_map/ppermute | solution.py:391
  9.2 0.6 %shard_map.68.plan = s32[8,128]{1,0:T(8,128)S(1)} custom-call(s32[8]{0:T(128)S(1)} %copy-done.3, s32[8]{0:T(128)S(1)} %copy-done.4), custom_call_target="tpu_custom_call" | custom-call | bytes 262144 | tf_op jit(solution)/shard_map/pallas_call | solution.py:428
  9.8 1.2 %collective-permute-done.1.rest_1_ = bf16[2,32,512]{2,1,0:T(8,128)(2,1)S(1)} collective-permute-done((bf16[2,32,512]{2,1,0:T(8,128)(2,1)S(1)}, bf16[2,32,512]{2,1,0:T(8,128)(2,1)S(1)}, u32[]{:S(2)}, u32[]{:S(2)}) %collective-permute-start.1) | collective-permute-done | bytes 65568 | tf_op jit(solution)/shard_map/ppermute | solution.py:391
  11.0 3.2 %collective-permute-done.2.rest_2_ = bf16[2,32,512]{2,1,0:T(8,128)(2,1)S(1)} collective-permute-done((bf16[2,32,512]{2,1,0:T(8,128)(2,1)S(1)}, bf16[2,32,512]{2,1,0:T(8,128)(2,1)S(1)}, u32[]{:S(2)}, u32[]{:S(2)}) %collective-permute-start.2) | collective-permute-done | bytes 65568 | tf_op jit(solution)/shard_map/ppermute | solution.py:391
  14.6 1.6 %collective-permute-start.4 = (bf16[4,32,512]{2,1,0:T(8,128)(2,1)S(1)}, bf16[4,32,512]{2,1,0:T(8,128)(2,1)S(1)}, u32[]{:S(2)}, u32[]{:S(2)}) collective-permute-start(bf16[4,32,512]{2,1,0:T(8,128)(2,1)S(1)} %get-tuple-element.34), channel_id=1, source_target_pairs={{0,2},{2,0},{4,6},{6,4},{8,10},{10,8},{12,14},{14,12},{1,3},{3,1},... | collective-permute-start | bytes 393224 | tf_op jit(solution)/shard_map/ppermute | solution.py:400
  16.1 3.6 %collective-permute-done.4.arrived.old_arrived = bf16[4,32,512]{2,1,0:T(8,128)(2,1)S(1)} collective-permute-done((bf16[4,32,512]{2,1,0:T(8,128)(2,1)S(1)}, bf16[4,32,512]{2,1,0:T(8,128)(2,1)S(1)}, u32[]{:S(2)}, u32[]{:S(2)}) %collective-permute-start.4) | collective-permute-done | bytes 131104 | tf_op jit(solution)/shard_map/ppermute | solution.py:400
  19.8 2.6 %collective-permute-start.5 = (bf16[32,512]{1,0:T(8,128)(2,1)S(1)}, bf16[32,512]{1,0:T(8,128)(2,1)S(1)}, u32[]{:S(2)}, u32[]{:S(2)}) collective-permute-start(bf16[32,512]{1,0:T(8,128)(2,1)S(1)} %get-tuple-element.36), channel_id=1, source_target_pairs={{0,12},{2,14},{4,8},{6,10},{8,4},{10,6},{12,0},{14,2},{1,13},{3,15... | collective-permute-start | bytes 98312 | tf_op jit(solution)/shard_map/ppermute | solution.py:391
  22.4 1.8 %collective-permute-start.7 = (bf16[32,512]{1,0:T(8,128)(2,1)S(1)}, bf16[32,512]{1,0:T(8,128)(2,1)S(1)}, u32[]{:S(2)}, u32[]{:S(2)}) collective-permute-start(bf16[32,512]{1,0:T(8,128)(2,1)S(1)} %get-tuple-element.38), channel_id=1, source_target_pairs={{0,4},{2,6},{4,0},{6,2},{8,12},{10,14},{12,8},{14,10},{1,5},{3,7},... | collective-permute-start | bytes 98312 | tf_op jit(solution)/shard_map/ppermute | solution.py:391
  24.2 0.4 shard_map.71.stay
  24.6 0.9 %collective-permute-done.5.rest_1_ = bf16[32,512]{1,0:T(8,128)(2,1)S(1)} collective-permute-done((bf16[32,512]{1,0:T(8,128)(2,1)S(1)}, bf16[32,512]{1,0:T(8,128)(2,1)S(1)}, u32[]{:S(2)}, u32[]{:S(2)}) %collective-permute-start.5) | collective-permute-done | bytes 32800 | tf_op jit(solution)/shard_map/ppermute | solution.py:391
  25.5 1.7 %collective-permute-done.6.rest_2_ = bf16[32,512]{1,0:T(8,128)(2,1)S(1)} collective-permute-done((bf16[32,512]{1,0:T(8,128)(2,1)S(1)}, bf16[32,512]{1,0:T(8,128)(2,1)S(1)}, u32[]{:S(2)}, u32[]{:S(2)}) %collective-permute-start.6) | collective-permute-done | bytes 32800 | tf_op jit(solution)/shard_map/ppermute | solution.py:391
  27.4 1.3 %collective-permute-done.8.other = bf16[128,512]{1,0:T(8,128)(2,1)S(1)} collective-permute-done((bf16[128,512]{1,0:T(8,128)(2,1)S(1)}, bf16[128,512]{1,0:T(8,128)(2,1)S(1)}, u32[]{:S(2)}, u32[]{:S(2)}) %collective-permute-start.8) | collective-permute-done | bytes 131104 | tf_op jit(solution)/shard_map/ppermute | solution.py:396
  28.7 1.0 %shard_map.75 = (bf16[272,128]{1,0:T(8,128)(2,1)S(1)}, bf16[272,128]{1,0:T(8,128)(2,1)S(1)}, bf16[272,128]{1,0:T(8,128)(2,1)S(1)}, bf16[272,128]{1,0:T(8,128)(2,1)S(1)}, bf16[2,128,512]{2,1,0:T(8,128)(2,1)S(1)}) custom-call(bf16[2,128,512]{2,1,0:T(8,128)(2,1)S(1)} %get-tuple-element.32.vector.start, bf16[128,512]{1,0:T(8,128)(2,1)S(1)} %shard_map.74.own.first, ...), custom_call_target="tpu_custom_call" | custom-call | flops 452984832 | bytes 262144 | tf_op jit(solution)/shard_map/pallas_call | solution.py:454
  29.7 1.9 %collective-permute-start.9 = (bf16[272,128]{1,0:T(8,128)(2,1)S(1)}, bf16[272,128]{1,0:T(8,128)(2,1)S(1)}, u32[]{:S(2)}, u32[]{:S(2)}) collective-permute-start(bf16[272,128]{1,0:T(8,128)(2,1)S(1)} %get-tuple-element.40), channel_id=1, source_target_pairs={{0,12},{2,14},{4,8},{6,10},{8,4},{10,6},{12,0},{14,2},{1,13},{3,15... | collective-permute-start | bytes 208904 | tf_op jit(solution)/shard_map/ppermute | solution.py:391
  31.6 0.6 %collective-permute-start.10 = (bf16[272,128]{1,0:T(8,128)(2,1)S(1)}, bf16[272,128]{1,0:T(8,128)(2,1)S(1)}, u32[]{:S(2)}, u32[]{:S(2)}) collective-permute-start(bf16[272,128]{1,0:T(8,128)(2,1)S(1)} %get-tuple-element.41), channel_id=1, source_target_pairs={{0,8},{2,10},{4,12},{6,14},{8,0},{10,2},{12,4},{14,6},{1,9},{3,11}... | collective-permute-start | bytes 208904 | tf_op jit(solution)/shard_map/ppermute | solution.py:391
  32.2 2.0 %collective-permute-start.11 = (bf16[272,128]{1,0:T(8,128)(2,1)S(1)}, bf16[272,128]{1,0:T(8,128)(2,1)S(1)}, u32[]{:S(2)}, u32[]{:S(2)}) collective-permute-start(bf16[272,128]{1,0:T(8,128)(2,1)S(1)} %get-tuple-element.42), channel_id=1, source_target_pairs={{0,4},{2,6},{4,0},{6,2},{8,12},{10,14},{12,8},{14,10},{1,5},{3,7},... | collective-permute-start | bytes 208904 | tf_op jit(solution)/shard_map/ppermute | solution.py:391
  34.2 2.5 %collective-permute-done.9.rest_5_ = bf16[272,128]{1,0:T(8,128)(2,1)S(1)} collective-permute-done((bf16[272,128]{1,0:T(8,128)(2,1)S(1)}, bf16[272,128]{1,0:T(8,128)(2,1)S(1)}, u32[]{:S(2)}, u32[]{:S(2)}) %collective-permute-start.9) | collective-permute-done | bytes 69664 | tf_op jit(solution)/shard_map/ppermute | solution.py:391
  36.7 2.3 %collective-permute-done.10.rest_6_ = bf16[272,128]{1,0:T(8,128)(2,1)S(1)} collective-permute-done((bf16[272,128]{1,0:T(8,128)(2,1)S(1)}, bf16[272,128]{1,0:T(8,128)(2,1)S(1)}, u32[]{:S(2)}, u32[]{:S(2)}) %collective-permute-start.10) | collective-permute-done | bytes 69664 | tf_op jit(solution)/shard_map/ppermute | solution.py:391
  39.0 0.5 shard_map.76
  39.5 1.6 %collective-permute-start.12 = (bf16[528,128]{1,0:T(8,128)(2,1)S(1)}, bf16[528,128]{1,0:T(8,128)(2,1)S(1)}, u32[]{:S(2)}, u32[]{:S(2)}) collective-permute-start(bf16[528,128]{1,0:T(8,128)(2,1)S(1)} %get-tuple-element.45), channel_id=1, source_target_pairs={{0,2},{2,0},{4,6},{6,4},{8,10},{10,8},{12,14},{14,12},{1,3},{3,1},... | collective-permute-start | bytes 405512 | tf_op jit(solution)/shard_map/ppermute | solution.py:400
  41.1 4.1 %collective-permute-done.12.arrived = bf16[528,128]{1,0:T(8,128)(2,1)S(1)} collective-permute-done((bf16[528,128]{1,0:T(8,128)(2,1)S(1)}, bf16[528,128]{1,0:T(8,128)(2,1)S(1)}, u32[]{:S(2)}, u32[]{:S(2)}) %collective-permute-start.12) | collective-permute-done | bytes 135200 | tf_op jit(solution)/shard_map/ppermute | solution.py:400
  45.1 0.4 shard_map.77
  45.5 2.0 %collective-permute-start.13 = (bf16[32,512]{1,0:T(8,128)(2,1)S(1)}, bf16[32,512]{1,0:T(8,128)(2,1)S(1)}, u32[]{:S(2)}, u32[]{:S(2)}) collective-permute-start(bf16[32,512]{1,0:T(8,128)(2,1)S(1)} %get-tuple-element.49), channel_id=1, source_target_pairs={{0,12},{2,14},{4,8},{6,10},{8,4},{10,6},{12,0},{14,2},{1,13},{3,15... | collective-permute-start | bytes 98312 | tf_op jit(solution)/shard_map/ppermute | solution.py:391
  47.5 2.5 %collective-permute-start.15 = (bf16[32,512]{1,0:T(8,128)(2,1)S(1)}, bf16[32,512]{1,0:T(8,128)(2,1)S(1)}, u32[]{:S(2)}, u32[]{:S(2)}) collective-permute-start(bf16[32,512]{1,0:T(8,128)(2,1)S(1)} %get-tuple-element.51), channel_id=1, source_target_pairs={{0,4},{2,6},{4,0},{6,2},{8,12},{10,14},{12,8},{14,10},{1,5},{3,7},... | collective-permute-start | bytes 98312 | tf_op jit(solution)/shard_map/ppermute | solution.py:391
  50.0 0.4 shard_map.78.stay_2
  50.4 0.9 %collective-permute-done.13.rest_1_ = bf16[32,512]{1,0:T(8,128)(2,1)S(1)} collective-permute-done((bf16[32,512]{1,0:T(8,128)(2,1)S(1)}, bf16[32,512]{1,0:T(8,128)(2,1)S(1)}, u32[]{:S(2)}, u32[]{:S(2)}) %collective-permute-start.13) | collective-permute-done | bytes 32800 | tf_op jit(solution)/shard_map/ppermute | solution.py:391
  51.3 1.0 %collective-permute-done.14.rest_2_ = bf16[32,512]{1,0:T(8,128)(2,1)S(1)} collective-permute-done((bf16[32,512]{1,0:T(8,128)(2,1)S(1)}, bf16[32,512]{1,0:T(8,128)(2,1)S(1)}, u32[]{:S(2)}, u32[]{:S(2)}) %collective-permute-start.14) | collective-permute-done | bytes 32800 | tf_op jit(solution)/shard_map/ppermute | solution.py:391
  52.3 0.8 %shard_map.79 = (bf16[128,512]{1,0:T(8,128)(2,1)}, bf16[128,512]{1,0:T(8,128)(2,1)}) custom-call(s32[8,128]{1,0:T(8,128)S(1)} %shard_map.68.plan, f32[8,128]{1,0:T(8,128)S(1)} %get-tuple-element.46.factors, bf16[128,512]{1,0:T(8,128)(2,1)S(1)} %shard_map.71.stay, f32[128,512]{1,0:T(8,128)S(1)} %shard_map.78.stay_2, ...), custom_call_target="tpu_custom_call" | custom-call | bytes 262144 | tf_op jit(solution)/shard_map/pallas_call | solution.py:465
  (22 shorter events, 0.7 us)
Async XLA Ops:
  0.6 1.9 %copy-start = (bf16[1,3,1024,512]{3,2,1,0:T(8,128)(2,1)S(1)}, bf16[1,3,1024,512]{3,2,1,0:T(8,128)(2,1)}, u32[]{:S(2)}) copy-start(bf16[1,3,1024,512]{3,2,1,0:T(8,128)(2,1)} %left.7) | copy-start | bytes 9437188
  0.6 1.9 %copy-start.1 = (bf16[3,128,128]{2,1,0:T(8,128)(2,1)S(1)}, bf16[3,128,128]{2,1,0:T(8,128)(2,1)}, u32[]{:S(2)}) copy-start(bf16[3,128,128]{2,1,0:T(8,128)(2,1)} %right.7) | copy-start | bytes 294916
  0.7 1.9 %copy-start.2 = (bf16[1,128,512]{2,1,0:T(8,128)(2,1)S(1)}, bf16[1,128,512]{2,1,0:T(8,128)(2,1)}, u32[]{:S(2)}) copy-start(bf16[1,128,512]{2,1,0:T(8,128)(2,1)} %param.5) | copy-start | bytes 393220
  0.7 1.9 %copy-start.3 = (s32[8]{0:T(128)S(1)}, s32[8]{0:T(128)}, u32[]{:S(2)}) copy-start(s32[8]{0:T(128)} %widths.1) | copy-start | bytes 100
  0.7 1.9 %copy-start.4 = (s32[8]{0:T(128)S(1)}, s32[8]{0:T(128)}, u32[]{:S(2)}) copy-start(s32[8]{0:T(128)} %holders.1) | copy-start | bytes 100
  0.7 1.7 %collective-permute-start = (bf16[128,512]{1,0:T(8,128)(2,1)}, bf16[128,512]{1,0:T(8,128)(2,1)S(1)}, u32[]{:S(2)}, u32[]{:S(2)}) collective-permute-start(bf16[128,512]{1,0:T(8,128)(2,1)} %bitcast.5), channel_id=1, source_target_pairs={{0,1},{1,0},{2,3},{3,2},{4,5},{5,4},{6,7},{7,6},{8,9},{9,8},{10,11... | collective-permute-start | bytes 393224 | tf_op jit(solution)/shard_map/ppermute | solution.py:396
  3.4 7.6 %collective-permute-start.1 = (bf16[2,32,512]{2,1,0:T(8,128)(2,1)S(1)}, bf16[2,32,512]{2,1,0:T(8,128)(2,1)S(1)}, u32[]{:S(2)}, u32[]{:S(2)}) collective-permute-start(bf16[2,32,512]{2,1,0:T(8,128)(2,1)S(1)} %get-tuple-element.29), channel_id=1, source_target_pairs={{0,12},{2,14},{4,8},{6,10},{8,4},{10,6},{12,0},{14,2},{1,13},{3,15... | collective-permute-start | bytes 196616 | tf_op jit(solution)/shard_map/ppermute | solution.py:391
  8.6 5.7 %collective-permute-start.2 = (bf16[2,32,512]{2,1,0:T(8,128)(2,1)S(1)}, bf16[2,32,512]{2,1,0:T(8,128)(2,1)S(1)}, u32[]{:S(2)}, u32[]{:S(2)}) collective-permute-start(bf16[2,32,512]{2,1,0:T(8,128)(2,1)S(1)} %get-tuple-element.30), channel_id=1, source_target_pairs={{0,8},{2,10},{4,12},{6,14},{8,0},{10,2},{12,4},{14,6},{1,9},{3,11}... | collective-permute-start | bytes 196616 | tf_op jit(solution)/shard_map/ppermute | solution.py:391
  8.6 5.7 %collective-permute-start.3 = (bf16[2,32,512]{2,1,0:T(8,128)(2,1)S(1)}, bf16[2,32,512]{2,1,0:T(8,128)(2,1)S(1)}, u32[]{:S(2)}, u32[]{:S(2)}) collective-permute-start(bf16[2,32,512]{2,1,0:T(8,128)(2,1)S(1)} %get-tuple-element.31), channel_id=1, source_target_pairs={{0,4},{2,6},{4,0},{6,2},{8,12},{10,14},{12,8},{14,10},{1,5},{3,7},... | collective-permute-start | bytes 196616 | tf_op jit(solution)/shard_map/ppermute | solution.py:391
  14.6 5.1 %collective-permute-start.4 = (bf16[4,32,512]{2,1,0:T(8,128)(2,1)S(1)}, bf16[4,32,512]{2,1,0:T(8,128)(2,1)S(1)}, u32[]{:S(2)}, u32[]{:S(2)}) collective-permute-start(bf16[4,32,512]{2,1,0:T(8,128)(2,1)S(1)} %get-tuple-element.34), channel_id=1, source_target_pairs={{0,2},{2,0},{4,6},{6,4},{8,10},{10,8},{12,14},{14,12},{1,3},{3,1},... | collective-permute-start | bytes 393224 | tf_op jit(solution)/shard_map/ppermute | solution.py:400
  19.8 5.8 %collective-permute-start.5 = (bf16[32,512]{1,0:T(8,128)(2,1)S(1)}, bf16[32,512]{1,0:T(8,128)(2,1)S(1)}, u32[]{:S(2)}, u32[]{:S(2)}) collective-permute-start(bf16[32,512]{1,0:T(8,128)(2,1)S(1)} %get-tuple-element.36), channel_id=1, source_target_pairs={{0,12},{2,14},{4,8},{6,10},{8,4},{10,6},{12,0},{14,2},{1,13},{3,15... | collective-permute-start | bytes 98312 | tf_op jit(solution)/shard_map/ppermute | solution.py:391
  22.4 4.8 %collective-permute-start.6 = (bf16[32,512]{1,0:T(8,128)(2,1)S(1)}, bf16[32,512]{1,0:T(8,128)(2,1)S(1)}, u32[]{:S(2)}, u32[]{:S(2)}) collective-permute-start(bf16[32,512]{1,0:T(8,128)(2,1)S(1)} %get-tuple-element.37), channel_id=1, source_target_pairs={{0,8},{2,10},{4,12},{6,14},{8,0},{10,2},{12,4},{14,6},{1,9},{3,11}... | collective-permute-start | bytes 98312 | tf_op jit(solution)/shard_map/ppermute | solution.py:391
  22.4 4.8 %collective-permute-start.7 = (bf16[32,512]{1,0:T(8,128)(2,1)S(1)}, bf16[32,512]{1,0:T(8,128)(2,1)S(1)}, u32[]{:S(2)}, u32[]{:S(2)}) collective-permute-start(bf16[32,512]{1,0:T(8,128)(2,1)S(1)} %get-tuple-element.38), channel_id=1, source_target_pairs={{0,4},{2,6},{4,0},{6,2},{8,12},{10,14},{12,8},{14,10},{1,5},{3,7},... | collective-permute-start | bytes 98312 | tf_op jit(solution)/shard_map/ppermute | solution.py:391
  27.3 1.4 %collective-permute-start.8 = (bf16[128,512]{1,0:T(8,128)(2,1)S(1)}, bf16[128,512]{1,0:T(8,128)(2,1)S(1)}, u32[]{:S(2)}, u32[]{:S(2)}) collective-permute-start(bf16[128,512]{1,0:T(8,128)(2,1)S(1)} %shard_map.74.own.first), channel_id=1, source_target_pairs={{0,1},{1,0},{2,3},{3,2},{4,5},{5,4},{6,7},{7,6},{8,9},{9,8},{10,11... | collective-permute-start | bytes 393224 | tf_op jit(solution)/shard_map/ppermute | solution.py:396
  29.7 6.9 %collective-permute-start.9 = (bf16[272,128]{1,0:T(8,128)(2,1)S(1)}, bf16[272,128]{1,0:T(8,128)(2,1)S(1)}, u32[]{:S(2)}, u32[]{:S(2)}) collective-permute-start(bf16[272,128]{1,0:T(8,128)(2,1)S(1)} %get-tuple-element.40), channel_id=1, source_target_pairs={{0,12},{2,14},{4,8},{6,10},{8,4},{10,6},{12,0},{14,2},{1,13},{3,15... | collective-permute-start | bytes 208904 | tf_op jit(solution)/shard_map/ppermute | solution.py:391
  31.6 7.3 %collective-permute-start.10 = (bf16[272,128]{1,0:T(8,128)(2,1)S(1)}, bf16[272,128]{1,0:T(8,128)(2,1)S(1)}, u32[]{:S(2)}, u32[]{:S(2)}) collective-permute-start(bf16[272,128]{1,0:T(8,128)(2,1)S(1)} %get-tuple-element.41), channel_id=1, source_target_pairs={{0,8},{2,10},{4,12},{6,14},{8,0},{10,2},{12,4},{14,6},{1,9},{3,11}... | collective-permute-start | bytes 208904 | tf_op jit(solution)/shard_map/ppermute | solution.py:391
  32.2 6.8 %collective-permute-start.11 = (bf16[272,128]{1,0:T(8,128)(2,1)S(1)}, bf16[272,128]{1,0:T(8,128)(2,1)S(1)}, u32[]{:S(2)}, u32[]{:S(2)}) collective-permute-start(bf16[272,128]{1,0:T(8,128)(2,1)S(1)} %get-tuple-element.42), channel_id=1, source_target_pairs={{0,4},{2,6},{4,0},{6,2},{8,12},{10,14},{12,8},{14,10},{1,5},{3,7},... | collective-permute-start | bytes 208904 | tf_op jit(solution)/shard_map/ppermute | solution.py:391
  39.5 5.7 %collective-permute-start.12 = (bf16[528,128]{1,0:T(8,128)(2,1)S(1)}, bf16[528,128]{1,0:T(8,128)(2,1)S(1)}, u32[]{:S(2)}, u32[]{:S(2)}) collective-permute-start(bf16[528,128]{1,0:T(8,128)(2,1)S(1)} %get-tuple-element.45), channel_id=1, source_target_pairs={{0,2},{2,0},{4,6},{6,4},{8,10},{10,8},{12,14},{14,12},{1,3},{3,1},... | collective-permute-start | bytes 405512 | tf_op jit(solution)/shard_map/ppermute | solution.py:400
  45.5 5.8 %collective-permute-start.13 = (bf16[32,512]{1,0:T(8,128)(2,1)S(1)}, bf16[32,512]{1,0:T(8,128)(2,1)S(1)}, u32[]{:S(2)}, u32[]{:S(2)}) collective-permute-start(bf16[32,512]{1,0:T(8,128)(2,1)S(1)} %get-tuple-element.49), channel_id=1, source_target_pairs={{0,12},{2,14},{4,8},{6,10},{8,4},{10,6},{12,0},{14,2},{1,13},{3,15... | collective-permute-start | bytes 98312 | tf_op jit(solution)/shard_map/ppermute | solution.py:391
  47.5 4.8 %collective-permute-start.14 = (bf16[32,512]{1,0:T(8,128)(2,1)S(1)}, bf16[32,512]{1,0:T(8,128)(2,1)S(1)}, u32[]{:S(2)}, u32[]{:S(2)}) collective-permute-start(bf16[32,512]{1,0:T(8,128)(2,1)S(1)} %get-tuple-element.50), channel_id=1, source_target_pairs={{0,8},{2,10},{4,12},{6,14},{8,0},{10,2},{12,4},{14,6},{1,9},{3,11}... | collective-permute-start | bytes 98312 | tf_op jit(solution)/shard_map/ppermute | solution.py:391
  47.5 4.8 %collective-permute-start.15 = (bf16[32,512]{1,0:T(8,128)(2,1)S(1)}, bf16[32,512]{1,0:T(8,128)(2,1)S(1)}, u32[]{:S(2)}, u32[]{:S(2)}) collective-permute-start(bf16[32,512]{1,0:T(8,128)(2,1)S(1)} %get-tuple-element.51), channel_id=1, source_target_pairs={{0,4},{2,6},{4,0},{6,2},{8,12},{10,14},{12,8},{14,10},{1,5},{3,7},... | collective-permute-start | bytes 98312 | tf_op jit(solution)/shard_map/ppermute | solution.py:391

commit v19 on v18

--- a/solution.py
+++ b/solution.py
@@ -113,6 +113,7 @@
 TAG = 16
 LINES = 2
 STEPS = (0, 3, 2, 1)
+EARLY, LATE = (1, 2), (0, 3)
 
 
 def plan_kernel(widths, holders, plan, slot_of):
@@ -182,37 +183,45 @@
     stay[...] = block.astype(stay.dtype)
 
 
-def line_targets(plan, places):
+def line_targets(plan, part):
     line = lax.axis_index("sec") % LINES
+    places = len(STEPS)
     codes = [jnp.max(plan[2 + i : 3 + i, :]) for i in range(2)]
-    for place in range(places):
+    for index in part:
         for crossing in range(2):
-            target = place * LINES + (line ^ crossing)
+            target = (own_place() ^ STEPS[index]) * LINES + (line ^ crossing)
             entries = [(code >> (target * 4)) & (2 * LINES * places - 1) for code in codes]
             source = [entry & (LINES * places - 1) for entry in entries]
             here = [
                 (entry >= LINES * places) & (slot % LINES == line)
                 for entry, slot in zip(entries, source)
             ]
-            yield place, crossing, here, source
-
-
-def merge_kernel(plan, *rest):
-    *pieces, keep, cross, table = rest
-    for step, piece in zip(STEPS, pieces):
-        table[own_place() ^ step] = piece[...]
-    for place, crossing, here, source in line_targets(plan, keep.shape[0]):
+            yield index, crossing, here, source
+
+
+def merge_targets(plan, part, table, keep, cross):
+    for index, crossing, here, source in line_targets(plan, part):
         total = 0.0
         for i in range(2):
             block = table[source[i] // LINES, i].astype(jnp.float32)
             total = total + jnp.where(here[i], block, 0.0)
-        (keep, cross)[crossing][place] = total.astype(jnp.bfloat16)
+        (keep, cross)[crossing][part.index(index)] = total.astype(jnp.bfloat16)
+
+
+def merge_early_kernel(plan, *rest):
+    *pieces, table, keep, cross = rest
+    for step, piece in zip(STEPS, pieces):
+        table[own_place() ^ step] = piece[...]
+    merge_targets(plan, EARLY, table, keep, cross)
+
+
+def merge_late_kernel(plan, table, keep, cross):
+    merge_targets(plan, LATE, table, keep, cross)
 
 
 def join_kernel(keep, arrived, *outs):
-    for step, out in zip(STEPS, outs):
-        place = own_place() ^ step
-        total = keep[place].astype(jnp.float32) + arrived[place].astype(jnp.float32)
+    for i, out in enumerate(outs):
+        total = keep[i].astype(jnp.float32) + arrived[i].astype(jnp.float32)
         out[...] = total.astype(jnp.bfloat16)
 
 
@@ -290,21 +299,21 @@
 
 
 def mix_kernel(plan, *rest):
-    keep, cross, tag_out, old, new = rest[-5:]
+    keep, early, late, tag_out, new = rest[-5:]
+    old, *pieces = rest[:-5]
     places, rows, half = keep.shape
     chunks = half // LANES
     tag = jnp.zeros((TAG, LANES), jnp.float32)
-    for i, step in enumerate(STEPS):
-        old[own_place() ^ step] = rest[i][...]
-        new[own_place() ^ step] = rest[places + i][...]
-        label = rest[places + i][pl.ds(2 * chunks * rows, TAG), :]
+    for step, piece in zip(STEPS, pieces):
+        new[own_place() ^ step] = piece[...]
+        label = piece[pl.ds(2 * chunks * rows, TAG), :]
         tag = tag + label.astype(jnp.float32)
     tag_out[...] = tag.astype(jnp.bfloat16)
-    cross[pl.ds(places * chunks * rows, TAG), :] = tag.astype(jnp.bfloat16)
+    early[pl.ds(len(EARLY) * chunks * rows, TAG), :] = tag.astype(jnp.bfloat16)
     overlaps, norms, quotients, _ = read_tag(tag)
     shifts = quotients - line_quotient(overlaps, norms, lax.axis_index("sec") % LINES)
     lane = lax.broadcasted_iota(jnp.int32, (1, LANES), 1)
-    for place, crossing, here, source in line_targets(plan, keep.shape[0]):
+    for index, crossing, here, source in line_targets(plan, range(places)):
         total = 0.0
         for i in range(2):
             where = source[i] // LINES
@@ -317,43 +326,56 @@
             total = total + jnp.where(here[i], block, 0.0)
         if crossing:
             total = total.astype(jnp.bfloat16)
+            out, part = (early, EARLY) if index in EARLY else (late, LATE)
             for c in range(chunks):
-                target = pl.ds((place * chunks + c) * rows, rows)
-                cross[target, :] = total[:, c * LANES : (c + 1) * LANES]
+                target = pl.ds((part.index(index) * chunks + c) * rows, rows)
+                out[target, :] = total[:, c * LANES : (c + 1) * LANES]
         else:
-            keep[place] = total
-
-
-def join_mixed_kernel(plan, tag_line, keep, arrived, old_keep, old_arrived, *rest):
+            keep[index] = total
+
+
+def join_early_kernel(plan, tag_line, keep, arrived, old_keep, old_arrived, *rest):
     *outs, factors = rest
     places, rows, half = keep.shape
-    chunks = half // LANES
     slots = places * LINES
     me = lax.axis_index("sec")
     live_count = places * rows * plan[1:2, 0:1].astype(jnp.float32)
     tag = tag_line[...].astype(jnp.float32)
-    tag = tag + arrived[pl.ds(places * chunks * rows, TAG), :].astype(jnp.float32)
+    tag = tag + arrived[pl.ds(arrived.shape[0] - TAG, TAG), :].astype(jnp.float32)
     overlaps, norms, quotients, rests = read_tag(tag)
     quotient = total_of(overlaps) / total_of(norms)
     lane = lax.broadcasted_iota(jnp.int32, (1, LANES), 1)
     shifts = jnp.where(lane < slots, quotients - quotient, 0.0)
     resid_norm = total_of(rests + shifts * shifts * norms)
     scale = lax.rsqrt(resid_norm / live_count + 1e-06)
-    row = lax.broadcasted_iota(jnp.int32, factors.shape, 0)
     own_shift = total_of(jnp.where(lane == me, shifts, 0.0))
-    factors[...] = jnp.where(row == 0, scale, scale * own_shift)
     line = me % LINES
     shift_here = line_quotient(overlaps, norms, line) - quotient
     shift_there = line_quotient(overlaps, norms, 1 - line) - quotient
-    for step, out in zip(STEPS, outs):
-        place = own_place() ^ step
-        starts = [pl.multiple_of((place * chunks + c) * rows, rows) for c in range(chunks)]
+    row = lax.broadcasted_iota(jnp.int32, factors.shape, 0)
+    values = jnp.where(row == 0, scale, scale * own_shift)
+    values = jnp.where(row == 2, shift_here, values)
+    factors[...] = jnp.where(row == 3, shift_there, values)
+    weights = (scale, shift_here, shift_there)
+    join_mixed(EARLY, weights, keep, arrived, old_keep, old_arrived, outs)
+
+
+def join_late_kernel(factors, keep, arrived, old_keep, old_arrived, *outs):
+    weights = [factors[i : i + 1, 0:1] for i in (0, 2, 3)]
+    join_mixed(LATE, weights, keep, arrived, old_keep, old_arrived, outs)
+
+
+def join_mixed(part, weights, keep, arrived, old_keep, old_arrived, outs):
+    scale, shift_here, shift_there = weights
+    rows, half = outs[0].shape
+    chunks = half // LANES
+    for i, index in enumerate(part):
         block = jnp.concatenate(
-            [arrived[pl.ds(start, rows), :] for start in starts], axis=1
+            [arrived[pl.ds((i * chunks + c) * rows, rows), :] for c in range(chunks)], axis=1
         ).astype(jnp.float32)
-        block = block + shift_there * old_arrived[place].astype(jnp.float32)
-        block = block + keep[place] + shift_here * old_keep[place].astype(jnp.float32)
-        out[...] = (scale * block).astype(jnp.bfloat16)
+        block = block + shift_there * old_arrived[i].astype(jnp.float32)
+        block = block + keep[index] + shift_here * old_keep[i].astype(jnp.float32)
+        outs[i][...] = (scale * block).astype(jnp.bfloat16)
 
 
 def final_kernel(plan, factors, stay, stay_2, first, *rest):
@@ -413,16 +435,18 @@
     wide = jax.ShapeDtypeStruct((right_dim, half), jnp.float32)
     pair = jax.ShapeDtypeStruct((2, rows, half), jnp.bfloat16)
     single = jax.ShapeDtypeStruct((rows, half), jnp.bfloat16)
-    singles = jax.ShapeDtypeStruct((places, rows, half), jnp.bfloat16)
     wides = jax.ShapeDtypeStruct((places, rows, half), jnp.float32)
     chunked = rows * half // LANES
     tagged = jax.ShapeDtypeStruct((2 * chunked + TAG, LANES), jnp.bfloat16)
-    crossing = jax.ShapeDtypeStruct((places * chunked + TAG, LANES), jnp.bfloat16)
+    twos = jax.ShapeDtypeStruct((2, rows, half), jnp.bfloat16)
+    early = jax.ShapeDtypeStruct((2 * chunked + TAG, LANES), jnp.bfloat16)
+    late = jax.ShapeDtypeStruct((2 * chunked, LANES), jnp.bfloat16)
     label = jax.ShapeDtypeStruct((TAG, LANES), jnp.bfloat16)
     factor_shape = jax.ShapeDtypeStruct((8, LANES), jnp.float32)
     plan_shape = jax.ShapeDtypeStruct((8, LANES), jnp.int32)
     split = [pltpu.VMEM((places, rows, half), jnp.bfloat16)]
-    tables = [pltpu.VMEM((places, *shape.shape), jnp.bfloat16) for shape in (pair, tagged)]
+    table_shape = jax.ShapeDtypeStruct((places, *pair.shape), jnp.bfloat16)
+    new_table = [pltpu.VMEM((places, *tagged.shape), jnp.bfloat16)]
 
     slot_table = [pltpu.SMEM((slots,), jnp.int32)]
     plan = call(plan_kernel, [SMEM, SMEM], plan_shape, slot_table)(widths, holders)
@@ -442,11 +466,15 @@
     )
     old = along_line(pieces, slots)
     stay = call(stay_kernel, [VMEM] * 3, block, flops=dots // 3)(start_full, right_env, left_env)
-    old_keep, cross = call(
-        merge_kernel, [VMEM] * (1 + places), (singles, singles), tables[:1]
+    table, keep_early, cross = call(
+        merge_early_kernel, [VMEM] * (1 + places), (table_shape, twos, twos)
     )(plan, *old)
-    old_arrived = across(cross, slots)
-    joined = call(join_kernel, [VMEM, VMEM], (single,) * places)(old_keep, old_arrived)
+    old_early = across(cross, slots)
+    keep_late, cross = call(merge_late_kernel, [VMEM] * 2, (twos, twos))(plan, table)
+    old_late = across(cross, slots)
+    far = call(join_kernel, [VMEM] * 2, (single,) * 2)(keep_early, old_early)
+    near = call(join_kernel, [VMEM] * 2, (single,) * 2)(keep_late, old_late)
+    joined = (near[0], *far, near[1])
     first = call(sum_kernel, [VMEM] * (2 + places), block)(
         plan, stay, *along_line(joined, slots)
     )
@@ -456,12 +484,17 @@
     )(start_full, first, other_core(first), right_env, left_env)
     new = along_line(pieces, slots)
     stay_2 = call(stay_kernel, [VMEM] * 3, wide, flops=dots // 3)(deflated, right_env, left_env)
-    keep, cross, tag = call(
-        mix_kernel, [VMEM] * (1 + 2 * places), (wides, crossing, label), tables
-    )(plan, *old, *new)
-    *joined, factors = call(
-        join_mixed_kernel, [VMEM] * 6, (single,) * places + (factor_shape,)
-    )(plan, tag, keep, across(cross, slots), old_keep, old_arrived)
+    keep, *cross, tag = call(
+        mix_kernel, [VMEM] * (2 + places), (wides, early, late, label), new_table
+    )(plan, table, *new)
+    new_early, new_late = (across(piece, slots) for piece in cross)
+    *far, factors = call(join_early_kernel, [VMEM] * 6, (single, single, factor_shape))(
+        plan, tag, keep, new_early, keep_early, old_early
+    )
+    near = call(join_late_kernel, [VMEM] * 5, (single,) * 2)(
+        factors, keep, new_late, keep_late, old_late
+    )
+    joined = (near[0], *far, near[1])
     second, first = call(final_kernel, [VMEM] * (5 + places), (block, block))(
         plan, factors, stay, stay_2, first, *along_line(joined, slots)
     )

time: 53.2 us -> 52.2 us (0.981)
  waiting for transfers between devices: 23.8 us -> 21.4 us
  starting transfers between devices: 22.9 us -> 24.1 us
    ppermute x2 -> x4, waiting for transfers between devices: 7.63 us -> 5.24 us  [across(): lax.ppermute(piece, 'sec', [(slot, slot ^ 1) for slot in range(slots)])]
    ppermute x2 -> x4, starting transfers between devices: 3.17 us -> 4.25 us  [across(): lax.ppermute(piece, 'sec', [(slot, slot ^ 1) for slot in range(slots)])]
    pallas_call x4 -> x7, Pallas kernels: 1.22 us -> 1.46 us  [the longest x1 0.49 us: on_device(): call(mix_kernel, [VMEM] * (2 + places), (wides, early, late, label), new_...]
  transfers between devices with their start and end apart: 16 -> 18, of which waited for: 12 -> 12; matrix products, arithmetic and copies ran while one was open for 0% -> 0% of each run, Pallas kernels for 3% -> 4%
where the time goes in v19:
time: 52.2 us; the launch traced here: 52.1 us
  starting transfers between devices  24.1 us (46%)
  waiting for transfers between devices  21.4 us (41%)
  Pallas kernels  5.7 us (11%)
  between operations  0.78 us (1%)
    ppermute x12, starting transfers between devices, along_line(): sent.append(lax.ppermute(piece, 'sec', pairs) if step else piece)  19.2 us
    ppermute x12, waiting for transfers between devices, along_line(): sent.append(lax.ppermute(piece, 'sec', pairs) if step else piece)  13.6 us
    ppermute x4, waiting for transfers between devices, across(): lax.ppermute(piece, 'sec', [(slot, slot ^ 1) for slot in range(slots)])  5.24 us
    ppermute x4, starting transfers between devices, across(): lax.ppermute(piece, 'sec', [(slot, slot ^ 1) for slot in range(slots)])  4.25 us
    ppermute x2, waiting for transfers between devices, other_core(): return lax.ppermute(block, 'env', [(0, 1), (1, 0)])  2.53 us
  transfers between devices with their start and end apart: 18, of which 12 were waited for; matrix products, arithmetic and copies ran while one was open for 0% of the time, Pallas kernels for 4%

profile of v19, /device:TPU:0, one launch (start us, length us, event | category | flops | bytes accessed | tf_op | source)
XLA Modules:
  0.0 52.1 jit_solution(2289446402513391604)
XLA Ops:
  0.7 0.5 collective-permute-start
  1.2 1.2 %collective-permute-done.other = bf16[128,512]{1,0:T(8,128)(2,1)S(1)} collective-permute-done((bf16[128,512]{1,0:T(8,128)(2,1)}, bf16[128,512]{1,0:T(8,128)(2,1)S(1)}, u32[]{:S(2)}, u32[]{:S(2)}) %collective-permute-start) | collective-permute-done | bytes 131104 | tf_op jit(solution)/shard_map/ppermute | solution.py:418
  2.5 0.9 %shard_map.70 = (bf16[2,32,512]{2,1,0:T(8,128)(2,1)S(1)}, bf16[2,32,512]{2,1,0:T(8,128)(2,1)S(1)}, bf16[2,32,512]{2,1,0:T(8,128)(2,1)S(1)}, bf16[2,32,512]{2,1,0:T(8,128)(2,1)S(1)}, bf16[2,128,512]{2,1,0:T(8,128)(2,1)S(1)}) custom-call(s32[8,512]{1,0:T(8,128)S(1)} %shard_map.69.columns, s32[1,8]{1,0:T(1,128)S(1)} %bitcast.7, s32[1,8]{1,0:T(1,128)S(1)} %bitcast.8, ...), custom_call_target="tpu_custom_call" | custom-call | flops 452984832 | bytes 262144 | tf_op jit(solution)/shard_map/pallas_call | solution.py:456
  3.4 5.1 %collective-permute-start.1 = (bf16[2,32,512]{2,1,0:T(8,128)(2,1)S(1)}, bf16[2,32,512]{2,1,0:T(8,128)(2,1)S(1)}, u32[]{:S(2)}, u32[]{:S(2)}) collective-permute-start(bf16[2,32,512]{2,1,0:T(8,128)(2,1)S(1)} %get-tuple-element.33), channel_id=1, source_target_pairs={{0,12},{2,14},{4,8},{6,10},{8,4},{10,6},{12,0},{14,2},{1,13},{3,15... | collective-permute-start | bytes 196616 | tf_op jit(solution)/shard_map/ppermute | solution.py:413
  8.6 0.6 %collective-permute-start.3 = (bf16[2,32,512]{2,1,0:T(8,128)(2,1)S(1)}, bf16[2,32,512]{2,1,0:T(8,128)(2,1)S(1)}, u32[]{:S(2)}, u32[]{:S(2)}) collective-permute-start(bf16[2,32,512]{2,1,0:T(8,128)(2,1)S(1)} %get-tuple-element.35), channel_id=1, source_target_pairs={{0,4},{2,6},{4,0},{6,2},{8,12},{10,14},{12,8},{14,10},{1,5},{3,7},... | collective-permute-start | bytes 196616 | tf_op jit(solution)/shard_map/ppermute | solution.py:413
  9.2 0.6 %shard_map.68.plan = s32[8,128]{1,0:T(8,128)S(1)} custom-call(s32[8]{0:T(128)S(1)} %copy-done.3, s32[8]{0:T(128)S(1)} %copy-done.4), custom_call_target="tpu_custom_call" | custom-call | bytes 262144 | tf_op jit(solution)/shard_map/pallas_call | solution.py:452
  9.8 1.2 %collective-permute-done.1.rest_1_ = bf16[2,32,512]{2,1,0:T(8,128)(2,1)S(1)} collective-permute-done((bf16[2,32,512]{2,1,0:T(8,128)(2,1)S(1)}, bf16[2,32,512]{2,1,0:T(8,128)(2,1)S(1)}, u32[]{:S(2)}, u32[]{:S(2)}) %collective-permute-start.1) | collective-permute-done | bytes 65568 | tf_op jit(solution)/shard_map/ppermute | solution.py:413
  11.0 3.2 %collective-permute-done.2.rest_2_ = bf16[2,32,512]{2,1,0:T(8,128)(2,1)S(1)} collective-permute-done((bf16[2,32,512]{2,1,0:T(8,128)(2,1)S(1)}, bf16[2,32,512]{2,1,0:T(8,128)(2,1)S(1)}, u32[]{:S(2)}, u32[]{:S(2)}) %collective-permute-start.2) | collective-permute-done | bytes 65568 | tf_op jit(solution)/shard_map/ppermute | solution.py:413
  14.5 1.5 %collective-permute-start.5 = (bf16[2,32,512]{2,1,0:T(8,128)(2,1)S(1)}, bf16[2,32,512]{2,1,0:T(8,128)(2,1)S(1)}, u32[]{:S(2)}, u32[]{:S(2)}) collective-permute-start(bf16[2,32,512]{2,1,0:T(8,128)(2,1)S(1)} %get-tuple-element.42), channel_id=1, source_target_pairs={{0,2},{2,0},{4,6},{6,4},{8,10},{10,8},{12,14},{14,12},{1,3},{3,1},... | collective-permute-start | bytes 196616 | tf_op jit(solution)/shard_map/ppermute | solution.py:422
  16.4 0.6 %collective-permute-start.4 = (bf16[2,32,512]{2,1,0:T(8,128)(2,1)S(1)}, bf16[2,32,512]{2,1,0:T(8,128)(2,1)S(1)}, u32[]{:S(2)}, u32[]{:S(2)}) collective-permute-start(bf16[2,32,512]{2,1,0:T(8,128)(2,1)S(1)} %get-tuple-element.39), channel_id=1, source_target_pairs={{0,2},{2,0},{4,6},{6,4},{8,10},{10,8},{12,14},{14,12},{1,3},{3,1},... | collective-permute-start | bytes 196616 | tf_op jit(solution)/shard_map/ppermute | solution.py:422
  17.0 2.3 %collective-permute-done.5.arrived.old_arrived = bf16[2,32,512]{2,1,0:T(8,128)(2,1)S(1)} collective-permute-done((bf16[2,32,512]{2,1,0:T(8,128)(2,1)S(1)}, bf16[2,32,512]{2,1,0:T(8,128)(2,1)S(1)}, u32[]{:S(2)}, u32[]{:S(2)}) %collective-permute-start.5) | collective-permute-done | bytes 65568 | tf_op jit(solution)/shard_map/ppermute | solution.py:422
  19.3 2.6 %collective-permute-start.6 = (bf16[32,512]{1,0:T(8,128)(2,1)S(1)}, bf16[32,512]{1,0:T(8,128)(2,1)S(1)}, u32[]{:S(2)}, u32[]{:S(2)}) collective-permute-start(bf16[32,512]{1,0:T(8,128)(2,1)S(1)} %get-tuple-element.43), channel_id=1, source_target_pairs={{0,12},{2,14},{4,8},{6,10},{8,4},{10,6},{12,0},{14,2},{1,13},{3,15... | collective-permute-start | bytes 98312 | tf_op jit(solution)/shard_map/ppermute | solution.py:413
  21.9 1.9 %collective-permute-start.8 = (bf16[32,512]{1,0:T(8,128)(2,1)S(1)}, bf16[32,512]{1,0:T(8,128)(2,1)S(1)}, u32[]{:S(2)}, u32[]{:S(2)}) collective-permute-start(bf16[32,512]{1,0:T(8,128)(2,1)S(1)} %get-tuple-element.45), channel_id=1, source_target_pairs={{0,4},{2,6},{4,0},{6,2},{8,12},{10,14},{12,8},{14,10},{1,5},{3,7},... | collective-permute-start | bytes 98312 | tf_op jit(solution)/shard_map/ppermute | solution.py:413
  23.8 0.4 shard_map.72.stay
  24.3 0.8 %collective-permute-done.6.rest_1_ = bf16[32,512]{1,0:T(8,128)(2,1)S(1)} collective-permute-done((bf16[32,512]{1,0:T(8,128)(2,1)S(1)}, bf16[32,512]{1,0:T(8,128)(2,1)S(1)}, u32[]{:S(2)}, u32[]{:S(2)}) %collective-permute-start.6) | collective-permute-done | bytes 32800 | tf_op jit(solution)/shard_map/ppermute | solution.py:413
  25.1 1.6 %collective-permute-done.7.rest_2_ = bf16[32,512]{1,0:T(8,128)(2,1)S(1)} collective-permute-done((bf16[32,512]{1,0:T(8,128)(2,1)S(1)}, bf16[32,512]{1,0:T(8,128)(2,1)S(1)}, u32[]{:S(2)}, u32[]{:S(2)}) %collective-permute-start.7) | collective-permute-done | bytes 32800 | tf_op jit(solution)/shard_map/ppermute | solution.py:413
  26.9 1.3 %collective-permute-done.9.other = bf16[128,512]{1,0:T(8,128)(2,1)S(1)} collective-permute-done((bf16[128,512]{1,0:T(8,128)(2,1)S(1)}, bf16[128,512]{1,0:T(8,128)(2,1)S(1)}, u32[]{:S(2)}, u32[]{:S(2)}) %collective-permute-start.9) | collective-permute-done | bytes 131104 | tf_op jit(solution)/shard_map/ppermute | solution.py:418
  28.2 1.0 %shard_map.77 = (bf16[272,128]{1,0:T(8,128)(2,1)S(1)}, bf16[272,128]{1,0:T(8,128)(2,1)S(1)}, bf16[272,128]{1,0:T(8,128)(2,1)S(1)}, bf16[272,128]{1,0:T(8,128)(2,1)S(1)}, bf16[2,128,512]{2,1,0:T(8,128)(2,1)S(1)}) custom-call(bf16[2,128,512]{2,1,0:T(8,128)(2,1)S(1)} %get-tuple-element.37.vector.start, bf16[128,512]{1,0:T(8,128)(2,1)S(1)} %shard_map.76.own.first, ...), custom_call_target="tpu_custom_call" | custom-call | flops 452984832 | bytes 262144 | tf_op jit(solution)/shard_map/pallas_call | solution.py:482
  29.3 2.0 %collective-permute-start.10 = (bf16[272,128]{1,0:T(8,128)(2,1)S(1)}, bf16[272,128]{1,0:T(8,128)(2,1)S(1)}, u32[]{:S(2)}, u32[]{:S(2)}) collective-permute-start(bf16[272,128]{1,0:T(8,128)(2,1)S(1)} %get-tuple-element.47), channel_id=1, source_target_pairs={{0,12},{2,14},{4,8},{6,10},{8,4},{10,6},{12,0},{14,2},{1,13},{3,15... | collective-permute-start | bytes 208904 | tf_op jit(solution)/shard_map/ppermute | solution.py:413
  31.2 0.6 %collective-permute-start.11 = (bf16[272,128]{1,0:T(8,128)(2,1)S(1)}, bf16[272,128]{1,0:T(8,128)(2,1)S(1)}, u32[]{:S(2)}, u32[]{:S(2)}) collective-permute-start(bf16[272,128]{1,0:T(8,128)(2,1)S(1)} %get-tuple-element.48), channel_id=1, source_target_pairs={{0,8},{2,10},{4,12},{6,14},{8,0},{10,2},{12,4},{14,6},{1,9},{3,11}... | collective-permute-start | bytes 208904 | tf_op jit(solution)/shard_map/ppermute | solution.py:413
  31.8 1.9 %collective-permute-start.12 = (bf16[272,128]{1,0:T(8,128)(2,1)S(1)}, bf16[272,128]{1,0:T(8,128)(2,1)S(1)}, u32[]{:S(2)}, u32[]{:S(2)}) collective-permute-start(bf16[272,128]{1,0:T(8,128)(2,1)S(1)} %get-tuple-element.49), channel_id=1, source_target_pairs={{0,4},{2,6},{4,0},{6,2},{8,12},{10,14},{12,8},{14,10},{1,5},{3,7},... | collective-permute-start | bytes 208904 | tf_op jit(solution)/shard_map/ppermute | solution.py:413
  33.7 2.4 %collective-permute-done.10.rest_2_ = bf16[272,128]{1,0:T(8,128)(2,1)S(1)} collective-permute-done((bf16[272,128]{1,0:T(8,128)(2,1)S(1)}, bf16[272,128]{1,0:T(8,128)(2,1)S(1)}, u32[]{:S(2)}, u32[]{:S(2)}) %collective-permute-start.10) | collective-permute-done | bytes 69664 | tf_op jit(solution)/shard_map/ppermute | solution.py:413
  36.1 2.5 %collective-permute-done.11.rest_3_ = bf16[272,128]{1,0:T(8,128)(2,1)S(1)} collective-permute-done((bf16[272,128]{1,0:T(8,128)(2,1)S(1)}, bf16[272,128]{1,0:T(8,128)(2,1)S(1)}, u32[]{:S(2)}, u32[]{:S(2)}) %collective-permute-start.11) | collective-permute-done | bytes 69664 | tf_op jit(solution)/shard_map/ppermute | solution.py:413
  38.6 0.5 shard_map.78
  39.1 1.3 %collective-permute-start.13 = (bf16[272,128]{1,0:T(8,128)(2,1)S(1)}, bf16[272,128]{1,0:T(8,128)(2,1)S(1)}, u32[]{:S(2)}, u32[]{:S(2)}) collective-permute-start(bf16[272,128]{1,0:T(8,128)(2,1)S(1)} %get-tuple-element.52), channel_id=1, source_target_pairs={{0,2},{2,0},{4,6},{6,4},{8,10},{10,8},{12,14},{14,12},{1,3},{3,1},... | collective-permute-start | bytes 208904 | tf_op jit(solution)/shard_map/ppermute | solution.py:422
  40.4 0.8 %collective-permute-start.14 = (bf16[256,128]{1,0:T(8,128)(2,1)S(1)}, bf16[256,128]{1,0:T(8,128)(2,1)S(1)}, u32[]{:S(2)}, u32[]{:S(2)}) collective-permute-start(bf16[256,128]{1,0:T(8,128)(2,1)S(1)} %get-tuple-element.55), channel_id=1, source_target_pairs={{0,2},{2,0},{4,6},{6,4},{8,10},{10,8},{12,14},{14,12},{1,3},{3,1},... | collective-permute-start | bytes 196616 | tf_op jit(solution)/shard_map/ppermute | solution.py:422
  41.2 2.9 %collective-permute-done.13.arrived = bf16[272,128]{1,0:T(8,128)(2,1)S(1)} collective-permute-done((bf16[272,128]{1,0:T(8,128)(2,1)S(1)}, bf16[272,128]{1,0:T(8,128)(2,1)S(1)}, u32[]{:S(2)}, u32[]{:S(2)}) %collective-permute-start.13) | collective-permute-done | bytes 69664 | tf_op jit(solution)/shard_map/ppermute | solution.py:422
  44.4 1.9 %collective-permute-start.15 = (bf16[32,512]{1,0:T(8,128)(2,1)S(1)}, bf16[32,512]{1,0:T(8,128)(2,1)S(1)}, u32[]{:S(2)}, u32[]{:S(2)}) collective-permute-start(bf16[32,512]{1,0:T(8,128)(2,1)S(1)} %get-tuple-element.57), channel_id=1, source_target_pairs={{0,12},{2,14},{4,8},{6,10},{8,4},{10,6},{12,0},{14,2},{1,13},{3,15... | collective-permute-start | bytes 98312 | tf_op jit(solution)/shard_map/ppermute | solution.py:413
  46.5 2.6 %collective-permute-start.17 = (bf16[32,512]{1,0:T(8,128)(2,1)S(1)}, bf16[32,512]{1,0:T(8,128)(2,1)S(1)}, u32[]{:S(2)}, u32[]{:S(2)}) collective-permute-start(bf16[32,512]{1,0:T(8,128)(2,1)S(1)} %get-tuple-element.59), channel_id=1, source_target_pairs={{0,4},{2,6},{4,0},{6,2},{8,12},{10,14},{12,8},{14,10},{1,5},{3,7},... | collective-permute-start | bytes 98312 | tf_op jit(solution)/shard_map/ppermute | solution.py:413
  49.5 0.7 %collective-permute-done.15.rest_1_ = bf16[32,512]{1,0:T(8,128)(2,1)S(1)} collective-permute-done((bf16[32,512]{1,0:T(8,128)(2,1)S(1)}, bf16[32,512]{1,0:T(8,128)(2,1)S(1)}, u32[]{:S(2)}, u32[]{:S(2)}) %collective-permute-start.15) | collective-permute-done | bytes 32800 | tf_op jit(solution)/shard_map/ppermute | solution.py:413
  50.2 1.1 %collective-permute-done.16.rest_2_ = bf16[32,512]{1,0:T(8,128)(2,1)S(1)} collective-permute-done((bf16[32,512]{1,0:T(8,128)(2,1)S(1)}, bf16[32,512]{1,0:T(8,128)(2,1)S(1)}, u32[]{:S(2)}, u32[]{:S(2)}) %collective-permute-start.16) | collective-permute-done | bytes 32800 | tf_op jit(solution)/shard_map/ppermute | solution.py:413
  51.3 0.8 %shard_map.82 = (bf16[128,512]{1,0:T(8,128)(2,1)}, bf16[128,512]{1,0:T(8,128)(2,1)}) custom-call(s32[8,128]{1,0:T(8,128)S(1)} %shard_map.68.plan, f32[8,128]{1,0:T(8,128)S(1)} %get-tuple-element.53.factors, bf16[128,512]{1,0:T(8,128)(2,1)S(1)} %shard_map.72.stay, f32[128,512]{1,0:T(8,128)S(1)} %shard_map.80.stay_2, ...), custom_call_target="tpu_custom_call" | custom-call | bytes 262144 | tf_op jit(solution)/shard_map/pallas_call | solution.py:498
  (29 shorter events, 1.7 us)
Async XLA Ops:
  0.6 1.9 %copy-start = (bf16[1,3,1024,512]{3,2,1,0:T(8,128)(2,1)S(1)}, bf16[1,3,1024,512]{3,2,1,0:T(8,128)(2,1)}, u32[]{:S(2)}) copy-start(bf16[1,3,1024,512]{3,2,1,0:T(8,128)(2,1)} %left.7) | copy-start | bytes 9437188
  0.6 1.9 %copy-start.1 = (bf16[3,128,128]{2,1,0:T(8,128)(2,1)S(1)}, bf16[3,128,128]{2,1,0:T(8,128)(2,1)}, u32[]{:S(2)}) copy-start(bf16[3,128,128]{2,1,0:T(8,128)(2,1)} %right.7) | copy-start | bytes 294916
  0.7 1.9 %copy-start.2 = (bf16[1,128,512]{2,1,0:T(8,128)(2,1)S(1)}, bf16[1,128,512]{2,1,0:T(8,128)(2,1)}, u32[]{:S(2)}) copy-start(bf16[1,128,512]{2,1,0:T(8,128)(2,1)} %param.5) | copy-start | bytes 393220
  0.7 1.9 %copy-start.3 = (s32[8]{0:T(128)S(1)}, s32[8]{0:T(128)}, u32[]{:S(2)}) copy-start(s32[8]{0:T(128)} %widths.1) | copy-start | bytes 100
  0.7 1.9 %copy-start.4 = (s32[8]{0:T(128)S(1)}, s32[8]{0:T(128)}, u32[]{:S(2)}) copy-start(s32[8]{0:T(128)} %holders.1) | copy-start | bytes 100
  0.7 1.7 %collective-permute-start = (bf16[128,512]{1,0:T(8,128)(2,1)}, bf16[128,512]{1,0:T(8,128)(2,1)S(1)}, u32[]{:S(2)}, u32[]{:S(2)}) collective-permute-start(bf16[128,512]{1,0:T(8,128)(2,1)} %bitcast.5), channel_id=1, source_target_pairs={{0,1},{1,0},{2,3},{3,2},{4,5},{5,4},{6,7},{7,6},{8,9},{9,8},{10,11... | collective-permute-start | bytes 393224 | tf_op jit(solution)/shard_map/ppermute | solution.py:418
  3.4 7.6 %collective-permute-start.1 = (bf16[2,32,512]{2,1,0:T(8,128)(2,1)S(1)}, bf16[2,32,512]{2,1,0:T(8,128)(2,1)S(1)}, u32[]{:S(2)}, u32[]{:S(2)}) collective-permute-start(bf16[2,32,512]{2,1,0:T(8,128)(2,1)S(1)} %get-tuple-element.33), channel_id=1, source_target_pairs={{0,12},{2,14},{4,8},{6,10},{8,4},{10,6},{12,0},{14,2},{1,13},{3,15... | collective-permute-start | bytes 196616 | tf_op jit(solution)/shard_map/ppermute | solution.py:413
  8.6 5.7 %collective-permute-start.2 = (bf16[2,32,512]{2,1,0:T(8,128)(2,1)S(1)}, bf16[2,32,512]{2,1,0:T(8,128)(2,1)S(1)}, u32[]{:S(2)}, u32[]{:S(2)}) collective-permute-start(bf16[2,32,512]{2,1,0:T(8,128)(2,1)S(1)} %get-tuple-element.34), channel_id=1, source_target_pairs={{0,8},{2,10},{4,12},{6,14},{8,0},{10,2},{12,4},{14,6},{1,9},{3,11}... | collective-permute-start | bytes 196616 | tf_op jit(solution)/shard_map/ppermute | solution.py:413
  8.6 5.7 %collective-permute-start.3 = (bf16[2,32,512]{2,1,0:T(8,128)(2,1)S(1)}, bf16[2,32,512]{2,1,0:T(8,128)(2,1)S(1)}, u32[]{:S(2)}, u32[]{:S(2)}) collective-permute-start(bf16[2,32,512]{2,1,0:T(8,128)(2,1)S(1)} %get-tuple-element.35), channel_id=1, source_target_pairs={{0,4},{2,6},{4,0},{6,2},{8,12},{10,14},{12,8},{14,10},{1,5},{3,7},... | collective-permute-start | bytes 196616 | tf_op jit(solution)/shard_map/ppermute | solution.py:413
  14.5 4.7 %collective-permute-start.5 = (bf16[2,32,512]{2,1,0:T(8,128)(2,1)S(1)}, bf16[2,32,512]{2,1,0:T(8,128)(2,1)S(1)}, u32[]{:S(2)}, u32[]{:S(2)}) collective-permute-start(bf16[2,32,512]{2,1,0:T(8,128)(2,1)S(1)} %get-tuple-element.42), channel_id=1, source_target_pairs={{0,2},{2,0},{4,6},{6,4},{8,10},{10,8},{12,14},{14,12},{1,3},{3,1},... | collective-permute-start | bytes 196616 | tf_op jit(solution)/shard_map/ppermute | solution.py:422
  16.4 5.5 %collective-permute-start.4 = (bf16[2,32,512]{2,1,0:T(8,128)(2,1)S(1)}, bf16[2,32,512]{2,1,0:T(8,128)(2,1)S(1)}, u32[]{:S(2)}, u32[]{:S(2)}) collective-permute-start(bf16[2,32,512]{2,1,0:T(8,128)(2,1)S(1)} %get-tuple-element.39), channel_id=1, source_target_pairs={{0,2},{2,0},{4,6},{6,4},{8,10},{10,8},{12,14},{14,12},{1,3},{3,1},... | collective-permute-start | bytes 196616 | tf_op jit(solution)/shard_map/ppermute | solution.py:422
  19.3 5.8 %collective-permute-start.6 = (bf16[32,512]{1,0:T(8,128)(2,1)S(1)}, bf16[32,512]{1,0:T(8,128)(2,1)S(1)}, u32[]{:S(2)}, u32[]{:S(2)}) collective-permute-start(bf16[32,512]{1,0:T(8,128)(2,1)S(1)} %get-tuple-element.43), channel_id=1, source_target_pairs={{0,12},{2,14},{4,8},{6,10},{8,4},{10,6},{12,0},{14,2},{1,13},{3,15... | collective-permute-start | bytes 98312 | tf_op jit(solution)/shard_map/ppermute | solution.py:413
  21.9 4.8 %collective-permute-start.7 = (bf16[32,512]{1,0:T(8,128)(2,1)S(1)}, bf16[32,512]{1,0:T(8,128)(2,1)S(1)}, u32[]{:S(2)}, u32[]{:S(2)}) collective-permute-start(bf16[32,512]{1,0:T(8,128)(2,1)S(1)} %get-tuple-element.44), channel_id=1, source_target_pairs={{0,8},{2,10},{4,12},{6,14},{8,0},{10,2},{12,4},{14,6},{1,9},{3,11}... | collective-permute-start | bytes 98312 | tf_op jit(solution)/shard_map/ppermute | solution.py:413
  21.9 4.8 %collective-permute-start.8 = (bf16[32,512]{1,0:T(8,128)(2,1)S(1)}, bf16[32,512]{1,0:T(8,128)(2,1)S(1)}, u32[]{:S(2)}, u32[]{:S(2)}) collective-permute-start(bf16[32,512]{1,0:T(8,128)(2,1)S(1)} %get-tuple-element.45), channel_id=1, source_target_pairs={{0,4},{2,6},{4,0},{6,2},{8,12},{10,14},{12,8},{14,10},{1,5},{3,7},... | collective-permute-start | bytes 98312 | tf_op jit(solution)/shard_map/ppermute | solution.py:413
  26.8 1.4 %collective-permute-start.9 = (bf16[128,512]{1,0:T(8,128)(2,1)S(1)}, bf16[128,512]{1,0:T(8,128)(2,1)S(1)}, u32[]{:S(2)}, u32[]{:S(2)}) collective-permute-start(bf16[128,512]{1,0:T(8,128)(2,1)S(1)} %shard_map.76.own.first), channel_id=1, source_target_pairs={{0,1},{1,0},{2,3},{3,2},{4,5},{5,4},{6,7},{7,6},{8,9},{9,8},{10,11... | collective-permute-start | bytes 393224 | tf_op jit(solution)/shard_map/ppermute | solution.py:418
  29.3 6.8 %collective-permute-start.10 = (bf16[272,128]{1,0:T(8,128)(2,1)S(1)}, bf16[272,128]{1,0:T(8,128)(2,1)S(1)}, u32[]{:S(2)}, u32[]{:S(2)}) collective-permute-start(bf16[272,128]{1,0:T(8,128)(2,1)S(1)} %get-tuple-element.47), channel_id=1, source_target_pairs={{0,12},{2,14},{4,8},{6,10},{8,4},{10,6},{12,0},{14,2},{1,13},{3,15... | collective-permute-start | bytes 208904 | tf_op jit(solution)/shard_map/ppermute | solution.py:413
  31.2 7.4 %collective-permute-start.11 = (bf16[272,128]{1,0:T(8,128)(2,1)S(1)}, bf16[272,128]{1,0:T(8,128)(2,1)S(1)}, u32[]{:S(2)}, u32[]{:S(2)}) collective-permute-start(bf16[272,128]{1,0:T(8,128)(2,1)S(1)} %get-tuple-element.48), channel_id=1, source_target_pairs={{0,8},{2,10},{4,12},{6,14},{8,0},{10,2},{12,4},{14,6},{1,9},{3,11}... | collective-permute-start | bytes 208904 | tf_op jit(solution)/shard_map/ppermute | solution.py:413
  31.8 6.8 %collective-permute-start.12 = (bf16[272,128]{1,0:T(8,128)(2,1)S(1)}, bf16[272,128]{1,0:T(8,128)(2,1)S(1)}, u32[]{:S(2)}, u32[]{:S(2)}) collective-permute-start(bf16[272,128]{1,0:T(8,128)(2,1)S(1)} %get-tuple-element.49), channel_id=1, source_target_pairs={{0,4},{2,6},{4,0},{6,2},{8,12},{10,14},{12,8},{14,10},{1,5},{3,7},... | collective-permute-start | bytes 208904 | tf_op jit(solution)/shard_map/ppermute | solution.py:413
  39.1 5.0 %collective-permute-start.13 = (bf16[272,128]{1,0:T(8,128)(2,1)S(1)}, bf16[272,128]{1,0:T(8,128)(2,1)S(1)}, u32[]{:S(2)}, u32[]{:S(2)}) collective-permute-start(bf16[272,128]{1,0:T(8,128)(2,1)S(1)} %get-tuple-element.52), channel_id=1, source_target_pairs={{0,2},{2,0},{4,6},{6,4},{8,10},{10,8},{12,14},{14,12},{1,3},{3,1},... | collective-permute-start | bytes 208904 | tf_op jit(solution)/shard_map/ppermute | solution.py:422
  40.4 6.0 %collective-permute-start.14 = (bf16[256,128]{1,0:T(8,128)(2,1)S(1)}, bf16[256,128]{1,0:T(8,128)(2,1)S(1)}, u32[]{:S(2)}, u32[]{:S(2)}) collective-permute-start(bf16[256,128]{1,0:T(8,128)(2,1)S(1)} %get-tuple-element.55), channel_id=1, source_target_pairs={{0,2},{2,0},{4,6},{6,4},{8,10},{10,8},{12,14},{14,12},{1,3},{3,1},... | collective-permute-start | bytes 196616 | tf_op jit(solution)/shard_map/ppermute | solution.py:422
  44.4 5.8 %collective-permute-start.15 = (bf16[32,512]{1,0:T(8,128)(2,1)S(1)}, bf16[32,512]{1,0:T(8,128)(2,1)S(1)}, u32[]{:S(2)}, u32[]{:S(2)}) collective-permute-start(bf16[32,512]{1,0:T(8,128)(2,1)S(1)} %get-tuple-element.57), channel_id=1, source_target_pairs={{0,12},{2,14},{4,8},{6,10},{8,4},{10,6},{12,0},{14,2},{1,13},{3,15... | collective-permute-start | bytes 98312 | tf_op jit(solution)/shard_map/ppermute | solution.py:413
  46.4 4.9 %collective-permute-start.16 = (bf16[32,512]{1,0:T(8,128)(2,1)S(1)}, bf16[32,512]{1,0:T(8,128)(2,1)S(1)}, u32[]{:S(2)}, u32[]{:S(2)}) collective-permute-start(bf16[32,512]{1,0:T(8,128)(2,1)S(1)} %get-tuple-element.58), channel_id=1, source_target_pairs={{0,8},{2,10},{4,12},{6,14},{8,0},{10,2},{12,4},{14,6},{1,9},{3,11}... | collective-permute-start | bytes 98312 | tf_op jit(solution)/shard_map/ppermute | solution.py:413
  46.5 4.8 %collective-permute-start.17 = (bf16[32,512]{1,0:T(8,128)(2,1)S(1)}, bf16[32,512]{1,0:T(8,128)(2,1)S(1)}, u32[]{:S(2)}, u32[]{:S(2)}) collective-permute-start(bf16[32,512]{1,0:T(8,128)(2,1)S(1)} %get-tuple-element.59), channel_id=1, source_target_pairs={{0,4},{2,6},{4,0},{6,2},{8,12},{10,14},{12,8},{14,10},{1,5},{3,7},... | collective-permute-start | bytes 98312 | tf_op jit(solution)/shard_map/ppermute | solution.py:413

commit v20 on v19

--- a/solution.py
+++ b/solution.py
@@ -112,7 +112,7 @@
 LANES = 128
 TAG = 16
 LINES = 2
-STEPS = (0, 3, 2, 1)
+STEPS = (0, 3, 1, 2)
 EARLY, LATE = (1, 2), (0, 3)
 
 

time: 52.2 us -> 52.6 us (level)
    ppermute x12, waiting for transfers between devices: 13.6 us -> 14.4 us  [along_line(): sent.append(lax.ppermute(piece, 'sec', pairs) if step else piece)]
  transfers between devices with their start and end apart: 18 -> 18, of which waited for: 12 -> 15; matrix products, arithmetic and copies ran while one was open for 0% -> 0% of each run, Pallas kernels for 4% -> 4%
where the time goes in v20:
time: 52.6 us; the launch traced here: 52.5 us
  starting transfers between devices  24.1 us (46%)
  waiting for transfers between devices  21.8 us (41%)
  Pallas kernels  5.7 us (11%)
  between operations  0.78 us (1%)
    ppermute x12, starting transfers between devices, along_line(): sent.append(lax.ppermute(piece, 'sec', pairs) if step else piece)  19.2 us
    ppermute x12, waiting for transfers between devices, along_line(): sent.append(lax.ppermute(piece, 'sec', pairs) if step else piece)  14.4 us
    ppermute x4, waiting for transfers between devices, across(): lax.ppermute(piece, 'sec', [(slot, slot ^ 1) for slot in range(slots)])  4.83 us
    ppermute x4, starting transfers between devices, across(): lax.ppermute(piece, 'sec', [(slot, slot ^ 1) for slot in range(slots)])  4.25 us
    ppermute x2, waiting for transfers between devices, other_core(): return lax.ppermute(block, 'env', [(0, 1), (1, 0)])  2.53 us
  transfers between devices with their start and end apart: 18, of which 15 were waited for; matrix products, arithmetic and copies ran while one was open for 0% of the time, Pallas kernels for 4%

profile of v20, /device:TPU:0, one launch (start us, length us, event | category | flops | bytes accessed | tf_op | source)
XLA Modules:
  0.0 52.5 jit_solution(6703418465466195735)
XLA Ops:
  0.7 0.5 collective-permute-start
  1.2 1.2 %collective-permute-done.other = bf16[128,512]{1,0:T(8,128)(2,1)S(1)} collective-permute-done((bf16[128,512]{1,0:T(8,128)(2,1)}, bf16[128,512]{1,0:T(8,128)(2,1)S(1)}, u32[]{:S(2)}, u32[]{:S(2)}) %collective-permute-start) | collective-permute-done | bytes 131104 | tf_op jit(solution)/shard_map/ppermute | solution.py:418
  2.5 0.9 %shard_map.70 = (bf16[2,32,512]{2,1,0:T(8,128)(2,1)S(1)}, bf16[2,32,512]{2,1,0:T(8,128)(2,1)S(1)}, bf16[2,32,512]{2,1,0:T(8,128)(2,1)S(1)}, bf16[2,32,512]{2,1,0:T(8,128)(2,1)S(1)}, bf16[2,128,512]{2,1,0:T(8,128)(2,1)S(1)}) custom-call(s32[8,512]{1,0:T(8,128)S(1)} %shard_map.69.columns, s32[1,8]{1,0:T(1,128)S(1)} %bitcast.7, s32[1,8]{1,0:T(1,128)S(1)} %bitcast.8, ...), custom_call_target="tpu_custom_call" | custom-call | flops 452984832 | bytes 262144 | tf_op jit(solution)/shard_map/pallas_call | solution.py:456
  3.4 5.1 %collective-permute-start.1 = (bf16[2,32,512]{2,1,0:T(8,128)(2,1)S(1)}, bf16[2,32,512]{2,1,0:T(8,128)(2,1)S(1)}, u32[]{:S(2)}, u32[]{:S(2)}) collective-permute-start(bf16[2,32,512]{2,1,0:T(8,128)(2,1)S(1)} %get-tuple-element.33), channel_id=1, source_target_pairs={{0,12},{2,14},{4,8},{6,10},{8,4},{10,6},{12,0},{14,2},{1,13},{3,15... | collective-permute-start | bytes 196616 | tf_op jit(solution)/shard_map/ppermute | solution.py:413
  8.6 0.6 %collective-permute-start.3 = (bf16[2,32,512]{2,1,0:T(8,128)(2,1)S(1)}, bf16[2,32,512]{2,1,0:T(8,128)(2,1)S(1)}, u32[]{:S(2)}, u32[]{:S(2)}) collective-permute-start(bf16[2,32,512]{2,1,0:T(8,128)(2,1)S(1)} %get-tuple-element.35), channel_id=1, source_target_pairs={{0,8},{2,10},{4,12},{6,14},{8,0},{10,2},{12,4},{14,6},{1,9},{3,11}... | collective-permute-start | bytes 196616 | tf_op jit(solution)/shard_map/ppermute | solution.py:413
  9.2 0.6 %shard_map.68.plan = s32[8,128]{1,0:T(8,128)S(1)} custom-call(s32[8]{0:T(128)S(1)} %copy-done.3, s32[8]{0:T(128)S(1)} %copy-done.4), custom_call_target="tpu_custom_call" | custom-call | bytes 262144 | tf_op jit(solution)/shard_map/pallas_call | solution.py:452
  9.8 1.6 %collective-permute-done.1.rest_1_ = bf16[2,32,512]{2,1,0:T(8,128)(2,1)S(1)} collective-permute-done((bf16[2,32,512]{2,1,0:T(8,128)(2,1)S(1)}, bf16[2,32,512]{2,1,0:T(8,128)(2,1)S(1)}, u32[]{:S(2)}, u32[]{:S(2)}) %collective-permute-start.1) | collective-permute-done | bytes 65568 | tf_op jit(solution)/shard_map/ppermute | solution.py:413
  11.5 1.8 %collective-permute-done.2.rest_2_ = bf16[2,32,512]{2,1,0:T(8,128)(2,1)S(1)} collective-permute-done((bf16[2,32,512]{2,1,0:T(8,128)(2,1)S(1)}, bf16[2,32,512]{2,1,0:T(8,128)(2,1)S(1)}, u32[]{:S(2)}, u32[]{:S(2)}) %collective-permute-start.2) | collective-permute-done | bytes 65568 | tf_op jit(solution)/shard_map/ppermute | solution.py:413
  13.3 1.0 %collective-permute-done.3.rest_3_ = bf16[2,32,512]{2,1,0:T(8,128)(2,1)S(1)} collective-permute-done((bf16[2,32,512]{2,1,0:T(8,128)(2,1)S(1)}, bf16[2,32,512]{2,1,0:T(8,128)(2,1)S(1)}, u32[]{:S(2)}, u32[]{:S(2)}) %collective-permute-start.3) | collective-permute-done | bytes 65568 | tf_op jit(solution)/shard_map/ppermute | solution.py:413
  14.6 1.5 %collective-permute-start.5 = (bf16[2,32,512]{2,1,0:T(8,128)(2,1)S(1)}, bf16[2,32,512]{2,1,0:T(8,128)(2,1)S(1)}, u32[]{:S(2)}, u32[]{:S(2)}) collective-permute-start(bf16[2,32,512]{2,1,0:T(8,128)(2,1)S(1)} %get-tuple-element.42), channel_id=1, source_target_pairs={{0,2},{2,0},{4,6},{6,4},{8,10},{10,8},{12,14},{14,12},{1,3},{3,1},... | collective-permute-start | bytes 196616 | tf_op jit(solution)/shard_map/ppermute | solution.py:422
  16.4 0.6 %collective-permute-start.4 = (bf16[2,32,512]{2,1,0:T(8,128)(2,1)S(1)}, bf16[2,32,512]{2,1,0:T(8,128)(2,1)S(1)}, u32[]{:S(2)}, u32[]{:S(2)}) collective-permute-start(bf16[2,32,512]{2,1,0:T(8,128)(2,1)S(1)} %get-tuple-element.39), channel_id=1, source_target_pairs={{0,2},{2,0},{4,6},{6,4},{8,10},{10,8},{12,14},{14,12},{1,3},{3,1},... | collective-permute-start | bytes 196616 | tf_op jit(solution)/shard_map/ppermute | solution.py:422
  17.0 1.9 %collective-permute-done.5.arrived.old_arrived = bf16[2,32,512]{2,1,0:T(8,128)(2,1)S(1)} collective-permute-done((bf16[2,32,512]{2,1,0:T(8,128)(2,1)S(1)}, bf16[2,32,512]{2,1,0:T(8,128)(2,1)S(1)}, u32[]{:S(2)}, u32[]{:S(2)}) %collective-permute-start.5) | collective-permute-done | bytes 65568 | tf_op jit(solution)/shard_map/ppermute | solution.py:422
  18.9 2.7 %collective-permute-start.6 = (bf16[32,512]{1,0:T(8,128)(2,1)S(1)}, bf16[32,512]{1,0:T(8,128)(2,1)S(1)}, u32[]{:S(2)}, u32[]{:S(2)}) collective-permute-start(bf16[32,512]{1,0:T(8,128)(2,1)S(1)} %get-tuple-element.43), channel_id=1, source_target_pairs={{0,12},{2,14},{4,8},{6,10},{8,4},{10,6},{12,0},{14,2},{1,13},{3,15... | collective-permute-start | bytes 98312 | tf_op jit(solution)/shard_map/ppermute | solution.py:413
  21.7 1.8 %collective-permute-start.8 = (bf16[32,512]{1,0:T(8,128)(2,1)S(1)}, bf16[32,512]{1,0:T(8,128)(2,1)S(1)}, u32[]{:S(2)}, u32[]{:S(2)}) collective-permute-start(bf16[32,512]{1,0:T(8,128)(2,1)S(1)} %get-tuple-element.45), channel_id=1, source_target_pairs={{0,8},{2,10},{4,12},{6,14},{8,0},{10,2},{12,4},{14,6},{1,9},{3,11}... | collective-permute-start | bytes 98312 | tf_op jit(solution)/shard_map/ppermute | solution.py:413
  23.9 0.8 %collective-permute-done.6.rest_1_ = bf16[32,512]{1,0:T(8,128)(2,1)S(1)} collective-permute-done((bf16[32,512]{1,0:T(8,128)(2,1)S(1)}, bf16[32,512]{1,0:T(8,128)(2,1)S(1)}, u32[]{:S(2)}, u32[]{:S(2)}) %collective-permute-start.6) | collective-permute-done | bytes 32800 | tf_op jit(solution)/shard_map/ppermute | solution.py:413
  24.7 0.9 %collective-permute-done.7.rest_2_ = bf16[32,512]{1,0:T(8,128)(2,1)S(1)} collective-permute-done((bf16[32,512]{1,0:T(8,128)(2,1)S(1)}, bf16[32,512]{1,0:T(8,128)(2,1)S(1)}, u32[]{:S(2)}, u32[]{:S(2)}) %collective-permute-start.7) | collective-permute-done | bytes 32800 | tf_op jit(solution)/shard_map/ppermute | solution.py:413
  25.6 1.0 %collective-permute-done.8.rest_3_ = bf16[32,512]{1,0:T(8,128)(2,1)S(1)} collective-permute-done((bf16[32,512]{1,0:T(8,128)(2,1)S(1)}, bf16[32,512]{1,0:T(8,128)(2,1)S(1)}, u32[]{:S(2)}, u32[]{:S(2)}) %collective-permute-start.8) | collective-permute-done | bytes 32800 | tf_op jit(solution)/shard_map/ppermute | solution.py:413
  26.7 1.3 %collective-permute-done.9.other = bf16[128,512]{1,0:T(8,128)(2,1)S(1)} collective-permute-done((bf16[128,512]{1,0:T(8,128)(2,1)S(1)}, bf16[128,512]{1,0:T(8,128)(2,1)S(1)}, u32[]{:S(2)}, u32[]{:S(2)}) %collective-permute-start.9) | collective-permute-done | bytes 131104 | tf_op jit(solution)/shard_map/ppermute | solution.py:418
  28.1 1.0 %shard_map.77 = (bf16[272,128]{1,0:T(8,128)(2,1)S(1)}, bf16[272,128]{1,0:T(8,128)(2,1)S(1)}, bf16[272,128]{1,0:T(8,128)(2,1)S(1)}, bf16[272,128]{1,0:T(8,128)(2,1)S(1)}, bf16[2,128,512]{2,1,0:T(8,128)(2,1)S(1)}) custom-call(bf16[2,128,512]{2,1,0:T(8,128)(2,1)S(1)} %get-tuple-element.37.vector.start, bf16[128,512]{1,0:T(8,128)(2,1)S(1)} %shard_map.76.own.first, ...), custom_call_target="tpu_custom_call" | custom-call | flops 452984832 | bytes 262144 | tf_op jit(solution)/shard_map/pallas_call | solution.py:482
  29.1 2.0 %collective-permute-start.10 = (bf16[272,128]{1,0:T(8,128)(2,1)S(1)}, bf16[272,128]{1,0:T(8,128)(2,1)S(1)}, u32[]{:S(2)}, u32[]{:S(2)}) collective-permute-start(bf16[272,128]{1,0:T(8,128)(2,1)S(1)} %get-tuple-element.47), channel_id=1, source_target_pairs={{0,12},{2,14},{4,8},{6,10},{8,4},{10,6},{12,0},{14,2},{1,13},{3,15... | collective-permute-start | bytes 208904 | tf_op jit(solution)/shard_map/ppermute | solution.py:413
  31.5 2.1 %collective-permute-start.12 = (bf16[272,128]{1,0:T(8,128)(2,1)S(1)}, bf16[272,128]{1,0:T(8,128)(2,1)S(1)}, u32[]{:S(2)}, u32[]{:S(2)}) collective-permute-start(bf16[272,128]{1,0:T(8,128)(2,1)S(1)} %get-tuple-element.49), channel_id=1, source_target_pairs={{0,8},{2,10},{4,12},{6,14},{8,0},{10,2},{12,4},{14,6},{1,9},{3,11}... | collective-permute-start | bytes 208904 | tf_op jit(solution)/shard_map/ppermute | solution.py:413
  33.6 2.4 %collective-permute-done.10.rest_2_ = bf16[272,128]{1,0:T(8,128)(2,1)S(1)} collective-permute-done((bf16[272,128]{1,0:T(8,128)(2,1)S(1)}, bf16[272,128]{1,0:T(8,128)(2,1)S(1)}, u32[]{:S(2)}, u32[]{:S(2)}) %collective-permute-start.10) | collective-permute-done | bytes 69664 | tf_op jit(solution)/shard_map/ppermute | solution.py:413
  36.0 0.7 %collective-permute-done.11.rest_3_ = bf16[272,128]{1,0:T(8,128)(2,1)S(1)} collective-permute-done((bf16[272,128]{1,0:T(8,128)(2,1)S(1)}, bf16[272,128]{1,0:T(8,128)(2,1)S(1)}, u32[]{:S(2)}, u32[]{:S(2)}) %collective-permute-start.11) | collective-permute-done | bytes 69664 | tf_op jit(solution)/shard_map/ppermute | solution.py:413
  36.7 2.6 %collective-permute-done.12.rest_4_ = bf16[272,128]{1,0:T(8,128)(2,1)S(1)} collective-permute-done((bf16[272,128]{1,0:T(8,128)(2,1)S(1)}, bf16[272,128]{1,0:T(8,128)(2,1)S(1)}, u32[]{:S(2)}, u32[]{:S(2)}) %collective-permute-start.12) | collective-permute-done | bytes 69664 | tf_op jit(solution)/shard_map/ppermute | solution.py:413
  39.3 0.5 shard_map.78
  39.8 1.7 %collective-permute-start.13 = (bf16[272,128]{1,0:T(8,128)(2,1)S(1)}, bf16[272,128]{1,0:T(8,128)(2,1)S(1)}, u32[]{:S(2)}, u32[]{:S(2)}) collective-permute-start(bf16[272,128]{1,0:T(8,128)(2,1)S(1)} %get-tuple-element.52), channel_id=1, source_target_pairs={{0,2},{2,0},{4,6},{6,4},{8,10},{10,8},{12,14},{14,12},{1,3},{3,1},... | collective-permute-start | bytes 208904 | tf_op jit(solution)/shard_map/ppermute | solution.py:422
  41.9 2.9 %collective-permute-done.13.arrived = bf16[272,128]{1,0:T(8,128)(2,1)S(1)} collective-permute-done((bf16[272,128]{1,0:T(8,128)(2,1)S(1)}, bf16[272,128]{1,0:T(8,128)(2,1)S(1)}, u32[]{:S(2)}, u32[]{:S(2)}) %collective-permute-start.13) | collective-permute-done | bytes 69664 | tf_op jit(solution)/shard_map/ppermute | solution.py:422
  45.2 1.2 %collective-permute-start.15 = (bf16[32,512]{1,0:T(8,128)(2,1)S(1)}, bf16[32,512]{1,0:T(8,128)(2,1)S(1)}, u32[]{:S(2)}, u32[]{:S(2)}) collective-permute-start(bf16[32,512]{1,0:T(8,128)(2,1)S(1)} %get-tuple-element.57), channel_id=1, source_target_pairs={{0,12},{2,14},{4,8},{6,10},{8,4},{10,6},{12,0},{14,2},{1,13},{3,15... | collective-permute-start | bytes 98312 | tf_op jit(solution)/shard_map/ppermute | solution.py:413
  46.5 3.3 %collective-permute-start.17 = (bf16[32,512]{1,0:T(8,128)(2,1)S(1)}, bf16[32,512]{1,0:T(8,128)(2,1)S(1)}, u32[]{:S(2)}, u32[]{:S(2)}) collective-permute-start(bf16[32,512]{1,0:T(8,128)(2,1)S(1)} %get-tuple-element.59), channel_id=1, source_target_pairs={{0,8},{2,10},{4,12},{6,14},{8,0},{10,2},{12,4},{14,6},{1,9},{3,11}... | collective-permute-start | bytes 98312 | tf_op jit(solution)/shard_map/ppermute | solution.py:413
  50.2 0.7 %collective-permute-done.15.rest_1_ = bf16[32,512]{1,0:T(8,128)(2,1)S(1)} collective-permute-done((bf16[32,512]{1,0:T(8,128)(2,1)S(1)}, bf16[32,512]{1,0:T(8,128)(2,1)S(1)}, u32[]{:S(2)}, u32[]{:S(2)}) %collective-permute-start.15) | collective-permute-done | bytes 32800 | tf_op jit(solution)/shard_map/ppermute | solution.py:413
  51.0 0.7 %collective-permute-done.17.rest_3_ = bf16[32,512]{1,0:T(8,128)(2,1)S(1)} collective-permute-done((bf16[32,512]{1,0:T(8,128)(2,1)S(1)}, bf16[32,512]{1,0:T(8,128)(2,1)S(1)}, u32[]{:S(2)}, u32[]{:S(2)}) %collective-permute-start.17) | collective-permute-done | bytes 32800 | tf_op jit(solution)/shard_map/ppermute | solution.py:413
  51.7 0.8 %shard_map.82 = (bf16[128,512]{1,0:T(8,128)(2,1)}, bf16[128,512]{1,0:T(8,128)(2,1)}) custom-call(s32[8,128]{1,0:T(8,128)S(1)} %shard_map.68.plan, f32[8,128]{1,0:T(8,128)S(1)} %get-tuple-element.53.factors, bf16[128,512]{1,0:T(8,128)(2,1)S(1)} %shard_map.72.stay, f32[128,512]{1,0:T(8,128)S(1)} %shard_map.80.stay_2, ...), custom_call_target="tpu_custom_call" | custom-call | bytes 262144 | tf_op jit(solution)/shard_map/pallas_call | solution.py:498
  (29 shorter events, 2.9 us)
Async XLA Ops:
  0.6 1.9 %copy-start = (bf16[1,3,1024,512]{3,2,1,0:T(8,128)(2,1)S(1)}, bf16[1,3,1024,512]{3,2,1,0:T(8,128)(2,1)}, u32[]{:S(2)}) copy-start(bf16[1,3,1024,512]{3,2,1,0:T(8,128)(2,1)} %left.7) | copy-start | bytes 9437188
  0.6 1.9 %copy-start.1 = (bf16[3,128,128]{2,1,0:T(8,128)(2,1)S(1)}, bf16[3,128,128]{2,1,0:T(8,128)(2,1)}, u32[]{:S(2)}) copy-start(bf16[3,128,128]{2,1,0:T(8,128)(2,1)} %right.7) | copy-start | bytes 294916
  0.7 1.9 %copy-start.2 = (bf16[1,128,512]{2,1,0:T(8,128)(2,1)S(1)}, bf16[1,128,512]{2,1,0:T(8,128)(2,1)}, u32[]{:S(2)}) copy-start(bf16[1,128,512]{2,1,0:T(8,128)(2,1)} %param.5) | copy-start | bytes 393220
  0.7 1.9 %copy-start.3 = (s32[8]{0:T(128)S(1)}, s32[8]{0:T(128)}, u32[]{:S(2)}) copy-start(s32[8]{0:T(128)} %widths.1) | copy-start | bytes 100
  0.7 1.9 %copy-start.4 = (s32[8]{0:T(128)S(1)}, s32[8]{0:T(128)}, u32[]{:S(2)}) copy-start(s32[8]{0:T(128)} %holders.1) | copy-start | bytes 100
  0.7 1.7 %collective-permute-start = (bf16[128,512]{1,0:T(8,128)(2,1)}, bf16[128,512]{1,0:T(8,128)(2,1)S(1)}, u32[]{:S(2)}, u32[]{:S(2)}) collective-permute-start(bf16[128,512]{1,0:T(8,128)(2,1)} %bitcast.5), channel_id=1, source_target_pairs={{0,1},{1,0},{2,3},{3,2},{4,5},{5,4},{6,7},{7,6},{8,9},{9,8},{10,11... | collective-permute-start | bytes 393224 | tf_op jit(solution)/shard_map/ppermute | solution.py:418
  3.4 8.0 %collective-permute-start.1 = (bf16[2,32,512]{2,1,0:T(8,128)(2,1)S(1)}, bf16[2,32,512]{2,1,0:T(8,128)(2,1)S(1)}, u32[]{:S(2)}, u32[]{:S(2)}) collective-permute-start(bf16[2,32,512]{2,1,0:T(8,128)(2,1)S(1)} %get-tuple-element.33), channel_id=1, source_target_pairs={{0,12},{2,14},{4,8},{6,10},{8,4},{10,6},{12,0},{14,2},{1,13},{3,15... | collective-permute-start | bytes 196616 | tf_op jit(solution)/shard_map/ppermute | solution.py:413
  8.6 4.7 %collective-permute-start.2 = (bf16[2,32,512]{2,1,0:T(8,128)(2,1)S(1)}, bf16[2,32,512]{2,1,0:T(8,128)(2,1)S(1)}, u32[]{:S(2)}, u32[]{:S(2)}) collective-permute-start(bf16[2,32,512]{2,1,0:T(8,128)(2,1)S(1)} %get-tuple-element.34), channel_id=1, source_target_pairs={{0,4},{2,6},{4,0},{6,2},{8,12},{10,14},{12,8},{14,10},{1,5},{3,7},... | collective-permute-start | bytes 196616 | tf_op jit(solution)/shard_map/ppermute | solution.py:413
  8.6 5.7 %collective-permute-start.3 = (bf16[2,32,512]{2,1,0:T(8,128)(2,1)S(1)}, bf16[2,32,512]{2,1,0:T(8,128)(2,1)S(1)}, u32[]{:S(2)}, u32[]{:S(2)}) collective-permute-start(bf16[2,32,512]{2,1,0:T(8,128)(2,1)S(1)} %get-tuple-element.35), channel_id=1, source_target_pairs={{0,8},{2,10},{4,12},{6,14},{8,0},{10,2},{12,4},{14,6},{1,9},{3,11}... | collective-permute-start | bytes 196616 | tf_op jit(solution)/shard_map/ppermute | solution.py:413
  14.6 4.3 %collective-permute-start.5 = (bf16[2,32,512]{2,1,0:T(8,128)(2,1)S(1)}, bf16[2,32,512]{2,1,0:T(8,128)(2,1)S(1)}, u32[]{:S(2)}, u32[]{:S(2)}) collective-permute-start(bf16[2,32,512]{2,1,0:T(8,128)(2,1)S(1)} %get-tuple-element.42), channel_id=1, source_target_pairs={{0,2},{2,0},{4,6},{6,4},{8,10},{10,8},{12,14},{14,12},{1,3},{3,1},... | collective-permute-start | bytes 196616 | tf_op jit(solution)/shard_map/ppermute | solution.py:422
  16.4 5.3 %collective-permute-start.4 = (bf16[2,32,512]{2,1,0:T(8,128)(2,1)S(1)}, bf16[2,32,512]{2,1,0:T(8,128)(2,1)S(1)}, u32[]{:S(2)}, u32[]{:S(2)}) collective-permute-start(bf16[2,32,512]{2,1,0:T(8,128)(2,1)S(1)} %get-tuple-element.39), channel_id=1, source_target_pairs={{0,2},{2,0},{4,6},{6,4},{8,10},{10,8},{12,14},{14,12},{1,3},{3,1},... | collective-permute-start | bytes 196616 | tf_op jit(solution)/shard_map/ppermute | solution.py:422
  18.9 5.8 %collective-permute-start.6 = (bf16[32,512]{1,0:T(8,128)(2,1)S(1)}, bf16[32,512]{1,0:T(8,128)(2,1)S(1)}, u32[]{:S(2)}, u32[]{:S(2)}) collective-permute-start(bf16[32,512]{1,0:T(8,128)(2,1)S(1)} %get-tuple-element.43), channel_id=1, source_target_pairs={{0,12},{2,14},{4,8},{6,10},{8,4},{10,6},{12,0},{14,2},{1,13},{3,15... | collective-permute-start | bytes 98312 | tf_op jit(solution)/shard_map/ppermute | solution.py:413
  21.7 3.9 %collective-permute-start.7 = (bf16[32,512]{1,0:T(8,128)(2,1)S(1)}, bf16[32,512]{1,0:T(8,128)(2,1)S(1)}, u32[]{:S(2)}, u32[]{:S(2)}) collective-permute-start(bf16[32,512]{1,0:T(8,128)(2,1)S(1)} %get-tuple-element.44), channel_id=1, source_target_pairs={{0,4},{2,6},{4,0},{6,2},{8,12},{10,14},{12,8},{14,10},{1,5},{3,7},... | collective-permute-start | bytes 98312 | tf_op jit(solution)/shard_map/ppermute | solution.py:413
  21.7 4.9 %collective-permute-start.8 = (bf16[32,512]{1,0:T(8,128)(2,1)S(1)}, bf16[32,512]{1,0:T(8,128)(2,1)S(1)}, u32[]{:S(2)}, u32[]{:S(2)}) collective-permute-start(bf16[32,512]{1,0:T(8,128)(2,1)S(1)} %get-tuple-element.45), channel_id=1, source_target_pairs={{0,8},{2,10},{4,12},{6,14},{8,0},{10,2},{12,4},{14,6},{1,9},{3,11}... | collective-permute-start | bytes 98312 | tf_op jit(solution)/shard_map/ppermute | solution.py:413
  26.7 1.4 %collective-permute-start.9 = (bf16[128,512]{1,0:T(8,128)(2,1)S(1)}, bf16[128,512]{1,0:T(8,128)(2,1)S(1)}, u32[]{:S(2)}, u32[]{:S(2)}) collective-permute-start(bf16[128,512]{1,0:T(8,128)(2,1)S(1)} %shard_map.76.own.first), channel_id=1, source_target_pairs={{0,1},{1,0},{2,3},{3,2},{4,5},{5,4},{6,7},{7,6},{8,9},{9,8},{10,11... | collective-permute-start | bytes 393224 | tf_op jit(solution)/shard_map/ppermute | solution.py:418
  29.1 6.9 %collective-permute-start.10 = (bf16[272,128]{1,0:T(8,128)(2,1)S(1)}, bf16[272,128]{1,0:T(8,128)(2,1)S(1)}, u32[]{:S(2)}, u32[]{:S(2)}) collective-permute-start(bf16[272,128]{1,0:T(8,128)(2,1)S(1)} %get-tuple-element.47), channel_id=1, source_target_pairs={{0,12},{2,14},{4,8},{6,10},{8,4},{10,6},{12,0},{14,2},{1,13},{3,15... | collective-permute-start | bytes 208904 | tf_op jit(solution)/shard_map/ppermute | solution.py:413
  31.1 5.7 %collective-permute-start.11 = (bf16[272,128]{1,0:T(8,128)(2,1)S(1)}, bf16[272,128]{1,0:T(8,128)(2,1)S(1)}, u32[]{:S(2)}, u32[]{:S(2)}) collective-permute-start(bf16[272,128]{1,0:T(8,128)(2,1)S(1)} %get-tuple-element.48), channel_id=1, source_target_pairs={{0,4},{2,6},{4,0},{6,2},{8,12},{10,14},{12,8},{14,10},{1,5},{3,7},... | collective-permute-start | bytes 208904 | tf_op jit(solution)/shard_map/ppermute | solution.py:413
  31.5 7.9 %collective-permute-start.12 = (bf16[272,128]{1,0:T(8,128)(2,1)S(1)}, bf16[272,128]{1,0:T(8,128)(2,1)S(1)}, u32[]{:S(2)}, u32[]{:S(2)}) collective-permute-start(bf16[272,128]{1,0:T(8,128)(2,1)S(1)} %get-tuple-element.49), channel_id=1, source_target_pairs={{0,8},{2,10},{4,12},{6,14},{8,0},{10,2},{12,4},{14,6},{1,9},{3,11}... | collective-permute-start | bytes 208904 | tf_op jit(solution)/shard_map/ppermute | solution.py:413
  39.8 5.0 %collective-permute-start.13 = (bf16[272,128]{1,0:T(8,128)(2,1)S(1)}, bf16[272,128]{1,0:T(8,128)(2,1)S(1)}, u32[]{:S(2)}, u32[]{:S(2)}) collective-permute-start(bf16[272,128]{1,0:T(8,128)(2,1)S(1)} %get-tuple-element.52), channel_id=1, source_target_pairs={{0,2},{2,0},{4,6},{6,4},{8,10},{10,8},{12,14},{14,12},{1,3},{3,1},... | collective-permute-start | bytes 208904 | tf_op jit(solution)/shard_map/ppermute | solution.py:422
  41.6 4.9 %collective-permute-start.14 = (bf16[256,128]{1,0:T(8,128)(2,1)S(1)}, bf16[256,128]{1,0:T(8,128)(2,1)S(1)}, u32[]{:S(2)}, u32[]{:S(2)}) collective-permute-start(bf16[256,128]{1,0:T(8,128)(2,1)S(1)} %get-tuple-element.55), channel_id=1, source_target_pairs={{0,2},{2,0},{4,6},{6,4},{8,10},{10,8},{12,14},{14,12},{1,3},{3,1},... | collective-permute-start | bytes 196616 | tf_op jit(solution)/shard_map/ppermute | solution.py:422
  45.2 5.8 %collective-permute-start.15 = (bf16[32,512]{1,0:T(8,128)(2,1)S(1)}, bf16[32,512]{1,0:T(8,128)(2,1)S(1)}, u32[]{:S(2)}, u32[]{:S(2)}) collective-permute-start(bf16[32,512]{1,0:T(8,128)(2,1)S(1)} %get-tuple-element.57), channel_id=1, source_target_pairs={{0,12},{2,14},{4,8},{6,10},{8,4},{10,6},{12,0},{14,2},{1,13},{3,15... | collective-permute-start | bytes 98312 | tf_op jit(solution)/shard_map/ppermute | solution.py:413
  46.4 4.5 %collective-permute-start.16 = (bf16[32,512]{1,0:T(8,128)(2,1)S(1)}, bf16[32,512]{1,0:T(8,128)(2,1)S(1)}, u32[]{:S(2)}, u32[]{:S(2)}) collective-permute-start(bf16[32,512]{1,0:T(8,128)(2,1)S(1)} %get-tuple-element.58), channel_id=1, source_target_pairs={{0,4},{2,6},{4,0},{6,2},{8,12},{10,14},{12,8},{14,10},{1,5},{3,7},... | collective-permute-start | bytes 98312 | tf_op jit(solution)/shard_map/ppermute | solution.py:413
  46.5 5.2 %collective-permute-start.17 = (bf16[32,512]{1,0:T(8,128)(2,1)S(1)}, bf16[32,512]{1,0:T(8,128)(2,1)S(1)}, u32[]{:S(2)}, u32[]{:S(2)}) collective-permute-start(bf16[32,512]{1,0:T(8,128)(2,1)S(1)} %get-tuple-element.59), channel_id=1, source_target_pairs={{0,8},{2,10},{4,12},{6,14},{8,0},{10,2},{12,4},{14,6},{1,9},{3,11}... | collective-permute-start | bytes 98312 | tf_op jit(solution)/shard_map/ppermute | solution.py:413

commit v21 on v19

--- a/solution.py
+++ b/solution.py
@@ -113,7 +113,7 @@
 TAG = 16
 LINES = 2
 STEPS = (0, 3, 2, 1)
-EARLY, LATE = (1, 2), (0, 3)
+EARLY, LATE = (1,), (0, 2, 3)
 
 
 def plan_kernel(widths, holders, plan, slot_of):
@@ -438,9 +438,10 @@
     wides = jax.ShapeDtypeStruct((places, rows, half), jnp.float32)
     chunked = rows * half // LANES
     tagged = jax.ShapeDtypeStruct((2 * chunked + TAG, LANES), jnp.bfloat16)
-    twos = jax.ShapeDtypeStruct((2, rows, half), jnp.bfloat16)
-    early = jax.ShapeDtypeStruct((2 * chunked + TAG, LANES), jnp.bfloat16)
-    late = jax.ShapeDtypeStruct((2 * chunked, LANES), jnp.bfloat16)
+    few = jax.ShapeDtypeStruct((len(EARLY), rows, half), jnp.bfloat16)
+    most = jax.ShapeDtypeStruct((len(LATE), rows, half), jnp.bfloat16)
+    early = jax.ShapeDtypeStruct((len(EARLY) * chunked + TAG, LANES), jnp.bfloat16)
+    late = jax.ShapeDtypeStruct((len(LATE) * chunked, LANES), jnp.bfloat16)
     label = jax.ShapeDtypeStruct((TAG, LANES), jnp.bfloat16)
     factor_shape = jax.ShapeDtypeStruct((8, LANES), jnp.float32)
     plan_shape = jax.ShapeDtypeStruct((8, LANES), jnp.int32)
@@ -467,14 +468,14 @@
     old = along_line(pieces, slots)
     stay = call(stay_kernel, [VMEM] * 3, block, flops=dots // 3)(start_full, right_env, left_env)
     table, keep_early, cross = call(
-        merge_early_kernel, [VMEM] * (1 + places), (table_shape, twos, twos)
+        merge_early_kernel, [VMEM] * (1 + places), (table_shape, few, few)
     )(plan, *old)
     old_early = across(cross, slots)
-    keep_late, cross = call(merge_late_kernel, [VMEM] * 2, (twos, twos))(plan, table)
+    keep_late, cross = call(merge_late_kernel, [VMEM] * 2, (most, most))(plan, table)
     old_late = across(cross, slots)
-    far = call(join_kernel, [VMEM] * 2, (single,) * 2)(keep_early, old_early)
-    near = call(join_kernel, [VMEM] * 2, (single,) * 2)(keep_late, old_late)
-    joined = (near[0], *far, near[1])
+    far = call(join_kernel, [VMEM] * 2, (single,) * len(EARLY))(keep_early, old_early)
+    near = call(join_kernel, [VMEM] * 2, (single,) * len(LATE))(keep_late, old_late)
+    joined = (near[0], *far, *near[1:])
     first = call(sum_kernel, [VMEM] * (2 + places), block)(
         plan, stay, *along_line(joined, slots)
     )
@@ -488,13 +489,13 @@
         mix_kernel, [VMEM] * (2 + places), (wides, early, late, label), new_table
     )(plan, table, *new)
     new_early, new_late = (across(piece, slots) for piece in cross)
-    *far, factors = call(join_early_kernel, [VMEM] * 6, (single, single, factor_shape))(
+    *far, factors = call(join_early_kernel, [VMEM] * 6, (single,) * len(EARLY) + (factor_shape,))(
         plan, tag, keep, new_early, keep_early, old_early
     )
-    near = call(join_late_kernel, [VMEM] * 5, (single,) * 2)(
+    near = call(join_late_kernel, [VMEM] * 5, (single,) * len(LATE))(
         factors, keep, new_late, keep_late, old_late
     )
-    joined = (near[0], *far, near[1])
+    joined = (near[0], *far, *near[1:])
     second, first = call(final_kernel, [VMEM] * (5 + places), (block, block))(
         plan, factors, stay, stay_2, first, *along_line(joined, slots)
     )

time: 52.2 us -> 54 us (1.034)
  waiting for transfers between devices: 21.4 us -> 23.3 us
    ppermute x4, waiting for transfers between devices: 5.24 us -> 6.88 us  [across(): lax.ppermute(piece, 'sec', [(slot, slot ^ 1) for slot in range(slots)])]
where the time goes in v21:
time: 54 us; the launch traced here: 53.9 us
  starting transfers between devices  24 us (44%)
  waiting for transfers between devices  23.3 us (43%)
  Pallas kernels  5.7 us (11%)
  between operations  0.8 us (1%)
    ppermute x12, starting transfers between devices, along_line(): sent.append(lax.ppermute(piece, 'sec', pairs) if step else piece)  19.2 us
    ppermute x12, waiting for transfers between devices, along_line(): sent.append(lax.ppermute(piece, 'sec', pairs) if step else piece)  13.8 us
    ppermute x4, waiting for transfers between devices, across(): lax.ppermute(piece, 'sec', [(slot, slot ^ 1) for slot in range(slots)])  6.88 us
    ppermute x4, starting transfers between devices, across(): lax.ppermute(piece, 'sec', [(slot, slot ^ 1) for slot in range(slots)])  4.18 us
    ppermute x2, waiting for transfers between devices, other_core(): return lax.ppermute(block, 'env', [(0, 1), (1, 0)])  2.53 us
  transfers between devices with their start and end apart: 18, of which 12 were waited for; matrix products, arithmetic and copies ran while one was open for 0% of the time, Pallas kernels for 4%

profile of v21, /device:TPU:0, one launch (start us, length us, event | category | flops | bytes accessed | tf_op | source)
XLA Modules:
  0.0 53.9 jit_solution(6303159528586868142)
XLA Ops:
  0.7 0.5 collective-permute-start
  1.2 1.2 %collective-permute-done.other = bf16[128,512]{1,0:T(8,128)(2,1)S(1)} collective-permute-done((bf16[128,512]{1,0:T(8,128)(2,1)}, bf16[128,512]{1,0:T(8,128)(2,1)S(1)}, u32[]{:S(2)}, u32[]{:S(2)}) %collective-permute-start) | collective-permute-done | bytes 131104 | tf_op jit(solution)/shard_map/ppermute | solution.py:418
  2.5 0.9 %shard_map.70 = (bf16[2,32,512]{2,1,0:T(8,128)(2,1)S(1)}, bf16[2,32,512]{2,1,0:T(8,128)(2,1)S(1)}, bf16[2,32,512]{2,1,0:T(8,128)(2,1)S(1)}, bf16[2,32,512]{2,1,0:T(8,128)(2,1)S(1)}, bf16[2,128,512]{2,1,0:T(8,128)(2,1)S(1)}) custom-call(s32[8,512]{1,0:T(8,128)S(1)} %shard_map.69.columns, s32[1,8]{1,0:T(1,128)S(1)} %bitcast.7, s32[1,8]{1,0:T(1,128)S(1)} %bitcast.8, ...), custom_call_target="tpu_custom_call" | custom-call | flops 452984832 | bytes 262144 | tf_op jit(solution)/shard_map/pallas_call | solution.py:457
  3.4 5.1 %collective-permute-start.1 = (bf16[2,32,512]{2,1,0:T(8,128)(2,1)S(1)}, bf16[2,32,512]{2,1,0:T(8,128)(2,1)S(1)}, u32[]{:S(2)}, u32[]{:S(2)}) collective-permute-start(bf16[2,32,512]{2,1,0:T(8,128)(2,1)S(1)} %get-tuple-element.32), channel_id=1, source_target_pairs={{0,12},{2,14},{4,8},{6,10},{8,4},{10,6},{12,0},{14,2},{1,13},{3,15... | collective-permute-start | bytes 196616 | tf_op jit(solution)/shard_map/ppermute | solution.py:413
  8.6 0.6 %collective-permute-start.3 = (bf16[2,32,512]{2,1,0:T(8,128)(2,1)S(1)}, bf16[2,32,512]{2,1,0:T(8,128)(2,1)S(1)}, u32[]{:S(2)}, u32[]{:S(2)}) collective-permute-start(bf16[2,32,512]{2,1,0:T(8,128)(2,1)S(1)} %get-tuple-element.34), channel_id=1, source_target_pairs={{0,4},{2,6},{4,0},{6,2},{8,12},{10,14},{12,8},{14,10},{1,5},{3,7},... | collective-permute-start | bytes 196616 | tf_op jit(solution)/shard_map/ppermute | solution.py:413
  9.2 0.6 %shard_map.68.plan = s32[8,128]{1,0:T(8,128)S(1)} custom-call(s32[8]{0:T(128)S(1)} %copy-done.3, s32[8]{0:T(128)S(1)} %copy-done.4), custom_call_target="tpu_custom_call" | custom-call | bytes 262144 | tf_op jit(solution)/shard_map/pallas_call | solution.py:453
  9.8 1.2 %collective-permute-done.1.rest_1_ = bf16[2,32,512]{2,1,0:T(8,128)(2,1)S(1)} collective-permute-done((bf16[2,32,512]{2,1,0:T(8,128)(2,1)S(1)}, bf16[2,32,512]{2,1,0:T(8,128)(2,1)S(1)}, u32[]{:S(2)}, u32[]{:S(2)}) %collective-permute-start.1) | collective-permute-done | bytes 65568 | tf_op jit(solution)/shard_map/ppermute | solution.py:413
  11.0 3.2 %collective-permute-done.2.rest_2_ = bf16[2,32,512]{2,1,0:T(8,128)(2,1)S(1)} collective-permute-done((bf16[2,32,512]{2,1,0:T(8,128)(2,1)S(1)}, bf16[2,32,512]{2,1,0:T(8,128)(2,1)S(1)}, u32[]{:S(2)}, u32[]{:S(2)}) %collective-permute-start.2) | collective-permute-done | bytes 65568 | tf_op jit(solution)/shard_map/ppermute | solution.py:413
  14.8 1.5 %collective-permute-start.4 = (bf16[3,32,512]{2,1,0:T(8,128)(2,1)S(1)}, bf16[3,32,512]{2,1,0:T(8,128)(2,1)S(1)}, u32[]{:S(2)}, u32[]{:S(2)}) collective-permute-start(bf16[3,32,512]{2,1,0:T(8,128)(2,1)S(1)} %get-tuple-element.38), channel_id=1, source_target_pairs={{0,2},{2,0},{4,6},{6,4},{8,10},{10,8},{12,14},{14,12},{1,3},{3,1},... | collective-permute-start | bytes 294920 | tf_op jit(solution)/shard_map/ppermute | solution.py:422
  16.4 0.5 %collective-permute-start.5 = (bf16[1,32,512]{2,1,0:T(8,128)(2,1)S(1)}, bf16[1,32,512]{2,1,0:T(8,128)(2,1)S(1)}, u32[]{:S(2)}, u32[]{:S(2)}) collective-permute-start(bf16[1,32,512]{2,1,0:T(8,128)(2,1)S(1)} %get-tuple-element.41), channel_id=1, source_target_pairs={{0,2},{2,0},{4,6},{6,4},{8,10},{10,8},{12,14},{14,12},{1,3},{3,1},... | collective-permute-start | bytes 98312 | tf_op jit(solution)/shard_map/ppermute | solution.py:422
  16.9 3.4 %collective-permute-done.5.arrived.old_arrived = bf16[1,32,512]{2,1,0:T(8,128)(2,1)S(1)} collective-permute-done((bf16[1,32,512]{2,1,0:T(8,128)(2,1)S(1)}, bf16[1,32,512]{2,1,0:T(8,128)(2,1)S(1)}, u32[]{:S(2)}, u32[]{:S(2)}) %collective-permute-start.5) | collective-permute-done | bytes 32800 | tf_op jit(solution)/shard_map/ppermute | solution.py:422
  20.3 2.7 %collective-permute-start.6 = (bf16[32,512]{1,0:T(8,128)(2,1)S(1)}, bf16[32,512]{1,0:T(8,128)(2,1)S(1)}, u32[]{:S(2)}, u32[]{:S(2)}) collective-permute-start(bf16[32,512]{1,0:T(8,128)(2,1)S(1)} %shard_map.75), channel_id=1, source_target_pairs={{0,12},{2,14},{4,8},{6,10},{8,4},{10,6},{12,0},{14,2},{1,13},{3,15... | collective-permute-start | bytes 98312 | tf_op jit(solution)/shard_map/ppermute | solution.py:413
  23.1 1.7 %collective-permute-start.8 = (bf16[32,512]{1,0:T(8,128)(2,1)S(1)}, bf16[32,512]{1,0:T(8,128)(2,1)S(1)}, u32[]{:S(2)}, u32[]{:S(2)}) collective-permute-start(bf16[32,512]{1,0:T(8,128)(2,1)S(1)} %get-tuple-element.43), channel_id=1, source_target_pairs={{0,4},{2,6},{4,0},{6,2},{8,12},{10,14},{12,8},{14,10},{1,5},{3,7},... | collective-permute-start | bytes 98312 | tf_op jit(solution)/shard_map/ppermute | solution.py:413
  24.8 0.4 shard_map.72.stay
  25.3 0.8 %collective-permute-done.6.rest_1_ = bf16[32,512]{1,0:T(8,128)(2,1)S(1)} collective-permute-done((bf16[32,512]{1,0:T(8,128)(2,1)S(1)}, bf16[32,512]{1,0:T(8,128)(2,1)S(1)}, u32[]{:S(2)}, u32[]{:S(2)}) %collective-permute-start.6) | collective-permute-done | bytes 32800 | tf_op jit(solution)/shard_map/ppermute | solution.py:413
  26.1 1.9 %collective-permute-done.7.rest_2_ = bf16[32,512]{1,0:T(8,128)(2,1)S(1)} collective-permute-done((bf16[32,512]{1,0:T(8,128)(2,1)S(1)}, bf16[32,512]{1,0:T(8,128)(2,1)S(1)}, u32[]{:S(2)}, u32[]{:S(2)}) %collective-permute-start.7) | collective-permute-done | bytes 32800 | tf_op jit(solution)/shard_map/ppermute | solution.py:413
  28.1 1.3 %collective-permute-done.9.other = bf16[128,512]{1,0:T(8,128)(2,1)S(1)} collective-permute-done((bf16[128,512]{1,0:T(8,128)(2,1)S(1)}, bf16[128,512]{1,0:T(8,128)(2,1)S(1)}, u32[]{:S(2)}, u32[]{:S(2)}) %collective-permute-start.9) | collective-permute-done | bytes 131104 | tf_op jit(solution)/shard_map/ppermute | solution.py:418
  29.4 1.0 %shard_map.77 = (bf16[272,128]{1,0:T(8,128)(2,1)S(1)}, bf16[272,128]{1,0:T(8,128)(2,1)S(1)}, bf16[272,128]{1,0:T(8,128)(2,1)S(1)}, bf16[272,128]{1,0:T(8,128)(2,1)S(1)}, bf16[2,128,512]{2,1,0:T(8,128)(2,1)S(1)}) custom-call(bf16[2,128,512]{2,1,0:T(8,128)(2,1)S(1)} %get-tuple-element.36.vector.start, bf16[128,512]{1,0:T(8,128)(2,1)S(1)} %shard_map.76.own.first, ...), custom_call_target="tpu_custom_call" | custom-call | flops 452984832 | bytes 262144 | tf_op jit(solution)/shard_map/pallas_call | solution.py:483
  30.5 1.9 %collective-permute-start.10 = (bf16[272,128]{1,0:T(8,128)(2,1)S(1)}, bf16[272,128]{1,0:T(8,128)(2,1)S(1)}, u32[]{:S(2)}, u32[]{:S(2)}) collective-permute-start(bf16[272,128]{1,0:T(8,128)(2,1)S(1)} %get-tuple-element.45), channel_id=1, source_target_pairs={{0,12},{2,14},{4,8},{6,10},{8,4},{10,6},{12,0},{14,2},{1,13},{3,15... | collective-permute-start | bytes 208904 | tf_op jit(solution)/shard_map/ppermute | solution.py:413
  32.3 0.5 collective-permute-start.11
  32.8 2.1 %collective-permute-start.12 = (bf16[272,128]{1,0:T(8,128)(2,1)S(1)}, bf16[272,128]{1,0:T(8,128)(2,1)S(1)}, u32[]{:S(2)}, u32[]{:S(2)}) collective-permute-start(bf16[272,128]{1,0:T(8,128)(2,1)S(1)} %get-tuple-element.47), channel_id=1, source_target_pairs={{0,4},{2,6},{4,0},{6,2},{8,12},{10,14},{12,8},{14,10},{1,5},{3,7},... | collective-permute-start | bytes 208904 | tf_op jit(solution)/shard_map/ppermute | solution.py:413
  34.9 2.5 %collective-permute-done.10.rest_2_ = bf16[272,128]{1,0:T(8,128)(2,1)S(1)} collective-permute-done((bf16[272,128]{1,0:T(8,128)(2,1)S(1)}, bf16[272,128]{1,0:T(8,128)(2,1)S(1)}, u32[]{:S(2)}, u32[]{:S(2)}) %collective-permute-start.10) | collective-permute-done | bytes 69664 | tf_op jit(solution)/shard_map/ppermute | solution.py:413
  37.4 2.2 %collective-permute-done.11.rest_3_ = bf16[272,128]{1,0:T(8,128)(2,1)S(1)} collective-permute-done((bf16[272,128]{1,0:T(8,128)(2,1)S(1)}, bf16[272,128]{1,0:T(8,128)(2,1)S(1)}, u32[]{:S(2)}, u32[]{:S(2)}) %collective-permute-start.11) | collective-permute-done | bytes 69664 | tf_op jit(solution)/shard_map/ppermute | solution.py:413
  39.6 0.5 shard_map.78
  40.1 1.3 %collective-permute-start.14 = (bf16[384,128]{1,0:T(8,128)(2,1)S(1)}, bf16[384,128]{1,0:T(8,128)(2,1)S(1)}, u32[]{:S(2)}, u32[]{:S(2)}) collective-permute-start(bf16[384,128]{1,0:T(8,128)(2,1)S(1)} %get-tuple-element.53), channel_id=1, source_target_pairs={{0,2},{2,0},{4,6},{6,4},{8,10},{10,8},{12,14},{14,12},{1,3},{3,1},... | collective-permute-start | bytes 294920 | tf_op jit(solution)/shard_map/ppermute | solution.py:422
  41.4 0.8 %collective-permute-start.13 = (bf16[144,128]{1,0:T(8,128)(2,1)S(1)}, bf16[144,128]{1,0:T(8,128)(2,1)S(1)}, u32[]{:S(2)}, u32[]{:S(2)}) collective-permute-start(bf16[144,128]{1,0:T(8,128)(2,1)S(1)} %get-tuple-element.50), channel_id=1, source_target_pairs={{0,2},{2,0},{4,6},{6,4},{8,10},{10,8},{12,14},{14,12},{1,3},{3,1},... | collective-permute-start | bytes 110600 | tf_op jit(solution)/shard_map/ppermute | solution.py:422
  42.2 3.5 %collective-permute-done.13.arrived = bf16[144,128]{1,0:T(8,128)(2,1)S(1)} collective-permute-done((bf16[144,128]{1,0:T(8,128)(2,1)S(1)}, bf16[144,128]{1,0:T(8,128)(2,1)S(1)}, u32[]{:S(2)}, u32[]{:S(2)}) %collective-permute-start.13) | collective-permute-done | bytes 36896 | tf_op jit(solution)/shard_map/ppermute | solution.py:422
  46.0 2.1 %collective-permute-start.15 = (bf16[32,512]{1,0:T(8,128)(2,1)S(1)}, bf16[32,512]{1,0:T(8,128)(2,1)S(1)}, u32[]{:S(2)}, u32[]{:S(2)}) collective-permute-start(bf16[32,512]{1,0:T(8,128)(2,1)S(1)} %get-tuple-element.55), channel_id=1, source_target_pairs={{0,12},{2,14},{4,8},{6,10},{8,4},{10,6},{12,0},{14,2},{1,13},{3,15... | collective-permute-start | bytes 98312 | tf_op jit(solution)/shard_map/ppermute | solution.py:413
  48.3 2.3 %collective-permute-start.17 = (bf16[32,512]{1,0:T(8,128)(2,1)S(1)}, bf16[32,512]{1,0:T(8,128)(2,1)S(1)}, u32[]{:S(2)}, u32[]{:S(2)}) collective-permute-start(bf16[32,512]{1,0:T(8,128)(2,1)S(1)} %get-tuple-element.57), channel_id=1, source_target_pairs={{0,4},{2,6},{4,0},{6,2},{8,12},{10,14},{12,8},{14,10},{1,5},{3,7},... | collective-permute-start | bytes 98312 | tf_op jit(solution)/shard_map/ppermute | solution.py:413
  51.1 0.7 %collective-permute-done.15.rest_1_ = bf16[32,512]{1,0:T(8,128)(2,1)S(1)} collective-permute-done((bf16[32,512]{1,0:T(8,128)(2,1)S(1)}, bf16[32,512]{1,0:T(8,128)(2,1)S(1)}, u32[]{:S(2)}, u32[]{:S(2)}) %collective-permute-start.15) | collective-permute-done | bytes 32800 | tf_op jit(solution)/shard_map/ppermute | solution.py:413
  51.8 1.3 %collective-permute-done.16.rest_2_ = bf16[32,512]{1,0:T(8,128)(2,1)S(1)} collective-permute-done((bf16[32,512]{1,0:T(8,128)(2,1)S(1)}, bf16[32,512]{1,0:T(8,128)(2,1)S(1)}, u32[]{:S(2)}, u32[]{:S(2)}) %collective-permute-start.16) | collective-permute-done | bytes 32800 | tf_op jit(solution)/shard_map/ppermute | solution.py:413
  53.1 0.8 %shard_map.82 = (bf16[128,512]{1,0:T(8,128)(2,1)}, bf16[128,512]{1,0:T(8,128)(2,1)}) custom-call(s32[8,128]{1,0:T(8,128)S(1)} %shard_map.68.plan, f32[8,128]{1,0:T(8,128)S(1)} %get-tuple-element.51.factors, bf16[128,512]{1,0:T(8,128)(2,1)S(1)} %shard_map.72.stay, f32[128,512]{1,0:T(8,128)S(1)} %shard_map.80.stay_2, ...), custom_call_target="tpu_custom_call" | custom-call | bytes 262144 | tf_op jit(solution)/shard_map/pallas_call | solution.py:499
  (29 shorter events, 1.9 us)
Async XLA Ops:
  0.6 1.9 %copy-start = (bf16[1,3,1024,512]{3,2,1,0:T(8,128)(2,1)S(1)}, bf16[1,3,1024,512]{3,2,1,0:T(8,128)(2,1)}, u32[]{:S(2)}) copy-start(bf16[1,3,1024,512]{3,2,1,0:T(8,128)(2,1)} %left.7) | copy-start | bytes 9437188
  0.6 1.9 %copy-start.1 = (bf16[3,128,128]{2,1,0:T(8,128)(2,1)S(1)}, bf16[3,128,128]{2,1,0:T(8,128)(2,1)}, u32[]{:S(2)}) copy-start(bf16[3,128,128]{2,1,0:T(8,128)(2,1)} %right.7) | copy-start | bytes 294916
  0.7 1.9 %copy-start.2 = (bf16[1,128,512]{2,1,0:T(8,128)(2,1)S(1)}, bf16[1,128,512]{2,1,0:T(8,128)(2,1)}, u32[]{:S(2)}) copy-start(bf16[1,128,512]{2,1,0:T(8,128)(2,1)} %param.5) | copy-start | bytes 393220
  0.7 1.9 %copy-start.3 = (s32[8]{0:T(128)S(1)}, s32[8]{0:T(128)}, u32[]{:S(2)}) copy-start(s32[8]{0:T(128)} %widths.1) | copy-start | bytes 100
  0.7 1.9 %copy-start.4 = (s32[8]{0:T(128)S(1)}, s32[8]{0:T(128)}, u32[]{:S(2)}) copy-start(s32[8]{0:T(128)} %holders.1) | copy-start | bytes 100
  0.7 1.7 %collective-permute-start = (bf16[128,512]{1,0:T(8,128)(2,1)}, bf16[128,512]{1,0:T(8,128)(2,1)S(1)}, u32[]{:S(2)}, u32[]{:S(2)}) collective-permute-start(bf16[128,512]{1,0:T(8,128)(2,1)} %bitcast.5), channel_id=1, source_target_pairs={{0,1},{1,0},{2,3},{3,2},{4,5},{5,4},{6,7},{7,6},{8,9},{9,8},{10,11... | collective-permute-start | bytes 393224 | tf_op jit(solution)/shard_map/ppermute | solution.py:418
  3.4 7.6 %collective-permute-start.1 = (bf16[2,32,512]{2,1,0:T(8,128)(2,1)S(1)}, bf16[2,32,512]{2,1,0:T(8,128)(2,1)S(1)}, u32[]{:S(2)}, u32[]{:S(2)}) collective-permute-start(bf16[2,32,512]{2,1,0:T(8,128)(2,1)S(1)} %get-tuple-element.32), channel_id=1, source_target_pairs={{0,12},{2,14},{4,8},{6,10},{8,4},{10,6},{12,0},{14,2},{1,13},{3,15... | collective-permute-start | bytes 196616 | tf_op jit(solution)/shard_map/ppermute | solution.py:413
  8.6 5.7 %collective-permute-start.2 = (bf16[2,32,512]{2,1,0:T(8,128)(2,1)S(1)}, bf16[2,32,512]{2,1,0:T(8,128)(2,1)S(1)}, u32[]{:S(2)}, u32[]{:S(2)}) collective-permute-start(bf16[2,32,512]{2,1,0:T(8,128)(2,1)S(1)} %get-tuple-element.33), channel_id=1, source_target_pairs={{0,8},{2,10},{4,12},{6,14},{8,0},{10,2},{12,4},{14,6},{1,9},{3,11}... | collective-permute-start | bytes 196616 | tf_op jit(solution)/shard_map/ppermute | solution.py:413
  8.6 5.7 %collective-permute-start.3 = (bf16[2,32,512]{2,1,0:T(8,128)(2,1)S(1)}, bf16[2,32,512]{2,1,0:T(8,128)(2,1)S(1)}, u32[]{:S(2)}, u32[]{:S(2)}) collective-permute-start(bf16[2,32,512]{2,1,0:T(8,128)(2,1)S(1)} %get-tuple-element.34), channel_id=1, source_target_pairs={{0,4},{2,6},{4,0},{6,2},{8,12},{10,14},{12,8},{14,10},{1,5},{3,7},... | collective-permute-start | bytes 196616 | tf_op jit(solution)/shard_map/ppermute | solution.py:413
  14.8 8.2 %collective-permute-start.4 = (bf16[3,32,512]{2,1,0:T(8,128)(2,1)S(1)}, bf16[3,32,512]{2,1,0:T(8,128)(2,1)S(1)}, u32[]{:S(2)}, u32[]{:S(2)}) collective-permute-start(bf16[3,32,512]{2,1,0:T(8,128)(2,1)S(1)} %get-tuple-element.38), channel_id=1, source_target_pairs={{0,2},{2,0},{4,6},{6,4},{8,10},{10,8},{12,14},{14,12},{1,3},{3,1},... | collective-permute-start | bytes 294920 | tf_op jit(solution)/shard_map/ppermute | solution.py:422
  16.4 3.9 %collective-permute-start.5 = (bf16[1,32,512]{2,1,0:T(8,128)(2,1)S(1)}, bf16[1,32,512]{2,1,0:T(8,128)(2,1)S(1)}, u32[]{:S(2)}, u32[]{:S(2)}) collective-permute-start(bf16[1,32,512]{2,1,0:T(8,128)(2,1)S(1)} %get-tuple-element.41), channel_id=1, source_target_pairs={{0,2},{2,0},{4,6},{6,4},{8,10},{10,8},{12,14},{14,12},{1,3},{3,1},... | collective-permute-start | bytes 98312 | tf_op jit(solution)/shard_map/ppermute | solution.py:422
  20.3 5.8 %collective-permute-start.6 = (bf16[32,512]{1,0:T(8,128)(2,1)S(1)}, bf16[32,512]{1,0:T(8,128)(2,1)S(1)}, u32[]{:S(2)}, u32[]{:S(2)}) collective-permute-start(bf16[32,512]{1,0:T(8,128)(2,1)S(1)} %shard_map.75), channel_id=1, source_target_pairs={{0,12},{2,14},{4,8},{6,10},{8,4},{10,6},{12,0},{14,2},{1,13},{3,15... | collective-permute-start | bytes 98312 | tf_op jit(solution)/shard_map/ppermute | solution.py:413
  23.0 4.9 %collective-permute-start.7 = (bf16[32,512]{1,0:T(8,128)(2,1)S(1)}, bf16[32,512]{1,0:T(8,128)(2,1)S(1)}, u32[]{:S(2)}, u32[]{:S(2)}) collective-permute-start(bf16[32,512]{1,0:T(8,128)(2,1)S(1)} %get-tuple-element.42), channel_id=1, source_target_pairs={{0,8},{2,10},{4,12},{6,14},{8,0},{10,2},{12,4},{14,6},{1,9},{3,11}... | collective-permute-start | bytes 98312 | tf_op jit(solution)/shard_map/ppermute | solution.py:413
  23.1 4.8 %collective-permute-start.8 = (bf16[32,512]{1,0:T(8,128)(2,1)S(1)}, bf16[32,512]{1,0:T(8,128)(2,1)S(1)}, u32[]{:S(2)}, u32[]{:S(2)}) collective-permute-start(bf16[32,512]{1,0:T(8,128)(2,1)S(1)} %get-tuple-element.43), channel_id=1, source_target_pairs={{0,4},{2,6},{4,0},{6,2},{8,12},{10,14},{12,8},{14,10},{1,5},{3,7},... | collective-permute-start | bytes 98312 | tf_op jit(solution)/shard_map/ppermute | solution.py:413
  28.0 1.4 %collective-permute-start.9 = (bf16[128,512]{1,0:T(8,128)(2,1)S(1)}, bf16[128,512]{1,0:T(8,128)(2,1)S(1)}, u32[]{:S(2)}, u32[]{:S(2)}) collective-permute-start(bf16[128,512]{1,0:T(8,128)(2,1)S(1)} %shard_map.76.own.first), channel_id=1, source_target_pairs={{0,1},{1,0},{2,3},{3,2},{4,5},{5,4},{6,7},{7,6},{8,9},{9,8},{10,11... | collective-permute-start | bytes 393224 | tf_op jit(solution)/shard_map/ppermute | solution.py:418
  30.5 6.9 %collective-permute-start.10 = (bf16[272,128]{1,0:T(8,128)(2,1)S(1)}, bf16[272,128]{1,0:T(8,128)(2,1)S(1)}, u32[]{:S(2)}, u32[]{:S(2)}) collective-permute-start(bf16[272,128]{1,0:T(8,128)(2,1)S(1)} %get-tuple-element.45), channel_id=1, source_target_pairs={{0,12},{2,14},{4,8},{6,10},{8,4},{10,6},{12,0},{14,2},{1,13},{3,15... | collective-permute-start | bytes 208904 | tf_op jit(solution)/shard_map/ppermute | solution.py:413
  32.3 7.3 %collective-permute-start.11 = (bf16[272,128]{1,0:T(8,128)(2,1)S(1)}, bf16[272,128]{1,0:T(8,128)(2,1)S(1)}, u32[]{:S(2)}, u32[]{:S(2)}) collective-permute-start(bf16[272,128]{1,0:T(8,128)(2,1)S(1)} %get-tuple-element.46), channel_id=1, source_target_pairs={{0,8},{2,10},{4,12},{6,14},{8,0},{10,2},{12,4},{14,6},{1,9},{3,11}... | collective-permute-start | bytes 208904 | tf_op jit(solution)/shard_map/ppermute | solution.py:413
  32.8 6.8 %collective-permute-start.12 = (bf16[272,128]{1,0:T(8,128)(2,1)S(1)}, bf16[272,128]{1,0:T(8,128)(2,1)S(1)}, u32[]{:S(2)}, u32[]{:S(2)}) collective-permute-start(bf16[272,128]{1,0:T(8,128)(2,1)S(1)} %get-tuple-element.47), channel_id=1, source_target_pairs={{0,4},{2,6},{4,0},{6,2},{8,12},{10,14},{12,8},{14,10},{1,5},{3,7},... | collective-permute-start | bytes 208904 | tf_op jit(solution)/shard_map/ppermute | solution.py:413
  40.1 8.0 %collective-permute-start.14 = (bf16[384,128]{1,0:T(8,128)(2,1)S(1)}, bf16[384,128]{1,0:T(8,128)(2,1)S(1)}, u32[]{:S(2)}, u32[]{:S(2)}) collective-permute-start(bf16[384,128]{1,0:T(8,128)(2,1)S(1)} %get-tuple-element.53), channel_id=1, source_target_pairs={{0,2},{2,0},{4,6},{6,4},{8,10},{10,8},{12,14},{14,12},{1,3},{3,1},... | collective-permute-start | bytes 294920 | tf_op jit(solution)/shard_map/ppermute | solution.py:422
  41.4 4.3 %collective-permute-start.13 = (bf16[144,128]{1,0:T(8,128)(2,1)S(1)}, bf16[144,128]{1,0:T(8,128)(2,1)S(1)}, u32[]{:S(2)}, u32[]{:S(2)}) collective-permute-start(bf16[144,128]{1,0:T(8,128)(2,1)S(1)} %get-tuple-element.50), channel_id=1, source_target_pairs={{0,2},{2,0},{4,6},{6,4},{8,10},{10,8},{12,14},{14,12},{1,3},{3,1},... | collective-permute-start | bytes 110600 | tf_op jit(solution)/shard_map/ppermute | solution.py:422
  46.0 5.8 %collective-permute-start.15 = (bf16[32,512]{1,0:T(8,128)(2,1)S(1)}, bf16[32,512]{1,0:T(8,128)(2,1)S(1)}, u32[]{:S(2)}, u32[]{:S(2)}) collective-permute-start(bf16[32,512]{1,0:T(8,128)(2,1)S(1)} %get-tuple-element.55), channel_id=1, source_target_pairs={{0,12},{2,14},{4,8},{6,10},{8,4},{10,6},{12,0},{14,2},{1,13},{3,15... | collective-permute-start | bytes 98312 | tf_op jit(solution)/shard_map/ppermute | solution.py:413
  48.2 4.9 %collective-permute-start.16 = (bf16[32,512]{1,0:T(8,128)(2,1)S(1)}, bf16[32,512]{1,0:T(8,128)(2,1)S(1)}, u32[]{:S(2)}, u32[]{:S(2)}) collective-permute-start(bf16[32,512]{1,0:T(8,128)(2,1)S(1)} %get-tuple-element.56), channel_id=1, source_target_pairs={{0,8},{2,10},{4,12},{6,14},{8,0},{10,2},{12,4},{14,6},{1,9},{3,11}... | collective-permute-start | bytes 98312 | tf_op jit(solution)/shard_map/ppermute | solution.py:413
  48.3 4.8 %collective-permute-start.17 = (bf16[32,512]{1,0:T(8,128)(2,1)S(1)}, bf16[32,512]{1,0:T(8,128)(2,1)S(1)}, u32[]{:S(2)}, u32[]{:S(2)}) collective-permute-start(bf16[32,512]{1,0:T(8,128)(2,1)S(1)} %get-tuple-element.57), channel_id=1, source_target_pairs={{0,4},{2,6},{4,0},{6,2},{8,12},{10,14},{12,8},{14,10},{1,5},{3,7},... | collective-permute-start | bytes 98312 | tf_op jit(solution)/shard_map/ppermute | solution.py:413

commit v22 on v19

--- a/solution.py
+++ b/solution.py
@@ -471,6 +471,7 @@
     )(plan, *old)
     old_early = across(cross, slots)
     keep_late, cross = call(merge_late_kernel, [VMEM] * 2, (twos, twos))(plan, table)
+    old_early, cross = lax.optimization_barrier((old_early, cross))
     old_late = across(cross, slots)
     far = call(join_kernel, [VMEM] * 2, (single,) * 2)(keep_early, old_early)
     near = call(join_kernel, [VMEM] * 2, (single,) * 2)(keep_late, old_late)
@@ -487,7 +488,8 @@
     keep, *cross, tag = call(
         mix_kernel, [VMEM] * (2 + places), (wides, early, late, label), new_table
     )(plan, table, *new)
-    new_early, new_late = (across(piece, slots) for piece in cross)
+    new_early, cross_late = lax.optimization_barrier((across(cross[0], slots), cross[1]))
+    new_late = across(cross_late, slots)
     *far, factors = call(join_early_kernel, [VMEM] * 6, (single, single, factor_shape))(
         plan, tag, keep, new_early, keep_early, old_early
     )

time: 52.2 us -> 54.1 us (1.036)
  waiting for transfers between devices: 21.4 us -> 23.3 us
    ppermute x4, waiting for transfers between devices: 5.24 us -> 6.56 us  [across(): lax.ppermute(piece, 'sec', [(slot, slot ^ 1) for slot in range(slots)])]
    ppermute x12, waiting for transfers between devices: 13.6 us -> 14.2 us  [along_line(): sent.append(lax.ppermute(piece, 'sec', pairs) if step else piece)]
    ppermute x12, starting transfers between devices: 19.2 us -> 18.7 us  [along_line(): sent.append(lax.ppermute(piece, 'sec', pairs) if step else piece)]
    ppermute x4, starting transfers between devices: 4.25 us -> 4.8 us  [across(): lax.ppermute(piece, 'sec', [(slot, slot ^ 1) for slot in range(slots)])]
  transfers between devices with their start and end apart: 18 -> 18, of which waited for: 12 -> 14; matrix products, arithmetic and copies ran while one was open for 0% -> 0% of each run, Pallas kernels for 4% -> 4%
where the time goes in v22:
time: 54.1 us; the launch traced here: 53.9 us
  starting transfers between devices  24.1 us (45%)
  waiting for transfers between devices  23.3 us (43%)
  Pallas kernels  5.7 us (11%)
  between operations  0.78 us (1%)
    ppermute x12, starting transfers between devices, along_line(): sent.append(lax.ppermute(piece, 'sec', pairs) if step else piece)  18.7 us
    ppermute x12, waiting for transfers between devices, along_line(): sent.append(lax.ppermute(piece, 'sec', pairs) if step else piece)  14.2 us
    ppermute x4, waiting for transfers between devices, across(): lax.ppermute(piece, 'sec', [(slot, slot ^ 1) for slot in range(slots)])  6.56 us
    ppermute x4, starting transfers between devices, across(): lax.ppermute(piece, 'sec', [(slot, slot ^ 1) for slot in range(slots)])  4.8 us
    ppermute x2, waiting for transfers between devices, other_core(): return lax.ppermute(block, 'env', [(0, 1), (1, 0)])  2.53 us
  transfers between devices with their start and end apart: 18, of which 14 were waited for; matrix products, arithmetic and copies ran while one was open for 0% of the time, Pallas kernels for 4%

profile of v22, /device:TPU:0, one launch (start us, length us, event | category | flops | bytes accessed | tf_op | source)
XLA Modules:
  0.0 53.9 jit_solution(14123868473504790412)
XLA Ops:
  0.7 0.5 collective-permute-start
  1.2 1.2 %collective-permute-done.other = bf16[128,512]{1,0:T(8,128)(2,1)S(1)} collective-permute-done((bf16[128,512]{1,0:T(8,128)(2,1)}, bf16[128,512]{1,0:T(8,128)(2,1)S(1)}, u32[]{:S(2)}, u32[]{:S(2)}) %collective-permute-start) | collective-permute-done | bytes 131104 | tf_op jit(solution)/shard_map/ppermute | solution.py:418
  2.5 0.9 %shard_map.70 = (bf16[2,32,512]{2,1,0:T(8,128)(2,1)S(1)}, bf16[2,32,512]{2,1,0:T(8,128)(2,1)S(1)}, bf16[2,32,512]{2,1,0:T(8,128)(2,1)S(1)}, bf16[2,32,512]{2,1,0:T(8,128)(2,1)S(1)}, bf16[2,128,512]{2,1,0:T(8,128)(2,1)S(1)}) custom-call(s32[8,512]{1,0:T(8,128)S(1)} %shard_map.69.columns, s32[1,8]{1,0:T(1,128)S(1)} %bitcast.7, s32[1,8]{1,0:T(1,128)S(1)} %bitcast.8, ...), custom_call_target="tpu_custom_call" | custom-call | flops 452984832 | bytes 262144 | tf_op jit(solution)/shard_map/pallas_call | solution.py:456
  3.4 5.1 %collective-permute-start.1 = (bf16[2,32,512]{2,1,0:T(8,128)(2,1)S(1)}, bf16[2,32,512]{2,1,0:T(8,128)(2,1)S(1)}, u32[]{:S(2)}, u32[]{:S(2)}) collective-permute-start(bf16[2,32,512]{2,1,0:T(8,128)(2,1)S(1)} %get-tuple-element.37), channel_id=1, source_target_pairs={{0,12},{2,14},{4,8},{6,10},{8,4},{10,6},{12,0},{14,2},{1,13},{3,15... | collective-permute-start | bytes 196616 | tf_op jit(solution)/shard_map/ppermute | solution.py:413
  8.6 0.6 %collective-permute-start.3 = (bf16[2,32,512]{2,1,0:T(8,128)(2,1)S(1)}, bf16[2,32,512]{2,1,0:T(8,128)(2,1)S(1)}, u32[]{:S(2)}, u32[]{:S(2)}) collective-permute-start(bf16[2,32,512]{2,1,0:T(8,128)(2,1)S(1)} %get-tuple-element.39), channel_id=1, source_target_pairs={{0,4},{2,6},{4,0},{6,2},{8,12},{10,14},{12,8},{14,10},{1,5},{3,7},... | collective-permute-start | bytes 196616 | tf_op jit(solution)/shard_map/ppermute | solution.py:413
  9.2 0.6 %shard_map.68.plan = s32[8,128]{1,0:T(8,128)S(1)} custom-call(s32[8]{0:T(128)S(1)} %copy-done.3, s32[8]{0:T(128)S(1)} %copy-done.4), custom_call_target="tpu_custom_call" | custom-call | bytes 262144 | tf_op jit(solution)/shard_map/pallas_call | solution.py:452
  9.8 1.2 %collective-permute-done.1.rest_1_ = bf16[2,32,512]{2,1,0:T(8,128)(2,1)S(1)} collective-permute-done((bf16[2,32,512]{2,1,0:T(8,128)(2,1)S(1)}, bf16[2,32,512]{2,1,0:T(8,128)(2,1)S(1)}, u32[]{:S(2)}, u32[]{:S(2)}) %collective-permute-start.1) | collective-permute-done | bytes 65568 | tf_op jit(solution)/shard_map/ppermute | solution.py:413
  11.0 3.2 %collective-permute-done.2.rest_2_ = bf16[2,32,512]{2,1,0:T(8,128)(2,1)S(1)} collective-permute-done((bf16[2,32,512]{2,1,0:T(8,128)(2,1)S(1)}, bf16[2,32,512]{2,1,0:T(8,128)(2,1)S(1)}, u32[]{:S(2)}, u32[]{:S(2)}) %collective-permute-start.2) | collective-permute-done | bytes 65568 | tf_op jit(solution)/shard_map/ppermute | solution.py:413
  14.5 1.5 %collective-permute-start.4 = (bf16[2,32,512]{2,1,0:T(8,128)(2,1)S(1)}, bf16[2,32,512]{2,1,0:T(8,128)(2,1)S(1)}, u32[]{:S(2)}, u32[]{:S(2)}) collective-permute-start(bf16[2,32,512]{2,1,0:T(8,128)(2,1)S(1)} %get-tuple-element.43), channel_id=1, source_target_pairs={{0,2},{2,0},{4,6},{6,4},{8,10},{10,8},{12,14},{14,12},{1,3},{3,1},... | collective-permute-start | bytes 196616 | tf_op jit(solution)/shard_map/ppermute | solution.py:422
  16.4 2.5 %collective-permute-done.4.arrived.old_arrived = bf16[2,32,512]{2,1,0:T(8,128)(2,1)S(1)} collective-permute-done((bf16[2,32,512]{2,1,0:T(8,128)(2,1)S(1)}, bf16[2,32,512]{2,1,0:T(8,128)(2,1)S(1)}, u32[]{:S(2)}, u32[]{:S(2)}) %collective-permute-start.4) | collective-permute-done | bytes 65568 | tf_op jit(solution)/shard_map/ppermute | solution.py:422
  18.9 1.5 %collective-permute-start.5 = (bf16[2,32,512]{2,1,0:T(8,128)(2,1)S(1)}, bf16[2,32,512]{2,1,0:T(8,128)(2,1)S(1)}, u32[]{:S(2)}, u32[]{:S(2)}) collective-permute-start(bf16[2,32,512]{2,1,0:T(8,128)(2,1)S(1)} %get-tuple-element.45), channel_id=1, source_target_pairs={{0,2},{2,0},{4,6},{6,4},{8,10},{10,8},{12,14},{14,12},{1,3},{3,1},... | collective-permute-start | bytes 196616 | tf_op jit(solution)/shard_map/ppermute | solution.py:422
  20.4 2.7 %collective-permute-start.6 = (bf16[32,512]{1,0:T(8,128)(2,1)S(1)}, bf16[32,512]{1,0:T(8,128)(2,1)S(1)}, u32[]{:S(2)}, u32[]{:S(2)}) collective-permute-start(bf16[32,512]{1,0:T(8,128)(2,1)S(1)} %get-tuple-element.49), channel_id=1, source_target_pairs={{0,12},{2,14},{4,8},{6,10},{8,4},{10,6},{12,0},{14,2},{1,13},{3,15... | collective-permute-start | bytes 98312 | tf_op jit(solution)/shard_map/ppermute | solution.py:413
  23.2 1.8 %collective-permute-start.8 = (bf16[32,512]{1,0:T(8,128)(2,1)S(1)}, bf16[32,512]{1,0:T(8,128)(2,1)S(1)}, u32[]{:S(2)}, u32[]{:S(2)}) collective-permute-start(bf16[32,512]{1,0:T(8,128)(2,1)S(1)} %get-tuple-element.51), channel_id=1, source_target_pairs={{0,4},{2,6},{4,0},{6,2},{8,12},{10,14},{12,8},{14,10},{1,5},{3,7},... | collective-permute-start | bytes 98312 | tf_op jit(solution)/shard_map/ppermute | solution.py:413
  25.3 0.8 %collective-permute-done.6.rest_1_ = bf16[32,512]{1,0:T(8,128)(2,1)S(1)} collective-permute-done((bf16[32,512]{1,0:T(8,128)(2,1)S(1)}, bf16[32,512]{1,0:T(8,128)(2,1)S(1)}, u32[]{:S(2)}, u32[]{:S(2)}) %collective-permute-start.6) | collective-permute-done | bytes 32800 | tf_op jit(solution)/shard_map/ppermute | solution.py:413
  26.2 1.8 %collective-permute-done.7.rest_2_ = bf16[32,512]{1,0:T(8,128)(2,1)S(1)} collective-permute-done((bf16[32,512]{1,0:T(8,128)(2,1)S(1)}, bf16[32,512]{1,0:T(8,128)(2,1)S(1)}, u32[]{:S(2)}, u32[]{:S(2)}) %collective-permute-start.7) | collective-permute-done | bytes 32800 | tf_op jit(solution)/shard_map/ppermute | solution.py:413
  28.1 1.3 %collective-permute-done.9.other = bf16[128,512]{1,0:T(8,128)(2,1)S(1)} collective-permute-done((bf16[128,512]{1,0:T(8,128)(2,1)S(1)}, bf16[128,512]{1,0:T(8,128)(2,1)S(1)}, u32[]{:S(2)}, u32[]{:S(2)}) %collective-permute-start.9) | collective-permute-done | bytes 131104 | tf_op jit(solution)/shard_map/ppermute | solution.py:418
  29.4 1.0 %shard_map.77 = (bf16[272,128]{1,0:T(8,128)(2,1)S(1)}, bf16[272,128]{1,0:T(8,128)(2,1)S(1)}, bf16[272,128]{1,0:T(8,128)(2,1)S(1)}, bf16[272,128]{1,0:T(8,128)(2,1)S(1)}, bf16[2,128,512]{2,1,0:T(8,128)(2,1)S(1)}) custom-call(bf16[2,128,512]{2,1,0:T(8,128)(2,1)S(1)} %get-tuple-element.41.vector.start, bf16[128,512]{1,0:T(8,128)(2,1)S(1)} %shard_map.76.own.first, ...), custom_call_target="tpu_custom_call" | custom-call | flops 452984832 | bytes 262144 | tf_op jit(solution)/shard_map/pallas_call | solution.py:483
  30.5 2.0 %collective-permute-start.10 = (bf16[272,128]{1,0:T(8,128)(2,1)S(1)}, bf16[272,128]{1,0:T(8,128)(2,1)S(1)}, u32[]{:S(2)}, u32[]{:S(2)}) collective-permute-start(bf16[272,128]{1,0:T(8,128)(2,1)S(1)} %get-tuple-element.53), channel_id=1, source_target_pairs={{0,12},{2,14},{4,8},{6,10},{8,4},{10,6},{12,0},{14,2},{1,13},{3,15... | collective-permute-start | bytes 208904 | tf_op jit(solution)/shard_map/ppermute | solution.py:413
  32.5 0.4 collective-permute-start.11
  32.9 2.0 %collective-permute-start.12 = (bf16[272,128]{1,0:T(8,128)(2,1)S(1)}, bf16[272,128]{1,0:T(8,128)(2,1)S(1)}, u32[]{:S(2)}, u32[]{:S(2)}) collective-permute-start(bf16[272,128]{1,0:T(8,128)(2,1)S(1)} %get-tuple-element.55), channel_id=1, source_target_pairs={{0,4},{2,6},{4,0},{6,2},{8,12},{10,14},{12,8},{14,10},{1,5},{3,7},... | collective-permute-start | bytes 208904 | tf_op jit(solution)/shard_map/ppermute | solution.py:413
  34.9 2.4 %collective-permute-done.10.rest_2_ = bf16[272,128]{1,0:T(8,128)(2,1)S(1)} collective-permute-done((bf16[272,128]{1,0:T(8,128)(2,1)S(1)}, bf16[272,128]{1,0:T(8,128)(2,1)S(1)}, u32[]{:S(2)}, u32[]{:S(2)}) %collective-permute-start.10) | collective-permute-done | bytes 69664 | tf_op jit(solution)/shard_map/ppermute | solution.py:413
  37.3 2.3 %collective-permute-done.11.rest_3_ = bf16[272,128]{1,0:T(8,128)(2,1)S(1)} collective-permute-done((bf16[272,128]{1,0:T(8,128)(2,1)S(1)}, bf16[272,128]{1,0:T(8,128)(2,1)S(1)}, u32[]{:S(2)}, u32[]{:S(2)}) %collective-permute-start.11) | collective-permute-done | bytes 69664 | tf_op jit(solution)/shard_map/ppermute | solution.py:413
  39.6 0.5 shard_map.78
  40.1 0.9 %collective-permute-start.13 = (bf16[272,128]{1,0:T(8,128)(2,1)S(1)}, bf16[272,128]{1,0:T(8,128)(2,1)S(1)}, u32[]{:S(2)}, u32[]{:S(2)}) collective-permute-start(bf16[272,128]{1,0:T(8,128)(2,1)S(1)} %get-tuple-element.58), channel_id=1, source_target_pairs={{0,2},{2,0},{4,6},{6,4},{8,10},{10,8},{12,14},{14,12},{1,3},{3,1},... | collective-permute-start | bytes 208904 | tf_op jit(solution)/shard_map/ppermute | solution.py:422
  41.0 3.5 %collective-permute-done.13.arrived = bf16[272,128]{1,0:T(8,128)(2,1)S(1)} collective-permute-done((bf16[272,128]{1,0:T(8,128)(2,1)S(1)}, bf16[272,128]{1,0:T(8,128)(2,1)S(1)}, u32[]{:S(2)}, u32[]{:S(2)}) %collective-permute-start.13) | collective-permute-done | bytes 69664 | tf_op jit(solution)/shard_map/ppermute | solution.py:422
  44.5 0.8 %collective-permute-start.14 = (bf16[256,128]{1,0:T(8,128)(2,1)S(1)}, bf16[256,128]{1,0:T(8,128)(2,1)S(1)}, u32[]{:S(2)}, u32[]{:S(2)}) collective-permute-start(bf16[256,128]{1,0:T(8,128)(2,1)S(1)} %get-tuple-element.63), channel_id=1, source_target_pairs={{0,2},{2,0},{4,6},{6,4},{8,10},{10,8},{12,14},{14,12},{1,3},{3,1},... | collective-permute-start | bytes 196616 | tf_op jit(solution)/shard_map/ppermute | solution.py:422
  45.7 2.5 %collective-permute-start.15 = (bf16[32,512]{1,0:T(8,128)(2,1)S(1)}, bf16[32,512]{1,0:T(8,128)(2,1)S(1)}, u32[]{:S(2)}, u32[]{:S(2)}) collective-permute-start(bf16[32,512]{1,0:T(8,128)(2,1)S(1)} %get-tuple-element.65), channel_id=1, source_target_pairs={{0,12},{2,14},{4,8},{6,10},{8,4},{10,6},{12,0},{14,2},{1,13},{3,15... | collective-permute-start | bytes 98312 | tf_op jit(solution)/shard_map/ppermute | solution.py:413
  48.2 0.6 %collective-permute-done.14.arrived = bf16[256,128]{1,0:T(8,128)(2,1)S(1)} collective-permute-done((bf16[256,128]{1,0:T(8,128)(2,1)S(1)}, bf16[256,128]{1,0:T(8,128)(2,1)S(1)}, u32[]{:S(2)}, u32[]{:S(2)}) %collective-permute-start.14) | collective-permute-done | bytes 65568 | tf_op jit(solution)/shard_map/ppermute | solution.py:422
  48.8 1.4 %collective-permute-start.17 = (bf16[32,512]{1,0:T(8,128)(2,1)S(1)}, bf16[32,512]{1,0:T(8,128)(2,1)S(1)}, u32[]{:S(2)}, u32[]{:S(2)}) collective-permute-start(bf16[32,512]{1,0:T(8,128)(2,1)S(1)} %get-tuple-element.67), channel_id=1, source_target_pairs={{0,4},{2,6},{4,0},{6,2},{8,12},{10,14},{12,8},{14,10},{1,5},{3,7},... | collective-permute-start | bytes 98312 | tf_op jit(solution)/shard_map/ppermute | solution.py:413
  50.7 0.9 %collective-permute-done.15.rest_1_ = bf16[32,512]{1,0:T(8,128)(2,1)S(1)} collective-permute-done((bf16[32,512]{1,0:T(8,128)(2,1)S(1)}, bf16[32,512]{1,0:T(8,128)(2,1)S(1)}, u32[]{:S(2)}, u32[]{:S(2)}) %collective-permute-start.15) | collective-permute-done | bytes 32800 | tf_op jit(solution)/shard_map/ppermute | solution.py:413
  51.6 1.5 %collective-permute-done.16.rest_2_ = bf16[32,512]{1,0:T(8,128)(2,1)S(1)} collective-permute-done((bf16[32,512]{1,0:T(8,128)(2,1)S(1)}, bf16[32,512]{1,0:T(8,128)(2,1)S(1)}, u32[]{:S(2)}, u32[]{:S(2)}) %collective-permute-start.16) | collective-permute-done | bytes 32800 | tf_op jit(solution)/shard_map/ppermute | solution.py:413
  53.2 0.8 %shard_map.82 = (bf16[128,512]{1,0:T(8,128)(2,1)}, bf16[128,512]{1,0:T(8,128)(2,1)}) custom-call(s32[8,128]{1,0:T(8,128)S(1)} %shard_map.68.plan, f32[8,128]{1,0:T(8,128)S(1)} %get-tuple-element.61.factors, bf16[128,512]{1,0:T(8,128)(2,1)S(1)} %shard_map.72.stay, f32[128,512]{1,0:T(8,128)S(1)} %shard_map.80.stay_2, ...), custom_call_target="tpu_custom_call" | custom-call | bytes 262144 | tf_op jit(solution)/shard_map/pallas_call | solution.py:500
  (29 shorter events, 2.2 us)
Async XLA Ops:
  0.6 1.9 %copy-start = (bf16[1,3,1024,512]{3,2,1,0:T(8,128)(2,1)S(1)}, bf16[1,3,1024,512]{3,2,1,0:T(8,128)(2,1)}, u32[]{:S(2)}) copy-start(bf16[1,3,1024,512]{3,2,1,0:T(8,128)(2,1)} %left.7) | copy-start | bytes 9437188
  0.6 1.9 %copy-start.1 = (bf16[3,128,128]{2,1,0:T(8,128)(2,1)S(1)}, bf16[3,128,128]{2,1,0:T(8,128)(2,1)}, u32[]{:S(2)}) copy-start(bf16[3,128,128]{2,1,0:T(8,128)(2,1)} %right.7) | copy-start | bytes 294916
  0.7 1.9 %copy-start.2 = (bf16[1,128,512]{2,1,0:T(8,128)(2,1)S(1)}, bf16[1,128,512]{2,1,0:T(8,128)(2,1)}, u32[]{:S(2)}) copy-start(bf16[1,128,512]{2,1,0:T(8,128)(2,1)} %param.5) | copy-start | bytes 393220
  0.7 1.9 %copy-start.3 = (s32[8]{0:T(128)S(1)}, s32[8]{0:T(128)}, u32[]{:S(2)}) copy-start(s32[8]{0:T(128)} %widths.1) | copy-start | bytes 100
  0.7 1.9 %copy-start.4 = (s32[8]{0:T(128)S(1)}, s32[8]{0:T(128)}, u32[]{:S(2)}) copy-start(s32[8]{0:T(128)} %holders.1) | copy-start | bytes 100
  0.7 1.7 %collective-permute-start = (bf16[128,512]{1,0:T(8,128)(2,1)}, bf16[128,512]{1,0:T(8,128)(2,1)S(1)}, u32[]{:S(2)}, u32[]{:S(2)}) collective-permute-start(bf16[128,512]{1,0:T(8,128)(2,1)} %bitcast.5), channel_id=1, source_target_pairs={{0,1},{1,0},{2,3},{3,2},{4,5},{5,4},{6,7},{7,6},{8,9},{9,8},{10,11... | collective-permute-start | bytes 393224 | tf_op jit(solution)/shard_map/ppermute | solution.py:418
  3.4 7.6 %collective-permute-start.1 = (bf16[2,32,512]{2,1,0:T(8,128)(2,1)S(1)}, bf16[2,32,512]{2,1,0:T(8,128)(2,1)S(1)}, u32[]{:S(2)}, u32[]{:S(2)}) collective-permute-start(bf16[2,32,512]{2,1,0:T(8,128)(2,1)S(1)} %get-tuple-element.37), channel_id=1, source_target_pairs={{0,12},{2,14},{4,8},{6,10},{8,4},{10,6},{12,0},{14,2},{1,13},{3,15... | collective-permute-start | bytes 196616 | tf_op jit(solution)/shard_map/ppermute | solution.py:413
  8.6 5.7 %collective-permute-start.2 = (bf16[2,32,512]{2,1,0:T(8,128)(2,1)S(1)}, bf16[2,32,512]{2,1,0:T(8,128)(2,1)S(1)}, u32[]{:S(2)}, u32[]{:S(2)}) collective-permute-start(bf16[2,32,512]{2,1,0:T(8,128)(2,1)S(1)} %get-tuple-element.38), channel_id=1, source_target_pairs={{0,8},{2,10},{4,12},{6,14},{8,0},{10,2},{12,4},{14,6},{1,9},{3,11}... | collective-permute-start | bytes 196616 | tf_op jit(solution)/shard_map/ppermute | solution.py:413
  8.6 5.7 %collective-permute-start.3 = (bf16[2,32,512]{2,1,0:T(8,128)(2,1)S(1)}, bf16[2,32,512]{2,1,0:T(8,128)(2,1)S(1)}, u32[]{:S(2)}, u32[]{:S(2)}) collective-permute-start(bf16[2,32,512]{2,1,0:T(8,128)(2,1)S(1)} %get-tuple-element.39), channel_id=1, source_target_pairs={{0,4},{2,6},{4,0},{6,2},{8,12},{10,14},{12,8},{14,10},{1,5},{3,7},... | collective-permute-start | bytes 196616 | tf_op jit(solution)/shard_map/ppermute | solution.py:413
  14.5 4.3 %collective-permute-start.4 = (bf16[2,32,512]{2,1,0:T(8,128)(2,1)S(1)}, bf16[2,32,512]{2,1,0:T(8,128)(2,1)S(1)}, u32[]{:S(2)}, u32[]{:S(2)}) collective-permute-start(bf16[2,32,512]{2,1,0:T(8,128)(2,1)S(1)} %get-tuple-element.43), channel_id=1, source_target_pairs={{0,2},{2,0},{4,6},{6,4},{8,10},{10,8},{12,14},{14,12},{1,3},{3,1},... | collective-permute-start | bytes 196616 | tf_op jit(solution)/shard_map/ppermute | solution.py:422
  18.9 4.3 %collective-permute-start.5 = (bf16[2,32,512]{2,1,0:T(8,128)(2,1)S(1)}, bf16[2,32,512]{2,1,0:T(8,128)(2,1)S(1)}, u32[]{:S(2)}, u32[]{:S(2)}) collective-permute-start(bf16[2,32,512]{2,1,0:T(8,128)(2,1)S(1)} %get-tuple-element.45), channel_id=1, source_target_pairs={{0,2},{2,0},{4,6},{6,4},{8,10},{10,8},{12,14},{14,12},{1,3},{3,1},... | collective-permute-start | bytes 196616 | tf_op jit(solution)/shard_map/ppermute | solution.py:422
  20.4 5.8 %collective-permute-start.6 = (bf16[32,512]{1,0:T(8,128)(2,1)S(1)}, bf16[32,512]{1,0:T(8,128)(2,1)S(1)}, u32[]{:S(2)}, u32[]{:S(2)}) collective-permute-start(bf16[32,512]{1,0:T(8,128)(2,1)S(1)} %get-tuple-element.49), channel_id=1, source_target_pairs={{0,12},{2,14},{4,8},{6,10},{8,4},{10,6},{12,0},{14,2},{1,13},{3,15... | collective-permute-start | bytes 98312 | tf_op jit(solution)/shard_map/ppermute | solution.py:413
  23.1 4.8 %collective-permute-start.7 = (bf16[32,512]{1,0:T(8,128)(2,1)S(1)}, bf16[32,512]{1,0:T(8,128)(2,1)S(1)}, u32[]{:S(2)}, u32[]{:S(2)}) collective-permute-start(bf16[32,512]{1,0:T(8,128)(2,1)S(1)} %get-tuple-element.50), channel_id=1, source_target_pairs={{0,8},{2,10},{4,12},{6,14},{8,0},{10,2},{12,4},{14,6},{1,9},{3,11}... | collective-permute-start | bytes 98312 | tf_op jit(solution)/shard_map/ppermute | solution.py:413
  23.2 4.8 %collective-permute-start.8 = (bf16[32,512]{1,0:T(8,128)(2,1)S(1)}, bf16[32,512]{1,0:T(8,128)(2,1)S(1)}, u32[]{:S(2)}, u32[]{:S(2)}) collective-permute-start(bf16[32,512]{1,0:T(8,128)(2,1)S(1)} %get-tuple-element.51), channel_id=1, source_target_pairs={{0,4},{2,6},{4,0},{6,2},{8,12},{10,14},{12,8},{14,10},{1,5},{3,7},... | collective-permute-start | bytes 98312 | tf_op jit(solution)/shard_map/ppermute | solution.py:413
  28.0 1.4 %collective-permute-start.9 = (bf16[128,512]{1,0:T(8,128)(2,1)S(1)}, bf16[128,512]{1,0:T(8,128)(2,1)S(1)}, u32[]{:S(2)}, u32[]{:S(2)}) collective-permute-start(bf16[128,512]{1,0:T(8,128)(2,1)S(1)} %shard_map.76.own.first), channel_id=1, source_target_pairs={{0,1},{1,0},{2,3},{3,2},{4,5},{5,4},{6,7},{7,6},{8,9},{9,8},{10,11... | collective-permute-start | bytes 393224 | tf_op jit(solution)/shard_map/ppermute | solution.py:418
  30.5 6.8 %collective-permute-start.10 = (bf16[272,128]{1,0:T(8,128)(2,1)S(1)}, bf16[272,128]{1,0:T(8,128)(2,1)S(1)}, u32[]{:S(2)}, u32[]{:S(2)}) collective-permute-start(bf16[272,128]{1,0:T(8,128)(2,1)S(1)} %get-tuple-element.53), channel_id=1, source_target_pairs={{0,12},{2,14},{4,8},{6,10},{8,4},{10,6},{12,0},{14,2},{1,13},{3,15... | collective-permute-start | bytes 208904 | tf_op jit(solution)/shard_map/ppermute | solution.py:413
  32.5 7.1 %collective-permute-start.11 = (bf16[272,128]{1,0:T(8,128)(2,1)S(1)}, bf16[272,128]{1,0:T(8,128)(2,1)S(1)}, u32[]{:S(2)}, u32[]{:S(2)}) collective-permute-start(bf16[272,128]{1,0:T(8,128)(2,1)S(1)} %get-tuple-element.54), channel_id=1, source_target_pairs={{0,8},{2,10},{4,12},{6,14},{8,0},{10,2},{12,4},{14,6},{1,9},{3,11}... | collective-permute-start | bytes 208904 | tf_op jit(solution)/shard_map/ppermute | solution.py:413
  32.9 6.7 %collective-permute-start.12 = (bf16[272,128]{1,0:T(8,128)(2,1)S(1)}, bf16[272,128]{1,0:T(8,128)(2,1)S(1)}, u32[]{:S(2)}, u32[]{:S(2)}) collective-permute-start(bf16[272,128]{1,0:T(8,128)(2,1)S(1)} %get-tuple-element.55), channel_id=1, source_target_pairs={{0,4},{2,6},{4,0},{6,2},{8,12},{10,14},{12,8},{14,10},{1,5},{3,7},... | collective-permute-start | bytes 208904 | tf_op jit(solution)/shard_map/ppermute | solution.py:413
  40.1 4.4 %collective-permute-start.13 = (bf16[272,128]{1,0:T(8,128)(2,1)S(1)}, bf16[272,128]{1,0:T(8,128)(2,1)S(1)}, u32[]{:S(2)}, u32[]{:S(2)}) collective-permute-start(bf16[272,128]{1,0:T(8,128)(2,1)S(1)} %get-tuple-element.58), channel_id=1, source_target_pairs={{0,2},{2,0},{4,6},{6,4},{8,10},{10,8},{12,14},{14,12},{1,3},{3,1},... | collective-permute-start | bytes 208904 | tf_op jit(solution)/shard_map/ppermute | solution.py:422
  44.5 4.3 %collective-permute-start.14 = (bf16[256,128]{1,0:T(8,128)(2,1)S(1)}, bf16[256,128]{1,0:T(8,128)(2,1)S(1)}, u32[]{:S(2)}, u32[]{:S(2)}) collective-permute-start(bf16[256,128]{1,0:T(8,128)(2,1)S(1)} %get-tuple-element.63), channel_id=1, source_target_pairs={{0,2},{2,0},{4,6},{6,4},{8,10},{10,8},{12,14},{14,12},{1,3},{3,1},... | collective-permute-start | bytes 196616 | tf_op jit(solution)/shard_map/ppermute | solution.py:422
  45.7 5.9 %collective-permute-start.15 = (bf16[32,512]{1,0:T(8,128)(2,1)S(1)}, bf16[32,512]{1,0:T(8,128)(2,1)S(1)}, u32[]{:S(2)}, u32[]{:S(2)}) collective-permute-start(bf16[32,512]{1,0:T(8,128)(2,1)S(1)} %get-tuple-element.65), channel_id=1, source_target_pairs={{0,12},{2,14},{4,8},{6,10},{8,4},{10,6},{12,0},{14,2},{1,13},{3,15... | collective-permute-start | bytes 98312 | tf_op jit(solution)/shard_map/ppermute | solution.py:413
  48.2 4.9 %collective-permute-start.16 = (bf16[32,512]{1,0:T(8,128)(2,1)S(1)}, bf16[32,512]{1,0:T(8,128)(2,1)S(1)}, u32[]{:S(2)}, u32[]{:S(2)}) collective-permute-start(bf16[32,512]{1,0:T(8,128)(2,1)S(1)} %get-tuple-element.66), channel_id=1, source_target_pairs={{0,8},{2,10},{4,12},{6,14},{8,0},{10,2},{12,4},{14,6},{1,9},{3,11}... | collective-permute-start | bytes 98312 | tf_op jit(solution)/shard_map/ppermute | solution.py:413
  48.8 4.3 %collective-permute-start.17 = (bf16[32,512]{1,0:T(8,128)(2,1)S(1)}, bf16[32,512]{1,0:T(8,128)(2,1)S(1)}, u32[]{:S(2)}, u32[]{:S(2)}) collective-permute-start(bf16[32,512]{1,0:T(8,128)(2,1)S(1)} %get-tuple-element.67), channel_id=1, source_target_pairs={{0,4},{2,6},{4,0},{6,2},{8,12},{10,14},{12,8},{14,10},{1,5},{3,7},... | collective-permute-start | bytes 98312 | tf_op jit(solution)/shard_map/ppermute | solution.py:413

commit v23 on v19

--- a/solution.py
+++ b/solution.py
@@ -142,9 +142,15 @@
     return first_column + lax.broadcasted_iota(jnp.int32, (1, half), 1) < plan[0:1, 0:1]
 
 
-def apply_term(right, left, vector, term):
-    products = jnp.dot(right[term], vector, preferred_element_type=jnp.float32)
-    return jnp.dot(products.astype(jnp.bfloat16), left, preferred_element_type=jnp.float32)
+def contract_right(right, vector, first, terms):
+    rows = right.shape[1]
+    stacked = right[pl.ds(first, terms)].reshape(terms * rows, rows)
+    products = jnp.dot(stacked, vector, preferred_element_type=jnp.float32)
+    return products.astype(jnp.bfloat16)
+
+
+def contract_left(products, left):
+    return jnp.dot(products, left, preferred_element_type=jnp.float32)
 
 
 def in_order(own, other):
@@ -171,15 +177,19 @@
         live = h * half + columns[0:1, :] < width
         start[h] = jnp.where(live, part, jnp.zeros_like(part))
     vector = jnp.concatenate([start[0], start[1]], axis=1)
+    products = contract_right(right, vector, 1, 2)
+    rows = products.shape[0] // 2
     for term in (1, 2):
-        block = apply_term(right, left[0, term], vector, term).astype(jnp.bfloat16)
+        block = contract_left(products[(term - 1) * rows : term * rows], left[0, term])
+        block = block.astype(jnp.bfloat16)
         block_vmem[...] = block.reshape(block_vmem.shape)
         for step, piece in zip(STEPS, pieces):
             piece[term - 1] = block_vmem[own_place() ^ step]
 
 
 def stay_kernel(vector, right, left, stay):
-    block = apply_term(right, left[0, 0], jnp.concatenate([vector[0], vector[1]], axis=1), 0)
+    products = contract_right(right, jnp.concatenate([vector[0], vector[1]], axis=1), 0, 1)
+    block = contract_left(products, left[0, 0])
     stay[...] = block.astype(stay.dtype)
 
 
@@ -273,8 +283,12 @@
     tag = make_tag((overlap, norm, quotient, rest_norm), lax.axis_index("sec"))
     for piece in pieces:
         piece[pl.ds(2 * chunks * rows, TAG), :] = tag
+    products = contract_right(right, vector, 1, 2)
+    right_rows = products.shape[0] // 2
     for term in (1, 2):
-        block = apply_term(right, left[0, term], vector, term)
+        block = contract_left(
+            products[(term - 1) * right_rows : term * right_rows], left[0, term]
+        )
         block_vmem[...] = block.astype(jnp.bfloat16).reshape(block_vmem.shape)
         for step, piece in zip(STEPS, pieces):
             part = block_vmem[own_place() ^ step]
@@ -298,22 +312,14 @@
     return jnp.where(norm > 0, overlap / jnp.where(norm > 0, norm, 1.0), 0.0)
 
 
-def mix_kernel(plan, *rest):
-    keep, early, late, tag_out, new = rest[-5:]
-    old, *pieces = rest[:-5]
-    places, rows, half = keep.shape
+def mix_targets(plan, part, old, new, tag, keep, cross):
+    rows, half = keep.shape[1:]
     chunks = half // LANES
-    tag = jnp.zeros((TAG, LANES), jnp.float32)
-    for step, piece in zip(STEPS, pieces):
-        new[own_place() ^ step] = piece[...]
-        label = piece[pl.ds(2 * chunks * rows, TAG), :]
-        tag = tag + label.astype(jnp.float32)
-    tag_out[...] = tag.astype(jnp.bfloat16)
-    early[pl.ds(len(EARLY) * chunks * rows, TAG), :] = tag.astype(jnp.bfloat16)
     overlaps, norms, quotients, _ = read_tag(tag)
     shifts = quotients - line_quotient(overlaps, norms, lax.axis_index("sec") % LINES)
     lane = lax.broadcasted_iota(jnp.int32, (1, LANES), 1)
-    for index, crossing, here, source in line_targets(plan, range(places)):
+    for index, crossing, here, source in line_targets(plan, part):
+        position = part.index(index)
         total = 0.0
         for i in range(2):
             where = source[i] // LINES
@@ -326,17 +332,32 @@
             total = total + jnp.where(here[i], block, 0.0)
         if crossing:
             total = total.astype(jnp.bfloat16)
-            out, part = (early, EARLY) if index in EARLY else (late, LATE)
             for c in range(chunks):
-                target = pl.ds((part.index(index) * chunks + c) * rows, rows)
-                out[target, :] = total[:, c * LANES : (c + 1) * LANES]
+                target = pl.ds((position * chunks + c) * rows, rows)
+                cross[target, :] = total[:, c * LANES : (c + 1) * LANES]
         else:
-            keep[index] = total
+            keep[position] = total
+
+
+def mix_early_kernel(plan, old, *rest):
+    *pieces, new, keep, cross, tag_out = rest
+    tag = jnp.zeros((TAG, LANES), jnp.float32)
+    for step, piece in zip(STEPS, pieces):
+        new[own_place() ^ step] = piece[...]
+        tag = tag + piece[pl.ds(piece.shape[0] - TAG, TAG), :].astype(jnp.float32)
+    tag_out[...] = tag.astype(jnp.bfloat16)
+    cross[pl.ds(cross.shape[0] - TAG, TAG), :] = tag.astype(jnp.bfloat16)
+    mix_targets(plan, EARLY, old, new, tag, keep, cross)
+
+
+def mix_late_kernel(plan, old, new, tag, keep, cross):
+    mix_targets(plan, LATE, old, new, tag[...].astype(jnp.float32), keep, cross)
 
 
 def join_early_kernel(plan, tag_line, keep, arrived, old_keep, old_arrived, *rest):
     *outs, factors = rest
-    places, rows, half = keep.shape
+    rows = keep.shape[1]
+    places = len(STEPS)
     slots = places * LINES
     me = lax.axis_index("sec")
     live_count = places * rows * plan[1:2, 0:1].astype(jnp.float32)
@@ -357,25 +378,25 @@
     values = jnp.where(row == 2, shift_here, values)
     factors[...] = jnp.where(row == 3, shift_there, values)
     weights = (scale, shift_here, shift_there)
-    join_mixed(EARLY, weights, keep, arrived, old_keep, old_arrived, outs)
+    join_mixed(weights, keep, arrived, old_keep, old_arrived, outs)
 
 
 def join_late_kernel(factors, keep, arrived, old_keep, old_arrived, *outs):
     weights = [factors[i : i + 1, 0:1] for i in (0, 2, 3)]
-    join_mixed(LATE, weights, keep, arrived, old_keep, old_arrived, outs)
-
-
-def join_mixed(part, weights, keep, arrived, old_keep, old_arrived, outs):
+    join_mixed(weights, keep, arrived, old_keep, old_arrived, outs)
+
+
+def join_mixed(weights, keep, arrived, old_keep, old_arrived, outs):
     scale, shift_here, shift_there = weights
     rows, half = outs[0].shape
     chunks = half // LANES
-    for i, index in enumerate(part):
+    for i, out in enumerate(outs):
         block = jnp.concatenate(
             [arrived[pl.ds((i * chunks + c) * rows, rows), :] for c in range(chunks)], axis=1
         ).astype(jnp.float32)
         block = block + shift_there * old_arrived[i].astype(jnp.float32)
-        block = block + keep[index] + shift_here * old_keep[i].astype(jnp.float32)
-        outs[i][...] = (scale * block).astype(jnp.bfloat16)
+        block = block + keep[i] + shift_here * old_keep[i].astype(jnp.float32)
+        out[...] = (scale * block).astype(jnp.bfloat16)
 
 
 def final_kernel(plan, factors, stay, stay_2, first, *rest):
@@ -435,7 +456,7 @@
     wide = jax.ShapeDtypeStruct((right_dim, half), jnp.float32)
     pair = jax.ShapeDtypeStruct((2, rows, half), jnp.bfloat16)
     single = jax.ShapeDtypeStruct((rows, half), jnp.bfloat16)
-    wides = jax.ShapeDtypeStruct((places, rows, half), jnp.float32)
+    wides = jax.ShapeDtypeStruct((2, rows, half), jnp.float32)
     chunked = rows * half // LANES
     tagged = jax.ShapeDtypeStruct((2 * chunked + TAG, LANES), jnp.bfloat16)
     twos = jax.ShapeDtypeStruct((2, rows, half), jnp.bfloat16)
@@ -446,7 +467,7 @@
     plan_shape = jax.ShapeDtypeStruct((8, LANES), jnp.int32)
     split = [pltpu.VMEM((places, rows, half), jnp.bfloat16)]
     table_shape = jax.ShapeDtypeStruct((places, *pair.shape), jnp.bfloat16)
-    new_table = [pltpu.VMEM((places, *tagged.shape), jnp.bfloat16)]
+    new_shape = jax.ShapeDtypeStruct((places, *tagged.shape), jnp.bfloat16)
 
     slot_table = [pltpu.SMEM((slots,), jnp.int32)]
     plan = call(plan_kernel, [SMEM, SMEM], plan_shape, slot_table)(widths, holders)
@@ -484,15 +505,17 @@
     )(start_full, first, other_core(first), right_env, left_env)
     new = along_line(pieces, slots)
     stay_2 = call(stay_kernel, [VMEM] * 3, wide, flops=dots // 3)(deflated, right_env, left_env)
-    keep, *cross, tag = call(
-        mix_kernel, [VMEM] * (2 + places), (wides, early, late, label), new_table
+    new_table, wide_early, cross, tag = call(
+        mix_early_kernel, [VMEM] * (2 + places), (new_shape, wides, early, label)
     )(plan, table, *new)
-    new_early, new_late = (across(piece, slots) for piece in cross)
+    new_early = across(cross, slots)
+    wide_late, cross = call(mix_late_kernel, [VMEM] * 4, (wides, late))(plan, table, new_table, tag)
+    new_late = across(cross, slots)
     *far, factors = call(join_early_kernel, [VMEM] * 6, (single, single, factor_shape))(
-        plan, tag, keep, new_early, keep_early, old_early
+        plan, tag, wide_early, new_early, keep_early, old_early
     )
     near = call(join_late_kernel, [VMEM] * 5, (single,) * 2)(
-        factors, keep, new_late, keep_late, old_late
+        factors, wide_late, new_late, keep_late, old_late
     )
     joined = (near[0], *far, near[1])
     second, first = call(final_kernel, [VMEM] * (5 + places), (block, block))(

time: 52.2 us -> 52.2 us (level)
    ppermute x4, waiting for transfers between devices: 5.24 us -> 4.54 us  [across(): lax.ppermute(piece, 'sec', [(slot, slot ^ 1) for slot in range(slots)])]
    ppermute x12, waiting for transfers between devices: 13.6 us -> 14.2 us  [along_line(): sent.append(lax.ppermute(piece, 'sec', pairs) if step else piece)]
  transfers between devices with their start and end apart: 18 -> 18, of which waited for: 12 -> 12; matrix products, arithmetic and copies ran while one was open for 0% -> 0% of each run, Pallas kernels for 4% -> 5%
where the time goes in v23:
time: 52.2 us; the launch traced here: 52.1 us
  starting transfers between devices  24.1 us (46%)
  waiting for transfers between devices  21.3 us (41%)
  Pallas kernels  5.74 us (11%)
  between operations  0.79 us (2%)
    ppermute x12, starting transfers between devices, along_line(): sent.append(lax.ppermute(piece, 'sec', pairs) if step else piece)  19.2 us
    ppermute x12, waiting for transfers between devices, along_line(): sent.append(lax.ppermute(piece, 'sec', pairs) if step else piece)  14.2 us
    ppermute x4, waiting for transfers between devices, across(): lax.ppermute(piece, 'sec', [(slot, slot ^ 1) for slot in range(slots)])  4.54 us
    ppermute x4, starting transfers between devices, across(): lax.ppermute(piece, 'sec', [(slot, slot ^ 1) for slot in range(slots)])  4.31 us
    ppermute x2, waiting for transfers between devices, other_core(): return lax.ppermute(block, 'env', [(0, 1), (1, 0)])  2.53 us
  transfers between devices with their start and end apart: 18, of which 12 were waited for; matrix products, arithmetic and copies ran while one was open for 0% of the time, Pallas kernels for 5%

profile of v23, /device:TPU:0, one launch (start us, length us, event | category | flops | bytes accessed | tf_op | source)
XLA Modules:
  0.0 52.1 jit_solution(14837439474588899304)
XLA Ops:
  0.7 0.5 collective-permute-start
  1.2 1.2 %collective-permute-done.other = bf16[128,512]{1,0:T(8,128)(2,1)S(1)} collective-permute-done((bf16[128,512]{1,0:T(8,128)(2,1)}, bf16[128,512]{1,0:T(8,128)(2,1)S(1)}, u32[]{:S(2)}, u32[]{:S(2)}) %collective-permute-start) | collective-permute-done | bytes 131104 | tf_op jit(solution)/shard_map/ppermute | solution.py:439
  2.5 0.8 %shard_map.70 = (bf16[2,32,512]{2,1,0:T(8,128)(2,1)S(1)}, bf16[2,32,512]{2,1,0:T(8,128)(2,1)S(1)}, bf16[2,32,512]{2,1,0:T(8,128)(2,1)S(1)}, bf16[2,32,512]{2,1,0:T(8,128)(2,1)S(1)}, bf16[2,128,512]{2,1,0:T(8,128)(2,1)S(1)}) custom-call(s32[8,512]{1,0:T(8,128)S(1)} %shard_map.69.columns, s32[1,8]{1,0:T(1,128)S(1)} %bitcast.7, s32[1,8]{1,0:T(1,128)S(1)} %bitcast.8, ...), custom_call_target="tpu_custom_call" | custom-call | flops 452984832 | bytes 262144 | tf_op jit(solution)/shard_map/pallas_call | solution.py:477
  3.3 5.1 %collective-permute-start.1 = (bf16[2,32,512]{2,1,0:T(8,128)(2,1)S(1)}, bf16[2,32,512]{2,1,0:T(8,128)(2,1)S(1)}, u32[]{:S(2)}, u32[]{:S(2)}) collective-permute-start(bf16[2,32,512]{2,1,0:T(8,128)(2,1)S(1)} %get-tuple-element.35), channel_id=1, source_target_pairs={{0,12},{2,14},{4,8},{6,10},{8,4},{10,6},{12,0},{14,2},{1,13},{3,15... | collective-permute-start | bytes 196616 | tf_op jit(solution)/shard_map/ppermute | solution.py:434
  8.4 0.6 %collective-permute-start.3 = (bf16[2,32,512]{2,1,0:T(8,128)(2,1)S(1)}, bf16[2,32,512]{2,1,0:T(8,128)(2,1)S(1)}, u32[]{:S(2)}, u32[]{:S(2)}) collective-permute-start(bf16[2,32,512]{2,1,0:T(8,128)(2,1)S(1)} %get-tuple-element.37), channel_id=1, source_target_pairs={{0,4},{2,6},{4,0},{6,2},{8,12},{10,14},{12,8},{14,10},{1,5},{3,7},... | collective-permute-start | bytes 196616 | tf_op jit(solution)/shard_map/ppermute | solution.py:434
  9.1 0.6 %shard_map.68.plan = s32[8,128]{1,0:T(8,128)S(1)} custom-call(s32[8]{0:T(128)S(1)} %copy-done.3, s32[8]{0:T(128)S(1)} %copy-done.4), custom_call_target="tpu_custom_call" | custom-call | bytes 262144 | tf_op jit(solution)/shard_map/pallas_call | solution.py:473
  9.7 1.2 %collective-permute-done.1.rest_1_ = bf16[2,32,512]{2,1,0:T(8,128)(2,1)S(1)} collective-permute-done((bf16[2,32,512]{2,1,0:T(8,128)(2,1)S(1)}, bf16[2,32,512]{2,1,0:T(8,128)(2,1)S(1)}, u32[]{:S(2)}, u32[]{:S(2)}) %collective-permute-start.1) | collective-permute-done | bytes 65568 | tf_op jit(solution)/shard_map/ppermute | solution.py:434
  10.9 3.2 %collective-permute-done.2.rest_2_ = bf16[2,32,512]{2,1,0:T(8,128)(2,1)S(1)} collective-permute-done((bf16[2,32,512]{2,1,0:T(8,128)(2,1)S(1)}, bf16[2,32,512]{2,1,0:T(8,128)(2,1)S(1)}, u32[]{:S(2)}, u32[]{:S(2)}) %collective-permute-start.2) | collective-permute-done | bytes 65568 | tf_op jit(solution)/shard_map/ppermute | solution.py:434
  14.4 1.6 %collective-permute-start.5 = (bf16[2,32,512]{2,1,0:T(8,128)(2,1)S(1)}, bf16[2,32,512]{2,1,0:T(8,128)(2,1)S(1)}, u32[]{:S(2)}, u32[]{:S(2)}) collective-permute-start(bf16[2,32,512]{2,1,0:T(8,128)(2,1)S(1)} %get-tuple-element.44), channel_id=1, source_target_pairs={{0,2},{2,0},{4,6},{6,4},{8,10},{10,8},{12,14},{14,12},{1,3},{3,1},... | collective-permute-start | bytes 196616 | tf_op jit(solution)/shard_map/ppermute | solution.py:443
  16.2 0.6 %collective-permute-start.4 = (bf16[2,32,512]{2,1,0:T(8,128)(2,1)S(1)}, bf16[2,32,512]{2,1,0:T(8,128)(2,1)S(1)}, u32[]{:S(2)}, u32[]{:S(2)}) collective-permute-start(bf16[2,32,512]{2,1,0:T(8,128)(2,1)S(1)} %get-tuple-element.41), channel_id=1, source_target_pairs={{0,2},{2,0},{4,6},{6,4},{8,10},{10,8},{12,14},{14,12},{1,3},{3,1},... | collective-permute-start | bytes 196616 | tf_op jit(solution)/shard_map/ppermute | solution.py:443
  16.8 2.3 %collective-permute-done.5.arrived.old_arrived = bf16[2,32,512]{2,1,0:T(8,128)(2,1)S(1)} collective-permute-done((bf16[2,32,512]{2,1,0:T(8,128)(2,1)S(1)}, bf16[2,32,512]{2,1,0:T(8,128)(2,1)S(1)}, u32[]{:S(2)}, u32[]{:S(2)}) %collective-permute-start.5) | collective-permute-done | bytes 65568 | tf_op jit(solution)/shard_map/ppermute | solution.py:443
  19.2 2.6 %collective-permute-start.6 = (bf16[32,512]{1,0:T(8,128)(2,1)S(1)}, bf16[32,512]{1,0:T(8,128)(2,1)S(1)}, u32[]{:S(2)}, u32[]{:S(2)}) collective-permute-start(bf16[32,512]{1,0:T(8,128)(2,1)S(1)} %get-tuple-element.45), channel_id=1, source_target_pairs={{0,12},{2,14},{4,8},{6,10},{8,4},{10,6},{12,0},{14,2},{1,13},{3,15... | collective-permute-start | bytes 98312 | tf_op jit(solution)/shard_map/ppermute | solution.py:434
  21.8 1.9 %collective-permute-start.8 = (bf16[32,512]{1,0:T(8,128)(2,1)S(1)}, bf16[32,512]{1,0:T(8,128)(2,1)S(1)}, u32[]{:S(2)}, u32[]{:S(2)}) collective-permute-start(bf16[32,512]{1,0:T(8,128)(2,1)S(1)} %get-tuple-element.47), channel_id=1, source_target_pairs={{0,4},{2,6},{4,0},{6,2},{8,12},{10,14},{12,8},{14,10},{1,5},{3,7},... | collective-permute-start | bytes 98312 | tf_op jit(solution)/shard_map/ppermute | solution.py:434
  23.7 0.4 shard_map.72.stay
  24.1 0.8 %collective-permute-done.6.rest_1_ = bf16[32,512]{1,0:T(8,128)(2,1)S(1)} collective-permute-done((bf16[32,512]{1,0:T(8,128)(2,1)S(1)}, bf16[32,512]{1,0:T(8,128)(2,1)S(1)}, u32[]{:S(2)}, u32[]{:S(2)}) %collective-permute-start.6) | collective-permute-done | bytes 32800 | tf_op jit(solution)/shard_map/ppermute | solution.py:434
  24.9 1.6 %collective-permute-done.7.rest_2_ = bf16[32,512]{1,0:T(8,128)(2,1)S(1)} collective-permute-done((bf16[32,512]{1,0:T(8,128)(2,1)S(1)}, bf16[32,512]{1,0:T(8,128)(2,1)S(1)}, u32[]{:S(2)}, u32[]{:S(2)}) %collective-permute-start.7) | collective-permute-done | bytes 32800 | tf_op jit(solution)/shard_map/ppermute | solution.py:434
  26.8 1.3 %collective-permute-done.9.other = bf16[128,512]{1,0:T(8,128)(2,1)S(1)} collective-permute-done((bf16[128,512]{1,0:T(8,128)(2,1)S(1)}, bf16[128,512]{1,0:T(8,128)(2,1)S(1)}, u32[]{:S(2)}, u32[]{:S(2)}) %collective-permute-start.9) | collective-permute-done | bytes 131104 | tf_op jit(solution)/shard_map/ppermute | solution.py:439
  28.1 0.9 %shard_map.77 = (bf16[272,128]{1,0:T(8,128)(2,1)S(1)}, bf16[272,128]{1,0:T(8,128)(2,1)S(1)}, bf16[272,128]{1,0:T(8,128)(2,1)S(1)}, bf16[272,128]{1,0:T(8,128)(2,1)S(1)}, bf16[2,128,512]{2,1,0:T(8,128)(2,1)S(1)}) custom-call(bf16[2,128,512]{2,1,0:T(8,128)(2,1)S(1)} %get-tuple-element.39.vector.start, bf16[128,512]{1,0:T(8,128)(2,1)S(1)} %shard_map.76.own.first, ...), custom_call_target="tpu_custom_call" | custom-call | flops 452984832 | bytes 262144 | tf_op jit(solution)/shard_map/pallas_call | solution.py:503
  29.0 1.9 %collective-permute-start.10 = (bf16[272,128]{1,0:T(8,128)(2,1)S(1)}, bf16[272,128]{1,0:T(8,128)(2,1)S(1)}, u32[]{:S(2)}, u32[]{:S(2)}) collective-permute-start(bf16[272,128]{1,0:T(8,128)(2,1)S(1)} %get-tuple-element.49), channel_id=1, source_target_pairs={{0,12},{2,14},{4,8},{6,10},{8,4},{10,6},{12,0},{14,2},{1,13},{3,15... | collective-permute-start | bytes 208904 | tf_op jit(solution)/shard_map/ppermute | solution.py:434
  30.9 0.6 %collective-permute-start.11 = (bf16[272,128]{1,0:T(8,128)(2,1)S(1)}, bf16[272,128]{1,0:T(8,128)(2,1)S(1)}, u32[]{:S(2)}, u32[]{:S(2)}) collective-permute-start(bf16[272,128]{1,0:T(8,128)(2,1)S(1)} %get-tuple-element.50), channel_id=1, source_target_pairs={{0,8},{2,10},{4,12},{6,14},{8,0},{10,2},{12,4},{14,6},{1,9},{3,11}... | collective-permute-start | bytes 208904 | tf_op jit(solution)/shard_map/ppermute | solution.py:434
  31.5 1.9 %collective-permute-start.12 = (bf16[272,128]{1,0:T(8,128)(2,1)S(1)}, bf16[272,128]{1,0:T(8,128)(2,1)S(1)}, u32[]{:S(2)}, u32[]{:S(2)}) collective-permute-start(bf16[272,128]{1,0:T(8,128)(2,1)S(1)} %get-tuple-element.51), channel_id=1, source_target_pairs={{0,4},{2,6},{4,0},{6,2},{8,12},{10,14},{12,8},{14,10},{1,5},{3,7},... | collective-permute-start | bytes 208904 | tf_op jit(solution)/shard_map/ppermute | solution.py:434
  33.4 2.4 %collective-permute-done.10.rest_1_ = bf16[272,128]{1,0:T(8,128)(2,1)S(1)} collective-permute-done((bf16[272,128]{1,0:T(8,128)(2,1)S(1)}, bf16[272,128]{1,0:T(8,128)(2,1)S(1)}, u32[]{:S(2)}, u32[]{:S(2)}) %collective-permute-start.10) | collective-permute-done | bytes 69664 | tf_op jit(solution)/shard_map/ppermute | solution.py:434
  35.8 2.5 %collective-permute-done.11.rest_2_ = bf16[272,128]{1,0:T(8,128)(2,1)S(1)} collective-permute-done((bf16[272,128]{1,0:T(8,128)(2,1)S(1)}, bf16[272,128]{1,0:T(8,128)(2,1)S(1)}, u32[]{:S(2)}, u32[]{:S(2)}) %collective-permute-start.11) | collective-permute-done | bytes 69664 | tf_op jit(solution)/shard_map/ppermute | solution.py:434
  38.7 1.3 %collective-permute-start.13 = (bf16[272,128]{1,0:T(8,128)(2,1)S(1)}, bf16[272,128]{1,0:T(8,128)(2,1)S(1)}, u32[]{:S(2)}, u32[]{:S(2)}) collective-permute-start(bf16[272,128]{1,0:T(8,128)(2,1)S(1)} %get-tuple-element.54), channel_id=1, source_target_pairs={{0,2},{2,0},{4,6},{6,4},{8,10},{10,8},{12,14},{14,12},{1,3},{3,1},... | collective-permute-start | bytes 208904 | tf_op jit(solution)/shard_map/ppermute | solution.py:443
  40.4 0.9 %collective-permute-start.14 = (bf16[256,128]{1,0:T(8,128)(2,1)S(1)}, bf16[256,128]{1,0:T(8,128)(2,1)S(1)}, u32[]{:S(2)}, u32[]{:S(2)}) collective-permute-start(bf16[256,128]{1,0:T(8,128)(2,1)S(1)} %get-tuple-element.59), channel_id=1, source_target_pairs={{0,2},{2,0},{4,6},{6,4},{8,10},{10,8},{12,14},{14,12},{1,3},{3,1},... | collective-permute-start | bytes 196616 | tf_op jit(solution)/shard_map/ppermute | solution.py:443
  41.3 2.2 %collective-permute-done.13.arrived = bf16[272,128]{1,0:T(8,128)(2,1)S(1)} collective-permute-done((bf16[272,128]{1,0:T(8,128)(2,1)S(1)}, bf16[272,128]{1,0:T(8,128)(2,1)S(1)}, u32[]{:S(2)}, u32[]{:S(2)}) %collective-permute-start.13) | collective-permute-done | bytes 69664 | tf_op jit(solution)/shard_map/ppermute | solution.py:443
  43.9 2.6 %collective-permute-start.15 = (bf16[32,512]{1,0:T(8,128)(2,1)S(1)}, bf16[32,512]{1,0:T(8,128)(2,1)S(1)}, u32[]{:S(2)}, u32[]{:S(2)}) collective-permute-start(bf16[32,512]{1,0:T(8,128)(2,1)S(1)} %get-tuple-element.61), channel_id=1, source_target_pairs={{0,12},{2,14},{4,8},{6,10},{8,4},{10,6},{12,0},{14,2},{1,13},{3,15... | collective-permute-start | bytes 98312 | tf_op jit(solution)/shard_map/ppermute | solution.py:434
  46.6 1.9 %collective-permute-start.17 = (bf16[32,512]{1,0:T(8,128)(2,1)S(1)}, bf16[32,512]{1,0:T(8,128)(2,1)S(1)}, u32[]{:S(2)}, u32[]{:S(2)}) collective-permute-start(bf16[32,512]{1,0:T(8,128)(2,1)S(1)} %get-tuple-element.63), channel_id=1, source_target_pairs={{0,4},{2,6},{4,0},{6,2},{8,12},{10,14},{12,8},{14,10},{1,5},{3,7},... | collective-permute-start | bytes 98312 | tf_op jit(solution)/shard_map/ppermute | solution.py:434
  48.5 0.4 shard_map.80.stay_2
  48.9 0.7 %collective-permute-done.15.rest_1_ = bf16[32,512]{1,0:T(8,128)(2,1)S(1)} collective-permute-done((bf16[32,512]{1,0:T(8,128)(2,1)S(1)}, bf16[32,512]{1,0:T(8,128)(2,1)S(1)}, u32[]{:S(2)}, u32[]{:S(2)}) %collective-permute-start.15) | collective-permute-done | bytes 32800 | tf_op jit(solution)/shard_map/ppermute | solution.py:434
  49.6 1.7 %collective-permute-done.16.rest_2_ = bf16[32,512]{1,0:T(8,128)(2,1)S(1)} collective-permute-done((bf16[32,512]{1,0:T(8,128)(2,1)S(1)}, bf16[32,512]{1,0:T(8,128)(2,1)S(1)}, u32[]{:S(2)}, u32[]{:S(2)}) %collective-permute-start.16) | collective-permute-done | bytes 32800 | tf_op jit(solution)/shard_map/ppermute | solution.py:434
  51.3 0.8 %shard_map.83 = (bf16[128,512]{1,0:T(8,128)(2,1)}, bf16[128,512]{1,0:T(8,128)(2,1)}) custom-call(s32[8,128]{1,0:T(8,128)S(1)} %shard_map.68.plan, f32[8,128]{1,0:T(8,128)S(1)} %get-tuple-element.55.factors, bf16[128,512]{1,0:T(8,128)(2,1)S(1)} %shard_map.72.stay, f32[128,512]{1,0:T(8,128)S(1)} %shard_map.80.stay_2, ...), custom_call_target="tpu_custom_call" | custom-call | bytes 262144 | tf_op jit(solution)/shard_map/pallas_call | solution.py:521
  (30 shorter events, 2.1 us)
Async XLA Ops:
  0.6 1.9 %copy-start = (bf16[1,3,1024,512]{3,2,1,0:T(8,128)(2,1)S(1)}, bf16[1,3,1024,512]{3,2,1,0:T(8,128)(2,1)}, u32[]{:S(2)}) copy-start(bf16[1,3,1024,512]{3,2,1,0:T(8,128)(2,1)} %left.7) | copy-start | bytes 9437188
  0.6 1.9 %copy-start.1 = (bf16[3,128,128]{2,1,0:T(8,128)(2,1)S(1)}, bf16[3,128,128]{2,1,0:T(8,128)(2,1)}, u32[]{:S(2)}) copy-start(bf16[3,128,128]{2,1,0:T(8,128)(2,1)} %right.7) | copy-start | bytes 294916
  0.7 1.9 %copy-start.2 = (bf16[1,128,512]{2,1,0:T(8,128)(2,1)S(1)}, bf16[1,128,512]{2,1,0:T(8,128)(2,1)}, u32[]{:S(2)}) copy-start(bf16[1,128,512]{2,1,0:T(8,128)(2,1)} %param.5) | copy-start | bytes 393220
  0.7 1.9 %copy-start.3 = (s32[8]{0:T(128)S(1)}, s32[8]{0:T(128)}, u32[]{:S(2)}) copy-start(s32[8]{0:T(128)} %widths.1) | copy-start | bytes 100
  0.7 1.9 %copy-start.4 = (s32[8]{0:T(128)S(1)}, s32[8]{0:T(128)}, u32[]{:S(2)}) copy-start(s32[8]{0:T(128)} %holders.1) | copy-start | bytes 100
  0.7 1.7 %collective-permute-start = (bf16[128,512]{1,0:T(8,128)(2,1)}, bf16[128,512]{1,0:T(8,128)(2,1)S(1)}, u32[]{:S(2)}, u32[]{:S(2)}) collective-permute-start(bf16[128,512]{1,0:T(8,128)(2,1)} %bitcast.5), channel_id=1, source_target_pairs={{0,1},{1,0},{2,3},{3,2},{4,5},{5,4},{6,7},{7,6},{8,9},{9,8},{10,11... | collective-permute-start | bytes 393224 | tf_op jit(solution)/shard_map/ppermute | solution.py:439
  3.3 7.6 %collective-permute-start.1 = (bf16[2,32,512]{2,1,0:T(8,128)(2,1)S(1)}, bf16[2,32,512]{2,1,0:T(8,128)(2,1)S(1)}, u32[]{:S(2)}, u32[]{:S(2)}) collective-permute-start(bf16[2,32,512]{2,1,0:T(8,128)(2,1)S(1)} %get-tuple-element.35), channel_id=1, source_target_pairs={{0,12},{2,14},{4,8},{6,10},{8,4},{10,6},{12,0},{14,2},{1,13},{3,15... | collective-permute-start | bytes 196616 | tf_op jit(solution)/shard_map/ppermute | solution.py:434
  8.4 5.7 %collective-permute-start.2 = (bf16[2,32,512]{2,1,0:T(8,128)(2,1)S(1)}, bf16[2,32,512]{2,1,0:T(8,128)(2,1)S(1)}, u32[]{:S(2)}, u32[]{:S(2)}) collective-permute-start(bf16[2,32,512]{2,1,0:T(8,128)(2,1)S(1)} %get-tuple-element.36), channel_id=1, source_target_pairs={{0,8},{2,10},{4,12},{6,14},{8,0},{10,2},{12,4},{14,6},{1,9},{3,11}... | collective-permute-start | bytes 196616 | tf_op jit(solution)/shard_map/ppermute | solution.py:434
  8.4 5.7 %collective-permute-start.3 = (bf16[2,32,512]{2,1,0:T(8,128)(2,1)S(1)}, bf16[2,32,512]{2,1,0:T(8,128)(2,1)S(1)}, u32[]{:S(2)}, u32[]{:S(2)}) collective-permute-start(bf16[2,32,512]{2,1,0:T(8,128)(2,1)S(1)} %get-tuple-element.37), channel_id=1, source_target_pairs={{0,4},{2,6},{4,0},{6,2},{8,12},{10,14},{12,8},{14,10},{1,5},{3,7},... | collective-permute-start | bytes 196616 | tf_op jit(solution)/shard_map/ppermute | solution.py:434
  14.4 4.7 %collective-permute-start.5 = (bf16[2,32,512]{2,1,0:T(8,128)(2,1)S(1)}, bf16[2,32,512]{2,1,0:T(8,128)(2,1)S(1)}, u32[]{:S(2)}, u32[]{:S(2)}) collective-permute-start(bf16[2,32,512]{2,1,0:T(8,128)(2,1)S(1)} %get-tuple-element.44), channel_id=1, source_target_pairs={{0,2},{2,0},{4,6},{6,4},{8,10},{10,8},{12,14},{14,12},{1,3},{3,1},... | collective-permute-start | bytes 196616 | tf_op jit(solution)/shard_map/ppermute | solution.py:443
  16.2 5.6 %collective-permute-start.4 = (bf16[2,32,512]{2,1,0:T(8,128)(2,1)S(1)}, bf16[2,32,512]{2,1,0:T(8,128)(2,1)S(1)}, u32[]{:S(2)}, u32[]{:S(2)}) collective-permute-start(bf16[2,32,512]{2,1,0:T(8,128)(2,1)S(1)} %get-tuple-element.41), channel_id=1, source_target_pairs={{0,2},{2,0},{4,6},{6,4},{8,10},{10,8},{12,14},{14,12},{1,3},{3,1},... | collective-permute-start | bytes 196616 | tf_op jit(solution)/shard_map/ppermute | solution.py:443
  19.2 5.8 %collective-permute-start.6 = (bf16[32,512]{1,0:T(8,128)(2,1)S(1)}, bf16[32,512]{1,0:T(8,128)(2,1)S(1)}, u32[]{:S(2)}, u32[]{:S(2)}) collective-permute-start(bf16[32,512]{1,0:T(8,128)(2,1)S(1)} %get-tuple-element.45), channel_id=1, source_target_pairs={{0,12},{2,14},{4,8},{6,10},{8,4},{10,6},{12,0},{14,2},{1,13},{3,15... | collective-permute-start | bytes 98312 | tf_op jit(solution)/shard_map/ppermute | solution.py:434
  21.8 4.8 %collective-permute-start.7 = (bf16[32,512]{1,0:T(8,128)(2,1)S(1)}, bf16[32,512]{1,0:T(8,128)(2,1)S(1)}, u32[]{:S(2)}, u32[]{:S(2)}) collective-permute-start(bf16[32,512]{1,0:T(8,128)(2,1)S(1)} %get-tuple-element.46), channel_id=1, source_target_pairs={{0,8},{2,10},{4,12},{6,14},{8,0},{10,2},{12,4},{14,6},{1,9},{3,11}... | collective-permute-start | bytes 98312 | tf_op jit(solution)/shard_map/ppermute | solution.py:434
  21.8 4.8 %collective-permute-start.8 = (bf16[32,512]{1,0:T(8,128)(2,1)S(1)}, bf16[32,512]{1,0:T(8,128)(2,1)S(1)}, u32[]{:S(2)}, u32[]{:S(2)}) collective-permute-start(bf16[32,512]{1,0:T(8,128)(2,1)S(1)} %get-tuple-element.47), channel_id=1, source_target_pairs={{0,4},{2,6},{4,0},{6,2},{8,12},{10,14},{12,8},{14,10},{1,5},{3,7},... | collective-permute-start | bytes 98312 | tf_op jit(solution)/shard_map/ppermute | solution.py:434
  26.7 1.4 %collective-permute-start.9 = (bf16[128,512]{1,0:T(8,128)(2,1)S(1)}, bf16[128,512]{1,0:T(8,128)(2,1)S(1)}, u32[]{:S(2)}, u32[]{:S(2)}) collective-permute-start(bf16[128,512]{1,0:T(8,128)(2,1)S(1)} %shard_map.76.own.first), channel_id=1, source_target_pairs={{0,1},{1,0},{2,3},{3,2},{4,5},{5,4},{6,7},{7,6},{8,9},{9,8},{10,11... | collective-permute-start | bytes 393224 | tf_op jit(solution)/shard_map/ppermute | solution.py:439
  29.0 6.8 %collective-permute-start.10 = (bf16[272,128]{1,0:T(8,128)(2,1)S(1)}, bf16[272,128]{1,0:T(8,128)(2,1)S(1)}, u32[]{:S(2)}, u32[]{:S(2)}) collective-permute-start(bf16[272,128]{1,0:T(8,128)(2,1)S(1)} %get-tuple-element.49), channel_id=1, source_target_pairs={{0,12},{2,14},{4,8},{6,10},{8,4},{10,6},{12,0},{14,2},{1,13},{3,15... | collective-permute-start | bytes 208904 | tf_op jit(solution)/shard_map/ppermute | solution.py:434
  30.9 7.4 %collective-permute-start.11 = (bf16[272,128]{1,0:T(8,128)(2,1)S(1)}, bf16[272,128]{1,0:T(8,128)(2,1)S(1)}, u32[]{:S(2)}, u32[]{:S(2)}) collective-permute-start(bf16[272,128]{1,0:T(8,128)(2,1)S(1)} %get-tuple-element.50), channel_id=1, source_target_pairs={{0,8},{2,10},{4,12},{6,14},{8,0},{10,2},{12,4},{14,6},{1,9},{3,11}... | collective-permute-start | bytes 208904 | tf_op jit(solution)/shard_map/ppermute | solution.py:434
  31.5 6.8 %collective-permute-start.12 = (bf16[272,128]{1,0:T(8,128)(2,1)S(1)}, bf16[272,128]{1,0:T(8,128)(2,1)S(1)}, u32[]{:S(2)}, u32[]{:S(2)}) collective-permute-start(bf16[272,128]{1,0:T(8,128)(2,1)S(1)} %get-tuple-element.51), channel_id=1, source_target_pairs={{0,4},{2,6},{4,0},{6,2},{8,12},{10,14},{12,8},{14,10},{1,5},{3,7},... | collective-permute-start | bytes 208904 | tf_op jit(solution)/shard_map/ppermute | solution.py:434
  38.7 4.8 %collective-permute-start.13 = (bf16[272,128]{1,0:T(8,128)(2,1)S(1)}, bf16[272,128]{1,0:T(8,128)(2,1)S(1)}, u32[]{:S(2)}, u32[]{:S(2)}) collective-permute-start(bf16[272,128]{1,0:T(8,128)(2,1)S(1)} %get-tuple-element.54), channel_id=1, source_target_pairs={{0,2},{2,0},{4,6},{6,4},{8,10},{10,8},{12,14},{14,12},{1,3},{3,1},... | collective-permute-start | bytes 208904 | tf_op jit(solution)/shard_map/ppermute | solution.py:443
  40.4 6.0 %collective-permute-start.14 = (bf16[256,128]{1,0:T(8,128)(2,1)S(1)}, bf16[256,128]{1,0:T(8,128)(2,1)S(1)}, u32[]{:S(2)}, u32[]{:S(2)}) collective-permute-start(bf16[256,128]{1,0:T(8,128)(2,1)S(1)} %get-tuple-element.59), channel_id=1, source_target_pairs={{0,2},{2,0},{4,6},{6,4},{8,10},{10,8},{12,14},{14,12},{1,3},{3,1},... | collective-permute-start | bytes 196616 | tf_op jit(solution)/shard_map/ppermute | solution.py:443
  43.9 5.8 %collective-permute-start.15 = (bf16[32,512]{1,0:T(8,128)(2,1)S(1)}, bf16[32,512]{1,0:T(8,128)(2,1)S(1)}, u32[]{:S(2)}, u32[]{:S(2)}) collective-permute-start(bf16[32,512]{1,0:T(8,128)(2,1)S(1)} %get-tuple-element.61), channel_id=1, source_target_pairs={{0,12},{2,14},{4,8},{6,10},{8,4},{10,6},{12,0},{14,2},{1,13},{3,15... | collective-permute-start | bytes 98312 | tf_op jit(solution)/shard_map/ppermute | solution.py:434
  46.5 4.8 %collective-permute-start.16 = (bf16[32,512]{1,0:T(8,128)(2,1)S(1)}, bf16[32,512]{1,0:T(8,128)(2,1)S(1)}, u32[]{:S(2)}, u32[]{:S(2)}) collective-permute-start(bf16[32,512]{1,0:T(8,128)(2,1)S(1)} %get-tuple-element.62), channel_id=1, source_target_pairs={{0,8},{2,10},{4,12},{6,14},{8,0},{10,2},{12,4},{14,6},{1,9},{3,11}... | collective-permute-start | bytes 98312 | tf_op jit(solution)/shard_map/ppermute | solution.py:434
  46.6 4.7 %collective-permute-start.17 = (bf16[32,512]{1,0:T(8,128)(2,1)S(1)}, bf16[32,512]{1,0:T(8,128)(2,1)S(1)}, u32[]{:S(2)}, u32[]{:S(2)}) collective-permute-start(bf16[32,512]{1,0:T(8,128)(2,1)S(1)} %get-tuple-element.63), channel_id=1, source_target_pairs={{0,4},{2,6},{4,0},{6,2},{8,12},{10,14},{12,8},{14,10},{1,5},{3,7},... | collective-permute-start | bytes 98312 | tf_op jit(solution)/shard_map/ppermute | solution.py:434

commit v24 on v19

--- a/solution.py
+++ b/solution.py
@@ -142,9 +142,15 @@
     return first_column + lax.broadcasted_iota(jnp.int32, (1, half), 1) < plan[0:1, 0:1]
 
 
-def apply_term(right, left, vector, term):
-    products = jnp.dot(right[term], vector, preferred_element_type=jnp.float32)
-    return jnp.dot(products.astype(jnp.bfloat16), left, preferred_element_type=jnp.float32)
+def contract_right(right, vector, first, terms):
+    rows = right.shape[1]
+    stacked = right[pl.ds(first, terms)].reshape(terms * rows, rows)
+    products = jnp.dot(stacked, vector, preferred_element_type=jnp.float32)
+    return products.astype(jnp.bfloat16)
+
+
+def contract_left(products, left):
+    return jnp.dot(products, left, preferred_element_type=jnp.float32)
 
 
 def in_order(own, other):
@@ -171,15 +177,19 @@
         live = h * half + columns[0:1, :] < width
         start[h] = jnp.where(live, part, jnp.zeros_like(part))
     vector = jnp.concatenate([start[0], start[1]], axis=1)
+    products = contract_right(right, vector, 1, 2)
+    rows = products.shape[0] // 2
     for term in (1, 2):
-        block = apply_term(right, left[0, term], vector, term).astype(jnp.bfloat16)
+        block = contract_left(products[(term - 1) * rows : term * rows], left[0, term])
+        block = block.astype(jnp.bfloat16)
         block_vmem[...] = block.reshape(block_vmem.shape)
         for step, piece in zip(STEPS, pieces):
             piece[term - 1] = block_vmem[own_place() ^ step]
 
 
 def stay_kernel(vector, right, left, stay):
-    block = apply_term(right, left[0, 0], jnp.concatenate([vector[0], vector[1]], axis=1), 0)
+    products = contract_right(right, jnp.concatenate([vector[0], vector[1]], axis=1), 0, 1)
+    block = contract_left(products, left[0, 0])
     stay[...] = block.astype(stay.dtype)
 
 
@@ -273,8 +283,12 @@
     tag = make_tag((overlap, norm, quotient, rest_norm), lax.axis_index("sec"))
     for piece in pieces:
         piece[pl.ds(2 * chunks * rows, TAG), :] = tag
+    products = contract_right(right, vector, 1, 2)
+    right_rows = products.shape[0] // 2
     for term in (1, 2):
-        block = apply_term(right, left[0, term], vector, term)
+        block = contract_left(
+            products[(term - 1) * right_rows : term * right_rows], left[0, term]
+        )
         block_vmem[...] = block.astype(jnp.bfloat16).reshape(block_vmem.shape)
         for step, piece in zip(STEPS, pieces):
             part = block_vmem[own_place() ^ step]

time: 52.2 us -> 51.9 us (level)
  no operation moved by 1% of the time
where the time goes in v24:
time: 51.9 us; the launch traced here: 51.8 us
  starting transfers between devices  24.1 us (46%)
  waiting for transfers between devices  21.4 us (41%)
  Pallas kernels  5.41 us (10%)
  between operations  0.78 us (2%)
    ppermute x12, starting transfers between devices, along_line(): sent.append(lax.ppermute(piece, 'sec', pairs) if step else piece)  19.2 us
    ppermute x12, waiting for transfers between devices, along_line(): sent.append(lax.ppermute(piece, 'sec', pairs) if step else piece)  13.6 us
    ppermute x4, waiting for transfers between devices, across(): lax.ppermute(piece, 'sec', [(slot, slot ^ 1) for slot in range(slots)])  5.24 us
    ppermute x4, starting transfers between devices, across(): lax.ppermute(piece, 'sec', [(slot, slot ^ 1) for slot in range(slots)])  4.25 us
    ppermute x2, waiting for transfers between devices, other_core(): return lax.ppermute(block, 'env', [(0, 1), (1, 0)])  2.53 us
  transfers between devices with their start and end apart: 18, of which 12 were waited for; matrix products, arithmetic and copies ran while one was open for 0% of the time, Pallas kernels for 4%

profile of v24, /device:TPU:0, one launch (start us, length us, event | category | flops | bytes accessed | tf_op | source)
XLA Modules:
  0.0 51.8 jit_solution(16484690494289822497)
XLA Ops:
  0.7 0.5 collective-permute-start
  1.2 1.2 %collective-permute-done.other = bf16[128,512]{1,0:T(8,128)(2,1)S(1)} collective-permute-done((bf16[128,512]{1,0:T(8,128)(2,1)}, bf16[128,512]{1,0:T(8,128)(2,1)S(1)}, u32[]{:S(2)}, u32[]{:S(2)}) %collective-permute-start) | collective-permute-done | bytes 131104 | tf_op jit(solution)/shard_map/ppermute | solution.py:432
  2.5 0.8 %shard_map.70 = (bf16[2,32,512]{2,1,0:T(8,128)(2,1)S(1)}, bf16[2,32,512]{2,1,0:T(8,128)(2,1)S(1)}, bf16[2,32,512]{2,1,0:T(8,128)(2,1)S(1)}, bf16[2,32,512]{2,1,0:T(8,128)(2,1)S(1)}, bf16[2,128,512]{2,1,0:T(8,128)(2,1)S(1)}) custom-call(s32[8,512]{1,0:T(8,128)S(1)} %shard_map.69.columns, s32[1,8]{1,0:T(1,128)S(1)} %bitcast.7, s32[1,8]{1,0:T(1,128)S(1)} %bitcast.8, ...), custom_call_target="tpu_custom_call" | custom-call | flops 452984832 | bytes 262144 | tf_op jit(solution)/shard_map/pallas_call | solution.py:470
  3.3 5.1 %collective-permute-start.1 = (bf16[2,32,512]{2,1,0:T(8,128)(2,1)S(1)}, bf16[2,32,512]{2,1,0:T(8,128)(2,1)S(1)}, u32[]{:S(2)}, u32[]{:S(2)}) collective-permute-start(bf16[2,32,512]{2,1,0:T(8,128)(2,1)S(1)} %get-tuple-element.33), channel_id=1, source_target_pairs={{0,12},{2,14},{4,8},{6,10},{8,4},{10,6},{12,0},{14,2},{1,13},{3,15... | collective-permute-start | bytes 196616 | tf_op jit(solution)/shard_map/ppermute | solution.py:427
  8.4 0.6 %collective-permute-start.3 = (bf16[2,32,512]{2,1,0:T(8,128)(2,1)S(1)}, bf16[2,32,512]{2,1,0:T(8,128)(2,1)S(1)}, u32[]{:S(2)}, u32[]{:S(2)}) collective-permute-start(bf16[2,32,512]{2,1,0:T(8,128)(2,1)S(1)} %get-tuple-element.35), channel_id=1, source_target_pairs={{0,4},{2,6},{4,0},{6,2},{8,12},{10,14},{12,8},{14,10},{1,5},{3,7},... | collective-permute-start | bytes 196616 | tf_op jit(solution)/shard_map/ppermute | solution.py:427
  9.1 0.6 %shard_map.68.plan = s32[8,128]{1,0:T(8,128)S(1)} custom-call(s32[8]{0:T(128)S(1)} %copy-done.3, s32[8]{0:T(128)S(1)} %copy-done.4), custom_call_target="tpu_custom_call" | custom-call | bytes 262144 | tf_op jit(solution)/shard_map/pallas_call | solution.py:466
  9.7 1.2 %collective-permute-done.1.rest_1_ = bf16[2,32,512]{2,1,0:T(8,128)(2,1)S(1)} collective-permute-done((bf16[2,32,512]{2,1,0:T(8,128)(2,1)S(1)}, bf16[2,32,512]{2,1,0:T(8,128)(2,1)S(1)}, u32[]{:S(2)}, u32[]{:S(2)}) %collective-permute-start.1) | collective-permute-done | bytes 65568 | tf_op jit(solution)/shard_map/ppermute | solution.py:427
  10.9 3.2 %collective-permute-done.2.rest_2_ = bf16[2,32,512]{2,1,0:T(8,128)(2,1)S(1)} collective-permute-done((bf16[2,32,512]{2,1,0:T(8,128)(2,1)S(1)}, bf16[2,32,512]{2,1,0:T(8,128)(2,1)S(1)}, u32[]{:S(2)}, u32[]{:S(2)}) %collective-permute-start.2) | collective-permute-done | bytes 65568 | tf_op jit(solution)/shard_map/ppermute | solution.py:427
  14.4 1.6 %collective-permute-start.5 = (bf16[2,32,512]{2,1,0:T(8,128)(2,1)S(1)}, bf16[2,32,512]{2,1,0:T(8,128)(2,1)S(1)}, u32[]{:S(2)}, u32[]{:S(2)}) collective-permute-start(bf16[2,32,512]{2,1,0:T(8,128)(2,1)S(1)} %get-tuple-element.42), channel_id=1, source_target_pairs={{0,2},{2,0},{4,6},{6,4},{8,10},{10,8},{12,14},{14,12},{1,3},{3,1},... | collective-permute-start | bytes 196616 | tf_op jit(solution)/shard_map/ppermute | solution.py:436
  16.2 0.6 %collective-permute-start.4 = (bf16[2,32,512]{2,1,0:T(8,128)(2,1)S(1)}, bf16[2,32,512]{2,1,0:T(8,128)(2,1)S(1)}, u32[]{:S(2)}, u32[]{:S(2)}) collective-permute-start(bf16[2,32,512]{2,1,0:T(8,128)(2,1)S(1)} %get-tuple-element.39), channel_id=1, source_target_pairs={{0,2},{2,0},{4,6},{6,4},{8,10},{10,8},{12,14},{14,12},{1,3},{3,1},... | collective-permute-start | bytes 196616 | tf_op jit(solution)/shard_map/ppermute | solution.py:436
  16.8 2.3 %collective-permute-done.5.arrived.old_arrived = bf16[2,32,512]{2,1,0:T(8,128)(2,1)S(1)} collective-permute-done((bf16[2,32,512]{2,1,0:T(8,128)(2,1)S(1)}, bf16[2,32,512]{2,1,0:T(8,128)(2,1)S(1)}, u32[]{:S(2)}, u32[]{:S(2)}) %collective-permute-start.5) | collective-permute-done | bytes 65568 | tf_op jit(solution)/shard_map/ppermute | solution.py:436
  19.2 2.6 %collective-permute-start.6 = (bf16[32,512]{1,0:T(8,128)(2,1)S(1)}, bf16[32,512]{1,0:T(8,128)(2,1)S(1)}, u32[]{:S(2)}, u32[]{:S(2)}) collective-permute-start(bf16[32,512]{1,0:T(8,128)(2,1)S(1)} %get-tuple-element.43), channel_id=1, source_target_pairs={{0,12},{2,14},{4,8},{6,10},{8,4},{10,6},{12,0},{14,2},{1,13},{3,15... | collective-permute-start | bytes 98312 | tf_op jit(solution)/shard_map/ppermute | solution.py:427
  21.8 1.9 %collective-permute-start.8 = (bf16[32,512]{1,0:T(8,128)(2,1)S(1)}, bf16[32,512]{1,0:T(8,128)(2,1)S(1)}, u32[]{:S(2)}, u32[]{:S(2)}) collective-permute-start(bf16[32,512]{1,0:T(8,128)(2,1)S(1)} %get-tuple-element.45), channel_id=1, source_target_pairs={{0,4},{2,6},{4,0},{6,2},{8,12},{10,14},{12,8},{14,10},{1,5},{3,7},... | collective-permute-start | bytes 98312 | tf_op jit(solution)/shard_map/ppermute | solution.py:427
  23.7 0.4 shard_map.72.stay
  24.1 0.8 %collective-permute-done.6.rest_1_ = bf16[32,512]{1,0:T(8,128)(2,1)S(1)} collective-permute-done((bf16[32,512]{1,0:T(8,128)(2,1)S(1)}, bf16[32,512]{1,0:T(8,128)(2,1)S(1)}, u32[]{:S(2)}, u32[]{:S(2)}) %collective-permute-start.6) | collective-permute-done | bytes 32800 | tf_op jit(solution)/shard_map/ppermute | solution.py:427
  24.9 1.6 %collective-permute-done.7.rest_2_ = bf16[32,512]{1,0:T(8,128)(2,1)S(1)} collective-permute-done((bf16[32,512]{1,0:T(8,128)(2,1)S(1)}, bf16[32,512]{1,0:T(8,128)(2,1)S(1)}, u32[]{:S(2)}, u32[]{:S(2)}) %collective-permute-start.7) | collective-permute-done | bytes 32800 | tf_op jit(solution)/shard_map/ppermute | solution.py:427
  26.8 1.3 %collective-permute-done.9.other = bf16[128,512]{1,0:T(8,128)(2,1)S(1)} collective-permute-done((bf16[128,512]{1,0:T(8,128)(2,1)S(1)}, bf16[128,512]{1,0:T(8,128)(2,1)S(1)}, u32[]{:S(2)}, u32[]{:S(2)}) %collective-permute-start.9) | collective-permute-done | bytes 131104 | tf_op jit(solution)/shard_map/ppermute | solution.py:432
  28.1 0.9 %shard_map.77 = (bf16[272,128]{1,0:T(8,128)(2,1)S(1)}, bf16[272,128]{1,0:T(8,128)(2,1)S(1)}, bf16[272,128]{1,0:T(8,128)(2,1)S(1)}, bf16[272,128]{1,0:T(8,128)(2,1)S(1)}, bf16[2,128,512]{2,1,0:T(8,128)(2,1)S(1)}) custom-call(bf16[2,128,512]{2,1,0:T(8,128)(2,1)S(1)} %get-tuple-element.37.vector.start, bf16[128,512]{1,0:T(8,128)(2,1)S(1)} %shard_map.76.own.first, ...), custom_call_target="tpu_custom_call" | custom-call | flops 452984832 | bytes 262144 | tf_op jit(solution)/shard_map/pallas_call | solution.py:496
  29.0 2.0 %collective-permute-start.10 = (bf16[272,128]{1,0:T(8,128)(2,1)S(1)}, bf16[272,128]{1,0:T(8,128)(2,1)S(1)}, u32[]{:S(2)}, u32[]{:S(2)}) collective-permute-start(bf16[272,128]{1,0:T(8,128)(2,1)S(1)} %get-tuple-element.47), channel_id=1, source_target_pairs={{0,12},{2,14},{4,8},{6,10},{8,4},{10,6},{12,0},{14,2},{1,13},{3,15... | collective-permute-start | bytes 208904 | tf_op jit(solution)/shard_map/ppermute | solution.py:427
  30.9 0.6 %collective-permute-start.11 = (bf16[272,128]{1,0:T(8,128)(2,1)S(1)}, bf16[272,128]{1,0:T(8,128)(2,1)S(1)}, u32[]{:S(2)}, u32[]{:S(2)}) collective-permute-start(bf16[272,128]{1,0:T(8,128)(2,1)S(1)} %get-tuple-element.48), channel_id=1, source_target_pairs={{0,8},{2,10},{4,12},{6,14},{8,0},{10,2},{12,4},{14,6},{1,9},{3,11}... | collective-permute-start | bytes 208904 | tf_op jit(solution)/shard_map/ppermute | solution.py:427
  31.5 1.9 %collective-permute-start.12 = (bf16[272,128]{1,0:T(8,128)(2,1)S(1)}, bf16[272,128]{1,0:T(8,128)(2,1)S(1)}, u32[]{:S(2)}, u32[]{:S(2)}) collective-permute-start(bf16[272,128]{1,0:T(8,128)(2,1)S(1)} %get-tuple-element.49), channel_id=1, source_target_pairs={{0,4},{2,6},{4,0},{6,2},{8,12},{10,14},{12,8},{14,10},{1,5},{3,7},... | collective-permute-start | bytes 208904 | tf_op jit(solution)/shard_map/ppermute | solution.py:427
  33.4 2.4 %collective-permute-done.10.rest_2_ = bf16[272,128]{1,0:T(8,128)(2,1)S(1)} collective-permute-done((bf16[272,128]{1,0:T(8,128)(2,1)S(1)}, bf16[272,128]{1,0:T(8,128)(2,1)S(1)}, u32[]{:S(2)}, u32[]{:S(2)}) %collective-permute-start.10) | collective-permute-done | bytes 69664 | tf_op jit(solution)/shard_map/ppermute | solution.py:427
  35.8 2.5 %collective-permute-done.11.rest_3_ = bf16[272,128]{1,0:T(8,128)(2,1)S(1)} collective-permute-done((bf16[272,128]{1,0:T(8,128)(2,1)S(1)}, bf16[272,128]{1,0:T(8,128)(2,1)S(1)}, u32[]{:S(2)}, u32[]{:S(2)}) %collective-permute-start.11) | collective-permute-done | bytes 69664 | tf_op jit(solution)/shard_map/ppermute | solution.py:427
  38.3 0.5 shard_map.78
  38.8 1.3 %collective-permute-start.13 = (bf16[272,128]{1,0:T(8,128)(2,1)S(1)}, bf16[272,128]{1,0:T(8,128)(2,1)S(1)}, u32[]{:S(2)}, u32[]{:S(2)}) collective-permute-start(bf16[272,128]{1,0:T(8,128)(2,1)S(1)} %get-tuple-element.52), channel_id=1, source_target_pairs={{0,2},{2,0},{4,6},{6,4},{8,10},{10,8},{12,14},{14,12},{1,3},{3,1},... | collective-permute-start | bytes 208904 | tf_op jit(solution)/shard_map/ppermute | solution.py:436
  40.1 0.8 %collective-permute-start.14 = (bf16[256,128]{1,0:T(8,128)(2,1)S(1)}, bf16[256,128]{1,0:T(8,128)(2,1)S(1)}, u32[]{:S(2)}, u32[]{:S(2)}) collective-permute-start(bf16[256,128]{1,0:T(8,128)(2,1)S(1)} %get-tuple-element.55), channel_id=1, source_target_pairs={{0,2},{2,0},{4,6},{6,4},{8,10},{10,8},{12,14},{14,12},{1,3},{3,1},... | collective-permute-start | bytes 196616 | tf_op jit(solution)/shard_map/ppermute | solution.py:436
  40.9 2.9 %collective-permute-done.13.arrived = bf16[272,128]{1,0:T(8,128)(2,1)S(1)} collective-permute-done((bf16[272,128]{1,0:T(8,128)(2,1)S(1)}, bf16[272,128]{1,0:T(8,128)(2,1)S(1)}, u32[]{:S(2)}, u32[]{:S(2)}) %collective-permute-start.13) | collective-permute-done | bytes 69664 | tf_op jit(solution)/shard_map/ppermute | solution.py:436
  44.2 1.9 %collective-permute-start.15 = (bf16[32,512]{1,0:T(8,128)(2,1)S(1)}, bf16[32,512]{1,0:T(8,128)(2,1)S(1)}, u32[]{:S(2)}, u32[]{:S(2)}) collective-permute-start(bf16[32,512]{1,0:T(8,128)(2,1)S(1)} %get-tuple-element.57), channel_id=1, source_target_pairs={{0,12},{2,14},{4,8},{6,10},{8,4},{10,6},{12,0},{14,2},{1,13},{3,15... | collective-permute-start | bytes 98312 | tf_op jit(solution)/shard_map/ppermute | solution.py:427
  46.2 2.6 %collective-permute-start.17 = (bf16[32,512]{1,0:T(8,128)(2,1)S(1)}, bf16[32,512]{1,0:T(8,128)(2,1)S(1)}, u32[]{:S(2)}, u32[]{:S(2)}) collective-permute-start(bf16[32,512]{1,0:T(8,128)(2,1)S(1)} %get-tuple-element.59), channel_id=1, source_target_pairs={{0,4},{2,6},{4,0},{6,2},{8,12},{10,14},{12,8},{14,10},{1,5},{3,7},... | collective-permute-start | bytes 98312 | tf_op jit(solution)/shard_map/ppermute | solution.py:427
  49.2 0.8 %collective-permute-done.15.rest_1_ = bf16[32,512]{1,0:T(8,128)(2,1)S(1)} collective-permute-done((bf16[32,512]{1,0:T(8,128)(2,1)S(1)}, bf16[32,512]{1,0:T(8,128)(2,1)S(1)}, u32[]{:S(2)}, u32[]{:S(2)}) %collective-permute-start.15) | collective-permute-done | bytes 32800 | tf_op jit(solution)/shard_map/ppermute | solution.py:427
  49.9 1.1 %collective-permute-done.16.rest_2_ = bf16[32,512]{1,0:T(8,128)(2,1)S(1)} collective-permute-done((bf16[32,512]{1,0:T(8,128)(2,1)S(1)}, bf16[32,512]{1,0:T(8,128)(2,1)S(1)}, u32[]{:S(2)}, u32[]{:S(2)}) %collective-permute-start.16) | collective-permute-done | bytes 32800 | tf_op jit(solution)/shard_map/ppermute | solution.py:427
  51.0 0.8 %shard_map.82 = (bf16[128,512]{1,0:T(8,128)(2,1)}, bf16[128,512]{1,0:T(8,128)(2,1)}) custom-call(s32[8,128]{1,0:T(8,128)S(1)} %shard_map.68.plan, f32[8,128]{1,0:T(8,128)S(1)} %get-tuple-element.53.factors, bf16[128,512]{1,0:T(8,128)(2,1)S(1)} %shard_map.72.stay, f32[128,512]{1,0:T(8,128)S(1)} %shard_map.80.stay_2, ...), custom_call_target="tpu_custom_call" | custom-call | bytes 262144 | tf_op jit(solution)/shard_map/pallas_call | solution.py:512
  (29 shorter events, 1.7 us)
Async XLA Ops:
  0.6 1.9 %copy-start = (bf16[1,3,1024,512]{3,2,1,0:T(8,128)(2,1)S(1)}, bf16[1,3,1024,512]{3,2,1,0:T(8,128)(2,1)}, u32[]{:S(2)}) copy-start(bf16[1,3,1024,512]{3,2,1,0:T(8,128)(2,1)} %left.7) | copy-start | bytes 9437188
  0.6 1.9 %copy-start.1 = (bf16[3,128,128]{2,1,0:T(8,128)(2,1)S(1)}, bf16[3,128,128]{2,1,0:T(8,128)(2,1)}, u32[]{:S(2)}) copy-start(bf16[3,128,128]{2,1,0:T(8,128)(2,1)} %right.7) | copy-start | bytes 294916
  0.7 1.9 %copy-start.2 = (bf16[1,128,512]{2,1,0:T(8,128)(2,1)S(1)}, bf16[1,128,512]{2,1,0:T(8,128)(2,1)}, u32[]{:S(2)}) copy-start(bf16[1,128,512]{2,1,0:T(8,128)(2,1)} %param.5) | copy-start | bytes 393220
  0.7 1.9 %copy-start.3 = (s32[8]{0:T(128)S(1)}, s32[8]{0:T(128)}, u32[]{:S(2)}) copy-start(s32[8]{0:T(128)} %widths.1) | copy-start | bytes 100
  0.7 1.9 %copy-start.4 = (s32[8]{0:T(128)S(1)}, s32[8]{0:T(128)}, u32[]{:S(2)}) copy-start(s32[8]{0:T(128)} %holders.1) | copy-start | bytes 100
  0.7 1.7 %collective-permute-start = (bf16[128,512]{1,0:T(8,128)(2,1)}, bf16[128,512]{1,0:T(8,128)(2,1)S(1)}, u32[]{:S(2)}, u32[]{:S(2)}) collective-permute-start(bf16[128,512]{1,0:T(8,128)(2,1)} %bitcast.5), channel_id=1, source_target_pairs={{0,1},{1,0},{2,3},{3,2},{4,5},{5,4},{6,7},{7,6},{8,9},{9,8},{10,11... | collective-permute-start | bytes 393224 | tf_op jit(solution)/shard_map/ppermute | solution.py:432
  3.3 7.6 %collective-permute-start.1 = (bf16[2,32,512]{2,1,0:T(8,128)(2,1)S(1)}, bf16[2,32,512]{2,1,0:T(8,128)(2,1)S(1)}, u32[]{:S(2)}, u32[]{:S(2)}) collective-permute-start(bf16[2,32,512]{2,1,0:T(8,128)(2,1)S(1)} %get-tuple-element.33), channel_id=1, source_target_pairs={{0,12},{2,14},{4,8},{6,10},{8,4},{10,6},{12,0},{14,2},{1,13},{3,15... | collective-permute-start | bytes 196616 | tf_op jit(solution)/shard_map/ppermute | solution.py:427
  8.4 5.7 %collective-permute-start.2 = (bf16[2,32,512]{2,1,0:T(8,128)(2,1)S(1)}, bf16[2,32,512]{2,1,0:T(8,128)(2,1)S(1)}, u32[]{:S(2)}, u32[]{:S(2)}) collective-permute-start(bf16[2,32,512]{2,1,0:T(8,128)(2,1)S(1)} %get-tuple-element.34), channel_id=1, source_target_pairs={{0,8},{2,10},{4,12},{6,14},{8,0},{10,2},{12,4},{14,6},{1,9},{3,11}... | collective-permute-start | bytes 196616 | tf_op jit(solution)/shard_map/ppermute | solution.py:427
  8.4 5.7 %collective-permute-start.3 = (bf16[2,32,512]{2,1,0:T(8,128)(2,1)S(1)}, bf16[2,32,512]{2,1,0:T(8,128)(2,1)S(1)}, u32[]{:S(2)}, u32[]{:S(2)}) collective-permute-start(bf16[2,32,512]{2,1,0:T(8,128)(2,1)S(1)} %get-tuple-element.35), channel_id=1, source_target_pairs={{0,4},{2,6},{4,0},{6,2},{8,12},{10,14},{12,8},{14,10},{1,5},{3,7},... | collective-permute-start | bytes 196616 | tf_op jit(solution)/shard_map/ppermute | solution.py:427
  14.4 4.7 %collective-permute-start.5 = (bf16[2,32,512]{2,1,0:T(8,128)(2,1)S(1)}, bf16[2,32,512]{2,1,0:T(8,128)(2,1)S(1)}, u32[]{:S(2)}, u32[]{:S(2)}) collective-permute-start(bf16[2,32,512]{2,1,0:T(8,128)(2,1)S(1)} %get-tuple-element.42), channel_id=1, source_target_pairs={{0,2},{2,0},{4,6},{6,4},{8,10},{10,8},{12,14},{14,12},{1,3},{3,1},... | collective-permute-start | bytes 196616 | tf_op jit(solution)/shard_map/ppermute | solution.py:436
  16.2 5.6 %collective-permute-start.4 = (bf16[2,32,512]{2,1,0:T(8,128)(2,1)S(1)}, bf16[2,32,512]{2,1,0:T(8,128)(2,1)S(1)}, u32[]{:S(2)}, u32[]{:S(2)}) collective-permute-start(bf16[2,32,512]{2,1,0:T(8,128)(2,1)S(1)} %get-tuple-element.39), channel_id=1, source_target_pairs={{0,2},{2,0},{4,6},{6,4},{8,10},{10,8},{12,14},{14,12},{1,3},{3,1},... | collective-permute-start | bytes 196616 | tf_op jit(solution)/shard_map/ppermute | solution.py:436
  19.2 5.8 %collective-permute-start.6 = (bf16[32,512]{1,0:T(8,128)(2,1)S(1)}, bf16[32,512]{1,0:T(8,128)(2,1)S(1)}, u32[]{:S(2)}, u32[]{:S(2)}) collective-permute-start(bf16[32,512]{1,0:T(8,128)(2,1)S(1)} %get-tuple-element.43), channel_id=1, source_target_pairs={{0,12},{2,14},{4,8},{6,10},{8,4},{10,6},{12,0},{14,2},{1,13},{3,15... | collective-permute-start | bytes 98312 | tf_op jit(solution)/shard_map/ppermute | solution.py:427
  21.8 4.8 %collective-permute-start.7 = (bf16[32,512]{1,0:T(8,128)(2,1)S(1)}, bf16[32,512]{1,0:T(8,128)(2,1)S(1)}, u32[]{:S(2)}, u32[]{:S(2)}) collective-permute-start(bf16[32,512]{1,0:T(8,128)(2,1)S(1)} %get-tuple-element.44), channel_id=1, source_target_pairs={{0,8},{2,10},{4,12},{6,14},{8,0},{10,2},{12,4},{14,6},{1,9},{3,11}... | collective-permute-start | bytes 98312 | tf_op jit(solution)/shard_map/ppermute | solution.py:427
  21.8 4.8 %collective-permute-start.8 = (bf16[32,512]{1,0:T(8,128)(2,1)S(1)}, bf16[32,512]{1,0:T(8,128)(2,1)S(1)}, u32[]{:S(2)}, u32[]{:S(2)}) collective-permute-start(bf16[32,512]{1,0:T(8,128)(2,1)S(1)} %get-tuple-element.45), channel_id=1, source_target_pairs={{0,4},{2,6},{4,0},{6,2},{8,12},{10,14},{12,8},{14,10},{1,5},{3,7},... | collective-permute-start | bytes 98312 | tf_op jit(solution)/shard_map/ppermute | solution.py:427
  26.7 1.4 %collective-permute-start.9 = (bf16[128,512]{1,0:T(8,128)(2,1)S(1)}, bf16[128,512]{1,0:T(8,128)(2,1)S(1)}, u32[]{:S(2)}, u32[]{:S(2)}) collective-permute-start(bf16[128,512]{1,0:T(8,128)(2,1)S(1)} %shard_map.76.own.first), channel_id=1, source_target_pairs={{0,1},{1,0},{2,3},{3,2},{4,5},{5,4},{6,7},{7,6},{8,9},{9,8},{10,11... | collective-permute-start | bytes 393224 | tf_op jit(solution)/shard_map/ppermute | solution.py:432
  29.0 6.8 %collective-permute-start.10 = (bf16[272,128]{1,0:T(8,128)(2,1)S(1)}, bf16[272,128]{1,0:T(8,128)(2,1)S(1)}, u32[]{:S(2)}, u32[]{:S(2)}) collective-permute-start(bf16[272,128]{1,0:T(8,128)(2,1)S(1)} %get-tuple-element.47), channel_id=1, source_target_pairs={{0,12},{2,14},{4,8},{6,10},{8,4},{10,6},{12,0},{14,2},{1,13},{3,15... | collective-permute-start | bytes 208904 | tf_op jit(solution)/shard_map/ppermute | solution.py:427
  30.9 7.4 %collective-permute-start.11 = (bf16[272,128]{1,0:T(8,128)(2,1)S(1)}, bf16[272,128]{1,0:T(8,128)(2,1)S(1)}, u32[]{:S(2)}, u32[]{:S(2)}) collective-permute-start(bf16[272,128]{1,0:T(8,128)(2,1)S(1)} %get-tuple-element.48), channel_id=1, source_target_pairs={{0,8},{2,10},{4,12},{6,14},{8,0},{10,2},{12,4},{14,6},{1,9},{3,11}... | collective-permute-start | bytes 208904 | tf_op jit(solution)/shard_map/ppermute | solution.py:427
  31.5 6.8 %collective-permute-start.12 = (bf16[272,128]{1,0:T(8,128)(2,1)S(1)}, bf16[272,128]{1,0:T(8,128)(2,1)S(1)}, u32[]{:S(2)}, u32[]{:S(2)}) collective-permute-start(bf16[272,128]{1,0:T(8,128)(2,1)S(1)} %get-tuple-element.49), channel_id=1, source_target_pairs={{0,4},{2,6},{4,0},{6,2},{8,12},{10,14},{12,8},{14,10},{1,5},{3,7},... | collective-permute-start | bytes 208904 | tf_op jit(solution)/shard_map/ppermute | solution.py:427
  38.8 5.0 %collective-permute-start.13 = (bf16[272,128]{1,0:T(8,128)(2,1)S(1)}, bf16[272,128]{1,0:T(8,128)(2,1)S(1)}, u32[]{:S(2)}, u32[]{:S(2)}) collective-permute-start(bf16[272,128]{1,0:T(8,128)(2,1)S(1)} %get-tuple-element.52), channel_id=1, source_target_pairs={{0,2},{2,0},{4,6},{6,4},{8,10},{10,8},{12,14},{14,12},{1,3},{3,1},... | collective-permute-start | bytes 208904 | tf_op jit(solution)/shard_map/ppermute | solution.py:436
  40.1 6.0 %collective-permute-start.14 = (bf16[256,128]{1,0:T(8,128)(2,1)S(1)}, bf16[256,128]{1,0:T(8,128)(2,1)S(1)}, u32[]{:S(2)}, u32[]{:S(2)}) collective-permute-start(bf16[256,128]{1,0:T(8,128)(2,1)S(1)} %get-tuple-element.55), channel_id=1, source_target_pairs={{0,2},{2,0},{4,6},{6,4},{8,10},{10,8},{12,14},{14,12},{1,3},{3,1},... | collective-permute-start | bytes 196616 | tf_op jit(solution)/shard_map/ppermute | solution.py:436
  44.2 5.8 %collective-permute-start.15 = (bf16[32,512]{1,0:T(8,128)(2,1)S(1)}, bf16[32,512]{1,0:T(8,128)(2,1)S(1)}, u32[]{:S(2)}, u32[]{:S(2)}) collective-permute-start(bf16[32,512]{1,0:T(8,128)(2,1)S(1)} %get-tuple-element.57), channel_id=1, source_target_pairs={{0,12},{2,14},{4,8},{6,10},{8,4},{10,6},{12,0},{14,2},{1,13},{3,15... | collective-permute-start | bytes 98312 | tf_op jit(solution)/shard_map/ppermute | solution.py:427
  46.1 4.9 %collective-permute-start.16 = (bf16[32,512]{1,0:T(8,128)(2,1)S(1)}, bf16[32,512]{1,0:T(8,128)(2,1)S(1)}, u32[]{:S(2)}, u32[]{:S(2)}) collective-permute-start(bf16[32,512]{1,0:T(8,128)(2,1)S(1)} %get-tuple-element.58), channel_id=1, source_target_pairs={{0,8},{2,10},{4,12},{6,14},{8,0},{10,2},{12,4},{14,6},{1,9},{3,11}... | collective-permute-start | bytes 98312 | tf_op jit(solution)/shard_map/ppermute | solution.py:427
  46.2 4.8 %collective-permute-start.17 = (bf16[32,512]{1,0:T(8,128)(2,1)S(1)}, bf16[32,512]{1,0:T(8,128)(2,1)S(1)}, u32[]{:S(2)}, u32[]{:S(2)}) collective-permute-start(bf16[32,512]{1,0:T(8,128)(2,1)S(1)} %get-tuple-element.59), channel_id=1, source_target_pairs={{0,4},{2,6},{4,0},{6,2},{8,12},{10,14},{12,8},{14,10},{1,5},{3,7},... | collective-permute-start | bytes 98312 | tf_op jit(solution)/shard_map/ppermute | solution.py:427

commit v25 on v24

--- a/solution.py
+++ b/solution.py
@@ -392,9 +392,12 @@
         outs[i][...] = (scale * block).astype(jnp.bfloat16)
 
 
-def final_kernel(plan, factors, stay, stay_2, first, *rest):
-    *pieces, second, first_out = rest
-    first_out[...] = first[...]
+def write_kernel(block, out):
+    out[...] = block[...]
+
+
+def final_kernel(plan, factors, stay, stay_2, *rest):
+    *pieces, second = rest
     live = live_columns(plan, stay.shape[1])
     scale, shift = factors[0:1, 0:1], factors[1:2, 0:1]
     for step, piece in zip(STEPS, pieces):
@@ -497,6 +500,8 @@
         second_kernel, [VMEM] * 5, (tagged,) * places + (both,), split, dots
     )(start_full, first, other_core(first), right_env, left_env)
     new = along_line(pieces, slots)
+    written = call(write_kernel, [VMEM], block)(first)
+    new, first = lax.optimization_barrier((new, written))
     stay_2 = call(stay_kernel, [VMEM] * 3, wide, flops=dots // 3)(deflated, right_env, left_env)
     keep, *cross, tag = call(
         mix_kernel, [VMEM] * (2 + places), (wides, early, late, label), new_table
@@ -509,8 +514,8 @@
         factors, keep, new_late, keep_late, old_late
     )
     joined = (near[0], *far, near[1])
-    second, first = call(final_kernel, [VMEM] * (5 + places), (block, block))(
-        plan, factors, stay, stay_2, first, *along_line(joined, slots)
+    second = call(final_kernel, [VMEM] * (4 + places), block)(
+        plan, factors, stay, stay_2, *along_line(joined, slots)
     )
     return first[None], second[None]
 

time: 51.9 us -> 51.9 us (level)
  waiting for transfers between devices: 21.4 us -> 20.7 us
  Pallas kernels: 5.41 us -> 6.07 us
    ppermute x12, waiting for transfers between devices: 13.6 us -> 12.9 us  [along_line(): sent.append(lax.ppermute(piece, 'sec', pairs) if step else piece)]
    pallas_call x1 -> x2, Pallas kernels: 0.77 us -> 1.42 us  [the longest x1 0.76 us: on_device(): call(final_kernel, [VMEM] * (4 + places), block)]
  transfers between devices with their start and end apart: 18 -> 18, of which waited for: 12 -> 12; matrix products, arithmetic and copies ran while one was open for 0% -> 0% of each run, Pallas kernels for 4% -> 5%
where the time goes in v25:
time: 51.9 us; the launch traced here: 51.8 us
  starting transfers between devices  24.1 us (46%)
  waiting for transfers between devices  20.7 us (40%)
  Pallas kernels  6.07 us (12%)
  between operations  0.78 us (2%)
    ppermute x12, starting transfers between devices, along_line(): sent.append(lax.ppermute(piece, 'sec', pairs) if step else piece)  19.2 us
    ppermute x12, waiting for transfers between devices, along_line(): sent.append(lax.ppermute(piece, 'sec', pairs) if step else piece)  12.9 us
    ppermute x4, waiting for transfers between devices, across(): lax.ppermute(piece, 'sec', [(slot, slot ^ 1) for slot in range(slots)])  5.24 us
    ppermute x4, starting transfers between devices, across(): lax.ppermute(piece, 'sec', [(slot, slot ^ 1) for slot in range(slots)])  4.25 us
    ppermute x2, waiting for transfers between devices, other_core(): return lax.ppermute(block, 'env', [(0, 1), (1, 0)])  2.53 us
  transfers between devices with their start and end apart: 18, of which 12 were waited for; matrix products, arithmetic and copies ran while one was open for 0% of the time, Pallas kernels for 5%

profile of v25, /device:TPU:0, one launch (start us, length us, event | category | flops | bytes accessed | tf_op | source)
XLA Modules:
  0.0 51.8 jit_solution(13331870153983293081)
XLA Ops:
  0.7 0.5 %collective-permute-start = (bf16[128,512]{1,0:T(8,128)(2,1)}, bf16[128,512]{1,0:T(8,128)(2,1)S(1)}, u32[]{:S(2)}, u32[]{:S(2)}) collective-permute-start(bf16[128,512]{1,0:T(8,128)(2,1)} %bitcast.5), channel_id=1, source_target_pairs={{0,1},{1,0},{2,3},{3,2},{4,5},{5,4},{6,7},{7,6},{8,9},{9,8},{10,11... | collective-permute-start | bytes 393224 | tf_op jit(solution)/shard_map/ppermute | solution.py:435
  1.2 1.2 %collective-permute-done.other = bf16[128,512]{1,0:T(8,128)(2,1)S(1)} collective-permute-done((bf16[128,512]{1,0:T(8,128)(2,1)}, bf16[128,512]{1,0:T(8,128)(2,1)S(1)}, u32[]{:S(2)}, u32[]{:S(2)}) %collective-permute-start) | collective-permute-done | bytes 131104 | tf_op jit(solution)/shard_map/ppermute | solution.py:435
  2.5 0.8 %shard_map.69 = (bf16[2,32,512]{2,1,0:T(8,128)(2,1)S(1)}, bf16[2,32,512]{2,1,0:T(8,128)(2,1)S(1)}, bf16[2,32,512]{2,1,0:T(8,128)(2,1)S(1)}, bf16[2,32,512]{2,1,0:T(8,128)(2,1)S(1)}, bf16[2,128,512]{2,1,0:T(8,128)(2,1)S(1)}) custom-call(s32[8,512]{1,0:T(8,128)S(1)} %shard_map.68.columns, s32[1,8]{1,0:T(1,128)S(1)} %bitcast.7, s32[1,8]{1,0:T(1,128)S(1)} %bitcast.8, ...), custom_call_target="tpu_custom_call" | custom-call | flops 452984832 | bytes 262144 | tf_op jit(solution)/shard_map/pallas_call | solution.py:473
  3.3 5.1 %collective-permute-start.1 = (bf16[2,32,512]{2,1,0:T(8,128)(2,1)S(1)}, bf16[2,32,512]{2,1,0:T(8,128)(2,1)S(1)}, u32[]{:S(2)}, u32[]{:S(2)}) collective-permute-start(bf16[2,32,512]{2,1,0:T(8,128)(2,1)S(1)} %get-tuple-element.37), channel_id=1, source_target_pairs={{0,12},{2,14},{4,8},{6,10},{8,4},{10,6},{12,0},{14,2},{1,13},{3,15... | collective-permute-start | bytes 196616 | tf_op jit(solution)/shard_map/ppermute | solution.py:430
  8.4 0.6 %collective-permute-start.3 = (bf16[2,32,512]{2,1,0:T(8,128)(2,1)S(1)}, bf16[2,32,512]{2,1,0:T(8,128)(2,1)S(1)}, u32[]{:S(2)}, u32[]{:S(2)}) collective-permute-start(bf16[2,32,512]{2,1,0:T(8,128)(2,1)S(1)} %get-tuple-element.39), channel_id=1, source_target_pairs={{0,4},{2,6},{4,0},{6,2},{8,12},{10,14},{12,8},{14,10},{1,5},{3,7},... | collective-permute-start | bytes 196616 | tf_op jit(solution)/shard_map/ppermute | solution.py:430
  9.1 0.6 %shard_map.70.plan = s32[8,128]{1,0:T(8,128)S(1)} custom-call(s32[8]{0:T(128)S(1)} %copy-done.3, s32[8]{0:T(128)S(1)} %copy-done.4), custom_call_target="tpu_custom_call" | custom-call | bytes 262144 | tf_op jit(solution)/shard_map/pallas_call | solution.py:469
  9.7 1.2 %collective-permute-done.1.rest_1_ = bf16[2,32,512]{2,1,0:T(8,128)(2,1)S(1)} collective-permute-done((bf16[2,32,512]{2,1,0:T(8,128)(2,1)S(1)}, bf16[2,32,512]{2,1,0:T(8,128)(2,1)S(1)}, u32[]{:S(2)}, u32[]{:S(2)}) %collective-permute-start.1) | collective-permute-done | bytes 65568 | tf_op jit(solution)/shard_map/ppermute | solution.py:430
  10.9 3.2 %collective-permute-done.2.rest_2_ = bf16[2,32,512]{2,1,0:T(8,128)(2,1)S(1)} collective-permute-done((bf16[2,32,512]{2,1,0:T(8,128)(2,1)S(1)}, bf16[2,32,512]{2,1,0:T(8,128)(2,1)S(1)}, u32[]{:S(2)}, u32[]{:S(2)}) %collective-permute-start.2) | collective-permute-done | bytes 65568 | tf_op jit(solution)/shard_map/ppermute | solution.py:430
  14.4 1.6 %collective-permute-start.5 = (bf16[2,32,512]{2,1,0:T(8,128)(2,1)S(1)}, bf16[2,32,512]{2,1,0:T(8,128)(2,1)S(1)}, u32[]{:S(2)}, u32[]{:S(2)}) collective-permute-start(bf16[2,32,512]{2,1,0:T(8,128)(2,1)S(1)} %get-tuple-element.45), channel_id=1, source_target_pairs={{0,2},{2,0},{4,6},{6,4},{8,10},{10,8},{12,14},{14,12},{1,3},{3,1},... | collective-permute-start | bytes 196616 | tf_op jit(solution)/shard_map/ppermute | solution.py:439
  16.2 0.6 %collective-permute-start.4 = (bf16[2,32,512]{2,1,0:T(8,128)(2,1)S(1)}, bf16[2,32,512]{2,1,0:T(8,128)(2,1)S(1)}, u32[]{:S(2)}, u32[]{:S(2)}) collective-permute-start(bf16[2,32,512]{2,1,0:T(8,128)(2,1)S(1)} %get-tuple-element.42), channel_id=1, source_target_pairs={{0,2},{2,0},{4,6},{6,4},{8,10},{10,8},{12,14},{14,12},{1,3},{3,1},... | collective-permute-start | bytes 196616 | tf_op jit(solution)/shard_map/ppermute | solution.py:439
  16.8 2.3 %collective-permute-done.5.arrived.old_arrived = bf16[2,32,512]{2,1,0:T(8,128)(2,1)S(1)} collective-permute-done((bf16[2,32,512]{2,1,0:T(8,128)(2,1)S(1)}, bf16[2,32,512]{2,1,0:T(8,128)(2,1)S(1)}, u32[]{:S(2)}, u32[]{:S(2)}) %collective-permute-start.5) | collective-permute-done | bytes 65568 | tf_op jit(solution)/shard_map/ppermute | solution.py:439
  19.2 2.6 %collective-permute-start.6 = (bf16[32,512]{1,0:T(8,128)(2,1)S(1)}, bf16[32,512]{1,0:T(8,128)(2,1)S(1)}, u32[]{:S(2)}, u32[]{:S(2)}) collective-permute-start(bf16[32,512]{1,0:T(8,128)(2,1)S(1)} %get-tuple-element.46), channel_id=1, source_target_pairs={{0,12},{2,14},{4,8},{6,10},{8,4},{10,6},{12,0},{14,2},{1,13},{3,15... | collective-permute-start | bytes 98312 | tf_op jit(solution)/shard_map/ppermute | solution.py:430
  21.8 1.9 %collective-permute-start.8 = (bf16[32,512]{1,0:T(8,128)(2,1)S(1)}, bf16[32,512]{1,0:T(8,128)(2,1)S(1)}, u32[]{:S(2)}, u32[]{:S(2)}) collective-permute-start(bf16[32,512]{1,0:T(8,128)(2,1)S(1)} %get-tuple-element.48), channel_id=1, source_target_pairs={{0,4},{2,6},{4,0},{6,2},{8,12},{10,14},{12,8},{14,10},{1,5},{3,7},... | collective-permute-start | bytes 98312 | tf_op jit(solution)/shard_map/ppermute | solution.py:430
  24.1 0.8 %collective-permute-done.6.rest_1_ = bf16[32,512]{1,0:T(8,128)(2,1)S(1)} collective-permute-done((bf16[32,512]{1,0:T(8,128)(2,1)S(1)}, bf16[32,512]{1,0:T(8,128)(2,1)S(1)}, u32[]{:S(2)}, u32[]{:S(2)}) %collective-permute-start.6) | collective-permute-done | bytes 32800 | tf_op jit(solution)/shard_map/ppermute | solution.py:430
  24.9 1.6 %collective-permute-done.7.rest_2_ = bf16[32,512]{1,0:T(8,128)(2,1)S(1)} collective-permute-done((bf16[32,512]{1,0:T(8,128)(2,1)S(1)}, bf16[32,512]{1,0:T(8,128)(2,1)S(1)}, u32[]{:S(2)}, u32[]{:S(2)}) %collective-permute-start.7) | collective-permute-done | bytes 32800 | tf_op jit(solution)/shard_map/ppermute | solution.py:430
  26.8 1.3 %collective-permute-done.9.other = bf16[128,512]{1,0:T(8,128)(2,1)S(1)} collective-permute-done((bf16[128,512]{1,0:T(8,128)(2,1)S(1)}, bf16[128,512]{1,0:T(8,128)(2,1)S(1)}, u32[]{:S(2)}, u32[]{:S(2)}) %collective-permute-start.9) | collective-permute-done | bytes 131104 | tf_op jit(solution)/shard_map/ppermute | solution.py:435
  28.1 0.9 %shard_map.77 = (bf16[272,128]{1,0:T(8,128)(2,1)S(1)}, bf16[272,128]{1,0:T(8,128)(2,1)S(1)}, bf16[272,128]{1,0:T(8,128)(2,1)S(1)}, bf16[272,128]{1,0:T(8,128)(2,1)S(1)}, bf16[2,128,512]{2,1,0:T(8,128)(2,1)S(1)}) custom-call(bf16[2,128,512]{2,1,0:T(8,128)(2,1)S(1)} %get-tuple-element.35.vector.start, bf16[128,512]{1,0:T(8,128)(2,1)S(1)} %shard_map.76.own.block, ...), custom_call_target="tpu_custom_call" | custom-call | flops 452984832 | bytes 262144 | tf_op jit(solution)/shard_map/pallas_call | solution.py:499
  29.0 1.9 %collective-permute-start.10 = (bf16[272,128]{1,0:T(8,128)(2,1)S(1)}, bf16[272,128]{1,0:T(8,128)(2,1)S(1)}, u32[]{:S(2)}, u32[]{:S(2)}) collective-permute-start(bf16[272,128]{1,0:T(8,128)(2,1)S(1)} %get-tuple-element.50), channel_id=1, source_target_pairs={{0,12},{2,14},{4,8},{6,10},{8,4},{10,6},{12,0},{14,2},{1,13},{3,15... | collective-permute-start | bytes 208904 | tf_op jit(solution)/shard_map/ppermute | solution.py:430
  30.9 0.6 %collective-permute-start.11 = (bf16[272,128]{1,0:T(8,128)(2,1)S(1)}, bf16[272,128]{1,0:T(8,128)(2,1)S(1)}, u32[]{:S(2)}, u32[]{:S(2)}) collective-permute-start(bf16[272,128]{1,0:T(8,128)(2,1)S(1)} %get-tuple-element.51), channel_id=1, source_target_pairs={{0,8},{2,10},{4,12},{6,14},{8,0},{10,2},{12,4},{14,6},{1,9},{3,11}... | collective-permute-start | bytes 208904 | tf_op jit(solution)/shard_map/ppermute | solution.py:430
  31.5 1.9 %collective-permute-start.12 = (bf16[272,128]{1,0:T(8,128)(2,1)S(1)}, bf16[272,128]{1,0:T(8,128)(2,1)S(1)}, u32[]{:S(2)}, u32[]{:S(2)}) collective-permute-start(bf16[272,128]{1,0:T(8,128)(2,1)S(1)} %get-tuple-element.52), channel_id=1, source_target_pairs={{0,4},{2,6},{4,0},{6,2},{8,12},{10,14},{12,8},{14,10},{1,5},{3,7},... | collective-permute-start | bytes 208904 | tf_op jit(solution)/shard_map/ppermute | solution.py:430
  33.4 0.7 %shard_map.78 = bf16[128,512]{1,0:T(8,128)(2,1)} custom-call(bf16[128,512]{1,0:T(8,128)(2,1)S(1)} %shard_map.76.own.block), custom_call_target="tpu_custom_call" | custom-call | bytes 262144 | tf_op jit(solution)/shard_map/pallas_call | solution.py:503
  34.1 1.7 %collective-permute-done.10.rest_2_ = bf16[272,128]{1,0:T(8,128)(2,1)S(1)} collective-permute-done((bf16[272,128]{1,0:T(8,128)(2,1)S(1)}, bf16[272,128]{1,0:T(8,128)(2,1)S(1)}, u32[]{:S(2)}, u32[]{:S(2)}) %collective-permute-start.10) | collective-permute-done | bytes 69664 | tf_op jit(solution)/shard_map/ppermute | solution.py:430
  35.8 2.5 %collective-permute-done.11.rest_3_ = bf16[272,128]{1,0:T(8,128)(2,1)S(1)} collective-permute-done((bf16[272,128]{1,0:T(8,128)(2,1)S(1)}, bf16[272,128]{1,0:T(8,128)(2,1)S(1)}, u32[]{:S(2)}, u32[]{:S(2)}) %collective-permute-start.11) | collective-permute-done | bytes 69664 | tf_op jit(solution)/shard_map/ppermute | solution.py:430
  38.3 0.5 shard_map.79
  38.8 1.3 %collective-permute-start.13 = (bf16[272,128]{1,0:T(8,128)(2,1)S(1)}, bf16[272,128]{1,0:T(8,128)(2,1)S(1)}, u32[]{:S(2)}, u32[]{:S(2)}) collective-permute-start(bf16[272,128]{1,0:T(8,128)(2,1)S(1)} %get-tuple-element.60), channel_id=1, source_target_pairs={{0,2},{2,0},{4,6},{6,4},{8,10},{10,8},{12,14},{14,12},{1,3},{3,1},... | collective-permute-start | bytes 208904 | tf_op jit(solution)/shard_map/ppermute | solution.py:439
  40.1 0.8 %collective-permute-start.14 = (bf16[256,128]{1,0:T(8,128)(2,1)S(1)}, bf16[256,128]{1,0:T(8,128)(2,1)S(1)}, u32[]{:S(2)}, u32[]{:S(2)}) collective-permute-start(bf16[256,128]{1,0:T(8,128)(2,1)S(1)} %get-tuple-element.63), channel_id=1, source_target_pairs={{0,2},{2,0},{4,6},{6,4},{8,10},{10,8},{12,14},{14,12},{1,3},{3,1},... | collective-permute-start | bytes 196616 | tf_op jit(solution)/shard_map/ppermute | solution.py:439
  40.9 2.9 %collective-permute-done.13.arrived = bf16[272,128]{1,0:T(8,128)(2,1)S(1)} collective-permute-done((bf16[272,128]{1,0:T(8,128)(2,1)S(1)}, bf16[272,128]{1,0:T(8,128)(2,1)S(1)}, u32[]{:S(2)}, u32[]{:S(2)}) %collective-permute-start.13) | collective-permute-done | bytes 69664 | tf_op jit(solution)/shard_map/ppermute | solution.py:439
  44.2 1.9 %collective-permute-start.15 = (bf16[32,512]{1,0:T(8,128)(2,1)S(1)}, bf16[32,512]{1,0:T(8,128)(2,1)S(1)}, u32[]{:S(2)}, u32[]{:S(2)}) collective-permute-start(bf16[32,512]{1,0:T(8,128)(2,1)S(1)} %get-tuple-element.65), channel_id=1, source_target_pairs={{0,12},{2,14},{4,8},{6,10},{8,4},{10,6},{12,0},{14,2},{1,13},{3,15... | collective-permute-start | bytes 98312 | tf_op jit(solution)/shard_map/ppermute | solution.py:430
  46.2 2.6 %collective-permute-start.17 = (bf16[32,512]{1,0:T(8,128)(2,1)S(1)}, bf16[32,512]{1,0:T(8,128)(2,1)S(1)}, u32[]{:S(2)}, u32[]{:S(2)}) collective-permute-start(bf16[32,512]{1,0:T(8,128)(2,1)S(1)} %get-tuple-element.67), channel_id=1, source_target_pairs={{0,4},{2,6},{4,0},{6,2},{8,12},{10,14},{12,8},{14,10},{1,5},{3,7},... | collective-permute-start | bytes 98312 | tf_op jit(solution)/shard_map/ppermute | solution.py:430
  49.2 0.7 %collective-permute-done.15.rest_1_ = bf16[32,512]{1,0:T(8,128)(2,1)S(1)} collective-permute-done((bf16[32,512]{1,0:T(8,128)(2,1)S(1)}, bf16[32,512]{1,0:T(8,128)(2,1)S(1)}, u32[]{:S(2)}, u32[]{:S(2)}) %collective-permute-start.15) | collective-permute-done | bytes 32800 | tf_op jit(solution)/shard_map/ppermute | solution.py:430
  49.9 1.1 %collective-permute-done.16.rest_2_ = bf16[32,512]{1,0:T(8,128)(2,1)S(1)} collective-permute-done((bf16[32,512]{1,0:T(8,128)(2,1)S(1)}, bf16[32,512]{1,0:T(8,128)(2,1)S(1)}, u32[]{:S(2)}, u32[]{:S(2)}) %collective-permute-start.16) | collective-permute-done | bytes 32800 | tf_op jit(solution)/shard_map/ppermute | solution.py:430
  51.0 0.8 %shard_map.83 = bf16[128,512]{1,0:T(8,128)(2,1)} custom-call(s32[8,128]{1,0:T(8,128)S(1)} %shard_map.70.plan, f32[8,128]{1,0:T(8,128)S(1)} %get-tuple-element.61.factors, bf16[128,512]{1,0:T(8,128)(2,1)S(1)} %shard_map.71.stay, f32[128,512]{1,0:T(8,128)S(1)} %shard_map.81.stay_2, bf16[32,512]{1,0:T(8,128)(2,1)S(1)} %get-tuple-element.64.rest_0_, ...), custom_call_target="tpu_custom_call" | custom-call | bytes 262144 | tf_op jit(solution)/shard_map/pallas_call | solution.py:517
  (30 shorter events, 2.1 us)
Async XLA Ops:
  0.6 1.9 %copy-start = (bf16[1,3,1024,512]{3,2,1,0:T(8,128)(2,1)S(1)}, bf16[1,3,1024,512]{3,2,1,0:T(8,128)(2,1)}, u32[]{:S(2)}) copy-start(bf16[1,3,1024,512]{3,2,1,0:T(8,128)(2,1)} %left.7) | copy-start | bytes 9437188
  0.6 1.9 %copy-start.1 = (bf16[3,128,128]{2,1,0:T(8,128)(2,1)S(1)}, bf16[3,128,128]{2,1,0:T(8,128)(2,1)}, u32[]{:S(2)}) copy-start(bf16[3,128,128]{2,1,0:T(8,128)(2,1)} %right.7) | copy-start | bytes 294916
  0.7 1.9 %copy-start.2 = (bf16[1,128,512]{2,1,0:T(8,128)(2,1)S(1)}, bf16[1,128,512]{2,1,0:T(8,128)(2,1)}, u32[]{:S(2)}) copy-start(bf16[1,128,512]{2,1,0:T(8,128)(2,1)} %param.5) | copy-start | bytes 393220
  0.7 1.9 %copy-start.3 = (s32[8]{0:T(128)S(1)}, s32[8]{0:T(128)}, u32[]{:S(2)}) copy-start(s32[8]{0:T(128)} %widths.1) | copy-start | bytes 100
  0.7 1.9 %copy-start.4 = (s32[8]{0:T(128)S(1)}, s32[8]{0:T(128)}, u32[]{:S(2)}) copy-start(s32[8]{0:T(128)} %holders.1) | copy-start | bytes 100
  0.7 1.7 %collective-permute-start = (bf16[128,512]{1,0:T(8,128)(2,1)}, bf16[128,512]{1,0:T(8,128)(2,1)S(1)}, u32[]{:S(2)}, u32[]{:S(2)}) collective-permute-start(bf16[128,512]{1,0:T(8,128)(2,1)} %bitcast.5), channel_id=1, source_target_pairs={{0,1},{1,0},{2,3},{3,2},{4,5},{5,4},{6,7},{7,6},{8,9},{9,8},{10,11... | collective-permute-start | bytes 393224 | tf_op jit(solution)/shard_map/ppermute | solution.py:435
  3.3 7.6 %collective-permute-start.1 = (bf16[2,32,512]{2,1,0:T(8,128)(2,1)S(1)}, bf16[2,32,512]{2,1,0:T(8,128)(2,1)S(1)}, u32[]{:S(2)}, u32[]{:S(2)}) collective-permute-start(bf16[2,32,512]{2,1,0:T(8,128)(2,1)S(1)} %get-tuple-element.37), channel_id=1, source_target_pairs={{0,12},{2,14},{4,8},{6,10},{8,4},{10,6},{12,0},{14,2},{1,13},{3,15... | collective-permute-start | bytes 196616 | tf_op jit(solution)/shard_map/ppermute | solution.py:430
  8.4 5.7 %collective-permute-start.2 = (bf16[2,32,512]{2,1,0:T(8,128)(2,1)S(1)}, bf16[2,32,512]{2,1,0:T(8,128)(2,1)S(1)}, u32[]{:S(2)}, u32[]{:S(2)}) collective-permute-start(bf16[2,32,512]{2,1,0:T(8,128)(2,1)S(1)} %get-tuple-element.38), channel_id=1, source_target_pairs={{0,8},{2,10},{4,12},{6,14},{8,0},{10,2},{12,4},{14,6},{1,9},{3,11}... | collective-permute-start | bytes 196616 | tf_op jit(solution)/shard_map/ppermute | solution.py:430
  8.4 5.7 %collective-permute-start.3 = (bf16[2,32,512]{2,1,0:T(8,128)(2,1)S(1)}, bf16[2,32,512]{2,1,0:T(8,128)(2,1)S(1)}, u32[]{:S(2)}, u32[]{:S(2)}) collective-permute-start(bf16[2,32,512]{2,1,0:T(8,128)(2,1)S(1)} %get-tuple-element.39), channel_id=1, source_target_pairs={{0,4},{2,6},{4,0},{6,2},{8,12},{10,14},{12,8},{14,10},{1,5},{3,7},... | collective-permute-start | bytes 196616 | tf_op jit(solution)/shard_map/ppermute | solution.py:430
  14.4 4.7 %collective-permute-start.5 = (bf16[2,32,512]{2,1,0:T(8,128)(2,1)S(1)}, bf16[2,32,512]{2,1,0:T(8,128)(2,1)S(1)}, u32[]{:S(2)}, u32[]{:S(2)}) collective-permute-start(bf16[2,32,512]{2,1,0:T(8,128)(2,1)S(1)} %get-tuple-element.45), channel_id=1, source_target_pairs={{0,2},{2,0},{4,6},{6,4},{8,10},{10,8},{12,14},{14,12},{1,3},{3,1},... | collective-permute-start | bytes 196616 | tf_op jit(solution)/shard_map/ppermute | solution.py:439
  16.2 5.6 %collective-permute-start.4 = (bf16[2,32,512]{2,1,0:T(8,128)(2,1)S(1)}, bf16[2,32,512]{2,1,0:T(8,128)(2,1)S(1)}, u32[]{:S(2)}, u32[]{:S(2)}) collective-permute-start(bf16[2,32,512]{2,1,0:T(8,128)(2,1)S(1)} %get-tuple-element.42), channel_id=1, source_target_pairs={{0,2},{2,0},{4,6},{6,4},{8,10},{10,8},{12,14},{14,12},{1,3},{3,1},... | collective-permute-start | bytes 196616 | tf_op jit(solution)/shard_map/ppermute | solution.py:439
  19.2 5.8 %collective-permute-start.6 = (bf16[32,512]{1,0:T(8,128)(2,1)S(1)}, bf16[32,512]{1,0:T(8,128)(2,1)S(1)}, u32[]{:S(2)}, u32[]{:S(2)}) collective-permute-start(bf16[32,512]{1,0:T(8,128)(2,1)S(1)} %get-tuple-element.46), channel_id=1, source_target_pairs={{0,12},{2,14},{4,8},{6,10},{8,4},{10,6},{12,0},{14,2},{1,13},{3,15... | collective-permute-start | bytes 98312 | tf_op jit(solution)/shard_map/ppermute | solution.py:430
  21.8 4.8 %collective-permute-start.7 = (bf16[32,512]{1,0:T(8,128)(2,1)S(1)}, bf16[32,512]{1,0:T(8,128)(2,1)S(1)}, u32[]{:S(2)}, u32[]{:S(2)}) collective-permute-start(bf16[32,512]{1,0:T(8,128)(2,1)S(1)} %get-tuple-element.47), channel_id=1, source_target_pairs={{0,8},{2,10},{4,12},{6,14},{8,0},{10,2},{12,4},{14,6},{1,9},{3,11}... | collective-permute-start | bytes 98312 | tf_op jit(solution)/shard_map/ppermute | solution.py:430
  21.8 4.8 %collective-permute-start.8 = (bf16[32,512]{1,0:T(8,128)(2,1)S(1)}, bf16[32,512]{1,0:T(8,128)(2,1)S(1)}, u32[]{:S(2)}, u32[]{:S(2)}) collective-permute-start(bf16[32,512]{1,0:T(8,128)(2,1)S(1)} %get-tuple-element.48), channel_id=1, source_target_pairs={{0,4},{2,6},{4,0},{6,2},{8,12},{10,14},{12,8},{14,10},{1,5},{3,7},... | collective-permute-start | bytes 98312 | tf_op jit(solution)/shard_map/ppermute | solution.py:430
  26.7 1.4 %collective-permute-start.9 = (bf16[128,512]{1,0:T(8,128)(2,1)S(1)}, bf16[128,512]{1,0:T(8,128)(2,1)S(1)}, u32[]{:S(2)}, u32[]{:S(2)}) collective-permute-start(bf16[128,512]{1,0:T(8,128)(2,1)S(1)} %shard_map.76.own.block), channel_id=1, source_target_pairs={{0,1},{1,0},{2,3},{3,2},{4,5},{5,4},{6,7},{7,6},{8,9},{9,8},{10,11... | collective-permute-start | bytes 393224 | tf_op jit(solution)/shard_map/ppermute | solution.py:435
  29.0 6.8 %collective-permute-start.10 = (bf16[272,128]{1,0:T(8,128)(2,1)S(1)}, bf16[272,128]{1,0:T(8,128)(2,1)S(1)}, u32[]{:S(2)}, u32[]{:S(2)}) collective-permute-start(bf16[272,128]{1,0:T(8,128)(2,1)S(1)} %get-tuple-element.50), channel_id=1, source_target_pairs={{0,12},{2,14},{4,8},{6,10},{8,4},{10,6},{12,0},{14,2},{1,13},{3,15... | collective-permute-start | bytes 208904 | tf_op jit(solution)/shard_map/ppermute | solution.py:430
  30.9 7.4 %collective-permute-start.11 = (bf16[272,128]{1,0:T(8,128)(2,1)S(1)}, bf16[272,128]{1,0:T(8,128)(2,1)S(1)}, u32[]{:S(2)}, u32[]{:S(2)}) collective-permute-start(bf16[272,128]{1,0:T(8,128)(2,1)S(1)} %get-tuple-element.51), channel_id=1, source_target_pairs={{0,8},{2,10},{4,12},{6,14},{8,0},{10,2},{12,4},{14,6},{1,9},{3,11}... | collective-permute-start | bytes 208904 | tf_op jit(solution)/shard_map/ppermute | solution.py:430
  31.5 6.8 %collective-permute-start.12 = (bf16[272,128]{1,0:T(8,128)(2,1)S(1)}, bf16[272,128]{1,0:T(8,128)(2,1)S(1)}, u32[]{:S(2)}, u32[]{:S(2)}) collective-permute-start(bf16[272,128]{1,0:T(8,128)(2,1)S(1)} %get-tuple-element.52), channel_id=1, source_target_pairs={{0,4},{2,6},{4,0},{6,2},{8,12},{10,14},{12,8},{14,10},{1,5},{3,7},... | collective-permute-start | bytes 208904 | tf_op jit(solution)/shard_map/ppermute | solution.py:430
  38.8 5.0 %collective-permute-start.13 = (bf16[272,128]{1,0:T(8,128)(2,1)S(1)}, bf16[272,128]{1,0:T(8,128)(2,1)S(1)}, u32[]{:S(2)}, u32[]{:S(2)}) collective-permute-start(bf16[272,128]{1,0:T(8,128)(2,1)S(1)} %get-tuple-element.60), channel_id=1, source_target_pairs={{0,2},{2,0},{4,6},{6,4},{8,10},{10,8},{12,14},{14,12},{1,3},{3,1},... | collective-permute-start | bytes 208904 | tf_op jit(solution)/shard_map/ppermute | solution.py:439
  40.1 6.0 %collective-permute-start.14 = (bf16[256,128]{1,0:T(8,128)(2,1)S(1)}, bf16[256,128]{1,0:T(8,128)(2,1)S(1)}, u32[]{:S(2)}, u32[]{:S(2)}) collective-permute-start(bf16[256,128]{1,0:T(8,128)(2,1)S(1)} %get-tuple-element.63), channel_id=1, source_target_pairs={{0,2},{2,0},{4,6},{6,4},{8,10},{10,8},{12,14},{14,12},{1,3},{3,1},... | collective-permute-start | bytes 196616 | tf_op jit(solution)/shard_map/ppermute | solution.py:439
  44.2 5.8 %collective-permute-start.15 = (bf16[32,512]{1,0:T(8,128)(2,1)S(1)}, bf16[32,512]{1,0:T(8,128)(2,1)S(1)}, u32[]{:S(2)}, u32[]{:S(2)}) collective-permute-start(bf16[32,512]{1,0:T(8,128)(2,1)S(1)} %get-tuple-element.65), channel_id=1, source_target_pairs={{0,12},{2,14},{4,8},{6,10},{8,4},{10,6},{12,0},{14,2},{1,13},{3,15... | collective-permute-start | bytes 98312 | tf_op jit(solution)/shard_map/ppermute | solution.py:430
  46.1 4.9 %collective-permute-start.16 = (bf16[32,512]{1,0:T(8,128)(2,1)S(1)}, bf16[32,512]{1,0:T(8,128)(2,1)S(1)}, u32[]{:S(2)}, u32[]{:S(2)}) collective-permute-start(bf16[32,512]{1,0:T(8,128)(2,1)S(1)} %get-tuple-element.66), channel_id=1, source_target_pairs={{0,8},{2,10},{4,12},{6,14},{8,0},{10,2},{12,4},{14,6},{1,9},{3,11}... | collective-permute-start | bytes 98312 | tf_op jit(solution)/shard_map/ppermute | solution.py:430
  46.2 4.8 %collective-permute-start.17 = (bf16[32,512]{1,0:T(8,128)(2,1)S(1)}, bf16[32,512]{1,0:T(8,128)(2,1)S(1)}, u32[]{:S(2)}, u32[]{:S(2)}) collective-permute-start(bf16[32,512]{1,0:T(8,128)(2,1)S(1)} %get-tuple-element.67), channel_id=1, source_target_pairs={{0,4},{2,6},{4,0},{6,2},{8,12},{10,14},{12,8},{14,10},{1,5},{3,7},... | collective-permute-start | bytes 98312 | tf_op jit(solution)/shard_map/ppermute | solution.py:430

commit v26 on v24

--- a/solution.py
+++ b/solution.py
@@ -112,7 +112,7 @@
 LANES = 128
 TAG = 16
 LINES = 2
-STEPS = (0, 3, 2, 1)
+STEPS = (0, 2, 3, 1)
 EARLY, LATE = (1, 2), (0, 3)
 
 

time: 51.9 us -> 53.2 us (1.025)
  waiting for transfers between devices: 21.4 us -> 24.7 us
  starting transfers between devices: 24.1 us -> 22 us
    ppermute x12, waiting for transfers between devices: 13.6 us -> 17 us  [along_line(): sent.append(lax.ppermute(piece, 'sec', pairs) if step else piece)]
    ppermute x12, starting transfers between devices: 19.2 us -> 17.2 us  [along_line(): sent.append(lax.ppermute(piece, 'sec', pairs) if step else piece)]
where the time goes in v26:
time: 53.2 us; the launch traced here: 53 us
  waiting for transfers between devices  24.7 us (46%)
  starting transfers between devices  22 us (41%)
  Pallas kernels  5.41 us (10%)
  between operations  0.79 us (1%)
    ppermute x12, starting transfers between devices, along_line(): sent.append(lax.ppermute(piece, 'sec', pairs) if step else piece)  17.2 us
    ppermute x12, waiting for transfers between devices, along_line(): sent.append(lax.ppermute(piece, 'sec', pairs) if step else piece)  17 us
    ppermute x4, waiting for transfers between devices, across(): lax.ppermute(piece, 'sec', [(slot, slot ^ 1) for slot in range(slots)])  5.13 us
    ppermute x4, starting transfers between devices, across(): lax.ppermute(piece, 'sec', [(slot, slot ^ 1) for slot in range(slots)])  4.25 us
    ppermute x2, waiting for transfers between devices, other_core(): return lax.ppermute(block, 'env', [(0, 1), (1, 0)])  2.53 us
  transfers between devices with their start and end apart: 18, of which 12 were waited for; matrix products, arithmetic and copies ran while one was open for 0% of the time, Pallas kernels for 4%

profile of v26, /device:TPU:0, one launch (start us, length us, event | category | flops | bytes accessed | tf_op | source)
XLA Modules:
  0.0 53.0 jit_solution(9133266754758647586)
XLA Ops:
  0.7 0.5 collective-permute-start
  1.2 1.2 %collective-permute-done.other = bf16[128,512]{1,0:T(8,128)(2,1)S(1)} collective-permute-done((bf16[128,512]{1,0:T(8,128)(2,1)}, bf16[128,512]{1,0:T(8,128)(2,1)S(1)}, u32[]{:S(2)}, u32[]{:S(2)}) %collective-permute-start) | collective-permute-done | bytes 131104 | tf_op jit(solution)/shard_map/ppermute | solution.py:432
  2.5 0.8 %shard_map.70 = (bf16[2,32,512]{2,1,0:T(8,128)(2,1)S(1)}, bf16[2,32,512]{2,1,0:T(8,128)(2,1)S(1)}, bf16[2,32,512]{2,1,0:T(8,128)(2,1)S(1)}, bf16[2,32,512]{2,1,0:T(8,128)(2,1)S(1)}, bf16[2,128,512]{2,1,0:T(8,128)(2,1)S(1)}) custom-call(s32[8,512]{1,0:T(8,128)S(1)} %shard_map.69.columns, s32[1,8]{1,0:T(1,128)S(1)} %bitcast.7, s32[1,8]{1,0:T(1,128)S(1)} %bitcast.8, ...), custom_call_target="tpu_custom_call" | custom-call | flops 452984832 | bytes 262144 | tf_op jit(solution)/shard_map/pallas_call | solution.py:470
  3.3 4.1 %collective-permute-start.1 = (bf16[2,32,512]{2,1,0:T(8,128)(2,1)S(1)}, bf16[2,32,512]{2,1,0:T(8,128)(2,1)S(1)}, u32[]{:S(2)}, u32[]{:S(2)}) collective-permute-start(bf16[2,32,512]{2,1,0:T(8,128)(2,1)S(1)} %get-tuple-element.33), channel_id=1, source_target_pairs={{0,8},{2,10},{4,12},{6,14},{8,0},{10,2},{12,4},{14,6},{1,9},{3,11}... | collective-permute-start | bytes 196616 | tf_op jit(solution)/shard_map/ppermute | solution.py:427
  7.4 1.3 %collective-permute-start.2 = (bf16[2,32,512]{2,1,0:T(8,128)(2,1)S(1)}, bf16[2,32,512]{2,1,0:T(8,128)(2,1)S(1)}, u32[]{:S(2)}, u32[]{:S(2)}) collective-permute-start(bf16[2,32,512]{2,1,0:T(8,128)(2,1)S(1)} %get-tuple-element.34), channel_id=1, source_target_pairs={{0,12},{2,14},{4,8},{6,10},{8,4},{10,6},{12,0},{14,2},{1,13},{3,15... | collective-permute-start | bytes 196616 | tf_op jit(solution)/shard_map/ppermute | solution.py:427
  9.0 0.6 %shard_map.68.plan = s32[8,128]{1,0:T(8,128)S(1)} custom-call(s32[8]{0:T(128)S(1)} %copy-done.3, s32[8]{0:T(128)S(1)} %copy-done.4), custom_call_target="tpu_custom_call" | custom-call | bytes 262144 | tf_op jit(solution)/shard_map/pallas_call | solution.py:466
  9.6 1.6 %collective-permute-done.1.rest_1_ = bf16[2,32,512]{2,1,0:T(8,128)(2,1)S(1)} collective-permute-done((bf16[2,32,512]{2,1,0:T(8,128)(2,1)S(1)}, bf16[2,32,512]{2,1,0:T(8,128)(2,1)S(1)}, u32[]{:S(2)}, u32[]{:S(2)}) %collective-permute-start.1) | collective-permute-done | bytes 65568 | tf_op jit(solution)/shard_map/ppermute | solution.py:427
  11.2 2.6 %collective-permute-done.2.rest_2_ = bf16[2,32,512]{2,1,0:T(8,128)(2,1)S(1)} collective-permute-done((bf16[2,32,512]{2,1,0:T(8,128)(2,1)S(1)}, bf16[2,32,512]{2,1,0:T(8,128)(2,1)S(1)}, u32[]{:S(2)}, u32[]{:S(2)}) %collective-permute-start.2) | collective-permute-done | bytes 65568 | tf_op jit(solution)/shard_map/ppermute | solution.py:427
  14.0 1.8 %collective-permute-start.5 = (bf16[2,32,512]{2,1,0:T(8,128)(2,1)S(1)}, bf16[2,32,512]{2,1,0:T(8,128)(2,1)S(1)}, u32[]{:S(2)}, u32[]{:S(2)}) collective-permute-start(bf16[2,32,512]{2,1,0:T(8,128)(2,1)S(1)} %get-tuple-element.42), channel_id=1, source_target_pairs={{0,2},{2,0},{4,6},{6,4},{8,10},{10,8},{12,14},{14,12},{1,3},{3,1},... | collective-permute-start | bytes 196616 | tf_op jit(solution)/shard_map/ppermute | solution.py:436
  16.4 2.2 %collective-permute-done.5.arrived.old_arrived = bf16[2,32,512]{2,1,0:T(8,128)(2,1)S(1)} collective-permute-done((bf16[2,32,512]{2,1,0:T(8,128)(2,1)S(1)}, bf16[2,32,512]{2,1,0:T(8,128)(2,1)S(1)}, u32[]{:S(2)}, u32[]{:S(2)}) %collective-permute-start.5) | collective-permute-done | bytes 65568 | tf_op jit(solution)/shard_map/ppermute | solution.py:436
  18.6 3.0 %collective-permute-start.6 = (bf16[32,512]{1,0:T(8,128)(2,1)S(1)}, bf16[32,512]{1,0:T(8,128)(2,1)S(1)}, u32[]{:S(2)}, u32[]{:S(2)}) collective-permute-start(bf16[32,512]{1,0:T(8,128)(2,1)S(1)} %get-tuple-element.43), channel_id=1, source_target_pairs={{0,8},{2,10},{4,12},{6,14},{8,0},{10,2},{12,4},{14,6},{1,9},{3,11}... | collective-permute-start | bytes 98312 | tf_op jit(solution)/shard_map/ppermute | solution.py:427
  21.6 0.7 %collective-permute-start.7 = (bf16[32,512]{1,0:T(8,128)(2,1)S(1)}, bf16[32,512]{1,0:T(8,128)(2,1)S(1)}, u32[]{:S(2)}, u32[]{:S(2)}) collective-permute-start(bf16[32,512]{1,0:T(8,128)(2,1)S(1)} %get-tuple-element.44), channel_id=1, source_target_pairs={{0,12},{2,14},{4,8},{6,10},{8,4},{10,6},{12,0},{14,2},{1,13},{3,15... | collective-permute-start | bytes 98312 | tf_op jit(solution)/shard_map/ppermute | solution.py:427
  22.4 0.6 %collective-permute-start.8 = (bf16[32,512]{1,0:T(8,128)(2,1)S(1)}, bf16[32,512]{1,0:T(8,128)(2,1)S(1)}, u32[]{:S(2)}, u32[]{:S(2)}) collective-permute-start(bf16[32,512]{1,0:T(8,128)(2,1)S(1)} %get-tuple-element.45), channel_id=1, source_target_pairs={{0,4},{2,6},{4,0},{6,2},{8,12},{10,14},{12,8},{14,10},{1,5},{3,7},... | collective-permute-start | bytes 98312 | tf_op jit(solution)/shard_map/ppermute | solution.py:427
  22.9 0.4 shard_map.72.stay
  23.5 3.8 %collective-permute-done.7.rest_2_ = bf16[32,512]{1,0:T(8,128)(2,1)S(1)} collective-permute-done((bf16[32,512]{1,0:T(8,128)(2,1)S(1)}, bf16[32,512]{1,0:T(8,128)(2,1)S(1)}, u32[]{:S(2)}, u32[]{:S(2)}) %collective-permute-start.7) | collective-permute-done | bytes 32800 | tf_op jit(solution)/shard_map/ppermute | solution.py:427
  27.5 1.3 %collective-permute-done.9.other = bf16[128,512]{1,0:T(8,128)(2,1)S(1)} collective-permute-done((bf16[128,512]{1,0:T(8,128)(2,1)S(1)}, bf16[128,512]{1,0:T(8,128)(2,1)S(1)}, u32[]{:S(2)}, u32[]{:S(2)}) %collective-permute-start.9) | collective-permute-done | bytes 131104 | tf_op jit(solution)/shard_map/ppermute | solution.py:432
  28.8 0.9 %shard_map.77 = (bf16[272,128]{1,0:T(8,128)(2,1)S(1)}, bf16[272,128]{1,0:T(8,128)(2,1)S(1)}, bf16[272,128]{1,0:T(8,128)(2,1)S(1)}, bf16[272,128]{1,0:T(8,128)(2,1)S(1)}, bf16[2,128,512]{2,1,0:T(8,128)(2,1)S(1)}) custom-call(bf16[2,128,512]{2,1,0:T(8,128)(2,1)S(1)} %get-tuple-element.37.vector.start, bf16[128,512]{1,0:T(8,128)(2,1)S(1)} %shard_map.76.own.first, ...), custom_call_target="tpu_custom_call" | custom-call | flops 452984832 | bytes 262144 | tf_op jit(solution)/shard_map/pallas_call | solution.py:496
  29.7 1.0 %collective-permute-start.10 = (bf16[272,128]{1,0:T(8,128)(2,1)S(1)}, bf16[272,128]{1,0:T(8,128)(2,1)S(1)}, u32[]{:S(2)}, u32[]{:S(2)}) collective-permute-start(bf16[272,128]{1,0:T(8,128)(2,1)S(1)} %get-tuple-element.47), channel_id=1, source_target_pairs={{0,8},{2,10},{4,12},{6,14},{8,0},{10,2},{12,4},{14,6},{1,9},{3,11}... | collective-permute-start | bytes 208904 | tf_op jit(solution)/shard_map/ppermute | solution.py:427
  30.8 1.2 %collective-permute-start.11 = (bf16[272,128]{1,0:T(8,128)(2,1)S(1)}, bf16[272,128]{1,0:T(8,128)(2,1)S(1)}, u32[]{:S(2)}, u32[]{:S(2)}) collective-permute-start(bf16[272,128]{1,0:T(8,128)(2,1)S(1)} %get-tuple-element.48), channel_id=1, source_target_pairs={{0,12},{2,14},{4,8},{6,10},{8,4},{10,6},{12,0},{14,2},{1,13},{3,15... | collective-permute-start | bytes 208904 | tf_op jit(solution)/shard_map/ppermute | solution.py:427
  32.0 1.3 %collective-permute-start.12 = (bf16[272,128]{1,0:T(8,128)(2,1)S(1)}, bf16[272,128]{1,0:T(8,128)(2,1)S(1)}, u32[]{:S(2)}, u32[]{:S(2)}) collective-permute-start(bf16[272,128]{1,0:T(8,128)(2,1)S(1)} %get-tuple-element.49), channel_id=1, source_target_pairs={{0,4},{2,6},{4,0},{6,2},{8,12},{10,14},{12,8},{14,10},{1,5},{3,7},... | collective-permute-start | bytes 208904 | tf_op jit(solution)/shard_map/ppermute | solution.py:427
  33.3 4.2 %collective-permute-done.10.rest_2_ = bf16[272,128]{1,0:T(8,128)(2,1)S(1)} collective-permute-done((bf16[272,128]{1,0:T(8,128)(2,1)S(1)}, bf16[272,128]{1,0:T(8,128)(2,1)S(1)}, u32[]{:S(2)}, u32[]{:S(2)}) %collective-permute-start.10) | collective-permute-done | bytes 69664 | tf_op jit(solution)/shard_map/ppermute | solution.py:427
  37.5 1.3 %collective-permute-done.12.rest_4_ = bf16[272,128]{1,0:T(8,128)(2,1)S(1)} collective-permute-done((bf16[272,128]{1,0:T(8,128)(2,1)S(1)}, bf16[272,128]{1,0:T(8,128)(2,1)S(1)}, u32[]{:S(2)}, u32[]{:S(2)}) %collective-permute-start.12) | collective-permute-done | bytes 69664 | tf_op jit(solution)/shard_map/ppermute | solution.py:427
  38.8 0.5 shard_map.78
  39.3 1.3 %collective-permute-start.13 = (bf16[272,128]{1,0:T(8,128)(2,1)S(1)}, bf16[272,128]{1,0:T(8,128)(2,1)S(1)}, u32[]{:S(2)}, u32[]{:S(2)}) collective-permute-start(bf16[272,128]{1,0:T(8,128)(2,1)S(1)} %get-tuple-element.52), channel_id=1, source_target_pairs={{0,2},{2,0},{4,6},{6,4},{8,10},{10,8},{12,14},{14,12},{1,3},{3,1},... | collective-permute-start | bytes 208904 | tf_op jit(solution)/shard_map/ppermute | solution.py:436
  40.7 0.8 %collective-permute-start.14 = (bf16[256,128]{1,0:T(8,128)(2,1)S(1)}, bf16[256,128]{1,0:T(8,128)(2,1)S(1)}, u32[]{:S(2)}, u32[]{:S(2)}) collective-permute-start(bf16[256,128]{1,0:T(8,128)(2,1)S(1)} %get-tuple-element.55), channel_id=1, source_target_pairs={{0,2},{2,0},{4,6},{6,4},{8,10},{10,8},{12,14},{14,12},{1,3},{3,1},... | collective-permute-start | bytes 196616 | tf_op jit(solution)/shard_map/ppermute | solution.py:436
  41.4 3.0 %collective-permute-done.13.arrived = bf16[272,128]{1,0:T(8,128)(2,1)S(1)} collective-permute-done((bf16[272,128]{1,0:T(8,128)(2,1)S(1)}, bf16[272,128]{1,0:T(8,128)(2,1)S(1)}, u32[]{:S(2)}, u32[]{:S(2)}) %collective-permute-start.13) | collective-permute-done | bytes 69664 | tf_op jit(solution)/shard_map/ppermute | solution.py:436
  44.7 1.7 %collective-permute-start.15 = (bf16[32,512]{1,0:T(8,128)(2,1)S(1)}, bf16[32,512]{1,0:T(8,128)(2,1)S(1)}, u32[]{:S(2)}, u32[]{:S(2)}) collective-permute-start(bf16[32,512]{1,0:T(8,128)(2,1)S(1)} %get-tuple-element.57), channel_id=1, source_target_pairs={{0,8},{2,10},{4,12},{6,14},{8,0},{10,2},{12,4},{14,6},{1,9},{3,11}... | collective-permute-start | bytes 98312 | tf_op jit(solution)/shard_map/ppermute | solution.py:427
  46.4 1.4 %collective-permute-start.16 = (bf16[32,512]{1,0:T(8,128)(2,1)S(1)}, bf16[32,512]{1,0:T(8,128)(2,1)S(1)}, u32[]{:S(2)}, u32[]{:S(2)}) collective-permute-start(bf16[32,512]{1,0:T(8,128)(2,1)S(1)} %get-tuple-element.58), channel_id=1, source_target_pairs={{0,12},{2,14},{4,8},{6,10},{8,4},{10,6},{12,0},{14,2},{1,13},{3,15... | collective-permute-start | bytes 98312 | tf_op jit(solution)/shard_map/ppermute | solution.py:427
  47.9 0.5 collective-permute-start.17
  48.9 1.1 %collective-permute-done.15.rest_1_ = bf16[32,512]{1,0:T(8,128)(2,1)S(1)} collective-permute-done((bf16[32,512]{1,0:T(8,128)(2,1)S(1)}, bf16[32,512]{1,0:T(8,128)(2,1)S(1)}, u32[]{:S(2)}, u32[]{:S(2)}) %collective-permute-start.15) | collective-permute-done | bytes 32800 | tf_op jit(solution)/shard_map/ppermute | solution.py:427
  50.0 2.2 %collective-permute-done.16.rest_2_ = bf16[32,512]{1,0:T(8,128)(2,1)S(1)} collective-permute-done((bf16[32,512]{1,0:T(8,128)(2,1)S(1)}, bf16[32,512]{1,0:T(8,128)(2,1)S(1)}, u32[]{:S(2)}, u32[]{:S(2)}) %collective-permute-start.16) | collective-permute-done | bytes 32800 | tf_op jit(solution)/shard_map/ppermute | solution.py:427
  52.3 0.8 %shard_map.82 = (bf16[128,512]{1,0:T(8,128)(2,1)}, bf16[128,512]{1,0:T(8,128)(2,1)}) custom-call(s32[8,128]{1,0:T(8,128)S(1)} %shard_map.68.plan, f32[8,128]{1,0:T(8,128)S(1)} %get-tuple-element.53.factors, bf16[128,512]{1,0:T(8,128)(2,1)S(1)} %shard_map.72.stay, f32[128,512]{1,0:T(8,128)S(1)} %shard_map.80.stay_2, ...), custom_call_target="tpu_custom_call" | custom-call | bytes 262144 | tf_op jit(solution)/shard_map/pallas_call | solution.py:512
  (29 shorter events, 2.5 us)
Async XLA Ops:
  0.6 1.9 %copy-start = (bf16[1,3,1024,512]{3,2,1,0:T(8,128)(2,1)S(1)}, bf16[1,3,1024,512]{3,2,1,0:T(8,128)(2,1)}, u32[]{:S(2)}) copy-start(bf16[1,3,1024,512]{3,2,1,0:T(8,128)(2,1)} %left.7) | copy-start | bytes 9437188
  0.6 1.9 %copy-start.1 = (bf16[3,128,128]{2,1,0:T(8,128)(2,1)S(1)}, bf16[3,128,128]{2,1,0:T(8,128)(2,1)}, u32[]{:S(2)}) copy-start(bf16[3,128,128]{2,1,0:T(8,128)(2,1)} %right.7) | copy-start | bytes 294916
  0.7 1.9 %copy-start.2 = (bf16[1,128,512]{2,1,0:T(8,128)(2,1)S(1)}, bf16[1,128,512]{2,1,0:T(8,128)(2,1)}, u32[]{:S(2)}) copy-start(bf16[1,128,512]{2,1,0:T(8,128)(2,1)} %param.5) | copy-start | bytes 393220
  0.7 1.9 %copy-start.3 = (s32[8]{0:T(128)S(1)}, s32[8]{0:T(128)}, u32[]{:S(2)}) copy-start(s32[8]{0:T(128)} %widths.1) | copy-start | bytes 100
  0.7 1.9 %copy-start.4 = (s32[8]{0:T(128)S(1)}, s32[8]{0:T(128)}, u32[]{:S(2)}) copy-start(s32[8]{0:T(128)} %holders.1) | copy-start | bytes 100
  0.7 1.7 %collective-permute-start = (bf16[128,512]{1,0:T(8,128)(2,1)}, bf16[128,512]{1,0:T(8,128)(2,1)S(1)}, u32[]{:S(2)}, u32[]{:S(2)}) collective-permute-start(bf16[128,512]{1,0:T(8,128)(2,1)} %bitcast.5), channel_id=1, source_target_pairs={{0,1},{1,0},{2,3},{3,2},{4,5},{5,4},{6,7},{7,6},{8,9},{9,8},{10,11... | collective-permute-start | bytes 393224 | tf_op jit(solution)/shard_map/ppermute | solution.py:432
  3.3 7.9 %collective-permute-start.1 = (bf16[2,32,512]{2,1,0:T(8,128)(2,1)S(1)}, bf16[2,32,512]{2,1,0:T(8,128)(2,1)S(1)}, u32[]{:S(2)}, u32[]{:S(2)}) collective-permute-start(bf16[2,32,512]{2,1,0:T(8,128)(2,1)S(1)} %get-tuple-element.33), channel_id=1, source_target_pairs={{0,8},{2,10},{4,12},{6,14},{8,0},{10,2},{12,4},{14,6},{1,9},{3,11}... | collective-permute-start | bytes 196616 | tf_op jit(solution)/shard_map/ppermute | solution.py:427
  7.4 6.3 %collective-permute-start.2 = (bf16[2,32,512]{2,1,0:T(8,128)(2,1)S(1)}, bf16[2,32,512]{2,1,0:T(8,128)(2,1)S(1)}, u32[]{:S(2)}, u32[]{:S(2)}) collective-permute-start(bf16[2,32,512]{2,1,0:T(8,128)(2,1)S(1)} %get-tuple-element.34), channel_id=1, source_target_pairs={{0,12},{2,14},{4,8},{6,10},{8,4},{10,6},{12,0},{14,2},{1,13},{3,15... | collective-permute-start | bytes 196616 | tf_op jit(solution)/shard_map/ppermute | solution.py:427
  8.8 5.0 %collective-permute-start.3 = (bf16[2,32,512]{2,1,0:T(8,128)(2,1)S(1)}, bf16[2,32,512]{2,1,0:T(8,128)(2,1)S(1)}, u32[]{:S(2)}, u32[]{:S(2)}) collective-permute-start(bf16[2,32,512]{2,1,0:T(8,128)(2,1)S(1)} %get-tuple-element.35), channel_id=1, source_target_pairs={{0,4},{2,6},{4,0},{6,2},{8,12},{10,14},{12,8},{14,10},{1,5},{3,7},... | collective-permute-start | bytes 196616 | tf_op jit(solution)/shard_map/ppermute | solution.py:427
  14.0 4.6 %collective-permute-start.5 = (bf16[2,32,512]{2,1,0:T(8,128)(2,1)S(1)}, bf16[2,32,512]{2,1,0:T(8,128)(2,1)S(1)}, u32[]{:S(2)}, u32[]{:S(2)}) collective-permute-start(bf16[2,32,512]{2,1,0:T(8,128)(2,1)S(1)} %get-tuple-element.42), channel_id=1, source_target_pairs={{0,2},{2,0},{4,6},{6,4},{8,10},{10,8},{12,14},{14,12},{1,3},{3,1},... | collective-permute-start | bytes 196616 | tf_op jit(solution)/shard_map/ppermute | solution.py:436
  16.0 6.3 %collective-permute-start.4 = (bf16[2,32,512]{2,1,0:T(8,128)(2,1)S(1)}, bf16[2,32,512]{2,1,0:T(8,128)(2,1)S(1)}, u32[]{:S(2)}, u32[]{:S(2)}) collective-permute-start(bf16[2,32,512]{2,1,0:T(8,128)(2,1)S(1)} %get-tuple-element.39), channel_id=1, source_target_pairs={{0,2},{2,0},{4,6},{6,4},{8,10},{10,8},{12,14},{14,12},{1,3},{3,1},... | collective-permute-start | bytes 196616 | tf_op jit(solution)/shard_map/ppermute | solution.py:436
  18.6 4.9 %collective-permute-start.6 = (bf16[32,512]{1,0:T(8,128)(2,1)S(1)}, bf16[32,512]{1,0:T(8,128)(2,1)S(1)}, u32[]{:S(2)}, u32[]{:S(2)}) collective-permute-start(bf16[32,512]{1,0:T(8,128)(2,1)S(1)} %get-tuple-element.43), channel_id=1, source_target_pairs={{0,8},{2,10},{4,12},{6,14},{8,0},{10,2},{12,4},{14,6},{1,9},{3,11}... | collective-permute-start | bytes 98312 | tf_op jit(solution)/shard_map/ppermute | solution.py:427
  21.6 5.7 %collective-permute-start.7 = (bf16[32,512]{1,0:T(8,128)(2,1)S(1)}, bf16[32,512]{1,0:T(8,128)(2,1)S(1)}, u32[]{:S(2)}, u32[]{:S(2)}) collective-permute-start(bf16[32,512]{1,0:T(8,128)(2,1)S(1)} %get-tuple-element.44), channel_id=1, source_target_pairs={{0,12},{2,14},{4,8},{6,10},{8,4},{10,6},{12,0},{14,2},{1,13},{3,15... | collective-permute-start | bytes 98312 | tf_op jit(solution)/shard_map/ppermute | solution.py:427
  22.4 5.0 %collective-permute-start.8 = (bf16[32,512]{1,0:T(8,128)(2,1)S(1)}, bf16[32,512]{1,0:T(8,128)(2,1)S(1)}, u32[]{:S(2)}, u32[]{:S(2)}) collective-permute-start(bf16[32,512]{1,0:T(8,128)(2,1)S(1)} %get-tuple-element.45), channel_id=1, source_target_pairs={{0,4},{2,6},{4,0},{6,2},{8,12},{10,14},{12,8},{14,10},{1,5},{3,7},... | collective-permute-start | bytes 98312 | tf_op jit(solution)/shard_map/ppermute | solution.py:427
  27.4 1.4 %collective-permute-start.9 = (bf16[128,512]{1,0:T(8,128)(2,1)S(1)}, bf16[128,512]{1,0:T(8,128)(2,1)S(1)}, u32[]{:S(2)}, u32[]{:S(2)}) collective-permute-start(bf16[128,512]{1,0:T(8,128)(2,1)S(1)} %shard_map.76.own.first), channel_id=1, source_target_pairs={{0,1},{1,0},{2,3},{3,2},{4,5},{5,4},{6,7},{7,6},{8,9},{9,8},{10,11... | collective-permute-start | bytes 393224 | tf_op jit(solution)/shard_map/ppermute | solution.py:432
  29.7 7.8 %collective-permute-start.10 = (bf16[272,128]{1,0:T(8,128)(2,1)S(1)}, bf16[272,128]{1,0:T(8,128)(2,1)S(1)}, u32[]{:S(2)}, u32[]{:S(2)}) collective-permute-start(bf16[272,128]{1,0:T(8,128)(2,1)S(1)} %get-tuple-element.47), channel_id=1, source_target_pairs={{0,8},{2,10},{4,12},{6,14},{8,0},{10,2},{12,4},{14,6},{1,9},{3,11}... | collective-permute-start | bytes 208904 | tf_op jit(solution)/shard_map/ppermute | solution.py:427
  30.8 6.8 %collective-permute-start.11 = (bf16[272,128]{1,0:T(8,128)(2,1)S(1)}, bf16[272,128]{1,0:T(8,128)(2,1)S(1)}, u32[]{:S(2)}, u32[]{:S(2)}) collective-permute-start(bf16[272,128]{1,0:T(8,128)(2,1)S(1)} %get-tuple-element.48), channel_id=1, source_target_pairs={{0,12},{2,14},{4,8},{6,10},{8,4},{10,6},{12,0},{14,2},{1,13},{3,15... | collective-permute-start | bytes 208904 | tf_op jit(solution)/shard_map/ppermute | solution.py:427
  32.0 6.8 %collective-permute-start.12 = (bf16[272,128]{1,0:T(8,128)(2,1)S(1)}, bf16[272,128]{1,0:T(8,128)(2,1)S(1)}, u32[]{:S(2)}, u32[]{:S(2)}) collective-permute-start(bf16[272,128]{1,0:T(8,128)(2,1)S(1)} %get-tuple-element.49), channel_id=1, source_target_pairs={{0,4},{2,6},{4,0},{6,2},{8,12},{10,14},{12,8},{14,10},{1,5},{3,7},... | collective-permute-start | bytes 208904 | tf_op jit(solution)/shard_map/ppermute | solution.py:427
  39.3 5.1 %collective-permute-start.13 = (bf16[272,128]{1,0:T(8,128)(2,1)S(1)}, bf16[272,128]{1,0:T(8,128)(2,1)S(1)}, u32[]{:S(2)}, u32[]{:S(2)}) collective-permute-start(bf16[272,128]{1,0:T(8,128)(2,1)S(1)} %get-tuple-element.52), channel_id=1, source_target_pairs={{0,2},{2,0},{4,6},{6,4},{8,10},{10,8},{12,14},{14,12},{1,3},{3,1},... | collective-permute-start | bytes 208904 | tf_op jit(solution)/shard_map/ppermute | solution.py:436
  40.7 7.2 %collective-permute-start.14 = (bf16[256,128]{1,0:T(8,128)(2,1)S(1)}, bf16[256,128]{1,0:T(8,128)(2,1)S(1)}, u32[]{:S(2)}, u32[]{:S(2)}) collective-permute-start(bf16[256,128]{1,0:T(8,128)(2,1)S(1)} %get-tuple-element.55), channel_id=1, source_target_pairs={{0,2},{2,0},{4,6},{6,4},{8,10},{10,8},{12,14},{14,12},{1,3},{3,1},... | collective-permute-start | bytes 196616 | tf_op jit(solution)/shard_map/ppermute | solution.py:436
  44.7 5.2 %collective-permute-start.15 = (bf16[32,512]{1,0:T(8,128)(2,1)S(1)}, bf16[32,512]{1,0:T(8,128)(2,1)S(1)}, u32[]{:S(2)}, u32[]{:S(2)}) collective-permute-start(bf16[32,512]{1,0:T(8,128)(2,1)S(1)} %get-tuple-element.57), channel_id=1, source_target_pairs={{0,8},{2,10},{4,12},{6,14},{8,0},{10,2},{12,4},{14,6},{1,9},{3,11}... | collective-permute-start | bytes 98312 | tf_op jit(solution)/shard_map/ppermute | solution.py:427
  46.4 5.8 %collective-permute-start.16 = (bf16[32,512]{1,0:T(8,128)(2,1)S(1)}, bf16[32,512]{1,0:T(8,128)(2,1)S(1)}, u32[]{:S(2)}, u32[]{:S(2)}) collective-permute-start(bf16[32,512]{1,0:T(8,128)(2,1)S(1)} %get-tuple-element.58), channel_id=1, source_target_pairs={{0,12},{2,14},{4,8},{6,10},{8,4},{10,6},{12,0},{14,2},{1,13},{3,15... | collective-permute-start | bytes 98312 | tf_op jit(solution)/shard_map/ppermute | solution.py:427
  47.9 4.3 %collective-permute-start.17 = (bf16[32,512]{1,0:T(8,128)(2,1)S(1)}, bf16[32,512]{1,0:T(8,128)(2,1)S(1)}, u32[]{:S(2)}, u32[]{:S(2)}) collective-permute-start(bf16[32,512]{1,0:T(8,128)(2,1)S(1)} %get-tuple-element.59), channel_id=1, source_target_pairs={{0,4},{2,6},{4,0},{6,2},{8,12},{10,14},{12,8},{14,10},{1,5},{3,7},... | collective-permute-start | bytes 98312 | tf_op jit(solution)/shard_map/ppermute | solution.py:427
